TPU v7x, 32 devices: a whole 2x2x4 slice. The times are simulated.
32 devices in a mesh: groups: 2 (over y), recv: 4 (over z), win: 2 (over x), freq: 2 (over core).
Axes of the slice: x: 2, y: 2, z: 4, core: 2. Of those that a mesh axis runs over, the one named last changes fastest.
Arguments:
- spectra: bfloat16 [2, 2, 1024, 4096], P('win', None, ('groups', 'recv'), 'freq'), parts along dimension 2, may hold values from -6 to 6
- window_keep: int32 [4], P(('groups', 'win')), parts along dimension 0, may hold values from 0 to 1, as said below
- owners: int32 [8], P('groups'), parts along dimension 0, may hold values from 0 to 3, as said below
- pair_src: int32 [4, 512], P(None, ('groups', 'recv')), parts along dimension 1, may hold values from 0 to 127
- pair_rec: int32 [4, 512], P(None, ('groups', 'recv')), parts along dimension 1, may hold values from 0 to 127
- pair_count: int32 [4, 8], P(None, ('groups', 'recv')), parts along dimension 1, may hold values from 1 to 64, 128 in all within a row
- observed: float32 [4, 512, 4096], P(None, ('groups', 'recv'), ('win', 'freq')), parts along dimension 1, may hold values from -6 to 6
Outputs:
- normed: float32 [4, 512, 4096], P(None, ('groups', 'recv'), ('win', 'freq')), parts along dimension 1
- adjoint: float32 [1024, 4096], P(('groups', 'recv'), ('win', 'freq')), parts along dimension 0
There are 2 independent parts, one for each index of `groups`. A program takes and returns all parts, laid end to end along the dimension named above; each array names one. Nothing has to cross between parts.
Inputs may be any that keep to these rules, and one draw needn't show every extreme that they name: `owners`: distinct receiver blocks. `pair_count`: within one part, for each source block some receiver block holds exactly 64 used slots, and that source block's counts over all receiver blocks of the part sum to 64 * 4 / 2. `window_keep`: within one part at least one window is kept and at least one is dropped.
All inputs are finite; a program needn't handle non-finite values.
Results may differ from a plain program's by a relative error of at most 0.0037.
Values may be sent and summed in bfloat16 or wider, within the bound.
No kernel may reach another device: no remote copies, remote signals or barrier semaphores. Data moves between devices by JAX's collectives and lax.ppermute only.
A program may use at most 128 MiB of HBM per device.

v0:
```python
import math

import jax
import jax.numpy as jnp
from jax import lax
from jax.sharding import PartitionSpec as P

EPSILON = 1e-06


def spread(block, axis, source):
    block = jnp.where(lax.axis_index(axis) == source, block, jnp.zeros_like(block))
    return lax.psum(block, axis)


def dft_table(first_bin, bin_count, bin_total, lag_total):
    frequency = first_bin + jnp.arange(bin_count, dtype=jnp.int32)
    shifts = jnp.arange(lag_total, dtype=jnp.int32) - lag_total // 2
    period = 2 * bin_total
    phase_index = frequency[:, None] * shifts[None, :] % period
    angles = phase_index.astype(jnp.float32) * (2.0 * math.pi / period)
    return jnp.concatenate([jnp.cos(angles), -jnp.sin(angles)], axis=0).astype(jnp.bfloat16)


def shards(spectra, window_keep, owners, pair_src, pair_rec, pair_count, observed):
    windows = spectra.shape[0]
    channels = spectra.shape[2]
    bins_dev = spectra.shape[3]
    pair_slots = pair_src.shape[1]
    blocks = owners.shape[0]
    lag_dev = observed.shape[2]
    lag_total = lag_dev * lax.axis_size("win") * lax.axis_size("freq")
    bin_total = bins_dev * lax.axis_size("freq")
    lag_scale = 1.0 / math.sqrt(bin_total * windows * lax.axis_size("win"))
    cosine_table = dft_table(lax.axis_index("freq") * bins_dev, bins_dev, bin_total, lag_total)
    kept_weight = window_keep.astype(jnp.float32)
    valid_slots = (jnp.arange(pair_slots, dtype=jnp.int32)[None, :] < pair_count).astype(
        jnp.float32
    )

    def fetch_block(block_index):
        return spread(spectra, "recv", owners[block_index])

    def cross_rows(source_block, block_index):
        source = jnp.take(source_block, pair_src[block_index], axis=2).astype(jnp.float32)
        receiver = jnp.take(spectra, pair_rec[block_index], axis=2).astype(jnp.float32)
        real_part = source[:, 0] * receiver[:, 0] + source[:, 1] * receiver[:, 1]
        imag_part = source[:, 1] * receiver[:, 0] - source[:, 0] * receiver[:, 1]
        return jnp.concatenate([real_part, imag_part], axis=-1).astype(jnp.bfloat16)

    def lag_terms(cross):
        summed_terms = kept_weight[0] * jnp.dot(
            cross[0], cosine_table, preferred_element_type=jnp.float32
        )
        return summed_terms

    def to_lags(terms):
        return lax.psum_scatter(terms, ("win", "freq"), scatter_dimension=1, tiled=True)

    pieces = [
        to_lags(lag_terms(cross_rows(fetch_block(block_index), block_index)))
        for block_index in range(blocks)
    ]
    summed = jnp.stack(pieces)
    corr = summed * lag_scale * valid_slots[:, :, None]
    square_part = jnp.sum(corr * corr, axis=2)
    product_part = jnp.sum(corr * observed, axis=2)
    square, product = lax.psum((square_part, product_part), ("win", "freq"))
    scale_norm = jnp.sqrt(square / lag_total + EPSILON)
    normed = corr / scale_norm[:, :, None]
    bending = (square / (scale_norm * scale_norm) - product / scale_norm) / lag_total
    gradient = (
        valid_slots[:, :, None]
        * (normed - observed - normed * bending[:, :, None])
        / scale_norm[:, :, None]
    )
    selector = (
        pair_src[:, :, None] == jnp.arange(channels, dtype=jnp.int32)[None, None, :]
    ).astype(jnp.float32)
    returned = jnp.einsum("bpc,bpl->bcl", selector, gradient, precision=lax.Precision.HIGHEST)
    routing = (
        owners[:, None] == jnp.arange(lax.axis_size("recv"), dtype=jnp.int32)[None, :]
    ).astype(jnp.float32)
    outgoing = jnp.einsum("br,bcl->rcl", routing, returned, precision=lax.Precision.HIGHEST)
    incoming = lax.all_to_all(outgoing, "recv", split_axis=0, concat_axis=0, tiled=True)
    adjoint = jnp.sum(incoming, axis=0)
    return (normed, adjoint)


def solution(mesh):
    return jax.shard_map(
        shards,
        mesh=mesh,
        in_specs=(
            P("win", None, ("groups", "recv"), "freq"),
            P(("groups", "win")),
            P("groups"),
            P(None, ("groups", "recv")),
            P(None, ("groups", "recv")),
            P(None, ("groups", "recv")),
            P(None, ("groups", "recv"), ("win", "freq")),
        ),
        out_specs=(
            P(None, ("groups", "recv"), ("win", "freq")),
            P(("groups", "recv"), ("win", "freq")),
        ),
        check_vma=False,
    )
```

profile of v0, /device:TPU:0, one launch (start us, length us, event | category | flops | bytes accessed | tf_op | source)
XLA Modules:
  0.0 386.1 jit_solution(3987074294718112827)
XLA Ops:
  7.2 1.4 fusion.44
  11.1 6.6 %broadcast_select_fusion.3 = (bf16[1,2,128,2048]{3,1,2,0:T(2,128)(2,1)}, bf16[2,128,2048]{2,0,1:T(2,128)(2,1)S(1)}, bf16[1,2,128,2048]{3,1,2,0:T(2,128)(2,1)}, b...) fusion(pred[]{:T(512)S(6)} %eq.40, bf16[1,2,128,2048]{3,2,1,0:T(8,128)(2,1)} %param.9, pred[]{:T(512)S(6)} %eq.41, ...), kind=kLoop, calls=%fused_computation.28 | loop fusion | flops 2097152 | bytes 6291460 | tf_op jit(solution)/shard_map/jit(_where)/select_n | solution.py:12
  19.6 2.4 gather_fusion.7
  21.9 2.4 gather_fusion.5
  24.3 1.6 gather_fusion.3
  25.9 1.6 gather_fusion.1
  27.5 1.9 fusion.12
  29.4 2.2 fusion.16
  32.3 136.7 %cosine_convert_fusion = (bf16[2048,4096]{1,0:T(8,128)(2,1)}, bf16[2048,4096]{1,0:T(8,128)(2,1)}) fusion(s32[4096]{0:T(1024)S(1)} %iota_add_fusion, s32[2048]{0:T(1024)S(1)} %iota_add_fusion.1), kind=kLoop, calls=%fused_computation.18 | loop fusion | flops 142606336 | bytes 33579008 | tf_op jit(solution)/shard_map/convert.12
  169.0 7.7 %all-reduce.4.cloned.1.call-done = (bf16[1,2,128,2048]{3,1,2,0:T(2,128)(2,1)}, bf16[1,2,128,2048]{3,1,2,0:T(2,128)(2,1)}, bf16[1,2,128,2048]{3,1,2,0:T(2,128)(2,1)}, bf16[1,2,128,2048]{3,1,2,0:T(2,128)(2,1)}) async-done(((bf16[1,2,128,2048]{3,1,2,0:T(2,128)(2,1)}, bf16[1,2,128,2048]{3,1,2,0:T(2,128)(2,1)}, bf16[1,2,128,2048]{3,1,2,0:T(2,128)(2,1)}, bf16[1,2,128,2048]{3,1,2,0:T(2,128)(2,1)}), ...) | async-done | bytes 4194320 | tf_op jit(solution)/shard_map/psum | solution.py:13
  176.6 3.6 gather_fusion.2
  180.2 3.6 gather_fusion
  183.8 3.1 fusion.11
  186.9 3.1 add_convert_fusion.2
  190.4 14.0 %convolution_multiply_fusion.2 = f32[64,4096]{1,0:T(8,128)} fusion(bf16[64,2048]{1,0:T(8,128)(2,1)S(1)} %bitcast.115, bf16[64,2048]{1,0:T(8,128)(2,1)S(1)} %bitcast.111, f32[]{:T(128)} %bitcast, bf16[2048,4096]{1,0:T(8,128)(2,1)} %get-tuple-element.41, bf16[2048,4096]{1,0:T(8,128)(2,1)} %get-tuple-element.40), kind=kOutput, calls=%fused_computation.21 | convolution fusion | flops 2215903232 | bytes 35127300 | tf_op jit(solution)/shard_map/dot_general | solution.py:52
  204.6 3.6 gather_fusion.6
  208.2 3.6 gather_fusion.4
  211.8 3.1 fusion.15
  214.9 1.6 add_convert_fusion.1
  216.9 14.3 %convolution_multiply_fusion.1 = f32[64,4096]{1,0:T(8,128)} fusion(bf16[64,2048]{1,0:T(8,128)(2,1)S(1)} %bitcast.116, bf16[64,2048]{1,0:T(8,128)(2,1)S(1)} %bitcast.113, f32[]{:T(128)} %bitcast, bf16[2048,4096]{1,0:T(8,128)(2,1)} %get-tuple-element.41, bf16[2048,4096]{1,0:T(8,128)(2,1)} %get-tuple-element.40), kind=kOutput, calls=%fused_computation.20 | convolution fusion | flops 2215903232 | bytes 35127300 | tf_op jit(solution)/shard_map/dot_general | solution.py:52
  231.3 1.7 add_convert_fusion.3
  233.4 14.6 %convolution_multiply_fusion.3 = f32[64,4096]{1,0:T(8,128)} fusion(bf16[64,2048]{1,0:T(8,128)(2,1)S(1)} %bitcast.117, bf16[64,2048]{1,0:T(8,128)(2,1)S(1)} %bitcast.114, f32[]{:T(128)} %bitcast, bf16[2048,4096]{1,0:T(8,128)(2,1)} %get-tuple-element.41, bf16[2048,4096]{1,0:T(8,128)(2,1)} %get-tuple-element.40), kind=kOutput, calls=%fused_computation.22 | convolution fusion | flops 2215903232 | bytes 35127300 | tf_op jit(solution)/shard_map/dot_general | solution.py:52
  248.3 1.7 add_convert_fusion
  250.3 14.5 %convolution_multiply_fusion = f32[64,4096]{1,0:T(8,128)} fusion(bf16[64,2048]{1,0:T(8,128)(2,1)S(1)} %bitcast.112, bf16[64,2048]{1,0:T(8,128)(2,1)S(1)} %bitcast.110, f32[]{:T(128)} %bitcast, bf16[2048,4096]{1,0:T(8,128)(2,1)} %get-tuple-element.41, bf16[2048,4096]{1,0:T(8,128)(2,1)} %get-tuple-element.40), kind=kOutput, calls=%fused_computation.19 | convolution fusion | flops 2215903232 | bytes 35127300 | tf_op jit(solution)/shard_map/dot_general | solution.py:52
  265.1 18.2 %reduce-scatter.5.cloned.1.call-done = f32[64,1024]{1,0:T(8,128)} async-done(((f32[64,4096]{1,0:T(8,128)}), f32[64,1024]{1,0:T(8,128)}) %reduce-scatter.5.cloned.1.call-update) | async-done | bytes 262160 | tf_op jit(solution)/shard_map/reduce_scatter | solution.py:58
  283.3 27.9 %reduce-scatter.11.cloned.1.call-done = f32[64,1024]{1,0:T(8,128)} async-done(((f32[64,4096]{1,0:T(8,128)}), f32[64,1024]{1,0:T(8,128)}) %reduce-scatter.11.cloned.1.call-update) | async-done | bytes 262160 | tf_op jit(solution)/shard_map/reduce_scatter | solution.py:58
  311.2 1.5 multiply_reduce_fusion
  312.7 5.8 %all-reduce = (f32[4,64]{1,0:T(4,128)S(1)}, f32[4,64]{1,0:T(4,128)S(1)}) all-reduce(f32[4,64]{1,0:T(4,128)S(1)} %get-tuple-element.4, f32[4,64]{1,0:T(4,128)S(1)} %get-tuple-element.3), channel_id=1, replica_groups=mesh['groups'=2,'recv'=4,'win'=2,'freq'=2] {'win','freq'}, use_global_device_ids=true, to_apply=%region_9.11 | all-reduce | flops 512 | bytes 4096 | tf_op jit(solution)/shard_map/psum | solution.py:68
  318.4 1.4 broadcast_divide_fusion
  319.8 1.2 fusion.5
  321.1 3.2 fusion.3
  325.6 52.6 %all_to_all.5 = f32[4,128,1024]{2,1,0:T(8,128)S(1)} all-to-all(f32[4,128,1024]{2,1,0:T(8,128)S(1)} %copy.64), channel_id=1, replica_groups=mesh['groups'=2,'recv'=4,'win'=2,'freq'=2] {'recv'}, dimensions={0} | all-to-all | bytes 4194304 | tf_op jit(solution)/shard_map/all_to_all | solution.py:85
  (51 shorter events, 6.1 us)
Async XLA Ops:
  7.2 169.5 %all-reduce.4.cloned.1.call-start = ((), (), s32[]{:S(2)}) async-start(), calls=%async_computation.9 | async-start | bytes 8388608 | tf_op jit(solution)/shard_map/psum | solution.py:13
  17.7 247.3 %reduce-scatter.7.cloned.1.call-start = ((), (), s32[]{:S(2)}) async-start(), calls=%async_computation.6 | async-start | bytes 1310720 | tf_op jit(solution)/shard_map/reduce_scatter | solution.py:58
  204.4 60.7 %reduce-scatter.9.cloned.1.call-start = ((), (), s32[]{:S(2)}) async-start(), calls=%async_computation.7 | async-start | bytes 1310720 | tf_op jit(solution)/shard_map/reduce_scatter | solution.py:58
  216.9 14.4 %copy-start = (f32[1,2,64,2048]{3,1,2,0:T(2,128)S(1)}, f32[1,2,64,2048]{3,1,2,0:T(2,128)}, u32[]{:S(2)}) copy-start(f32[1,2,64,2048]{3,1,2,0:T(2,128)} %get-tuple-element.64) | copy-start | bytes 3145732
  231.3 52.0 %reduce-scatter.5.cloned.1.call-start = ((), (), s32[]{:S(2)}) async-start(), calls=%async_computation.5 | async-start | bytes 1310720 | tf_op jit(solution)/shard_map/reduce_scatter | solution.py:58
  233.3 15.0 %copy-start.1 = (f32[1,2,64,2048]{3,1,2,0:T(2,128)S(1)}, f32[1,2,64,2048]{3,1,2,0:T(2,128)}, u32[]{:S(2)}) copy-start(f32[1,2,64,2048]{3,1,2,0:T(2,128)} %get-tuple-element.67) | copy-start | bytes 3145732
  248.0 63.2 %reduce-scatter.11.cloned.1.call-start = ((), (), s32[]{:S(2)}) async-start(), calls=%async_computation.8 | async-start | bytes 1310720 | tf_op jit(solution)/shard_map/reduce_scatter | solution.py:58
  250.3 14.6 %copy-start.6 = (s32[4,1]{0,1:T(1,128)S(1)}, s32[4,1]{0,1:T(1,128)}, u32[]{:S(2)}) copy-start(s32[4,1]{0,1:T(1,128)} %param.14) | copy-start | bytes 52
  250.3 60.8 %copy-start.2 = (f32[4,64,1024]{2,1,0:T(8,128)S(1)}, f32[4,64,1024]{2,1,0:T(8,128)}, u32[]{:S(2)}) copy-start(f32[4,64,1024]{2,1,0:T(8,128)} %param.15) | copy-start | bytes 3145732
  250.3 69.5 %copy-start.5 = (s32[4,64]{1,0:T(4,128)S(1)}, s32[4,64]{1,0:T(4,128)}, u32[]{:S(2)}) copy-start(s32[4,64]{1,0:T(4,128)} %param.12) | copy-start | bytes 3076
  250.3 70.7 %copy-start.4 = (s32[4]{0:T(128)S(1)}, s32[4]{0:T(128)}, u32[]{:S(2)}) copy-start(s32[4]{0:T(128)} %param.11) | copy-start | bytes 52
  319.8 59.3 %copy-start.3 = (f32[4,64,1024]{2,1,0:T(8,128)}, f32[4,64,1024]{2,1,0:T(8,128)S(1)}, u32[]{:S(2)}) copy-start(f32[4,64,1024]{2,1,0:T(8,128)S(1)} %broadcast_divide_fusion) | copy-start | bytes 3145732
Sparse Core Ops, SparseCore 0:
  17.8 158.7 all-reduce.3
  204.5 23.7 reduce-scatter.6
  231.4 24.3 reduce-scatter.8
  258.3 24.9 reduce-scatter.4
  286.2 24.8 reduce-scatter.10
where the time goes:
time: 393 us; the launch traced here: 386 us
  other arithmetic  167 us (42%)
  matrix products  61.9 us (16%)
  blocking collectives  58.3 us (15%)
  waiting for transfers between devices  53.8 us (14%)
  local copies, waits for them, and re-layouts  26.3 us (7%)
  between operations  17.7 us (5%)
    another operation x5, other arithmetic  145 us
    dot_general x4, matrix products, lag_terms(): jnp.dot(cross[0], cosine_table, preferred_element_type=jnp.float32)  57.4 us
    all_to_all x1, blocking collectives, shards(): lax.all_to_all(outgoing, 'recv', split_axis=0, concat_axis=0, tiled=True)  52.6 us
    reduce_scatter x4, waiting for transfers between devices, to_lags(): lax.psum_scatter(terms, ('win', 'freq'), scatter_dimension=1, tiled=True)  46.1 us
    gather x4, local copies, waits for them, and re-layouts, cross_rows(): jnp.take(source_block, pair_src[block_index], axis=2).astype(jnp.float32)  14.4 us
    gather x4, local copies, waits for them, and re-layouts, cross_rows(): jnp.take(spectra, pair_rec[block_index], axis=2).astype(jnp.float32)  7.94 us
  transfers between devices with their start and end apart: 5, of which 3 were waited for; matrix products, arithmetic and copies ran while one was open for 54% of the time, Pallas kernels for 0%

commit v1 on v0

v1 whole, which is shorter than its diff:
```python
import functools
import math

import jax
import jax.numpy as jnp
import ml_dtypes
import numpy as np
from jax import lax
from jax.experimental import pallas as pl
from jax.experimental.pallas import tpu as pltpu
from jax.sharding import PartitionSpec as P

EPSILON = 1e-06
MIB = 1 << 20
LANES = 128
BF16 = jnp.bfloat16
F32 = jnp.float32


def shifted(value, axis, size, shift):
    if shift % size == 0:
        return value
    return lax.ppermute(value, axis, [(i, (i + shift) % size) for i in range(size)])


def table_kernel(row_cos, row_sin, base_cos, base_sin, table):
    ca, sa = row_cos[0], row_sin[0]
    cb, sb = base_cos[...], base_sin[...]
    table[0, :LANES] = (ca * cb - sa * sb).astype(BF16)
    table[0, LANES:] = (-(sa * cb + ca * sb)).astype(BF16)


def make_table(first_bin, classes, span, period):
    m = np.arange(LANES, dtype=np.int64)[:, None]
    u = np.arange(span, dtype=np.int64)[None, :]
    base = (classes * m * u % period) * (2.0 * math.pi / period)
    base_cos, base_sin = np.cos(base).astype(np.float32), np.sin(base).astype(np.float32)
    frequency = first_bin + jnp.arange(classes, dtype=jnp.int32)
    turns = frequency[:, None] * jnp.arange(span, dtype=jnp.int32)[None, :] % period
    angles = turns.astype(F32) * (2.0 * math.pi / period)
    row_cos, row_sin = jnp.cos(angles)[:, None, :], jnp.sin(angles)[:, None, :]
    row = pl.BlockSpec((1, 1, span), lambda r: (r, 0, 0))
    whole = pl.BlockSpec((LANES, span), lambda r: (0, 0))
    return pl.pallas_call(
        table_kernel,
        grid=(classes,),
        out_shape=jax.ShapeDtypeStruct((classes, 2 * LANES, span), BF16),
        in_specs=[row, row, whole, whole],
        out_specs=pl.BlockSpec((1, 2 * LANES, span), lambda r: (r, 0, 0)),
        compiler_params=pltpu.CompilerParams(vmem_limit_bytes=16 * MIB),
        cost_estimate=pl.CostEstimate(
            flops=6 * classes * LANES * span, bytes_accessed=6 * MIB, transcendentals=0
        ),
        name="table",
    )(row_cos, row_sin, jnp.asarray(base_cos), jnp.asarray(base_sin))


def rows_kernel(used, shifts, order, *refs):
    held, (perm, pick_src, pick_rec), outs = refs[:shifts], refs[shifts : shifts + 3], refs[shifts + 3 :]
    slots = outs[0].shape[2]
    blocks = outs[-1].shape[0]
    for u in range(used):
        for half in range(2):
            x = held[0][half]
            for s in range(1, shifts):
                x = jnp.where(order[u] == s, held[s][half], x)
            x = jnp.dot(x, perm[...], preferred_element_type=F32).astype(BF16)
            sent = jnp.dot(pick_src[...], x, preferred_element_type=F32).astype(BF16)
            for d, out in enumerate(outs[:-1]):
                out[u, half] = sent[d * slots : (d + 1) * slots]
            own = jnp.dot(pick_rec[...], x, preferred_element_type=F32).astype(BF16)
            for b in range(blocks):
                outs[-1][b, u, half] = own[b * slots : (b + 1) * slots]


def gather_rows(order, held, classes, pick_src, pick_rec, slots):
    shifts, used = len(held), order.shape[0]
    part = held[0].shape[-1]
    source = np.arange(part)
    perm = np.zeros((part, part), ml_dtypes.bfloat16)
    perm[source, source % classes * LANES + source // classes] = 1
    sends, blocks = pick_src.shape[0] // slots, pick_rec.shape[0] // slots
    sent = jax.ShapeDtypeStruct((used, 2, slots, part), BF16)
    own = jax.ShapeDtypeStruct((blocks, used, 2, slots, part), BF16)
    vmem = pl.BlockSpec(memory_space=pltpu.VMEM)
    return pl.pallas_call(
        functools.partial(rows_kernel, used, shifts),
        out_shape=[sent] * sends + [own],
        in_specs=[pl.BlockSpec(memory_space=pltpu.SMEM)] + [vmem] * (shifts + 3),
        out_specs=[vmem] * (sends + 1),
        compiler_params=pltpu.CompilerParams(vmem_limit_bytes=32 * MIB),
        cost_estimate=pl.CostEstimate(
            flops=4 * used * part * (128 * part + 512 * 128), bytes_accessed=8 * MIB, transcendentals=0
        ),
        name="rows",
    )(order, *held, jnp.asarray(perm), pick_src, pick_rec)


def combine(values, classes, outputs, origin, span, period):
    plain, scaled = [None] * outputs, [None] * outputs

    def add(into, k, value, sign):
        if into[k] is None:
            into[k] = value if sign > 0 else -value
        else:
            into[k] = into[k] + value if sign > 0 else into[k] - value

    for r, (real, imag) in enumerate(values):
        both = None
        for k in range(outputs):
            eighths = r * (span * k - origin) * 8 // period % 8
            assert r * (span * k - origin) * 8 % period == 0
            if eighths % 2 == 0:
                value, sign = ((real, 1), (imag, -1), (real, -1), (imag, 1))[eighths // 2]
                add(plain, k, value, sign)
            else:
                if both is None:
                    both = real + imag, real - imag
                value, sign = ((both[1], 1), (both[0], -1), (both[1], -1), (both[0], 1))[eighths // 2]
                add(scaled, k, value, sign)
    root = math.sqrt(0.5)
    return [a if b is None else a + root * b for a, b in zip(plain, scaled)]


def lags_kernel(geometry, place, weight, s_ref, r_ref, table, keep, send, lhs):
    classes, span, outputs, origin, period, chunk = geometry
    used, _, slots, _ = s_ref.shape
    lag_dev = keep.shape[-1]
    cores = 2
    for r in range(classes):
        bins = slice(r * LANES, (r + 1) * LANES)
        real = imag = None
        for u in range(used):
            sr, si = s_ref[u, 0, :, bins].astype(F32), s_ref[u, 1, :, bins].astype(F32)
            rr, ri = r_ref[0, u, 0, :, bins].astype(F32), r_ref[0, u, 1, :, bins].astype(F32)
            re, im = sr * rr + si * ri, si * rr - sr * ri
            if u:
                re, im = real + weight[u] * re, imag + weight[u] * im
            real, imag = re, im
        lhs[r, :slots, :LANES] = real.astype(BF16)
        lhs[r, :slots, LANES:] = imag.astype(BF16)
        lhs[r, slots:, :LANES] = imag.astype(BF16)
        lhs[r, slots:, LANES:] = (-real).astype(BF16)
    first = place[1] == 0
    for start in range(0, span, chunk):
        values = []
        for r in range(classes):
            y = jnp.dot(lhs[r], table[r, :, start : start + chunk], preferred_element_type=F32)
            values.append((y[:slots], y[slots:]))
        pieces = {}
        for k, value in enumerate(combine(values, classes, outputs, origin, span, period)):
            lag = span * k + start
            pieces[lag // (cores * lag_dev), lag // lag_dev % cores, lag % lag_dev] = value
        for (column, core, offset), value in pieces.items():
            lags = slice(offset, offset + chunk)

            @pl.when(place[1] == core)
            def _():
                keep[column, :, lags] = value

            @pl.when(place[1] != core)
            def _():
                send[column, :, lags] = value


def lag_parts(block, core, weight, rows, own, table, geometry, columns, lag_dev):
    classes, span, outputs, origin, period, chunk = geometry
    used, _, slots, part = rows.shape
    out = jax.ShapeDtypeStruct((columns, slots, lag_dev), F32)
    whole = lambda shape: pl.BlockSpec(shape, lambda i, place, weight: (0,) * len(shape))
    grid_spec = pltpu.PrefetchScalarGridSpec(
        num_scalar_prefetch=2,
        grid=(1,),
        in_specs=[
            whole(rows.shape),
            pl.BlockSpec((1,) + own.shape[1:], lambda i, place, weight: (place[0], 0, 0, 0, 0)),
            whole(table.shape),
        ],
        out_specs=[whole(out.shape)] * 2,
        scratch_shapes=[pltpu.VMEM((classes, 2 * slots, 2 * LANES), BF16)],
    )
    return pl.pallas_call(
        functools.partial(lags_kernel, geometry),
        grid_spec=grid_spec,
        out_shape=[out] * 2,
        compiler_params=pltpu.CompilerParams(vmem_limit_bytes=32 * MIB),
        cost_estimate=pl.CostEstimate(
            flops=8 * slots * part * span, bytes_accessed=8 * MIB, transcendentals=0
        ),
        name="lags",
    )(jnp.stack([block, core]).astype(jnp.int32), weight, rows, own, table)


def shards(spectra, window_keep, owners, pair_src, pair_rec, pair_count, observed):
    columns, cores, places = lax.axis_size("win"), lax.axis_size("freq"), lax.axis_size("recv")
    column, core, place = lax.axis_index("win"), lax.axis_index("freq"), lax.axis_index("recv")
    assert spectra.shape[0] == 1 and cores == 2
    channels, bins_dev = spectra.shape[2:]
    blocks, slots, lag_dev = observed.shape
    lag_total = lag_dev * columns * cores
    bin_total = bins_dev * cores
    period = 2 * bin_total
    part = bins_dev // columns
    classes = part // LANES
    span = period // classes
    geometry = (classes, span, lag_total // span, lag_total // 2, period, 256)
    lag_scale = 1.0 / math.sqrt(bin_total * columns)
    peers = columns * cores

    held = [
        shifted(
            lax.dynamic_slice(
                spectra[0], (0, 0, (column + s) % columns * part), (2, channels, part)
            ),
            "win",
            columns,
            s,
        )
        for s in range(columns)
    ]
    kept = window_keep[0]
    if columns == 2:
        order = (1 - kept)[None]
        weight = jnp.ones((1,), F32)
    else:
        keeps = jnp.stack([shifted(kept, "win", columns, s) for s in range(columns)])
        order = jnp.argsort(-keeps)[: columns - 1].astype(jnp.int32)
        weight = keeps[order].astype(F32)

    shifts = range(places)
    owns = [owners == (place - d) % places for d in shifts]
    unit_block = [jnp.argmax(o).astype(jnp.int32) for o in owns]
    wanted = [
        jnp.where(jnp.any(o), lax.dynamic_index_in_dim(pair_src, b, 0, False), -1)
        for o, b in zip(owns, unit_block)
    ]
    wanted = jnp.concatenate([shifted(x, "recv", places, -d) for d, x in zip(shifts, wanted)])
    channel_ids = jnp.arange(channels, dtype=jnp.int32)[None, :]
    pick_src = (wanted[:, None] == channel_ids).astype(BF16)
    pick_rec = (pair_rec.reshape(-1)[:, None] == channel_ids).astype(BF16)

    table = make_table(core * bins_dev + column * part, classes, span, period)
    *sent, own_rows = gather_rows(order, held, classes, pick_src, pick_rec, slots)
    arrived = [shifted(x, "recv", places, d) for d, x in zip(shifts, sent)]
    if places == blocks:
        units = list(zip(unit_block, arrived))
    else:
        stacked = jnp.stack(arrived)
        units = [
            (
                jnp.int32(b),
                lax.dynamic_index_in_dim(stacked, (place - owners[b]) % places, 0, False),
            )
            for b in range(blocks)
        ]

    def summed_lags(block, rows):
        keep, send = lag_parts(
            block, core, weight, rows, own_rows, table, geometry, columns, lag_dev
        )
        half = keep + shifted(send, "freq", cores, 1)
        total = lax.dynamic_index_in_dim(half, column, 0, False)
        for s in range(1, columns):
            out = lax.dynamic_index_in_dim(half, (column + s) % columns, 0, False)
            total = total + shifted(out.astype(BF16), "win", columns, s).astype(F32)
        return total

    normed = jnp.zeros_like(observed)
    gradients = []
    for block, rows in units:
        count = lax.dynamic_index_in_dim(pair_count, block, 0, False)
        valid = (jnp.arange(slots, dtype=jnp.int32) < count).astype(F32)[:, None]
        target = lax.dynamic_index_in_dim(observed, block, 0, False)
        corr = summed_lags(block, rows) * (lag_scale * valid)
        sums = jnp.stack([jnp.sum(corr * corr, axis=1), jnp.sum(corr * target, axis=1)])
        total = sums
        for s in range(1, peers):
            total = total + shifted(sums, ("win", "freq"), peers, s)
        square, product = total[0][:, None], total[1][:, None]
        scale_norm = jnp.sqrt(square / lag_total + EPSILON)
        unit_normed = corr / scale_norm
        bending = (square / (scale_norm * scale_norm) - product / scale_norm) / lag_total
        gradient = valid * (unit_normed - target - unit_normed * bending) / scale_norm
        gradients.append(gradient.astype(BF16))
        normed = lax.dynamic_update_slice(normed, unit_normed[None], (block, 0, 0))
    if places != blocks:
        stacked_gradients = jnp.stack(gradients)
        gradients = [
            lax.dynamic_index_in_dim(stacked_gradients, b, 0, False) for b in unit_block
        ]
    returned = jnp.concatenate([shifted(g, "recv", places, -d) for d, g in zip(shifts, gradients)])
    adjoint = lax.dot_general(
        pick_src, returned, (((0,), (0,)), ((), ())), preferred_element_type=F32
    )
    return (normed, adjoint)


def solution(mesh):
    return jax.shard_map(
        shards,
        mesh=mesh,
        in_specs=(
            P("win", None, ("groups", "recv"), "freq"),
            P(("groups", "win")),
            P("groups"),
            P(None, ("groups", "recv")),
            P(None, ("groups", "recv")),
            P(None, ("groups", "recv")),
            P(None, ("groups", "recv"), ("win", "freq")),
        ),
        out_specs=(
            P(None, ("groups", "recv"), ("win", "freq")),
            P(("groups", "recv"), ("win", "freq")),
        ),
        check_vma=False,
    )
```

time: 393 us -> 123 us (0.31); the launches traced: 386 us -> 122 us
  other arithmetic: 167 us -> 28.4 us
  matrix products: 61.9 us -> 1.13 us
  blocking collectives: 58.3 us -> 0 us
  starting transfers between devices: 0.67 us -> 33.3 us
  waiting for transfers between devices: 53.8 us -> 26.7 us
  local copies, waits for them, and re-layouts: 26.3 us -> 9.13 us
  Pallas kernels: 0 us -> 13.8 us
  between operations: 17.7 us -> 9.19 us
    another operation x5 -> x12, other arithmetic: 145 us -> 8.17 us  [the longest x4 5.39 us: shards(): unit_block = [jnp.argmax(o).astype(jnp.int32) for o in owns]]
    dot_general x6 -> x1, matrix products: 61.9 us -> 1.13 us  [shards(): lax.dot_general(pick_src, returned, (((0,), (0,)), ((), ())), preferred_e...]
    all_to_all x1 -> x0, blocking collectives: 52.6 us -> none  [shards(): lax.all_to_all(outgoing, 'recv', split_axis=0, concat_axis=0, tiled=True)]
    reduce_scatter x4 -> x0, waiting for transfers between devices: 46.1 us -> none  [to_lags(): lax.psum_scatter(terms, ('win', 'freq'), scatter_dimension=1, tiled=True)]
    ppermute x0 -> x30, starting transfers between devices: none -> 33.3 us  [shifted(): lax.ppermute(value, axis, [(i, (i + shift) % size) for i in range(size)])]
    ppermute x0 -> x30, waiting for transfers between devices: none -> 26.7 us  [shifted(): lax.ppermute(value, axis, [(i, (i + shift) % size) for i in range(size)])]
    gather x8 -> x0, local copies, waits for them, and re-layouts: 22.3 us -> none  [the longest x4 14.4 us: cross_rows(): jnp.take(source_block, pair_src[block_index], axis=2).astype(jnp.float32)]
    pallas_call x0 -> x6, Pallas kernels: none -> 13.8 us  [the longest x4 10.6 us: lag_parts(): pl.pallas_call(functools.partial(lags_kernel, geometry), grid_spec=grid_s...]
  transfers between devices with their start and end apart: 5 -> 30, of which waited for: 3 -> 5; matrix products, arithmetic and copies ran while one was open for 54% -> 18% of each run, Pallas kernels for 0% -> 10%
where the time goes in v1:
time: 123 us; the launch traced here: 122 us
  starting transfers between devices  33.3 us (27%)
  other arithmetic  28.4 us (23%)
  waiting for transfers between devices  26.7 us (22%)
  Pallas kernels  13.8 us (11%)
  between operations  9.19 us (7%)
  local copies, waits for them, and re-layouts  9.13 us (7%)
    ppermute x30, starting transfers between devices, shifted(): lax.ppermute(value, axis, [(i, (i + shift) % size) for i in range(size)])  33.3 us
    ppermute x30, waiting for transfers between devices, shifted(): lax.ppermute(value, axis, [(i, (i + shift) % size) for i in range(size)])  26.7 us
    pallas_call x4, Pallas kernels, lag_parts(): pl.pallas_call(functools.partial(lags_kernel, geometry), grid_spec=grid_s...  10.6 us
    another operation x4, other arithmetic, shards(): unit_block = [jnp.argmax(o).astype(jnp.int32) for o in owns]  5.39 us
    add x4, other arithmetic, summed_lags(): half = keep + shifted(send, 'freq', cores, 1)  4.16 us
    unnamed x18, local copies, waits for them, and re-layouts  3.82 us
    select_n x1, other arithmetic, shards(): jnp.where(jnp.any(o), lax.dynamic_index_in_dim(pair_src, b, 0, False), -1)  3.32 us
    convert_element_type x2, other arithmetic, shards(): valid = (jnp.arange(slots, dtype=jnp.int32) < count).astype(F32)[:, None]  3.1 us
  transfers between devices with their start and end apart: 30, of which 5 were waited for; matrix products, arithmetic and copies ran while one was open for 18% of the time, Pallas kernels for 10%

profile of v1, /device:TPU:0, one launch (start us, length us, event | category | flops | bytes accessed | tf_op | source)
XLA Modules:
  0.0 121.7 jit_solution(5166091013565543350)
XLA Ops:
  14.9 3.3 %fusion.46 = (s32[64]{0:T(128)S(1)}, s32[64]{0:T(128)S(1)}, s32[64]{0:T(128)S(1)}, s32[64]{0:T(128)S(1)}) fusion(pred[]{:T(512)} %get-tuple-element.44, s32[4,64]{1,0:T(4,128)} %param.13, s32[]{:T(128)S(6)} %select_n.152, s32[]{:T(128)S(6)} %select_n.157, pred[]{:T(512)} %get-tuple-element.45, s32[]{:T(128)S(6)} %select_n.167, pred[]{:T(512)} %get-tuple-element.46, ...), kind=kLoop, calls=%fused_computation.119 | loop fusion | flops 256 | bytes 2068 | tf_op jit(solution)/shard_map/jit(_where)/select_n | solution.py:234
  18.2 5.0 %collective-permute-start.1 = (s32[64]{0:T(128)S(1)}, s32[64]{0:T(128)S(1)}, u32[]{:S(2)}, u32[]{:S(2)}) collective-permute-start(s32[64]{0:T(128)S(1)} %get-tuple-element.57), channel_id=1, source_target_pairs={{0,12},{4,0},{8,4},{12,8},{1,13},{5,1},{9,5},{13,9},{2,14},{6,2},{... | collective-permute-start | bytes 776 | tf_op jit(solution)/shard_map/ppermute | solution.py:23
  25.6 1.6 %collective-permute-start = (bf16[2,128,1024]{2,1,0:T(8,128)(2,1)S(1)}, bf16[2,128,1024]{2,1,0:T(8,128)(2,1)S(1)}, u32[]{:S(2)}, u32[]{:S(2)}) collective-permute-start(bf16[2,128,1024]{2,1,0:T(8,128)(2,1)S(1)} %get-tuple-element.52), channel_id=1, source_target_pairs={{0,2},{2,0},{1,3},{3,1},{4,6},{6,4},{5,7},{7,5},{8,10},{10,8},{9,1... | collective-permute-start | bytes 1572872 | tf_op jit(solution)/shard_map/ppermute | solution.py:23
  29.1 1.5 %constant_dynamic-slice_fusion.1 = (s32[1,1]{0,1:T(1,128)}, s32[1,1]{0,1:T(1,128)}, s32[1,1]{0,1:T(1,128)}, s32[1,1]{0,1:T(1,128)}) fusion(s32[4,1]{0,1:T(1,128)} %param.15, s32[]{:T(128)S(6)} %select_n.162, s32[]{:T(128)S(6)} %select_n.157, s32[]{:T(128)S(6)} %select_n.152, s32[]{:T(128)S(6)} %select_n.167), kind=kLoop, calls=%fused_computation.81 | loop fusion | bytes 48 | tf_op jit(solution)/shard_map/jit(dynamic_index_in_dim)/dynamic_slice | solution.py:271
  33.4 5.0 %collective-permute-done.refs_1_ = bf16[2,128,1024]{2,1,0:T(8,128)(2,1)S(1)} collective-permute-done((bf16[2,128,1024]{2,1,0:T(8,128)(2,1)S(1)}, bf16[2,128,1024]{2,1,0:T(8,128)(2,1)S(1)}, u32[]{:S(2)}, u32[]{:S(2)}) %collective-permute-start) | collective-permute-done | bytes 524320 | tf_op jit(solution)/shard_map/ppermute | solution.py:23
  38.5 1.6 %copy-done.2 = bf16[1024,1024]{1,0:T(8,128)(2,1)S(1)} copy-done((bf16[1024,1024]{1,0:T(8,128)(2,1)S(1)}, bf16[1024,1024]{1,0:T(8,128)(2,1)}, u32[]{:S(2)}) %copy-start.2) | copy-done | bytes 2097176
  40.0 2.0 %rows.1 = (bf16[1,2,64,1024]{3,2,1,0:T(8,128)(2,1)S(1)}, bf16[1,2,64,1024]{3,2,1,0:T(8,128)(2,1)S(1)}, bf16[1,2,64,1024]{3,2,1,0:T(8,128)(2,1)S(1)}, bf16[1,2,64...) custom-call(s32[1]{0:T(128)S(6)} %sub.69.order, bf16[2,128,1024]{2,1,0:T(8,128)(2,1)S(1)} %get-tuple-element.53.refs_0_, ...), custom_call_target="tpu_custom_call" | custom-call | flops 805306368 | bytes 8388608 | tf_op jit(solution)/shard_map/rows/pallas_call | solution.py:86
  42.1 2.2 %collective-permute-start.15 = (bf16[1,2,64,1024]{3,2,1,0:T(8,128)(2,1)S(1)}, bf16[1,2,64,1024]{3,2,1,0:T(8,128)(2,1)S(1)}, u32[]{:S(2)}, u32[]{:S(2)}) collective-permute-start(bf16[1,2,64,1024]{3,2,1,0:T(8,128)(2,1)S(1)} %get-tuple-element.30), channel_id=1, source_target_pairs={{0,8},{4,12},{8,0},{12,4},{1,9},{5,13},{9,1},{13,5},{2,10},{6,14},... | collective-permute-start | bytes 786440 | tf_op jit(solution)/shard_map/ppermute | solution.py:23
  44.3 1.5 %collective-permute-start.9 = (bf16[1,2,64,1024]{3,2,1,0:T(8,128)(2,1)S(1)}, bf16[1,2,64,1024]{3,2,1,0:T(8,128)(2,1)S(1)}, u32[]{:S(2)}, u32[]{:S(2)}) collective-permute-start(bf16[1,2,64,1024]{3,2,1,0:T(8,128)(2,1)S(1)} %get-tuple-element.27), channel_id=1, source_target_pairs={{0,4},{4,8},{8,12},{12,0},{1,5},{5,9},{9,13},{13,1},{2,6},{6,10},{... | collective-permute-start | bytes 786440 | tf_op jit(solution)/shard_map/ppermute | solution.py:23
  47.7 2.3 %lags.4 = (f32[2,64,1024]{2,1,0:T(8,128)S(1)}, f32[2,64,1024]{2,1,0:T(8,128)S(1)}) custom-call(s32[2]{0:T(128)S(1)} %pad_add_fusion.1.place, f32[1]{0:T(128)} %constant.166.clone.1.weight, bf16[1,2,64,1024]{3,2,1,0:T(8,128)(2,1)S(1)} %get-tuple-element.23.s_ref, bf16[4,1,2,64,1024]{4,3,2,1,0:T(8,128)(2,1)S(1)} %get-tuple-element.24.r_ref, ...), custom_call_target="tpu_custom_call" | custom-call | flops 536870912 | bytes 8388608 | tf_op jit(solution)/shard_map/lags/pallas_call | solution.py:182
  50.1 2.4 %collective-permute-start.21 = (bf16[1,2,64,1024]{3,2,1,0:T(8,128)(2,1)}, bf16[1,2,64,1024]{3,2,1,0:T(8,128)(2,1)S(1)}, u32[]{:S(2)}, u32[]{:S(2)}) collective-permute-start(bf16[1,2,64,1024]{3,2,1,0:T(8,128)(2,1)} %get-tuple-element.33), channel_id=1, source_target_pairs={{0,12},{4,0},{8,4},{12,8},{1,13},{5,1},{9,5},{13,9},{2,14},{6,2},{... | collective-permute-start | bytes 786440 | tf_op jit(solution)/shard_map/ppermute | solution.py:23
  53.1 9.5 %collective-permute-done.15.s_ref = bf16[1,2,64,1024]{3,2,1,0:T(8,128)(2,1)S(1)} collective-permute-done((bf16[1,2,64,1024]{3,2,1,0:T(8,128)(2,1)S(1)}, bf16[1,2,64,1024]{3,2,1,0:T(8,128)(2,1)S(1)}, u32[]{:S(2)}, u32[]{:S(2)}) %collective-permute-start.15) | collective-permute-done | bytes 262176 | tf_op jit(solution)/shard_map/ppermute | solution.py:23
  62.6 3.1 %lags.6 = (f32[2,64,1024]{2,1,0:T(8,128)S(1)}, f32[2,64,1024]{2,1,0:T(8,128)}) custom-call(s32[2]{0:T(128)S(1)} %pad_add_fusion.3.place, f32[1]{0:T(128)} %constant.166.clone.1.weight, bf16[1,2,64,1024]{3,2,1,0:T(8,128)(2,1)S(1)} %collective-permute-done.15.s_ref, bf16[4,1,2,64,1024]{4,3,2,1,0:T(8,128)(2,1)S(1)} %get-tuple-element.24.r_ref, ...), custom_call_target="tpu_custom_call" | custom-call | flops 536870912 | bytes 8388608 | tf_op jit(solution)/shard_map/lags/pallas_call | solution.py:182
  65.7 3.1 %lags.5 = (f32[2,64,1024]{2,1,0:T(8,128)S(1)}, f32[2,64,1024]{2,1,0:T(8,128)}) custom-call(s32[2]{0:T(128)S(1)} %pad_add_fusion.2.place, f32[1]{0:T(128)} %constant.166.clone.1.weight, bf16[1,2,64,1024]{3,2,1,0:T(8,128)(2,1)S(1)} %collective-permute-done.9.s_ref, bf16[4,1,2,64,1024]{4,3,2,1,0:T(8,128)(2,1)S(1)} %get-tuple-element.24.r_ref, ...), custom_call_target="tpu_custom_call" | custom-call | flops 536870912 | bytes 8388608 | tf_op jit(solution)/shard_map/lags/pallas_call | solution.py:182
  69.9 2.2 %copy-done.1 = bf16[8,256,1024]{2,1,0:T(8,128)(2,1)S(1)} copy-done((bf16[8,256,1024]{2,1,0:T(8,128)(2,1)S(1)}, bf16[8,256,1024]{2,1,0:T(8,128)(2,1)}, u32[]{:S(2)}) %copy-start.1) | copy-done | bytes 4194328
  72.1 2.2 %lags.7 = (f32[2,64,1024]{2,1,0:T(8,128)S(1)}, f32[2,64,1024]{2,1,0:T(8,128)S(1)}) custom-call(s32[2]{0:T(128)S(1)} %pad_add_fusion.4.place, f32[1]{0:T(128)} %constant.166.clone.1.weight, bf16[1,2,64,1024]{3,2,1,0:T(8,128)(2,1)S(1)} %collective-permute-done.21.s_ref, bf16[4,1,2,64,1024]{4,3,2,1,0:T(8,128)(2,1)S(1)} %get-tuple-element.24.r_ref, ...), custom_call_target="tpu_custom_call" | custom-call | flops 536870912 | bytes 8388608 | tf_op jit(solution)/shard_map/lags/pallas_call | solution.py:182
  75.2 1.8 %compare_convert_fusion.1 = (f32[64]{0:T(128)}, f32[64]{0:T(128)}) fusion(s32[]{:T(128)} %bitcast.28, s32[]{:T(128)} %bitcast.19), kind=kLoop, calls=%fused_computation.92 | loop fusion | flops 256 | bytes 520 | tf_op jit(solution)/shard_map/convert_element_type | solution.py:272
  78.2 1.6 %collective-permute-start.5 = (bf16[64,1024]{1,0:T(8,128)(2,1)S(1)}, bf16[64,1024]{1,0:T(8,128)(2,1)S(1)}, u32[]{:S(2)}, u32[]{:S(2)}) collective-permute-start(bf16[64,1024]{1,0:T(8,128)(2,1)S(1)} %fusion.32), channel_id=1, source_target_pairs={{0,2},{2,0},{1,3},{3,1},{4,6},{6,4},{5,7},{7,5},{8,10},{10,8},{9,1... | collective-permute-start | bytes 393224 | tf_op jit(solution)/shard_map/ppermute | solution.py:23
  82.0 1.9 %add.238 = f32[2,64,1024]{2,1,0:T(8,128)} add(f32[2,64,1024]{2,1,0:T(8,128)S(1)} %get-tuple-element.28, f32[2,64,1024]{2,1,0:T(8,128)} %collective-permute-done.10) | non-fusion elementwise | flops 131072 | bytes 1572864 | tf_op jit(solution)/shard_map/add | solution.py:261
  84.9 1.6 %collective-permute-start.11 = (bf16[64,1024]{1,0:T(8,128)(2,1)S(1)}, bf16[64,1024]{1,0:T(8,128)(2,1)S(1)}, u32[]{:S(2)}, u32[]{:S(2)}) collective-permute-start(bf16[64,1024]{1,0:T(8,128)(2,1)S(1)} %fusion.33), channel_id=1, source_target_pairs={{0,2},{2,0},{1,3},{3,1},{4,6},{6,4},{5,7},{7,5},{8,10},{10,8},{9,1... | collective-permute-start | bytes 393224 | tf_op jit(solution)/shard_map/ppermute | solution.py:23
  89.0 2.3 %collective-permute-done.11 = bf16[64,1024]{1,0:T(8,128)(2,1)S(1)} collective-permute-done((bf16[64,1024]{1,0:T(8,128)(2,1)S(1)}, bf16[64,1024]{1,0:T(8,128)(2,1)S(1)}, u32[]{:S(2)}, u32[]{:S(2)}) %collective-permute-start.11) | collective-permute-done | bytes 131104 | tf_op jit(solution)/shard_map/ppermute | solution.py:23
  91.3 1.7 %collective-permute-done.23 = bf16[64,1024]{1,0:T(8,128)(2,1)S(1)} collective-permute-done((bf16[64,1024]{1,0:T(8,128)(2,1)S(1)}, bf16[64,1024]{1,0:T(8,128)(2,1)S(1)}, u32[]{:S(2)}, u32[]{:S(2)}) %collective-permute-start.23) | collective-permute-done | bytes 131104 | tf_op jit(solution)/shard_map/ppermute | solution.py:23
  93.1 1.4 %fusion.8 = (f32[64]{0:T(128)S(1)}, f32[64]{0:T(128)S(1)}, f32[64]{0:T(128)S(1)}, f32[64]{0:T(128)S(1)}, f32[64]{0:T(128)S(1)}, /*index=5*/f32[64]{0:T(128)S(1)}, f32[64]{0:T(128)S(1)}, f32[64]{0:T(128)S(1)}) fusion(f32[4,64,1024]{2,1,0:T(8,128)S(1)} %copy-done.5, s32[]{:T(128)S(6)} %select_n.167, f32[64]{0:T(128)S(1)} %compare_select_fusion, ...), kind=kLoop, calls=%fused_computation.13 | loop fusion | flops 1834496 | bytes 2624532 | tf_op jit(solution)/shard_map/reduce_sum | solution.py:275
  94.6 1.6 %collective-permute-start.19 = (f32[2,64]{1,0:T(2,128)S(1)}, f32[2,64]{1,0:T(2,128)S(1)}, u32[]{:S(2)}, u32[]{:S(2)}) collective-permute-start(f32[2,64]{1,0:T(2,128)S(1)} %pad_maximum_fusion.2), channel_id=1, source_target_pairs={{0,2},{1,3},{2,0},{3,1},{4,6},{5,7},{6,4},{7,5},{8,10},{9,11},{10,... | collective-permute-start | bytes 1544 | tf_op jit(solution)/shard_map/ppermute | solution.py:23
  96.1 1.4 %collective-permute-start.20 = (f32[2,64]{1,0:T(2,128)S(1)}, f32[2,64]{1,0:T(2,128)S(1)}, u32[]{:S(2)}, u32[]{:S(2)}) collective-permute-start(f32[2,64]{1,0:T(2,128)S(1)} %pad_maximum_fusion.2), channel_id=1, source_target_pairs={{0,3},{1,0},{2,1},{3,2},{4,7},{5,4},{6,5},{7,6},{8,11},{9,8},{10,9... | collective-permute-start | bytes 1544 | tf_op jit(solution)/shard_map/ppermute | solution.py:23
  98.2 1.4 %collective-permute-start.14 = (f32[2,64]{1,0:T(2,128)S(1)}, f32[2,64]{1,0:T(2,128)S(1)}, u32[]{:S(2)}, u32[]{:S(2)}) collective-permute-start(f32[2,64]{1,0:T(2,128)S(1)} %pad_maximum_fusion.1), channel_id=1, source_target_pairs={{0,3},{1,0},{2,1},{3,2},{4,7},{5,4},{6,5},{7,6},{8,11},{9,8},{10,9... | collective-permute-start | bytes 1544 | tf_op jit(solution)/shard_map/ppermute | solution.py:23
  99.6 1.6 %collective-permute-start.25 = (f32[2,64]{1,0:T(2,128)S(1)}, f32[2,64]{1,0:T(2,128)S(1)}, u32[]{:S(2)}, u32[]{:S(2)}) collective-permute-start(f32[2,64]{1,0:T(2,128)S(1)} %pad_maximum_fusion.3), channel_id=1, source_target_pairs={{0,2},{1,3},{2,0},{3,1},{4,6},{5,7},{6,4},{7,5},{8,10},{9,11},{10,... | collective-permute-start | bytes 1544 | tf_op jit(solution)/shard_map/ppermute | solution.py:23
  101.2 1.4 %collective-permute-start.26 = (f32[2,64]{1,0:T(2,128)S(1)}, f32[2,64]{1,0:T(2,128)S(1)}, u32[]{:S(2)}, u32[]{:S(2)}) collective-permute-start(f32[2,64]{1,0:T(2,128)S(1)} %pad_maximum_fusion.3), channel_id=1, source_target_pairs={{0,3},{1,0},{2,1},{3,2},{4,7},{5,4},{6,5},{7,6},{8,11},{9,8},{10,9... | collective-permute-start | bytes 1544 | tf_op jit(solution)/shard_map/ppermute | solution.py:23
  104.5 1.4 %collective-permute-start.8 = (f32[2,64]{1,0:T(2,128)S(1)}, f32[2,64]{1,0:T(2,128)S(1)}, u32[]{:S(2)}, u32[]{:S(2)}) collective-permute-start(f32[2,64]{1,0:T(2,128)S(1)} %pad_maximum_fusion), channel_id=1, source_target_pairs={{0,3},{1,0},{2,1},{3,2},{4,7},{5,4},{6,5},{7,6},{8,11},{9,8},{10,9... | collective-permute-start | bytes 1544 | tf_op jit(solution)/shard_map/ppermute | solution.py:23
  106.0 2.6 %collective-permute-start.28 = (bf16[64,1024]{1,0:T(8,128)(2,1)S(1)}, bf16[64,1024]{1,0:T(8,128)(2,1)S(1)}, u32[]{:S(2)}, u32[]{:S(2)}) collective-permute-start(bf16[64,1024]{1,0:T(8,128)(2,1)S(1)} %get-tuple-element.51), channel_id=1, source_target_pairs={{0,8},{4,12},{8,0},{12,4},{1,9},{5,13},{9,1},{13,5},{2,10},{6,14},... | collective-permute-start | bytes 393224 | tf_op jit(solution)/shard_map/ppermute | solution.py:23
  109.0 2.0 %collective-permute-start.29 = (bf16[64,1024]{1,0:T(8,128)(2,1)S(1)}, bf16[64,1024]{1,0:T(8,128)(2,1)S(1)}, u32[]{:S(2)}, u32[]{:S(2)}) collective-permute-start(bf16[64,1024]{1,0:T(8,128)(2,1)S(1)} %get-tuple-element.49), channel_id=1, source_target_pairs={{0,4},{4,8},{8,12},{12,0},{1,5},{5,9},{9,13},{13,1},{2,6},{6,10},{... | collective-permute-start | bytes 393224 | tf_op jit(solution)/shard_map/ppermute | solution.py:23
  112.5 8.0 %collective-permute-done.28 = bf16[64,1024]{1,0:T(8,128)(2,1)S(1)} collective-permute-done((bf16[64,1024]{1,0:T(8,128)(2,1)S(1)}, bf16[64,1024]{1,0:T(8,128)(2,1)S(1)}, u32[]{:S(2)}, u32[]{:S(2)}) %collective-permute-start.28) | collective-permute-done | bytes 131104 | tf_op jit(solution)/shard_map/ppermute | solution.py:23
  (105 shorter events, 30.2 us)
Async XLA Ops:
  0.6 45.8 %copy-start.3 = (f32[128,1024]{1,0:T(8,128)S(1)}, f32[128,1024]{1,0:T(8,128)}, u32[]{:S(2)}) copy-start(f32[128,1024]{1,0:T(8,128)} %constant.181.clone.base_cos) | copy-start | bytes 1572868
  0.6 45.8 %copy-start.4 = (f32[128,1024]{1,0:T(8,128)S(1)}, f32[128,1024]{1,0:T(8,128)}, u32[]{:S(2)}) copy-start(f32[128,1024]{1,0:T(8,128)} %constant.182.clone.base_sin) | copy-start | bytes 1572868
  18.2 15.0 %collective-permute-start.1 = (s32[64]{0:T(128)S(1)}, s32[64]{0:T(128)S(1)}, u32[]{:S(2)}, u32[]{:S(2)}) collective-permute-start(s32[64]{0:T(128)S(1)} %get-tuple-element.57), channel_id=1, source_target_pairs={{0,12},{4,0},{8,4},{12,8},{1,13},{5,1},{9,5},{13,9},{2,14},{6,2},{... | collective-permute-start | bytes 776 | tf_op jit(solution)/shard_map/ppermute | solution.py:23
  23.3 9.9 %collective-permute-start.2 = (s32[64]{0:T(128)S(1)}, s32[64]{0:T(128)S(1)}, u32[]{:S(2)}, u32[]{:S(2)}) collective-permute-start(s32[64]{0:T(128)S(1)} %get-tuple-element.59), channel_id=1, source_target_pairs={{0,8},{4,12},{8,0},{12,4},{1,9},{5,13},{9,1},{13,5},{2,10},{6,14},... | collective-permute-start | bytes 776 | tf_op jit(solution)/shard_map/ppermute | solution.py:23
  23.3 9.9 %collective-permute-start.3 = (s32[64]{0:T(128)S(1)}, s32[64]{0:T(128)S(1)}, u32[]{:S(2)}, u32[]{:S(2)}) collective-permute-start(s32[64]{0:T(128)S(1)} %get-tuple-element.58), channel_id=1, source_target_pairs={{0,4},{4,8},{8,12},{12,0},{1,5},{5,9},{9,13},{13,1},{2,6},{6,10},{... | collective-permute-start | bytes 776 | tf_op jit(solution)/shard_map/ppermute | solution.py:23
  25.6 12.9 %collective-permute-start = (bf16[2,128,1024]{2,1,0:T(8,128)(2,1)S(1)}, bf16[2,128,1024]{2,1,0:T(8,128)(2,1)S(1)}, u32[]{:S(2)}, u32[]{:S(2)}) collective-permute-start(bf16[2,128,1024]{2,1,0:T(8,128)(2,1)S(1)} %get-tuple-element.52), channel_id=1, source_target_pairs={{0,2},{2,0},{1,3},{3,1},{4,6},{6,4},{5,7},{7,5},{8,10},{10,8},{9,1... | collective-permute-start | bytes 1572872 | tf_op jit(solution)/shard_map/ppermute | solution.py:23
  42.1 20.5 %collective-permute-start.15 = (bf16[1,2,64,1024]{3,2,1,0:T(8,128)(2,1)S(1)}, bf16[1,2,64,1024]{3,2,1,0:T(8,128)(2,1)S(1)}, u32[]{:S(2)}, u32[]{:S(2)}) collective-permute-start(bf16[1,2,64,1024]{3,2,1,0:T(8,128)(2,1)S(1)} %get-tuple-element.30), channel_id=1, source_target_pairs={{0,8},{4,12},{8,0},{12,4},{1,9},{5,13},{9,1},{13,5},{2,10},{6,14},... | collective-permute-start | bytes 786440 | tf_op jit(solution)/shard_map/ppermute | solution.py:23
  44.3 21.4 %collective-permute-start.9 = (bf16[1,2,64,1024]{3,2,1,0:T(8,128)(2,1)S(1)}, bf16[1,2,64,1024]{3,2,1,0:T(8,128)(2,1)S(1)}, u32[]{:S(2)}, u32[]{:S(2)}) collective-permute-start(bf16[1,2,64,1024]{3,2,1,0:T(8,128)(2,1)S(1)} %get-tuple-element.27), channel_id=1, source_target_pairs={{0,4},{4,8},{8,12},{12,0},{1,5},{5,9},{9,13},{13,1},{2,6},{6,10},{... | collective-permute-start | bytes 786440 | tf_op jit(solution)/shard_map/ppermute | solution.py:23
  50.0 27.0 %collective-permute-start.4 = (f32[2,64,1024]{2,1,0:T(8,128)S(1)}, f32[2,64,1024]{2,1,0:T(8,128)}, u32[]{:S(2)}, u32[]{:S(2)}) collective-permute-start(f32[2,64,1024]{2,1,0:T(8,128)S(1)} %get-tuple-element.26), channel_id=1, source_target_pairs={{0,1},{1,0},{2,3},{3,2},{4,5},{5,4},{6,7},{7,6},{8,9},{9,8},{10,11... | collective-permute-start | bytes 1572872 | tf_op jit(solution)/shard_map/ppermute | solution.py:23
  50.1 19.9 %collective-permute-start.21 = (bf16[1,2,64,1024]{3,2,1,0:T(8,128)(2,1)}, bf16[1,2,64,1024]{3,2,1,0:T(8,128)(2,1)S(1)}, u32[]{:S(2)}, u32[]{:S(2)}) collective-permute-start(bf16[1,2,64,1024]{3,2,1,0:T(8,128)(2,1)} %get-tuple-element.33), channel_id=1, source_target_pairs={{0,12},{4,0},{8,4},{12,8},{1,13},{5,1},{9,5},{13,9},{2,14},{6,2},{... | collective-permute-start | bytes 786440 | tf_op jit(solution)/shard_map/ppermute | solution.py:23
  65.7 14.1 %collective-permute-start.16 = (f32[2,64,1024]{2,1,0:T(8,128)}, f32[2,64,1024]{2,1,0:T(8,128)}, u32[]{:S(2)}, u32[]{:S(2)}) collective-permute-start(f32[2,64,1024]{2,1,0:T(8,128)} %get-tuple-element.32), channel_id=1, source_target_pairs={{0,1},{1,0},{2,3},{3,2},{4,5},{5,4},{6,7},{7,6},{8,9},{9,8},{10,11... | collective-permute-start | bytes 1572872 | tf_op jit(solution)/shard_map/ppermute | solution.py:23
  68.7 13.3 %collective-permute-start.10 = (f32[2,64,1024]{2,1,0:T(8,128)}, f32[2,64,1024]{2,1,0:T(8,128)}, u32[]{:S(2)}, u32[]{:S(2)}) collective-permute-start(f32[2,64,1024]{2,1,0:T(8,128)} %get-tuple-element.29), channel_id=1, source_target_pairs={{0,1},{1,0},{2,3},{3,2},{4,5},{5,4},{6,7},{7,6},{8,9},{9,8},{10,11... | collective-permute-start | bytes 1572872 | tf_op jit(solution)/shard_map/ppermute | solution.py:23
  74.3 12.1 %collective-permute-start.22 = (f32[2,64,1024]{2,1,0:T(8,128)S(1)}, f32[2,64,1024]{2,1,0:T(8,128)S(1)}, u32[]{:S(2)}, u32[]{:S(2)}) collective-permute-start(f32[2,64,1024]{2,1,0:T(8,128)S(1)} %get-tuple-element.35), channel_id=1, source_target_pairs={{0,1},{1,0},{2,3},{3,2},{4,5},{5,4},{6,7},{7,6},{8,9},{9,8},{10,11... | collective-permute-start | bytes 1572872 | tf_op jit(solution)/shard_map/ppermute | solution.py:23
  78.2 10.8 %collective-permute-start.5 = (bf16[64,1024]{1,0:T(8,128)(2,1)S(1)}, bf16[64,1024]{1,0:T(8,128)(2,1)S(1)}, u32[]{:S(2)}, u32[]{:S(2)}) collective-permute-start(bf16[64,1024]{1,0:T(8,128)(2,1)S(1)} %fusion.32), channel_id=1, source_target_pairs={{0,2},{2,0},{1,3},{3,1},{4,6},{6,4},{5,7},{7,5},{8,10},{10,8},{9,1... | collective-permute-start | bytes 393224 | tf_op jit(solution)/shard_map/ppermute | solution.py:23
  81.5 7.5 %collective-permute-start.17 = (bf16[64,1024]{1,0:T(8,128)(2,1)}, bf16[64,1024]{1,0:T(8,128)(2,1)S(1)}, u32[]{:S(2)}, u32[]{:S(2)}) collective-permute-start(bf16[64,1024]{1,0:T(8,128)(2,1)} %fusion.34), channel_id=1, source_target_pairs={{0,2},{2,0},{1,3},{3,1},{4,6},{6,4},{5,7},{7,5},{8,10},{10,8},{9,1... | collective-permute-start | bytes 393224 | tf_op jit(solution)/shard_map/ppermute | solution.py:23
  84.9 6.4 %collective-permute-start.11 = (bf16[64,1024]{1,0:T(8,128)(2,1)S(1)}, bf16[64,1024]{1,0:T(8,128)(2,1)S(1)}, u32[]{:S(2)}, u32[]{:S(2)}) collective-permute-start(bf16[64,1024]{1,0:T(8,128)(2,1)S(1)} %fusion.33), channel_id=1, source_target_pairs={{0,2},{2,0},{1,3},{3,1},{4,6},{6,4},{5,7},{7,5},{8,10},{10,8},{9,1... | collective-permute-start | bytes 393224 | tf_op jit(solution)/shard_map/ppermute | solution.py:23
  86.6 6.5 %collective-permute-start.23 = (bf16[64,1024]{1,0:T(8,128)(2,1)S(1)}, bf16[64,1024]{1,0:T(8,128)(2,1)S(1)}, u32[]{:S(2)}, u32[]{:S(2)}) collective-permute-start(bf16[64,1024]{1,0:T(8,128)(2,1)S(1)} %fusion.35), channel_id=1, source_target_pairs={{0,2},{2,0},{1,3},{3,1},{4,6},{6,4},{5,7},{7,5},{8,10},{10,8},{9,1... | collective-permute-start | bytes 393224 | tf_op jit(solution)/shard_map/ppermute | solution.py:23
  94.5 3.6 %collective-permute-start.18 = (f32[2,64]{1,0:T(2,128)S(1)}, f32[2,64]{1,0:T(2,128)S(1)}, u32[]{:S(2)}, u32[]{:S(2)}) collective-permute-start(f32[2,64]{1,0:T(2,128)S(1)} %pad_maximum_fusion.2), channel_id=1, source_target_pairs={{0,1},{1,2},{2,3},{3,0},{4,5},{5,6},{6,7},{7,4},{8,9},{9,10},{10,1... | collective-permute-start | bytes 1544 | tf_op jit(solution)/shard_map/ppermute | solution.py:23
  94.6 5.0 %collective-permute-start.19 = (f32[2,64]{1,0:T(2,128)S(1)}, f32[2,64]{1,0:T(2,128)S(1)}, u32[]{:S(2)}, u32[]{:S(2)}) collective-permute-start(f32[2,64]{1,0:T(2,128)S(1)} %pad_maximum_fusion.2), channel_id=1, source_target_pairs={{0,2},{1,3},{2,0},{3,1},{4,6},{5,7},{6,4},{7,5},{8,10},{9,11},{10,... | collective-permute-start | bytes 1544 | tf_op jit(solution)/shard_map/ppermute | solution.py:23
  96.1 3.5 %collective-permute-start.20 = (f32[2,64]{1,0:T(2,128)S(1)}, f32[2,64]{1,0:T(2,128)S(1)}, u32[]{:S(2)}, u32[]{:S(2)}) collective-permute-start(f32[2,64]{1,0:T(2,128)S(1)} %pad_maximum_fusion.2), channel_id=1, source_target_pairs={{0,3},{1,0},{2,1},{3,2},{4,7},{5,4},{6,5},{7,6},{8,11},{9,8},{10,9... | collective-permute-start | bytes 1544 | tf_op jit(solution)/shard_map/ppermute | solution.py:23
  97.5 3.7 %collective-permute-start.12 = (f32[2,64]{1,0:T(2,128)S(1)}, f32[2,64]{1,0:T(2,128)S(1)}, u32[]{:S(2)}, u32[]{:S(2)}) collective-permute-start(f32[2,64]{1,0:T(2,128)S(1)} %pad_maximum_fusion.1), channel_id=1, source_target_pairs={{0,1},{1,2},{2,3},{3,0},{4,5},{5,6},{6,7},{7,4},{8,9},{9,10},{10,1... | collective-permute-start | bytes 1544 | tf_op jit(solution)/shard_map/ppermute | solution.py:23
  97.5 5.1 %collective-permute-start.13 = (f32[2,64]{1,0:T(2,128)S(1)}, f32[2,64]{1,0:T(2,128)S(1)}, u32[]{:S(2)}, u32[]{:S(2)}) collective-permute-start(f32[2,64]{1,0:T(2,128)S(1)} %pad_maximum_fusion.1), channel_id=1, source_target_pairs={{0,2},{1,3},{2,0},{3,1},{4,6},{5,7},{6,4},{7,5},{8,10},{9,11},{10,... | collective-permute-start | bytes 1544 | tf_op jit(solution)/shard_map/ppermute | solution.py:23
  98.2 4.5 %collective-permute-start.14 = (f32[2,64]{1,0:T(2,128)S(1)}, f32[2,64]{1,0:T(2,128)S(1)}, u32[]{:S(2)}, u32[]{:S(2)}) collective-permute-start(f32[2,64]{1,0:T(2,128)S(1)} %pad_maximum_fusion.1), channel_id=1, source_target_pairs={{0,3},{1,0},{2,1},{3,2},{4,7},{5,4},{6,5},{7,6},{8,11},{9,8},{10,9... | collective-permute-start | bytes 1544 | tf_op jit(solution)/shard_map/ppermute | solution.py:23
  99.6 4.9 %collective-permute-start.24 = (f32[2,64]{1,0:T(2,128)S(1)}, f32[2,64]{1,0:T(2,128)S(1)}, u32[]{:S(2)}, u32[]{:S(2)}) collective-permute-start(f32[2,64]{1,0:T(2,128)S(1)} %pad_maximum_fusion.3), channel_id=1, source_target_pairs={{0,1},{1,2},{2,3},{3,0},{4,5},{5,6},{6,7},{7,4},{8,9},{9,10},{10,1... | collective-permute-start | bytes 1544 | tf_op jit(solution)/shard_map/ppermute | solution.py:23
  99.6 6.4 %collective-permute-start.25 = (f32[2,64]{1,0:T(2,128)S(1)}, f32[2,64]{1,0:T(2,128)S(1)}, u32[]{:S(2)}, u32[]{:S(2)}) collective-permute-start(f32[2,64]{1,0:T(2,128)S(1)} %pad_maximum_fusion.3), channel_id=1, source_target_pairs={{0,2},{1,3},{2,0},{3,1},{4,6},{5,7},{6,4},{7,5},{8,10},{9,11},{10,... | collective-permute-start | bytes 1544 | tf_op jit(solution)/shard_map/ppermute | solution.py:23
  101.2 4.8 %collective-permute-start.26 = (f32[2,64]{1,0:T(2,128)S(1)}, f32[2,64]{1,0:T(2,128)S(1)}, u32[]{:S(2)}, u32[]{:S(2)}) collective-permute-start(f32[2,64]{1,0:T(2,128)S(1)} %pad_maximum_fusion.3), channel_id=1, source_target_pairs={{0,3},{1,0},{2,1},{3,2},{4,7},{5,4},{6,5},{7,6},{8,11},{9,8},{10,9... | collective-permute-start | bytes 1544 | tf_op jit(solution)/shard_map/ppermute | solution.py:23
  102.7 6.0 %collective-permute-start.6 = (f32[2,64]{1,0:T(2,128)S(1)}, f32[2,64]{1,0:T(2,128)S(1)}, u32[]{:S(2)}, u32[]{:S(2)}) collective-permute-start(f32[2,64]{1,0:T(2,128)S(1)} %pad_maximum_fusion), channel_id=1, source_target_pairs={{0,1},{1,2},{2,3},{3,0},{4,5},{5,6},{6,7},{7,4},{8,9},{9,10},{10,1... | collective-permute-start | bytes 1544 | tf_op jit(solution)/shard_map/ppermute | solution.py:23
  102.7 6.0 %collective-permute-start.7 = (f32[2,64]{1,0:T(2,128)S(1)}, f32[2,64]{1,0:T(2,128)S(1)}, u32[]{:S(2)}, u32[]{:S(2)}) collective-permute-start(f32[2,64]{1,0:T(2,128)S(1)} %pad_maximum_fusion), channel_id=1, source_target_pairs={{0,2},{1,3},{2,0},{3,1},{4,6},{5,7},{6,4},{7,5},{8,10},{9,11},{10,... | collective-permute-start | bytes 1544 | tf_op jit(solution)/shard_map/ppermute | solution.py:23
  104.5 4.1 %collective-permute-start.8 = (f32[2,64]{1,0:T(2,128)S(1)}, f32[2,64]{1,0:T(2,128)S(1)}, u32[]{:S(2)}, u32[]{:S(2)}) collective-permute-start(f32[2,64]{1,0:T(2,128)S(1)} %pad_maximum_fusion), channel_id=1, source_target_pairs={{0,3},{1,0},{2,1},{3,2},{4,7},{5,4},{6,5},{7,6},{8,11},{9,8},{10,9... | collective-permute-start | bytes 1544 | tf_op jit(solution)/shard_map/ppermute | solution.py:23
  106.0 6.5 %collective-permute-start.27 = (bf16[64,1024]{1,0:T(8,128)(2,1)S(1)}, bf16[64,1024]{1,0:T(8,128)(2,1)S(1)}, u32[]{:S(2)}, u32[]{:S(2)}) collective-permute-start(bf16[64,1024]{1,0:T(8,128)(2,1)S(1)} %get-tuple-element.50), channel_id=1, source_target_pairs={{0,12},{4,0},{8,4},{12,8},{1,13},{5,1},{9,5},{13,9},{2,14},{6,2},{... | collective-permute-start | bytes 393224 | tf_op jit(solution)/shard_map/ppermute | solution.py:23
  106.0 14.5 %collective-permute-start.28 = (bf16[64,1024]{1,0:T(8,128)(2,1)S(1)}, bf16[64,1024]{1,0:T(8,128)(2,1)S(1)}, u32[]{:S(2)}, u32[]{:S(2)}) collective-permute-start(bf16[64,1024]{1,0:T(8,128)(2,1)S(1)} %get-tuple-element.51), channel_id=1, source_target_pairs={{0,8},{4,12},{8,0},{12,4},{1,9},{5,13},{9,1},{13,5},{2,10},{6,14},... | collective-permute-start | bytes 393224 | tf_op jit(solution)/shard_map/ppermute | solution.py:23
  109.0 11.6 %collective-permute-start.29 = (bf16[64,1024]{1,0:T(8,128)(2,1)S(1)}, bf16[64,1024]{1,0:T(8,128)(2,1)S(1)}, u32[]{:S(2)}, u32[]{:S(2)}) collective-permute-start(bf16[64,1024]{1,0:T(8,128)(2,1)S(1)} %get-tuple-element.49), channel_id=1, source_target_pairs={{0,4},{4,8},{8,12},{12,0},{1,5},{5,9},{9,13},{13,1},{2,6},{6,10},{... | collective-permute-start | bytes 393224 | tf_op jit(solution)/shard_map/ppermute | solution.py:23
  (7 other events, 91.6 us)

commit v2 on v1

v2 whole, which is shorter than its diff:
```python
import functools
import math

import jax
import jax.numpy as jnp
import ml_dtypes
import numpy as np
from jax import lax
from jax.experimental import pallas as pl
from jax.experimental.pallas import tpu as pltpu
from jax.sharding import PartitionSpec as P

EPSILON = 1e-06
MIB = 1 << 20
LANES = 128
CHUNKS = 2
CORE, COLUMN, ORDER, BLOCK, COUNT = 0, 1, 2, 8, 16
BF16 = jnp.bfloat16
F32 = jnp.float32
VMEM = pl.BlockSpec(memory_space=pltpu.VMEM)
SMEM = pl.BlockSpec(memory_space=pltpu.SMEM)


def shifted(value, axis, size, shift):
    if shift % size == 0:
        return value
    return lax.ppermute(value, axis, [(i, (i + shift) % size) for i in range(size)])


def params(mib):
    return pltpu.CompilerParams(vmem_limit_bytes=mib * MIB)


def cost(flops, mib):
    return pl.CostEstimate(flops=int(flops), bytes_accessed=int(mib * MIB), transcendentals=0)


def table_kernel(row_cos, row_sin, base_cos, base_sin, table):
    ca, sa = row_cos[0], row_sin[0]
    cb, sb = base_cos[...], base_sin[...]
    table[0, :LANES] = (ca * cb - sa * sb).astype(BF16)
    table[0, LANES:] = (-(sa * cb + ca * sb)).astype(BF16)


def make_table(first_bin, classes, span, period):
    m = np.arange(LANES, dtype=np.int64)[:, None]
    u = np.arange(span, dtype=np.int64)[None, :]
    base = (classes * m * u % period) * (2.0 * math.pi / period)
    base_cos, base_sin = np.cos(base).astype(np.float32), np.sin(base).astype(np.float32)
    frequency = first_bin + jnp.arange(classes, dtype=jnp.int32)
    turns = frequency[:, None] * jnp.arange(span, dtype=jnp.int32)[None, :] % period
    angles = turns.astype(F32) * (2.0 * math.pi / period)
    row_cos, row_sin = jnp.cos(angles)[:, None, :], jnp.sin(angles)[:, None, :]
    row = pl.BlockSpec((1, 1, span), lambda r: (r, 0, 0))
    whole = pl.BlockSpec((LANES, span), lambda r: (0, 0))
    return pl.pallas_call(
        table_kernel,
        grid=(classes,),
        out_shape=jax.ShapeDtypeStruct((classes, 2 * LANES, span), BF16),
        in_specs=[row, row, whole, whole],
        out_specs=pl.BlockSpec((1, 2 * LANES, span), lambda r: (r, 0, 0)),
        compiler_params=params(16),
        cost_estimate=cost(6 * classes * LANES * span, 6),
        name="table",
    )(row_cos, row_sin, jnp.asarray(base_cos), jnp.asarray(base_sin))


def picks(ids, channels):
    row = jnp.concatenate([i[...] for i in ids], axis=1)
    return (lax.broadcasted_iota(jnp.int32, (channels, row.shape[1]), 0) == row).astype(BF16)


def rows_kernel(used, sends, scal, *refs):
    shifts = used + 1
    held, refs = refs[:shifts], refs[shifts:]
    perm, src_ids, rec_ids, outs = refs[0], refs[1 : 1 + sends], refs[1 + sends], refs[2 + sends :]
    rows_out, own_out = outs[: sends * CHUNKS], outs[sends * CHUNKS :]
    units, _, _, slots, _ = own_out[0].shape
    channels = held[0].shape[1]
    pick = picks(
        list(src_ids) + [rec_ids.at[d : d + 1] for d in range(units)], channels
    )
    for u in range(used):
        for half in range(2):
            x = held[0][half]
            for s in range(1, shifts):
                x = jnp.where(scal[ORDER + u] == s, held[s][half], x)
            x = jnp.dot(x, perm[...], preferred_element_type=F32).astype(BF16)
            y = lax.dot_general(
                pick, x, (((0,), (0,)), ((), ())), preferred_element_type=F32
            ).astype(BF16)
            for i, out in enumerate(rows_out):
                out[u, half] = y[i * slots : (i + 1) * slots]
            y = y[sends * CHUNKS * slots :]
            for d in range(units):
                for q, out in enumerate(own_out):
                    first = (d * CHUNKS + q) * slots
                    out[d, u, half] = y[first : first + slots]


def gather_rows(scal, held, classes, src_ids, rec_ids, units, slots):
    used, sends = len(held) - 1, len(src_ids)
    part = held[0].shape[-1]
    source = np.arange(part)
    perm = np.zeros((part, part), ml_dtypes.bfloat16)
    perm[source, source % classes * LANES + source // classes] = 1
    sent = jax.ShapeDtypeStruct((used, 2, slots, part), BF16)
    own = jax.ShapeDtypeStruct((units, used, 2, slots, part), BF16)
    outs = pl.pallas_call(
        functools.partial(rows_kernel, used, sends),
        out_shape=[sent] * (sends * CHUNKS) + [own] * CHUNKS,
        in_specs=[SMEM] + [VMEM] * (len(held) + 2 + sends),
        out_specs=[VMEM] * ((sends + 1) * CHUNKS),
        compiler_params=params(32),
        cost_estimate=cost(4 * used * part * (128 * part + 512 * 128), 6),
        name="rows",
    )(scal, *held, jnp.asarray(perm), *src_ids, rec_ids)
    sends_of = [outs[q : sends * CHUNKS : CHUNKS] for q in range(CHUNKS)]
    return sends_of, outs[sends * CHUNKS :]


def combine(values, classes, outputs, origin, span, period):
    plain, scaled = [None] * outputs, [None] * outputs

    def add(into, k, value, sign):
        if into[k] is None:
            into[k] = value if sign > 0 else -value
        else:
            into[k] = into[k] + value if sign > 0 else into[k] - value

    for r, (real, imag) in enumerate(values):
        both = None
        for k in range(outputs):
            eighths = r * (span * k - origin) * 8 // period % 8
            assert r * (span * k - origin) * 8 % period == 0
            if eighths % 2 == 0:
                value, sign = ((real, 1), (imag, -1), (real, -1), (imag, 1))[eighths // 2]
                add(plain, k, value, sign)
            else:
                if both is None:
                    both = real + imag, real - imag
                value, sign = ((both[1], 1), (both[0], -1), (both[1], -1), (both[0], 1))[eighths // 2]
                add(scaled, k, value, sign)
    root = math.sqrt(0.5)
    return [a if b is None else a + root * b for a, b in zip(plain, scaled)]


def lags_kernel(geometry, units, scal, weight, *refs):
    classes, span, outputs, origin, period, chunk = geometry
    s_refs, (r_ref, table, keep, send, lhs) = refs[:units], refs[units:]
    used, _, slots, _ = s_refs[0].shape
    rows = units * slots
    lag_dev = keep.shape[-1]
    cores = 2
    for d in range(units):
        at = slice(d * slots, (d + 1) * slots)
        turned = slice(rows + d * slots, rows + (d + 1) * slots)
        for r in range(classes):
            bins = slice(r * LANES, (r + 1) * LANES)
            real = imag = None
            for u in range(used):
                sr, si = s_refs[d][u, 0, :, bins].astype(F32), s_refs[d][u, 1, :, bins].astype(F32)
                rr, ri = r_ref[d, u, 0, :, bins].astype(F32), r_ref[d, u, 1, :, bins].astype(F32)
                re, im = sr * rr + si * ri, si * rr - sr * ri
                if u:
                    re, im = real + weight[u] * re, imag + weight[u] * im
                real, imag = re, im
            lhs[r, at, :LANES] = real.astype(BF16)
            lhs[r, at, LANES:] = imag.astype(BF16)
            lhs[r, turned, :LANES] = imag.astype(BF16)
            lhs[r, turned, LANES:] = (-real).astype(BF16)
    for start in range(0, span, chunk):
        values = []
        for r in range(classes):
            y = jnp.dot(lhs[r], table[r, :, start : start + chunk], preferred_element_type=F32)
            values.append((y[:rows], y[rows:]))
        for k, value in enumerate(combine(values, classes, outputs, origin, span, period)):
            lag = span * k + start
            column, core, offset = lag // (cores * lag_dev), lag // lag_dev % cores, lag % lag_dev
            lags = slice(offset, offset + chunk)

            @pl.when(scal[CORE] == core)
            def _():
                keep[column, :, lags] = value

            @pl.when(scal[CORE] != core)
            def _():
                send[column, :, lags] = value


def lag_parts(scal, weight, rows, own, table, geometry, columns, lag_dev):
    classes, span = geometry[:2]
    units = len(rows)
    used, _, slots, part = rows[0].shape
    out = jax.ShapeDtypeStruct((columns, units * slots, lag_dev), F32)
    return pl.pallas_call(
        functools.partial(lags_kernel, geometry, units),
        out_shape=[out] * 2,
        in_specs=[SMEM, SMEM] + [VMEM] * (units + 2),
        out_specs=[VMEM] * 2,
        scratch_shapes=[pltpu.VMEM((classes, 2 * units * slots, 2 * LANES), BF16)],
        compiler_params=params(32),
        cost_estimate=cost(8 * units * slots * part * span, 8),
        name="lags",
    )(scal, weight, *rows, own, table)


def stats_kernel(scale, chunk, units, others, scal, *refs):
    own, more, refs = refs[0], refs[1 : 1 + others], refs[1 + others :]
    targets, (corr, sums) = refs[:units], refs[units:]
    slots = targets[0].shape[1]
    columns = []
    for d in range(units):
        at = slice(d * slots, (d + 1) * slots)
        value = own[at]
        for m in more:
            value = value + m[at].astype(F32)
        slot = chunk * slots + lax.broadcasted_iota(jnp.int32, (slots, 1), 0)
        value = value * jnp.where(slot < scal[COUNT + d], scale, 0.0)
        corr[at] = value
        square = jnp.sum(value * value, axis=1, keepdims=True)
        product = jnp.sum(value * targets[d][0], axis=1, keepdims=True)
        lane = lax.broadcasted_iota(jnp.int32, (slots, LANES), 1)
        columns.append(jnp.where(lane == 0, square, jnp.where(lane == 1, product, 0.0)))
    sums[...] = jnp.concatenate(columns, axis=0).T[:8]


def target_specs(chunk, units, slots, lag_dev):
    return [
        pl.BlockSpec((1, slots, lag_dev), lambda i, scal, d=d: (scal[BLOCK + d], chunk, 0))
        for d in range(units)
    ]


def whole(shape):
    return pl.BlockSpec(shape, lambda i, scal: (0,) * len(shape))


def lag_stats(scal, scale, chunk, own, more, observed, units, slots):
    rows, lag_dev = own.shape
    outs = [jax.ShapeDtypeStruct((rows, lag_dev), F32), jax.ShapeDtypeStruct((8, rows), F32)]
    return pl.pallas_call(
        functools.partial(stats_kernel, scale, chunk, units, len(more)),
        grid_spec=pltpu.PrefetchScalarGridSpec(
            num_scalar_prefetch=1,
            grid=(1,),
            in_specs=[whole(own.shape)] * (1 + len(more))
            + target_specs(chunk, units, slots, lag_dev),
            out_specs=[whole(o.shape) for o in outs],
        ),
        out_shape=outs,
        compiler_params=params(16),
        cost_estimate=cost(8 * rows * lag_dev, 2),
        name="stats",
    )(scal, own, *more, *[observed] * units)


def slot_scales(sums, lag_total):
    total = sums[0][...]
    for s in sums[1:]:
        total = total + s[...]
    rows = total.shape[1]
    square, product = total[0:1], total[1:2]
    inverse = 1.0 / jnp.sqrt(square / lag_total + EPSILON)
    bending = (square * inverse * inverse - product * inverse) / lag_total
    sub = lax.broadcasted_iota(jnp.int32, (LANES, rows), 0)
    both = jnp.where(sub == 0, inverse, jnp.where(sub == 1, bending, 0.0)).T
    return both[:, 0:1], both[:, 1:2]


def gradient_kernel(lag_total, chunk, units, parts, scal, *refs):
    sums, corr, refs = refs[:parts], refs[parts], refs[parts + 1 :]
    targets, outs = refs[:units], refs[units:]
    slots = targets[0].shape[1]
    inverse, bending = slot_scales(sums, lag_total)
    for d in range(units):
        at = slice(d * slots, (d + 1) * slots)
        slot = chunk * slots + lax.broadcasted_iota(jnp.int32, (slots, 1), 0)
        valid = jnp.where(slot < scal[COUNT + d], inverse[at], 0.0)
        normed = corr[at] * inverse[at]
        gradient = (normed - targets[d][0] - normed * bending[at]) * valid
        outs[d][...] = gradient.astype(BF16)


def gradients(scal, lag_total, chunk, sums, corr, observed, units, slots):
    rows, lag_dev = corr.shape
    out = jax.ShapeDtypeStruct((slots, lag_dev), BF16)
    return pl.pallas_call(
        functools.partial(gradient_kernel, lag_total, chunk, units, len(sums)),
        grid_spec=pltpu.PrefetchScalarGridSpec(
            num_scalar_prefetch=1,
            grid=(1,),
            in_specs=[whole(sums[0].shape)] * len(sums)
            + [whole(corr.shape)]
            + target_specs(chunk, units, slots, lag_dev),
            out_specs=[whole(out.shape)] * units,
        ),
        out_shape=[out] * units,
        compiler_params=params(16),
        cost_estimate=cost(8 * rows * lag_dev, 1),
        name="gradient",
    )(scal, *sums, corr, *[observed] * units)


def normed_kernel(lag_total, parts, scal, *refs):
    out = refs[-1]
    slots = out.shape[1] // CHUNKS
    d = pl.program_id(0)
    for q in range(CHUNKS):
        sums, corr = refs[q * (parts + 1) : q * (parts + 1) + parts], refs[q * (parts + 1) + parts]
        inverse, _ = slot_scales(sums, lag_total)
        mine = inverse[0:slots]
        for i in range(1, inverse.shape[0] // slots):
            mine = jnp.where(d == i, inverse[i * slots : (i + 1) * slots], mine)
        out[0, q * slots : (q + 1) * slots] = corr[...] * mine


def normed_rows(scal, lag_total, sums, corr, observed, units, slots):
    lag_dev = corr[0].shape[1]
    ins, specs = [], []
    for s, c in zip(sums, corr):
        ins += [*s, c]
        specs += [whole(s[0].shape)] * len(s)
        specs += [pl.BlockSpec((slots, lag_dev), lambda i, scal: (i, 0))]
    return pl.pallas_call(
        functools.partial(normed_kernel, lag_total, len(sums[0])),
        grid_spec=pltpu.PrefetchScalarGridSpec(
            num_scalar_prefetch=1,
            grid=(units,),
            in_specs=specs,
            out_specs=pl.BlockSpec(
                (1, CHUNKS * slots, lag_dev), lambda i, scal: (scal[BLOCK + i], 0, 0)
            ),
        ),
        out_shape=jax.ShapeDtypeStruct(observed.shape, F32),
        compiler_params=params(16),
        cost_estimate=cost(2 * observed.size, 2),
        name="normed",
    )(scal, *ins)


def adjoint_kernel(sends, *refs):
    ids, parts, out = refs[:sends], refs[sends:-1], refs[-1]
    pick = picks(ids, out.shape[0])
    rows = jnp.concatenate([p[...] for p in parts], axis=0)
    out[...] = jnp.dot(pick, rows, preferred_element_type=F32)


def adjoint_rows(src_ids, parts, channels):
    lag_dev = parts[0].shape[1]
    return pl.pallas_call(
        functools.partial(adjoint_kernel, len(src_ids)),
        out_shape=jax.ShapeDtypeStruct((channels, lag_dev), F32),
        in_specs=[VMEM] * (len(src_ids) + len(parts)),
        out_specs=VMEM,
        compiler_params=params(16),
        cost_estimate=cost(2 * channels * lag_dev * 256, 1),
        name="adjoint",
    )(*src_ids, *parts)


def shards(spectra, window_keep, owners, pair_src, pair_rec, pair_count, observed):
    columns, cores, places = lax.axis_size("win"), lax.axis_size("freq"), lax.axis_size("recv")
    column, core, place = lax.axis_index("win"), lax.axis_index("freq"), lax.axis_index("recv")
    assert spectra.shape[0] == 1 and cores == 2
    channels, bins_dev = spectra.shape[2:]
    blocks, slots, lag_dev = observed.shape
    lag_total = lag_dev * columns * cores
    bin_total = bins_dev * cores
    period = 2 * bin_total
    part = bins_dev // columns
    classes = part // LANES
    span = period // classes
    geometry = (classes, span, lag_total // span, lag_total // 2, period, 256)
    lag_scale = 1.0 / math.sqrt(bin_total * columns)
    peers = columns * cores
    some = slots // CHUNKS
    shifts = range(places)

    held = [
        shifted(
            lax.dynamic_slice(
                spectra[0], (0, 0, (column + s) % columns * part), (2, channels, part)
            ),
            "win",
            columns,
            s,
        )
        for s in range(columns)
    ]
    kept = window_keep[0]
    if columns == 2:
        order = [1 - kept]
        weight = jnp.ones((1,), F32)
    else:
        keeps = jnp.stack([shifted(kept, "win", columns, s) for s in range(columns)])
        ranked = jnp.argsort(-keeps)[: columns - 1].astype(jnp.int32)
        order = [ranked[u] for u in range(columns - 1)]
        weight = keeps[ranked].astype(F32)

    direct = places == blocks
    lane = jnp.arange(LANES, dtype=jnp.int32)
    scal = jnp.where(lane == CORE, core, jnp.where(lane == COLUMN, column, 0))
    for u, o in enumerate(order):
        scal = jnp.where(lane == ORDER + u, o, scal)
    for b in range(blocks):
        unit = (place - owners[b]) % places if direct else b
        scal = jnp.where(lane == BLOCK + unit, b, scal)
        scal = jnp.where(lane == COUNT + unit, pair_count[b, 0], scal)

    def rows_of(ids, d):
        chosen = jnp.full((1, slots), -1, jnp.int32)
        for b in range(blocks):
            chosen = jnp.where(owners[b] == (place - d) % places, ids[b : b + 1], chosen)
        return chosen

    src_ids = [shifted(rows_of(pair_src, d), "recv", places, -d) for d in shifts]
    if direct:
        rec_ids = jnp.concatenate([rows_of(pair_rec, d) for d in shifts], axis=0)
    else:
        rec_ids = pair_rec

    table = make_table(core * bins_dev + column * part, classes, span, period)
    sends, own_rows = gather_rows(scal, held, classes, src_ids, rec_ids, blocks, some)
    corrs, all_sums, returned = [], [], [[] for _ in shifts]
    arrived = [[shifted(x, "recv", places, d) for d, x in zip(shifts, sent)] for sent in sends]
    for q in range(CHUNKS):
        rows = arrived[q]
        if not direct:
            stacked = jnp.stack(rows)
            rows = [
                lax.dynamic_index_in_dim(stacked, (place - owners[b]) % places, 0, False)
                for b in range(blocks)
            ]
        keep, send = lag_parts(scal, weight, rows, own_rows[q], table, geometry, columns, lag_dev)
        half = keep + shifted(send, "freq", cores, 1)
        own = lax.dynamic_index_in_dim(half, column, 0, False)
        more = [
            shifted(
                lax.dynamic_index_in_dim(half, (column + s) % columns, 0, False).astype(BF16),
                "win",
                columns,
                s,
            )
            for s in range(1, columns)
        ]
        corr, sums = lag_stats(scal, lag_scale, q, own, more, observed, blocks, some)
        sums = [shifted(sums, ("win", "freq"), peers, s) for s in range(peers)]
        grads = gradients(scal, lag_total, q, sums, corr, observed, blocks, some)
        if not direct:
            stacked = jnp.stack(list(grads) + [jnp.zeros_like(grads[0])])
            grads = []
            for d in shifts:
                block = jnp.int32(blocks)
                for b in range(blocks):
                    block = jnp.where(owners[b] == (place - d) % places, b, block)
                grads.append(lax.dynamic_index_in_dim(stacked, block, 0, False))
        for d, g in zip(shifts, grads):
            returned[d].append(shifted(g, "recv", places, -d))
        corrs.append(corr)
        all_sums.append(sums)
    normed = normed_rows(scal, lag_total, all_sums, corrs, observed, blocks, some)
    adjoint = adjoint_rows(src_ids, [g for unit in returned for g in unit], channels)
    return (normed, adjoint)


def solution(mesh):
    return jax.shard_map(
        shards,
        mesh=mesh,
        in_specs=(
            P("win", None, ("groups", "recv"), "freq"),
            P(("groups", "win")),
            P("groups"),
            P(None, ("groups", "recv")),
            P(None, ("groups", "recv")),
            P(None, ("groups", "recv")),
            P(None, ("groups", "recv"), ("win", "freq")),
        ),
        out_specs=(
            P(None, ("groups", "recv"), ("win", "freq")),
            P(("groups", "recv"), ("win", "freq")),
        ),
        check_vma=False,
    )
```

time: 123 us -> 105 us (0.85)
  other arithmetic: 28.4 us -> 10.6 us
  between operations: 9.19 us -> 14 us
  waiting for transfers between devices: 26.7 us -> 22.5 us
  Pallas kernels: 13.8 us -> 17 us
  starting transfers between devices: 33.3 us -> 31.3 us
    another operation x12 -> x0, other arithmetic: 8.17 us -> none  [the longest x4 5.39 us: shards(): unit_block = [jnp.argmax(o).astype(jnp.int32) for o in owns]]
    convert_element_type x6 -> x0, other arithmetic: 4.77 us -> none  [the longest x2 3.1 us: shards(): valid = (jnp.arange(slots, dtype=jnp.int32) < count).astype(F32)[:, None]]
    ppermute x30 -> x26, waiting for transfers between devices: 26.7 us -> 22.5 us  [shifted(): lax.ppermute(value, axis, [(i, (i + shift) % size) for i in range(size)])]
    pallas_call x5 -> x9, Pallas kernels: 12.6 us -> 15.8 us  [the longest x2 7.09 us: lag_parts(): pl.pallas_call(functools.partial(lags_kernel, geometry, units), out_shape...]
    slice x0 -> x2, local copies, waits for them, and re-layouts: none -> 2.91 us  [the longest x1 1.46 us: shards(): unit = (place - owners[b]) % places if direct else b]
    mul x3 -> x0, other arithmetic: 2.58 us -> none  [shards(): corr = summed_lags(block, rows) * (lag_scale * valid)]
    select_n x1 -> x5, other arithmetic: 3.32 us -> 5.74 us  [the longest x4 3.36 us: rows_of(): chosen = jnp.where(owners[b] == (place - d) % places, ids[b:b + 1], chosen)]
    ppermute x30 -> x26, starting transfers between devices: 33.3 us -> 31.3 us  [shifted(): lax.ppermute(value, axis, [(i, (i + shift) % size) for i in range(size)])]
  transfers between devices with their start and end apart: 30 -> 26, of which waited for: 5 -> 10; matrix products, arithmetic and copies ran while one was open for 18% -> 15% of each run, Pallas kernels for 10% -> 13%
where the time goes in v2:
time: 105 us
  starting transfers between devices  31.3 us (30%)
  waiting for transfers between devices  22.5 us (21%)
  Pallas kernels  17 us (16%)
  between operations  14 us (13%)
  other arithmetic  10.6 us (10%)
  local copies, waits for them, and re-layouts  9.09 us (9%)
    ppermute x26, starting transfers between devices, shifted(): lax.ppermute(value, axis, [(i, (i + shift) % size) for i in range(size)])  31.3 us
    ppermute x26, waiting for transfers between devices, shifted(): lax.ppermute(value, axis, [(i, (i + shift) % size) for i in range(size)])  22.5 us
    pallas_call x2, Pallas kernels, lag_parts(): pl.pallas_call(functools.partial(lags_kernel, geometry, units), out_shape...  7.09 us
    add x2, other arithmetic, shards(): half = keep + shifted(send, 'freq', cores, 1)  3.78 us
    select_n x4, other arithmetic, rows_of(): chosen = jnp.where(owners[b] == (place - d) % places, ids[b:b + 1], chosen)  3.36 us
    unnamed x12, local copies, waits for them, and re-layouts  2.61 us
    pallas_call x1, Pallas kernels, normed_rows(): pl.pallas_call(functools.partial(normed_kernel, lag_total, len(sums[0])),...  2.59 us
    select_n x1, other arithmetic, shards(): scal = jnp.where(lane == COUNT + unit, pair_count[b, 0], scal)  2.38 us
  transfers between devices with their start and end apart: 26, of which 10 were waited for; matrix products, arithmetic and copies ran while one was open for 15% of the time, Pallas kernels for 13%

profile of v2, /device:TPU:0, one launch (start us, length us, event | category | flops | bytes accessed | tf_op | source)
XLA Modules:
  0.0 104.6 jit_solution(6547730832363246989)
XLA Ops:
  0.7 1.4 %dynamic-slice_bitcast_fusion.2 = (bf16[2,128,1024]{2,1,0:T(8,128)(2,1)S(1)}, bf16[2,128,1024]{2,1,0:T(8,128)(2,1)S(1)}) fusion(bf16[1,2,128,2048]{3,2,1,0:T(8,128)(2,1)} %param.10, s32[]{:T(128)S(6)} %select_n.351, s32[]{:T(128)S(6)} %select_n.349), kind=kLoop, calls=%fused_computation.4 | loop fusion | bytes 2097160 | tf_op jit(solution)/shard_map/dynamic_slice | solution.py:382
  2.0 3.0 %collective-permute-start = (bf16[2,128,1024]{2,1,0:T(8,128)(2,1)S(1)}, bf16[2,128,1024]{2,1,0:T(8,128)(2,1)S(1)}, u32[]{:S(2)}, u32[]{:S(2)}) collective-permute-start(bf16[2,128,1024]{2,1,0:T(8,128)(2,1)S(1)} %get-tuple-element.54), channel_id=1, source_target_pairs={{0,2},{2,0},{1,3},{3,1},{4,6},{6,4},{5,7},{7,5},{8,10},{10,8},{9,1... | collective-permute-start | bytes 1572872 | tf_op jit(solution)/shard_map/ppermute | solution.py:27
  5.0 1.5 %fusion.10 = (s32[1]{0:T(128)}, s32[1]{0:T(128)}, s32[1]{0:T(128)}, s32[1]{0:T(128)}) fusion(s32[4]{0:T(128)} %param.12), kind=kLoop, calls=%fused_computation.65 | loop fusion | bytes 32 | tf_op jit(solution)/shard_map/slice | solution.py:407
  12.3 3.6 %collective-permute-start.1 = (s32[1,64]{1,0:T(1,128)S(1)}, s32[1,64]{1,0:T(1,128)S(1)}, u32[]{:S(2)}, u32[]{:S(2)}) collective-permute-start(s32[1,64]{1,0:T(1,128)S(1)} %get-tuple-element.64), channel_id=1, source_target_pairs={{0,12},{4,0},{8,4},{12,8},{1,13},{5,1},{9,5},{13,9},{2,14},{6,2},{... | collective-permute-start | bytes 776 | tf_op jit(solution)/shard_map/ppermute | solution.py:27
  27.6 1.5 %fusion.9 = (s32[1,1]{0,1:T(1,128)}, s32[1,1]{0,1:T(1,128)}, s32[1,1]{0,1:T(1,128)}, s32[1,1]{0,1:T(1,128)}) fusion(s32[4,1]{0,1:T(1,128)} %param.15), kind=kLoop, calls=%fused_computation.64 | loop fusion | bytes 32 | tf_op jit(solution)/shard_map/slice | solution.py:409
  29.1 2.4 %compare_select_fusion.10.scal = s32[128]{0:T(128)S(1)} fusion(s32[]{:T(128)S(6)} %axis_index.38, s32[]{:T(128)S(6)} %axis_index.35, s32[]{:T(128)} %bitcast.8, s32[]{:T(128)S(6)} %add.155, s32[]{:T(128)} %bitcast.7, s32[]{:T(128)S(6)} %add.154, s32[]{:T(128)S(6)} %add.152, s32[]{:T(128)} %bitcast.5, s32[]{:T(128)S(6)} %add.151, s32[]{:T(128)S(6)} %add.149, ...), kind=kLoop, calls=%fused_computation.28 | loop fusion | flops 2816 | bytes 572 | tf_op jit(solution)/shard_map/jit(_where)/select_n | solution.py:409
  31.5 1.6 %copy-done.1 = bf16[1024,1024]{1,0:T(8,128)(2,1)S(1)} copy-done((bf16[1024,1024]{1,0:T(8,128)(2,1)S(1)}, bf16[1024,1024]{1,0:T(8,128)(2,1)}, u32[]{:S(2)}) %copy-start.1) | copy-done | bytes 2097176
  33.1 1.8 %rows.1 = (bf16[1,2,32,1024]{3,2,1,0:T(8,128)(2,1)S(1)}, bf16[1,2,32,1024]{3,2,1,0:T(8,128)(2,1)S(1)}, bf16[1,2,32,1024]{3,2,1,0:T(8,128)(2,1)S(1)}, bf16[1,2,32...) custom-call(s32[128]{0:T(128)S(1)} %compare_select_fusion.10.scal, ...), custom_call_target="tpu_custom_call" | custom-call | flops 805306368 | bytes 6291456 | tf_op jit(solution)/shard_map/rows/pallas_call | solution.py:109
  35.0 2.5 %collective-permute-start.4 = (bf16[1,2,32,1024]{3,2,1,0:T(8,128)(2,1)S(1)}, bf16[1,2,32,1024]{3,2,1,0:T(8,128)(2,1)S(1)}, u32[]{:S(2)}, u32[]{:S(2)}) collective-permute-start(bf16[1,2,32,1024]{3,2,1,0:T(8,128)(2,1)S(1)} %get-tuple-element.29), channel_id=1, source_target_pairs={{0,4},{4,8},{8,12},{12,0},{1,5},{5,9},{9,13},{13,1},{2,6},{6,10},{... | collective-permute-start | bytes 393224 | tf_op jit(solution)/shard_map/ppermute | solution.py:27
  38.6 1.4 %collective-permute-start.6 = (bf16[1,2,32,1024]{3,2,1,0:T(8,128)(2,1)S(1)}, bf16[1,2,32,1024]{3,2,1,0:T(8,128)(2,1)S(1)}, u32[]{:S(2)}, u32[]{:S(2)}) collective-permute-start(bf16[1,2,32,1024]{3,2,1,0:T(8,128)(2,1)S(1)} %get-tuple-element.31), channel_id=1, source_target_pairs={{0,12},{4,0},{8,4},{12,8},{1,13},{5,1},{9,5},{13,9},{2,14},{6,2},{... | collective-permute-start | bytes 393224 | tf_op jit(solution)/shard_map/ppermute | solution.py:27
  40.6 2.0 %collective-permute-start.13 = (bf16[1,2,32,1024]{3,2,1,0:T(8,128)(2,1)S(1)}, bf16[1,2,32,1024]{3,2,1,0:T(8,128)(2,1)S(1)}, u32[]{:S(2)}, u32[]{:S(2)}) collective-permute-start(bf16[1,2,32,1024]{3,2,1,0:T(8,128)(2,1)S(1)} %get-tuple-element.39), channel_id=1, source_target_pairs={{0,8},{4,12},{8,0},{12,4},{1,9},{5,13},{9,1},{13,5},{2,10},{6,14},... | collective-permute-start | bytes 393224 | tf_op jit(solution)/shard_map/ppermute | solution.py:27
  45.4 1.2 %table.1.refs_5_ = bf16[8,256,1024]{2,1,0:T(8,128)(2,1)S(1)} custom-call(f32[8,1,1024]{2,1,0:T(1,128)S(1)} %get-tuple-element.57.row_cos, f32[8,1,1024]{2,1,0:T(1,128)S(1)} %get-tuple-element.56.row_sin, f32[128,1024]{1,0:T(8,128)S(1)} %copy-done.2, f32[128,1024]{1,0:T(8,128)S(1)} %copy-done.3), custom_call_target="tpu_custom_call" | custom-call | flops 6291456 | bytes 6291456 | tf_op jit(solution)/shard_map/table/pallas_call | solution.py:56
  46.6 4.1 %collective-permute-done.5.refs_2_ = bf16[1,2,32,1024]{3,2,1,0:T(8,128)(2,1)S(1)} collective-permute-done((bf16[1,2,32,1024]{3,2,1,0:T(8,128)(2,1)S(1)}, bf16[1,2,32,1024]{3,2,1,0:T(8,128)(2,1)S(1)}, u32[]{:S(2)}, u32[]{:S(2)}) %collective-permute-start.5) | collective-permute-done | bytes 131104 | tf_op jit(solution)/shard_map/ppermute | solution.py:27
  50.7 3.1 %lags.2 = (f32[2,128,1024]{2,1,0:T(8,128)S(1)}, f32[2,128,1024]{2,1,0:T(8,128)S(1)}) custom-call(s32[128]{0:T(128)S(1)} %compare_select_fusion.10.scal, f32[1]{0:T(128)} %constant.176.clone.1.weight, bf16[1,2,32,1024]{3,2,1,0:T(8,128)(2,1)S(1)} %get-tuple-element.28.refs_0_, bf16[1,2,32,1024]{3,2,1,0:T(8,128)(2,1)S(1)} %collective-permute-done.4.refs_1_, ...), custom_call_target="tpu_custom_call" | custom-call | flops 1073741824 | bytes 8388608 | tf_op jit(solution)/shard_map/lags/pallas_call | solution.py:196
  53.8 4.4 %collective-permute-done.13.refs_2_ = bf16[1,2,32,1024]{3,2,1,0:T(8,128)(2,1)S(1)} collective-permute-done((bf16[1,2,32,1024]{3,2,1,0:T(8,128)(2,1)S(1)}, bf16[1,2,32,1024]{3,2,1,0:T(8,128)(2,1)S(1)}, u32[]{:S(2)}, u32[]{:S(2)}) %collective-permute-start.13) | collective-permute-done | bytes 131104 | tf_op jit(solution)/shard_map/ppermute | solution.py:27
  58.2 4.0 %lags.3 = (f32[2,128,1024]{2,1,0:T(8,128)S(1)}, f32[2,128,1024]{2,1,0:T(8,128)}) custom-call(s32[128]{0:T(128)S(1)} %compare_select_fusion.10.scal, f32[1]{0:T(128)} %constant.176.clone.1.weight, bf16[1,2,32,1024]{3,2,1,0:T(8,128)(2,1)S(1)} %get-tuple-element.37.refs_0_, bf16[1,2,32,1024]{3,2,1,0:T(8,128)(2,1)S(1)} %collective-permute-done.12.refs_1_, ...), custom_call_target="tpu_custom_call" | custom-call | flops 1073741824 | bytes 8388608 | tf_op jit(solution)/shard_map/lags/pallas_call | solution.py:196
  62.3 2.4 %add.169 = f32[2,128,1024]{2,1,0:T(8,128)} add(f32[2,128,1024]{2,1,0:T(8,128)S(1)} %get-tuple-element.33, f32[2,128,1024]{2,1,0:T(8,128)} %collective-permute-done.7) | non-fusion elementwise | flops 262144 | bytes 3145728 | tf_op jit(solution)/shard_map/add | solution.py:436
  64.7 1.1 %fusion = bf16[128,1024]{1,0:T(8,128)(2,1)S(1)} fusion(f32[2,128,1024]{2,1,0:T(8,128)} %add.169, s32[]{:T(128)S(6)} %select_n.406), kind=kLoop, calls=%fused_computation.6 | loop fusion | bytes 524292 | tf_op jit(solution)/shard_map/convert_element_type | solution.py:440
  66.4 1.4 %add.172 = f32[2,128,1024]{2,1,0:T(8,128)S(1)} add(f32[2,128,1024]{2,1,0:T(8,128)S(1)} %get-tuple-element.42, f32[2,128,1024]{2,1,0:T(8,128)} %collective-permute-done.15) | non-fusion elementwise | flops 262144 | bytes 3145728 | tf_op jit(solution)/shard_map/add | solution.py:436
  68.8 1.6 %collective-permute-start.16 = (bf16[128,1024]{1,0:T(8,128)(2,1)S(1)}, bf16[128,1024]{1,0:T(8,128)(2,1)S(1)}, u32[]{:S(2)}, u32[]{:S(2)}) collective-permute-start(bf16[128,1024]{1,0:T(8,128)(2,1)S(1)} %fusion.1), channel_id=1, source_target_pairs={{0,2},{2,0},{1,3},{3,1},{4,6},{6,4},{5,7},{7,5},{8,10},{10,8},{9,1... | collective-permute-start | bytes 786440 | tf_op jit(solution)/shard_map/ppermute | solution.py:27
  70.3 1.1 %dynamic-slice_bitcast_fusion.1.refs_0_ = f32[128,1024]{1,0:T(8,128)S(1)} fusion(f32[2,128,1024]{2,1,0:T(8,128)} %add.169, s32[]{:T(128)S(6)} %select_n.405), kind=kLoop, calls=%fused_computation.3 | loop fusion | bytes 1048580 | tf_op jit(solution)/shard_map/jit(dynamic_index_in_dim)/squeeze | solution.py:437
  71.4 3.5 %collective-permute-done.8.refs_1_ = bf16[128,1024]{1,0:T(8,128)(2,1)S(1)} collective-permute-done((bf16[128,1024]{1,0:T(8,128)(2,1)S(1)}, bf16[128,1024]{1,0:T(8,128)(2,1)S(1)}, u32[]{:S(2)}, u32[]{:S(2)}) %collective-permute-start.8) | collective-permute-done | bytes 262176 | tf_op jit(solution)/shard_map/ppermute | solution.py:27
  76.3 1.4 %collective-permute-start.11 = (f32[8,128]{1,0:T(8,128)S(1)}, f32[8,128]{1,0:T(8,128)S(1)}, u32[]{:S(2)}, u32[]{:S(2)}) collective-permute-start(f32[8,128]{1,0:T(8,128)S(1)} %get-tuple-element.35.refs_0_), channel_id=1, source_target_pairs={{0,3},{1,0},{2,1},{3,2},{4,7},{5,4},{6,5},{7,6},{8,11},{9,8},{10,9... | collective-permute-start | bytes 12296 | tf_op jit(solution)/shard_map/ppermute | solution.py:27
  77.7 2.1 %collective-permute-done.9.refs_1_ = f32[8,128]{1,0:T(8,128)S(1)} collective-permute-done((f32[8,128]{1,0:T(8,128)S(1)}, f32[8,128]{1,0:T(8,128)S(1)}, u32[]{:S(2)}, u32[]{:S(2)}) %collective-permute-start.9) | collective-permute-done | bytes 4128 | tf_op jit(solution)/shard_map/ppermute | solution.py:27
  81.1 3.8 %collective-permute-start.20 = (bf16[32,1024]{1,0:T(8,128)(2,1)S(1)}, bf16[32,1024]{1,0:T(8,128)(2,1)S(1)}, u32[]{:S(2)}, u32[]{:S(2)}) collective-permute-start(bf16[32,1024]{1,0:T(8,128)(2,1)S(1)} %get-tuple-element.48), channel_id=1, source_target_pairs={{0,12},{4,0},{8,4},{12,8},{1,13},{5,1},{9,5},{13,9},{2,14},{6,2},{... | collective-permute-start | bytes 196616 | tf_op jit(solution)/shard_map/ppermute | solution.py:27
  86.4 1.4 %collective-permute-start.19 = (f32[8,128]{1,0:T(8,128)S(1)}, f32[8,128]{1,0:T(8,128)S(1)}, u32[]{:S(2)}, u32[]{:S(2)}) collective-permute-start(f32[8,128]{1,0:T(8,128)S(1)} %get-tuple-element.44.refs_5_.refs_0_), channel_id=1, source_target_pairs={{0,3},{1,0},{2,1},{3,2},{4,7},{5,4},{6,5},{7,6},{8,11},{9,8},{10,9... | collective-permute-start | bytes 12296 | tf_op jit(solution)/shard_map/ppermute | solution.py:27
  91.2 2.3 %collective-permute-start.23 = (bf16[32,1024]{1,0:T(8,128)(2,1)S(1)}, bf16[32,1024]{1,0:T(8,128)(2,1)S(1)}, u32[]{:S(2)}, u32[]{:S(2)}) collective-permute-start(bf16[32,1024]{1,0:T(8,128)(2,1)S(1)} %get-tuple-element.51), channel_id=1, source_target_pairs={{0,8},{4,12},{8,0},{12,4},{1,9},{5,13},{9,1},{13,5},{2,10},{6,14},... | collective-permute-start | bytes 196616 | tf_op jit(solution)/shard_map/ppermute | solution.py:27
  93.5 1.8 %collective-permute-start.24 = (bf16[32,1024]{1,0:T(8,128)(2,1)S(1)}, bf16[32,1024]{1,0:T(8,128)(2,1)S(1)}, u32[]{:S(2)}, u32[]{:S(2)}) collective-permute-start(bf16[32,1024]{1,0:T(8,128)(2,1)S(1)} %get-tuple-element.52), channel_id=1, source_target_pairs={{0,4},{4,8},{8,12},{12,0},{1,5},{5,9},{9,13},{13,1},{2,6},{6,10},{... | collective-permute-start | bytes 196616 | tf_op jit(solution)/shard_map/ppermute | solution.py:27
  95.3 2.6 %normed.1 = f32[4,64,1024]{2,1,0:T(8,128)} custom-call(s32[128]{0:T(128)S(1)} %compare_select_fusion.10.scal, f32[8,128]{1,0:T(8,128)S(1)} %get-tuple-element.35.refs_0_, f32[8,128]{1,0:T(8,128)S(1)} %collective-permute-done.9.refs_1_, f32[8,128]{1,0:T(8,128)S(1)} %collective-permute-done.10.refs_2_, f32[8,128]{1,0:T(8,128)S(1)} %collective-permute-done.11.refs_3_, ...), custom_call_target="tpu_custom_call" | custom-call | flops 524288 | bytes 2097152 | tf_op jit(solution)/shard_map/normed/pallas_call | solution.py:325
  97.9 4.2 %collective-permute-done.22.refs_8_ = bf16[32,1024]{1,0:T(8,128)(2,1)S(1)} collective-permute-done((bf16[32,1024]{1,0:T(8,128)(2,1)S(1)}, bf16[32,1024]{1,0:T(8,128)(2,1)S(1)}, u32[]{:S(2)}, u32[]{:S(2)}) %collective-permute-start.22) | collective-permute-done | bytes 65568 | tf_op jit(solution)/shard_map/ppermute | solution.py:27
  102.1 1.4 %collective-permute-done.23.refs_9_ = bf16[32,1024]{1,0:T(8,128)(2,1)S(1)} collective-permute-done((bf16[32,1024]{1,0:T(8,128)(2,1)S(1)}, bf16[32,1024]{1,0:T(8,128)(2,1)S(1)}, u32[]{:S(2)}, u32[]{:S(2)}) %collective-permute-start.23) | collective-permute-done | bytes 65568 | tf_op jit(solution)/shard_map/ppermute | solution.py:27
  103.5 1.1 %adjoint.1 = f32[128,1024]{1,0:T(8,128)} custom-call(s32[1,64]{1,0:T(1,128)S(1)} %get-tuple-element.65.refs_3_.refs_0_, s32[1,64]{1,0:T(1,128)S(1)} %collective-permute-done.1.refs_4_.refs_1_, s32[1,64]{1,0:T(1,128)S(1)} %collective-permute-done.2.refs_5_.refs_2_, s32[1,64]{1,0:T(1,128)S(1)} %collective-permute-done.3.refs_6_.refs_3_, ...), custom_call_target="tpu_custom_call" | custom-call | flops 67108864 | bytes 1048576 | tf_op jit(solution)/shard_map/adjoint/pallas_call | solution.py:351
  (60 shorter events, 18.2 us)
Async XLA Ops:
  0.6 44.7 %copy-start.2 = (f32[128,1024]{1,0:T(8,128)S(1)}, f32[128,1024]{1,0:T(8,128)}, u32[]{:S(2)}) copy-start(f32[128,1024]{1,0:T(8,128)} %constant.185.clone.base_cos) | copy-start | bytes 1572868
  0.6 44.7 %copy-start.3 = (f32[128,1024]{1,0:T(8,128)S(1)}, f32[128,1024]{1,0:T(8,128)}, u32[]{:S(2)}) copy-start(f32[128,1024]{1,0:T(8,128)} %constant.186.clone.base_sin) | copy-start | bytes 1572868
  2.0 29.5 %collective-permute-start = (bf16[2,128,1024]{2,1,0:T(8,128)(2,1)S(1)}, bf16[2,128,1024]{2,1,0:T(8,128)(2,1)S(1)}, u32[]{:S(2)}, u32[]{:S(2)}) collective-permute-start(bf16[2,128,1024]{2,1,0:T(8,128)(2,1)S(1)} %get-tuple-element.54), channel_id=1, source_target_pairs={{0,2},{2,0},{1,3},{3,1},{4,6},{6,4},{5,7},{7,5},{8,10},{10,8},{9,1... | collective-permute-start | bytes 1572872 | tf_op jit(solution)/shard_map/ppermute | solution.py:27
  12.3 19.2 %collective-permute-start.1 = (s32[1,64]{1,0:T(1,128)S(1)}, s32[1,64]{1,0:T(1,128)S(1)}, u32[]{:S(2)}, u32[]{:S(2)}) collective-permute-start(s32[1,64]{1,0:T(1,128)S(1)} %get-tuple-element.64), channel_id=1, source_target_pairs={{0,12},{4,0},{8,4},{12,8},{1,13},{5,1},{9,5},{13,9},{2,14},{6,2},{... | collective-permute-start | bytes 776 | tf_op jit(solution)/shard_map/ppermute | solution.py:27
  21.7 9.8 %collective-permute-start.2 = (s32[1,64]{1,0:T(1,128)S(1)}, s32[1,64]{1,0:T(1,128)S(1)}, u32[]{:S(2)}, u32[]{:S(2)}) collective-permute-start(s32[1,64]{1,0:T(1,128)S(1)} %get-tuple-element.63), channel_id=1, source_target_pairs={{0,8},{4,12},{8,0},{12,4},{1,9},{5,13},{9,1},{13,5},{2,10},{6,14},... | collective-permute-start | bytes 776 | tf_op jit(solution)/shard_map/ppermute | solution.py:27
  21.7 9.8 %collective-permute-start.3 = (s32[1,64]{1,0:T(1,128)S(1)}, s32[1,64]{1,0:T(1,128)S(1)}, u32[]{:S(2)}, u32[]{:S(2)}) collective-permute-start(s32[1,64]{1,0:T(1,128)S(1)} %get-tuple-element.62), channel_id=1, source_target_pairs={{0,4},{4,8},{8,12},{12,0},{1,5},{5,9},{9,13},{13,1},{2,6},{6,10},{... | collective-permute-start | bytes 776 | tf_op jit(solution)/shard_map/ppermute | solution.py:27
  31.5 1.6 %copy-start.1 = (bf16[1024,1024]{1,0:T(8,128)(2,1)S(1)}, bf16[1024,1024]{1,0:T(8,128)(2,1)}, u32[]{:S(2)}) copy-start(bf16[1024,1024]{1,0:T(8,128)(2,1)} %constant.187.clone.refs_2_) | copy-start | bytes 6291460
  35.0 8.4 %collective-permute-start.4 = (bf16[1,2,32,1024]{3,2,1,0:T(8,128)(2,1)S(1)}, bf16[1,2,32,1024]{3,2,1,0:T(8,128)(2,1)S(1)}, u32[]{:S(2)}, u32[]{:S(2)}) collective-permute-start(bf16[1,2,32,1024]{3,2,1,0:T(8,128)(2,1)S(1)} %get-tuple-element.29), channel_id=1, source_target_pairs={{0,4},{4,8},{8,12},{12,0},{1,5},{5,9},{9,13},{13,1},{2,6},{6,10},{... | collective-permute-start | bytes 393224 | tf_op jit(solution)/shard_map/ppermute | solution.py:27
  37.6 13.1 %collective-permute-start.5 = (bf16[1,2,32,1024]{3,2,1,0:T(8,128)(2,1)S(1)}, bf16[1,2,32,1024]{3,2,1,0:T(8,128)(2,1)S(1)}, u32[]{:S(2)}, u32[]{:S(2)}) collective-permute-start(bf16[1,2,32,1024]{3,2,1,0:T(8,128)(2,1)S(1)} %get-tuple-element.30), channel_id=1, source_target_pairs={{0,8},{4,12},{8,0},{12,4},{1,9},{5,13},{9,1},{13,5},{2,10},{6,14},... | collective-permute-start | bytes 393224 | tf_op jit(solution)/shard_map/ppermute | solution.py:27
  38.6 12.1 %collective-permute-start.6 = (bf16[1,2,32,1024]{3,2,1,0:T(8,128)(2,1)S(1)}, bf16[1,2,32,1024]{3,2,1,0:T(8,128)(2,1)S(1)}, u32[]{:S(2)}, u32[]{:S(2)}) collective-permute-start(bf16[1,2,32,1024]{3,2,1,0:T(8,128)(2,1)S(1)} %get-tuple-element.31), channel_id=1, source_target_pairs={{0,12},{4,0},{8,4},{12,8},{1,13},{5,1},{9,5},{13,9},{2,14},{6,2},{... | collective-permute-start | bytes 393224 | tf_op jit(solution)/shard_map/ppermute | solution.py:27
  40.0 13.8 %collective-permute-start.12 = (bf16[1,2,32,1024]{3,2,1,0:T(8,128)(2,1)S(1)}, bf16[1,2,32,1024]{3,2,1,0:T(8,128)(2,1)S(1)}, u32[]{:S(2)}, u32[]{:S(2)}) collective-permute-start(bf16[1,2,32,1024]{3,2,1,0:T(8,128)(2,1)S(1)} %get-tuple-element.38), channel_id=1, source_target_pairs={{0,4},{4,8},{8,12},{12,0},{1,5},{5,9},{9,13},{13,1},{2,6},{6,10},{... | collective-permute-start | bytes 393224 | tf_op jit(solution)/shard_map/ppermute | solution.py:27
  40.6 17.6 %collective-permute-start.13 = (bf16[1,2,32,1024]{3,2,1,0:T(8,128)(2,1)S(1)}, bf16[1,2,32,1024]{3,2,1,0:T(8,128)(2,1)S(1)}, u32[]{:S(2)}, u32[]{:S(2)}) collective-permute-start(bf16[1,2,32,1024]{3,2,1,0:T(8,128)(2,1)S(1)} %get-tuple-element.39), channel_id=1, source_target_pairs={{0,8},{4,12},{8,0},{12,4},{1,9},{5,13},{9,1},{13,5},{2,10},{6,14},... | collective-permute-start | bytes 393224 | tf_op jit(solution)/shard_map/ppermute | solution.py:27
  43.3 14.9 %collective-permute-start.14 = (bf16[1,2,32,1024]{3,2,1,0:T(8,128)(2,1)S(1)}, bf16[1,2,32,1024]{3,2,1,0:T(8,128)(2,1)S(1)}, u32[]{:S(2)}, u32[]{:S(2)}) collective-permute-start(bf16[1,2,32,1024]{3,2,1,0:T(8,128)(2,1)S(1)} %get-tuple-element.40), channel_id=1, source_target_pairs={{0,12},{4,0},{8,4},{12,8},{1,13},{5,1},{9,5},{13,9},{2,14},{6,2},{... | collective-permute-start | bytes 393224 | tf_op jit(solution)/shard_map/ppermute | solution.py:27
  53.7 8.5 %collective-permute-start.7 = (f32[2,128,1024]{2,1,0:T(8,128)S(1)}, f32[2,128,1024]{2,1,0:T(8,128)}, u32[]{:S(2)}, u32[]{:S(2)}) collective-permute-start(f32[2,128,1024]{2,1,0:T(8,128)S(1)} %get-tuple-element.34), channel_id=1, source_target_pairs={{0,1},{1,0},{2,3},{3,2},{4,5},{5,4},{6,7},{7,6},{8,9},{9,8},{10,11... | collective-permute-start | bytes 3145736 | tf_op jit(solution)/shard_map/ppermute | solution.py:27
  62.2 4.1 %collective-permute-start.15 = (f32[2,128,1024]{2,1,0:T(8,128)}, f32[2,128,1024]{2,1,0:T(8,128)}, u32[]{:S(2)}, u32[]{:S(2)}) collective-permute-start(f32[2,128,1024]{2,1,0:T(8,128)} %get-tuple-element.43), channel_id=1, source_target_pairs={{0,1},{1,0},{2,3},{3,2},{4,5},{5,4},{6,7},{7,6},{8,9},{9,8},{10,11... | collective-permute-start | bytes 3145736 | tf_op jit(solution)/shard_map/ppermute | solution.py:27
  62.2 12.7 %copy-start = (f32[4,64,1024]{2,1,0:T(8,128)S(1)}, f32[4,64,1024]{2,1,0:T(8,128)}, u32[]{:S(2)}) copy-start(f32[4,64,1024]{2,1,0:T(8,128)} %refs_8_.3) | copy-start | bytes 3145732
  65.8 9.2 %collective-permute-start.8 = (bf16[128,1024]{1,0:T(8,128)(2,1)S(1)}, bf16[128,1024]{1,0:T(8,128)(2,1)S(1)}, u32[]{:S(2)}, u32[]{:S(2)}) collective-permute-start(bf16[128,1024]{1,0:T(8,128)(2,1)S(1)} %fusion), channel_id=1, source_target_pairs={{0,2},{2,0},{1,3},{3,1},{4,6},{6,4},{5,7},{7,5},{8,10},{10,8},{9,1... | collective-permute-start | bytes 786440 | tf_op jit(solution)/shard_map/ppermute | solution.py:27
  67.7 1.0 copy-start.4
  68.8 16.2 %collective-permute-start.16 = (bf16[128,1024]{1,0:T(8,128)(2,1)S(1)}, bf16[128,1024]{1,0:T(8,128)(2,1)S(1)}, u32[]{:S(2)}, u32[]{:S(2)}) collective-permute-start(bf16[128,1024]{1,0:T(8,128)(2,1)S(1)} %fusion.1), channel_id=1, source_target_pairs={{0,2},{2,0},{1,3},{3,1},{4,6},{6,4},{5,7},{7,5},{8,10},{10,8},{9,1... | collective-permute-start | bytes 786440 | tf_op jit(solution)/shard_map/ppermute | solution.py:27
  71.4 13.5 %copy-start.5 = (f32[2,128,1024]{2,1,0:T(8,128)S(1)}, f32[2,128,1024]{2,1,0:T(8,128)}, u32[]{:S(2)}) copy-start(f32[2,128,1024]{2,1,0:T(8,128)} %copy-done.4) | copy-start | bytes 3145732
  75.7 4.2 %collective-permute-start.9 = (f32[8,128]{1,0:T(8,128)S(1)}, f32[8,128]{1,0:T(8,128)S(1)}, u32[]{:S(2)}, u32[]{:S(2)}) collective-permute-start(f32[8,128]{1,0:T(8,128)S(1)} %get-tuple-element.35.refs_0_), channel_id=1, source_target_pairs={{0,1},{1,2},{2,3},{3,0},{4,5},{5,6},{6,7},{7,4},{8,9},{9,10},{10,1... | collective-permute-start | bytes 12296 | tf_op jit(solution)/shard_map/ppermute | solution.py:27
  75.7 4.6 %collective-permute-start.10 = (f32[8,128]{1,0:T(8,128)S(1)}, f32[8,128]{1,0:T(8,128)S(1)}, u32[]{:S(2)}, u32[]{:S(2)}) collective-permute-start(f32[8,128]{1,0:T(8,128)S(1)} %get-tuple-element.35.refs_0_), channel_id=1, source_target_pairs={{0,2},{1,3},{2,0},{3,1},{4,6},{5,7},{6,4},{7,5},{8,10},{9,11},{10,... | collective-permute-start | bytes 12296 | tf_op jit(solution)/shard_map/ppermute | solution.py:27
  76.3 4.0 %collective-permute-start.11 = (f32[8,128]{1,0:T(8,128)S(1)}, f32[8,128]{1,0:T(8,128)S(1)}, u32[]{:S(2)}, u32[]{:S(2)}) collective-permute-start(f32[8,128]{1,0:T(8,128)S(1)} %get-tuple-element.35.refs_0_), channel_id=1, source_target_pairs={{0,3},{1,0},{2,1},{3,2},{4,7},{5,4},{6,5},{7,6},{8,11},{9,8},{10,9... | collective-permute-start | bytes 12296 | tf_op jit(solution)/shard_map/ppermute | solution.py:27
  81.1 14.2 %collective-permute-start.20 = (bf16[32,1024]{1,0:T(8,128)(2,1)S(1)}, bf16[32,1024]{1,0:T(8,128)(2,1)S(1)}, u32[]{:S(2)}, u32[]{:S(2)}) collective-permute-start(bf16[32,1024]{1,0:T(8,128)(2,1)S(1)} %get-tuple-element.48), channel_id=1, source_target_pairs={{0,12},{4,0},{8,4},{12,8},{1,13},{5,1},{9,5},{13,9},{2,14},{6,2},{... | collective-permute-start | bytes 196616 | tf_op jit(solution)/shard_map/ppermute | solution.py:27
  85.8 3.1 %collective-permute-start.17 = (f32[8,128]{1,0:T(8,128)S(1)}, f32[8,128]{1,0:T(8,128)S(1)}, u32[]{:S(2)}, u32[]{:S(2)}) collective-permute-start(f32[8,128]{1,0:T(8,128)S(1)} %get-tuple-element.44.refs_5_.refs_0_), channel_id=1, source_target_pairs={{0,1},{1,2},{2,3},{3,0},{4,5},{5,6},{6,7},{7,4},{8,9},{9,10},{10,1... | collective-permute-start | bytes 12296 | tf_op jit(solution)/shard_map/ppermute | solution.py:27
  85.8 3.6 %collective-permute-start.18 = (f32[8,128]{1,0:T(8,128)S(1)}, f32[8,128]{1,0:T(8,128)S(1)}, u32[]{:S(2)}, u32[]{:S(2)}) collective-permute-start(f32[8,128]{1,0:T(8,128)S(1)} %get-tuple-element.44.refs_5_.refs_0_), channel_id=1, source_target_pairs={{0,2},{1,3},{2,0},{3,1},{4,6},{5,7},{6,4},{7,5},{8,10},{9,11},{10,... | collective-permute-start | bytes 12296 | tf_op jit(solution)/shard_map/ppermute | solution.py:27
  86.4 3.1 %collective-permute-start.19 = (f32[8,128]{1,0:T(8,128)S(1)}, f32[8,128]{1,0:T(8,128)S(1)}, u32[]{:S(2)}, u32[]{:S(2)}) collective-permute-start(f32[8,128]{1,0:T(8,128)S(1)} %get-tuple-element.44.refs_5_.refs_0_), channel_id=1, source_target_pairs={{0,3},{1,0},{2,1},{3,2},{4,7},{5,4},{6,5},{7,6},{8,11},{9,8},{10,9... | collective-permute-start | bytes 12296 | tf_op jit(solution)/shard_map/ppermute | solution.py:27
  90.3 7.6 %collective-permute-start.21 = (bf16[32,1024]{1,0:T(8,128)(2,1)S(1)}, bf16[32,1024]{1,0:T(8,128)(2,1)S(1)}, u32[]{:S(2)}, u32[]{:S(2)}) collective-permute-start(bf16[32,1024]{1,0:T(8,128)(2,1)S(1)} %get-tuple-element.49), channel_id=1, source_target_pairs={{0,12},{4,0},{8,4},{12,8},{1,13},{5,1},{9,5},{13,9},{2,14},{6,2},{... | collective-permute-start | bytes 196616 | tf_op jit(solution)/shard_map/ppermute | solution.py:27
  90.6 11.5 %collective-permute-start.22 = (bf16[32,1024]{1,0:T(8,128)(2,1)S(1)}, bf16[32,1024]{1,0:T(8,128)(2,1)S(1)}, u32[]{:S(2)}, u32[]{:S(2)}) collective-permute-start(bf16[32,1024]{1,0:T(8,128)(2,1)S(1)} %get-tuple-element.50), channel_id=1, source_target_pairs={{0,8},{4,12},{8,0},{12,4},{1,9},{5,13},{9,1},{13,5},{2,10},{6,14},... | collective-permute-start | bytes 196616 | tf_op jit(solution)/shard_map/ppermute | solution.py:27
  91.2 12.3 %collective-permute-start.23 = (bf16[32,1024]{1,0:T(8,128)(2,1)S(1)}, bf16[32,1024]{1,0:T(8,128)(2,1)S(1)}, u32[]{:S(2)}, u32[]{:S(2)}) collective-permute-start(bf16[32,1024]{1,0:T(8,128)(2,1)S(1)} %get-tuple-element.51), channel_id=1, source_target_pairs={{0,8},{4,12},{8,0},{12,4},{1,9},{5,13},{9,1},{13,5},{2,10},{6,14},... | collective-permute-start | bytes 196616 | tf_op jit(solution)/shard_map/ppermute | solution.py:27
  93.5 10.0 %collective-permute-start.24 = (bf16[32,1024]{1,0:T(8,128)(2,1)S(1)}, bf16[32,1024]{1,0:T(8,128)(2,1)S(1)}, u32[]{:S(2)}, u32[]{:S(2)}) collective-permute-start(bf16[32,1024]{1,0:T(8,128)(2,1)S(1)} %get-tuple-element.52), channel_id=1, source_target_pairs={{0,4},{4,8},{8,12},{12,0},{1,5},{5,9},{9,13},{13,1},{2,6},{6,10},{... | collective-permute-start | bytes 196616 | tf_op jit(solution)/shard_map/ppermute | solution.py:27
  95.3 8.2 %collective-permute-start.25 = (bf16[32,1024]{1,0:T(8,128)(2,1)S(1)}, bf16[32,1024]{1,0:T(8,128)(2,1)S(1)}, u32[]{:S(2)}, u32[]{:S(2)}) collective-permute-start(bf16[32,1024]{1,0:T(8,128)(2,1)S(1)} %get-tuple-element.53), channel_id=1, source_target_pairs={{0,4},{4,8},{8,12},{12,0},{1,5},{5,9},{9,13},{13,1},{2,6},{6,10},{... | collective-permute-start | bytes 196616 | tf_op jit(solution)/shard_map/ppermute | solution.py:27

commit v3 on v2

--- a/solution.py
+++ b/solution.py
@@ -35,34 +35,70 @@
     return pl.CostEstimate(flops=int(flops), bytes_accessed=int(mib * MIB), transcendentals=0)
 
 
-def table_kernel(row_cos, row_sin, base_cos, base_sin, table):
-    ca, sa = row_cos[0], row_sin[0]
+def tables(classes, span, period, bins_dev, columns, cores):
+    u = np.arange(span, dtype=np.int64)[None, :]
+    first = np.arange(columns * cores, dtype=np.int64)[:, None] * (bins_dev // columns)
+    rows = (first + np.arange(classes)).reshape(-1, 1)
+    base = classes * np.arange(LANES, dtype=np.int64)[:, None]
+    out = []
+    for f in (rows, base):
+        angle = (f * u % period) * (2.0 * math.pi / period)
+        out += [np.cos(angle).astype(np.float32), np.sin(angle).astype(np.float32)]
+    return [jnp.asarray(t) for t in out]
+
+
+def start_kernel(blocks, direct, classes, window_keep, owners, pair_count, src, rec, *refs):
+    row_cos, row_sin, base_cos, base_sin = refs[:4]
+    scal, wanted, rec_ids, table = refs[4], refs[5:-2], refs[-2], refs[-1]
+    place, places = lax.axis_index("recv"), lax.axis_size("recv")
+    column, columns = lax.axis_index("win"), lax.axis_size("win")
+    core = lax.axis_index("freq")
+    scal[CORE] = core
+    scal[COLUMN] = column
+    scal[ORDER] = 1 - window_keep[0]
+    for b in range(blocks):
+        unit = lax.rem(place - owners[b] + places, places) if direct else b
+        scal[BLOCK + unit] = b
+        scal[COUNT + unit] = pair_count[b, 0]
+    for d, out in enumerate(wanted):
+        owner = lax.rem(place - d + places, places)
+        chosen = jnp.full(out.shape, -1, jnp.int32)
+        received = jnp.zeros(out.shape, jnp.int32)
+        for b in range(blocks):
+            mine = jnp.full(out.shape, owners[b], jnp.int32) == owner
+            chosen = jnp.where(mine, src[b : b + 1], chosen)
+            received = jnp.where(mine, rec[b : b + 1], received)
+        out[...] = chosen
+        if direct:
+            rec_ids[d : d + 1] = received
+    if not direct:
+        rec_ids[...] = rec[...]
+    first = (core * columns + column) * classes
     cb, sb = base_cos[...], base_sin[...]
-    table[0, :LANES] = (ca * cb - sa * sb).astype(BF16)
-    table[0, LANES:] = (-(sa * cb + ca * sb)).astype(BF16)
-
-
-def make_table(first_bin, classes, span, period):
-    m = np.arange(LANES, dtype=np.int64)[:, None]
-    u = np.arange(span, dtype=np.int64)[None, :]
-    base = (classes * m * u % period) * (2.0 * math.pi / period)
-    base_cos, base_sin = np.cos(base).astype(np.float32), np.sin(base).astype(np.float32)
-    frequency = first_bin + jnp.arange(classes, dtype=jnp.int32)
-    turns = frequency[:, None] * jnp.arange(span, dtype=jnp.int32)[None, :] % period
-    angles = turns.astype(F32) * (2.0 * math.pi / period)
-    row_cos, row_sin = jnp.cos(angles)[:, None, :], jnp.sin(angles)[:, None, :]
-    row = pl.BlockSpec((1, 1, span), lambda r: (r, 0, 0))
-    whole = pl.BlockSpec((LANES, span), lambda r: (0, 0))
-    return pl.pallas_call(
-        table_kernel,
-        grid=(classes,),
-        out_shape=jax.ShapeDtypeStruct((classes, 2 * LANES, span), BF16),
-        in_specs=[row, row, whole, whole],
-        out_specs=pl.BlockSpec((1, 2 * LANES, span), lambda r: (r, 0, 0)),
+    for r in range(classes):
+        ca, sa = row_cos[pl.ds(first + r, 1)], row_sin[pl.ds(first + r, 1)]
+        table[r, :LANES] = (ca * cb - sa * sb).astype(BF16)
+        table[r, LANES:] = (-(sa * cb + ca * sb)).astype(BF16)
+
+
+def start(window_keep, owners, pair_count, pair_src, pair_rec, places, trig, classes, span):
+    blocks, slots = pair_src.shape
+    ids = jax.ShapeDtypeStruct((1, slots), jnp.int32)
+    scal, *wanted, rec_ids, table = pl.pallas_call(
+        functools.partial(start_kernel, blocks, places == blocks, classes),
+        out_shape=[jax.ShapeDtypeStruct((LANES,), jnp.int32)]
+        + [ids] * places
+        + [
+            jax.ShapeDtypeStruct(pair_rec.shape, jnp.int32),
+            jax.ShapeDtypeStruct((classes, 2 * LANES, span), BF16),
+        ],
+        in_specs=[SMEM] * 3 + [VMEM] * 6,
+        out_specs=[SMEM] + [VMEM] * (places + 2),
         compiler_params=params(16),
         cost_estimate=cost(6 * classes * LANES * span, 6),
-        name="table",
-    )(row_cos, row_sin, jnp.asarray(base_cos), jnp.asarray(base_sin))
+        name="start",
+    )(window_keep, owners, pair_count, pair_src, pair_rec, *trig)
+    return scal, wanted, rec_ids, table
 
 
 def picks(ids, channels):
@@ -70,53 +106,56 @@
     return (lax.broadcasted_iota(jnp.int32, (channels, row.shape[1]), 0) == row).astype(BF16)
 
 
-def rows_kernel(used, sends, scal, *refs):
-    shifts = used + 1
-    held, refs = refs[:shifts], refs[shifts:]
-    perm, src_ids, rec_ids, outs = refs[0], refs[1 : 1 + sends], refs[1 + sends], refs[2 + sends :]
-    rows_out, own_out = outs[: sends * CHUNKS], outs[sends * CHUNKS :]
-    units, _, _, slots, _ = own_out[0].shape
-    channels = held[0].shape[1]
-    pick = picks(
-        list(src_ids) + [rec_ids.at[d : d + 1] for d in range(units)], channels
-    )
+def rows_kernel(half, used, sends, scal, spectra, *refs):
+    held, refs = refs[:used], refs[used:]
+    perm, src_ids, rec_ids, refs = refs[0], refs[1 : 1 + sends], refs[1 + sends], refs[2 + sends :]
+    early, refs = (refs[:sends], refs[sends:]) if half else (None, refs)
+    first, second, own_out = refs[:sends], refs[sends:-1], refs[-1]
+    units, _, slots, part = own_out.shape
+    some = first[0].shape[1]
+    channels = spectra.shape[2]
+    pick = picks(list(src_ids) + [rec_ids.at[d : d + 1] for d in range(units)], channels)
+    here = spectra[0, half, :, pl.ds(pl.multiple_of(scal[COLUMN] * part, part), part)]
     for u in range(used):
-        for half in range(2):
-            x = held[0][half]
-            for s in range(1, shifts):
-                x = jnp.where(scal[ORDER + u] == s, held[s][half], x)
-            x = jnp.dot(x, perm[...], preferred_element_type=F32).astype(BF16)
-            y = lax.dot_general(
-                pick, x, (((0,), (0,)), ((), ())), preferred_element_type=F32
-            ).astype(BF16)
-            for i, out in enumerate(rows_out):
-                out[u, half] = y[i * slots : (i + 1) * slots]
-            y = y[sends * CHUNKS * slots :]
-            for d in range(units):
-                for q, out in enumerate(own_out):
-                    first = (d * CHUNKS + q) * slots
-                    out[d, u, half] = y[first : first + slots]
-
-
-def gather_rows(scal, held, classes, src_ids, rec_ids, units, slots):
-    used, sends = len(held) - 1, len(src_ids)
+        x = here
+        for s in range(used):
+            x = jnp.where(scal[ORDER + u] == s + 1, held[s][...], x)
+        x = jnp.dot(x, perm[...], preferred_element_type=F32).astype(BF16)
+        y = lax.dot_general(
+            pick, x, (((0,), (0,)), ((), ())), preferred_element_type=F32
+        ).astype(BF16)
+        for d in range(sends):
+            at = d * slots
+            first[d][u] = y[at : at + some]
+            if half:
+                second[d][u, 0] = early[d][u]
+                second[d][u, 1] = y[at + some : at + slots]
+            else:
+                second[d][u] = y[at + some : at + slots]
+        for d in range(units):
+            at = (sends + d) * slots
+            own_out[d, u] = y[at : at + slots]
+
+
+def gather_rows(half, scal, spectra, held, perm, src_ids, rec_ids, early, some):
+    used, sends = len(held), len(src_ids)
     part = held[0].shape[-1]
-    source = np.arange(part)
-    perm = np.zeros((part, part), ml_dtypes.bfloat16)
-    perm[source, source % classes * LANES + source // classes] = 1
-    sent = jax.ShapeDtypeStruct((used, 2, slots, part), BF16)
-    own = jax.ShapeDtypeStruct((units, used, 2, slots, part), BF16)
+    units, slots = rec_ids.shape
+    shape = lambda *dims: jax.ShapeDtypeStruct(dims, BF16)
+    rest = slots - some
+    late = shape(used, 2, rest, part) if half else shape(used, rest, part)
     outs = pl.pallas_call(
-        functools.partial(rows_kernel, used, sends),
-        out_shape=[sent] * (sends * CHUNKS) + [own] * CHUNKS,
-        in_specs=[SMEM] + [VMEM] * (len(held) + 2 + sends),
-        out_specs=[VMEM] * ((sends + 1) * CHUNKS),
+        functools.partial(rows_kernel, half, used, sends),
+        out_shape=[shape(used, some, part)] * sends
+        + [late] * sends
+        + [shape(units, used, slots, part)],
+        in_specs=[SMEM] + [VMEM] * (used + 3 + sends + len(early)),
+        out_specs=[VMEM] * (2 * sends + 1),
         compiler_params=params(32),
-        cost_estimate=cost(4 * used * part * (128 * part + 512 * 128), 6),
+        cost_estimate=cost(2 * used * part * (128 * part + 512 * 128), 4),
         name="rows",
-    )(scal, *held, jnp.asarray(perm), *src_ids, rec_ids)
-    sends_of = [outs[q : sends * CHUNKS : CHUNKS] for q in range(CHUNKS)]
-    return sends_of, outs[sends * CHUNKS :]
+    )(scal, spectra, *held, perm, *src_ids, rec_ids, *early)
+    return outs[:sends], outs[sends:-1], outs[-1]
 
 
 def combine(values, classes, outputs, origin, span, period):
@@ -145,13 +184,15 @@
     return [a if b is None else a + root * b for a, b in zip(plain, scaled)]
 
 
-def lags_kernel(geometry, units, scal, weight, *refs):
+def lags_kernel(geometry, units, first, split, scal, weight, after, *refs):
     classes, span, outputs, origin, period, chunk = geometry
-    s_refs, (r_ref, table, keep, send, lhs) = refs[:units], refs[units:]
-    used, _, slots, _ = s_refs[0].shape
+    count = units * (2 if split else 1)
+    s_refs, (r_real, r_imag, table, keep, send, lhs) = refs[:count], refs[count:]
+    used, slots = s_refs[0].shape[0], s_refs[0].shape[-2]
     rows = units * slots
     lag_dev = keep.shape[-1]
     cores = 2
+    mine = slice(first, first + slots)
     for d in range(units):
         at = slice(d * slots, (d + 1) * slots)
         turned = slice(rows + d * slots, rows + (d + 1) * slots)
@@ -159,8 +200,12 @@
             bins = slice(r * LANES, (r + 1) * LANES)
             real = imag = None
             for u in range(used):
-                sr, si = s_refs[d][u, 0, :, bins].astype(F32), s_refs[d][u, 1, :, bins].astype(F32)
-                rr, ri = r_ref[d, u, 0, :, bins].astype(F32), r_ref[d, u, 1, :, bins].astype(F32)
+                if split:
+                    sr, si = s_refs[d][u, :, bins], s_refs[units + d][u, :, bins]
+                else:
+                    sr, si = s_refs[d][u, 0, :, bins], s_refs[d][u, 1, :, bins]
+                sr, si = sr.astype(F32), si.astype(F32)
+                rr, ri = r_real[d, u, mine, bins].astype(F32), r_imag[d, u, mine, bins].astype(F32)
                 re, im = sr * rr + si * ri, si * rr - sr * ri
                 if u:
                     re, im = real + weight[u] * re, imag + weight[u] * im
@@ -185,24 +230,55 @@
 
             @pl.when(scal[CORE] != core)
             def _():
-                send[column, :, lags] = value
-
-
-def lag_parts(scal, weight, rows, own, table, geometry, columns, lag_dev):
+                send[column, :, lags] = value.astype(BF16)
+
+
+def lag_parts(scal, weight, after, rows, own, first, table, geometry, columns, lag_dev):
     classes, span = geometry[:2]
-    units = len(rows)
-    used, _, slots, part = rows[0].shape
-    out = jax.ShapeDtypeStruct((columns, units * slots, lag_dev), F32)
+    units = own[0].shape[0]
+    split = len(rows) > units
+    slots, part = rows[0].shape[-2:]
+    shape = (columns, units * slots, lag_dev)
     return pl.pallas_call(
-        functools.partial(lags_kernel, geometry, units),
-        out_shape=[out] * 2,
-        in_specs=[SMEM, SMEM] + [VMEM] * (units + 2),
+        functools.partial(lags_kernel, geometry, units, first, split),
+        out_shape=[jax.ShapeDtypeStruct(shape, F32), jax.ShapeDtypeStruct(shape, BF16)],
+        in_specs=[SMEM, SMEM, pl.BlockSpec(memory_space=pl.ANY)] + [VMEM] * (len(rows) + 3),
         out_specs=[VMEM] * 2,
         scratch_shapes=[pltpu.VMEM((classes, 2 * units * slots, 2 * LANES), BF16)],
         compiler_params=params(32),
         cost_estimate=cost(8 * units * slots * part * span, 8),
         name="lags",
-    )(scal, weight, *rows, own, table)
+    )(scal, weight, after, *rows, *own, table)
+
+
+def cores_kernel(scal, keep, more, own, *sends):
+    columns = keep.shape[0]
+    for column in range(columns):
+        value = keep[column] + more[column].astype(F32)
+
+        @pl.when(scal[COLUMN] == column)
+        def _():
+            own[...] = value
+
+        for s, out in enumerate(sends):
+
+            @pl.when(lax.rem(scal[COLUMN] + s + 1, columns) == column)
+            def _():
+                out[...] = value.astype(BF16)
+
+
+def add_cores(scal, keep, more):
+    columns, rows, lag_dev = keep.shape
+    return pl.pallas_call(
+        cores_kernel,
+        out_shape=[jax.ShapeDtypeStruct((rows, lag_dev), F32)]
+        + [jax.ShapeDtypeStruct((rows, lag_dev), BF16)] * (columns - 1),
+        in_specs=[SMEM, VMEM, VMEM],
+        out_specs=[VMEM] * columns,
+        compiler_params=params(16),
+        cost_estimate=cost(2 * keep.size, 2),
+        name="cores",
+    )(scal, keep, more)
 
 
 def stats_kernel(scale, chunk, units, others, scal, *refs):
@@ -378,72 +454,68 @@
     shifts = range(places)
 
     held = [
-        shifted(
-            lax.dynamic_slice(
-                spectra[0], (0, 0, (column + s) % columns * part), (2, channels, part)
-            ),
-            "win",
-            columns,
-            s,
-        )
-        for s in range(columns)
-    ]
-    kept = window_keep[0]
-    if columns == 2:
-        order = [1 - kept]
-        weight = jnp.ones((1,), F32)
-    else:
-        keeps = jnp.stack([shifted(kept, "win", columns, s) for s in range(columns)])
-        ranked = jnp.argsort(-keeps)[: columns - 1].astype(jnp.int32)
-        order = [ranked[u] for u in range(columns - 1)]
-        weight = keeps[ranked].astype(F32)
-
-    direct = places == blocks
-    lane = jnp.arange(LANES, dtype=jnp.int32)
-    scal = jnp.where(lane == CORE, core, jnp.where(lane == COLUMN, column, 0))
-    for u, o in enumerate(order):
-        scal = jnp.where(lane == ORDER + u, o, scal)
-    for b in range(blocks):
-        unit = (place - owners[b]) % places if direct else b
-        scal = jnp.where(lane == BLOCK + unit, b, scal)
-        scal = jnp.where(lane == COUNT + unit, pair_count[b, 0], scal)
-
-    def rows_of(ids, d):
-        chosen = jnp.full((1, slots), -1, jnp.int32)
-        for b in range(blocks):
-            chosen = jnp.where(owners[b] == (place - d) % places, ids[b : b + 1], chosen)
-        return chosen
-
-    src_ids = [shifted(rows_of(pair_src, d), "recv", places, -d) for d in shifts]
-    if direct:
-        rec_ids = jnp.concatenate([rows_of(pair_rec, d) for d in shifts], axis=0)
-    else:
-        rec_ids = pair_rec
-
-    table = make_table(core * bins_dev + column * part, classes, span, period)
-    sends, own_rows = gather_rows(scal, held, classes, src_ids, rec_ids, blocks, some)
-    corrs, all_sums, returned = [], [], [[] for _ in shifts]
-    arrived = [[shifted(x, "recv", places, d) for d, x in zip(shifts, sent)] for sent in sends]
-    for q in range(CHUNKS):
-        rows = arrived[q]
-        if not direct:
-            stacked = jnp.stack(rows)
-            rows = [
-                lax.dynamic_index_in_dim(stacked, (place - owners[b]) % places, 0, False)
-                for b in range(blocks)
-            ]
-        keep, send = lag_parts(scal, weight, rows, own_rows[q], table, geometry, columns, lag_dev)
-        half = keep + shifted(send, "freq", cores, 1)
-        own = lax.dynamic_index_in_dim(half, column, 0, False)
-        more = [
+        [
             shifted(
-                lax.dynamic_index_in_dim(half, (column + s) % columns, 0, False).astype(BF16),
+                lax.dynamic_slice(
+                    spectra[0, half], (0, (column + s) % columns * part), (channels, part)
+                ),
                 "win",
                 columns,
                 s,
             )
             for s in range(1, columns)
         ]
+        for half in range(2)
+    ]
+    trig = tables(classes, span, period, bins_dev, columns, cores)
+    scal, wanted, rec_ids, table = start(
+        window_keep, owners, pair_count, pair_src, pair_rec, places, trig, classes, span
+    )
+    if columns == 2:
+        weight = jnp.ones((1,), F32)
+    else:
+        keeps = jnp.stack([shifted(window_keep[0], "win", columns, s) for s in range(columns)])
+        ranked = jnp.argsort(-keeps)[: columns - 1].astype(jnp.int32)
+        weight = keeps[ranked].astype(F32)
+        scal = lax.dynamic_update_slice(scal, ranked, (ORDER,))
+
+    direct = places == blocks
+    src_ids = [shifted(x, "recv", places, -d) for d, x in zip(shifts, wanted)]
+    source = np.arange(part)
+    perm = np.zeros((part, part), ml_dtypes.bfloat16)
+    perm[source, source % classes * LANES + source // classes] = 1
+    perm = jnp.asarray(perm)
+    first_real, rest_real, own_real = gather_rows(
+        0, scal, spectra, held[0], perm, src_ids, rec_ids, [], some
+    )
+    first_imag, rest, own_imag = gather_rows(
+        1, scal, spectra, held[1], perm, src_ids, rec_ids, rest_real, some
+    )
+    sent = [[first_real, first_imag], [rest]]
+    arrived = [
+        [[shifted(x, "recv", places, d) for d, x in zip(shifts, rows)] for rows in group]
+        for group in sent
+    ]
+    corrs, all_sums, returned = [], [], [[] for _ in shifts]
+    after = scal
+    for q in range(CHUNKS):
+        rows = arrived[q]
+        if not direct:
+            stacked = [jnp.stack(r) for r in rows]
+            rows = [
+                [
+                    lax.dynamic_index_in_dim(x, (place - owners[b]) % places, 0, False)
+                    for b in range(blocks)
+                ]
+                for x in stacked
+            ]
+        rows = [x for group in rows for x in group]
+        keep, send = lag_parts(
+            scal, weight, after, rows, (own_real, own_imag), q * some, table, geometry, columns, lag_dev
+        )
+        own, *sends = add_cores(scal, keep, shifted(send, "freq", cores, 1))
+        after = own
+        more = [shifted(x, "win", columns, s + 1) for s, x in enumerate(sends)]
         corr, sums = lag_stats(scal, lag_scale, q, own, more, observed, blocks, some)
         sums = [shifted(sums, ("win", "freq"), peers, s) for s in range(peers)]
         grads = gradients(scal, lag_total, q, sums, corr, observed, blocks, some)

time: 105 us -> 98.7 us (0.940)
  between operations: 14 us -> 1.46 us
  other arithmetic: 10.6 us -> 0 us
  waiting for transfers between devices: 22.5 us -> 28.3 us
  starting transfers between devices: 31.3 us -> 36.9 us
  local copies, waits for them, and re-layouts: 9.09 us -> 12.4 us
  Pallas kernels: 17 us -> 19.1 us
    ppermute x26 -> x30, waiting for transfers between devices: 22.5 us -> 28.3 us  [shifted(): lax.ppermute(value, axis, [(i, (i + shift) % size) for i in range(size)])]
    select_n x5 -> x0, other arithmetic: 5.74 us -> none  [the longest x4 3.36 us: rows_of(): chosen = jnp.where(owners[b] == (place - d) % places, ids[b:b + 1], chosen)]
    ppermute x26 -> x30, starting transfers between devices: 31.3 us -> 36.9 us  [shifted(): lax.ppermute(value, axis, [(i, (i + shift) % size) for i in range(size)])]
    unnamed x12 -> x21, local copies, waits for them, and re-layouts: 2.61 us -> 6.67 us
    add x3 -> x0, other arithmetic: 3.79 us -> none  [the longest x2 3.78 us: shards(): half = keep + shifted(send, 'freq', cores, 1)]
    pallas_call x4 -> x7, Pallas kernels: 10.2 us -> 12.4 us  [the longest x2 5.98 us: lag_parts(): pl.pallas_call(functools.partial(lags_kernel, geometry, units, first, spl...]
    dynamic_slice x1 -> x2, local copies, waits for them, and re-layouts: 1.35 us -> 3.33 us  [shards(): lax.dynamic_slice(spectra[0, half], (0, (column + s) % columns * part), (...]
    squeeze x2 -> x0, local copies, waits for them, and re-layouts: 1.12 us -> none  [shards(): own = lax.dynamic_index_in_dim(half, column, 0, False)]
  transfers between devices with their start and end apart: 26 -> 30, of which waited for: 10 -> 15; matrix products, arithmetic and copies ran while one was open for 15% -> 2% of each run, Pallas kernels for 13% -> 12%
where the time goes in v3:
time: 98.7 us; the launch traced here: 98.3 us
  starting transfers between devices  36.9 us (37%)
  waiting for transfers between devices  28.3 us (29%)
  Pallas kernels  19.1 us (19%)
  local copies, waits for them, and re-layouts  12.4 us (13%)
  between operations  1.46 us (1%)
    ppermute x30, starting transfers between devices, shifted(): lax.ppermute(value, axis, [(i, (i + shift) % size) for i in range(size)])  36.9 us
    ppermute x30, waiting for transfers between devices, shifted(): lax.ppermute(value, axis, [(i, (i + shift) % size) for i in range(size)])  28.3 us
    unnamed x21, local copies, waits for them, and re-layouts  6.67 us
    pallas_call x2, Pallas kernels, lag_parts(): pl.pallas_call(functools.partial(lags_kernel, geometry, units, first, spl...  5.98 us
    dynamic_slice x2, local copies, waits for them, and re-layouts, shards(): lax.dynamic_slice(spectra[0, half], (0, (column + s) % columns * part), (...  3.33 us
    pallas_call x2, Pallas kernels, gather_rows(): pl.pallas_call(functools.partial(rows_kernel, half, used, sends), out_sha...  2.97 us
    pallas_call x1, Pallas kernels, normed_rows(): pl.pallas_call(functools.partial(normed_kernel, lag_total, len(sums[0])),...  2.59 us
    slice x1, local copies, waits for them, and re-layouts, shards(): spectra[0, half]  2.43 us
  transfers between devices with their start and end apart: 30, of which 15 were waited for; matrix products, arithmetic and copies ran while one was open for 2% of the time, Pallas kernels for 12%

profile of v3, /device:TPU:0, one launch (start us, length us, event | category | flops | bytes accessed | tf_op | source)
XLA Modules:
  0.0 98.3 jit_solution(6942329780692236090)
XLA Ops:
  0.7 2.4 %fusion = (bf16[1,1,128,2048]{3,2,1,0:T(8,128)(2,1)}, bf16[1,1,128,2048]{3,2,1,0:T(8,128)(2,1)}) fusion(bf16[1,2,128,2048]{3,2,1,0:T(8,128)(2,1)} %spectra.3), kind=kLoop, calls=%fused_computation.2 | loop fusion | bytes 2097152 | tf_op jit(solution)/shard_map/slice | solution.py:460
  3.1 1.7 %dynamic-slice_bitcast_fusion.1 = bf16[128,1024]{1,0:T(8,128)(2,1)} fusion(bf16[1,1,128,2048]{3,2,1,0:T(8,128)(2,1)} %get-tuple-element.93, s32[]{:T(128)S(6)} %select_n.14), kind=kLoop, calls=%fused_computation.1 | loop fusion | bytes 524292 | tf_op jit(solution)/shard_map/dynamic_slice | solution.py:459
  4.8 2.9 %collective-permute-start = (bf16[128,1024]{1,0:T(8,128)(2,1)}, bf16[128,1024]{1,0:T(8,128)(2,1)}, u32[]{:S(2)}, u32[]{:S(2)}) collective-permute-start(bf16[128,1024]{1,0:T(8,128)(2,1)} %dynamic-slice_bitcast_fusion.1), channel_id=1, source_target_pairs={{0,2},{2,0},{1,3},{3,1},{4,6},{6,4},{5,7},{7,5},{8,10},{10,8},{9,1... | collective-permute-start | bytes 786440 | tf_op jit(solution)/shard_map/ppermute | solution.py:27
  7.7 1.7 %dynamic-slice_bitcast_fusion = bf16[128,1024]{1,0:T(8,128)(2,1)} fusion(bf16[1,1,128,2048]{3,2,1,0:T(8,128)(2,1)} %get-tuple-element.92, s32[]{:T(128)S(6)} %select_n.14), kind=kLoop, calls=%fused_computation | loop fusion | bytes 524292 | tf_op jit(solution)/shard_map/dynamic_slice | solution.py:459
  16.7 1.9 %start.1 = (s32[128]{0:T(128)S(1)}, s32[1,64]{1,0:T(1,128)S(1)}, s32[1,64]{1,0:T(1,128)S(1)}, s32[1,64]{1,0:T(1,128)S(1)}, s32[1,64]{1,0:T(1,128)S(1)}, /*index=...) custom-call(s32[1]{0:T(128)S(6)} %copy.15.window_keep, s32[4]{0:T(128)S(1)} %copy-done.9, s32[4,1]{1,0:T(4,128)S(1)} %copy.14.pair_count, ...), custom_call_target="tpu_custom_call" | custom-call | flops 6291456 | bytes 6291456 | tf_op jit(solution)/shard_map/start/pallas_call | solution.py:87
  18.6 4.2 %collective-permute-start.1 = (s32[1,64]{1,0:T(1,128)S(1)}, s32[1,64]{1,0:T(1,128)S(1)}, u32[]{:S(2)}, u32[]{:S(2)}) collective-permute-start(s32[1,64]{1,0:T(1,128)S(1)} %get-tuple-element.49), channel_id=1, source_target_pairs={{0,12},{4,0},{8,4},{12,8},{1,13},{5,1},{9,5},{13,9},{2,14},{6,2},{... | collective-permute-start | bytes 776 | tf_op jit(solution)/shard_map/ppermute | solution.py:27
  24.1 3.1 %collective-permute-done.2.refs_4_.refs_2_ = s32[1,64]{1,0:T(1,128)S(1)} collective-permute-done((s32[1,64]{1,0:T(1,128)S(1)}, s32[1,64]{1,0:T(1,128)S(1)}, u32[]{:S(2)}, u32[]{:S(2)}) %collective-permute-start.2) | collective-permute-done | bytes 288 | tf_op jit(solution)/shard_map/ppermute | solution.py:27
  28.2 1.7 %rows.2 = (bf16[1,32,1024]{2,1,0:T(8,128)(2,1)S(1)}, bf16[1,32,1024]{2,1,0:T(8,128)(2,1)S(1)}, bf16[1,32,1024]{2,1,0:T(8,128)(2,1)S(1)}, bf16[1,32,1024]{2,1,0:T...) custom-call(s32[128]{0:T(128)S(1)} %get-tuple-element.47.scal.after,, ...), custom_call_target="tpu_custom_call" | custom-call | flops 402653184 | bytes 4194304 | tf_op jit(solution)/shard_map/rows/pallas_call | solution.py:147
  29.9 1.2 %collective-permute-start.5 = (bf16[1,32,1024]{2,1,0:T(8,128)(2,1)S(1)}, bf16[1,32,1024]{2,1,0:T(8,128)(2,1)S(1)}, u32[]{:S(2)}, u32[]{:S(2)}) collective-permute-start(bf16[1,32,1024]{2,1,0:T(8,128)(2,1)S(1)} %get-tuple-element.55), channel_id=1, source_target_pairs={{0,8},{4,12},{8,0},{12,4},{1,9},{5,13},{9,1},{13,5},{2,10},{6,14},... | collective-permute-start | bytes 196616 | tf_op jit(solution)/shard_map/ppermute | solution.py:27
  31.1 2.8 %collective-permute-start.6 = (bf16[1,32,1024]{2,1,0:T(8,128)(2,1)S(1)}, bf16[1,32,1024]{2,1,0:T(8,128)(2,1)S(1)}, u32[]{:S(2)}, u32[]{:S(2)}) collective-permute-start(bf16[1,32,1024]{2,1,0:T(8,128)(2,1)S(1)} %get-tuple-element.56), channel_id=1, source_target_pairs={{0,12},{4,0},{8,4},{12,8},{1,13},{5,1},{9,5},{13,9},{2,14},{6,2},{... | collective-permute-start | bytes 196616 | tf_op jit(solution)/shard_map/ppermute | solution.py:27
  34.0 1.3 %rows.3 = (bf16[1,32,1024]{2,1,0:T(8,128)(2,1)S(1)}, bf16[1,32,1024]{2,1,0:T(8,128)(2,1)S(1)}, bf16[1,32,1024]{2,1,0:T(8,128)(2,1)S(1)}, bf16[1,32,1024]{2,1,0:T...) custom-call(s32[128]{0:T(128)S(1)} %get-tuple-element.47.scal.after,, ...), custom_call_target="tpu_custom_call" | custom-call | flops 402653184 | bytes 4194304 | tf_op jit(solution)/shard_map/rows/pallas_call | solution.py:147
  35.6 1.5 %collective-permute-start.9 = (bf16[1,32,1024]{2,1,0:T(8,128)(2,1)S(1)}, bf16[1,32,1024]{2,1,0:T(8,128)(2,1)S(1)}, u32[]{:S(2)}, u32[]{:S(2)}) collective-permute-start(bf16[1,32,1024]{2,1,0:T(8,128)(2,1)S(1)} %get-tuple-element.63), channel_id=1, source_target_pairs={{0,8},{4,12},{8,0},{12,4},{1,9},{5,13},{9,1},{13,5},{2,10},{6,14},... | collective-permute-start | bytes 196616 | tf_op jit(solution)/shard_map/ppermute | solution.py:27
  37.2 2.8 %collective-permute-start.10 = (bf16[1,32,1024]{2,1,0:T(8,128)(2,1)S(1)}, bf16[1,32,1024]{2,1,0:T(8,128)(2,1)S(1)}, u32[]{:S(2)}, u32[]{:S(2)}) collective-permute-start(bf16[1,32,1024]{2,1,0:T(8,128)(2,1)S(1)} %get-tuple-element.64), channel_id=1, source_target_pairs={{0,12},{4,0},{8,4},{12,8},{1,13},{5,1},{9,5},{13,9},{2,14},{6,2},{... | collective-permute-start | bytes 196616 | tf_op jit(solution)/shard_map/ppermute | solution.py:27
  40.0 1.4 %collective-permute-done.8.refs_5_ = bf16[1,32,1024]{2,1,0:T(8,128)(2,1)S(1)} collective-permute-done((bf16[1,32,1024]{2,1,0:T(8,128)(2,1)S(1)}, bf16[1,32,1024]{2,1,0:T(8,128)(2,1)S(1)}, u32[]{:S(2)}, u32[]{:S(2)}) %collective-permute-start.8) | collective-permute-done | bytes 65568 | tf_op jit(solution)/shard_map/ppermute | solution.py:27
  42.3 3.0 %lags.2 = (f32[2,128,1024]{2,1,0:T(8,128)S(1)}, bf16[2,128,1024]{2,1,0:T(8,128)(2,1)S(1)}) custom-call(s32[128]{0:T(128)S(1)} %get-tuple-element.47.scal.after, f32[1]{0:T(128)} %constant.32.clone.1.weight, s32[128]{0:T(128)S(1)} %get-tuple-element.47.scal.after, bf16[1,32,1024]{2,1,0:T(8,128)(2,1)S(1)} %get-tuple-element.53.refs_0_, ...), custom_call_target="tpu_custom_call" | custom-call | flops 1073741824 | bytes 8388608 | tf_op jit(solution)/shard_map/lags/pallas_call | solution.py:242
  45.4 1.7 %collective-permute-start.16 = (bf16[1,2,32,1024]{3,2,1,0:T(8,128)(2,1)S(1)}, bf16[1,2,32,1024]{3,2,1,0:T(8,128)(2,1)S(1)}, u32[]{:S(2)}, u32[]{:S(2)}) collective-permute-start(bf16[1,2,32,1024]{3,2,1,0:T(8,128)(2,1)S(1)} %get-tuple-element.75), channel_id=1, source_target_pairs={{0,4},{4,8},{8,12},{12,0},{1,5},{5,9},{9,13},{13,1},{2,6},{6,10},{... | collective-permute-start | bytes 393224 | tf_op jit(solution)/shard_map/ppermute | solution.py:27
  47.1 2.7 %collective-permute-start.17 = (bf16[1,2,32,1024]{3,2,1,0:T(8,128)(2,1)S(1)}, bf16[1,2,32,1024]{3,2,1,0:T(8,128)(2,1)S(1)}, u32[]{:S(2)}, u32[]{:S(2)}) collective-permute-start(bf16[1,2,32,1024]{3,2,1,0:T(8,128)(2,1)S(1)} %get-tuple-element.76), channel_id=1, source_target_pairs={{0,8},{4,12},{8,0},{12,4},{1,9},{5,13},{9,1},{13,5},{2,10},{6,14},... | collective-permute-start | bytes 393224 | tf_op jit(solution)/shard_map/ppermute | solution.py:27
  50.6 3.2 %collective-permute-done.16.refs_1_ = bf16[1,2,32,1024]{3,2,1,0:T(8,128)(2,1)S(1)} collective-permute-done((bf16[1,2,32,1024]{3,2,1,0:T(8,128)(2,1)S(1)}, bf16[1,2,32,1024]{3,2,1,0:T(8,128)(2,1)S(1)}, u32[]{:S(2)}, u32[]{:S(2)}) %collective-permute-start.16) | collective-permute-done | bytes 131104 | tf_op jit(solution)/shard_map/ppermute | solution.py:27
  53.7 5.3 %collective-permute-done.17.refs_2_ = bf16[1,2,32,1024]{3,2,1,0:T(8,128)(2,1)S(1)} collective-permute-done((bf16[1,2,32,1024]{3,2,1,0:T(8,128)(2,1)S(1)}, bf16[1,2,32,1024]{3,2,1,0:T(8,128)(2,1)S(1)}, u32[]{:S(2)}, u32[]{:S(2)}) %collective-permute-start.17) | collective-permute-done | bytes 131104 | tf_op jit(solution)/shard_map/ppermute | solution.py:27
  59.0 3.0 %lags.3 = (f32[2,128,1024]{2,1,0:T(8,128)S(1)}, bf16[2,128,1024]{2,1,0:T(8,128)(2,1)S(1)}) custom-call(s32[128]{0:T(128)S(1)} %get-tuple-element.47.scal.after, f32[1]{0:T(128)} %constant.32.clone.1.weight, f32[128,1024]{1,0:T(8,128)S(1)} %get-tuple-element.70.refs_0_.after, bf16[1,2,32,1024]{3,2,1,0:T(8,128)(2,1)S(1)} %get-tuple-element.74.refs_0_, ...), custom_call_target="tpu_custom_call" | custom-call | flops 1073741824 | bytes 8388608 | tf_op jit(solution)/shard_map/lags/pallas_call | solution.py:242
  62.1 1.6 %collective-permute-start.12 = (bf16[128,1024]{1,0:T(8,128)(2,1)S(1)}, bf16[128,1024]{1,0:T(8,128)(2,1)S(1)}, u32[]{:S(2)}, u32[]{:S(2)}) collective-permute-start(bf16[128,1024]{1,0:T(8,128)(2,1)S(1)} %get-tuple-element.71), channel_id=1, source_target_pairs={{0,2},{2,0},{1,3},{3,1},{4,6},{6,4},{5,7},{7,5},{8,10},{10,8},{9,1... | collective-permute-start | bytes 786440 | tf_op jit(solution)/shard_map/ppermute | solution.py:27
  64.7 1.6 %collective-permute-start.20 = (bf16[128,1024]{1,0:T(8,128)(2,1)S(1)}, bf16[128,1024]{1,0:T(8,128)(2,1)S(1)}, u32[]{:S(2)}, u32[]{:S(2)}) collective-permute-start(bf16[128,1024]{1,0:T(8,128)(2,1)S(1)} %get-tuple-element.81), channel_id=1, source_target_pairs={{0,2},{2,0},{1,3},{3,1},{4,6},{6,4},{5,7},{7,5},{8,10},{10,8},{9,1... | collective-permute-start | bytes 786440 | tf_op jit(solution)/shard_map/ppermute | solution.py:27
  66.3 5.0 %collective-permute-done.12.refs_1_ = bf16[128,1024]{1,0:T(8,128)(2,1)S(1)} collective-permute-done((bf16[128,1024]{1,0:T(8,128)(2,1)S(1)}, bf16[128,1024]{1,0:T(8,128)(2,1)S(1)}, u32[]{:S(2)}, u32[]{:S(2)}) %collective-permute-start.12) | collective-permute-done | bytes 262176 | tf_op jit(solution)/shard_map/ppermute | solution.py:27
  72.4 1.3 %collective-permute-start.14 = (f32[8,128]{1,0:T(8,128)S(1)}, f32[8,128]{1,0:T(8,128)S(1)}, u32[]{:S(2)}, u32[]{:S(2)}) collective-permute-start(f32[8,128]{1,0:T(8,128)S(1)} %get-tuple-element.72.refs_0_), channel_id=1, source_target_pairs={{0,2},{1,3},{2,0},{3,1},{4,6},{5,7},{6,4},{7,5},{8,10},{9,11},{10,... | collective-permute-start | bytes 12296 | tf_op jit(solution)/shard_map/ppermute | solution.py:27
  73.8 1.8 %collective-permute-done.15.refs_3_ = f32[8,128]{1,0:T(8,128)S(1)} collective-permute-done((f32[8,128]{1,0:T(8,128)S(1)}, f32[8,128]{1,0:T(8,128)S(1)}, u32[]{:S(2)}, u32[]{:S(2)}) %collective-permute-start.15) | collective-permute-done | bytes 4128 | tf_op jit(solution)/shard_map/ppermute | solution.py:27
  77.5 3.0 %collective-permute-start.24 = (bf16[32,1024]{1,0:T(8,128)(2,1)S(1)}, bf16[32,1024]{1,0:T(8,128)(2,1)S(1)}, u32[]{:S(2)}, u32[]{:S(2)}) collective-permute-start(bf16[32,1024]{1,0:T(8,128)(2,1)S(1)} %get-tuple-element.86), channel_id=1, source_target_pairs={{0,12},{4,0},{8,4},{12,8},{1,13},{5,1},{9,5},{13,9},{2,14},{6,2},{... | collective-permute-start | bytes 196616 | tf_op jit(solution)/shard_map/ppermute | solution.py:27
  83.0 1.8 %collective-permute-start.26 = (bf16[32,1024]{1,0:T(8,128)(2,1)S(1)}, bf16[32,1024]{1,0:T(8,128)(2,1)S(1)}, u32[]{:S(2)}, u32[]{:S(2)}) collective-permute-start(bf16[32,1024]{1,0:T(8,128)(2,1)S(1)} %get-tuple-element.88), channel_id=1, source_target_pairs={{0,8},{4,12},{8,0},{12,4},{1,9},{5,13},{9,1},{13,5},{2,10},{6,14},... | collective-permute-start | bytes 196616 | tf_op jit(solution)/shard_map/ppermute | solution.py:27
  86.7 2.8 %collective-permute-start.25 = (bf16[32,1024]{1,0:T(8,128)(2,1)S(1)}, bf16[32,1024]{1,0:T(8,128)(2,1)S(1)}, u32[]{:S(2)}, u32[]{:S(2)}) collective-permute-start(bf16[32,1024]{1,0:T(8,128)(2,1)S(1)} %get-tuple-element.87), channel_id=1, source_target_pairs={{0,12},{4,0},{8,4},{12,8},{1,13},{5,1},{9,5},{13,9},{2,14},{6,2},{... | collective-permute-start | bytes 196616 | tf_op jit(solution)/shard_map/ppermute | solution.py:27
  89.5 1.1 %collective-permute-start.29 = (bf16[32,1024]{1,0:T(8,128)(2,1)S(1)}, bf16[32,1024]{1,0:T(8,128)(2,1)S(1)}, u32[]{:S(2)}, u32[]{:S(2)}) collective-permute-start(bf16[32,1024]{1,0:T(8,128)(2,1)S(1)} %get-tuple-element.91), channel_id=1, source_target_pairs={{0,4},{4,8},{8,12},{12,0},{1,5},{5,9},{9,13},{13,1},{2,6},{6,10},{... | collective-permute-start | bytes 196616 | tf_op jit(solution)/shard_map/ppermute | solution.py:27
  90.6 2.6 %normed.1 = f32[4,64,1024]{2,1,0:T(8,128)} custom-call(s32[128]{0:T(128)S(1)} %get-tuple-element.47.scal.after, f32[8,128]{1,0:T(8,128)S(1)} %get-tuple-element.72.refs_0_, f32[8,128]{1,0:T(8,128)S(1)} %collective-permute-done.13.refs_1_, f32[8,128]{1,0:T(8,128)S(1)} %collective-permute-done.14.refs_2_, f32[8,128]{1,0:T(8,128)S(1)} %collective-permute-done.15.refs_3_, ...), custom_call_target="tpu_custom_call" | custom-call | flops 524288 | bytes 2097152 | tf_op jit(solution)/shard_map/normed/pallas_call | solution.py:401
  93.2 4.1 %collective-permute-done.27.refs_9_ = bf16[32,1024]{1,0:T(8,128)(2,1)S(1)} collective-permute-done((bf16[32,1024]{1,0:T(8,128)(2,1)S(1)}, bf16[32,1024]{1,0:T(8,128)(2,1)S(1)}, u32[]{:S(2)}, u32[]{:S(2)}) %collective-permute-start.27) | collective-permute-done | bytes 65568 | tf_op jit(solution)/shard_map/ppermute | solution.py:27
  97.2 1.1 %adjoint.1 = f32[128,1024]{1,0:T(8,128)} custom-call(s32[1,64]{1,0:T(1,128)S(1)} %get-tuple-element.48.refs_2_.refs_0_, s32[1,64]{1,0:T(1,128)S(1)} %collective-permute-done.1.refs_3_.refs_1_, s32[1,64]{1,0:T(1,128)S(1)} %collective-permute-done.2.refs_4_.refs_2_, s32[1,64]{1,0:T(1,128)S(1)} %collective-permute-done.3.refs_5_.refs_3_, ...), custom_call_target="tpu_custom_call" | custom-call | flops 67108864 | bytes 1048576 | tf_op jit(solution)/shard_map/adjoint/pallas_call | solution.py:427
  (65 shorter events, 19.6 us)
Async XLA Ops:
  0.6 27.5 %copy-start.2 = (bf16[1024,1024]{1,0:T(8,128)(2,1)S(1)}, bf16[1024,1024]{1,0:T(8,128)(2,1)}, u32[]{:S(2)}) copy-start(bf16[1024,1024]{1,0:T(8,128)(2,1)} %constant.43.clone.refs_1_) | copy-start | bytes 6291460
  0.6 27.5 %copy-start.1 = (bf16[1,2,128,2048]{3,2,1,0:T(8,128)(2,1)S(1)}, bf16[1,2,128,2048]{3,2,1,0:T(8,128)(2,1)}, u32[]{:S(2)}) copy-start(bf16[1,2,128,2048]{3,2,1,0:T(8,128)(2,1)} %spectra.3) | copy-start | bytes 3145732
  4.8 23.4 %collective-permute-start = (bf16[128,1024]{1,0:T(8,128)(2,1)}, bf16[128,1024]{1,0:T(8,128)(2,1)}, u32[]{:S(2)}, u32[]{:S(2)}) collective-permute-start(bf16[128,1024]{1,0:T(8,128)(2,1)} %dynamic-slice_bitcast_fusion.1), channel_id=1, source_target_pairs={{0,2},{2,0},{1,3},{3,1},{4,6},{6,4},{5,7},{7,5},{8,10},{10,8},{9,1... | collective-permute-start | bytes 786440 | tf_op jit(solution)/shard_map/ppermute | solution.py:27
  9.4 24.6 %collective-permute-start.7 = (bf16[128,1024]{1,0:T(8,128)(2,1)}, bf16[128,1024]{1,0:T(8,128)(2,1)S(1)}, u32[]{:S(2)}, u32[]{:S(2)}) collective-permute-start(bf16[128,1024]{1,0:T(8,128)(2,1)} %dynamic-slice_bitcast_fusion), channel_id=1, source_target_pairs={{0,2},{2,0},{1,3},{3,1},{4,6},{6,4},{5,7},{7,5},{8,10},{10,8},{9,1... | collective-permute-start | bytes 786440 | tf_op jit(solution)/shard_map/ppermute | solution.py:27
  18.6 5.5 %collective-permute-start.1 = (s32[1,64]{1,0:T(1,128)S(1)}, s32[1,64]{1,0:T(1,128)S(1)}, u32[]{:S(2)}, u32[]{:S(2)}) collective-permute-start(s32[1,64]{1,0:T(1,128)S(1)} %get-tuple-element.49), channel_id=1, source_target_pairs={{0,12},{4,0},{8,4},{12,8},{1,13},{5,1},{9,5},{13,9},{2,14},{6,2},{... | collective-permute-start | bytes 776 | tf_op jit(solution)/shard_map/ppermute | solution.py:27
  22.8 4.4 %collective-permute-start.2 = (s32[1,64]{1,0:T(1,128)S(1)}, s32[1,64]{1,0:T(1,128)S(1)}, u32[]{:S(2)}, u32[]{:S(2)}) collective-permute-start(s32[1,64]{1,0:T(1,128)S(1)} %get-tuple-element.50), channel_id=1, source_target_pairs={{0,8},{4,12},{8,0},{12,4},{1,9},{5,13},{9,1},{13,5},{2,10},{6,14},... | collective-permute-start | bytes 776 | tf_op jit(solution)/shard_map/ppermute | solution.py:27
  22.8 5.3 %collective-permute-start.3 = (s32[1,64]{1,0:T(1,128)S(1)}, s32[1,64]{1,0:T(1,128)S(1)}, u32[]{:S(2)}, u32[]{:S(2)}) collective-permute-start(s32[1,64]{1,0:T(1,128)S(1)} %get-tuple-element.51), channel_id=1, source_target_pairs={{0,4},{4,8},{8,12},{12,0},{1,5},{5,9},{9,13},{13,1},{2,6},{6,10},{... | collective-permute-start | bytes 776 | tf_op jit(solution)/shard_map/ppermute | solution.py:27
  29.9 7.3 %collective-permute-start.4 = (bf16[1,32,1024]{2,1,0:T(8,128)(2,1)S(1)}, bf16[1,32,1024]{2,1,0:T(8,128)(2,1)S(1)}, u32[]{:S(2)}, u32[]{:S(2)}) collective-permute-start(bf16[1,32,1024]{2,1,0:T(8,128)(2,1)S(1)} %get-tuple-element.54), channel_id=1, source_target_pairs={{0,4},{4,8},{8,12},{12,0},{1,5},{5,9},{9,13},{13,1},{2,6},{6,10},{... | collective-permute-start | bytes 196616 | tf_op jit(solution)/shard_map/ppermute | solution.py:27
  29.9 10.1 %collective-permute-start.5 = (bf16[1,32,1024]{2,1,0:T(8,128)(2,1)S(1)}, bf16[1,32,1024]{2,1,0:T(8,128)(2,1)S(1)}, u32[]{:S(2)}, u32[]{:S(2)}) collective-permute-start(bf16[1,32,1024]{2,1,0:T(8,128)(2,1)S(1)} %get-tuple-element.55), channel_id=1, source_target_pairs={{0,8},{4,12},{8,0},{12,4},{1,9},{5,13},{9,1},{13,5},{2,10},{6,14},... | collective-permute-start | bytes 196616 | tf_op jit(solution)/shard_map/ppermute | solution.py:27
  31.1 8.9 %collective-permute-start.6 = (bf16[1,32,1024]{2,1,0:T(8,128)(2,1)S(1)}, bf16[1,32,1024]{2,1,0:T(8,128)(2,1)S(1)}, u32[]{:S(2)}, u32[]{:S(2)}) collective-permute-start(bf16[1,32,1024]{2,1,0:T(8,128)(2,1)S(1)} %get-tuple-element.56), channel_id=1, source_target_pairs={{0,12},{4,0},{8,4},{12,8},{1,13},{5,1},{9,5},{13,9},{2,14},{6,2},{... | collective-permute-start | bytes 196616 | tf_op jit(solution)/shard_map/ppermute | solution.py:27
  35.3 6.2 %collective-permute-start.8 = (bf16[1,32,1024]{2,1,0:T(8,128)(2,1)S(1)}, bf16[1,32,1024]{2,1,0:T(8,128)(2,1)S(1)}, u32[]{:S(2)}, u32[]{:S(2)}) collective-permute-start(bf16[1,32,1024]{2,1,0:T(8,128)(2,1)S(1)} %get-tuple-element.62), channel_id=1, source_target_pairs={{0,4},{4,8},{8,12},{12,0},{1,5},{5,9},{9,13},{13,1},{2,6},{6,10},{... | collective-permute-start | bytes 196616 | tf_op jit(solution)/shard_map/ppermute | solution.py:27
  35.6 6.7 %collective-permute-start.9 = (bf16[1,32,1024]{2,1,0:T(8,128)(2,1)S(1)}, bf16[1,32,1024]{2,1,0:T(8,128)(2,1)S(1)}, u32[]{:S(2)}, u32[]{:S(2)}) collective-permute-start(bf16[1,32,1024]{2,1,0:T(8,128)(2,1)S(1)} %get-tuple-element.63), channel_id=1, source_target_pairs={{0,8},{4,12},{8,0},{12,4},{1,9},{5,13},{9,1},{13,5},{2,10},{6,14},... | collective-permute-start | bytes 196616 | tf_op jit(solution)/shard_map/ppermute | solution.py:27
  37.2 5.1 %collective-permute-start.10 = (bf16[1,32,1024]{2,1,0:T(8,128)(2,1)S(1)}, bf16[1,32,1024]{2,1,0:T(8,128)(2,1)S(1)}, u32[]{:S(2)}, u32[]{:S(2)}) collective-permute-start(bf16[1,32,1024]{2,1,0:T(8,128)(2,1)S(1)} %get-tuple-element.64), channel_id=1, source_target_pairs={{0,12},{4,0},{8,4},{12,8},{1,13},{5,1},{9,5},{13,9},{2,14},{6,2},{... | collective-permute-start | bytes 196616 | tf_op jit(solution)/shard_map/ppermute | solution.py:27
  45.3 4.5 %collective-permute-start.11 = (bf16[2,128,1024]{2,1,0:T(8,128)(2,1)S(1)}, bf16[2,128,1024]{2,1,0:T(8,128)(2,1)S(1)}, u32[]{:S(2)}, u32[]{:S(2)}) collective-permute-start(bf16[2,128,1024]{2,1,0:T(8,128)(2,1)S(1)} %get-tuple-element.69), channel_id=1, source_target_pairs={{0,1},{1,0},{2,3},{3,2},{4,5},{5,4},{6,7},{7,6},{8,9},{9,8},{10,11... | collective-permute-start | bytes 1572872 | tf_op jit(solution)/shard_map/ppermute | solution.py:27
  45.4 8.3 %collective-permute-start.16 = (bf16[1,2,32,1024]{3,2,1,0:T(8,128)(2,1)S(1)}, bf16[1,2,32,1024]{3,2,1,0:T(8,128)(2,1)S(1)}, u32[]{:S(2)}, u32[]{:S(2)}) collective-permute-start(bf16[1,2,32,1024]{3,2,1,0:T(8,128)(2,1)S(1)} %get-tuple-element.75), channel_id=1, source_target_pairs={{0,4},{4,8},{8,12},{12,0},{1,5},{5,9},{9,13},{13,1},{2,6},{6,10},{... | collective-permute-start | bytes 393224 | tf_op jit(solution)/shard_map/ppermute | solution.py:27
  47.1 11.9 %collective-permute-start.17 = (bf16[1,2,32,1024]{3,2,1,0:T(8,128)(2,1)S(1)}, bf16[1,2,32,1024]{3,2,1,0:T(8,128)(2,1)S(1)}, u32[]{:S(2)}, u32[]{:S(2)}) collective-permute-start(bf16[1,2,32,1024]{3,2,1,0:T(8,128)(2,1)S(1)} %get-tuple-element.76), channel_id=1, source_target_pairs={{0,8},{4,12},{8,0},{12,4},{1,9},{5,13},{9,1},{13,5},{2,10},{6,14},... | collective-permute-start | bytes 393224 | tf_op jit(solution)/shard_map/ppermute | solution.py:27
  49.8 9.2 %collective-permute-start.18 = (bf16[1,2,32,1024]{3,2,1,0:T(8,128)(2,1)S(1)}, bf16[1,2,32,1024]{3,2,1,0:T(8,128)(2,1)S(1)}, u32[]{:S(2)}, u32[]{:S(2)}) collective-permute-start(bf16[1,2,32,1024]{3,2,1,0:T(8,128)(2,1)S(1)} %get-tuple-element.77), channel_id=1, source_target_pairs={{0,12},{4,0},{8,4},{12,8},{1,13},{5,1},{9,5},{13,9},{2,14},{6,2},{... | collective-permute-start | bytes 393224 | tf_op jit(solution)/shard_map/ppermute | solution.py:27
  62.0 2.0 %collective-permute-start.19 = (bf16[2,128,1024]{2,1,0:T(8,128)(2,1)S(1)}, bf16[2,128,1024]{2,1,0:T(8,128)(2,1)S(1)}, u32[]{:S(2)}, u32[]{:S(2)}) collective-permute-start(bf16[2,128,1024]{2,1,0:T(8,128)(2,1)S(1)} %get-tuple-element.79), channel_id=1, source_target_pairs={{0,1},{1,0},{2,3},{3,2},{4,5},{5,4},{6,7},{7,6},{8,9},{9,8},{10,11... | collective-permute-start | bytes 1572872 | tf_op jit(solution)/shard_map/ppermute | solution.py:27
  62.1 9.2 %collective-permute-start.12 = (bf16[128,1024]{1,0:T(8,128)(2,1)S(1)}, bf16[128,1024]{1,0:T(8,128)(2,1)S(1)}, u32[]{:S(2)}, u32[]{:S(2)}) collective-permute-start(bf16[128,1024]{1,0:T(8,128)(2,1)S(1)} %get-tuple-element.71), channel_id=1, source_target_pairs={{0,2},{2,0},{1,3},{3,1},{4,6},{6,4},{5,7},{7,5},{8,10},{10,8},{9,1... | collective-permute-start | bytes 786440 | tf_op jit(solution)/shard_map/ppermute | solution.py:27
  64.7 15.8 %collective-permute-start.20 = (bf16[128,1024]{1,0:T(8,128)(2,1)S(1)}, bf16[128,1024]{1,0:T(8,128)(2,1)S(1)}, u32[]{:S(2)}, u32[]{:S(2)}) collective-permute-start(bf16[128,1024]{1,0:T(8,128)(2,1)S(1)} %get-tuple-element.81), channel_id=1, source_target_pairs={{0,2},{2,0},{1,3},{3,1},{4,6},{6,4},{5,7},{7,5},{8,10},{10,8},{9,1... | collective-permute-start | bytes 786440 | tf_op jit(solution)/shard_map/ppermute | solution.py:27
  72.0 3.6 %collective-permute-start.15 = (f32[8,128]{1,0:T(8,128)S(1)}, f32[8,128]{1,0:T(8,128)S(1)}, u32[]{:S(2)}, u32[]{:S(2)}) collective-permute-start(f32[8,128]{1,0:T(8,128)S(1)} %get-tuple-element.72.refs_0_), channel_id=1, source_target_pairs={{0,3},{1,0},{2,1},{3,2},{4,7},{5,4},{6,5},{7,6},{8,11},{9,8},{10,9... | collective-permute-start | bytes 12296 | tf_op jit(solution)/shard_map/ppermute | solution.py:27
  72.4 4.2 %collective-permute-start.14 = (f32[8,128]{1,0:T(8,128)S(1)}, f32[8,128]{1,0:T(8,128)S(1)}, u32[]{:S(2)}, u32[]{:S(2)}) collective-permute-start(f32[8,128]{1,0:T(8,128)S(1)} %get-tuple-element.72.refs_0_), channel_id=1, source_target_pairs={{0,2},{1,3},{2,0},{3,1},{4,6},{5,7},{6,4},{7,5},{8,10},{9,11},{10,... | collective-permute-start | bytes 12296 | tf_op jit(solution)/shard_map/ppermute | solution.py:27
  73.7 3.0 %collective-permute-start.13 = (f32[8,128]{1,0:T(8,128)S(1)}, f32[8,128]{1,0:T(8,128)S(1)}, u32[]{:S(2)}, u32[]{:S(2)}) collective-permute-start(f32[8,128]{1,0:T(8,128)S(1)} %get-tuple-element.72.refs_0_), channel_id=1, source_target_pairs={{0,1},{1,2},{2,3},{3,0},{4,5},{5,6},{6,7},{7,4},{8,9},{9,10},{10,1... | collective-permute-start | bytes 12296 | tf_op jit(solution)/shard_map/ppermute | solution.py:27
  77.5 12.0 %collective-permute-start.24 = (bf16[32,1024]{1,0:T(8,128)(2,1)S(1)}, bf16[32,1024]{1,0:T(8,128)(2,1)S(1)}, u32[]{:S(2)}, u32[]{:S(2)}) collective-permute-start(bf16[32,1024]{1,0:T(8,128)(2,1)S(1)} %get-tuple-element.86), channel_id=1, source_target_pairs={{0,12},{4,0},{8,4},{12,8},{1,13},{5,1},{9,5},{13,9},{2,14},{6,2},{... | collective-permute-start | bytes 196616 | tf_op jit(solution)/shard_map/ppermute | solution.py:27
  81.3 3.5 %collective-permute-start.23 = (f32[8,128]{1,0:T(8,128)S(1)}, f32[8,128]{1,0:T(8,128)S(1)}, u32[]{:S(2)}, u32[]{:S(2)}) collective-permute-start(f32[8,128]{1,0:T(8,128)S(1)} %get-tuple-element.82.refs_5_.refs_0_), channel_id=1, source_target_pairs={{0,3},{1,0},{2,1},{3,2},{4,7},{5,4},{6,5},{7,6},{8,11},{9,8},{10,9... | collective-permute-start | bytes 12296 | tf_op jit(solution)/shard_map/ppermute | solution.py:27
  82.1 3.6 %collective-permute-start.22 = (f32[8,128]{1,0:T(8,128)S(1)}, f32[8,128]{1,0:T(8,128)S(1)}, u32[]{:S(2)}, u32[]{:S(2)}) collective-permute-start(f32[8,128]{1,0:T(8,128)S(1)} %get-tuple-element.82.refs_5_.refs_0_), channel_id=1, source_target_pairs={{0,2},{1,3},{2,0},{3,1},{4,6},{5,7},{6,4},{7,5},{8,10},{9,11},{10,... | collective-permute-start | bytes 12296 | tf_op jit(solution)/shard_map/ppermute | solution.py:27
  82.8 3.0 %collective-permute-start.21 = (f32[8,128]{1,0:T(8,128)S(1)}, f32[8,128]{1,0:T(8,128)S(1)}, u32[]{:S(2)}, u32[]{:S(2)}) collective-permute-start(f32[8,128]{1,0:T(8,128)S(1)} %get-tuple-element.82.refs_5_.refs_0_), channel_id=1, source_target_pairs={{0,1},{1,2},{2,3},{3,0},{4,5},{5,6},{6,7},{7,4},{8,9},{9,10},{10,1... | collective-permute-start | bytes 12296 | tf_op jit(solution)/shard_map/ppermute | solution.py:27
  83.0 10.2 %collective-permute-start.26 = (bf16[32,1024]{1,0:T(8,128)(2,1)S(1)}, bf16[32,1024]{1,0:T(8,128)(2,1)S(1)}, u32[]{:S(2)}, u32[]{:S(2)}) collective-permute-start(bf16[32,1024]{1,0:T(8,128)(2,1)S(1)} %get-tuple-element.88), channel_id=1, source_target_pairs={{0,8},{4,12},{8,0},{12,4},{1,9},{5,13},{9,1},{13,5},{2,10},{6,14},... | collective-permute-start | bytes 196616 | tf_op jit(solution)/shard_map/ppermute | solution.py:27
  84.8 8.4 %collective-permute-start.28 = (bf16[32,1024]{1,0:T(8,128)(2,1)S(1)}, bf16[32,1024]{1,0:T(8,128)(2,1)S(1)}, u32[]{:S(2)}, u32[]{:S(2)}) collective-permute-start(bf16[32,1024]{1,0:T(8,128)(2,1)S(1)} %get-tuple-element.90), channel_id=1, source_target_pairs={{0,4},{4,8},{8,12},{12,0},{1,5},{5,9},{9,13},{13,1},{2,6},{6,10},{... | collective-permute-start | bytes 196616 | tf_op jit(solution)/shard_map/ppermute | solution.py:27
  86.7 6.5 %collective-permute-start.25 = (bf16[32,1024]{1,0:T(8,128)(2,1)S(1)}, bf16[32,1024]{1,0:T(8,128)(2,1)S(1)}, u32[]{:S(2)}, u32[]{:S(2)}) collective-permute-start(bf16[32,1024]{1,0:T(8,128)(2,1)S(1)} %get-tuple-element.87), channel_id=1, source_target_pairs={{0,12},{4,0},{8,4},{12,8},{1,13},{5,1},{9,5},{13,9},{2,14},{6,2},{... | collective-permute-start | bytes 196616 | tf_op jit(solution)/shard_map/ppermute | solution.py:27
  89.5 7.7 %collective-permute-start.27 = (bf16[32,1024]{1,0:T(8,128)(2,1)S(1)}, bf16[32,1024]{1,0:T(8,128)(2,1)S(1)}, u32[]{:S(2)}, u32[]{:S(2)}) collective-permute-start(bf16[32,1024]{1,0:T(8,128)(2,1)S(1)} %get-tuple-element.89), channel_id=1, source_target_pairs={{0,8},{4,12},{8,0},{12,4},{1,9},{5,13},{9,1},{13,5},{2,10},{6,14},... | collective-permute-start | bytes 196616 | tf_op jit(solution)/shard_map/ppermute | solution.py:27
  89.5 7.7 %collective-permute-start.29 = (bf16[32,1024]{1,0:T(8,128)(2,1)S(1)}, bf16[32,1024]{1,0:T(8,128)(2,1)S(1)}, u32[]{:S(2)}, u32[]{:S(2)}) collective-permute-start(bf16[32,1024]{1,0:T(8,128)(2,1)S(1)} %get-tuple-element.91), channel_id=1, source_target_pairs={{0,4},{4,8},{8,12},{12,0},{1,5},{5,9},{9,13},{13,1},{2,6},{6,10},{... | collective-permute-start | bytes 196616 | tf_op jit(solution)/shard_map/ppermute | solution.py:27
  (8 other events, 26.6 us)

commit v4 on v3

--- a/solution.py
+++ b/solution.py
@@ -21,51 +21,55 @@
 SMEM = pl.BlockSpec(memory_space=pltpu.SMEM)
 
 
-def shifted(value, axis, size, shift):
-    if shift % size == 0:
+def swapped(value, axis, size, step):
+    assert size & (size - 1) == 0
+    if step == 0:
         return value
-    return lax.ppermute(value, axis, [(i, (i + shift) % size) for i in range(size)])
+    return lax.ppermute(value, axis, [(i, i ^ step) for i in range(size)])
 
 
 def params(mib):
     return pltpu.CompilerParams(vmem_limit_bytes=mib * MIB)
 
 
-def cost(flops, mib):
-    return pl.CostEstimate(flops=int(flops), bytes_accessed=int(mib * MIB), transcendentals=0)
+SMALL = pl.CostEstimate(flops=1, bytes_accessed=1, transcendentals=0)
 
 
 def tables(classes, span, period, bins_dev, columns, cores):
     u = np.arange(span, dtype=np.int64)[None, :]
     first = np.arange(columns * cores, dtype=np.int64)[:, None] * (bins_dev // columns)
-    rows = (first + np.arange(classes)).reshape(-1, 1)
-    base = classes * np.arange(LANES, dtype=np.int64)[:, None]
-    out = []
-    for f in (rows, base):
-        angle = (f * u % period) * (2.0 * math.pi / period)
-        out += [np.cos(angle).astype(np.float32), np.sin(angle).astype(np.float32)]
-    return [jnp.asarray(t) for t in out]
-
-
-def start_kernel(blocks, direct, classes, window_keep, owners, pair_count, src, rec, *refs):
-    row_cos, row_sin, base_cos, base_sin = refs[:4]
-    scal, wanted, rec_ids, table = refs[4], refs[5:-2], refs[-2], refs[-1]
-    place, places = lax.axis_index("recv"), lax.axis_size("recv")
+    rows = (first + np.arange(classes)).reshape(-1)
+    high = 16 * classes * np.arange(LANES // 16, dtype=np.int64)
+    low = classes * np.arange(16, dtype=np.int64)
+    angle = (np.concatenate([rows, high, low])[:, None] * u % period) * (2.0 * math.pi / period)
+    return np.stack([np.cos(angle), np.sin(angle)]).astype(np.float32)
+
+
+def start_kernel(blocks, direct, classes, parts, *refs):
+    given, refs = refs[:6], refs[6:]
+    scal, wanted, rec_ids, table = refs[0], refs[1:-10], refs[-10], refs[-9]
+    held, base, sems = refs[-8:-2], refs[-2], refs[-1]
+    copies = [pltpu.make_async_copy(g, h, sems.at[i]) for i, (g, h) in enumerate(zip(given, held))]
+    for c in copies:
+        c.start()
+    for c in copies:
+        c.wait()
+    window_keep, owners, pair_count, src, rec, trig = held
+    place = lax.axis_index("recv")
     column, columns = lax.axis_index("win"), lax.axis_size("win")
     core = lax.axis_index("freq")
     scal[CORE] = core
     scal[COLUMN] = column
     scal[ORDER] = 1 - window_keep[0]
     for b in range(blocks):
-        unit = lax.rem(place - owners[b] + places, places) if direct else b
+        unit = place ^ owners[b] if direct else b
         scal[BLOCK + unit] = b
-        scal[COUNT + unit] = pair_count[b, 0]
+        scal[COUNT + unit] = pair_count[b]
     for d, out in enumerate(wanted):
-        owner = lax.rem(place - d + places, places)
         chosen = jnp.full(out.shape, -1, jnp.int32)
         received = jnp.zeros(out.shape, jnp.int32)
         for b in range(blocks):
-            mine = jnp.full(out.shape, owners[b], jnp.int32) == owner
+            mine = jnp.full(out.shape, owners[b], jnp.int32) == (place ^ d)
             chosen = jnp.where(mine, src[b : b + 1], chosen)
             received = jnp.where(mine, rec[b : b + 1], received)
         out[...] = chosen
@@ -73,31 +77,42 @@
             rec_ids[d : d + 1] = received
     if not direct:
         rec_ids[...] = rec[...]
+    rows = parts * classes
+    low = slice(rows + LANES // 16, rows + LANES // 16 + 16)
+    cl, sl = trig[0, low], trig[1, low]
+    for h in range(LANES // 16):
+        ch, sh = trig[0, rows + h : rows + h + 1], trig[1, rows + h : rows + h + 1]
+        base[0, 16 * h : 16 * h + 16] = ch * cl - sh * sl
+        base[1, 16 * h : 16 * h + 16] = sh * cl + ch * sl
     first = (core * columns + column) * classes
-    cb, sb = base_cos[...], base_sin[...]
+    cb, sb = base[0], base[1]
     for r in range(classes):
-        ca, sa = row_cos[pl.ds(first + r, 1)], row_sin[pl.ds(first + r, 1)]
+        ca, sa = trig[0, pl.ds(first + r, 1)], trig[1, pl.ds(first + r, 1)]
         table[r, :LANES] = (ca * cb - sa * sb).astype(BF16)
         table[r, LANES:] = (-(sa * cb + ca * sb)).astype(BF16)
 
 
-def start(window_keep, owners, pair_count, pair_src, pair_rec, places, trig, classes, span):
+def start(window_keep, owners, pair_count, pair_src, pair_rec, places, trig, classes, span, parts):
     blocks, slots = pair_src.shape
     ids = jax.ShapeDtypeStruct((1, slots), jnp.int32)
+    given = [window_keep, owners, pair_count[:, 0], pair_src, pair_rec, jnp.asarray(trig)]
     scal, *wanted, rec_ids, table = pl.pallas_call(
-        functools.partial(start_kernel, blocks, places == blocks, classes),
+        functools.partial(start_kernel, blocks, places == blocks, classes, parts),
         out_shape=[jax.ShapeDtypeStruct((LANES,), jnp.int32)]
         + [ids] * places
         + [
             jax.ShapeDtypeStruct(pair_rec.shape, jnp.int32),
             jax.ShapeDtypeStruct((classes, 2 * LANES, span), BF16),
         ],
-        in_specs=[SMEM] * 3 + [VMEM] * 6,
+        in_specs=[pl.BlockSpec(memory_space=pl.ANY)] * 6,
         out_specs=[SMEM] + [VMEM] * (places + 2),
+        scratch_shapes=[pltpu.SMEM(g.shape, g.dtype) for g in given[:3]]
+        + [pltpu.VMEM(g.shape, g.dtype) for g in given[3:]]
+        + [pltpu.VMEM((2, LANES, span), F32), pltpu.SemaphoreType.DMA((6,))],
         compiler_params=params(16),
-        cost_estimate=cost(6 * classes * LANES * span, 6),
+        cost_estimate=SMALL,
         name="start",
-    )(window_keep, owners, pair_count, pair_src, pair_rec, *trig)
+    )(*given)
     return scal, wanted, rec_ids, table
 
 
@@ -106,56 +121,48 @@
     return (lax.broadcasted_iota(jnp.int32, (channels, row.shape[1]), 0) == row).astype(BF16)
 
 
-def rows_kernel(half, used, sends, scal, spectra, *refs):
+def rows_kernel(used, sends, scal, spectra, *refs):
     held, refs = refs[:used], refs[used:]
     perm, src_ids, rec_ids, refs = refs[0], refs[1 : 1 + sends], refs[1 + sends], refs[2 + sends :]
-    early, refs = (refs[:sends], refs[sends:]) if half else (None, refs)
-    first, second, own_out = refs[:sends], refs[sends:-1], refs[-1]
-    units, _, slots, part = own_out.shape
-    some = first[0].shape[1]
+    chunks, own_out = refs[:-1], refs[-1]
+    units, _, _, slots, part = own_out.shape
+    some = slots // CHUNKS
     channels = spectra.shape[2]
     pick = picks(list(src_ids) + [rec_ids.at[d : d + 1] for d in range(units)], channels)
-    here = spectra[0, half, :, pl.ds(pl.multiple_of(scal[COLUMN] * part, part), part)]
+    bins = pl.ds(pl.multiple_of(scal[COLUMN] * part, part), part)
     for u in range(used):
-        x = here
-        for s in range(used):
-            x = jnp.where(scal[ORDER + u] == s + 1, held[s][...], x)
-        x = jnp.dot(x, perm[...], preferred_element_type=F32).astype(BF16)
-        y = lax.dot_general(
-            pick, x, (((0,), (0,)), ((), ())), preferred_element_type=F32
-        ).astype(BF16)
-        for d in range(sends):
-            at = d * slots
-            first[d][u] = y[at : at + some]
-            if half:
-                second[d][u, 0] = early[d][u]
-                second[d][u, 1] = y[at + some : at + slots]
-            else:
-                second[d][u] = y[at + some : at + slots]
-        for d in range(units):
-            at = (sends + d) * slots
-            own_out[d, u] = y[at : at + slots]
-
-
-def gather_rows(half, scal, spectra, held, perm, src_ids, rec_ids, early, some):
+        for half in range(2):
+            x = spectra[0, half, :, bins]
+            for s in range(used):
+                x = jnp.where(scal[ORDER + u] == s + 1, held[s][0, half], x)
+            x = jnp.dot(x, perm[...], preferred_element_type=F32).astype(BF16)
+            y = lax.dot_general(
+                pick, x, (((0,), (0,)), ((), ())), preferred_element_type=F32
+            ).astype(BF16)
+            for i, out in enumerate(chunks):
+                at = i % sends * slots + i // sends * some
+                out[u, half] = y[at : at + some]
+            for d in range(units):
+                at = (sends + d) * slots
+                own_out[d, u, half] = y[at : at + slots]
+
+
+def gather_rows(scal, spectra, held, perm, src_ids, rec_ids):
     used, sends = len(held), len(src_ids)
     part = held[0].shape[-1]
     units, slots = rec_ids.shape
-    shape = lambda *dims: jax.ShapeDtypeStruct(dims, BF16)
-    rest = slots - some
-    late = shape(used, 2, rest, part) if half else shape(used, rest, part)
+    sent = jax.ShapeDtypeStruct((used, 2, slots // CHUNKS, part), BF16)
     outs = pl.pallas_call(
-        functools.partial(rows_kernel, half, used, sends),
-        out_shape=[shape(used, some, part)] * sends
-        + [late] * sends
-        + [shape(units, used, slots, part)],
-        in_specs=[SMEM] + [VMEM] * (used + 3 + sends + len(early)),
-        out_specs=[VMEM] * (2 * sends + 1),
+        functools.partial(rows_kernel, used, sends),
+        out_shape=[sent] * (sends * CHUNKS)
+        + [jax.ShapeDtypeStruct((units, used, 2, slots, part), BF16)],
+        in_specs=[SMEM] + [VMEM] * (used + 3 + sends),
+        out_specs=[VMEM] * (CHUNKS * sends + 1),
         compiler_params=params(32),
-        cost_estimate=cost(2 * used * part * (128 * part + 512 * 128), 4),
+        cost_estimate=SMALL,
         name="rows",
-    )(scal, spectra, *held, perm, *src_ids, rec_ids, *early)
-    return outs[:sends], outs[sends:-1], outs[-1]
+    )(scal, spectra, *held, perm, *src_ids, rec_ids)
+    return [outs[q * sends : (q + 1) * sends] for q in range(CHUNKS)], outs[-1]
 
 
 def combine(values, classes, outputs, origin, span, period):
@@ -184,10 +191,9 @@
     return [a if b is None else a + root * b for a, b in zip(plain, scaled)]
 
 
-def lags_kernel(geometry, units, first, split, scal, weight, after, *refs):
+def lags_kernel(geometry, units, first, scal, weight, after, *refs):
     classes, span, outputs, origin, period, chunk = geometry
-    count = units * (2 if split else 1)
-    s_refs, (r_real, r_imag, table, keep, send, lhs) = refs[:count], refs[count:]
+    s_refs, (own, table, keep, send, lhs) = refs[:units], refs[units:]
     used, slots = s_refs[0].shape[0], s_refs[0].shape[-2]
     rows = units * slots
     lag_dev = keep.shape[-1]
@@ -200,12 +206,8 @@
             bins = slice(r * LANES, (r + 1) * LANES)
             real = imag = None
             for u in range(used):
-                if split:
-                    sr, si = s_refs[d][u, :, bins], s_refs[units + d][u, :, bins]
-                else:
-                    sr, si = s_refs[d][u, 0, :, bins], s_refs[d][u, 1, :, bins]
-                sr, si = sr.astype(F32), si.astype(F32)
-                rr, ri = r_real[d, u, mine, bins].astype(F32), r_imag[d, u, mine, bins].astype(F32)
+                sr, si = s_refs[d][u, 0, :, bins].astype(F32), s_refs[d][u, 1, :, bins].astype(F32)
+                rr, ri = own[d, u, 0, mine, bins].astype(F32), own[d, u, 1, mine, bins].astype(F32)
                 re, im = sr * rr + si * ri, si * rr - sr * ri
                 if u:
                     re, im = real + weight[u] * re, imag + weight[u] * im
@@ -235,20 +237,19 @@
 
 def lag_parts(scal, weight, after, rows, own, first, table, geometry, columns, lag_dev):
     classes, span = geometry[:2]
-    units = own[0].shape[0]
-    split = len(rows) > units
+    units = len(rows)
     slots, part = rows[0].shape[-2:]
     shape = (columns, units * slots, lag_dev)
     return pl.pallas_call(
-        functools.partial(lags_kernel, geometry, units, first, split),
+        functools.partial(lags_kernel, geometry, units, first),
         out_shape=[jax.ShapeDtypeStruct(shape, F32), jax.ShapeDtypeStruct(shape, BF16)],
-        in_specs=[SMEM, SMEM, pl.BlockSpec(memory_space=pl.ANY)] + [VMEM] * (len(rows) + 3),
+        in_specs=[SMEM, SMEM, pl.BlockSpec(memory_space=pl.ANY)] + [VMEM] * (units + 2),
         out_specs=[VMEM] * 2,
         scratch_shapes=[pltpu.VMEM((classes, 2 * units * slots, 2 * LANES), BF16)],
         compiler_params=params(32),
-        cost_estimate=cost(8 * units * slots * part * span, 8),
+        cost_estimate=SMALL,
         name="lags",
-    )(scal, weight, after, *rows, *own, table)
+    )(scal, weight, after, *rows, own, table)
 
 
 def cores_kernel(scal, keep, more, own, *sends):
@@ -262,7 +263,7 @@
 
         for s, out in enumerate(sends):
 
-            @pl.when(lax.rem(scal[COLUMN] + s + 1, columns) == column)
+            @pl.when(scal[COLUMN] ^ (s + 1) == column)
             def _():
                 out[...] = value.astype(BF16)
 
@@ -276,7 +277,7 @@
         in_specs=[SMEM, VMEM, VMEM],
         out_specs=[VMEM] * columns,
         compiler_params=params(16),
-        cost_estimate=cost(2 * keep.size, 2),
+        cost_estimate=SMALL,
         name="cores",
     )(scal, keep, more)
 
@@ -326,7 +327,7 @@
         ),
         out_shape=outs,
         compiler_params=params(16),
-        cost_estimate=cost(8 * rows * lag_dev, 2),
+        cost_estimate=SMALL,
         name="stats",
     )(scal, own, *more, *[observed] * units)
 
@@ -373,7 +374,7 @@
         ),
         out_shape=[out] * units,
         compiler_params=params(16),
-        cost_estimate=cost(8 * rows * lag_dev, 1),
+        cost_estimate=SMALL,
         name="gradient",
     )(scal, *sums, corr, *[observed] * units)
 
@@ -410,7 +411,7 @@
         ),
         out_shape=jax.ShapeDtypeStruct(observed.shape, F32),
         compiler_params=params(16),
-        cost_estimate=cost(2 * observed.size, 2),
+        cost_estimate=SMALL,
         name="normed",
     )(scal, *ins)
 
@@ -430,7 +431,7 @@
         in_specs=[VMEM] * (len(src_ids) + len(parts)),
         out_specs=VMEM,
         compiler_params=params(16),
-        cost_estimate=cost(2 * channels * lag_dev * 256, 1),
+        cost_estimate=SMALL,
         name="adjoint",
     )(*src_ids, *parts)
 
@@ -454,70 +455,53 @@
     shifts = range(places)
 
     held = [
-        [
-            shifted(
-                lax.dynamic_slice(
-                    spectra[0, half], (0, (column + s) % columns * part), (channels, part)
-                ),
-                "win",
-                columns,
-                s,
-            )
-            for s in range(1, columns)
-        ]
-        for half in range(2)
+        swapped(
+            lax.dynamic_slice(
+                spectra, (0, 0, 0, (column ^ s) * part), (1, 2, channels, part)
+            ),
+            "win",
+            columns,
+            s,
+        )
+        for s in range(1, columns)
     ]
     trig = tables(classes, span, period, bins_dev, columns, cores)
     scal, wanted, rec_ids, table = start(
-        window_keep, owners, pair_count, pair_src, pair_rec, places, trig, classes, span
+        window_keep, owners, pair_count, pair_src, pair_rec, places, trig, classes, span, peers
     )
     if columns == 2:
         weight = jnp.ones((1,), F32)
     else:
-        keeps = jnp.stack([shifted(window_keep[0], "win", columns, s) for s in range(columns)])
+        keeps = jnp.stack([swapped(window_keep[0], "win", columns, s) for s in range(columns)])
         ranked = jnp.argsort(-keeps)[: columns - 1].astype(jnp.int32)
         weight = keeps[ranked].astype(F32)
         scal = lax.dynamic_update_slice(scal, ranked, (ORDER,))
 
     direct = places == blocks
-    src_ids = [shifted(x, "recv", places, -d) for d, x in zip(shifts, wanted)]
+    src_ids = [swapped(x, "recv", places, d) for d, x in zip(shifts, wanted)]
     source = np.arange(part)
     perm = np.zeros((part, part), ml_dtypes.bfloat16)
     perm[source, source % classes * LANES + source // classes] = 1
-    perm = jnp.asarray(perm)
-    first_real, rest_real, own_real = gather_rows(
-        0, scal, spectra, held[0], perm, src_ids, rec_ids, [], some
-    )
-    first_imag, rest, own_imag = gather_rows(
-        1, scal, spectra, held[1], perm, src_ids, rec_ids, rest_real, some
-    )
-    sent = [[first_real, first_imag], [rest]]
-    arrived = [
-        [[shifted(x, "recv", places, d) for d, x in zip(shifts, rows)] for rows in group]
-        for group in sent
-    ]
+    sent, own_rows = gather_rows(scal, spectra, held, jnp.asarray(perm), src_ids, rec_ids)
+    arrived = [[swapped(x, "recv", places, d) for d, x in zip(shifts, rows)] for rows in sent]
     corrs, all_sums, returned = [], [], [[] for _ in shifts]
     after = scal
     for q in range(CHUNKS):
         rows = arrived[q]
         if not direct:
-            stacked = [jnp.stack(r) for r in rows]
+            stacked = jnp.stack(rows)
             rows = [
-                [
-                    lax.dynamic_index_in_dim(x, (place - owners[b]) % places, 0, False)
-                    for b in range(blocks)
-                ]
-                for x in stacked
+                lax.dynamic_index_in_dim(stacked, place ^ owners[b], 0, False)
+                for b in range(blocks)
             ]
-        rows = [x for group in rows for x in group]
         keep, send = lag_parts(
-            scal, weight, after, rows, (own_real, own_imag), q * some, table, geometry, columns, lag_dev
+            scal, weight, after, rows, own_rows, q * some, table, geometry, columns, lag_dev
         )
-        own, *sends = add_cores(scal, keep, shifted(send, "freq", cores, 1))
+        own, *sends = add_cores(scal, keep, swapped(send, "freq", cores, 1))
         after = own
-        more = [shifted(x, "win", columns, s + 1) for s, x in enumerate(sends)]
+        more = [swapped(x, "win", columns, s + 1) for s, x in enumerate(sends)]
         corr, sums = lag_stats(scal, lag_scale, q, own, more, observed, blocks, some)
-        sums = [shifted(sums, ("win", "freq"), peers, s) for s in range(peers)]
+        sums = [swapped(sums, ("win", "freq"), peers, s) for s in range(peers)]
         grads = gradients(scal, lag_total, q, sums, corr, observed, blocks, some)
         if not direct:
             stacked = jnp.stack(list(grads) + [jnp.zeros_like(grads[0])])
@@ -525,10 +509,10 @@
             for d in shifts:
                 block = jnp.int32(blocks)
                 for b in range(blocks):
-                    block = jnp.where(owners[b] == (place - d) % places, b, block)
+                    block = jnp.where(owners[b] == place ^ d, b, block)
                 grads.append(lax.dynamic_index_in_dim(stacked, block, 0, False))
         for d, g in zip(shifts, grads):
-            returned[d].append(shifted(g, "recv", places, -d))
+            returned[d].append(swapped(g, "recv", places, d))
         corrs.append(corr)
         all_sums.append(sums)
     normed = normed_rows(scal, lag_total, all_sums, corrs, observed, blocks, some)

time: 98.7 us -> 93 us (0.942)
  waiting for transfers between devices: 28.3 us -> 35.6 us
  starting transfers between devices: 36.9 us -> 30 us
  local copies, waits for them, and re-layouts: 12.4 us -> 7.59 us
  Pallas kernels: 19.1 us -> 18.1 us
    ppermute x30 -> x26, waiting for transfers between devices: 28.3 us -> 35.6 us  [swapped(): return lax.ppermute(value, axis, [(i, i ^ step) for i in range(size)])]
    ppermute x30 -> x26, starting transfers between devices: 36.9 us -> 30 us  [swapped(): return lax.ppermute(value, axis, [(i, i ^ step) for i in range(size)])]
    slice x1 -> x0, local copies, waits for them, and re-layouts: 2.43 us -> none  [shards(): spectra[0, half]]
    dynamic_slice x2 -> x1, local copies, waits for them, and re-layouts: 3.33 us -> 1.08 us  [shards(): lax.dynamic_slice(spectra, (0, 0, 0, (column ^ s) * part), (1, 2, channel...]
    pallas_call x4 -> x3, Pallas kernels: 8.95 us -> 7.92 us  [the longest x2 6.08 us: lag_parts(): pl.pallas_call(functools.partial(lags_kernel, geometry, units, first), ou...]
    unnamed x21 -> x16, local copies, waits for them, and re-layouts: 6.67 us -> 6.51 us
  transfers between devices with their start and end apart: 30 -> 26, of which waited for: 15 -> 12; matrix products, arithmetic and copies ran while one was open for 2% -> 0% of each run, Pallas kernels for 12% -> 10%
where the time goes in v4:
time: 93 us; the launch traced here: 92.7 us
  waiting for transfers between devices  35.6 us (38%)
  starting transfers between devices  30 us (32%)
  Pallas kernels  18.1 us (19%)
  local copies, waits for them, and re-layouts  7.59 us (8%)
  between operations  1.45 us (2%)
    ppermute x26, waiting for transfers between devices, swapped(): return lax.ppermute(value, axis, [(i, i ^ step) for i in range(size)])  35.6 us
    ppermute x26, starting transfers between devices, swapped(): return lax.ppermute(value, axis, [(i, i ^ step) for i in range(size)])  30 us
    unnamed x16, local copies, waits for them, and re-layouts  6.51 us
    pallas_call x2, Pallas kernels, lag_parts(): pl.pallas_call(functools.partial(lags_kernel, geometry, units, first), ou...  6.08 us
    pallas_call x1, Pallas kernels, normed_rows(): pl.pallas_call(functools.partial(normed_kernel, lag_total, len(sums[0])),...  2.59 us
    pallas_call x1, Pallas kernels, start(): pl.pallas_call(functools.partial(start_kernel, blocks, places == blocks,...  1.89 us
  transfers between devices with their start and end apart: 26, of which 12 were waited for; matrix products, arithmetic and copies ran while one was open for 0% of the time, Pallas kernels for 10%

profile of v4, /device:TPU:0, one launch (start us, length us, event | category | flops | bytes accessed | tf_op | source)
XLA Modules:
  0.0 92.7 jit_solution(17290140086391047180)
XLA Ops:
  0.6 1.1 %constant_dynamic-slice_fusion = bf16[1,2,128,1024]{3,2,1,0:T(8,128)(2,1)S(1)} fusion(bf16[1,2,128,2048]{3,2,1,0:T(8,128)(2,1)} %spectra.1, s32[]{:T(128)S(6)} %select_n.3), kind=kLoop, calls=%fused_computation | loop fusion | bytes 1048580 | tf_op jit(solution)/shard_map/dynamic_slice | solution.py:459
  1.7 3.0 %collective-permute-start = (bf16[1,2,128,1024]{3,2,1,0:T(8,128)(2,1)S(1)}, bf16[1,2,128,1024]{3,2,1,0:T(8,128)(2,1)S(1)}, u32[]{:S(2)}, u32[]{:S(2)}) collective-permute-start(bf16[1,2,128,1024]{3,2,1,0:T(8,128)(2,1)S(1)} %constant_dynamic-slice_fusion), channel_id=1, source_target_pairs={{0,2},{2,0},{1,3},{3,1},{4,6},{6,4},{5,7},{7,5},{8,10},{10,8},{9,1... | collective-permute-start | bytes 1572872 | tf_op jit(solution)/shard_map/ppermute | solution.py:28
  5.4 1.0 %copy-done.3 = f32[2,56,1024]{2,1,0:T(8,128)S(1)} copy-done((f32[2,56,1024]{2,1,0:T(8,128)S(1)}, f32[2,56,1024]{2,1,0:T(8,128)}, u32[]{:S(2)}) %copy-start.3) | copy-done | bytes 458776
  9.1 1.9 %start.1 = (s32[128]{0:T(128)S(1)}, s32[1,64]{1,0:T(1,128)S(1)}, s32[1,64]{1,0:T(1,128)S(1)}, s32[1,64]{1,0:T(1,128)S(1)}, s32[1,64]{1,0:T(1,128)S(1)}, /*index=...) custom-call(s32[1]{0:T(128)S(6)} %copy.11.refs_0_, s32[4]{0:T(128)S(1)} %copy-done.6, s32[4]{0:T(128)S(1)} %bitcast.1, ...), custom_call_target="tpu_custom_call" | custom-call | flops 1 | bytes 1 | tf_op jit(solution)/shard_map/start/pallas_call | solution.py:99
  11.0 1.6 %collective-permute-start.1 = (s32[1,64]{1,0:T(1,128)S(1)}, s32[1,64]{1,0:T(1,128)S(1)}, u32[]{:S(2)}, u32[]{:S(2)}) collective-permute-start(s32[1,64]{1,0:T(1,128)S(1)} %get-tuple-element.40), channel_id=1, source_target_pairs={{0,4},{4,0},{8,12},{12,8},{1,5},{5,1},{9,13},{13,9},{2,6},{6,2},{1... | collective-permute-start | bytes 776 | tf_op jit(solution)/shard_map/ppermute | solution.py:28
  12.6 2.6 %collective-permute-start.2 = (s32[1,64]{1,0:T(1,128)S(1)}, s32[1,64]{1,0:T(1,128)S(1)}, u32[]{:S(2)}, u32[]{:S(2)}) collective-permute-start(s32[1,64]{1,0:T(1,128)S(1)} %get-tuple-element.41), channel_id=1, source_target_pairs={{0,8},{4,12},{8,0},{12,4},{1,9},{5,13},{9,1},{13,5},{2,10},{6,14},... | collective-permute-start | bytes 776 | tf_op jit(solution)/shard_map/ppermute | solution.py:28
  15.4 1.6 %collective-permute-done.2.refs_4_.refs_2_ = s32[1,64]{1,0:T(1,128)S(1)} collective-permute-done((s32[1,64]{1,0:T(1,128)S(1)}, s32[1,64]{1,0:T(1,128)S(1)}, u32[]{:S(2)}, u32[]{:S(2)}) %collective-permute-start.2) | collective-permute-done | bytes 288 | tf_op jit(solution)/shard_map/ppermute | solution.py:28
  17.1 3.5 %collective-permute-done.3.refs_5_.refs_3_ = s32[1,64]{1,0:T(1,128)S(1)} collective-permute-done((s32[1,64]{1,0:T(1,128)S(1)}, s32[1,64]{1,0:T(1,128)S(1)}, u32[]{:S(2)}, u32[]{:S(2)}) %collective-permute-start.3) | collective-permute-done | bytes 288 | tf_op jit(solution)/shard_map/ppermute | solution.py:28
  20.5 1.2 %copy-done.1 = bf16[1,2,128,2048]{3,2,1,0:T(8,128)(2,1)S(1)} copy-done((bf16[1,2,128,2048]{3,2,1,0:T(8,128)(2,1)S(1)}, bf16[1,2,128,2048]{3,2,1,0:T(8,128)(2,1)}, u32[]{:S(2)}) %copy-start.1) | copy-done | bytes 1048600
  21.8 1.6 %copy-done.2 = bf16[1024,1024]{1,0:T(8,128)(2,1)S(1)} copy-done((bf16[1024,1024]{1,0:T(8,128)(2,1)S(1)}, bf16[1024,1024]{1,0:T(8,128)(2,1)}, u32[]{:S(2)}) %copy-start.2) | copy-done | bytes 2097176
  23.4 1.8 %rows.1 = (bf16[1,2,32,1024]{3,2,1,0:T(8,128)(2,1)S(1)}, bf16[1,2,32,1024]{3,2,1,0:T(8,128)(2,1)S(1)}, bf16[1,2,32,1024]{3,2,1,0:T(8,128)(2,1)S(1)}, bf16[1,2,32...) custom-call(s32[128]{0:T(128)S(1)} %get-tuple-element.38.scal.after,, ...), custom_call_target="tpu_custom_call" | custom-call | flops 1 | bytes 1 | tf_op jit(solution)/shard_map/rows/pallas_call | solution.py:155
  26.1 3.6 %collective-permute-start.6 = (bf16[1,2,32,1024]{3,2,1,0:T(8,128)(2,1)S(1)}, bf16[1,2,32,1024]{3,2,1,0:T(8,128)(2,1)S(1)}, u32[]{:S(2)}, u32[]{:S(2)}) collective-permute-start(bf16[1,2,32,1024]{3,2,1,0:T(8,128)(2,1)S(1)} %get-tuple-element.47), channel_id=1, source_target_pairs={{0,12},{4,8},{8,4},{12,0},{1,13},{5,9},{9,5},{13,1},{2,14},{6,10},... | collective-permute-start | bytes 393224 | tf_op jit(solution)/shard_map/ppermute | solution.py:28
  30.2 6.3 %collective-permute-done.5.refs_2_ = bf16[1,2,32,1024]{3,2,1,0:T(8,128)(2,1)S(1)} collective-permute-done((bf16[1,2,32,1024]{3,2,1,0:T(8,128)(2,1)S(1)}, bf16[1,2,32,1024]{3,2,1,0:T(8,128)(2,1)S(1)}, u32[]{:S(2)}, u32[]{:S(2)}) %collective-permute-start.5) | collective-permute-done | bytes 131104 | tf_op jit(solution)/shard_map/ppermute | solution.py:28
  36.6 3.0 %lags.2 = (f32[2,128,1024]{2,1,0:T(8,128)S(1)}, bf16[2,128,1024]{2,1,0:T(8,128)(2,1)S(1)}) custom-call(s32[128]{0:T(128)S(1)} %get-tuple-element.38.scal.after, f32[1]{0:T(128)} %constant.4.clone.1.weight, s32[128]{0:T(128)S(1)} %get-tuple-element.38.scal.after, bf16[1,2,32,1024]{3,2,1,0:T(8,128)(2,1)S(1)} %get-tuple-element.44.refs_0_, ...), custom_call_target="tpu_custom_call" | custom-call | flops 1 | bytes 1 | tf_op jit(solution)/shard_map/lags/pallas_call | solution.py:243
  39.7 2.0 %collective-permute-start.12 = (bf16[1,2,32,1024]{3,2,1,0:T(8,128)(2,1)S(1)}, bf16[1,2,32,1024]{3,2,1,0:T(8,128)(2,1)S(1)}, u32[]{:S(2)}, u32[]{:S(2)}) collective-permute-start(bf16[1,2,32,1024]{3,2,1,0:T(8,128)(2,1)S(1)} %get-tuple-element.57), channel_id=1, source_target_pairs={{0,4},{4,0},{8,12},{12,8},{1,5},{5,1},{9,13},{13,9},{2,6},{6,2},{1... | collective-permute-start | bytes 393224 | tf_op jit(solution)/shard_map/ppermute | solution.py:28
  41.7 2.4 %collective-permute-start.14 = (bf16[1,2,32,1024]{3,2,1,0:T(8,128)(2,1)S(1)}, bf16[1,2,32,1024]{3,2,1,0:T(8,128)(2,1)S(1)}, u32[]{:S(2)}, u32[]{:S(2)}) collective-permute-start(bf16[1,2,32,1024]{3,2,1,0:T(8,128)(2,1)S(1)} %get-tuple-element.59), channel_id=1, source_target_pairs={{0,12},{4,8},{8,4},{12,0},{1,13},{5,9},{9,5},{13,1},{2,14},{6,10},... | collective-permute-start | bytes 393224 | tf_op jit(solution)/shard_map/ppermute | solution.py:28
  44.9 2.3 %collective-permute-done.12.refs_1_ = bf16[1,2,32,1024]{3,2,1,0:T(8,128)(2,1)S(1)} collective-permute-done((bf16[1,2,32,1024]{3,2,1,0:T(8,128)(2,1)S(1)}, bf16[1,2,32,1024]{3,2,1,0:T(8,128)(2,1)S(1)}, u32[]{:S(2)}, u32[]{:S(2)}) %collective-permute-start.12) | collective-permute-done | bytes 131104 | tf_op jit(solution)/shard_map/ppermute | solution.py:28
  47.3 7.4 %collective-permute-done.13.refs_2_ = bf16[1,2,32,1024]{3,2,1,0:T(8,128)(2,1)S(1)} collective-permute-done((bf16[1,2,32,1024]{3,2,1,0:T(8,128)(2,1)S(1)}, bf16[1,2,32,1024]{3,2,1,0:T(8,128)(2,1)S(1)}, u32[]{:S(2)}, u32[]{:S(2)}) %collective-permute-start.13) | collective-permute-done | bytes 131104 | tf_op jit(solution)/shard_map/ppermute | solution.py:28
  54.6 3.0 %lags.3 = (f32[2,128,1024]{2,1,0:T(8,128)S(1)}, bf16[2,128,1024]{2,1,0:T(8,128)(2,1)S(1)}) custom-call(s32[128]{0:T(128)S(1)} %get-tuple-element.38.scal.after, f32[1]{0:T(128)} %constant.4.clone.1.weight, f32[128,1024]{1,0:T(8,128)S(1)} %get-tuple-element.52.refs_0_.after, bf16[1,2,32,1024]{3,2,1,0:T(8,128)(2,1)S(1)} %get-tuple-element.56.refs_0_, ...), custom_call_target="tpu_custom_call" | custom-call | flops 1 | bytes 1 | tf_op jit(solution)/shard_map/lags/pallas_call | solution.py:243
  58.4 1.3 %collective-permute-done.15.more = bf16[2,128,1024]{2,1,0:T(8,128)(2,1)S(1)} collective-permute-done((bf16[2,128,1024]{2,1,0:T(8,128)(2,1)S(1)}, bf16[2,128,1024]{2,1,0:T(8,128)(2,1)S(1)}, u32[]{:S(2)}, u32[]{:S(2)}) %collective-permute-start.15) | collective-permute-done | bytes 524320 | tf_op jit(solution)/shard_map/ppermute | solution.py:28
  61.0 5.9 %collective-permute-done.8.refs_1_ = bf16[128,1024]{1,0:T(8,128)(2,1)S(1)} collective-permute-done((bf16[128,1024]{1,0:T(8,128)(2,1)S(1)}, bf16[128,1024]{1,0:T(8,128)(2,1)S(1)}, u32[]{:S(2)}, u32[]{:S(2)}) %collective-permute-start.8) | collective-permute-done | bytes 262176 | tf_op jit(solution)/shard_map/ppermute | solution.py:28
  68.6 1.0 %collective-permute-start.9 = (f32[8,128]{1,0:T(8,128)S(1)}, f32[8,128]{1,0:T(8,128)S(1)}, u32[]{:S(2)}, u32[]{:S(2)}) collective-permute-start(f32[8,128]{1,0:T(8,128)S(1)} %get-tuple-element.54.refs_0_), channel_id=1, source_target_pairs={{0,1},{1,0},{2,3},{3,2},{4,5},{5,4},{6,7},{7,6},{8,9},{9,8},{10,11... | collective-permute-start | bytes 12296 | tf_op jit(solution)/shard_map/ppermute | solution.py:28
  69.6 2.1 %collective-permute-done.11.refs_3_ = f32[8,128]{1,0:T(8,128)S(1)} collective-permute-done((f32[8,128]{1,0:T(8,128)S(1)}, f32[8,128]{1,0:T(8,128)S(1)}, u32[]{:S(2)}, u32[]{:S(2)}) %collective-permute-start.11) | collective-permute-done | bytes 4128 | tf_op jit(solution)/shard_map/ppermute | solution.py:28
  73.1 2.7 %collective-permute-start.20 = (bf16[32,1024]{1,0:T(8,128)(2,1)S(1)}, bf16[32,1024]{1,0:T(8,128)(2,1)S(1)}, u32[]{:S(2)}, u32[]{:S(2)}) collective-permute-start(bf16[32,1024]{1,0:T(8,128)(2,1)S(1)} %get-tuple-element.68), channel_id=1, source_target_pairs={{0,4},{4,0},{8,12},{12,8},{1,5},{5,1},{9,13},{13,9},{2,6},{6,2},{1... | collective-permute-start | bytes 196616 | tf_op jit(solution)/shard_map/ppermute | solution.py:28
  76.6 1.4 %collective-permute-start.18 = (f32[8,128]{1,0:T(8,128)S(1)}, f32[8,128]{1,0:T(8,128)S(1)}, u32[]{:S(2)}, u32[]{:S(2)}) collective-permute-start(f32[8,128]{1,0:T(8,128)S(1)} %get-tuple-element.64.refs_5_.refs_0_), channel_id=1, source_target_pairs={{0,2},{1,3},{2,0},{3,1},{4,6},{5,7},{6,4},{7,5},{8,10},{9,11},{10,... | collective-permute-start | bytes 12296 | tf_op jit(solution)/shard_map/ppermute | solution.py:28
  78.4 1.2 %collective-permute-done.19.refs_8_.refs_3_ = f32[8,128]{1,0:T(8,128)S(1)} collective-permute-done((f32[8,128]{1,0:T(8,128)S(1)}, f32[8,128]{1,0:T(8,128)S(1)}, u32[]{:S(2)}, u32[]{:S(2)}) %collective-permute-start.19) | collective-permute-done | bytes 4128 | tf_op jit(solution)/shard_map/ppermute | solution.py:28
  79.6 1.4 %collective-permute-start.24 = (bf16[32,1024]{1,0:T(8,128)(2,1)S(1)}, bf16[32,1024]{1,0:T(8,128)(2,1)S(1)}, u32[]{:S(2)}, u32[]{:S(2)}) collective-permute-start(bf16[32,1024]{1,0:T(8,128)(2,1)S(1)} %get-tuple-element.72), channel_id=1, source_target_pairs={{0,12},{4,8},{8,4},{12,0},{1,13},{5,9},{9,5},{13,1},{2,14},{6,10},... | collective-permute-start | bytes 196616 | tf_op jit(solution)/shard_map/ppermute | solution.py:28
  82.8 2.1 %collective-permute-start.23 = (bf16[32,1024]{1,0:T(8,128)(2,1)S(1)}, bf16[32,1024]{1,0:T(8,128)(2,1)S(1)}, u32[]{:S(2)}, u32[]{:S(2)}) collective-permute-start(bf16[32,1024]{1,0:T(8,128)(2,1)S(1)} %get-tuple-element.71), channel_id=1, source_target_pairs={{0,8},{4,12},{8,0},{12,4},{1,9},{5,13},{9,1},{13,5},{2,10},{6,14},... | collective-permute-start | bytes 196616 | tf_op jit(solution)/shard_map/ppermute | solution.py:28
  84.9 1.4 %collective-permute-start.25 = (bf16[32,1024]{1,0:T(8,128)(2,1)S(1)}, bf16[32,1024]{1,0:T(8,128)(2,1)S(1)}, u32[]{:S(2)}, u32[]{:S(2)}) collective-permute-start(bf16[32,1024]{1,0:T(8,128)(2,1)S(1)} %get-tuple-element.73), channel_id=1, source_target_pairs={{0,12},{4,8},{8,4},{12,0},{1,13},{5,9},{9,5},{13,1},{2,14},{6,10},... | collective-permute-start | bytes 196616 | tf_op jit(solution)/shard_map/ppermute | solution.py:28
  86.3 2.6 %normed.1 = f32[4,64,1024]{2,1,0:T(8,128)} custom-call(s32[128]{0:T(128)S(1)} %get-tuple-element.38.scal.after, f32[8,128]{1,0:T(8,128)S(1)} %get-tuple-element.54.refs_0_, f32[8,128]{1,0:T(8,128)S(1)} %collective-permute-done.9.refs_1_, f32[8,128]{1,0:T(8,128)S(1)} %collective-permute-done.10.refs_2_, f32[8,128]{1,0:T(8,128)S(1)} %collective-permute-done.11.refs_3_, ...), custom_call_target="tpu_custom_call" | custom-call | flops 1 | bytes 1 | tf_op jit(solution)/shard_map/normed/pallas_call | solution.py:402
  88.9 2.7 %collective-permute-done.23.refs_9_ = bf16[32,1024]{1,0:T(8,128)(2,1)S(1)} collective-permute-done((bf16[32,1024]{1,0:T(8,128)(2,1)S(1)}, bf16[32,1024]{1,0:T(8,128)(2,1)S(1)}, u32[]{:S(2)}, u32[]{:S(2)}) %collective-permute-start.23) | collective-permute-done | bytes 65568 | tf_op jit(solution)/shard_map/ppermute | solution.py:28
  91.6 1.1 %adjoint.1 = f32[128,1024]{1,0:T(8,128)} custom-call(s32[1,64]{1,0:T(1,128)S(1)} %get-tuple-element.39.refs_2_.refs_0_, s32[1,64]{1,0:T(1,128)S(1)} %collective-permute-done.1.refs_3_.refs_1_, s32[1,64]{1,0:T(1,128)S(1)} %collective-permute-done.2.refs_4_.refs_2_, s32[1,64]{1,0:T(1,128)S(1)} %collective-permute-done.3.refs_5_.refs_3_, ...), custom_call_target="tpu_custom_call" | custom-call | flops 1 | bytes 1 | tf_op jit(solution)/shard_map/adjoint/pallas_call | solution.py:428
  (49 shorter events, 13.3 us)
Async XLA Ops:
  1.7 18.8 %collective-permute-start = (bf16[1,2,128,1024]{3,2,1,0:T(8,128)(2,1)S(1)}, bf16[1,2,128,1024]{3,2,1,0:T(8,128)(2,1)S(1)}, u32[]{:S(2)}, u32[]{:S(2)}) collective-permute-start(bf16[1,2,128,1024]{3,2,1,0:T(8,128)(2,1)S(1)} %constant_dynamic-slice_fusion), channel_id=1, source_target_pairs={{0,2},{2,0},{1,3},{3,1},{4,6},{6,4},{5,7},{7,5},{8,10},{10,8},{9,1... | collective-permute-start | bytes 1572872 | tf_op jit(solution)/shard_map/ppermute | solution.py:28
  5.4 1.0 %copy-start.3 = (f32[2,56,1024]{2,1,0:T(8,128)S(1)}, f32[2,56,1024]{2,1,0:T(8,128)}, u32[]{:S(2)}) copy-start(f32[2,56,1024]{2,1,0:T(8,128)} %constant.18.clone.refs_5_) | copy-start | bytes 1376260
  6.4 0.7 copy-start.4
  7.1 0.7 copy-start.5
  11.0 4.5 %collective-permute-start.1 = (s32[1,64]{1,0:T(1,128)S(1)}, s32[1,64]{1,0:T(1,128)S(1)}, u32[]{:S(2)}, u32[]{:S(2)}) collective-permute-start(s32[1,64]{1,0:T(1,128)S(1)} %get-tuple-element.40), channel_id=1, source_target_pairs={{0,4},{4,0},{8,12},{12,8},{1,5},{5,1},{9,13},{13,9},{2,6},{6,2},{1... | collective-permute-start | bytes 776 | tf_op jit(solution)/shard_map/ppermute | solution.py:28
  12.6 4.4 %collective-permute-start.2 = (s32[1,64]{1,0:T(1,128)S(1)}, s32[1,64]{1,0:T(1,128)S(1)}, u32[]{:S(2)}, u32[]{:S(2)}) collective-permute-start(s32[1,64]{1,0:T(1,128)S(1)} %get-tuple-element.41), channel_id=1, source_target_pairs={{0,8},{4,12},{8,0},{12,4},{1,9},{5,13},{9,1},{13,5},{2,10},{6,14},... | collective-permute-start | bytes 776 | tf_op jit(solution)/shard_map/ppermute | solution.py:28
  15.2 5.3 %collective-permute-start.3 = (s32[1,64]{1,0:T(1,128)S(1)}, s32[1,64]{1,0:T(1,128)S(1)}, u32[]{:S(2)}, u32[]{:S(2)}) collective-permute-start(s32[1,64]{1,0:T(1,128)S(1)} %get-tuple-element.42), channel_id=1, source_target_pairs={{0,12},{4,8},{8,4},{12,0},{1,13},{5,9},{9,5},{13,1},{2,14},{6,10},... | collective-permute-start | bytes 776 | tf_op jit(solution)/shard_map/ppermute | solution.py:28
  20.5 1.2 %copy-start.1 = (bf16[1,2,128,2048]{3,2,1,0:T(8,128)(2,1)S(1)}, bf16[1,2,128,2048]{3,2,1,0:T(8,128)(2,1)}, u32[]{:S(2)}) copy-start(bf16[1,2,128,2048]{3,2,1,0:T(8,128)(2,1)} %spectra.1) | copy-start | bytes 3145732
  21.8 1.6 %copy-start.2 = (bf16[1024,1024]{1,0:T(8,128)(2,1)S(1)}, bf16[1024,1024]{1,0:T(8,128)(2,1)}, u32[]{:S(2)}) copy-start(bf16[1024,1024]{1,0:T(8,128)(2,1)} %constant.19.clone.refs_1_) | copy-start | bytes 6291460
  25.2 5.0 %collective-permute-start.4 = (bf16[1,2,32,1024]{3,2,1,0:T(8,128)(2,1)S(1)}, bf16[1,2,32,1024]{3,2,1,0:T(8,128)(2,1)S(1)}, u32[]{:S(2)}, u32[]{:S(2)}) collective-permute-start(bf16[1,2,32,1024]{3,2,1,0:T(8,128)(2,1)S(1)} %get-tuple-element.45), channel_id=1, source_target_pairs={{0,4},{4,0},{8,12},{12,8},{1,5},{5,1},{9,13},{13,9},{2,6},{6,2},{1... | collective-permute-start | bytes 393224 | tf_op jit(solution)/shard_map/ppermute | solution.py:28
  25.3 11.3 %collective-permute-start.5 = (bf16[1,2,32,1024]{3,2,1,0:T(8,128)(2,1)S(1)}, bf16[1,2,32,1024]{3,2,1,0:T(8,128)(2,1)S(1)}, u32[]{:S(2)}, u32[]{:S(2)}) collective-permute-start(bf16[1,2,32,1024]{3,2,1,0:T(8,128)(2,1)S(1)} %get-tuple-element.46), channel_id=1, source_target_pairs={{0,8},{4,12},{8,0},{12,4},{1,9},{5,13},{9,1},{13,5},{2,10},{6,14},... | collective-permute-start | bytes 393224 | tf_op jit(solution)/shard_map/ppermute | solution.py:28
  26.1 10.5 %collective-permute-start.6 = (bf16[1,2,32,1024]{3,2,1,0:T(8,128)(2,1)S(1)}, bf16[1,2,32,1024]{3,2,1,0:T(8,128)(2,1)S(1)}, u32[]{:S(2)}, u32[]{:S(2)}) collective-permute-start(bf16[1,2,32,1024]{3,2,1,0:T(8,128)(2,1)S(1)} %get-tuple-element.47), channel_id=1, source_target_pairs={{0,12},{4,8},{8,4},{12,0},{1,13},{5,9},{9,5},{13,1},{2,14},{6,10},... | collective-permute-start | bytes 393224 | tf_op jit(solution)/shard_map/ppermute | solution.py:28
  39.6 4.6 %collective-permute-start.7 = (bf16[2,128,1024]{2,1,0:T(8,128)(2,1)S(1)}, bf16[2,128,1024]{2,1,0:T(8,128)(2,1)S(1)}, u32[]{:S(2)}, u32[]{:S(2)}) collective-permute-start(bf16[2,128,1024]{2,1,0:T(8,128)(2,1)S(1)} %get-tuple-element.51), channel_id=1, source_target_pairs={{0,1},{1,0},{2,3},{3,2},{4,5},{5,4},{6,7},{7,6},{8,9},{9,8},{10,11... | collective-permute-start | bytes 1572872 | tf_op jit(solution)/shard_map/ppermute | solution.py:28
  39.7 7.6 %collective-permute-start.12 = (bf16[1,2,32,1024]{3,2,1,0:T(8,128)(2,1)S(1)}, bf16[1,2,32,1024]{3,2,1,0:T(8,128)(2,1)S(1)}, u32[]{:S(2)}, u32[]{:S(2)}) collective-permute-start(bf16[1,2,32,1024]{3,2,1,0:T(8,128)(2,1)S(1)} %get-tuple-element.57), channel_id=1, source_target_pairs={{0,4},{4,0},{8,12},{12,8},{1,5},{5,1},{9,13},{13,9},{2,6},{6,2},{1... | collective-permute-start | bytes 393224 | tf_op jit(solution)/shard_map/ppermute | solution.py:28
  41.7 12.9 %collective-permute-start.13 = (bf16[1,2,32,1024]{3,2,1,0:T(8,128)(2,1)S(1)}, bf16[1,2,32,1024]{3,2,1,0:T(8,128)(2,1)S(1)}, u32[]{:S(2)}, u32[]{:S(2)}) collective-permute-start(bf16[1,2,32,1024]{3,2,1,0:T(8,128)(2,1)S(1)} %get-tuple-element.58), channel_id=1, source_target_pairs={{0,8},{4,12},{8,0},{12,4},{1,9},{5,13},{9,1},{13,5},{2,10},{6,14},... | collective-permute-start | bytes 393224 | tf_op jit(solution)/shard_map/ppermute | solution.py:28
  41.7 12.9 %collective-permute-start.14 = (bf16[1,2,32,1024]{3,2,1,0:T(8,128)(2,1)S(1)}, bf16[1,2,32,1024]{3,2,1,0:T(8,128)(2,1)S(1)}, u32[]{:S(2)}, u32[]{:S(2)}) collective-permute-start(bf16[1,2,32,1024]{3,2,1,0:T(8,128)(2,1)S(1)} %get-tuple-element.59), channel_id=1, source_target_pairs={{0,12},{4,8},{8,4},{12,0},{1,13},{5,9},{9,5},{13,1},{2,14},{6,10},... | collective-permute-start | bytes 393224 | tf_op jit(solution)/shard_map/ppermute | solution.py:28
  44.9 22.0 %copy-start = (f32[4,64,1024]{2,1,0:T(8,128)S(1)}, f32[4,64,1024]{2,1,0:T(8,128)}, u32[]{:S(2)}) copy-start(f32[4,64,1024]{2,1,0:T(8,128)} %refs_8_.3) | copy-start | bytes 3145732
  57.7 2.0 %collective-permute-start.15 = (bf16[2,128,1024]{2,1,0:T(8,128)(2,1)S(1)}, bf16[2,128,1024]{2,1,0:T(8,128)(2,1)S(1)}, u32[]{:S(2)}, u32[]{:S(2)}) collective-permute-start(bf16[2,128,1024]{2,1,0:T(8,128)(2,1)S(1)} %get-tuple-element.61), channel_id=1, source_target_pairs={{0,1},{1,0},{2,3},{3,2},{4,5},{5,4},{6,7},{7,6},{8,9},{9,8},{10,11... | collective-permute-start | bytes 1572872 | tf_op jit(solution)/shard_map/ppermute | solution.py:28
  57.8 9.2 %collective-permute-start.8 = (bf16[128,1024]{1,0:T(8,128)(2,1)S(1)}, bf16[128,1024]{1,0:T(8,128)(2,1)S(1)}, u32[]{:S(2)}, u32[]{:S(2)}) collective-permute-start(bf16[128,1024]{1,0:T(8,128)(2,1)S(1)} %get-tuple-element.53), channel_id=1, source_target_pairs={{0,2},{2,0},{1,3},{3,1},{4,6},{6,4},{5,7},{7,5},{8,10},{10,8},{9,1... | collective-permute-start | bytes 786440 | tf_op jit(solution)/shard_map/ppermute | solution.py:28
  60.4 15.4 %collective-permute-start.16 = (bf16[128,1024]{1,0:T(8,128)(2,1)S(1)}, bf16[128,1024]{1,0:T(8,128)(2,1)S(1)}, u32[]{:S(2)}, u32[]{:S(2)}) collective-permute-start(bf16[128,1024]{1,0:T(8,128)(2,1)S(1)} %get-tuple-element.63), channel_id=1, source_target_pairs={{0,2},{2,0},{1,3},{3,1},{4,6},{6,4},{5,7},{7,5},{8,10},{10,8},{9,1... | collective-permute-start | bytes 786440 | tf_op jit(solution)/shard_map/ppermute | solution.py:28
  67.7 4.0 %collective-permute-start.11 = (f32[8,128]{1,0:T(8,128)S(1)}, f32[8,128]{1,0:T(8,128)S(1)}, u32[]{:S(2)}, u32[]{:S(2)}) collective-permute-start(f32[8,128]{1,0:T(8,128)S(1)} %get-tuple-element.54.refs_0_), channel_id=1, source_target_pairs={{0,3},{1,2},{2,1},{3,0},{4,7},{5,6},{6,5},{7,4},{8,11},{9,10},{10,... | collective-permute-start | bytes 12296 | tf_op jit(solution)/shard_map/ppermute | solution.py:28
  67.8 4.5 %collective-permute-start.10 = (f32[8,128]{1,0:T(8,128)S(1)}, f32[8,128]{1,0:T(8,128)S(1)}, u32[]{:S(2)}, u32[]{:S(2)}) collective-permute-start(f32[8,128]{1,0:T(8,128)S(1)} %get-tuple-element.54.refs_0_), channel_id=1, source_target_pairs={{0,2},{1,3},{2,0},{3,1},{4,6},{5,7},{6,4},{7,5},{8,10},{9,11},{10,... | collective-permute-start | bytes 12296 | tf_op jit(solution)/shard_map/ppermute | solution.py:28
  68.6 3.7 %collective-permute-start.9 = (f32[8,128]{1,0:T(8,128)S(1)}, f32[8,128]{1,0:T(8,128)S(1)}, u32[]{:S(2)}, u32[]{:S(2)}) collective-permute-start(f32[8,128]{1,0:T(8,128)S(1)} %get-tuple-element.54.refs_0_), channel_id=1, source_target_pairs={{0,1},{1,0},{2,3},{3,2},{4,5},{5,4},{6,7},{7,6},{8,9},{9,8},{10,11... | collective-permute-start | bytes 12296 | tf_op jit(solution)/shard_map/ppermute | solution.py:28
  73.1 11.8 %collective-permute-start.20 = (bf16[32,1024]{1,0:T(8,128)(2,1)S(1)}, bf16[32,1024]{1,0:T(8,128)(2,1)S(1)}, u32[]{:S(2)}, u32[]{:S(2)}) collective-permute-start(bf16[32,1024]{1,0:T(8,128)(2,1)S(1)} %get-tuple-element.68), channel_id=1, source_target_pairs={{0,4},{4,0},{8,12},{12,8},{1,5},{5,1},{9,13},{13,9},{2,6},{6,2},{1... | collective-permute-start | bytes 196616 | tf_op jit(solution)/shard_map/ppermute | solution.py:28
  76.5 3.1 %collective-permute-start.19 = (f32[8,128]{1,0:T(8,128)S(1)}, f32[8,128]{1,0:T(8,128)S(1)}, u32[]{:S(2)}, u32[]{:S(2)}) collective-permute-start(f32[8,128]{1,0:T(8,128)S(1)} %get-tuple-element.64.refs_5_.refs_0_), channel_id=1, source_target_pairs={{0,3},{1,2},{2,1},{3,0},{4,7},{5,6},{6,5},{7,4},{8,11},{9,10},{10,... | collective-permute-start | bytes 12296 | tf_op jit(solution)/shard_map/ppermute | solution.py:28
  76.6 4.4 %collective-permute-start.18 = (f32[8,128]{1,0:T(8,128)S(1)}, f32[8,128]{1,0:T(8,128)S(1)}, u32[]{:S(2)}, u32[]{:S(2)}) collective-permute-start(f32[8,128]{1,0:T(8,128)S(1)} %get-tuple-element.64.refs_5_.refs_0_), channel_id=1, source_target_pairs={{0,2},{1,3},{2,0},{3,1},{4,6},{5,7},{6,4},{7,5},{8,10},{9,11},{10,... | collective-permute-start | bytes 12296 | tf_op jit(solution)/shard_map/ppermute | solution.py:28
  77.9 3.0 %collective-permute-start.17 = (f32[8,128]{1,0:T(8,128)S(1)}, f32[8,128]{1,0:T(8,128)S(1)}, u32[]{:S(2)}, u32[]{:S(2)}) collective-permute-start(f32[8,128]{1,0:T(8,128)S(1)} %get-tuple-element.64.refs_5_.refs_0_), channel_id=1, source_target_pairs={{0,1},{1,0},{2,3},{3,2},{4,5},{5,4},{6,7},{7,6},{8,9},{9,8},{10,11... | collective-permute-start | bytes 12296 | tf_op jit(solution)/shard_map/ppermute | solution.py:28
  78.4 10.4 %collective-permute-start.22 = (bf16[32,1024]{1,0:T(8,128)(2,1)S(1)}, bf16[32,1024]{1,0:T(8,128)(2,1)S(1)}, u32[]{:S(2)}, u32[]{:S(2)}) collective-permute-start(bf16[32,1024]{1,0:T(8,128)(2,1)S(1)} %get-tuple-element.70), channel_id=1, source_target_pairs={{0,8},{4,12},{8,0},{12,4},{1,9},{5,13},{9,1},{13,5},{2,10},{6,14},... | collective-permute-start | bytes 196616 | tf_op jit(solution)/shard_map/ppermute | solution.py:28
  79.6 9.3 %collective-permute-start.24 = (bf16[32,1024]{1,0:T(8,128)(2,1)S(1)}, bf16[32,1024]{1,0:T(8,128)(2,1)S(1)}, u32[]{:S(2)}, u32[]{:S(2)}) collective-permute-start(bf16[32,1024]{1,0:T(8,128)(2,1)S(1)} %get-tuple-element.72), channel_id=1, source_target_pairs={{0,12},{4,8},{8,4},{12,0},{1,13},{5,9},{9,5},{13,1},{2,14},{6,10},... | collective-permute-start | bytes 196616 | tf_op jit(solution)/shard_map/ppermute | solution.py:28
  81.8 7.1 %collective-permute-start.21 = (bf16[32,1024]{1,0:T(8,128)(2,1)S(1)}, bf16[32,1024]{1,0:T(8,128)(2,1)S(1)}, u32[]{:S(2)}, u32[]{:S(2)}) collective-permute-start(bf16[32,1024]{1,0:T(8,128)(2,1)S(1)} %get-tuple-element.69), channel_id=1, source_target_pairs={{0,4},{4,0},{8,12},{12,8},{1,5},{5,1},{9,13},{13,9},{2,6},{6,2},{1... | collective-permute-start | bytes 196616 | tf_op jit(solution)/shard_map/ppermute | solution.py:28
  82.8 8.8 %collective-permute-start.23 = (bf16[32,1024]{1,0:T(8,128)(2,1)S(1)}, bf16[32,1024]{1,0:T(8,128)(2,1)S(1)}, u32[]{:S(2)}, u32[]{:S(2)}) collective-permute-start(bf16[32,1024]{1,0:T(8,128)(2,1)S(1)} %get-tuple-element.71), channel_id=1, source_target_pairs={{0,8},{4,12},{8,0},{12,4},{1,9},{5,13},{9,1},{13,5},{2,10},{6,14},... | collective-permute-start | bytes 196616 | tf_op jit(solution)/shard_map/ppermute | solution.py:28
  84.9 6.7 %collective-permute-start.25 = (bf16[32,1024]{1,0:T(8,128)(2,1)S(1)}, bf16[32,1024]{1,0:T(8,128)(2,1)S(1)}, u32[]{:S(2)}, u32[]{:S(2)}) collective-permute-start(bf16[32,1024]{1,0:T(8,128)(2,1)S(1)} %get-tuple-element.73), channel_id=1, source_target_pairs={{0,12},{4,8},{8,4},{12,0},{1,13},{5,9},{9,5},{13,1},{2,14},{6,10},... | collective-permute-start | bytes 196616 | tf_op jit(solution)/shard_map/ppermute | solution.py:28
  (2 other events, 1.3 us)

commit v5 on v4

v5 whole, which is shorter than its diff:
```python
import functools
import math

import jax
import jax.numpy as jnp
import ml_dtypes
import numpy as np
from jax import lax
from jax.experimental import pallas as pl
from jax.experimental.pallas import tpu as pltpu
from jax.sharding import PartitionSpec as P

EPSILON = 1e-06
MIB = 1 << 20
LANES = 128
CORE, COLUMN, ORDER, BLOCK, COUNT = 0, 1, 2, 8, 16
BF16 = jnp.bfloat16
F32 = jnp.float32
VMEM = pl.BlockSpec(memory_space=pltpu.VMEM)
SMEM = pl.BlockSpec(memory_space=pltpu.SMEM)
HBM = pl.BlockSpec(memory_space=pltpu.HBM)


def swapped(value, axis, size, step):
    assert size & (size - 1) == 0
    if step == 0:
        return value
    return lax.ppermute(value, axis, [(i, i ^ step) for i in range(size)])


def params(mib):
    return pltpu.CompilerParams(vmem_limit_bytes=mib * MIB)


SMALL = pl.CostEstimate(flops=1, bytes_accessed=1, transcendentals=0)
LARGE = pl.CostEstimate(flops=10**12, bytes_accessed=64 * MIB, transcendentals=0)


def tables(classes, span, period, bins_dev, columns, cores):
    u = np.arange(span, dtype=np.int64)[None, :]
    piece = np.arange(columns * cores, dtype=np.int64)[:, None]
    first = piece % cores * bins_dev + piece // cores * (bins_dev // columns)
    rows = (first + np.arange(classes)).reshape(-1)
    high = 16 * classes * np.arange(LANES // 16, dtype=np.int64)
    low = classes * np.arange(16, dtype=np.int64)
    angle = (np.concatenate([rows, high, low])[:, None] * u % period) * (2.0 * math.pi / period)
    return np.stack([np.cos(angle), np.sin(angle)]).astype(np.float32)


def fetch(pairs, sems):
    copies = [pltpu.make_async_copy(a, b, sems.at[i]) for i, (a, b) in enumerate(pairs)]
    for c in copies:
        c.start()
    for c in copies:
        c.wait()


def index_kernel(blocks, direct, *refs):
    given, refs = refs[:5], refs[5:]
    scal, wanted, rec_ids, held, sems = refs[0], refs[1:-7], refs[-7], refs[-6:-1], refs[-1]
    fetch(zip(given, held), sems)
    window_keep, owners, pair_count, src, rec = held
    place = lax.axis_index("recv")
    column, columns = lax.axis_index("win"), lax.axis_size("win")
    core = lax.axis_index("freq")
    scal[CORE] = core
    scal[COLUMN] = column
    scal[ORDER] = 1 - window_keep[0]
    for b in range(blocks):
        unit = place ^ owners[b] if direct else b
        scal[BLOCK + unit] = b
        scal[COUNT + unit] = pair_count[b]
    for d, out in enumerate(wanted):
        chosen = jnp.full(out.shape, -1, jnp.int32)
        received = jnp.zeros(out.shape, jnp.int32)
        for b in range(blocks):
            mine = jnp.full(out.shape, owners[b], jnp.int32) == (place ^ d)
            chosen = jnp.where(mine, src[b : b + 1], chosen)
            received = jnp.where(mine, rec[b : b + 1], received)
        out[...] = chosen
        if direct:
            rec_ids[d : d + 1] = received
    if not direct:
        rec_ids[...] = rec[...]


def index(window_keep, owners, pair_count, pair_src, pair_rec, places):
    blocks, slots = pair_src.shape
    ids = jax.ShapeDtypeStruct((1, slots), jnp.int32)
    given = [window_keep, owners, pair_count[:, 0], pair_src, pair_rec]
    scal, *wanted, rec_ids = pl.pallas_call(
        functools.partial(index_kernel, blocks, places == blocks),
        out_shape=[jax.ShapeDtypeStruct((LANES,), jnp.int32)]
        + [ids] * places
        + [jax.ShapeDtypeStruct(pair_rec.shape, jnp.int32)],
        in_specs=[HBM] * 5,
        out_specs=[SMEM] + [VMEM] * (places + 1),
        scratch_shapes=[pltpu.SMEM(g.shape, g.dtype) for g in given[:3]]
        + [pltpu.VMEM(g.shape, g.dtype) for g in given[3:]]
        + [pltpu.SemaphoreType.DMA((5,))],
        compiler_params=params(16),
        cost_estimate=SMALL,
        name="index",
    )(*given)
    return scal, wanted, rec_ids


def table_kernel(classes, parts, scal, given, spectra, table, perm, here, trig, base, sems):
    part = here.shape[-1]
    bins = pl.ds(pl.multiple_of(scal[COLUMN] * part, part), part)
    fetch([(given, trig), (spectra.at[0, :, :, bins], here)], sems)
    rows = parts * classes
    low = slice(rows + LANES // 16, rows + LANES // 16 + 16)
    cl, sl = trig[0, low], trig[1, low]
    for h in range(LANES // 16):
        ch, sh = trig[0, rows + h : rows + h + 1], trig[1, rows + h : rows + h + 1]
        base[0, 16 * h : 16 * h + 16] = ch * cl - sh * sl
        base[1, 16 * h : 16 * h + 16] = sh * cl + ch * sl
    first = (scal[CORE] + 2 * scal[COLUMN]) * classes
    cb, sb = base[0], base[1]
    for r in range(classes):
        ca, sa = trig[0, pl.ds(first + r, 1)], trig[1, pl.ds(first + r, 1)]
        table[r, :LANES] = (ca * cb - sa * sb).astype(BF16)
        table[r, LANES:] = (-(sa * cb + ca * sb)).astype(BF16)
    source = lax.broadcasted_iota(jnp.int32, (part, LANES), 0)
    target = classes * lax.broadcasted_iota(jnp.int32, (part, LANES), 1)
    for r in range(classes):
        perm[:, r * LANES : (r + 1) * LANES] = (source == target + r).astype(BF16)


def make_table(scal, spectra, trig, classes, span, parts, part):
    channels = spectra.shape[2]
    return pl.pallas_call(
        functools.partial(table_kernel, classes, parts),
        out_shape=[
            jax.ShapeDtypeStruct((classes, 2 * LANES, span), BF16),
            jax.ShapeDtypeStruct((part, part), BF16),
            jax.ShapeDtypeStruct((2, channels, part), BF16),
        ],
        in_specs=[SMEM, HBM, HBM],
        out_specs=[VMEM] * 3,
        scratch_shapes=[
            pltpu.VMEM(trig.shape, F32),
            pltpu.VMEM((2, LANES, span), F32),
            pltpu.SemaphoreType.DMA((2,)),
        ],
        compiler_params=params(24),
        cost_estimate=SMALL,
        name="table",
    )(scal, jnp.asarray(trig), spectra)


def picks(ids, channels):
    row = jnp.concatenate([i[...] for i in ids], axis=1)
    return (lax.broadcasted_iota(jnp.int32, (channels, row.shape[1]), 0) == row).astype(BF16)


def rows_kernel(used, sends, messages, scal, here, *refs):
    held, refs = refs[:used], refs[used:]
    perm, src_ids, rec_ids, refs = refs[0], refs[1 : 1 + sends], refs[1 + sends], refs[2 + sends :]
    outs, own_out = refs[:-1], refs[-1]
    units, _, _, slots, part = own_out.shape
    channels = here.shape[1]
    pick = picks(list(src_ids) + [rec_ids.at[d : d + 1] for d in range(units)], channels)
    for u in range(used):
        for half in range(2):
            x = here[half]
            for s in range(used):
                x = jnp.where(scal[ORDER + u] == s + 1, held[s][0, half], x)
            x = jnp.dot(x, perm[...], preferred_element_type=F32).astype(BF16)
            y = lax.dot_general(
                pick, x, (((0,), (0,)), ((), ())), preferred_element_type=F32
            ).astype(BF16)
            for (d, first, count), out in zip(messages, outs):
                at = d * slots + first
                out[u, half] = y[at : at + count]
            for d in range(units):
                at = (sends + d) * slots
                own_out[d, u, half] = y[at : at + slots]


def gather_rows(scal, here, held, perm, src_ids, rec_ids, messages):
    used, sends = len(held), len(src_ids)
    part = held[0].shape[-1]
    units, slots = rec_ids.shape
    *sent, own = pl.pallas_call(
        functools.partial(rows_kernel, used, sends, messages),
        out_shape=[jax.ShapeDtypeStruct((used, 2, m[2], part), BF16) for m in messages]
        + [jax.ShapeDtypeStruct((units, used, 2, slots, part), BF16)],
        in_specs=[SMEM] + [VMEM] * (used + 3 + sends),
        out_specs=[VMEM] * (len(messages) + 1),
        compiler_params=params(32),
        cost_estimate=SMALL,
        name="rows",
    )(scal, here, *held, perm, *src_ids, rec_ids)
    return sent, own


def combine(values, classes, outputs, origin, span, period):
    plain, scaled = [None] * outputs, [None] * outputs

    def add(into, k, value, sign):
        if into[k] is None:
            into[k] = value if sign > 0 else -value
        else:
            into[k] = into[k] + value if sign > 0 else into[k] - value

    for r, (real, imag) in enumerate(values):
        both = None
        for k in range(outputs):
            eighths = r * (span * k - origin) * 8 // period % 8
            assert r * (span * k - origin) * 8 % period == 0
            if eighths % 2 == 0:
                value, sign = ((real, 1), (imag, -1), (real, -1), (imag, 1))[eighths // 2]
                add(plain, k, value, sign)
            else:
                if both is None:
                    both = real + imag, real - imag
                value, sign = ((both[1], 1), (both[0], -1), (both[1], -1), (both[0], 1))[eighths // 2]
                add(scaled, k, value, sign)
    root = math.sqrt(0.5)
    return [a if b is None else a + root * b for a, b in zip(plain, scaled)]


def placed(pieces):
    at = 0
    for unit, first, count in pieces:
        yield unit, first, count, slice(at, at + count)
        at += count


def cross_kernel(pieces, weight, *refs):
    s_refs, own, lhs = refs[:-2], refs[-2], refs[-1]
    used = own.shape[1]
    rows = lhs.shape[1] // 2
    for s_ref, (unit, first, count, at) in zip(s_refs, placed(pieces)):
        turned = slice(rows + at.start, rows + at.stop)
        mine = slice(first, first + count)
        sent = mine if s_ref.shape[2] > count else slice(0, count)
        for r in range(lhs.shape[0]):
            bins = slice(r * LANES, (r + 1) * LANES)
            real = imag = None
            for u in range(used):
                sr, si = (s_ref[u, half, sent, bins].astype(F32) for half in range(2))
                rr, ri = (own[unit, u, half, mine, bins].astype(F32) for half in range(2))
                re, im = sr * rr + si * ri, si * rr - sr * ri
                if u:
                    re, im = real + weight[u] * re, imag + weight[u] * im
                real, imag = re, im
            lhs[r, at, :LANES] = real.astype(BF16)
            lhs[r, at, LANES:] = imag.astype(BF16)
            lhs[r, turned, :LANES] = imag.astype(BF16)
            lhs[r, turned, LANES:] = (-real).astype(BF16)


def cross_rows(weight, rows, own, pieces, classes):
    count = sum(p[2] for p in pieces)
    return pl.pallas_call(
        functools.partial(cross_kernel, pieces),
        out_shape=jax.ShapeDtypeStruct((classes, 2 * count, 2 * LANES), BF16),
        in_specs=[SMEM] + [VMEM] * (len(rows) + 1),
        out_specs=VMEM,
        compiler_params=params(16),
        cost_estimate=LARGE,
        name="cross",
    )(weight, *rows, own)


def lags_kernel(geometry, direct, skip, scal, *refs):
    classes, span, outputs, origin, period, chunk = geometry
    lhs, table, keep, *sends, sums = refs[skip:]
    rows = lhs.shape[1] // 2
    lag_dev = keep.shape[-1]
    cores = 2
    for start in range(0, span, chunk):
        values = []
        for r in range(classes):
            y = jnp.dot(lhs[r], table[r, :, start : start + chunk], preferred_element_type=F32)
            values.append((y[:rows], y[rows:]))
        for k, value in enumerate(combine(values, classes, outputs, origin, span, period)):
            lag = span * k + start
            lags = slice(lag % lag_dev, lag % lag_dev + chunk)
            sums[lag // lag_dev, :, lags] = value
    if direct:
        piece = cores * scal[COLUMN] + scal[CORE]
        keep[...] = sums[piece]
        for d, out in enumerate(sends):
            out[...] = sums[piece ^ (d + 1)].astype(BF16)
    else:
        for column in range(keep.shape[0]):
            keep[column] = sums[cores * column + scal[CORE]]
            sends[0][column] = sums[cores * column + 1 - scal[CORE]].astype(BF16)


def lag_parts(scal, after, lhs, table, geometry, columns, lag_dev, direct):
    shape = (lhs.shape[1] // 2, lag_dev)
    pieces = 2 * columns
    if direct:
        outs = [jax.ShapeDtypeStruct(shape, F32)] + [jax.ShapeDtypeStruct(shape, BF16)] * (pieces - 1)
    else:
        outs = [jax.ShapeDtypeStruct((columns, *shape), t) for t in (F32, BF16)]
    return pl.pallas_call(
        functools.partial(lags_kernel, geometry, direct, len(after)),
        out_shape=outs,
        in_specs=[SMEM] + [pl.BlockSpec(memory_space=pl.ANY)] * len(after) + [VMEM] * 2,
        out_specs=[VMEM] * len(outs),
        scratch_shapes=[pltpu.VMEM((pieces, *shape), F32)],
        compiler_params=params(32),
        cost_estimate=SMALL,
        name="lags",
    )(scal, *after, lhs, table)


def cores_kernel(scal, keep, more, own, *sends):
    columns = keep.shape[0]
    for column in range(columns):
        value = keep[column] + more[column].astype(F32)

        @pl.when(scal[COLUMN] == column)
        def _():
            own[...] = value

        for s, out in enumerate(sends):

            @pl.when(scal[COLUMN] ^ (s + 1) == column)
            def _():
                out[...] = value.astype(BF16)


def add_cores(scal, keep, more):
    columns, rows, lag_dev = keep.shape
    return pl.pallas_call(
        cores_kernel,
        out_shape=[jax.ShapeDtypeStruct((rows, lag_dev), F32)]
        + [jax.ShapeDtypeStruct((rows, lag_dev), BF16)] * (columns - 1),
        in_specs=[SMEM, VMEM, VMEM],
        out_specs=[VMEM] * columns,
        compiler_params=params(16),
        cost_estimate=SMALL,
        name="cores",
    )(scal, keep, more)


def stats_kernel(scale, pieces, others, scal, *refs):
    own, more, refs = refs[0], refs[1 : 1 + others], refs[1 + others :]
    targets, (corr, sums) = refs[: len(pieces)], refs[len(pieces) :]
    columns = []
    for target, (unit, first, count, at) in zip(targets, placed(pieces)):
        value = own[at]
        for m in more:
            value = value + m[at].astype(F32)
        slot = first + lax.broadcasted_iota(jnp.int32, (count, 1), 0)
        value = value * jnp.where(slot < scal[COUNT + unit], scale, 0.0)
        corr[at] = value
        square = jnp.sum(value * value, axis=1, keepdims=True)
        product = jnp.sum(value * target[0], axis=1, keepdims=True)
        lane = lax.broadcasted_iota(jnp.int32, (count, LANES), 1)
        columns.append(jnp.where(lane == 0, square, jnp.where(lane == 1, product, 0.0)))
    sums[...] = jnp.concatenate(columns, axis=0).T[:8]


def target_specs(pieces, lag_dev):
    return [
        pl.BlockSpec(
            (1, count, lag_dev),
            lambda i, scal, unit=unit, block=first // count: (scal[BLOCK + unit], block, 0),
        )
        for unit, first, count in pieces
    ]


def whole(shape):
    return pl.BlockSpec(shape, lambda i, scal: (0,) * len(shape))


def lag_stats(scal, scale, pieces, own, more, observed):
    rows, lag_dev = own.shape
    outs = [jax.ShapeDtypeStruct((rows, lag_dev), F32), jax.ShapeDtypeStruct((8, rows), F32)]
    return pl.pallas_call(
        functools.partial(stats_kernel, scale, pieces, len(more)),
        grid_spec=pltpu.PrefetchScalarGridSpec(
            num_scalar_prefetch=1,
            grid=(1,),
            in_specs=[whole(own.shape)] * (1 + len(more)) + target_specs(pieces, lag_dev),
            out_specs=[whole(o.shape) for o in outs],
        ),
        out_shape=outs,
        compiler_params=params(16),
        cost_estimate=SMALL,
        name="stats",
    )(scal, own, *more, *[observed] * len(pieces))


def slot_scales(sums, lag_total):
    total = sums[0][...]
    for s in sums[1:]:
        total = total + s[...]
    rows = total.shape[1]
    square, product = total[0:1], total[1:2]
    inverse = 1.0 / jnp.sqrt(square / lag_total + EPSILON)
    bending = (square * inverse * inverse - product * inverse) / lag_total
    sub = lax.broadcasted_iota(jnp.int32, (LANES, rows), 0)
    both = jnp.where(sub == 0, inverse, jnp.where(sub == 1, bending, 0.0)).T
    return both[:, 0:1], both[:, 1:2]


def gradient_kernel(lag_total, pieces, parts, scal, *refs):
    sums, corr, refs = refs[:parts], refs[parts], refs[parts + 1 :]
    targets, outs = refs[: len(pieces)], refs[len(pieces) :]
    inverse, bending = slot_scales(sums, lag_total)
    for target, out, (unit, first, count, at) in zip(targets, outs, placed(pieces)):
        slot = first + lax.broadcasted_iota(jnp.int32, (count, 1), 0)
        valid = jnp.where(slot < scal[COUNT + unit], inverse[at], 0.0)
        normed = corr[at] * inverse[at]
        out[...] = ((normed - target[0] - normed * bending[at]) * valid).astype(BF16)


def gradients(scal, lag_total, pieces, sums, corr, observed):
    lag_dev = corr.shape[1]
    outs = [jax.ShapeDtypeStruct((p[2], lag_dev), BF16) for p in pieces]
    return pl.pallas_call(
        functools.partial(gradient_kernel, lag_total, pieces, len(sums)),
        grid_spec=pltpu.PrefetchScalarGridSpec(
            num_scalar_prefetch=1,
            grid=(1,),
            in_specs=[whole(sums[0].shape)] * len(sums)
            + [whole(corr.shape)]
            + target_specs(pieces, lag_dev),
            out_specs=[whole(o.shape) for o in outs],
        ),
        out_shape=outs,
        compiler_params=params(16),
        cost_estimate=SMALL,
        name="gradient",
    )(scal, *sums, corr, *[observed] * len(pieces))


def normed_kernel(lag_total, chunks, parts, scal, *refs):
    out = refs[-1]
    for q, pieces in enumerate(chunks):
        sums, corr = refs[q * (parts + 1) : q * (parts + 1) + parts], refs[q * (parts + 1) + parts]
        inverse, _ = slot_scales(sums, lag_total)
        for unit, first, count, at in placed(pieces):

            @pl.when(pl.program_id(0) == unit)
            def _():
                out[0, first : first + count] = corr[at] * inverse[at]


def normed_rows(scal, lag_total, chunks, sums, corr, observed):
    blocks, slots, lag_dev = observed.shape
    ins = [x for s, c in zip(sums, corr) for x in (*s, c)]
    return pl.pallas_call(
        functools.partial(normed_kernel, lag_total, chunks, len(sums[0])),
        grid_spec=pltpu.PrefetchScalarGridSpec(
            num_scalar_prefetch=1,
            grid=(blocks,),
            in_specs=[whole(x.shape) for x in ins],
            out_specs=pl.BlockSpec((1, slots, lag_dev), lambda i, scal: (scal[BLOCK + i], 0, 0)),
        ),
        out_shape=jax.ShapeDtypeStruct(observed.shape, F32),
        compiler_params=params(16),
        cost_estimate=SMALL,
        name="normed",
    )(scal, *ins)


def adjoint_kernel(pieces, *refs):
    ids, parts, out = refs[: len(pieces)], refs[len(pieces) : -1], refs[-1]
    pick = picks([i.at[:, p[1] : p[1] + p[2]] for i, p in zip(ids, pieces)], out.shape[0])
    rows = jnp.concatenate([p[...] for p in parts], axis=0)
    out[...] = jnp.dot(pick, rows, preferred_element_type=F32)


def adjoint_rows(src_ids, pieces, parts, channels):
    lag_dev = parts[0].shape[1]
    return pl.pallas_call(
        functools.partial(adjoint_kernel, pieces),
        out_shape=jax.ShapeDtypeStruct((channels, lag_dev), F32),
        in_specs=[VMEM] * (2 * len(parts)),
        out_specs=VMEM,
        compiler_params=params(16),
        cost_estimate=SMALL,
        name="adjoint",
    )(*[src_ids[p[0]] for p in pieces], *parts)


def shards(spectra, window_keep, owners, pair_src, pair_rec, pair_count, observed):
    columns, cores, places = lax.axis_size("win"), lax.axis_size("freq"), lax.axis_size("recv")
    column, core, place = lax.axis_index("win"), lax.axis_index("freq"), lax.axis_index("recv")
    assert spectra.shape[0] == 1 and cores == 2
    channels, bins_dev = spectra.shape[2:]
    blocks, slots, lag_dev = observed.shape
    lag_total = lag_dev * columns * cores
    bin_total = bins_dev * cores
    period = 2 * bin_total
    part = bins_dev // columns
    classes = part // LANES
    span = period // classes
    geometry = (classes, span, lag_total // span, lag_total // 2, period, 256)
    lag_scale = 1.0 / math.sqrt(bin_total * columns)
    peers = columns * cores
    some = slots // 2
    shifts = range(places)

    held = [
        swapped(
            lax.dynamic_slice(
                spectra, (0, 0, 0, (column ^ s) * part), (1, 2, channels, part)
            ),
            "win",
            columns,
            s,
        )
        for s in range(1, columns)
    ]
    scal, wanted, rec_ids = index(
        window_keep, owners, pair_count, pair_src, pair_rec, places
    )
    if columns == 2:
        weight = jnp.ones((1,), F32)
    else:
        keeps = jnp.stack([swapped(window_keep[0], "win", columns, s) for s in range(columns)])
        ranked = jnp.argsort(-keeps)[: columns - 1].astype(jnp.int32)
        weight = keeps[ranked].astype(F32)
        scal = lax.dynamic_update_slice(scal, ranked, (ORDER,))

    direct = places == blocks
    src_ids = [swapped(x, "recv", places, d) for d, x in zip(shifts, wanted)]
    trig = tables(classes, span, period, bins_dev, columns, cores)
    table, perm, here = make_table(scal, spectra, trig, classes, span, peers, part)
    if direct and blocks == 4:
        chunks = [
            [(1, 0, slots), (2, 0, some), (3, 0, some)],
            [(0, 0, slots), (2, some, some), (3, some, some)],
        ]
    else:
        chunks = [[(d, first, some) for d in range(blocks)] for first in (0, some)]
    if direct:
        messages = [piece for pieces in chunks for piece in pieces]
    else:
        messages = [(d, 0, slots) for d in shifts]
    sent, own_rows = gather_rows(scal, here, held, perm, src_ids, rec_ids, messages)
    arrived = [swapped(x, "recv", places, m[0]) for m, x in zip(messages, sent)]
    if not direct:
        stacked = jnp.stack(arrived)
        whole_rows = [
            lax.dynamic_index_in_dim(stacked, place ^ owners[b], 0, False) for b in range(blocks)
        ]
        arrived = [whole_rows[piece[0]] for pieces in chunks for piece in pieces]
    corrs, all_sums, returned, returned_pieces = [], [], [], []
    after = []
    for q, pieces in enumerate(chunks):
        rows = arrived[len(pieces) * q : len(pieces) * (q + 1)]
        straight = q < len(chunks) - 1
        lhs = cross_rows(weight, rows, own_rows, pieces, classes)
        own, *sends = lag_parts(scal, after, lhs, table, geometry, columns, lag_dev, straight)
        if straight:
            more = [swapped(x, ("win", "freq"), peers, d + 1) for d, x in enumerate(sends)]
            after = more
        else:
            own, *sends = add_cores(scal, own, swapped(sends[0], "freq", cores, 1))
            more = [swapped(x, "win", columns, s + 1) for s, x in enumerate(sends)]
        corr, sums = lag_stats(scal, lag_scale, pieces, own, more, observed)
        sums = [swapped(sums, ("win", "freq"), peers, s) for s in range(peers)]
        grads = gradients(scal, lag_total, pieces, sums, corr, observed)
        if not direct:
            stacked = jnp.stack(list(grads) + [jnp.zeros_like(grads[0])])
            grads = []
            for d in shifts:
                block = jnp.int32(blocks)
                for b in range(blocks):
                    block = jnp.where(owners[b] == place ^ d, b, block)
                grads.append(lax.dynamic_index_in_dim(stacked, block, 0, False))
            pieces = [(d, pieces[0][1], some) for d in shifts]
        returned += [swapped(g, "recv", places, p[0]) for p, g in zip(pieces, grads)]
        returned_pieces += pieces
        corrs.append(corr)
        all_sums.append(sums)
    normed = normed_rows(scal, lag_total, chunks, all_sums, corrs, observed)
    adjoint = adjoint_rows(src_ids, returned_pieces, returned, channels)
    return (normed, adjoint)


def solution(mesh):
    return jax.shard_map(
        shards,
        mesh=mesh,
        in_specs=(
            P("win", None, ("groups", "recv"), "freq"),
            P(("groups", "win")),
            P("groups"),
            P(None, ("groups", "recv")),
            P(None, ("groups", "recv")),
            P(None, ("groups", "recv")),
            P(None, ("groups", "recv"), ("win", "freq")),
        ),
        out_specs=(
            P(None, ("groups", "recv"), ("win", "freq")),
            P(("groups", "recv"), ("win", "freq")),
        ),
        check_vma=False,
    )
```

time: 93 us -> 95.1 us (1.023)
  waiting for transfers between devices: 35.6 us -> 29.6 us
  Pallas kernels: 18.1 us -> 23 us
  starting transfers between devices: 30 us -> 33.9 us
    ppermute x26 -> x25, waiting for transfers between devices: 35.6 us -> 29.6 us  [swapped(): return lax.ppermute(value, axis, [(i, i ^ step) for i in range(size)])]
    pallas_call x10 -> x13, Pallas kernels: 16.6 us -> 22.2 us  [the longest x2 5.7 us: lag_parts(): pl.pallas_call(functools.partial(lags_kernel, geometry, direct, len(after...]
    ppermute x26 -> x25, starting transfers between devices: 30 us -> 33.9 us  [swapped(): return lax.ppermute(value, axis, [(i, i ^ step) for i in range(size)])]
    unnamed x16 -> x38, local copies, waits for them, and re-layouts: 6.51 us -> 5.61 us
  transfers between devices with their start and end apart: 26 -> 25, of which waited for: 12 -> 11; matrix products, arithmetic and copies ran while one was open for 0% -> 0% of each run, Pallas kernels for 10% -> 17%
where the time goes in v5:
time: 95.1 us; the launch traced here: 94.7 us
  starting transfers between devices  33.9 us (36%)
  waiting for transfers between devices  29.6 us (31%)
  Pallas kernels  23 us (24%)
  local copies, waits for them, and re-layouts  6.69 us (7%)
  between operations  1.55 us (2%)
    ppermute x25, starting transfers between devices, swapped(): return lax.ppermute(value, axis, [(i, i ^ step) for i in range(size)])  33.9 us
    ppermute x25, waiting for transfers between devices, swapped(): return lax.ppermute(value, axis, [(i, i ^ step) for i in range(size)])  29.6 us
    pallas_call x2, Pallas kernels, lag_parts(): pl.pallas_call(functools.partial(lags_kernel, geometry, direct, len(after...  5.7 us
    unnamed x38, local copies, waits for them, and re-layouts  5.61 us
    pallas_call x1, Pallas kernels, normed_rows(): pl.pallas_call(functools.partial(normed_kernel, lag_total, chunks, len(su...  3.12 us
    pallas_call x1, Pallas kernels, make_table(): pl.pallas_call(functools.partial(table_kernel, classes, parts), out_shape...  2.72 us
    pallas_call x2, Pallas kernels, lag_stats(): pl.pallas_call(functools.partial(stats_kernel, scale, pieces, len(more)),...  2.71 us
    pallas_call x1, Pallas kernels, gather_rows(): pl.pallas_call(functools.partial(rows_kernel, used, sends, messages), out...  2.47 us
  transfers between devices with their start and end apart: 25, of which 11 were waited for; matrix products, arithmetic and copies ran while one was open for 0% of the time, Pallas kernels for 17%

profile of v5, /device:TPU:0, one launch (start us, length us, event | category | flops | bytes accessed | tf_op | source)
XLA Modules:
  0.0 94.7 jit_solution(626537108275954836)
XLA Ops:
  0.6 1.1 %constant_dynamic-slice_fusion = bf16[1,2,128,1024]{3,2,1,0:T(8,128)(2,1)S(1)} fusion(bf16[1,2,128,2048]{3,2,1,0:T(8,128)(2,1)} %spectra.1, s32[]{:T(128)S(6)} %select_n.3), kind=kLoop, calls=%fused_computation | loop fusion | bytes 1048580 | tf_op jit(solution)/shard_map/dynamic_slice | solution.py:508
  1.7 3.0 %collective-permute-start = (bf16[1,2,128,1024]{3,2,1,0:T(8,128)(2,1)S(1)}, bf16[1,2,128,1024]{3,2,1,0:T(8,128)(2,1)S(1)}, u32[]{:S(2)}, u32[]{:S(2)}) collective-permute-start(bf16[1,2,128,1024]{3,2,1,0:T(8,128)(2,1)S(1)} %constant_dynamic-slice_fusion), channel_id=1, source_target_pairs={{0,2},{2,0},{1,3},{3,1},{4,6},{6,4},{5,7},{7,5},{8,10},{10,8},{9,1... | collective-permute-start | bytes 1572872 | tf_op jit(solution)/shard_map/ppermute | solution.py:28
  8.1 1.2 %index.1 = (s32[128]{0:T(128)S(1)}, s32[1,64]{1,0:T(1,128)S(1)}, s32[1,64]{1,0:T(1,128)S(1)}, s32[1,64]{1,0:T(1,128)S(1)}, s32[1,64]{1,0:T(1,128)S(1)}, /*index=5*/s32[4,64]{1,0:T(4,128)S(1)}) custom-call(s32[1]{0:T(128)S(6)} %copy.10.refs_0_, s32[4]{0:T(128)S(1)} %copy-done.17, s32[4]{0:T(128)S(1)} %bitcast.1, s32[4,64]{1,0:T(4,128)S(1)} %copy-done.11, ...), custom_call_target="tpu_custom_call" | custom-call | flops 1 | bytes 1 | tf_op jit(solution)/shard_map/index/pallas_call | solution.py:91
  9.3 1.6 %collective-permute-start.1 = (s32[1,64]{1,0:T(1,128)S(1)}, s32[1,64]{1,0:T(1,128)S(1)}, u32[]{:S(2)}, u32[]{:S(2)}) collective-permute-start(s32[1,64]{1,0:T(1,128)S(1)} %get-tuple-element.40), channel_id=1, source_target_pairs={{0,4},{4,0},{8,12},{12,8},{1,5},{5,1},{9,13},{13,9},{2,6},{6,2},{1... | collective-permute-start | bytes 776 | tf_op jit(solution)/shard_map/ppermute | solution.py:28
  10.9 2.6 %collective-permute-start.2 = (s32[1,64]{1,0:T(1,128)S(1)}, s32[1,64]{1,0:T(1,128)S(1)}, u32[]{:S(2)}, u32[]{:S(2)}) collective-permute-start(s32[1,64]{1,0:T(1,128)S(1)} %get-tuple-element.41), channel_id=1, source_target_pairs={{0,8},{4,12},{8,0},{12,4},{1,9},{5,13},{9,1},{13,5},{2,10},{6,14},... | collective-permute-start | bytes 776 | tf_op jit(solution)/shard_map/ppermute | solution.py:28
  13.8 1.2 %copy-done.3 = bf16[1,2,128,2048]{3,2,1,0:T(8,128)(2,1)S(1)} copy-done((bf16[1,2,128,2048]{3,2,1,0:T(8,128)(2,1)S(1)}, bf16[1,2,128,2048]{3,2,1,0:T(8,128)(2,1)}, u32[]{:S(2)}) %copy-start.3) | copy-done | bytes 1048600
  15.0 1.0 %copy-done.4 = f32[2,56,1024]{2,1,0:T(8,128)S(1)} copy-done((f32[2,56,1024]{2,1,0:T(8,128)S(1)}, f32[2,56,1024]{2,1,0:T(8,128)}, u32[]{:S(2)}) %copy-start.4) | copy-done | bytes 458776
  16.0 2.7 %table.1 = (bf16[8,256,1024]{2,1,0:T(8,128)(2,1)S(1)}, bf16[1024,1024]{1,0:T(8,128)(2,1)S(1)}, bf16[2,128,1024]{2,1,0:T(8,128)(2,1)S(1)}) custom-call(s32[128]{0:T(128)S(1)} %get-tuple-element.36.scal, f32[2,56,1024]{2,1,0:T(8,128)S(1)} %copy-done.4, bf16[1,2,128,2048]{3,2,1,0:T(8,128)(2,1)S(1)} %copy-done.3), custom_call_target="tpu_custom_call" | custom-call | flops 1 | bytes 1 | tf_op jit(solution)/shard_map/table/pallas_call | solution.py:133
  18.9 2.5 %rows.1 = (bf16[1,2,64,1024]{3,2,1,0:T(8,128)(2,1)S(1)}, bf16[1,2,32,1024]{3,2,1,0:T(8,128)(2,1)S(1)}, bf16[1,2,32,1024]{3,2,1,0:T(8,128)(2,1)S(1)}, bf16[1,2,64...) custom-call(s32[128]{0:T(128)S(1)} %get-tuple-element.36.scal, ...), custom_call_target="tpu_custom_call" | custom-call | flops 1 | bytes 1 | tf_op jit(solution)/shard_map/rows/pallas_call | solution.py:186
  22.0 3.5 %collective-permute-start.5 = (bf16[1,2,32,1024]{3,2,1,0:T(8,128)(2,1)S(1)}, bf16[1,2,32,1024]{3,2,1,0:T(8,128)(2,1)S(1)}, u32[]{:S(2)}, u32[]{:S(2)}) collective-permute-start(bf16[1,2,32,1024]{3,2,1,0:T(8,128)(2,1)S(1)} %get-tuple-element.45), channel_id=1, source_target_pairs={{0,8},{4,12},{8,0},{12,4},{1,9},{5,13},{9,1},{13,5},{2,10},{6,14},... | collective-permute-start | bytes 393224 | tf_op jit(solution)/shard_map/ppermute | solution.py:28
  25.7 1.2 %collective-permute-start.13 = (bf16[1,2,32,1024]{3,2,1,0:T(8,128)(2,1)}, bf16[1,2,32,1024]{3,2,1,0:T(8,128)(2,1)}, u32[]{:S(2)}, u32[]{:S(2)}) collective-permute-start(bf16[1,2,32,1024]{3,2,1,0:T(8,128)(2,1)} %get-tuple-element.56), channel_id=1, source_target_pairs={{0,8},{4,12},{8,0},{12,4},{1,9},{5,13},{9,1},{13,5},{2,10},{6,14},... | collective-permute-start | bytes 393224 | tf_op jit(solution)/shard_map/ppermute | solution.py:28
  26.9 2.4 %collective-permute-start.14 = (bf16[1,2,32,1024]{3,2,1,0:T(8,128)(2,1)}, bf16[1,2,32,1024]{3,2,1,0:T(8,128)(2,1)}, u32[]{:S(2)}, u32[]{:S(2)}) collective-permute-start(bf16[1,2,32,1024]{3,2,1,0:T(8,128)(2,1)} %get-tuple-element.57), channel_id=1, source_target_pairs={{0,12},{4,8},{8,4},{12,0},{1,13},{5,9},{9,5},{13,1},{2,14},{6,10},... | collective-permute-start | bytes 393224 | tf_op jit(solution)/shard_map/ppermute | solution.py:28
  29.3 2.5 %collective-permute-done.5.refs_1_ = bf16[1,2,32,1024]{3,2,1,0:T(8,128)(2,1)S(1)} collective-permute-done((bf16[1,2,32,1024]{3,2,1,0:T(8,128)(2,1)S(1)}, bf16[1,2,32,1024]{3,2,1,0:T(8,128)(2,1)S(1)}, u32[]{:S(2)}, u32[]{:S(2)}) %collective-permute-start.5) | collective-permute-done | bytes 131104 | tf_op jit(solution)/shard_map/ppermute | solution.py:28
  31.8 5.9 %collective-permute-done.6.refs_2_ = bf16[1,2,32,1024]{3,2,1,0:T(8,128)(2,1)S(1)} collective-permute-done((bf16[1,2,32,1024]{3,2,1,0:T(8,128)(2,1)S(1)}, bf16[1,2,32,1024]{3,2,1,0:T(8,128)(2,1)S(1)}, u32[]{:S(2)}, u32[]{:S(2)}) %collective-permute-start.6) | collective-permute-done | bytes 131104 | tf_op jit(solution)/shard_map/ppermute | solution.py:28
  38.7 3.3 %lags.2 = (f32[128,1024]{1,0:T(8,128)S(1)}, bf16[128,1024]{1,0:T(8,128)(2,1)}, bf16[128,1024]{1,0:T(8,128)(2,1)}, bf16[128,1024]{1,0:T(8,128)(2,1)}) custom-call(s32[128]{0:T(128)S(1)} %copy-done.6, bf16[8,256,256]{2,1,0:T(8,128)(2,1)S(1)} %cross.2.refs_0_, bf16[8,256,1024]{2,1,0:T(8,128)(2,1)S(1)} %get-tuple-element.48.refs_1_.refs_4_), custom_call_target="tpu_custom_call" | custom-call | flops 1 | bytes 1 | tf_op jit(solution)/shard_map/lags/pallas_call | solution.py:302
  42.5 1.3 %collective-permute-start.9 = (bf16[128,1024]{1,0:T(8,128)(2,1)}, bf16[128,1024]{1,0:T(8,128)(2,1)}, u32[]{:S(2)}, u32[]{:S(2)}) collective-permute-start(bf16[128,1024]{1,0:T(8,128)(2,1)} %get-tuple-element.52), channel_id=1, source_target_pairs={{0,3},{1,2},{2,1},{3,0},{4,7},{5,6},{6,5},{7,4},{8,11},{9,10},{10,... | collective-permute-start | bytes 786440 | tf_op jit(solution)/shard_map/ppermute | solution.py:28
  43.8 2.1 %collective-permute-done.13.refs_1_ = bf16[1,2,32,1024]{3,2,1,0:T(8,128)(2,1)} collective-permute-done((bf16[1,2,32,1024]{3,2,1,0:T(8,128)(2,1)}, bf16[1,2,32,1024]{3,2,1,0:T(8,128)(2,1)}, u32[]{:S(2)}, u32[]{:S(2)}) %collective-permute-start.13) | collective-permute-done | bytes 131104 | tf_op jit(solution)/shard_map/ppermute | solution.py:28
  46.0 1.4 %cross.3.refs_3_ = bf16[8,256,256]{2,1,0:T(8,128)(2,1)S(1)} custom-call(f32[1]{0:T(128)} %constant.3.clone.1.weight, bf16[1,2,64,1024]{3,2,1,0:T(8,128)(2,1)S(1)} %get-tuple-element.55.refs_0_, bf16[1,2,32,1024]{3,2,1,0:T(8,128)(2,1)} %collective-permute-done.13.refs_1_, bf16[1,2,32,1024]{3,2,1,0:T(8,128)(2,1)} %collective-permute-done.14.refs_2_, ...), custom_call_target="tpu_custom_call" | custom-call | flops 999999995904 | bytes 67108864 | tf_op jit(solution)/shard_map/cross/pallas_call | solution.py:258
  47.4 4.0 %collective-permute-done.8.refs_2_.refs_1_ = bf16[128,1024]{1,0:T(8,128)(2,1)} collective-permute-done((bf16[128,1024]{1,0:T(8,128)(2,1)}, bf16[128,1024]{1,0:T(8,128)(2,1)}, u32[]{:S(2)}, u32[]{:S(2)}) %collective-permute-start.8) | collective-permute-done | bytes 262176 | tf_op jit(solution)/shard_map/ppermute | solution.py:28
  51.4 4.8 %collective-permute-done.9.refs_3_.refs_2_ = bf16[128,1024]{1,0:T(8,128)(2,1)} collective-permute-done((bf16[128,1024]{1,0:T(8,128)(2,1)}, bf16[128,1024]{1,0:T(8,128)(2,1)}, u32[]{:S(2)}, u32[]{:S(2)}) %collective-permute-start.9) | collective-permute-done | bytes 262176 | tf_op jit(solution)/shard_map/ppermute | solution.py:28
  56.2 2.4 %lags.3 = (f32[2,128,1024]{2,1,0:T(8,128)S(1)}, bf16[2,128,1024]{2,1,0:T(8,128)(2,1)S(1)}) custom-call(s32[128]{0:T(128)S(1)} %copy-done.6, bf16[128,1024]{1,0:T(8,128)(2,1)} %collective-permute-done.7.refs_1_.refs_0_, bf16[128,1024]{1,0:T(8,128)(2,1)} %collective-permute-done.8.refs_2_.refs_1_, bf16[128,1024]{1,0:T(8,128)(2,1)} %collective-permute-done.9.refs_3_.refs_2_, ...), custom_call_target="tpu_custom_call" | custom-call | flops 1 | bytes 1 | tf_op jit(solution)/shard_map/lags/pallas_call | solution.py:302
  59.0 1.7 %collective-permute-done.15.more = bf16[2,128,1024]{2,1,0:T(8,128)(2,1)S(1)} collective-permute-done((bf16[2,128,1024]{2,1,0:T(8,128)(2,1)S(1)}, bf16[2,128,1024]{2,1,0:T(8,128)(2,1)S(1)}, u32[]{:S(2)}, u32[]{:S(2)}) %collective-permute-start.15) | collective-permute-done | bytes 524320 | tf_op jit(solution)/shard_map/ppermute | solution.py:28
  62.0 1.9 %stats.2 = (f32[128,1024]{1,0:T(8,128)S(1)}, f32[8,128]{1,0:T(8,128)S(1)}) custom-call(s32[128]{0:T(128)S(1)} %copy-done.6, f32[128,1024]{1,0:T(8,128)S(1)} %get-tuple-element.49.refs_0_, bf16[128,1024]{1,0:T(8,128)(2,1)} %collective-permute-done.7.refs_1_.refs_0_, bf16[128,1024]{1,0:T(8,128)(2,1)} %collective-permute-done.8.refs_2_.refs_1_, ...), custom_call_target="tpu_custom_call" | custom-call | flops 1 | bytes 1 | tf_op jit(solution)/shard_map/stats/pallas_call | solution.py:379
  63.9 1.1 %collective-permute-start.12 = (f32[8,128]{1,0:T(8,128)S(1)}, f32[8,128]{1,0:T(8,128)S(1)}, u32[]{:S(2)}, u32[]{:S(2)}) collective-permute-start(f32[8,128]{1,0:T(8,128)S(1)} %get-tuple-element.53.refs_0_), channel_id=1, source_target_pairs={{0,3},{1,2},{2,1},{3,0},{4,7},{5,6},{6,5},{7,4},{8,11},{9,10},{10,... | collective-permute-start | bytes 12296 | tf_op jit(solution)/shard_map/ppermute | solution.py:28
  65.8 3.4 %collective-permute-done.12.refs_3_ = f32[8,128]{1,0:T(8,128)S(1)} collective-permute-done((f32[8,128]{1,0:T(8,128)S(1)}, f32[8,128]{1,0:T(8,128)S(1)}, u32[]{:S(2)}, u32[]{:S(2)}) %collective-permute-start.12) | collective-permute-done | bytes 4128 | tf_op jit(solution)/shard_map/ppermute | solution.py:28
  70.9 6.8 %collective-permute-start.20 = (bf16[64,1024]{1,0:T(8,128)(2,1)S(1)}, bf16[64,1024]{1,0:T(8,128)(2,1)S(1)}, u32[]{:S(2)}, u32[]{:S(2)}) collective-permute-start(bf16[64,1024]{1,0:T(8,128)(2,1)S(1)} %get-tuple-element.64), channel_id=1, source_target_pairs={{0,4},{4,0},{8,12},{12,8},{1,5},{5,1},{9,13},{13,9},{2,6},{6,2},{1... | collective-permute-start | bytes 393224 | tf_op jit(solution)/shard_map/ppermute | solution.py:28
  78.5 1.4 %collective-permute-start.18 = (f32[8,128]{1,0:T(8,128)S(1)}, f32[8,128]{1,0:T(8,128)S(1)}, u32[]{:S(2)}, u32[]{:S(2)}) collective-permute-start(f32[8,128]{1,0:T(8,128)S(1)} %get-tuple-element.62.refs_5_.refs_0_), channel_id=1, source_target_pairs={{0,2},{1,3},{2,0},{3,1},{4,6},{5,7},{6,4},{7,5},{8,10},{9,11},{10,... | collective-permute-start | bytes 12296 | tf_op jit(solution)/shard_map/ppermute | solution.py:28
  81.6 1.9 %collective-permute-start.22 = (bf16[32,1024]{1,0:T(8,128)(2,1)S(1)}, bf16[32,1024]{1,0:T(8,128)(2,1)S(1)}, u32[]{:S(2)}, u32[]{:S(2)}) collective-permute-start(bf16[32,1024]{1,0:T(8,128)(2,1)S(1)} %get-tuple-element.66), channel_id=1, source_target_pairs={{0,12},{4,8},{8,4},{12,0},{1,13},{5,9},{9,5},{13,1},{2,14},{6,10},... | collective-permute-start | bytes 196616 | tf_op jit(solution)/shard_map/ppermute | solution.py:28
  85.2 2.0 %collective-permute-start.24 = (bf16[32,1024]{1,0:T(8,128)(2,1)S(1)}, bf16[32,1024]{1,0:T(8,128)(2,1)S(1)}, u32[]{:S(2)}, u32[]{:S(2)}) collective-permute-start(bf16[32,1024]{1,0:T(8,128)(2,1)S(1)} %get-tuple-element.69), channel_id=1, source_target_pairs={{0,12},{4,8},{8,4},{12,0},{1,13},{5,9},{9,5},{13,1},{2,14},{6,10},... | collective-permute-start | bytes 196616 | tf_op jit(solution)/shard_map/ppermute | solution.py:28
  87.1 3.1 %normed.1 = f32[4,64,1024]{2,1,0:T(8,128)} custom-call(s32[128]{0:T(128)S(1)} %copy-done.6, f32[8,128]{1,0:T(8,128)S(1)} %get-tuple-element.53.refs_0_, f32[8,128]{1,0:T(8,128)S(1)} %collective-permute-done.10.refs_1_, f32[8,128]{1,0:T(8,128)S(1)} %collective-permute-done.11.refs_2_, f32[8,128]{1,0:T(8,128)S(1)} %collective-permute-done.12.refs_3_, ...), custom_call_target="tpu_custom_call" | custom-call | flops 1 | bytes 1 | tf_op jit(solution)/shard_map/normed/pallas_call | solution.py:453
  90.3 3.3 %collective-permute-done.23.refs_10_ = bf16[32,1024]{1,0:T(8,128)(2,1)S(1)} collective-permute-done((bf16[32,1024]{1,0:T(8,128)(2,1)S(1)}, bf16[32,1024]{1,0:T(8,128)(2,1)S(1)}, u32[]{:S(2)}, u32[]{:S(2)}) %collective-permute-start.23) | collective-permute-done | bytes 65568 | tf_op jit(solution)/shard_map/ppermute | solution.py:28
  93.6 1.1 %adjoint.1 = f32[128,1024]{1,0:T(8,128)} custom-call(s32[1,64]{1,0:T(1,128)S(1)} %copy-done.16, s32[1,64]{1,0:T(1,128)S(1)} %copy-done.8, s32[1,64]{1,0:T(1,128)S(1)} %copy-done.10, s32[1,64]{1,0:T(1,128)S(1)} %copy-done.14, s32[1,64]{1,0:T(1,128)S(1)} %copy-done.8, s32[1,64]{1,0:T(1,128)S(1)} %copy-done.10, ...), custom_call_target="tpu_custom_call" | custom-call | flops 1 | bytes 1 | tf_op jit(solution)/shard_map/adjoint/pallas_call | solution.py:477
  (71 shorter events, 13.6 us)
Async XLA Ops:
  1.7 17.2 %collective-permute-start = (bf16[1,2,128,1024]{3,2,1,0:T(8,128)(2,1)S(1)}, bf16[1,2,128,1024]{3,2,1,0:T(8,128)(2,1)S(1)}, u32[]{:S(2)}, u32[]{:S(2)}) collective-permute-start(bf16[1,2,128,1024]{3,2,1,0:T(8,128)(2,1)S(1)} %constant_dynamic-slice_fusion), channel_id=1, source_target_pairs={{0,2},{2,0},{1,3},{3,1},{4,6},{6,4},{5,7},{7,5},{8,10},{10,8},{9,1... | collective-permute-start | bytes 1572872 | tf_op jit(solution)/shard_map/ppermute | solution.py:28
  9.3 28.5 %copy-start.13 = (s32[1,64]{1,0:T(1,128)}, s32[1,64]{1,0:T(1,128)S(1)}, u32[]{:S(2)}) copy-start(s32[1,64]{1,0:T(1,128)S(1)} %get-tuple-element.39.refs_2_.refs_3_) | copy-start | bytes 772
  9.3 28.7 %copy-start.5 = (s32[128]{0:T(128)}, s32[128]{0:T(128)S(1)}, u32[]{:S(2)}) copy-start(s32[128]{0:T(128)S(1)} %get-tuple-element.36.scal) | copy-start | bytes 1540
  9.3 9.4 %collective-permute-start.1 = (s32[1,64]{1,0:T(1,128)S(1)}, s32[1,64]{1,0:T(1,128)S(1)}, u32[]{:S(2)}, u32[]{:S(2)}) collective-permute-start(s32[1,64]{1,0:T(1,128)S(1)} %get-tuple-element.40), channel_id=1, source_target_pairs={{0,4},{4,0},{8,12},{12,8},{1,5},{5,1},{9,13},{13,9},{2,6},{6,2},{1... | collective-permute-start | bytes 776 | tf_op jit(solution)/shard_map/ppermute | solution.py:28
  10.9 7.8 %collective-permute-start.2 = (s32[1,64]{1,0:T(1,128)S(1)}, s32[1,64]{1,0:T(1,128)S(1)}, u32[]{:S(2)}, u32[]{:S(2)}) collective-permute-start(s32[1,64]{1,0:T(1,128)S(1)} %get-tuple-element.41), channel_id=1, source_target_pairs={{0,8},{4,12},{8,0},{12,4},{1,9},{5,13},{9,1},{13,5},{2,10},{6,14},... | collective-permute-start | bytes 776 | tf_op jit(solution)/shard_map/ppermute | solution.py:28
  13.5 5.3 %collective-permute-start.3 = (s32[1,64]{1,0:T(1,128)S(1)}, s32[1,64]{1,0:T(1,128)S(1)}, u32[]{:S(2)}, u32[]{:S(2)}) collective-permute-start(s32[1,64]{1,0:T(1,128)S(1)} %get-tuple-element.42), channel_id=1, source_target_pairs={{0,12},{4,8},{8,4},{12,0},{1,13},{5,9},{9,5},{13,1},{2,14},{6,10},... | collective-permute-start | bytes 776 | tf_op jit(solution)/shard_map/ppermute | solution.py:28
  18.7 19.3 %copy-start.1 = (bf16[8,256,1024]{2,1,0:T(8,128)(2,1)}, bf16[8,256,1024]{2,1,0:T(8,128)(2,1)S(1)}, u32[]{:S(2)}) copy-start(bf16[8,256,1024]{2,1,0:T(8,128)(2,1)S(1)} %get-tuple-element.48.refs_1_.refs_4_) | copy-start | bytes 12582916
  18.8 19.3 %copy-start.15 = (s32[1,64]{1,0:T(1,128)}, s32[1,64]{1,0:T(1,128)S(1)}, u32[]{:S(2)}) copy-start(s32[1,64]{1,0:T(1,128)S(1)} %collective-permute-done.1.refs_3_.refs_0_) | copy-start | bytes 772
  18.8 19.3 %copy-start.7 = (s32[1,64]{1,0:T(1,128)}, s32[1,64]{1,0:T(1,128)S(1)}, u32[]{:S(2)}) copy-start(s32[1,64]{1,0:T(1,128)S(1)} %collective-permute-done.2.refs_4_.refs_1_) | copy-start | bytes 772
  18.9 19.2 %copy-start.9 = (s32[1,64]{1,0:T(1,128)}, s32[1,64]{1,0:T(1,128)S(1)}, u32[]{:S(2)}) copy-start(s32[1,64]{1,0:T(1,128)S(1)} %collective-permute-done.3.refs_5_.refs_2_) | copy-start | bytes 772
  21.3 16.4 %collective-permute-start.4 = (bf16[1,2,64,1024]{3,2,1,0:T(8,128)(2,1)S(1)}, bf16[1,2,64,1024]{3,2,1,0:T(8,128)(2,1)S(1)}, u32[]{:S(2)}, u32[]{:S(2)}) collective-permute-start(bf16[1,2,64,1024]{3,2,1,0:T(8,128)(2,1)S(1)} %get-tuple-element.44), channel_id=1, source_target_pairs={{0,4},{4,0},{8,12},{12,8},{1,5},{5,1},{9,13},{13,9},{2,6},{6,2},{1... | collective-permute-start | bytes 786440 | tf_op jit(solution)/shard_map/ppermute | solution.py:28
  22.0 9.8 %collective-permute-start.5 = (bf16[1,2,32,1024]{3,2,1,0:T(8,128)(2,1)S(1)}, bf16[1,2,32,1024]{3,2,1,0:T(8,128)(2,1)S(1)}, u32[]{:S(2)}, u32[]{:S(2)}) collective-permute-start(bf16[1,2,32,1024]{3,2,1,0:T(8,128)(2,1)S(1)} %get-tuple-element.45), channel_id=1, source_target_pairs={{0,8},{4,12},{8,0},{12,4},{1,9},{5,13},{9,1},{13,5},{2,10},{6,14},... | collective-permute-start | bytes 393224 | tf_op jit(solution)/shard_map/ppermute | solution.py:28
  25.5 12.3 %collective-permute-start.6 = (bf16[1,2,32,1024]{3,2,1,0:T(8,128)(2,1)S(1)}, bf16[1,2,32,1024]{3,2,1,0:T(8,128)(2,1)S(1)}, u32[]{:S(2)}, u32[]{:S(2)}) collective-permute-start(bf16[1,2,32,1024]{3,2,1,0:T(8,128)(2,1)S(1)} %get-tuple-element.46), channel_id=1, source_target_pairs={{0,12},{4,8},{8,4},{12,0},{1,13},{5,9},{9,5},{13,1},{2,14},{6,10},... | collective-permute-start | bytes 393224 | tf_op jit(solution)/shard_map/ppermute | solution.py:28
  25.7 20.2 %collective-permute-start.13 = (bf16[1,2,32,1024]{3,2,1,0:T(8,128)(2,1)}, bf16[1,2,32,1024]{3,2,1,0:T(8,128)(2,1)}, u32[]{:S(2)}, u32[]{:S(2)}) collective-permute-start(bf16[1,2,32,1024]{3,2,1,0:T(8,128)(2,1)} %get-tuple-element.56), channel_id=1, source_target_pairs={{0,8},{4,12},{8,0},{12,4},{1,9},{5,13},{9,1},{13,5},{2,10},{6,14},... | collective-permute-start | bytes 393224 | tf_op jit(solution)/shard_map/ppermute | solution.py:28
  26.9 19.1 %collective-permute-start.14 = (bf16[1,2,32,1024]{3,2,1,0:T(8,128)(2,1)}, bf16[1,2,32,1024]{3,2,1,0:T(8,128)(2,1)}, u32[]{:S(2)}, u32[]{:S(2)}) collective-permute-start(bf16[1,2,32,1024]{3,2,1,0:T(8,128)(2,1)} %get-tuple-element.57), channel_id=1, source_target_pairs={{0,12},{4,8},{8,4},{12,0},{1,13},{5,9},{9,5},{13,1},{2,14},{6,10},... | collective-permute-start | bytes 393224 | tf_op jit(solution)/shard_map/ppermute | solution.py:28
  42.0 5.4 %collective-permute-start.7 = (bf16[128,1024]{1,0:T(8,128)(2,1)}, bf16[128,1024]{1,0:T(8,128)(2,1)}, u32[]{:S(2)}, u32[]{:S(2)}) collective-permute-start(bf16[128,1024]{1,0:T(8,128)(2,1)} %get-tuple-element.50), channel_id=1, source_target_pairs={{0,1},{1,0},{2,3},{3,2},{4,5},{5,4},{6,7},{7,6},{8,9},{9,8},{10,11... | collective-permute-start | bytes 786440 | tf_op jit(solution)/shard_map/ppermute | solution.py:28
  42.0 9.4 %collective-permute-start.8 = (bf16[128,1024]{1,0:T(8,128)(2,1)}, bf16[128,1024]{1,0:T(8,128)(2,1)}, u32[]{:S(2)}, u32[]{:S(2)}) collective-permute-start(bf16[128,1024]{1,0:T(8,128)(2,1)} %get-tuple-element.51), channel_id=1, source_target_pairs={{0,2},{1,3},{2,0},{3,1},{4,6},{5,7},{6,4},{7,5},{8,10},{9,11},{10,... | collective-permute-start | bytes 786440 | tf_op jit(solution)/shard_map/ppermute | solution.py:28
  42.5 13.7 %collective-permute-start.9 = (bf16[128,1024]{1,0:T(8,128)(2,1)}, bf16[128,1024]{1,0:T(8,128)(2,1)}, u32[]{:S(2)}, u32[]{:S(2)}) collective-permute-start(bf16[128,1024]{1,0:T(8,128)(2,1)} %get-tuple-element.52), channel_id=1, source_target_pairs={{0,3},{1,2},{2,1},{3,0},{4,7},{5,6},{6,5},{7,4},{8,11},{9,10},{10,... | collective-permute-start | bytes 786440 | tf_op jit(solution)/shard_map/ppermute | solution.py:28
  58.7 2.0 %collective-permute-start.15 = (bf16[2,128,1024]{2,1,0:T(8,128)(2,1)S(1)}, bf16[2,128,1024]{2,1,0:T(8,128)(2,1)S(1)}, u32[]{:S(2)}, u32[]{:S(2)}) collective-permute-start(bf16[2,128,1024]{2,1,0:T(8,128)(2,1)S(1)} %get-tuple-element.59), channel_id=1, source_target_pairs={{0,1},{1,0},{2,3},{3,2},{4,5},{5,4},{6,7},{7,6},{8,9},{9,8},{10,11... | collective-permute-start | bytes 1572872 | tf_op jit(solution)/shard_map/ppermute | solution.py:28
  61.4 16.3 %collective-permute-start.16 = (bf16[128,1024]{1,0:T(8,128)(2,1)S(1)}, bf16[128,1024]{1,0:T(8,128)(2,1)S(1)}, u32[]{:S(2)}, u32[]{:S(2)}) collective-permute-start(bf16[128,1024]{1,0:T(8,128)(2,1)S(1)} %get-tuple-element.61), channel_id=1, source_target_pairs={{0,2},{2,0},{1,3},{3,1},{4,6},{6,4},{5,7},{7,5},{8,10},{10,8},{9,1... | collective-permute-start | bytes 786440 | tf_op jit(solution)/shard_map/ppermute | solution.py:28
  63.9 5.3 %collective-permute-start.12 = (f32[8,128]{1,0:T(8,128)S(1)}, f32[8,128]{1,0:T(8,128)S(1)}, u32[]{:S(2)}, u32[]{:S(2)}) collective-permute-start(f32[8,128]{1,0:T(8,128)S(1)} %get-tuple-element.53.refs_0_), channel_id=1, source_target_pairs={{0,3},{1,2},{2,1},{3,0},{4,7},{5,6},{6,5},{7,4},{8,11},{9,10},{10,... | collective-permute-start | bytes 12296 | tf_op jit(solution)/shard_map/ppermute | solution.py:28
  65.0 5.1 %collective-permute-start.11 = (f32[8,128]{1,0:T(8,128)S(1)}, f32[8,128]{1,0:T(8,128)S(1)}, u32[]{:S(2)}, u32[]{:S(2)}) collective-permute-start(f32[8,128]{1,0:T(8,128)S(1)} %get-tuple-element.53.refs_0_), channel_id=1, source_target_pairs={{0,2},{1,3},{2,0},{3,1},{4,6},{5,7},{6,4},{7,5},{8,10},{9,11},{10,... | collective-permute-start | bytes 12296 | tf_op jit(solution)/shard_map/ppermute | solution.py:28
  65.6 4.5 %collective-permute-start.10 = (f32[8,128]{1,0:T(8,128)S(1)}, f32[8,128]{1,0:T(8,128)S(1)}, u32[]{:S(2)}, u32[]{:S(2)}) collective-permute-start(f32[8,128]{1,0:T(8,128)S(1)} %get-tuple-element.53.refs_0_), channel_id=1, source_target_pairs={{0,1},{1,0},{2,3},{3,2},{4,5},{5,4},{6,7},{7,6},{8,9},{9,8},{10,11... | collective-permute-start | bytes 12296 | tf_op jit(solution)/shard_map/ppermute | solution.py:28
  70.9 19.4 %collective-permute-start.20 = (bf16[64,1024]{1,0:T(8,128)(2,1)S(1)}, bf16[64,1024]{1,0:T(8,128)(2,1)S(1)}, u32[]{:S(2)}, u32[]{:S(2)}) collective-permute-start(bf16[64,1024]{1,0:T(8,128)(2,1)S(1)} %get-tuple-element.64), channel_id=1, source_target_pairs={{0,4},{4,0},{8,12},{12,8},{1,5},{5,1},{9,13},{13,9},{2,6},{6,2},{1... | collective-permute-start | bytes 393224 | tf_op jit(solution)/shard_map/ppermute | solution.py:28
  77.7 15.9 %copy-start.16 = (s32[1,64]{1,0:T(1,128)S(1)}, s32[1,64]{1,0:T(1,128)}, u32[]{:S(2)}) copy-start(s32[1,64]{1,0:T(1,128)} %copy-done.15) | copy-start | bytes 772
  78.5 3.1 %collective-permute-start.19 = (f32[8,128]{1,0:T(8,128)S(1)}, f32[8,128]{1,0:T(8,128)S(1)}, u32[]{:S(2)}, u32[]{:S(2)}) collective-permute-start(f32[8,128]{1,0:T(8,128)S(1)} %get-tuple-element.62.refs_5_.refs_0_), channel_id=1, source_target_pairs={{0,3},{1,2},{2,1},{3,0},{4,7},{5,6},{6,5},{7,4},{8,11},{9,10},{10,... | collective-permute-start | bytes 12296 | tf_op jit(solution)/shard_map/ppermute | solution.py:28
  78.5 4.9 %collective-permute-start.18 = (f32[8,128]{1,0:T(8,128)S(1)}, f32[8,128]{1,0:T(8,128)S(1)}, u32[]{:S(2)}, u32[]{:S(2)}) collective-permute-start(f32[8,128]{1,0:T(8,128)S(1)} %get-tuple-element.62.refs_5_.refs_0_), channel_id=1, source_target_pairs={{0,2},{1,3},{2,0},{3,1},{4,6},{5,7},{6,4},{7,5},{8,10},{9,11},{10,... | collective-permute-start | bytes 12296 | tf_op jit(solution)/shard_map/ppermute | solution.py:28
  79.9 3.5 %collective-permute-start.17 = (f32[8,128]{1,0:T(8,128)S(1)}, f32[8,128]{1,0:T(8,128)S(1)}, u32[]{:S(2)}, u32[]{:S(2)}) collective-permute-start(f32[8,128]{1,0:T(8,128)S(1)} %get-tuple-element.62.refs_5_.refs_0_), channel_id=1, source_target_pairs={{0,1},{1,0},{2,3},{3,2},{4,5},{5,4},{6,7},{7,6},{8,9},{9,8},{10,11... | collective-permute-start | bytes 12296 | tf_op jit(solution)/shard_map/ppermute | solution.py:28
  80.4 9.9 %collective-permute-start.21 = (bf16[32,1024]{1,0:T(8,128)(2,1)S(1)}, bf16[32,1024]{1,0:T(8,128)(2,1)S(1)}, u32[]{:S(2)}, u32[]{:S(2)}) collective-permute-start(bf16[32,1024]{1,0:T(8,128)(2,1)S(1)} %get-tuple-element.65), channel_id=1, source_target_pairs={{0,8},{4,12},{8,0},{12,4},{1,9},{5,13},{9,1},{13,5},{2,10},{6,14},... | collective-permute-start | bytes 196616 | tf_op jit(solution)/shard_map/ppermute | solution.py:28
  81.6 8.7 %collective-permute-start.22 = (bf16[32,1024]{1,0:T(8,128)(2,1)S(1)}, bf16[32,1024]{1,0:T(8,128)(2,1)S(1)}, u32[]{:S(2)}, u32[]{:S(2)}) collective-permute-start(bf16[32,1024]{1,0:T(8,128)(2,1)S(1)} %get-tuple-element.66), channel_id=1, source_target_pairs={{0,12},{4,8},{8,4},{12,0},{1,13},{5,9},{9,5},{13,1},{2,14},{6,10},... | collective-permute-start | bytes 196616 | tf_op jit(solution)/shard_map/ppermute | solution.py:28
  84.2 9.4 %collective-permute-start.23 = (bf16[32,1024]{1,0:T(8,128)(2,1)S(1)}, bf16[32,1024]{1,0:T(8,128)(2,1)S(1)}, u32[]{:S(2)}, u32[]{:S(2)}) collective-permute-start(bf16[32,1024]{1,0:T(8,128)(2,1)S(1)} %get-tuple-element.68), channel_id=1, source_target_pairs={{0,8},{4,12},{8,0},{12,4},{1,9},{5,13},{9,1},{13,5},{2,10},{6,14},... | collective-permute-start | bytes 196616 | tf_op jit(solution)/shard_map/ppermute | solution.py:28
  85.2 8.4 %collective-permute-start.24 = (bf16[32,1024]{1,0:T(8,128)(2,1)S(1)}, bf16[32,1024]{1,0:T(8,128)(2,1)S(1)}, u32[]{:S(2)}, u32[]{:S(2)}) collective-permute-start(bf16[32,1024]{1,0:T(8,128)(2,1)S(1)} %get-tuple-element.69), channel_id=1, source_target_pairs={{0,12},{4,8},{8,4},{12,0},{1,13},{5,9},{9,5},{13,1},{2,14},{6,10},... | collective-permute-start | bytes 196616 | tf_op jit(solution)/shard_map/ppermute | solution.py:28
  (12 other events, 78.2 us)

commit v6 on v5

--- a/solution.py
+++ b/solution.py
@@ -13,6 +13,7 @@
 EPSILON = 1e-06
 MIB = 1 << 20
 LANES = 128
+SPLIT = 4
 CORE, COLUMN, ORDER, BLOCK, COUNT = 0, 1, 2, 8, 16
 BF16 = jnp.bfloat16
 F32 = jnp.float32
@@ -33,7 +34,7 @@
 
 
 SMALL = pl.CostEstimate(flops=1, bytes_accessed=1, transcendentals=0)
-LARGE = pl.CostEstimate(flops=10**12, bytes_accessed=64 * MIB, transcendentals=0)
+LARGE = pl.CostEstimate(flops=2 * 10**10, bytes_accessed=MIB, transcendentals=0)
 
 
 def tables(classes, span, period, bins_dev, columns, cores):
@@ -105,10 +106,7 @@
     return scal, wanted, rec_ids
 
 
-def table_kernel(classes, parts, scal, given, spectra, table, perm, here, trig, base, sems):
-    part = here.shape[-1]
-    bins = pl.ds(pl.multiple_of(scal[COLUMN] * part, part), part)
-    fetch([(given, trig), (spectra.at[0, :, :, bins], here)], sems)
+def table_kernel(classes, parts, scal, trig, table, base):
     rows = parts * classes
     low = slice(rows + LANES // 16, rows + LANES // 16 + 16)
     cl, sl = trig[0, low], trig[1, low]
@@ -122,32 +120,39 @@
         ca, sa = trig[0, pl.ds(first + r, 1)], trig[1, pl.ds(first + r, 1)]
         table[r, :LANES] = (ca * cb - sa * sb).astype(BF16)
         table[r, LANES:] = (-(sa * cb + ca * sb)).astype(BF16)
+
+
+def make_table(scal, trig, classes, span, parts):
+    return pl.pallas_call(
+        functools.partial(table_kernel, classes, parts),
+        out_shape=jax.ShapeDtypeStruct((classes, 2 * LANES, span), BF16),
+        in_specs=[SMEM, VMEM],
+        out_specs=VMEM,
+        scratch_shapes=[pltpu.VMEM((2, LANES, span), F32)],
+        compiler_params=params(12),
+        cost_estimate=SMALL,
+        name="table",
+    )(scal, jnp.asarray(trig))
+
+
+def perm_kernel(perm):
+    part = perm.shape[0]
+    classes = part // LANES
     source = lax.broadcasted_iota(jnp.int32, (part, LANES), 0)
     target = classes * lax.broadcasted_iota(jnp.int32, (part, LANES), 1)
     for r in range(classes):
         perm[:, r * LANES : (r + 1) * LANES] = (source == target + r).astype(BF16)
 
 
-def make_table(scal, spectra, trig, classes, span, parts, part):
-    channels = spectra.shape[2]
-    return pl.pallas_call(
-        functools.partial(table_kernel, classes, parts),
-        out_shape=[
-            jax.ShapeDtypeStruct((classes, 2 * LANES, span), BF16),
-            jax.ShapeDtypeStruct((part, part), BF16),
-            jax.ShapeDtypeStruct((2, channels, part), BF16),
-        ],
-        in_specs=[SMEM, HBM, HBM],
-        out_specs=[VMEM] * 3,
-        scratch_shapes=[
-            pltpu.VMEM(trig.shape, F32),
-            pltpu.VMEM((2, LANES, span), F32),
-            pltpu.SemaphoreType.DMA((2,)),
-        ],
-        compiler_params=params(24),
-        cost_estimate=SMALL,
-        name="table",
-    )(scal, jnp.asarray(trig), spectra)
+def make_perm(part):
+    return pl.pallas_call(
+        perm_kernel,
+        out_shape=jax.ShapeDtypeStruct((part, part), BF16),
+        out_specs=VMEM,
+        compiler_params=params(8),
+        cost_estimate=SMALL,
+        name="perm",
+    )()
 
 
 def picks(ids, channels):
@@ -160,11 +165,11 @@
     perm, src_ids, rec_ids, refs = refs[0], refs[1 : 1 + sends], refs[1 + sends], refs[2 + sends :]
     outs, own_out = refs[:-1], refs[-1]
     units, _, _, slots, part = own_out.shape
-    channels = here.shape[1]
+    channels = here.shape[2]
     pick = picks(list(src_ids) + [rec_ids.at[d : d + 1] for d in range(units)], channels)
     for u in range(used):
         for half in range(2):
-            x = here[half]
+            x = here[0, half]
             for s in range(used):
                 x = jnp.where(scal[ORDER + u] == s + 1, held[s][0, half], x)
             x = jnp.dot(x, perm[...], preferred_element_type=F32).astype(BF16)
@@ -189,7 +194,7 @@
         + [jax.ShapeDtypeStruct((units, used, 2, slots, part), BF16)],
         in_specs=[SMEM] + [VMEM] * (used + 3 + sends),
         out_specs=[VMEM] * (len(messages) + 1),
-        compiler_params=params(32),
+        compiler_params=params(16),
         cost_estimate=SMALL,
         name="rows",
     )(scal, here, *held, perm, *src_ids, rec_ids)
@@ -260,13 +265,13 @@
         out_shape=jax.ShapeDtypeStruct((classes, 2 * count, 2 * LANES), BF16),
         in_specs=[SMEM] + [VMEM] * (len(rows) + 1),
         out_specs=VMEM,
-        compiler_params=params(16),
+        compiler_params=params(8),
         cost_estimate=LARGE,
         name="cross",
     )(weight, *rows, own)
 
 
-def lags_kernel(geometry, direct, skip, scal, *refs):
+def lags_kernel(geometry, skip, scal, *refs):
     classes, span, outputs, origin, period, chunk = geometry
     lhs, table, keep, *sends, sums = refs[skip:]
     rows = lhs.shape[1] // 2
@@ -281,64 +286,61 @@
             lag = span * k + start
             lags = slice(lag % lag_dev, lag % lag_dev + chunk)
             sums[lag // lag_dev, :, lags] = value
-    if direct:
-        piece = cores * scal[COLUMN] + scal[CORE]
-        keep[...] = sums[piece]
-        for d, out in enumerate(sends):
-            out[...] = sums[piece ^ (d + 1)].astype(BF16)
-    else:
-        for column in range(keep.shape[0]):
-            keep[column] = sums[cores * column + scal[CORE]]
-            sends[0][column] = sums[cores * column + 1 - scal[CORE]].astype(BF16)
-
-
-def lag_parts(scal, after, lhs, table, geometry, columns, lag_dev, direct):
-    shape = (lhs.shape[1] // 2, lag_dev)
-    pieces = 2 * columns
-    if direct:
-        outs = [jax.ShapeDtypeStruct(shape, F32)] + [jax.ShapeDtypeStruct(shape, BF16)] * (pieces - 1)
-    else:
-        outs = [jax.ShapeDtypeStruct((columns, *shape), t) for t in (F32, BF16)]
-    return pl.pallas_call(
-        functools.partial(lags_kernel, geometry, direct, len(after)),
-        out_shape=outs,
+    for column in range(keep.shape[0]):
+        keep[column] = sums[cores * column + scal[CORE]]
+        for i, out in enumerate(sends):
+            at = slice(i * out.shape[1], (i + 1) * out.shape[1])
+            out[column] = sums[cores * column + 1 - scal[CORE], at].astype(BF16)
+
+
+def lag_parts(scal, after, lhs, table, geometry, columns, lag_dev, split):
+    rows = lhs.shape[1] // 2
+    shape = lambda count: (columns, count, lag_dev)
+    return pl.pallas_call(
+        functools.partial(lags_kernel, geometry, len(after)),
+        out_shape=[jax.ShapeDtypeStruct(shape(rows), F32)]
+        + [jax.ShapeDtypeStruct(shape(rows // split), BF16)] * split,
         in_specs=[SMEM] + [pl.BlockSpec(memory_space=pl.ANY)] * len(after) + [VMEM] * 2,
-        out_specs=[VMEM] * len(outs),
-        scratch_shapes=[pltpu.VMEM((pieces, *shape), F32)],
-        compiler_params=params(32),
-        cost_estimate=SMALL,
+        out_specs=[VMEM] * (split + 1),
+        scratch_shapes=[pltpu.VMEM((2 * columns, rows, lag_dev), F32)],
+        compiler_params=params(16),
+        cost_estimate=LARGE,
         name="lags",
     )(scal, *after, lhs, table)
 
 
-def cores_kernel(scal, keep, more, own, *sends):
+def cores_kernel(skip, split, scal, *refs):
+    keep, *refs = refs[skip:]
+    more, own, sends = refs[:split], refs[split], refs[split + 1 :]
     columns = keep.shape[0]
-    for column in range(columns):
-        value = keep[column] + more[column].astype(F32)
-
-        @pl.when(scal[COLUMN] == column)
-        def _():
-            own[...] = value
-
-        for s, out in enumerate(sends):
-
-            @pl.when(scal[COLUMN] ^ (s + 1) == column)
+    for i, m in enumerate(more):
+        at = slice(i * m.shape[1], (i + 1) * m.shape[1])
+        for column in range(columns):
+            value = keep[column, at] + m[column].astype(F32)
+
+            @pl.when(scal[COLUMN] == column)
             def _():
-                out[...] = value.astype(BF16)
-
-
-def add_cores(scal, keep, more):
+                own[at] = value
+
+            for s, out in enumerate(sends):
+
+                @pl.when(scal[COLUMN] ^ (s + 1) == column)
+                def _():
+                    out[at] = value.astype(BF16)
+
+
+def add_cores(scal, after, keep, more):
     columns, rows, lag_dev = keep.shape
     return pl.pallas_call(
-        cores_kernel,
+        functools.partial(cores_kernel, len(after), len(more)),
         out_shape=[jax.ShapeDtypeStruct((rows, lag_dev), F32)]
         + [jax.ShapeDtypeStruct((rows, lag_dev), BF16)] * (columns - 1),
-        in_specs=[SMEM, VMEM, VMEM],
+        in_specs=[SMEM] + [pl.BlockSpec(memory_space=pl.ANY)] * len(after) + [VMEM] * (1 + len(more)),
         out_specs=[VMEM] * columns,
-        compiler_params=params(16),
+        compiler_params=params(8),
         cost_estimate=SMALL,
         name="cores",
-    )(scal, keep, more)
+    )(scal, *after, keep, *more)
 
 
 def stats_kernel(scale, pieces, others, scal, *refs):
@@ -512,7 +514,7 @@
             columns,
             s,
         )
-        for s in range(1, columns)
+        for s in range(columns)
     ]
     scal, wanted, rec_ids = index(
         window_keep, owners, pair_count, pair_src, pair_rec, places
@@ -528,7 +530,7 @@
     direct = places == blocks
     src_ids = [swapped(x, "recv", places, d) for d, x in zip(shifts, wanted)]
     trig = tables(classes, span, period, bins_dev, columns, cores)
-    table, perm, here = make_table(scal, spectra, trig, classes, span, peers, part)
+    table = make_table(scal, trig, classes, span, peers)
     if direct and blocks == 4:
         chunks = [
             [(1, 0, slots), (2, 0, some), (3, 0, some)],
@@ -540,7 +542,9 @@
         messages = [piece for pieces in chunks for piece in pieces]
     else:
         messages = [(d, 0, slots) for d in shifts]
-    sent, own_rows = gather_rows(scal, here, held, perm, src_ids, rec_ids, messages)
+    sent, own_rows = gather_rows(
+        scal, held[0], held[1:], make_perm(part), src_ids, rec_ids, messages
+    )
     arrived = [swapped(x, "recv", places, m[0]) for m, x in zip(messages, sent)]
     if not direct:
         stacked = jnp.stack(arrived)
@@ -552,15 +556,14 @@
     after = []
     for q, pieces in enumerate(chunks):
         rows = arrived[len(pieces) * q : len(pieces) * (q + 1)]
-        straight = q < len(chunks) - 1
         lhs = cross_rows(weight, rows, own_rows, pieces, classes)
-        own, *sends = lag_parts(scal, after, lhs, table, geometry, columns, lag_dev, straight)
-        if straight:
-            more = [swapped(x, ("win", "freq"), peers, d + 1) for d, x in enumerate(sends)]
-            after = more
-        else:
-            own, *sends = add_cores(scal, own, swapped(sends[0], "freq", cores, 1))
-            more = [swapped(x, "win", columns, s + 1) for s, x in enumerate(sends)]
+        keep, *sends = lag_parts(
+            scal, after[:1], lhs, table, geometry, columns, lag_dev, SPLIT if q else 1
+        )
+        sends = [swapped(x, "freq", cores, 1) for x in sends]
+        own, *sends = add_cores(scal, after[1:], keep, sends)
+        more = [swapped(x, "win", columns, s + 1) for s, x in enumerate(sends)]
+        after = [own, *more]
         corr, sums = lag_stats(scal, lag_scale, pieces, own, more, observed)
         sums = [swapped(sums, ("win", "freq"), peers, s) for s in range(peers)]
         grads = gradients(scal, lag_total, pieces, sums, corr, observed)

time: 95.1 us -> 82.7 us (0.87)
  Pallas kernels: 23 us -> 19.5 us
  waiting for transfers between devices: 29.6 us -> 26.1 us
  local copies, waits for them, and re-layouts: 6.69 us -> 4 us
  starting transfers between devices: 33.9 us -> 31.5 us
    ppermute x25 -> x27, waiting for transfers between devices: 29.6 us -> 26.1 us  [swapped(): return lax.ppermute(value, axis, [(i, i ^ step) for i in range(size)])]
    unnamed x38 -> x12, local copies, waits for them, and re-layouts: 5.61 us -> 2.68 us
    ppermute x25 -> x27, starting transfers between devices: 33.9 us -> 31.5 us  [swapped(): return lax.ppermute(value, axis, [(i, i ^ step) for i in range(size)])]
    pallas_call x2, Pallas kernels: 2.71 us -> 1.54 us  [lag_stats(): pl.pallas_call(functools.partial(stats_kernel, scale, pieces, len(more)),...]
    pallas_call x2, Pallas kernels: 1.64 us -> 0.52 us  [cross_rows(): pl.pallas_call(functools.partial(cross_kernel, pieces), out_shape=jax.Sha...]
    pallas_call x3 -> x5, Pallas kernels: 6.42 us -> 6.82 us  [the longest x2 4.79 us: lag_parts(): pl.pallas_call(functools.partial(lags_kernel, geometry, len(after)), out_...]
  transfers between devices with their start and end apart: 25 -> 27, of which waited for: 11 -> 14; matrix products, arithmetic and copies ran while one was open for 0% -> 0% of each run, Pallas kernels for 17% -> 18%
where the time goes in v6:
time: 82.7 us; the launch traced here: 82.5 us
  starting transfers between devices  31.5 us (38%)
  waiting for transfers between devices  26.1 us (32%)
  Pallas kernels  19.5 us (24%)
  local copies, waits for them, and re-layouts  4 us (5%)
  between operations  1.48 us (2%)
    ppermute x27, starting transfers between devices, swapped(): return lax.ppermute(value, axis, [(i, i ^ step) for i in range(size)])  31.5 us
    ppermute x27, waiting for transfers between devices, swapped(): return lax.ppermute(value, axis, [(i, i ^ step) for i in range(size)])  26.1 us
    pallas_call x2, Pallas kernels, lag_parts(): pl.pallas_call(functools.partial(lags_kernel, geometry, len(after)), out_...  4.79 us
    pallas_call x1, Pallas kernels, normed_rows(): pl.pallas_call(functools.partial(normed_kernel, lag_total, chunks, len(su...  3.12 us
    unnamed x12, local copies, waits for them, and re-layouts  2.68 us
    pallas_call x1, Pallas kernels, gather_rows(): pl.pallas_call(functools.partial(rows_kernel, used, sends, messages), out...  1.83 us
    pallas_call x1, Pallas kernels, make_table(): pl.pallas_call(functools.partial(table_kernel, classes, parts), out_shape...  1.77 us
  transfers between devices with their start and end apart: 27, of which 14 were waited for; matrix products, arithmetic and copies ran while one was open for 0% of the time, Pallas kernels for 18%

profile of v6, /device:TPU:0, one launch (start us, length us, event | category | flops | bytes accessed | tf_op | source)
XLA Modules:
  0.0 82.5 jit_solution(6558009456761039994)
XLA Ops:
  0.7 1.3 %constant_dynamic-slice_fusion = (bf16[1,2,128,1024]{3,2,1,0:T(8,128)(2,1)S(1)}, bf16[1,2,128,1024]{3,2,1,0:T(8,128)(2,1)S(1)}) fusion(bf16[1,2,128,2048]{3,2,1,0:T(8,128)(2,1)} %param.8, s32[]{:T(128)S(6)} %select_n.7, s32[]{:T(128)S(6)} %select_n.6), kind=kLoop, calls=%fused_computation | loop fusion | bytes 2097160 | tf_op jit(solution)/shard_map/dynamic_slice | solution.py:510
  2.0 3.0 %collective-permute-start = (bf16[1,2,128,1024]{3,2,1,0:T(8,128)(2,1)S(1)}, bf16[1,2,128,1024]{3,2,1,0:T(8,128)(2,1)S(1)}, u32[]{:S(2)}, u32[]{:S(2)}) collective-permute-start(bf16[1,2,128,1024]{3,2,1,0:T(8,128)(2,1)S(1)} %get-tuple-element.70), channel_id=1, source_target_pairs={{0,2},{2,0},{1,3},{3,1},{4,6},{6,4},{5,7},{7,5},{8,10},{10,8},{9,1... | collective-permute-start | bytes 1572872 | tf_op jit(solution)/shard_map/ppermute | solution.py:29
  8.3 1.2 %index.1 = (s32[128]{0:T(128)S(1)}, s32[1,64]{1,0:T(1,128)S(1)}, s32[1,64]{1,0:T(1,128)S(1)}, s32[1,64]{1,0:T(1,128)S(1)}, s32[1,64]{1,0:T(1,128)S(1)}, /*index=5*/s32[4,64]{1,0:T(4,128)S(1)}) custom-call(s32[1]{0:T(128)S(6)} %copy.10.refs_0_, s32[4]{0:T(128)S(1)} %copy-done.4, s32[4]{0:T(128)S(1)} %bitcast.1, s32[4,64]{1,0:T(4,128)S(1)} %copy-done.2, ...), custom_call_target="tpu_custom_call" | custom-call | flops 1 | bytes 1 | tf_op jit(solution)/shard_map/index/pallas_call | solution.py:92
  9.5 1.6 %collective-permute-start.1 = (s32[1,64]{1,0:T(1,128)S(1)}, s32[1,64]{1,0:T(1,128)S(1)}, u32[]{:S(2)}, u32[]{:S(2)}) collective-permute-start(s32[1,64]{1,0:T(1,128)S(1)} %get-tuple-element.38), channel_id=1, source_target_pairs={{0,4},{4,0},{8,12},{12,8},{1,5},{5,1},{9,13},{13,9},{2,6},{6,2},{1... | collective-permute-start | bytes 776 | tf_op jit(solution)/shard_map/ppermute | solution.py:29
  11.2 2.6 %collective-permute-start.2 = (s32[1,64]{1,0:T(1,128)S(1)}, s32[1,64]{1,0:T(1,128)S(1)}, u32[]{:S(2)}, u32[]{:S(2)}) collective-permute-start(s32[1,64]{1,0:T(1,128)S(1)} %get-tuple-element.39), channel_id=1, source_target_pairs={{0,8},{4,12},{8,0},{12,4},{1,9},{5,13},{9,1},{13,5},{2,10},{6,14},... | collective-permute-start | bytes 776 | tf_op jit(solution)/shard_map/ppermute | solution.py:29
  14.6 1.0 %collective-permute-done.2.refs_4_.refs_1_ = s32[1,64]{1,0:T(1,128)S(1)} collective-permute-done((s32[1,64]{1,0:T(1,128)S(1)}, s32[1,64]{1,0:T(1,128)S(1)}, u32[]{:S(2)}, u32[]{:S(2)}) %collective-permute-start.2) | collective-permute-done | bytes 288 | tf_op jit(solution)/shard_map/ppermute | solution.py:29
  15.6 3.5 %collective-permute-done.3.refs_5_.refs_2_ = s32[1,64]{1,0:T(1,128)S(1)} collective-permute-done((s32[1,64]{1,0:T(1,128)S(1)}, s32[1,64]{1,0:T(1,128)S(1)}, u32[]{:S(2)}, u32[]{:S(2)}) %collective-permute-start.3) | collective-permute-done | bytes 288 | tf_op jit(solution)/shard_map/ppermute | solution.py:29
  19.1 1.8 %rows.1 = (bf16[1,2,64,1024]{3,2,1,0:T(8,128)(2,1)S(1)}, bf16[1,2,32,1024]{3,2,1,0:T(8,128)(2,1)S(1)}, bf16[1,2,32,1024]{3,2,1,0:T(8,128)(2,1)S(1)}, bf16[1,2,64...) custom-call(s32[128]{0:T(128)S(1)} %get-tuple-element.36.scal, ...), custom_call_target="tpu_custom_call" | custom-call | flops 1 | bytes 1 | tf_op jit(solution)/shard_map/rows/pallas_call | solution.py:191
  21.0 2.2 %collective-permute-start.5 = (bf16[1,2,32,1024]{3,2,1,0:T(8,128)(2,1)S(1)}, bf16[1,2,32,1024]{3,2,1,0:T(8,128)(2,1)S(1)}, u32[]{:S(2)}, u32[]{:S(2)}) collective-permute-start(bf16[1,2,32,1024]{3,2,1,0:T(8,128)(2,1)S(1)} %get-tuple-element.43), channel_id=1, source_target_pairs={{0,8},{4,12},{8,0},{12,4},{1,9},{5,13},{9,1},{13,5},{2,10},{6,14},... | collective-permute-start | bytes 393224 | tf_op jit(solution)/shard_map/ppermute | solution.py:29
  23.2 2.2 %collective-permute-start.6 = (bf16[1,2,32,1024]{3,2,1,0:T(8,128)(2,1)S(1)}, bf16[1,2,32,1024]{3,2,1,0:T(8,128)(2,1)S(1)}, u32[]{:S(2)}, u32[]{:S(2)}) collective-permute-start(bf16[1,2,32,1024]{3,2,1,0:T(8,128)(2,1)S(1)} %get-tuple-element.44), channel_id=1, source_target_pairs={{0,12},{4,8},{8,4},{12,0},{1,13},{5,9},{9,5},{13,1},{2,14},{6,10},... | collective-permute-start | bytes 393224 | tf_op jit(solution)/shard_map/ppermute | solution.py:29
  25.4 1.8 %table.1.refs_1_.refs_2_ = bf16[8,256,1024]{2,1,0:T(8,128)(2,1)S(1)} custom-call(s32[128]{0:T(128)S(1)} %get-tuple-element.36.scal, f32[2,56,1024]{2,1,0:T(8,128)S(1)} %copy-done.1), custom_call_target="tpu_custom_call" | custom-call | flops 1 | bytes 1 | tf_op jit(solution)/shard_map/table/pallas_call | solution.py:126
  27.3 1.7 %collective-permute-start.13 = (bf16[1,2,32,1024]{3,2,1,0:T(8,128)(2,1)S(1)}, bf16[1,2,32,1024]{3,2,1,0:T(8,128)(2,1)S(1)}, u32[]{:S(2)}, u32[]{:S(2)}) collective-permute-start(bf16[1,2,32,1024]{3,2,1,0:T(8,128)(2,1)S(1)} %get-tuple-element.54), channel_id=1, source_target_pairs={{0,12},{4,8},{8,4},{12,0},{1,13},{5,9},{9,5},{13,1},{2,14},{6,10},... | collective-permute-start | bytes 393224 | tf_op jit(solution)/shard_map/ppermute | solution.py:29
  29.0 1.7 %collective-permute-done.5.refs_1_ = bf16[1,2,32,1024]{3,2,1,0:T(8,128)(2,1)S(1)} collective-permute-done((bf16[1,2,32,1024]{3,2,1,0:T(8,128)(2,1)S(1)}, bf16[1,2,32,1024]{3,2,1,0:T(8,128)(2,1)S(1)}, u32[]{:S(2)}, u32[]{:S(2)}) %collective-permute-start.5) | collective-permute-done | bytes 131104 | tf_op jit(solution)/shard_map/ppermute | solution.py:29
  30.6 5.4 %collective-permute-done.6.refs_2_ = bf16[1,2,32,1024]{3,2,1,0:T(8,128)(2,1)S(1)} collective-permute-done((bf16[1,2,32,1024]{3,2,1,0:T(8,128)(2,1)S(1)}, bf16[1,2,32,1024]{3,2,1,0:T(8,128)(2,1)S(1)}, u32[]{:S(2)}, u32[]{:S(2)}) %collective-permute-start.6) | collective-permute-done | bytes 131104 | tf_op jit(solution)/shard_map/ppermute | solution.py:29
  36.3 2.4 %lags.2 = (f32[2,128,1024]{2,1,0:T(8,128)S(1)}, bf16[2,128,1024]{2,1,0:T(8,128)(2,1)S(1)}) custom-call(s32[128]{0:T(128)S(1)} %get-tuple-element.36.scal, bf16[8,256,256]{2,1,0:T(8,128)(2,1)S(1)} %cross.2.refs_0_, bf16[8,256,1024]{2,1,0:T(8,128)(2,1)S(1)} %table.1.refs_1_.refs_2_), custom_call_target="tpu_custom_call" | custom-call | flops 20000000000 | bytes 1048576 | tf_op jit(solution)/shard_map/lags/pallas_call | solution.py:299
  38.8 5.1 %collective-permute-done.12.refs_1_ = bf16[1,2,32,1024]{3,2,1,0:T(8,128)(2,1)S(1)} collective-permute-done((bf16[1,2,32,1024]{3,2,1,0:T(8,128)(2,1)S(1)}, bf16[1,2,32,1024]{3,2,1,0:T(8,128)(2,1)S(1)}, u32[]{:S(2)}, u32[]{:S(2)}) %collective-permute-start.12) | collective-permute-done | bytes 131104 | tf_op jit(solution)/shard_map/ppermute | solution.py:29
  44.9 1.6 %collective-permute-start.8 = (bf16[128,1024]{1,0:T(8,128)(2,1)S(1)}, bf16[128,1024]{1,0:T(8,128)(2,1)S(1)}, u32[]{:S(2)}, u32[]{:S(2)}) collective-permute-start(bf16[128,1024]{1,0:T(8,128)(2,1)S(1)} %get-tuple-element.49), channel_id=1, source_target_pairs={{0,2},{2,0},{1,3},{3,1},{4,6},{6,4},{5,7},{7,5},{8,10},{10,8},{9,1... | collective-permute-start | bytes 786440 | tf_op jit(solution)/shard_map/ppermute | solution.py:29
  46.5 2.4 %lags.3 = (f32[2,128,1024]{2,1,0:T(8,128)S(1)}, bf16[2,32,1024]{2,1,0:T(8,128)(2,1)S(1)}, bf16[2,32,1024]{2,1,0:T(8,128)(2,1)S(1)}, bf16[2,32,1024]{2,1,0:T(8,128)(2,1)S(1)}, bf16[2,32,1024]{2,1,0:T(8,128)(2,1)S(1)}) custom-call(s32[128]{0:T(128)S(1)} %get-tuple-element.36.scal, f32[128,1024]{1,0:T(8,128)S(1)} %get-tuple-element.48.refs_0_, ...), custom_call_target="tpu_custom_call" | custom-call | flops 20000000000 | bytes 1048576 | tf_op jit(solution)/shard_map/lags/pallas_call | solution.py:299
  52.1 1.6 %collective-permute-start.18 = (bf16[128,1024]{1,0:T(8,128)(2,1)S(1)}, bf16[128,1024]{1,0:T(8,128)(2,1)S(1)}, u32[]{:S(2)}, u32[]{:S(2)}) collective-permute-start(bf16[128,1024]{1,0:T(8,128)(2,1)S(1)} %get-tuple-element.61), channel_id=1, source_target_pairs={{0,2},{2,0},{1,3},{3,1},{4,6},{6,4},{5,7},{7,5},{8,10},{10,8},{9,1... | collective-permute-start | bytes 786440 | tf_op jit(solution)/shard_map/ppermute | solution.py:29
  55.1 1.2 %collective-permute-start.9 = (f32[8,128]{1,0:T(8,128)S(1)}, f32[8,128]{1,0:T(8,128)S(1)}, u32[]{:S(2)}, u32[]{:S(2)}) collective-permute-start(f32[8,128]{1,0:T(8,128)S(1)} %get-tuple-element.50.refs_0_), channel_id=1, source_target_pairs={{0,1},{1,0},{2,3},{3,2},{4,5},{5,4},{6,7},{7,6},{8,9},{9,8},{10,11... | collective-permute-start | bytes 12296 | tf_op jit(solution)/shard_map/ppermute | solution.py:29
  56.3 3.1 %collective-permute-done.11.refs_3_ = f32[8,128]{1,0:T(8,128)S(1)} collective-permute-done((f32[8,128]{1,0:T(8,128)S(1)}, f32[8,128]{1,0:T(8,128)S(1)}, u32[]{:S(2)}, u32[]{:S(2)}) %collective-permute-start.11) | collective-permute-done | bytes 4128 | tf_op jit(solution)/shard_map/ppermute | solution.py:29
  59.4 1.1 %collective-permute-done.10.refs_2_ = f32[8,128]{1,0:T(8,128)S(1)} collective-permute-done((f32[8,128]{1,0:T(8,128)S(1)}, f32[8,128]{1,0:T(8,128)S(1)}, u32[]{:S(2)}, u32[]{:S(2)}) %collective-permute-start.10) | collective-permute-done | bytes 4128 | tf_op jit(solution)/shard_map/ppermute | solution.py:29
  60.5 0.8 gradient.2
  61.3 3.8 %collective-permute-start.22 = (bf16[64,1024]{1,0:T(8,128)(2,1)S(1)}, bf16[64,1024]{1,0:T(8,128)(2,1)S(1)}, u32[]{:S(2)}, u32[]{:S(2)}) collective-permute-start(bf16[64,1024]{1,0:T(8,128)(2,1)S(1)} %get-tuple-element.64), channel_id=1, source_target_pairs={{0,4},{4,0},{8,12},{12,8},{1,5},{5,1},{9,13},{13,9},{2,6},{6,2},{1... | collective-permute-start | bytes 393224 | tf_op jit(solution)/shard_map/ppermute | solution.py:29
  65.9 1.0 %collective-permute-start.21 = (f32[8,128]{1,0:T(8,128)S(1)}, f32[8,128]{1,0:T(8,128)S(1)}, u32[]{:S(2)}, u32[]{:S(2)}) collective-permute-start(f32[8,128]{1,0:T(8,128)S(1)} %get-tuple-element.62.refs_5_.refs_0_), channel_id=1, source_target_pairs={{0,3},{1,2},{2,1},{3,0},{4,7},{5,6},{6,5},{7,4},{8,11},{9,10},{10,... | collective-permute-start | bytes 12296 | tf_op jit(solution)/shard_map/ppermute | solution.py:29
  67.8 1.4 %collective-permute-start.23 = (bf16[32,1024]{1,0:T(8,128)(2,1)S(1)}, bf16[32,1024]{1,0:T(8,128)(2,1)S(1)}, u32[]{:S(2)}, u32[]{:S(2)}) collective-permute-start(bf16[32,1024]{1,0:T(8,128)(2,1)S(1)} %get-tuple-element.65), channel_id=1, source_target_pairs={{0,8},{4,12},{8,0},{12,4},{1,9},{5,13},{9,1},{13,5},{2,10},{6,14},... | collective-permute-start | bytes 196616 | tf_op jit(solution)/shard_map/ppermute | solution.py:29
  69.2 2.6 %collective-permute-start.24 = (bf16[32,1024]{1,0:T(8,128)(2,1)S(1)}, bf16[32,1024]{1,0:T(8,128)(2,1)S(1)}, u32[]{:S(2)}, u32[]{:S(2)}) collective-permute-start(bf16[32,1024]{1,0:T(8,128)(2,1)S(1)} %get-tuple-element.66), channel_id=1, source_target_pairs={{0,12},{4,8},{8,4},{12,0},{1,13},{5,9},{9,5},{13,1},{2,14},{6,10},... | collective-permute-start | bytes 196616 | tf_op jit(solution)/shard_map/ppermute | solution.py:29
  72.7 0.9 %collective-permute-start.25 = (bf16[32,1024]{1,0:T(8,128)(2,1)S(1)}, bf16[32,1024]{1,0:T(8,128)(2,1)S(1)}, u32[]{:S(2)}, u32[]{:S(2)}) collective-permute-start(bf16[32,1024]{1,0:T(8,128)(2,1)S(1)} %get-tuple-element.68), channel_id=1, source_target_pairs={{0,8},{4,12},{8,0},{12,4},{1,9},{5,13},{9,1},{13,5},{2,10},{6,14},... | collective-permute-start | bytes 196616 | tf_op jit(solution)/shard_map/ppermute | solution.py:29
  73.6 1.0 %collective-permute-start.26 = (bf16[32,1024]{1,0:T(8,128)(2,1)S(1)}, bf16[32,1024]{1,0:T(8,128)(2,1)S(1)}, u32[]{:S(2)}, u32[]{:S(2)}) collective-permute-start(bf16[32,1024]{1,0:T(8,128)(2,1)S(1)} %get-tuple-element.69), channel_id=1, source_target_pairs={{0,12},{4,8},{8,4},{12,0},{1,13},{5,9},{9,5},{13,1},{2,14},{6,10},... | collective-permute-start | bytes 196616 | tf_op jit(solution)/shard_map/ppermute | solution.py:29
  74.6 3.1 %normed.1 = f32[4,64,1024]{2,1,0:T(8,128)} custom-call(s32[128]{0:T(128)S(1)} %get-tuple-element.36.scal, f32[8,128]{1,0:T(8,128)S(1)} %get-tuple-element.50.refs_0_, f32[8,128]{1,0:T(8,128)S(1)} %collective-permute-done.9.refs_1_, f32[8,128]{1,0:T(8,128)S(1)} %collective-permute-done.10.refs_2_, f32[8,128]{1,0:T(8,128)S(1)} %collective-permute-done.11.refs_3_, ...), custom_call_target="tpu_custom_call" | custom-call | flops 1 | bytes 1 | tf_op jit(solution)/shard_map/normed/pallas_call | solution.py:455
  77.9 3.5 %collective-permute-done.25.refs_10_ = bf16[32,1024]{1,0:T(8,128)(2,1)S(1)} collective-permute-done((bf16[32,1024]{1,0:T(8,128)(2,1)S(1)}, bf16[32,1024]{1,0:T(8,128)(2,1)S(1)}, u32[]{:S(2)}, u32[]{:S(2)}) %collective-permute-start.25) | collective-permute-done | bytes 65568 | tf_op jit(solution)/shard_map/ppermute | solution.py:29
  81.4 1.1 %adjoint.1 = f32[128,1024]{1,0:T(8,128)} custom-call(s32[1,64]{1,0:T(1,128)S(1)} %collective-permute-done.1.refs_3_.refs_0_, s32[1,64]{1,0:T(1,128)S(1)} %collective-permute-done.2.refs_4_.refs_1_, s32[1,64]{1,0:T(1,128)S(1)} %collective-permute-done.3.refs_5_.refs_2_, s32[1,64]{1,0:T(1,128)S(1)} %get-tuple-element.37.refs_2_.refs_3_, ...), custom_call_target="tpu_custom_call" | custom-call | flops 1 | bytes 1 | tf_op jit(solution)/shard_map/adjoint/pallas_call | solution.py:479
  (51 shorter events, 12.3 us)
Async XLA Ops:
  0.6 24.8 %copy-start.1 = (f32[2,56,1024]{2,1,0:T(8,128)S(1)}, f32[2,56,1024]{2,1,0:T(8,128)}, u32[]{:S(2)}) copy-start(f32[2,56,1024]{2,1,0:T(8,128)} %constant.16.clone.trig) | copy-start | bytes 1376260
  2.0 17.1 %collective-permute-start = (bf16[1,2,128,1024]{3,2,1,0:T(8,128)(2,1)S(1)}, bf16[1,2,128,1024]{3,2,1,0:T(8,128)(2,1)S(1)}, u32[]{:S(2)}, u32[]{:S(2)}) collective-permute-start(bf16[1,2,128,1024]{3,2,1,0:T(8,128)(2,1)S(1)} %get-tuple-element.70), channel_id=1, source_target_pairs={{0,2},{2,0},{1,3},{3,1},{4,6},{6,4},{5,7},{7,5},{8,10},{10,8},{9,1... | collective-permute-start | bytes 1572872 | tf_op jit(solution)/shard_map/ppermute | solution.py:29
  5.6 0.7 copy-start.2
  6.3 0.7 copy-start.3
  7.0 0.7 copy-start.4
  9.5 5.1 %collective-permute-start.1 = (s32[1,64]{1,0:T(1,128)S(1)}, s32[1,64]{1,0:T(1,128)S(1)}, u32[]{:S(2)}, u32[]{:S(2)}) collective-permute-start(s32[1,64]{1,0:T(1,128)S(1)} %get-tuple-element.38), channel_id=1, source_target_pairs={{0,4},{4,0},{8,12},{12,8},{1,5},{5,1},{9,13},{13,9},{2,6},{6,2},{1... | collective-permute-start | bytes 776 | tf_op jit(solution)/shard_map/ppermute | solution.py:29
  11.2 4.4 %collective-permute-start.2 = (s32[1,64]{1,0:T(1,128)S(1)}, s32[1,64]{1,0:T(1,128)S(1)}, u32[]{:S(2)}, u32[]{:S(2)}) collective-permute-start(s32[1,64]{1,0:T(1,128)S(1)} %get-tuple-element.39), channel_id=1, source_target_pairs={{0,8},{4,12},{8,0},{12,4},{1,9},{5,13},{9,1},{13,5},{2,10},{6,14},... | collective-permute-start | bytes 776 | tf_op jit(solution)/shard_map/ppermute | solution.py:29
  13.8 5.3 %collective-permute-start.3 = (s32[1,64]{1,0:T(1,128)S(1)}, s32[1,64]{1,0:T(1,128)S(1)}, u32[]{:S(2)}, u32[]{:S(2)}) collective-permute-start(s32[1,64]{1,0:T(1,128)S(1)} %get-tuple-element.40), channel_id=1, source_target_pairs={{0,12},{4,8},{8,4},{12,0},{1,13},{5,9},{9,5},{13,1},{2,14},{6,10},... | collective-permute-start | bytes 776 | tf_op jit(solution)/shard_map/ppermute | solution.py:29
  21.0 15.1 %collective-permute-start.4 = (bf16[1,2,64,1024]{3,2,1,0:T(8,128)(2,1)S(1)}, bf16[1,2,64,1024]{3,2,1,0:T(8,128)(2,1)S(1)}, u32[]{:S(2)}, u32[]{:S(2)}) collective-permute-start(bf16[1,2,64,1024]{3,2,1,0:T(8,128)(2,1)S(1)} %get-tuple-element.42), channel_id=1, source_target_pairs={{0,4},{4,0},{8,12},{12,8},{1,5},{5,1},{9,13},{13,9},{2,6},{6,2},{1... | collective-permute-start | bytes 786440 | tf_op jit(solution)/shard_map/ppermute | solution.py:29
  21.0 9.6 %collective-permute-start.5 = (bf16[1,2,32,1024]{3,2,1,0:T(8,128)(2,1)S(1)}, bf16[1,2,32,1024]{3,2,1,0:T(8,128)(2,1)S(1)}, u32[]{:S(2)}, u32[]{:S(2)}) collective-permute-start(bf16[1,2,32,1024]{3,2,1,0:T(8,128)(2,1)S(1)} %get-tuple-element.43), channel_id=1, source_target_pairs={{0,8},{4,12},{8,0},{12,4},{1,9},{5,13},{9,1},{13,5},{2,10},{6,14},... | collective-permute-start | bytes 393224 | tf_op jit(solution)/shard_map/ppermute | solution.py:29
  23.2 12.8 %collective-permute-start.6 = (bf16[1,2,32,1024]{3,2,1,0:T(8,128)(2,1)S(1)}, bf16[1,2,32,1024]{3,2,1,0:T(8,128)(2,1)S(1)}, u32[]{:S(2)}, u32[]{:S(2)}) collective-permute-start(bf16[1,2,32,1024]{3,2,1,0:T(8,128)(2,1)S(1)} %get-tuple-element.44), channel_id=1, source_target_pairs={{0,12},{4,8},{8,4},{12,0},{1,13},{5,9},{9,5},{13,1},{2,14},{6,10},... | collective-permute-start | bytes 393224 | tf_op jit(solution)/shard_map/ppermute | solution.py:29
  27.2 16.7 %collective-permute-start.12 = (bf16[1,2,32,1024]{3,2,1,0:T(8,128)(2,1)S(1)}, bf16[1,2,32,1024]{3,2,1,0:T(8,128)(2,1)S(1)}, u32[]{:S(2)}, u32[]{:S(2)}) collective-permute-start(bf16[1,2,32,1024]{3,2,1,0:T(8,128)(2,1)S(1)} %get-tuple-element.53), channel_id=1, source_target_pairs={{0,8},{4,12},{8,0},{12,4},{1,9},{5,13},{9,1},{13,5},{2,10},{6,14},... | collective-permute-start | bytes 393224 | tf_op jit(solution)/shard_map/ppermute | solution.py:29
  27.3 16.7 %collective-permute-start.13 = (bf16[1,2,32,1024]{3,2,1,0:T(8,128)(2,1)S(1)}, bf16[1,2,32,1024]{3,2,1,0:T(8,128)(2,1)S(1)}, u32[]{:S(2)}, u32[]{:S(2)}) collective-permute-start(bf16[1,2,32,1024]{3,2,1,0:T(8,128)(2,1)S(1)} %get-tuple-element.54), channel_id=1, source_target_pairs={{0,12},{4,8},{8,4},{12,0},{1,13},{5,9},{9,5},{13,1},{2,14},{6,10},... | collective-permute-start | bytes 393224 | tf_op jit(solution)/shard_map/ppermute | solution.py:29
  38.7 5.5 %collective-permute-start.7 = (bf16[2,128,1024]{2,1,0:T(8,128)(2,1)S(1)}, bf16[2,128,1024]{2,1,0:T(8,128)(2,1)S(1)}, u32[]{:S(2)}, u32[]{:S(2)}) collective-permute-start(bf16[2,128,1024]{2,1,0:T(8,128)(2,1)S(1)} %get-tuple-element.47), channel_id=1, source_target_pairs={{0,1},{1,0},{2,3},{3,2},{4,5},{5,4},{6,7},{7,6},{8,9},{9,8},{10,11... | collective-permute-start | bytes 1572872 | tf_op jit(solution)/shard_map/ppermute | solution.py:29
  44.9 6.4 %collective-permute-start.8 = (bf16[128,1024]{1,0:T(8,128)(2,1)S(1)}, bf16[128,1024]{1,0:T(8,128)(2,1)S(1)}, u32[]{:S(2)}, u32[]{:S(2)}) collective-permute-start(bf16[128,1024]{1,0:T(8,128)(2,1)S(1)} %get-tuple-element.49), channel_id=1, source_target_pairs={{0,2},{2,0},{1,3},{3,1},{4,6},{6,4},{5,7},{7,5},{8,10},{10,8},{9,1... | collective-permute-start | bytes 786440 | tf_op jit(solution)/shard_map/ppermute | solution.py:29
  46.5 7.2 %copy-start = (f32[4,64,1024]{2,1,0:T(8,128)S(1)}, f32[4,64,1024]{2,1,0:T(8,128)}, u32[]{:S(2)}) copy-start(f32[4,64,1024]{2,1,0:T(8,128)} %refs_7_.3) | copy-start | bytes 3145732
  48.9 1.4 %collective-permute-start.14 = (bf16[2,32,1024]{2,1,0:T(8,128)(2,1)S(1)}, bf16[2,32,1024]{2,1,0:T(8,128)(2,1)S(1)}, u32[]{:S(2)}, u32[]{:S(2)}) collective-permute-start(bf16[2,32,1024]{2,1,0:T(8,128)(2,1)S(1)} %get-tuple-element.56), channel_id=1, source_target_pairs={{0,1},{1,0},{2,3},{3,2},{4,5},{5,4},{6,7},{7,6},{8,9},{9,8},{10,11... | collective-permute-start | bytes 393224 | tf_op jit(solution)/shard_map/ppermute | solution.py:29
  49.0 1.5 %collective-permute-start.15 = (bf16[2,32,1024]{2,1,0:T(8,128)(2,1)S(1)}, bf16[2,32,1024]{2,1,0:T(8,128)(2,1)S(1)}, u32[]{:S(2)}, u32[]{:S(2)}) collective-permute-start(bf16[2,32,1024]{2,1,0:T(8,128)(2,1)S(1)} %get-tuple-element.57), channel_id=1, source_target_pairs={{0,1},{1,0},{2,3},{3,2},{4,5},{5,4},{6,7},{7,6},{8,9},{9,8},{10,11... | collective-permute-start | bytes 393224 | tf_op jit(solution)/shard_map/ppermute | solution.py:29
  49.5 1.3 %collective-permute-start.16 = (bf16[2,32,1024]{2,1,0:T(8,128)(2,1)S(1)}, bf16[2,32,1024]{2,1,0:T(8,128)(2,1)S(1)}, u32[]{:S(2)}, u32[]{:S(2)}) collective-permute-start(bf16[2,32,1024]{2,1,0:T(8,128)(2,1)S(1)} %get-tuple-element.58), channel_id=1, source_target_pairs={{0,1},{1,0},{2,3},{3,2},{4,5},{5,4},{6,7},{7,6},{8,9},{9,8},{10,11... | collective-permute-start | bytes 393224 | tf_op jit(solution)/shard_map/ppermute | solution.py:29
  49.6 1.5 %collective-permute-start.17 = (bf16[2,32,1024]{2,1,0:T(8,128)(2,1)S(1)}, bf16[2,32,1024]{2,1,0:T(8,128)(2,1)S(1)}, u32[]{:S(2)}, u32[]{:S(2)}) collective-permute-start(bf16[2,32,1024]{2,1,0:T(8,128)(2,1)S(1)} %get-tuple-element.59), channel_id=1, source_target_pairs={{0,1},{1,0},{2,3},{3,2},{4,5},{5,4},{6,7},{7,6},{8,9},{9,8},{10,11... | collective-permute-start | bytes 393224 | tf_op jit(solution)/shard_map/ppermute | solution.py:29
  52.1 13.1 %collective-permute-start.18 = (bf16[128,1024]{1,0:T(8,128)(2,1)S(1)}, bf16[128,1024]{1,0:T(8,128)(2,1)S(1)}, u32[]{:S(2)}, u32[]{:S(2)}) collective-permute-start(bf16[128,1024]{1,0:T(8,128)(2,1)S(1)} %get-tuple-element.61), channel_id=1, source_target_pairs={{0,2},{2,0},{1,3},{3,1},{4,6},{6,4},{5,7},{7,5},{8,10},{10,8},{9,1... | collective-permute-start | bytes 786440 | tf_op jit(solution)/shard_map/ppermute | solution.py:29
  54.4 5.0 %collective-permute-start.11 = (f32[8,128]{1,0:T(8,128)S(1)}, f32[8,128]{1,0:T(8,128)S(1)}, u32[]{:S(2)}, u32[]{:S(2)}) collective-permute-start(f32[8,128]{1,0:T(8,128)S(1)} %get-tuple-element.50.refs_0_), channel_id=1, source_target_pairs={{0,3},{1,2},{2,1},{3,0},{4,7},{5,6},{6,5},{7,4},{8,11},{9,10},{10,... | collective-permute-start | bytes 12296 | tf_op jit(solution)/shard_map/ppermute | solution.py:29
  54.5 6.0 %collective-permute-start.10 = (f32[8,128]{1,0:T(8,128)S(1)}, f32[8,128]{1,0:T(8,128)S(1)}, u32[]{:S(2)}, u32[]{:S(2)}) collective-permute-start(f32[8,128]{1,0:T(8,128)S(1)} %get-tuple-element.50.refs_0_), channel_id=1, source_target_pairs={{0,2},{1,3},{2,0},{3,1},{4,6},{5,7},{6,4},{7,5},{8,10},{9,11},{10,... | collective-permute-start | bytes 12296 | tf_op jit(solution)/shard_map/ppermute | solution.py:29
  55.1 5.4 %collective-permute-start.9 = (f32[8,128]{1,0:T(8,128)S(1)}, f32[8,128]{1,0:T(8,128)S(1)}, u32[]{:S(2)}, u32[]{:S(2)}) collective-permute-start(f32[8,128]{1,0:T(8,128)S(1)} %get-tuple-element.50.refs_0_), channel_id=1, source_target_pairs={{0,1},{1,0},{2,3},{3,2},{4,5},{5,4},{6,7},{7,6},{8,9},{9,8},{10,11... | collective-permute-start | bytes 12296 | tf_op jit(solution)/shard_map/ppermute | solution.py:29
  61.3 16.6 %collective-permute-start.22 = (bf16[64,1024]{1,0:T(8,128)(2,1)S(1)}, bf16[64,1024]{1,0:T(8,128)(2,1)S(1)}, u32[]{:S(2)}, u32[]{:S(2)}) collective-permute-start(bf16[64,1024]{1,0:T(8,128)(2,1)S(1)} %get-tuple-element.64), channel_id=1, source_target_pairs={{0,4},{4,0},{8,12},{12,8},{1,5},{5,1},{9,13},{13,9},{2,6},{6,2},{1... | collective-permute-start | bytes 393224 | tf_op jit(solution)/shard_map/ppermute | solution.py:29
  65.9 3.3 %collective-permute-start.21 = (f32[8,128]{1,0:T(8,128)S(1)}, f32[8,128]{1,0:T(8,128)S(1)}, u32[]{:S(2)}, u32[]{:S(2)}) collective-permute-start(f32[8,128]{1,0:T(8,128)S(1)} %get-tuple-element.62.refs_5_.refs_0_), channel_id=1, source_target_pairs={{0,3},{1,2},{2,1},{3,0},{4,7},{5,6},{6,5},{7,4},{8,11},{9,10},{10,... | collective-permute-start | bytes 12296 | tf_op jit(solution)/shard_map/ppermute | solution.py:29
  66.9 4.9 %collective-permute-start.20 = (f32[8,128]{1,0:T(8,128)S(1)}, f32[8,128]{1,0:T(8,128)S(1)}, u32[]{:S(2)}, u32[]{:S(2)}) collective-permute-start(f32[8,128]{1,0:T(8,128)S(1)} %get-tuple-element.62.refs_5_.refs_0_), channel_id=1, source_target_pairs={{0,2},{1,3},{2,0},{3,1},{4,6},{5,7},{6,4},{7,5},{8,10},{9,11},{10,... | collective-permute-start | bytes 12296 | tf_op jit(solution)/shard_map/ppermute | solution.py:29
  67.6 4.2 %collective-permute-start.19 = (f32[8,128]{1,0:T(8,128)S(1)}, f32[8,128]{1,0:T(8,128)S(1)}, u32[]{:S(2)}, u32[]{:S(2)}) collective-permute-start(f32[8,128]{1,0:T(8,128)S(1)} %get-tuple-element.62.refs_5_.refs_0_), channel_id=1, source_target_pairs={{0,1},{1,0},{2,3},{3,2},{4,5},{5,4},{6,7},{7,6},{8,9},{9,8},{10,11... | collective-permute-start | bytes 12296 | tf_op jit(solution)/shard_map/ppermute | solution.py:29
  67.8 10.1 %collective-permute-start.23 = (bf16[32,1024]{1,0:T(8,128)(2,1)S(1)}, bf16[32,1024]{1,0:T(8,128)(2,1)S(1)}, u32[]{:S(2)}, u32[]{:S(2)}) collective-permute-start(bf16[32,1024]{1,0:T(8,128)(2,1)S(1)} %get-tuple-element.65), channel_id=1, source_target_pairs={{0,8},{4,12},{8,0},{12,4},{1,9},{5,13},{9,1},{13,5},{2,10},{6,14},... | collective-permute-start | bytes 196616 | tf_op jit(solution)/shard_map/ppermute | solution.py:29
  69.2 8.7 %collective-permute-start.24 = (bf16[32,1024]{1,0:T(8,128)(2,1)S(1)}, bf16[32,1024]{1,0:T(8,128)(2,1)S(1)}, u32[]{:S(2)}, u32[]{:S(2)}) collective-permute-start(bf16[32,1024]{1,0:T(8,128)(2,1)S(1)} %get-tuple-element.66), channel_id=1, source_target_pairs={{0,12},{4,8},{8,4},{12,0},{1,13},{5,9},{9,5},{13,1},{2,14},{6,10},... | collective-permute-start | bytes 196616 | tf_op jit(solution)/shard_map/ppermute | solution.py:29
  72.7 8.8 %collective-permute-start.25 = (bf16[32,1024]{1,0:T(8,128)(2,1)S(1)}, bf16[32,1024]{1,0:T(8,128)(2,1)S(1)}, u32[]{:S(2)}, u32[]{:S(2)}) collective-permute-start(bf16[32,1024]{1,0:T(8,128)(2,1)S(1)} %get-tuple-element.68), channel_id=1, source_target_pairs={{0,8},{4,12},{8,0},{12,4},{1,9},{5,13},{9,1},{13,5},{2,10},{6,14},... | collective-permute-start | bytes 196616 | tf_op jit(solution)/shard_map/ppermute | solution.py:29
  73.6 7.9 %collective-permute-start.26 = (bf16[32,1024]{1,0:T(8,128)(2,1)S(1)}, bf16[32,1024]{1,0:T(8,128)(2,1)S(1)}, u32[]{:S(2)}, u32[]{:S(2)}) collective-permute-start(bf16[32,1024]{1,0:T(8,128)(2,1)S(1)} %get-tuple-element.69), channel_id=1, source_target_pairs={{0,12},{4,8},{8,4},{12,0},{1,13},{5,9},{9,5},{13,1},{2,14},{6,10},... | collective-permute-start | bytes 196616 | tf_op jit(solution)/shard_map/ppermute | solution.py:29
  (1 other events, 0.7 us)

commit v7 on v6

--- a/solution.py
+++ b/solution.py
@@ -160,7 +160,7 @@
     return (lax.broadcasted_iota(jnp.int32, (channels, row.shape[1]), 0) == row).astype(BF16)
 
 
-def rows_kernel(used, sends, messages, scal, here, *refs):
+def rows_kernel(used, sends, messages, scal, after, here, *refs):
     held, refs = refs[:used], refs[used:]
     perm, src_ids, rec_ids, refs = refs[0], refs[1 : 1 + sends], refs[1 + sends], refs[2 + sends :]
     outs, own_out = refs[:-1], refs[-1]
@@ -184,7 +184,7 @@
                 own_out[d, u, half] = y[at : at + slots]
 
 
-def gather_rows(scal, here, held, perm, src_ids, rec_ids, messages):
+def gather_rows(scal, after, here, held, perm, src_ids, rec_ids, messages):
     used, sends = len(held), len(src_ids)
     part = held[0].shape[-1]
     units, slots = rec_ids.shape
@@ -192,12 +192,12 @@
         functools.partial(rows_kernel, used, sends, messages),
         out_shape=[jax.ShapeDtypeStruct((used, 2, m[2], part), BF16) for m in messages]
         + [jax.ShapeDtypeStruct((units, used, 2, slots, part), BF16)],
-        in_specs=[SMEM] + [VMEM] * (used + 3 + sends),
+        in_specs=[SMEM, pl.BlockSpec(memory_space=pl.ANY)] + [VMEM] * (used + 3 + sends),
         out_specs=[VMEM] * (len(messages) + 1),
         compiler_params=params(16),
         cost_estimate=SMALL,
         name="rows",
-    )(scal, here, *held, perm, *src_ids, rec_ids)
+    )(scal, after, here, *held, perm, *src_ids, rec_ids)
     return sent, own
 
 
@@ -234,7 +234,8 @@
         at += count
 
 
-def cross_kernel(pieces, weight, *refs):
+def cross_kernel(pieces, skip, weight, *refs):
+    refs = refs[skip:]
     s_refs, own, lhs = refs[:-2], refs[-2], refs[-1]
     used = own.shape[1]
     rows = lhs.shape[1] // 2
@@ -258,17 +259,17 @@
             lhs[r, turned, LANES:] = (-real).astype(BF16)
 
 
-def cross_rows(weight, rows, own, pieces, classes):
+def cross_rows(weight, after, rows, own, pieces, classes):
     count = sum(p[2] for p in pieces)
     return pl.pallas_call(
-        functools.partial(cross_kernel, pieces),
+        functools.partial(cross_kernel, pieces, len(after)),
         out_shape=jax.ShapeDtypeStruct((classes, 2 * count, 2 * LANES), BF16),
-        in_specs=[SMEM] + [VMEM] * (len(rows) + 1),
+        in_specs=[SMEM] + [pl.BlockSpec(memory_space=pl.ANY)] * len(after) + [VMEM] * (len(rows) + 1),
         out_specs=VMEM,
         compiler_params=params(8),
         cost_estimate=LARGE,
         name="cross",
-    )(weight, *rows, own)
+    )(weight, *after, *rows, own)
 
 
 def lags_kernel(geometry, skip, scal, *refs):
@@ -293,7 +294,7 @@
             out[column] = sums[cores * column + 1 - scal[CORE], at].astype(BF16)
 
 
-def lag_parts(scal, after, lhs, table, geometry, columns, lag_dev, split):
+def lag_parts(scal, after, lhs, table, geometry, columns, lag_dev, split, effort):
     rows = lhs.shape[1] // 2
     shape = lambda count: (columns, count, lag_dev)
     return pl.pallas_call(
@@ -304,7 +305,7 @@
         out_specs=[VMEM] * (split + 1),
         scratch_shapes=[pltpu.VMEM((2 * columns, rows, lag_dev), F32)],
         compiler_params=params(16),
-        cost_estimate=LARGE,
+        cost_estimate=effort,
         name="lags",
     )(scal, *after, lhs, table)
 
@@ -533,8 +534,8 @@
     table = make_table(scal, trig, classes, span, peers)
     if direct and blocks == 4:
         chunks = [
-            [(1, 0, slots), (2, 0, some), (3, 0, some)],
-            [(0, 0, slots), (2, some, some), (3, some, some)],
+            [(0, 0, slots), (1, 0, slots)],
+            [(2, 0, slots), (3, 0, slots)],
         ]
     else:
         chunks = [[(d, first, some) for d in range(blocks)] for first in (0, some)]
@@ -543,7 +544,7 @@
     else:
         messages = [(d, 0, slots) for d in shifts]
     sent, own_rows = gather_rows(
-        scal, held[0], held[1:], make_perm(part), src_ids, rec_ids, messages
+        scal, table, held[0], held[1:], make_perm(part), src_ids, rec_ids, messages
     )
     arrived = [swapped(x, "recv", places, m[0]) for m, x in zip(messages, sent)]
     if not direct:
@@ -556,9 +557,9 @@
     after = []
     for q, pieces in enumerate(chunks):
         rows = arrived[len(pieces) * q : len(pieces) * (q + 1)]
-        lhs = cross_rows(weight, rows, own_rows, pieces, classes)
+        lhs = cross_rows(weight, after[:1], rows, own_rows, pieces, classes)
         keep, *sends = lag_parts(
-            scal, after[:1], lhs, table, geometry, columns, lag_dev, SPLIT if q else 1
+            scal, [], lhs, table, geometry, columns, lag_dev, SPLIT if q else 2 * SPLIT, SMALL if q else LARGE
         )
         sends = [swapped(x, "freq", cores, 1) for x in sends]
         own, *sends = add_cores(scal, after[1:], keep, sends)

time: 82.7 us -> 78.8 us (0.953)
  starting transfers between devices: 31.5 us -> 27.8 us
    ppermute x27 -> x30, starting transfers between devices: 31.5 us -> 27.8 us  [swapped(): return lax.ppermute(value, axis, [(i, i ^ step) for i in range(size)])]
    ppermute x27 -> x30, waiting for transfers between devices: 26.1 us -> 25.6 us  [swapped(): return lax.ppermute(value, axis, [(i, i ^ step) for i in range(size)])]
  transfers between devices with their start and end apart: 27 -> 30, of which waited for: 14 -> 14; matrix products, arithmetic and copies ran while one was open for 0% -> 0% of each run, Pallas kernels for 18% -> 20%
where the time goes in v7:
time: 78.8 us; the launch traced here: 78.6 us
  starting transfers between devices  27.8 us (35%)
  waiting for transfers between devices  25.6 us (32%)
  Pallas kernels  19.6 us (25%)
  local copies, waits for them, and re-layouts  4.02 us (5%)
  between operations  1.49 us (2%)
    ppermute x30, starting transfers between devices, swapped(): return lax.ppermute(value, axis, [(i, i ^ step) for i in range(size)])  27.8 us
    ppermute x30, waiting for transfers between devices, swapped(): return lax.ppermute(value, axis, [(i, i ^ step) for i in range(size)])  25.6 us
    pallas_call x2, Pallas kernels, lag_parts(): pl.pallas_call(functools.partial(lags_kernel, geometry, len(after)), out_...  4.97 us
    pallas_call x1, Pallas kernels, normed_rows(): pl.pallas_call(functools.partial(normed_kernel, lag_total, chunks, len(su...  2.96 us
    unnamed x12, local copies, waits for them, and re-layouts  2.68 us
    pallas_call x1, Pallas kernels, gather_rows(): pl.pallas_call(functools.partial(rows_kernel, used, sends, messages), out...  1.81 us
    pallas_call x1, Pallas kernels, make_table(): pl.pallas_call(functools.partial(table_kernel, classes, parts), out_shape...  1.78 us
    pallas_call x2, Pallas kernels, gradients(): pl.pallas_call(functools.partial(gradient_kernel, lag_total, pieces, len(...  1.61 us
  transfers between devices with their start and end apart: 30, of which 14 were waited for; matrix products, arithmetic and copies ran while one was open for 0% of the time, Pallas kernels for 20%

profile of v7, /device:TPU:0, one launch (start us, length us, event | category | flops | bytes accessed | tf_op | source)
XLA Modules:
  0.0 78.6 jit_solution(10086638995316771948)
XLA Ops:
  0.7 1.3 %constant_dynamic-slice_fusion = (bf16[1,2,128,1024]{3,2,1,0:T(8,128)(2,1)S(1)}, bf16[1,2,128,1024]{3,2,1,0:T(8,128)(2,1)S(1)}) fusion(bf16[1,2,128,2048]{3,2,1,0:T(8,128)(2,1)} %param.8, s32[]{:T(128)S(6)} %select_n.7, s32[]{:T(128)S(6)} %select_n.6), kind=kLoop, calls=%fused_computation | loop fusion | bytes 2097160 | tf_op jit(solution)/shard_map/dynamic_slice | solution.py:511
  2.0 3.0 %collective-permute-start = (bf16[1,2,128,1024]{3,2,1,0:T(8,128)(2,1)S(1)}, bf16[1,2,128,1024]{3,2,1,0:T(8,128)(2,1)S(1)}, u32[]{:S(2)}, u32[]{:S(2)}) collective-permute-start(bf16[1,2,128,1024]{3,2,1,0:T(8,128)(2,1)S(1)} %get-tuple-element.76), channel_id=1, source_target_pairs={{0,2},{2,0},{1,3},{3,1},{4,6},{6,4},{5,7},{7,5},{8,10},{10,8},{9,1... | collective-permute-start | bytes 1572872 | tf_op jit(solution)/shard_map/ppermute | solution.py:29
  8.3 1.2 %index.1 = (s32[128]{0:T(128)S(1)}, s32[1,64]{1,0:T(1,128)S(1)}, s32[1,64]{1,0:T(1,128)S(1)}, s32[1,64]{1,0:T(1,128)S(1)}, s32[1,64]{1,0:T(1,128)S(1)}, /*index=5*/s32[4,64]{1,0:T(4,128)S(1)}) custom-call(s32[1]{0:T(128)S(6)} %copy.10.refs_0_, s32[4]{0:T(128)S(1)} %copy-done.4, s32[4]{0:T(128)S(1)} %bitcast.1, s32[4,64]{1,0:T(4,128)S(1)} %copy-done.2, ...), custom_call_target="tpu_custom_call" | custom-call | flops 1 | bytes 1 | tf_op jit(solution)/shard_map/index/pallas_call | solution.py:92
  9.6 1.6 %collective-permute-start.1 = (s32[1,64]{1,0:T(1,128)S(1)}, s32[1,64]{1,0:T(1,128)S(1)}, u32[]{:S(2)}, u32[]{:S(2)}) collective-permute-start(s32[1,64]{1,0:T(1,128)S(1)} %get-tuple-element.41), channel_id=1, source_target_pairs={{0,4},{4,0},{8,12},{12,8},{1,5},{5,1},{9,13},{13,9},{2,6},{6,2},{1... | collective-permute-start | bytes 776 | tf_op jit(solution)/shard_map/ppermute | solution.py:29
  11.2 2.6 %collective-permute-start.2 = (s32[1,64]{1,0:T(1,128)S(1)}, s32[1,64]{1,0:T(1,128)S(1)}, u32[]{:S(2)}, u32[]{:S(2)}) collective-permute-start(s32[1,64]{1,0:T(1,128)S(1)} %get-tuple-element.42), channel_id=1, source_target_pairs={{0,8},{4,12},{8,0},{12,4},{1,9},{5,13},{9,1},{13,5},{2,10},{6,14},... | collective-permute-start | bytes 776 | tf_op jit(solution)/shard_map/ppermute | solution.py:29
  14.6 1.8 %table.1.after.refs_1_ = bf16[8,256,1024]{2,1,0:T(8,128)(2,1)S(1)} custom-call(s32[128]{0:T(128)S(1)} %get-tuple-element.39.scal, f32[2,56,1024]{2,1,0:T(8,128)S(1)} %copy-done.1), custom_call_target="tpu_custom_call" | custom-call | flops 1 | bytes 1 | tf_op jit(solution)/shard_map/table/pallas_call | solution.py:126
  16.4 2.7 %collective-permute-done.3.refs_5_.refs_3_ = s32[1,64]{1,0:T(1,128)S(1)} collective-permute-done((s32[1,64]{1,0:T(1,128)S(1)}, s32[1,64]{1,0:T(1,128)S(1)}, u32[]{:S(2)}, u32[]{:S(2)}) %collective-permute-start.3) | collective-permute-done | bytes 288 | tf_op jit(solution)/shard_map/ppermute | solution.py:29
  19.1 1.8 %rows.1 = (bf16[1,2,64,1024]{3,2,1,0:T(8,128)(2,1)S(1)}, bf16[1,2,64,1024]{3,2,1,0:T(8,128)(2,1)S(1)}, bf16[1,2,64,1024]{3,2,1,0:T(8,128)(2,1)S(1)}, bf16[1,2,64...) custom-call(s32[128]{0:T(128)S(1)} %get-tuple-element.39.scal, bf16[8,256,1024]{2,1,0:T(8,128)(2,1)S(1)} %table.1.after.refs_1_, ...), custom_call_target="tpu_custom_call" | custom-call | flops 1 | bytes 1 | tf_op jit(solution)/shard_map/rows/pallas_call | solution.py:191
  21.0 2.2 %collective-permute-start.17 = (bf16[1,2,64,1024]{3,2,1,0:T(8,128)(2,1)S(1)}, bf16[1,2,64,1024]{3,2,1,0:T(8,128)(2,1)S(1)}, u32[]{:S(2)}, u32[]{:S(2)}) collective-permute-start(bf16[1,2,64,1024]{3,2,1,0:T(8,128)(2,1)S(1)} %get-tuple-element.61), channel_id=1, source_target_pairs={{0,8},{4,12},{8,0},{12,4},{1,9},{5,13},{9,1},{13,5},{2,10},{6,14},... | collective-permute-start | bytes 786440 | tf_op jit(solution)/shard_map/ppermute | solution.py:29
  23.2 2.2 %collective-permute-start.18 = (bf16[1,2,64,1024]{3,2,1,0:T(8,128)(2,1)S(1)}, bf16[1,2,64,1024]{3,2,1,0:T(8,128)(2,1)S(1)}, u32[]{:S(2)}, u32[]{:S(2)}) collective-permute-start(bf16[1,2,64,1024]{3,2,1,0:T(8,128)(2,1)S(1)} %get-tuple-element.62), channel_id=1, source_target_pairs={{0,12},{4,8},{8,4},{12,0},{1,13},{5,9},{9,5},{13,1},{2,14},{6,10},... | collective-permute-start | bytes 786440 | tf_op jit(solution)/shard_map/ppermute | solution.py:29
  25.4 5.8 %collective-permute-done.4.refs_1_ = bf16[1,2,64,1024]{3,2,1,0:T(8,128)(2,1)S(1)} collective-permute-done((bf16[1,2,64,1024]{3,2,1,0:T(8,128)(2,1)S(1)}, bf16[1,2,64,1024]{3,2,1,0:T(8,128)(2,1)S(1)}, u32[]{:S(2)}, u32[]{:S(2)}) %collective-permute-start.4) | collective-permute-done | bytes 262176 | tf_op jit(solution)/shard_map/ppermute | solution.py:29
  31.5 2.5 %lags.2 = (f32[2,128,1024]{2,1,0:T(8,128)S(1)}, bf16[2,16,1024]{2,1,0:T(8,128)(2,1)S(1)}, bf16[2,16,1024]{2,1,0:T(8,128)(2,1)S(1)}, bf16[2,16,1024]{2,1,0:T(8,12...) custom-call(s32[128]{0:T(128)S(1)} %get-tuple-element.39.scal, ...), custom_call_target="tpu_custom_call" | custom-call | flops 20000000000 | bytes 1048576 | tf_op jit(solution)/shard_map/lags/pallas_call | solution.py:300
  37.1 0.7 collective-permute-done.11.refs_7_
  38.0 0.8 %cores.2 = (f32[128,1024]{1,0:T(8,128)S(1)}, bf16[128,1024]{1,0:T(8,128)(2,1)S(1)}) custom-call(s32[128]{0:T(128)S(1)} %get-tuple-element.39.scal, f32[2,128,1024]{2,1,0:T(8,128)S(1)} %get-tuple-element.48.refs_0_, bf16[2,16,1024]{2,1,0:T(8,128)(2,1)S(1)} %collective-permute-done.5.refs_1_, bf16[2,16,1024]{2,1,0:T(8,128)(2,1)S(1)} %collective-permute-done.6.refs_2_, ...), custom_call_target="tpu_custom_call" | custom-call | flops 1 | bytes 1 | tf_op jit(solution)/shard_map/cores/pallas_call | solution.py:335
  38.8 0.9 %collective-permute-start.13 = (bf16[128,1024]{1,0:T(8,128)(2,1)S(1)}, bf16[128,1024]{1,0:T(8,128)(2,1)S(1)}, u32[]{:S(2)}, u32[]{:S(2)}) collective-permute-start(bf16[128,1024]{1,0:T(8,128)(2,1)S(1)} %get-tuple-element.58), channel_id=1, source_target_pairs={{0,2},{2,0},{1,3},{3,1},{4,6},{6,4},{5,7},{7,5},{8,10},{10,8},{9,1... | collective-permute-start | bytes 786440 | tf_op jit(solution)/shard_map/ppermute | solution.py:29
  39.8 2.7 %collective-permute-done.17.refs_1_ = bf16[1,2,64,1024]{3,2,1,0:T(8,128)(2,1)S(1)} collective-permute-done((bf16[1,2,64,1024]{3,2,1,0:T(8,128)(2,1)S(1)}, bf16[1,2,64,1024]{3,2,1,0:T(8,128)(2,1)S(1)}, u32[]{:S(2)}, u32[]{:S(2)}) %collective-permute-start.17) | collective-permute-done | bytes 262176 | tf_op jit(solution)/shard_map/ppermute | solution.py:29
  42.8 2.5 %lags.3 = (f32[2,128,1024]{2,1,0:T(8,128)S(1)}, bf16[2,32,1024]{2,1,0:T(8,128)(2,1)S(1)}, bf16[2,32,1024]{2,1,0:T(8,128)(2,1)S(1)}, bf16[2,32,1024]{2,1,0:T(8,128)(2,1)S(1)}, bf16[2,32,1024]{2,1,0:T(8,128)(2,1)S(1)}) custom-call(s32[128]{0:T(128)S(1)} %get-tuple-element.39.scal, bf16[8,256,256]{2,1,0:T(8,128)(2,1)S(1)} %cross.3.refs_0_, ...), custom_call_target="tpu_custom_call" | custom-call | flops 1 | bytes 1 | tf_op jit(solution)/shard_map/lags/pallas_call | solution.py:300
  48.2 1.0 %collective-permute-start.23 = (bf16[128,1024]{1,0:T(8,128)(2,1)S(1)}, bf16[128,1024]{1,0:T(8,128)(2,1)S(1)}, u32[]{:S(2)}, u32[]{:S(2)}) collective-permute-start(bf16[128,1024]{1,0:T(8,128)(2,1)S(1)} %get-tuple-element.69), channel_id=1, source_target_pairs={{0,2},{2,0},{1,3},{3,1},{4,6},{6,4},{5,7},{7,5},{8,10},{10,8},{9,1... | collective-permute-start | bytes 786440 | tf_op jit(solution)/shard_map/ppermute | solution.py:29
  49.2 0.8 stats.2
  50.6 1.0 %collective-permute-start.15 = (f32[8,128]{1,0:T(8,128)S(1)}, f32[8,128]{1,0:T(8,128)S(1)}, u32[]{:S(2)}, u32[]{:S(2)}) collective-permute-start(f32[8,128]{1,0:T(8,128)S(1)} %get-tuple-element.59.refs_0_), channel_id=1, source_target_pairs={{0,2},{1,3},{2,0},{3,1},{4,6},{5,7},{6,4},{7,5},{8,10},{9,11},{10,... | collective-permute-start | bytes 12296 | tf_op jit(solution)/shard_map/ppermute | solution.py:29
  51.9 4.9 %collective-permute-done.23.refs_1_ = bf16[128,1024]{1,0:T(8,128)(2,1)S(1)} collective-permute-done((bf16[128,1024]{1,0:T(8,128)(2,1)S(1)}, bf16[128,1024]{1,0:T(8,128)(2,1)S(1)}, u32[]{:S(2)}, u32[]{:S(2)}) %collective-permute-start.23) | collective-permute-done | bytes 262176 | tf_op jit(solution)/shard_map/ppermute | solution.py:29
  56.8 0.8 stats.3
  57.7 1.0 %collective-permute-start.25 = (f32[8,128]{1,0:T(8,128)S(1)}, f32[8,128]{1,0:T(8,128)S(1)}, u32[]{:S(2)}, u32[]{:S(2)}) collective-permute-start(f32[8,128]{1,0:T(8,128)S(1)} %get-tuple-element.70.refs_5_.refs_0_), channel_id=1, source_target_pairs={{0,2},{1,3},{2,0},{3,1},{4,6},{5,7},{6,4},{7,5},{8,10},{9,11},{10,... | collective-permute-start | bytes 12296 | tf_op jit(solution)/shard_map/ppermute | solution.py:29
  58.7 0.7 collective-permute-start.24
  59.5 0.8 %gradient.2 = (bf16[64,1024]{1,0:T(8,128)(2,1)S(1)}, bf16[64,1024]{1,0:T(8,128)(2,1)S(1)}) custom-call(s32[128]{0:T(128)S(1)} %get-tuple-element.39.scal, f32[8,128]{1,0:T(8,128)S(1)} %get-tuple-element.59.refs_0_, f32[8,128]{1,0:T(8,128)S(1)} %collective-permute-done.14.refs_1_, f32[8,128]{1,0:T(8,128)S(1)} %collective-permute-done.15.refs_2_, ...), custom_call_target="tpu_custom_call" | custom-call | flops 1 | bytes 1 | tf_op jit(solution)/shard_map/gradient/pallas_call | solution.py:424
  60.3 3.5 %collective-permute-start.27 = (bf16[64,1024]{1,0:T(8,128)(2,1)S(1)}, bf16[64,1024]{1,0:T(8,128)(2,1)S(1)}, u32[]{:S(2)}, u32[]{:S(2)}) collective-permute-start(bf16[64,1024]{1,0:T(8,128)(2,1)S(1)} %get-tuple-element.73), channel_id=1, source_target_pairs={{0,4},{4,0},{8,12},{12,8},{1,5},{5,1},{9,13},{13,9},{2,6},{6,2},{1... | collective-permute-start | bytes 393224 | tf_op jit(solution)/shard_map/ppermute | solution.py:29
  63.8 0.8 %gradient.3 = (bf16[64,1024]{1,0:T(8,128)(2,1)S(1)}, bf16[64,1024]{1,0:T(8,128)(2,1)S(1)}) custom-call(s32[128]{0:T(128)S(1)} %get-tuple-element.39.scal, f32[8,128]{1,0:T(8,128)S(1)} %get-tuple-element.70.refs_5_.refs_0_, f32[8,128]{1,0:T(8,128)S(1)} %collective-permute-done.24.refs_6_.refs_1_, f32[8,128]{1,0:T(8,128)S(1)} %collective-permute-done.25.refs_7_.refs_2_, ...), custom_call_target="tpu_custom_call" | custom-call | flops 1 | bytes 1 | tf_op jit(solution)/shard_map/gradient/pallas_call | solution.py:424
  64.6 2.4 %collective-permute-start.28 = (bf16[64,1024]{1,0:T(8,128)(2,1)S(1)}, bf16[64,1024]{1,0:T(8,128)(2,1)S(1)}, u32[]{:S(2)}, u32[]{:S(2)}) collective-permute-start(bf16[64,1024]{1,0:T(8,128)(2,1)S(1)} %get-tuple-element.74), channel_id=1, source_target_pairs={{0,8},{4,12},{8,0},{12,4},{1,9},{5,13},{9,1},{13,5},{2,10},{6,14},... | collective-permute-start | bytes 393224 | tf_op jit(solution)/shard_map/ppermute | solution.py:29
  67.0 1.3 %collective-permute-start.29 = (bf16[64,1024]{1,0:T(8,128)(2,1)S(1)}, bf16[64,1024]{1,0:T(8,128)(2,1)S(1)}, u32[]{:S(2)}, u32[]{:S(2)}) collective-permute-start(bf16[64,1024]{1,0:T(8,128)(2,1)S(1)} %get-tuple-element.75), channel_id=1, source_target_pairs={{0,12},{4,8},{8,4},{12,0},{1,13},{5,9},{9,5},{13,1},{2,14},{6,10},... | collective-permute-start | bytes 393224 | tf_op jit(solution)/shard_map/ppermute | solution.py:29
  68.4 3.0 %normed.1 = f32[4,64,1024]{2,1,0:T(8,128)} custom-call(s32[128]{0:T(128)S(1)} %get-tuple-element.39.scal, f32[8,128]{1,0:T(8,128)S(1)} %get-tuple-element.59.refs_0_, f32[8,128]{1,0:T(8,128)S(1)} %collective-permute-done.14.refs_1_, f32[8,128]{1,0:T(8,128)S(1)} %collective-permute-done.15.refs_2_, f32[8,128]{1,0:T(8,128)S(1)} %collective-permute-done.16.refs_3_, ...), custom_call_target="tpu_custom_call" | custom-call | flops 1 | bytes 1 | tf_op jit(solution)/shard_map/normed/pallas_call | solution.py:456
  71.3 6.2 %collective-permute-done.28.refs_6_ = bf16[64,1024]{1,0:T(8,128)(2,1)S(1)} collective-permute-done((bf16[64,1024]{1,0:T(8,128)(2,1)S(1)}, bf16[64,1024]{1,0:T(8,128)(2,1)S(1)}, u32[]{:S(2)}, u32[]{:S(2)}) %collective-permute-start.28) | collective-permute-done | bytes 131104 | tf_op jit(solution)/shard_map/ppermute | solution.py:29
  77.5 1.1 %adjoint.1 = f32[128,1024]{1,0:T(8,128)} custom-call(s32[1,64]{1,0:T(1,128)S(1)} %get-tuple-element.40.refs_2_.refs_0_, s32[1,64]{1,0:T(1,128)S(1)} %collective-permute-done.1.refs_3_.refs_1_, s32[1,64]{1,0:T(1,128)S(1)} %collective-permute-done.2.refs_4_.refs_2_, s32[1,64]{1,0:T(1,128)S(1)} %collective-permute-done.3.refs_5_.refs_3_, ...), custom_call_target="tpu_custom_call" | custom-call | flops 1 | bytes 1 | tf_op jit(solution)/shard_map/adjoint/pallas_call | solution.py:480
  (57 shorter events, 11.3 us)
Async XLA Ops:
  0.6 14.0 %copy-start.1 = (f32[2,56,1024]{2,1,0:T(8,128)S(1)}, f32[2,56,1024]{2,1,0:T(8,128)}, u32[]{:S(2)}) copy-start(f32[2,56,1024]{2,1,0:T(8,128)} %constant.16.clone.trig) | copy-start | bytes 1376260
  2.0 17.1 %collective-permute-start = (bf16[1,2,128,1024]{3,2,1,0:T(8,128)(2,1)S(1)}, bf16[1,2,128,1024]{3,2,1,0:T(8,128)(2,1)S(1)}, u32[]{:S(2)}, u32[]{:S(2)}) collective-permute-start(bf16[1,2,128,1024]{3,2,1,0:T(8,128)(2,1)S(1)} %get-tuple-element.76), channel_id=1, source_target_pairs={{0,2},{2,0},{1,3},{3,1},{4,6},{6,4},{5,7},{7,5},{8,10},{10,8},{9,1... | collective-permute-start | bytes 1572872 | tf_op jit(solution)/shard_map/ppermute | solution.py:29
  9.6 6.9 %collective-permute-start.1 = (s32[1,64]{1,0:T(1,128)S(1)}, s32[1,64]{1,0:T(1,128)S(1)}, u32[]{:S(2)}, u32[]{:S(2)}) collective-permute-start(s32[1,64]{1,0:T(1,128)S(1)} %get-tuple-element.41), channel_id=1, source_target_pairs={{0,4},{4,0},{8,12},{12,8},{1,5},{5,1},{9,13},{13,9},{2,6},{6,2},{1... | collective-permute-start | bytes 776 | tf_op jit(solution)/shard_map/ppermute | solution.py:29
  11.2 5.2 %collective-permute-start.2 = (s32[1,64]{1,0:T(1,128)S(1)}, s32[1,64]{1,0:T(1,128)S(1)}, u32[]{:S(2)}, u32[]{:S(2)}) collective-permute-start(s32[1,64]{1,0:T(1,128)S(1)} %get-tuple-element.42), channel_id=1, source_target_pairs={{0,8},{4,12},{8,0},{12,4},{1,9},{5,13},{9,1},{13,5},{2,10},{6,14},... | collective-permute-start | bytes 776 | tf_op jit(solution)/shard_map/ppermute | solution.py:29
  13.8 5.3 %collective-permute-start.3 = (s32[1,64]{1,0:T(1,128)S(1)}, s32[1,64]{1,0:T(1,128)S(1)}, u32[]{:S(2)}, u32[]{:S(2)}) collective-permute-start(s32[1,64]{1,0:T(1,128)S(1)} %get-tuple-element.43), channel_id=1, source_target_pairs={{0,12},{4,8},{8,4},{12,0},{1,13},{5,9},{9,5},{13,1},{2,14},{6,10},... | collective-permute-start | bytes 776 | tf_op jit(solution)/shard_map/ppermute | solution.py:29
  21.0 10.3 %collective-permute-start.4 = (bf16[1,2,64,1024]{3,2,1,0:T(8,128)(2,1)S(1)}, bf16[1,2,64,1024]{3,2,1,0:T(8,128)(2,1)S(1)}, u32[]{:S(2)}, u32[]{:S(2)}) collective-permute-start(bf16[1,2,64,1024]{3,2,1,0:T(8,128)(2,1)S(1)} %get-tuple-element.46), channel_id=1, source_target_pairs={{0,4},{4,0},{8,12},{12,8},{1,5},{5,1},{9,13},{13,9},{2,6},{6,2},{1... | collective-permute-start | bytes 786440 | tf_op jit(solution)/shard_map/ppermute | solution.py:29
  21.0 21.4 %collective-permute-start.17 = (bf16[1,2,64,1024]{3,2,1,0:T(8,128)(2,1)S(1)}, bf16[1,2,64,1024]{3,2,1,0:T(8,128)(2,1)S(1)}, u32[]{:S(2)}, u32[]{:S(2)}) collective-permute-start(bf16[1,2,64,1024]{3,2,1,0:T(8,128)(2,1)S(1)} %get-tuple-element.61), channel_id=1, source_target_pairs={{0,8},{4,12},{8,0},{12,4},{1,9},{5,13},{9,1},{13,5},{2,10},{6,14},... | collective-permute-start | bytes 786440 | tf_op jit(solution)/shard_map/ppermute | solution.py:29
  23.2 19.2 %collective-permute-start.18 = (bf16[1,2,64,1024]{3,2,1,0:T(8,128)(2,1)S(1)}, bf16[1,2,64,1024]{3,2,1,0:T(8,128)(2,1)S(1)}, u32[]{:S(2)}, u32[]{:S(2)}) collective-permute-start(bf16[1,2,64,1024]{3,2,1,0:T(8,128)(2,1)S(1)} %get-tuple-element.62), channel_id=1, source_target_pairs={{0,12},{4,8},{8,4},{12,0},{1,13},{5,9},{9,5},{13,1},{2,14},{6,10},... | collective-permute-start | bytes 786440 | tf_op jit(solution)/shard_map/ppermute | solution.py:29
  34.0 1.3 %collective-permute-start.5 = (bf16[2,16,1024]{2,1,0:T(8,128)(2,1)S(1)}, bf16[2,16,1024]{2,1,0:T(8,128)(2,1)S(1)}, u32[]{:S(2)}, u32[]{:S(2)}) collective-permute-start(bf16[2,16,1024]{2,1,0:T(8,128)(2,1)S(1)} %get-tuple-element.49), channel_id=1, source_target_pairs={{0,1},{1,0},{2,3},{3,2},{4,5},{5,4},{6,7},{7,6},{8,9},{9,8},{10,11... | collective-permute-start | bytes 196616 | tf_op jit(solution)/shard_map/ppermute | solution.py:29
  34.1 1.4 %collective-permute-start.6 = (bf16[2,16,1024]{2,1,0:T(8,128)(2,1)S(1)}, bf16[2,16,1024]{2,1,0:T(8,128)(2,1)S(1)}, u32[]{:S(2)}, u32[]{:S(2)}) collective-permute-start(bf16[2,16,1024]{2,1,0:T(8,128)(2,1)S(1)} %get-tuple-element.50), channel_id=1, source_target_pairs={{0,1},{1,0},{2,3},{3,2},{4,5},{5,4},{6,7},{7,6},{8,9},{9,8},{10,11... | collective-permute-start | bytes 196616 | tf_op jit(solution)/shard_map/ppermute | solution.py:29
  34.6 1.3 %collective-permute-start.7 = (bf16[2,16,1024]{2,1,0:T(8,128)(2,1)S(1)}, bf16[2,16,1024]{2,1,0:T(8,128)(2,1)S(1)}, u32[]{:S(2)}, u32[]{:S(2)}) collective-permute-start(bf16[2,16,1024]{2,1,0:T(8,128)(2,1)S(1)} %get-tuple-element.51), channel_id=1, source_target_pairs={{0,1},{1,0},{2,3},{3,2},{4,5},{5,4},{6,7},{7,6},{8,9},{9,8},{10,11... | collective-permute-start | bytes 196616 | tf_op jit(solution)/shard_map/ppermute | solution.py:29
  35.4 1.3 %collective-permute-start.8 = (bf16[2,16,1024]{2,1,0:T(8,128)(2,1)S(1)}, bf16[2,16,1024]{2,1,0:T(8,128)(2,1)S(1)}, u32[]{:S(2)}, u32[]{:S(2)}) collective-permute-start(bf16[2,16,1024]{2,1,0:T(8,128)(2,1)S(1)} %get-tuple-element.52), channel_id=1, source_target_pairs={{0,1},{1,0},{2,3},{3,2},{4,5},{5,4},{6,7},{7,6},{8,9},{9,8},{10,11... | collective-permute-start | bytes 196616 | tf_op jit(solution)/shard_map/ppermute | solution.py:29
  35.5 1.3 %collective-permute-start.9 = (bf16[2,16,1024]{2,1,0:T(8,128)(2,1)S(1)}, bf16[2,16,1024]{2,1,0:T(8,128)(2,1)S(1)}, u32[]{:S(2)}, u32[]{:S(2)}) collective-permute-start(bf16[2,16,1024]{2,1,0:T(8,128)(2,1)S(1)} %get-tuple-element.53), channel_id=1, source_target_pairs={{0,1},{1,0},{2,3},{3,2},{4,5},{5,4},{6,7},{7,6},{8,9},{9,8},{10,11... | collective-permute-start | bytes 196616 | tf_op jit(solution)/shard_map/ppermute | solution.py:29
  35.9 1.3 %collective-permute-start.10 = (bf16[2,16,1024]{2,1,0:T(8,128)(2,1)S(1)}, bf16[2,16,1024]{2,1,0:T(8,128)(2,1)S(1)}, u32[]{:S(2)}, u32[]{:S(2)}) collective-permute-start(bf16[2,16,1024]{2,1,0:T(8,128)(2,1)S(1)} %get-tuple-element.54), channel_id=1, source_target_pairs={{0,1},{1,0},{2,3},{3,2},{4,5},{5,4},{6,7},{7,6},{8,9},{9,8},{10,11... | collective-permute-start | bytes 196616 | tf_op jit(solution)/shard_map/ppermute | solution.py:29
  36.6 1.3 %collective-permute-start.11 = (bf16[2,16,1024]{2,1,0:T(8,128)(2,1)S(1)}, bf16[2,16,1024]{2,1,0:T(8,128)(2,1)S(1)}, u32[]{:S(2)}, u32[]{:S(2)}) collective-permute-start(bf16[2,16,1024]{2,1,0:T(8,128)(2,1)S(1)} %get-tuple-element.55), channel_id=1, source_target_pairs={{0,1},{1,0},{2,3},{3,2},{4,5},{5,4},{6,7},{7,6},{8,9},{9,8},{10,11... | collective-permute-start | bytes 196616 | tf_op jit(solution)/shard_map/ppermute | solution.py:29
  36.8 1.3 %collective-permute-start.12 = (bf16[2,16,1024]{2,1,0:T(8,128)(2,1)S(1)}, bf16[2,16,1024]{2,1,0:T(8,128)(2,1)S(1)}, u32[]{:S(2)}, u32[]{:S(2)}) collective-permute-start(bf16[2,16,1024]{2,1,0:T(8,128)(2,1)S(1)} %get-tuple-element.56), channel_id=1, source_target_pairs={{0,1},{1,0},{2,3},{3,2},{4,5},{5,4},{6,7},{7,6},{8,9},{9,8},{10,11... | collective-permute-start | bytes 196616 | tf_op jit(solution)/shard_map/ppermute | solution.py:29
  38.8 8.6 %collective-permute-start.13 = (bf16[128,1024]{1,0:T(8,128)(2,1)S(1)}, bf16[128,1024]{1,0:T(8,128)(2,1)S(1)}, u32[]{:S(2)}, u32[]{:S(2)}) collective-permute-start(bf16[128,1024]{1,0:T(8,128)(2,1)S(1)} %get-tuple-element.58), channel_id=1, source_target_pairs={{0,2},{2,0},{1,3},{3,1},{4,6},{6,4},{5,7},{7,5},{8,10},{10,8},{9,1... | collective-permute-start | bytes 786440 | tf_op jit(solution)/shard_map/ppermute | solution.py:29
  42.8 6.4 %copy-start = (f32[4,64,1024]{2,1,0:T(8,128)S(1)}, f32[4,64,1024]{2,1,0:T(8,128)}, u32[]{:S(2)}) copy-start(f32[4,64,1024]{2,1,0:T(8,128)} %refs_6_.3) | copy-start | bytes 3145732
  45.3 1.4 %collective-permute-start.19 = (bf16[2,32,1024]{2,1,0:T(8,128)(2,1)S(1)}, bf16[2,32,1024]{2,1,0:T(8,128)(2,1)S(1)}, u32[]{:S(2)}, u32[]{:S(2)}) collective-permute-start(bf16[2,32,1024]{2,1,0:T(8,128)(2,1)S(1)} %get-tuple-element.64), channel_id=1, source_target_pairs={{0,1},{1,0},{2,3},{3,2},{4,5},{5,4},{6,7},{7,6},{8,9},{9,8},{10,11... | collective-permute-start | bytes 393224 | tf_op jit(solution)/shard_map/ppermute | solution.py:29
  45.3 1.5 %collective-permute-start.20 = (bf16[2,32,1024]{2,1,0:T(8,128)(2,1)S(1)}, bf16[2,32,1024]{2,1,0:T(8,128)(2,1)S(1)}, u32[]{:S(2)}, u32[]{:S(2)}) collective-permute-start(bf16[2,32,1024]{2,1,0:T(8,128)(2,1)S(1)} %get-tuple-element.65), channel_id=1, source_target_pairs={{0,1},{1,0},{2,3},{3,2},{4,5},{5,4},{6,7},{7,6},{8,9},{9,8},{10,11... | collective-permute-start | bytes 393224 | tf_op jit(solution)/shard_map/ppermute | solution.py:29
  45.8 1.3 %collective-permute-start.21 = (bf16[2,32,1024]{2,1,0:T(8,128)(2,1)S(1)}, bf16[2,32,1024]{2,1,0:T(8,128)(2,1)S(1)}, u32[]{:S(2)}, u32[]{:S(2)}) collective-permute-start(bf16[2,32,1024]{2,1,0:T(8,128)(2,1)S(1)} %get-tuple-element.66), channel_id=1, source_target_pairs={{0,1},{1,0},{2,3},{3,2},{4,5},{5,4},{6,7},{7,6},{8,9},{9,8},{10,11... | collective-permute-start | bytes 393224 | tf_op jit(solution)/shard_map/ppermute | solution.py:29
  45.9 1.5 %collective-permute-start.22 = (bf16[2,32,1024]{2,1,0:T(8,128)(2,1)S(1)}, bf16[2,32,1024]{2,1,0:T(8,128)(2,1)S(1)}, u32[]{:S(2)}, u32[]{:S(2)}) collective-permute-start(bf16[2,32,1024]{2,1,0:T(8,128)(2,1)S(1)} %get-tuple-element.67), channel_id=1, source_target_pairs={{0,1},{1,0},{2,3},{3,2},{4,5},{5,4},{6,7},{7,6},{8,9},{9,8},{10,11... | collective-permute-start | bytes 393224 | tf_op jit(solution)/shard_map/ppermute | solution.py:29
  48.2 8.6 %collective-permute-start.23 = (bf16[128,1024]{1,0:T(8,128)(2,1)S(1)}, bf16[128,1024]{1,0:T(8,128)(2,1)S(1)}, u32[]{:S(2)}, u32[]{:S(2)}) collective-permute-start(bf16[128,1024]{1,0:T(8,128)(2,1)S(1)} %get-tuple-element.69), channel_id=1, source_target_pairs={{0,2},{2,0},{1,3},{3,1},{4,6},{6,4},{5,7},{7,5},{8,10},{10,8},{9,1... | collective-permute-start | bytes 786440 | tf_op jit(solution)/shard_map/ppermute | solution.py:29
  50.0 8.7 %collective-permute-start.16 = (f32[8,128]{1,0:T(8,128)S(1)}, f32[8,128]{1,0:T(8,128)S(1)}, u32[]{:S(2)}, u32[]{:S(2)}) collective-permute-start(f32[8,128]{1,0:T(8,128)S(1)} %get-tuple-element.59.refs_0_), channel_id=1, source_target_pairs={{0,3},{1,2},{2,1},{3,0},{4,7},{5,6},{6,5},{7,4},{8,11},{9,10},{10,... | collective-permute-start | bytes 12296 | tf_op jit(solution)/shard_map/ppermute | solution.py:29
  50.6 8.8 %collective-permute-start.15 = (f32[8,128]{1,0:T(8,128)S(1)}, f32[8,128]{1,0:T(8,128)S(1)}, u32[]{:S(2)}, u32[]{:S(2)}) collective-permute-start(f32[8,128]{1,0:T(8,128)S(1)} %get-tuple-element.59.refs_0_), channel_id=1, source_target_pairs={{0,2},{1,3},{2,0},{3,1},{4,6},{5,7},{6,4},{7,5},{8,10},{9,11},{10,... | collective-permute-start | bytes 12296 | tf_op jit(solution)/shard_map/ppermute | solution.py:29
  51.7 7.8 %collective-permute-start.14 = (f32[8,128]{1,0:T(8,128)S(1)}, f32[8,128]{1,0:T(8,128)S(1)}, u32[]{:S(2)}, u32[]{:S(2)}) collective-permute-start(f32[8,128]{1,0:T(8,128)S(1)} %get-tuple-element.59.refs_0_), channel_id=1, source_target_pairs={{0,1},{1,0},{2,3},{3,2},{4,5},{5,4},{6,7},{7,6},{8,9},{9,8},{10,11... | collective-permute-start | bytes 12296 | tf_op jit(solution)/shard_map/ppermute | solution.py:29
  57.6 6.2 %collective-permute-start.26 = (f32[8,128]{1,0:T(8,128)S(1)}, f32[8,128]{1,0:T(8,128)S(1)}, u32[]{:S(2)}, u32[]{:S(2)}) collective-permute-start(f32[8,128]{1,0:T(8,128)S(1)} %get-tuple-element.70.refs_5_.refs_0_), channel_id=1, source_target_pairs={{0,3},{1,2},{2,1},{3,0},{4,7},{5,6},{6,5},{7,4},{8,11},{9,10},{10,... | collective-permute-start | bytes 12296 | tf_op jit(solution)/shard_map/ppermute | solution.py:29
  57.7 6.1 %collective-permute-start.25 = (f32[8,128]{1,0:T(8,128)S(1)}, f32[8,128]{1,0:T(8,128)S(1)}, u32[]{:S(2)}, u32[]{:S(2)}) collective-permute-start(f32[8,128]{1,0:T(8,128)S(1)} %get-tuple-element.70.refs_5_.refs_0_), channel_id=1, source_target_pairs={{0,2},{1,3},{2,0},{3,1},{4,6},{5,7},{6,4},{7,5},{8,10},{9,11},{10,... | collective-permute-start | bytes 12296 | tf_op jit(solution)/shard_map/ppermute | solution.py:29
  58.7 5.1 %collective-permute-start.24 = (f32[8,128]{1,0:T(8,128)S(1)}, f32[8,128]{1,0:T(8,128)S(1)}, u32[]{:S(2)}, u32[]{:S(2)}) collective-permute-start(f32[8,128]{1,0:T(8,128)S(1)} %get-tuple-element.70.refs_5_.refs_0_), channel_id=1, source_target_pairs={{0,1},{1,0},{2,3},{3,2},{4,5},{5,4},{6,7},{7,6},{8,9},{9,8},{10,11... | collective-permute-start | bytes 12296 | tf_op jit(solution)/shard_map/ppermute | solution.py:29
  60.3 11.1 %collective-permute-start.27 = (bf16[64,1024]{1,0:T(8,128)(2,1)S(1)}, bf16[64,1024]{1,0:T(8,128)(2,1)S(1)}, u32[]{:S(2)}, u32[]{:S(2)}) collective-permute-start(bf16[64,1024]{1,0:T(8,128)(2,1)S(1)} %get-tuple-element.73), channel_id=1, source_target_pairs={{0,4},{4,0},{8,12},{12,8},{1,5},{5,1},{9,13},{13,9},{2,6},{6,2},{1... | collective-permute-start | bytes 393224 | tf_op jit(solution)/shard_map/ppermute | solution.py:29
  64.6 12.9 %collective-permute-start.28 = (bf16[64,1024]{1,0:T(8,128)(2,1)S(1)}, bf16[64,1024]{1,0:T(8,128)(2,1)S(1)}, u32[]{:S(2)}, u32[]{:S(2)}) collective-permute-start(bf16[64,1024]{1,0:T(8,128)(2,1)S(1)} %get-tuple-element.74), channel_id=1, source_target_pairs={{0,8},{4,12},{8,0},{12,4},{1,9},{5,13},{9,1},{13,5},{2,10},{6,14},... | collective-permute-start | bytes 393224 | tf_op jit(solution)/shard_map/ppermute | solution.py:29
  67.0 10.5 %collective-permute-start.29 = (bf16[64,1024]{1,0:T(8,128)(2,1)S(1)}, bf16[64,1024]{1,0:T(8,128)(2,1)S(1)}, u32[]{:S(2)}, u32[]{:S(2)}) collective-permute-start(bf16[64,1024]{1,0:T(8,128)(2,1)S(1)} %get-tuple-element.75), channel_id=1, source_target_pairs={{0,12},{4,8},{8,4},{12,0},{1,13},{5,9},{9,5},{13,1},{2,14},{6,10},... | collective-permute-start | bytes 393224 | tf_op jit(solution)/shard_map/ppermute | solution.py:29
  (4 other events, 2.7 us)

commit v8 on v7

--- a/solution.py
+++ b/solution.py
@@ -13,7 +13,7 @@
 EPSILON = 1e-06
 MIB = 1 << 20
 LANES = 128
-SPLIT = 4
+GROUP = (16, 32)
 CORE, COLUMN, ORDER, BLOCK, COUNT = 0, 1, 2, 8, 16
 BF16 = jnp.bfloat16
 F32 = jnp.float32
@@ -359,6 +359,9 @@
         product = jnp.sum(value * target[0], axis=1, keepdims=True)
         lane = lax.broadcasted_iota(jnp.int32, (count, LANES), 1)
         columns.append(jnp.where(lane == 0, square, jnp.where(lane == 1, product, 0.0)))
+    spare = sums.shape[1] - own.shape[0]
+    if spare:
+        columns.append(jnp.zeros((spare, LANES), F32))
     sums[...] = jnp.concatenate(columns, axis=0).T[:8]
 
 
@@ -378,7 +381,7 @@
 
 def lag_stats(scal, scale, pieces, own, more, observed):
     rows, lag_dev = own.shape
-    outs = [jax.ShapeDtypeStruct((rows, lag_dev), F32), jax.ShapeDtypeStruct((8, rows), F32)]
+    outs = [jax.ShapeDtypeStruct((rows, lag_dev), F32), jax.ShapeDtypeStruct((8, -(-rows // LANES) * LANES), F32)]
     return pl.pallas_call(
         functools.partial(stats_kernel, scale, pieces, len(more)),
         grid_spec=pltpu.PrefetchScalarGridSpec(
@@ -534,8 +537,8 @@
     table = make_table(scal, trig, classes, span, peers)
     if direct and blocks == 4:
         chunks = [
-            [(0, 0, slots), (1, 0, slots)],
-            [(2, 0, slots), (3, 0, slots)],
+            [(3, 0, slots), (1, 0, slots), (0, 0, slots)],
+            [(2, 0, slots)],
         ]
     else:
         chunks = [[(d, first, some) for d in range(blocks)] for first in (0, some)]
@@ -546,7 +549,11 @@
     sent, own_rows = gather_rows(
         scal, table, held[0], held[1:], make_perm(part), src_ids, rec_ids, messages
     )
-    arrived = [swapped(x, "recv", places, m[0]) for m, x in zip(messages, sent)]
+    arrived = []
+    for m, x in zip(messages, sent):
+        if direct and m[0] == 2:
+            arrived[0], x = lax.optimization_barrier((arrived[0], x))
+        arrived.append(swapped(x, "recv", places, m[0]))
     if not direct:
         stacked = jnp.stack(arrived)
         whole_rows = [
@@ -556,13 +563,13 @@
     corrs, all_sums, returned, returned_pieces = [], [], [], []
     after = []
     for q, pieces in enumerate(chunks):
-        rows = arrived[len(pieces) * q : len(pieces) * (q + 1)]
+        rows, arrived = arrived[: len(pieces)], arrived[len(pieces) :]
         lhs = cross_rows(weight, after[:1], rows, own_rows, pieces, classes)
         keep, *sends = lag_parts(
-            scal, [], lhs, table, geometry, columns, lag_dev, SPLIT if q else 2 * SPLIT, SMALL if q else LARGE
+            scal, [], lhs, table, geometry, columns, lag_dev, sum(p[2] for p in pieces) // GROUP[q], SMALL if q else LARGE
         )
         sends = [swapped(x, "freq", cores, 1) for x in sends]
-        own, *sends = add_cores(scal, after[1:], keep, sends)
+        own, *sends = add_cores(scal, [], keep, sends)
         more = [swapped(x, "win", columns, s + 1) for s, x in enumerate(sends)]
         after = [own, *more]
         corr, sums = lag_stats(scal, lag_scale, pieces, own, more, observed)

time: 78.8 us -> 78.6 us (level)
  local copies, waits for them, and re-layouts: 4.02 us -> 1.38 us
  waiting for transfers between devices: 25.6 us -> 27.6 us
    unnamed x12, local copies, waits for them, and re-layouts: 2.68 us -> 0.03 us
    ppermute x30 -> x32, waiting for transfers between devices: 25.6 us -> 27.6 us  [swapped(): return lax.ppermute(value, axis, [(i, i ^ step) for i in range(size)])]
    ppermute x30 -> x32, starting transfers between devices: 27.8 us -> 28.3 us  [swapped(): return lax.ppermute(value, axis, [(i, i ^ step) for i in range(size)])]
  transfers between devices with their start and end apart: 30 -> 32, of which waited for: 14 -> 17; matrix products, arithmetic and copies ran while one was open for 0% -> 0% of each run, Pallas kernels for 20% -> 21%
where the time goes in v8:
time: 78.6 us; the launch traced here: 78.5 us
  starting transfers between devices  28.3 us (36%)
  waiting for transfers between devices  27.6 us (35%)
  Pallas kernels  19.7 us (25%)
  between operations  1.54 us (2%)
  local copies, waits for them, and re-layouts  1.38 us (2%)
    ppermute x32, starting transfers between devices, swapped(): return lax.ppermute(value, axis, [(i, i ^ step) for i in range(size)])  28.3 us
    ppermute x32, waiting for transfers between devices, swapped(): return lax.ppermute(value, axis, [(i, i ^ step) for i in range(size)])  27.6 us
    pallas_call x2, Pallas kernels, lag_parts(): pl.pallas_call(functools.partial(lags_kernel, geometry, len(after)), out_...  4.88 us
    pallas_call x1, Pallas kernels, normed_rows(): pl.pallas_call(functools.partial(normed_kernel, lag_total, chunks, len(su...  2.95 us
    pallas_call x1, Pallas kernels, gather_rows(): pl.pallas_call(functools.partial(rows_kernel, used, sends, messages), out...  1.81 us
    pallas_call x1, Pallas kernels, make_table(): pl.pallas_call(functools.partial(table_kernel, classes, parts), out_shape...  1.78 us
    pallas_call x2, Pallas kernels, gradients(): pl.pallas_call(functools.partial(gradient_kernel, lag_total, pieces, len(...  1.66 us
    pallas_call x2, Pallas kernels, lag_stats(): pl.pallas_call(functools.partial(stats_kernel, scale, pieces, len(more)),...  1.57 us
  transfers between devices with their start and end apart: 32, of which 17 were waited for; matrix products, arithmetic and copies ran while one was open for 0% of the time, Pallas kernels for 21%

profile of v8, /device:TPU:0, one launch (start us, length us, event | category | flops | bytes accessed | tf_op | source)
XLA Modules:
  0.0 78.5 jit_solution(15391848694060374481)
XLA Ops:
  0.7 1.3 %constant_dynamic-slice_fusion = (bf16[1,2,128,1024]{3,2,1,0:T(8,128)(2,1)S(1)}, bf16[1,2,128,1024]{3,2,1,0:T(8,128)(2,1)S(1)}) fusion(bf16[1,2,128,2048]{3,2,1,0:T(8,128)(2,1)} %param.8, s32[]{:T(128)S(6)} %select_n.7, s32[]{:T(128)S(6)} %select_n.6), kind=kLoop, calls=%fused_computation | loop fusion | bytes 2097160 | tf_op jit(solution)/shard_map/dynamic_slice | solution.py:514
  2.0 3.0 %collective-permute-start = (bf16[1,2,128,1024]{3,2,1,0:T(8,128)(2,1)S(1)}, bf16[1,2,128,1024]{3,2,1,0:T(8,128)(2,1)S(1)}, u32[]{:S(2)}, u32[]{:S(2)}) collective-permute-start(bf16[1,2,128,1024]{3,2,1,0:T(8,128)(2,1)S(1)} %get-tuple-element.82), channel_id=1, source_target_pairs={{0,2},{2,0},{1,3},{3,1},{4,6},{6,4},{5,7},{7,5},{8,10},{10,8},{9,1... | collective-permute-start | bytes 1572872 | tf_op jit(solution)/shard_map/ppermute | solution.py:29
  5.7 1.2 %index.1 = (s32[128]{0:T(128)S(1)}, s32[1,64]{1,0:T(1,128)S(1)}, s32[1,64]{1,0:T(1,128)S(1)}, s32[1,64]{1,0:T(1,128)S(1)}, s32[1,64]{1,0:T(1,128)S(1)}, /*index=5*/s32[4,64]{1,0:T(4,128)S(1)}) custom-call(s32[1]{0:T(128)S(6)} %copy.10.refs_0_, s32[4]{0:T(128)S(1)} %copy-done.4, s32[4]{0:T(128)S(1)} %bitcast.1, s32[4,64]{1,0:T(4,128)S(1)} %copy-done.2, ...), custom_call_target="tpu_custom_call" | custom-call | flops 1 | bytes 1 | tf_op jit(solution)/shard_map/index/pallas_call | solution.py:92
  7.0 1.6 %collective-permute-start.1 = (s32[1,64]{1,0:T(1,128)S(1)}, s32[1,64]{1,0:T(1,128)S(1)}, u32[]{:S(2)}, u32[]{:S(2)}) collective-permute-start(s32[1,64]{1,0:T(1,128)S(1)} %get-tuple-element.44), channel_id=1, source_target_pairs={{0,4},{4,0},{8,12},{12,8},{1,5},{5,1},{9,13},{13,9},{2,6},{6,2},{1... | collective-permute-start | bytes 776 | tf_op jit(solution)/shard_map/ppermute | solution.py:29
  8.6 2.6 %collective-permute-start.2 = (s32[1,64]{1,0:T(1,128)S(1)}, s32[1,64]{1,0:T(1,128)S(1)}, u32[]{:S(2)}, u32[]{:S(2)}) collective-permute-start(s32[1,64]{1,0:T(1,128)S(1)} %get-tuple-element.45), channel_id=1, source_target_pairs={{0,8},{4,12},{8,0},{12,4},{1,9},{5,13},{9,1},{13,5},{2,10},{6,14},... | collective-permute-start | bytes 776 | tf_op jit(solution)/shard_map/ppermute | solution.py:29
  12.0 1.8 %table.1.after.refs_1_ = bf16[8,256,1024]{2,1,0:T(8,128)(2,1)S(1)} custom-call(s32[128]{0:T(128)S(1)} %get-tuple-element.42.scal, f32[2,56,1024]{2,1,0:T(8,128)S(1)} %copy-done.1), custom_call_target="tpu_custom_call" | custom-call | flops 1 | bytes 1 | tf_op jit(solution)/shard_map/table/pallas_call | solution.py:126
  13.8 2.7 %collective-permute-done.3.refs_5_.refs_0_ = s32[1,64]{1,0:T(1,128)S(1)} collective-permute-done((s32[1,64]{1,0:T(1,128)S(1)}, s32[1,64]{1,0:T(1,128)S(1)}, u32[]{:S(2)}, u32[]{:S(2)}) %collective-permute-start.3) | collective-permute-done | bytes 288 | tf_op jit(solution)/shard_map/ppermute | solution.py:29
  17.0 1.8 %rows.1 = (bf16[1,2,64,1024]{3,2,1,0:T(8,128)(2,1)S(1)}, bf16[1,2,64,1024]{3,2,1,0:T(8,128)(2,1)S(1)}, bf16[1,2,64,1024]{3,2,1,0:T(8,128)(2,1)S(1)}, bf16[1,2,64...) custom-call(s32[128]{0:T(128)S(1)} %get-tuple-element.42.scal, bf16[8,256,1024]{2,1,0:T(8,128)(2,1)S(1)} %table.1.after.refs_1_, ...), custom_call_target="tpu_custom_call" | custom-call | flops 1 | bytes 1 | tf_op jit(solution)/shard_map/rows/pallas_call | solution.py:191
  18.8 3.9 %collective-permute-start.4 = (bf16[1,2,64,1024]{3,2,1,0:T(8,128)(2,1)S(1)}, bf16[1,2,64,1024]{3,2,1,0:T(8,128)(2,1)S(1)}, u32[]{:S(2)}, u32[]{:S(2)}) collective-permute-start(bf16[1,2,64,1024]{3,2,1,0:T(8,128)(2,1)S(1)} %get-tuple-element.48), channel_id=1, source_target_pairs={{0,12},{4,8},{8,4},{12,0},{1,13},{5,9},{9,5},{13,1},{2,14},{6,10},... | collective-permute-start | bytes 786440 | tf_op jit(solution)/shard_map/ppermute | solution.py:29
  22.7 7.2 %collective-permute-done.4.refs_0_ = bf16[1,2,64,1024]{3,2,1,0:T(8,128)(2,1)S(1)} collective-permute-done((bf16[1,2,64,1024]{3,2,1,0:T(8,128)(2,1)S(1)}, bf16[1,2,64,1024]{3,2,1,0:T(8,128)(2,1)S(1)}, u32[]{:S(2)}, u32[]{:S(2)}) %collective-permute-start.4) | collective-permute-done | bytes 262176 | tf_op jit(solution)/shard_map/ppermute | solution.py:29
  29.9 4.5 %collective-permute-start.22 = (bf16[1,2,64,1024]{3,2,1,0:T(8,128)(2,1)S(1)}, bf16[1,2,64,1024]{3,2,1,0:T(8,128)(2,1)S(1)}, u32[]{:S(2)}, u32[]{:S(2)}) collective-permute-start(bf16[1,2,64,1024]{3,2,1,0:T(8,128)(2,1)S(1)} %get-tuple-element.71), channel_id=1, source_target_pairs={{0,8},{4,12},{8,0},{12,4},{1,9},{5,13},{9,1},{13,5},{2,10},{6,14},... | collective-permute-start | bytes 786440 | tf_op jit(solution)/shard_map/ppermute | solution.py:29
  34.5 2.0 %collective-permute-done.5.refs_1_ = bf16[1,2,64,1024]{3,2,1,0:T(8,128)(2,1)S(1)} collective-permute-done((bf16[1,2,64,1024]{3,2,1,0:T(8,128)(2,1)S(1)}, bf16[1,2,64,1024]{3,2,1,0:T(8,128)(2,1)S(1)}, u32[]{:S(2)}, u32[]{:S(2)}) %collective-permute-start.5) | collective-permute-done | bytes 262176 | tf_op jit(solution)/shard_map/ppermute | solution.py:29
  36.9 3.1 %lags.2 = (f32[2,192,1024]{2,1,0:T(8,128)S(1)}, bf16[2,16,1024]{2,1,0:T(8,128)(2,1)S(1)}, bf16[2,16,1024]{2,1,0:T(8,128)(2,1)S(1)}, bf16[2,16,1024]{2,1,0:T(8,12...) custom-call(s32[128]{0:T(128)S(1)} %get-tuple-element.42.scal, ...), custom_call_target="tpu_custom_call" | custom-call | flops 20000000000 | bytes 1048576 | tf_op jit(solution)/shard_map/lags/pallas_call | solution.py:300
  44.5 0.9 %cores.2 = (f32[192,1024]{1,0:T(8,128)S(1)}, bf16[192,1024]{1,0:T(8,128)(2,1)S(1)}) custom-call(s32[128]{0:T(128)S(1)} %get-tuple-element.42.scal, f32[2,192,1024]{2,1,0:T(8,128)S(1)} %get-tuple-element.54.refs_0_, bf16[2,16,1024]{2,1,0:T(8,128)(2,1)S(1)} %collective-permute-done.6.refs_1_, bf16[2,16,1024]{2,1,0:T(8,128)(2,1)S(1)} %collective-permute-done.7.refs_2_, ...), custom_call_target="tpu_custom_call" | custom-call | flops 1 | bytes 1 | tf_op jit(solution)/shard_map/cores/pallas_call | solution.py:335
  45.5 1.5 %collective-permute-start.18 = (bf16[192,1024]{1,0:T(8,128)(2,1)S(1)}, bf16[192,1024]{1,0:T(8,128)(2,1)S(1)}, u32[]{:S(2)}, u32[]{:S(2)}) collective-permute-start(bf16[192,1024]{1,0:T(8,128)(2,1)S(1)} %get-tuple-element.68), channel_id=1, source_target_pairs={{0,2},{2,0},{1,3},{3,1},{4,6},{6,4},{5,7},{7,5},{8,10},{10,8},{9,1... | collective-permute-start | bytes 1179656 | tf_op jit(solution)/shard_map/ppermute | solution.py:29
  47.2 1.7 %lags.3 = (f32[2,64,1024]{2,1,0:T(8,128)S(1)}, bf16[2,32,1024]{2,1,0:T(8,128)(2,1)S(1)}, bf16[2,32,1024]{2,1,0:T(8,128)(2,1)S(1)}) custom-call(s32[128]{0:T(128)S(1)} %get-tuple-element.42.scal, bf16[8,128,256]{2,1,0:T(8,128)(2,1)S(1)} %cross.3.refs_0_, bf16[8,256,1024]{2,1,0:T(8,128)(2,1)S(1)} %table.1.after.refs_1_), custom_call_target="tpu_custom_call" | custom-call | flops 1 | bytes 1 | tf_op jit(solution)/shard_map/lags/pallas_call | solution.py:300
  49.5 0.8 %collective-permute-done.23.refs_1_ = bf16[2,32,1024]{2,1,0:T(8,128)(2,1)S(1)} collective-permute-done((bf16[2,32,1024]{2,1,0:T(8,128)(2,1)S(1)}, bf16[2,32,1024]{2,1,0:T(8,128)(2,1)S(1)}, u32[]{:S(2)}, u32[]{:S(2)}) %collective-permute-start.23) | collective-permute-done | bytes 131104 | tf_op jit(solution)/shard_map/ppermute | solution.py:29
  50.5 0.6 cores.3
  51.8 5.7 %collective-permute-done.18.refs_1_ = bf16[192,1024]{1,0:T(8,128)(2,1)S(1)} collective-permute-done((bf16[192,1024]{1,0:T(8,128)(2,1)S(1)}, bf16[192,1024]{1,0:T(8,128)(2,1)S(1)}, u32[]{:S(2)}, u32[]{:S(2)}) %collective-permute-start.18) | collective-permute-done | bytes 393248 | tf_op jit(solution)/shard_map/ppermute | solution.py:29
  57.5 0.9 %stats.2 = (f32[192,1024]{1,0:T(8,128)S(1)}, f32[8,256]{1,0:T(8,128)S(1)}) custom-call(s32[128]{0:T(128)S(1)} %get-tuple-element.42.scal, f32[192,1024]{1,0:T(8,128)S(1)} %get-tuple-element.67.refs_0_, bf16[192,1024]{1,0:T(8,128)(2,1)S(1)} %collective-permute-done.18.refs_1_, f32[4,64,1024]{2,1,0:T(8,128)S(1)} %copy-done, f32[4,64,1024]{2,1,0:T(8,128)S(1)} %copy-done, ...), custom_call_target="tpu_custom_call" | custom-call | flops 1 | bytes 1 | tf_op jit(solution)/shard_map/stats/pallas_call | solution.py:385
  58.4 1.5 %collective-permute-start.20 = (f32[8,256]{1,0:T(8,128)S(1)}, f32[8,256]{1,0:T(8,128)S(1)}, u32[]{:S(2)}, u32[]{:S(2)}) collective-permute-start(f32[8,256]{1,0:T(8,128)S(1)} %get-tuple-element.69.refs_0_), channel_id=1, source_target_pairs={{0,2},{1,3},{2,0},{3,1},{4,6},{5,7},{6,4},{7,5},{8,10},{9,11},{10,... | collective-permute-start | bytes 24584 | tf_op jit(solution)/shard_map/ppermute | solution.py:29
  60.2 0.7 stats.3
  61.0 1.1 %collective-permute-start.28 = (f32[8,128]{1,0:T(8,128)S(1)}, f32[8,128]{1,0:T(8,128)S(1)}, u32[]{:S(2)}, u32[]{:S(2)}) collective-permute-start(f32[8,128]{1,0:T(8,128)S(1)} %get-tuple-element.77.refs_5_.refs_0_), channel_id=1, source_target_pairs={{0,3},{1,2},{2,1},{3,0},{4,7},{5,6},{6,5},{7,4},{8,11},{9,10},{10,... | collective-permute-start | bytes 12296 | tf_op jit(solution)/shard_map/ppermute | solution.py:29
  62.0 0.8 collective-permute-start.27
  62.8 0.9 %gradient.2 = (bf16[64,1024]{1,0:T(8,128)(2,1)S(1)}, bf16[64,1024]{1,0:T(8,128)(2,1)S(1)}, bf16[64,1024]{1,0:T(8,128)(2,1)S(1)}) custom-call(s32[128]{0:T(128)S(1)} %get-tuple-element.42.scal, f32[8,256]{1,0:T(8,128)S(1)} %get-tuple-element.69.refs_0_, f32[8,256]{1,0:T(8,128)S(1)} %collective-permute-done.19.refs_1_, ...), custom_call_target="tpu_custom_call" | custom-call | flops 1 | bytes 1 | tf_op jit(solution)/shard_map/gradient/pallas_call | solution.py:427
  64.0 1.6 %collective-permute-done.27.refs_7_.refs_2_ = f32[8,128]{1,0:T(8,128)S(1)} collective-permute-done((f32[8,128]{1,0:T(8,128)S(1)}, f32[8,128]{1,0:T(8,128)S(1)}, u32[]{:S(2)}, u32[]{:S(2)}) %collective-permute-start.27) | collective-permute-done | bytes 4128 | tf_op jit(solution)/shard_map/ppermute | solution.py:29
  65.7 0.8 gradient.3
  66.4 2.6 %collective-permute-start.31 = (bf16[64,1024]{1,0:T(8,128)(2,1)S(1)}, bf16[64,1024]{1,0:T(8,128)(2,1)S(1)}, u32[]{:S(2)}, u32[]{:S(2)}) collective-permute-start(bf16[64,1024]{1,0:T(8,128)(2,1)S(1)} %gradient.3), channel_id=1, source_target_pairs={{0,8},{4,12},{8,0},{12,4},{1,9},{5,13},{9,1},{13,5},{2,10},{6,14},... | collective-permute-start | bytes 393224 | tf_op jit(solution)/shard_map/ppermute | solution.py:29
  69.1 3.0 %normed.1 = f32[4,64,1024]{2,1,0:T(8,128)} custom-call(s32[128]{0:T(128)S(1)} %get-tuple-element.42.scal, f32[8,256]{1,0:T(8,128)S(1)} %get-tuple-element.69.refs_0_, f32[8,256]{1,0:T(8,128)S(1)} %collective-permute-done.19.refs_1_, f32[8,256]{1,0:T(8,128)S(1)} %collective-permute-done.20.refs_2_, f32[8,256]{1,0:T(8,128)S(1)} %collective-permute-done.21.refs_3_, ...), custom_call_target="tpu_custom_call" | custom-call | flops 1 | bytes 1 | tf_op jit(solution)/shard_map/normed/pallas_call | solution.py:459
  72.0 3.2 %collective-permute-done.30.refs_5_ = bf16[64,1024]{1,0:T(8,128)(2,1)S(1)} collective-permute-done((bf16[64,1024]{1,0:T(8,128)(2,1)S(1)}, bf16[64,1024]{1,0:T(8,128)(2,1)S(1)}, u32[]{:S(2)}, u32[]{:S(2)}) %collective-permute-start.30) | collective-permute-done | bytes 131104 | tf_op jit(solution)/shard_map/ppermute | solution.py:29
  75.2 2.2 %collective-permute-done.31.refs_7_ = bf16[64,1024]{1,0:T(8,128)(2,1)S(1)} collective-permute-done((bf16[64,1024]{1,0:T(8,128)(2,1)S(1)}, bf16[64,1024]{1,0:T(8,128)(2,1)S(1)}, u32[]{:S(2)}, u32[]{:S(2)}) %collective-permute-start.31) | collective-permute-done | bytes 131104 | tf_op jit(solution)/shard_map/ppermute | solution.py:29
  77.4 1.1 %adjoint.1 = f32[128,1024]{1,0:T(8,128)} custom-call(s32[1,64]{1,0:T(1,128)S(1)} %collective-permute-done.3.refs_5_.refs_0_, s32[1,64]{1,0:T(1,128)S(1)} %collective-permute-done.1.refs_3_.refs_1_, s32[1,64]{1,0:T(1,128)S(1)} %get-tuple-element.43.refs_2_, s32[1,64]{1,0:T(1,128)S(1)} %collective-permute-done.2.refs_4_.refs_3_, ...), custom_call_target="tpu_custom_call" | custom-call | flops 1 | bytes 1 | tf_op jit(solution)/shard_map/adjoint/pallas_call | solution.py:483
  (61 shorter events, 8.4 us)
Async XLA Ops:
  2.0 14.9 %collective-permute-start = (bf16[1,2,128,1024]{3,2,1,0:T(8,128)(2,1)S(1)}, bf16[1,2,128,1024]{3,2,1,0:T(8,128)(2,1)S(1)}, u32[]{:S(2)}, u32[]{:S(2)}) collective-permute-start(bf16[1,2,128,1024]{3,2,1,0:T(8,128)(2,1)S(1)} %get-tuple-element.82), channel_id=1, source_target_pairs={{0,2},{2,0},{1,3},{3,1},{4,6},{6,4},{5,7},{7,5},{8,10},{10,8},{9,1... | collective-permute-start | bytes 1572872 | tf_op jit(solution)/shard_map/ppermute | solution.py:29
  7.0 6.9 %collective-permute-start.1 = (s32[1,64]{1,0:T(1,128)S(1)}, s32[1,64]{1,0:T(1,128)S(1)}, u32[]{:S(2)}, u32[]{:S(2)}) collective-permute-start(s32[1,64]{1,0:T(1,128)S(1)} %get-tuple-element.44), channel_id=1, source_target_pairs={{0,4},{4,0},{8,12},{12,8},{1,5},{5,1},{9,13},{13,9},{2,6},{6,2},{1... | collective-permute-start | bytes 776 | tf_op jit(solution)/shard_map/ppermute | solution.py:29
  8.6 5.2 %collective-permute-start.2 = (s32[1,64]{1,0:T(1,128)S(1)}, s32[1,64]{1,0:T(1,128)S(1)}, u32[]{:S(2)}, u32[]{:S(2)}) collective-permute-start(s32[1,64]{1,0:T(1,128)S(1)} %get-tuple-element.45), channel_id=1, source_target_pairs={{0,8},{4,12},{8,0},{12,4},{1,9},{5,13},{9,1},{13,5},{2,10},{6,14},... | collective-permute-start | bytes 776 | tf_op jit(solution)/shard_map/ppermute | solution.py:29
  11.2 5.3 %collective-permute-start.3 = (s32[1,64]{1,0:T(1,128)S(1)}, s32[1,64]{1,0:T(1,128)S(1)}, u32[]{:S(2)}, u32[]{:S(2)}) collective-permute-start(s32[1,64]{1,0:T(1,128)S(1)} %get-tuple-element.46), channel_id=1, source_target_pairs={{0,12},{4,8},{8,4},{12,0},{1,13},{5,9},{9,5},{13,1},{2,14},{6,10},... | collective-permute-start | bytes 776 | tf_op jit(solution)/shard_map/ppermute | solution.py:29
  18.8 11.1 %collective-permute-start.4 = (bf16[1,2,64,1024]{3,2,1,0:T(8,128)(2,1)S(1)}, bf16[1,2,64,1024]{3,2,1,0:T(8,128)(2,1)S(1)}, u32[]{:S(2)}, u32[]{:S(2)}) collective-permute-start(bf16[1,2,64,1024]{3,2,1,0:T(8,128)(2,1)S(1)} %get-tuple-element.48), channel_id=1, source_target_pairs={{0,12},{4,8},{8,4},{12,0},{1,13},{5,9},{9,5},{13,1},{2,14},{6,10},... | collective-permute-start | bytes 786440 | tf_op jit(solution)/shard_map/ppermute | solution.py:29
  22.7 13.8 %collective-permute-start.5 = (bf16[1,2,64,1024]{3,2,1,0:T(8,128)(2,1)S(1)}, bf16[1,2,64,1024]{3,2,1,0:T(8,128)(2,1)S(1)}, u32[]{:S(2)}, u32[]{:S(2)}) collective-permute-start(bf16[1,2,64,1024]{3,2,1,0:T(8,128)(2,1)S(1)} %get-tuple-element.51), channel_id=1, source_target_pairs={{0,4},{4,0},{8,12},{12,8},{1,5},{5,1},{9,13},{13,9},{2,6},{6,2},{1... | collective-permute-start | bytes 786440 | tf_op jit(solution)/shard_map/ppermute | solution.py:29
  29.9 17.1 %collective-permute-start.22 = (bf16[1,2,64,1024]{3,2,1,0:T(8,128)(2,1)S(1)}, bf16[1,2,64,1024]{3,2,1,0:T(8,128)(2,1)S(1)}, u32[]{:S(2)}, u32[]{:S(2)}) collective-permute-start(bf16[1,2,64,1024]{3,2,1,0:T(8,128)(2,1)S(1)} %get-tuple-element.71), channel_id=1, source_target_pairs={{0,8},{4,12},{8,0},{12,4},{1,9},{5,13},{9,1},{13,5},{2,10},{6,14},... | collective-permute-start | bytes 786440 | tf_op jit(solution)/shard_map/ppermute | solution.py:29
  40.0 1.3 %collective-permute-start.6 = (bf16[2,16,1024]{2,1,0:T(8,128)(2,1)S(1)}, bf16[2,16,1024]{2,1,0:T(8,128)(2,1)S(1)}, u32[]{:S(2)}, u32[]{:S(2)}) collective-permute-start(bf16[2,16,1024]{2,1,0:T(8,128)(2,1)S(1)} %get-tuple-element.55), channel_id=1, source_target_pairs={{0,1},{1,0},{2,3},{3,2},{4,5},{5,4},{6,7},{7,6},{8,9},{9,8},{10,11... | collective-permute-start | bytes 196616 | tf_op jit(solution)/shard_map/ppermute | solution.py:29
  40.1 1.4 %collective-permute-start.7 = (bf16[2,16,1024]{2,1,0:T(8,128)(2,1)S(1)}, bf16[2,16,1024]{2,1,0:T(8,128)(2,1)S(1)}, u32[]{:S(2)}, u32[]{:S(2)}) collective-permute-start(bf16[2,16,1024]{2,1,0:T(8,128)(2,1)S(1)} %get-tuple-element.56), channel_id=1, source_target_pairs={{0,1},{1,0},{2,3},{3,2},{4,5},{5,4},{6,7},{7,6},{8,9},{9,8},{10,11... | collective-permute-start | bytes 196616 | tf_op jit(solution)/shard_map/ppermute | solution.py:29
  40.6 1.3 %collective-permute-start.8 = (bf16[2,16,1024]{2,1,0:T(8,128)(2,1)S(1)}, bf16[2,16,1024]{2,1,0:T(8,128)(2,1)S(1)}, u32[]{:S(2)}, u32[]{:S(2)}) collective-permute-start(bf16[2,16,1024]{2,1,0:T(8,128)(2,1)S(1)} %get-tuple-element.57), channel_id=1, source_target_pairs={{0,1},{1,0},{2,3},{3,2},{4,5},{5,4},{6,7},{7,6},{8,9},{9,8},{10,11... | collective-permute-start | bytes 196616 | tf_op jit(solution)/shard_map/ppermute | solution.py:29
  40.7 1.3 %collective-permute-start.9 = (bf16[2,16,1024]{2,1,0:T(8,128)(2,1)S(1)}, bf16[2,16,1024]{2,1,0:T(8,128)(2,1)S(1)}, u32[]{:S(2)}, u32[]{:S(2)}) collective-permute-start(bf16[2,16,1024]{2,1,0:T(8,128)(2,1)S(1)} %get-tuple-element.58), channel_id=1, source_target_pairs={{0,1},{1,0},{2,3},{3,2},{4,5},{5,4},{6,7},{7,6},{8,9},{9,8},{10,11... | collective-permute-start | bytes 196616 | tf_op jit(solution)/shard_map/ppermute | solution.py:29
  41.3 1.3 %collective-permute-start.10 = (bf16[2,16,1024]{2,1,0:T(8,128)(2,1)S(1)}, bf16[2,16,1024]{2,1,0:T(8,128)(2,1)S(1)}, u32[]{:S(2)}, u32[]{:S(2)}) collective-permute-start(bf16[2,16,1024]{2,1,0:T(8,128)(2,1)S(1)} %get-tuple-element.59), channel_id=1, source_target_pairs={{0,1},{1,0},{2,3},{3,2},{4,5},{5,4},{6,7},{7,6},{8,9},{9,8},{10,11... | collective-permute-start | bytes 196616 | tf_op jit(solution)/shard_map/ppermute | solution.py:29
  41.5 1.3 %collective-permute-start.11 = (bf16[2,16,1024]{2,1,0:T(8,128)(2,1)S(1)}, bf16[2,16,1024]{2,1,0:T(8,128)(2,1)S(1)}, u32[]{:S(2)}, u32[]{:S(2)}) collective-permute-start(bf16[2,16,1024]{2,1,0:T(8,128)(2,1)S(1)} %get-tuple-element.60), channel_id=1, source_target_pairs={{0,1},{1,0},{2,3},{3,2},{4,5},{5,4},{6,7},{7,6},{8,9},{9,8},{10,11... | collective-permute-start | bytes 196616 | tf_op jit(solution)/shard_map/ppermute | solution.py:29
  41.9 1.3 %collective-permute-start.12 = (bf16[2,16,1024]{2,1,0:T(8,128)(2,1)S(1)}, bf16[2,16,1024]{2,1,0:T(8,128)(2,1)S(1)}, u32[]{:S(2)}, u32[]{:S(2)}) collective-permute-start(bf16[2,16,1024]{2,1,0:T(8,128)(2,1)S(1)} %get-tuple-element.61), channel_id=1, source_target_pairs={{0,1},{1,0},{2,3},{3,2},{4,5},{5,4},{6,7},{7,6},{8,9},{9,8},{10,11... | collective-permute-start | bytes 196616 | tf_op jit(solution)/shard_map/ppermute | solution.py:29
  42.0 1.3 %collective-permute-start.13 = (bf16[2,16,1024]{2,1,0:T(8,128)(2,1)S(1)}, bf16[2,16,1024]{2,1,0:T(8,128)(2,1)S(1)}, u32[]{:S(2)}, u32[]{:S(2)}) collective-permute-start(bf16[2,16,1024]{2,1,0:T(8,128)(2,1)S(1)} %get-tuple-element.62), channel_id=1, source_target_pairs={{0,1},{1,0},{2,3},{3,2},{4,5},{5,4},{6,7},{7,6},{8,9},{9,8},{10,11... | collective-permute-start | bytes 196616 | tf_op jit(solution)/shard_map/ppermute | solution.py:29
  42.6 1.3 %collective-permute-start.14 = (bf16[2,16,1024]{2,1,0:T(8,128)(2,1)S(1)}, bf16[2,16,1024]{2,1,0:T(8,128)(2,1)S(1)}, u32[]{:S(2)}, u32[]{:S(2)}) collective-permute-start(bf16[2,16,1024]{2,1,0:T(8,128)(2,1)S(1)} %get-tuple-element.63), channel_id=1, source_target_pairs={{0,1},{1,0},{2,3},{3,2},{4,5},{5,4},{6,7},{7,6},{8,9},{9,8},{10,11... | collective-permute-start | bytes 196616 | tf_op jit(solution)/shard_map/ppermute | solution.py:29
  42.8 1.3 %collective-permute-start.15 = (bf16[2,16,1024]{2,1,0:T(8,128)(2,1)S(1)}, bf16[2,16,1024]{2,1,0:T(8,128)(2,1)S(1)}, u32[]{:S(2)}, u32[]{:S(2)}) collective-permute-start(bf16[2,16,1024]{2,1,0:T(8,128)(2,1)S(1)} %get-tuple-element.64), channel_id=1, source_target_pairs={{0,1},{1,0},{2,3},{3,2},{4,5},{5,4},{6,7},{7,6},{8,9},{9,8},{10,11... | collective-permute-start | bytes 196616 | tf_op jit(solution)/shard_map/ppermute | solution.py:29
  43.1 1.3 %collective-permute-start.16 = (bf16[2,16,1024]{2,1,0:T(8,128)(2,1)S(1)}, bf16[2,16,1024]{2,1,0:T(8,128)(2,1)S(1)}, u32[]{:S(2)}, u32[]{:S(2)}) collective-permute-start(bf16[2,16,1024]{2,1,0:T(8,128)(2,1)S(1)} %get-tuple-element.65), channel_id=1, source_target_pairs={{0,1},{1,0},{2,3},{3,2},{4,5},{5,4},{6,7},{7,6},{8,9},{9,8},{10,11... | collective-permute-start | bytes 196616 | tf_op jit(solution)/shard_map/ppermute | solution.py:29
  43.3 1.3 %collective-permute-start.17 = (bf16[2,16,1024]{2,1,0:T(8,128)(2,1)S(1)}, bf16[2,16,1024]{2,1,0:T(8,128)(2,1)S(1)}, u32[]{:S(2)}, u32[]{:S(2)}) collective-permute-start(bf16[2,16,1024]{2,1,0:T(8,128)(2,1)S(1)} %get-tuple-element.66), channel_id=1, source_target_pairs={{0,1},{1,0},{2,3},{3,2},{4,5},{5,4},{6,7},{7,6},{8,9},{9,8},{10,11... | collective-permute-start | bytes 196616 | tf_op jit(solution)/shard_map/ppermute | solution.py:29
  45.5 12.0 %collective-permute-start.18 = (bf16[192,1024]{1,0:T(8,128)(2,1)S(1)}, bf16[192,1024]{1,0:T(8,128)(2,1)S(1)}, u32[]{:S(2)}, u32[]{:S(2)}) collective-permute-start(bf16[192,1024]{1,0:T(8,128)(2,1)S(1)} %get-tuple-element.68), channel_id=1, source_target_pairs={{0,2},{2,0},{1,3},{3,1},{4,6},{6,4},{5,7},{7,5},{8,10},{10,8},{9,1... | collective-permute-start | bytes 1179656 | tf_op jit(solution)/shard_map/ppermute | solution.py:29
  48.9 1.4 %collective-permute-start.23 = (bf16[2,32,1024]{2,1,0:T(8,128)(2,1)S(1)}, bf16[2,32,1024]{2,1,0:T(8,128)(2,1)S(1)}, u32[]{:S(2)}, u32[]{:S(2)}) collective-permute-start(bf16[2,32,1024]{2,1,0:T(8,128)(2,1)S(1)} %get-tuple-element.73), channel_id=1, source_target_pairs={{0,1},{1,0},{2,3},{3,2},{4,5},{5,4},{6,7},{7,6},{8,9},{9,8},{10,11... | collective-permute-start | bytes 393224 | tf_op jit(solution)/shard_map/ppermute | solution.py:29
  49.1 1.5 %collective-permute-start.24 = (bf16[2,32,1024]{2,1,0:T(8,128)(2,1)S(1)}, bf16[2,32,1024]{2,1,0:T(8,128)(2,1)S(1)}, u32[]{:S(2)}, u32[]{:S(2)}) collective-permute-start(bf16[2,32,1024]{2,1,0:T(8,128)(2,1)S(1)} %get-tuple-element.74), channel_id=1, source_target_pairs={{0,1},{1,0},{2,3},{3,2},{4,5},{5,4},{6,7},{7,6},{8,9},{9,8},{10,11... | collective-permute-start | bytes 393224 | tf_op jit(solution)/shard_map/ppermute | solution.py:29
  51.2 9.1 %collective-permute-start.25 = (bf16[64,1024]{1,0:T(8,128)(2,1)S(1)}, bf16[64,1024]{1,0:T(8,128)(2,1)S(1)}, u32[]{:S(2)}, u32[]{:S(2)}) collective-permute-start(bf16[64,1024]{1,0:T(8,128)(2,1)S(1)} %get-tuple-element.76), channel_id=1, source_target_pairs={{0,2},{2,0},{1,3},{3,1},{4,6},{6,4},{5,7},{7,5},{8,10},{10,8},{9,1... | collective-permute-start | bytes 393224 | tf_op jit(solution)/shard_map/ppermute | solution.py:29
  58.3 4.5 %collective-permute-start.21 = (f32[8,256]{1,0:T(8,128)S(1)}, f32[8,256]{1,0:T(8,128)S(1)}, u32[]{:S(2)}, u32[]{:S(2)}) collective-permute-start(f32[8,256]{1,0:T(8,128)S(1)} %get-tuple-element.69.refs_0_), channel_id=1, source_target_pairs={{0,3},{1,2},{2,1},{3,0},{4,7},{5,6},{6,5},{7,4},{8,11},{9,10},{10,... | collective-permute-start | bytes 24584 | tf_op jit(solution)/shard_map/ppermute | solution.py:29
  58.4 4.4 %collective-permute-start.20 = (f32[8,256]{1,0:T(8,128)S(1)}, f32[8,256]{1,0:T(8,128)S(1)}, u32[]{:S(2)}, u32[]{:S(2)}) collective-permute-start(f32[8,256]{1,0:T(8,128)S(1)} %get-tuple-element.69.refs_0_), channel_id=1, source_target_pairs={{0,2},{1,3},{2,0},{3,1},{4,6},{5,7},{6,4},{7,5},{8,10},{9,11},{10,... | collective-permute-start | bytes 24584 | tf_op jit(solution)/shard_map/ppermute | solution.py:29
  59.9 2.9 %collective-permute-start.19 = (f32[8,256]{1,0:T(8,128)S(1)}, f32[8,256]{1,0:T(8,128)S(1)}, u32[]{:S(2)}, u32[]{:S(2)}) collective-permute-start(f32[8,256]{1,0:T(8,128)S(1)} %get-tuple-element.69.refs_0_), channel_id=1, source_target_pairs={{0,1},{1,0},{2,3},{3,2},{4,5},{5,4},{6,7},{7,6},{8,9},{9,8},{10,11... | collective-permute-start | bytes 24584 | tf_op jit(solution)/shard_map/ppermute | solution.py:29
  61.0 3.1 %collective-permute-start.28 = (f32[8,128]{1,0:T(8,128)S(1)}, f32[8,128]{1,0:T(8,128)S(1)}, u32[]{:S(2)}, u32[]{:S(2)}) collective-permute-start(f32[8,128]{1,0:T(8,128)S(1)} %get-tuple-element.77.refs_5_.refs_0_), channel_id=1, source_target_pairs={{0,3},{1,2},{2,1},{3,0},{4,7},{5,6},{6,5},{7,4},{8,11},{9,10},{10,... | collective-permute-start | bytes 12296 | tf_op jit(solution)/shard_map/ppermute | solution.py:29
  62.0 3.6 %collective-permute-start.27 = (f32[8,128]{1,0:T(8,128)S(1)}, f32[8,128]{1,0:T(8,128)S(1)}, u32[]{:S(2)}, u32[]{:S(2)}) collective-permute-start(f32[8,128]{1,0:T(8,128)S(1)} %get-tuple-element.77.refs_5_.refs_0_), channel_id=1, source_target_pairs={{0,2},{1,3},{2,0},{3,1},{4,6},{5,7},{6,4},{7,5},{8,10},{9,11},{10,... | collective-permute-start | bytes 12296 | tf_op jit(solution)/shard_map/ppermute | solution.py:29
  62.8 2.9 %collective-permute-start.26 = (f32[8,128]{1,0:T(8,128)S(1)}, f32[8,128]{1,0:T(8,128)S(1)}, u32[]{:S(2)}, u32[]{:S(2)}) collective-permute-start(f32[8,128]{1,0:T(8,128)S(1)} %get-tuple-element.77.refs_5_.refs_0_), channel_id=1, source_target_pairs={{0,1},{1,0},{2,3},{3,2},{4,5},{5,4},{6,7},{7,6},{8,9},{9,8},{10,11... | collective-permute-start | bytes 12296 | tf_op jit(solution)/shard_map/ppermute | solution.py:29
  63.8 8.3 %collective-permute-start.29 = (bf16[64,1024]{1,0:T(8,128)(2,1)S(1)}, bf16[64,1024]{1,0:T(8,128)(2,1)S(1)}, u32[]{:S(2)}, u32[]{:S(2)}) collective-permute-start(bf16[64,1024]{1,0:T(8,128)(2,1)S(1)} %get-tuple-element.79), channel_id=1, source_target_pairs={{0,12},{4,8},{8,4},{12,0},{1,13},{5,9},{9,5},{13,1},{2,14},{6,10},... | collective-permute-start | bytes 393224 | tf_op jit(solution)/shard_map/ppermute | solution.py:29
  63.8 11.4 %collective-permute-start.30 = (bf16[64,1024]{1,0:T(8,128)(2,1)S(1)}, bf16[64,1024]{1,0:T(8,128)(2,1)S(1)}, u32[]{:S(2)}, u32[]{:S(2)}) collective-permute-start(bf16[64,1024]{1,0:T(8,128)(2,1)S(1)} %get-tuple-element.80), channel_id=1, source_target_pairs={{0,4},{4,0},{8,12},{12,8},{1,5},{5,1},{9,13},{13,9},{2,6},{6,2},{1... | collective-permute-start | bytes 393224 | tf_op jit(solution)/shard_map/ppermute | solution.py:29
  66.4 11.0 %collective-permute-start.31 = (bf16[64,1024]{1,0:T(8,128)(2,1)S(1)}, bf16[64,1024]{1,0:T(8,128)(2,1)S(1)}, u32[]{:S(2)}, u32[]{:S(2)}) collective-permute-start(bf16[64,1024]{1,0:T(8,128)(2,1)S(1)} %gradient.3), channel_id=1, source_target_pairs={{0,8},{4,12},{8,0},{12,4},{1,9},{5,13},{9,1},{13,5},{2,10},{6,14},... | collective-permute-start | bytes 393224 | tf_op jit(solution)/shard_map/ppermute | solution.py:29
  (6 other events, 42.0 us)

commit v9 on v7

--- a/solution.py
+++ b/solution.py
@@ -20,6 +20,7 @@
 VMEM = pl.BlockSpec(memory_space=pltpu.VMEM)
 SMEM = pl.BlockSpec(memory_space=pltpu.SMEM)
 HBM = pl.BlockSpec(memory_space=pltpu.HBM)
+ANY = pl.BlockSpec(memory_space=pl.ANY)
 
 
 def swapped(value, axis, size, step):
@@ -160,45 +161,82 @@
     return (lax.broadcasted_iota(jnp.int32, (channels, row.shape[1]), 0) == row).astype(BF16)
 
 
-def rows_kernel(used, sends, messages, scal, after, here, *refs):
+def rows_kernel(half, used, sends, messages, ahead, scal, after, here, *refs):
     held, refs = refs[:used], refs[used:]
     perm, src_ids, rec_ids, refs = refs[0], refs[1 : 1 + sends], refs[1 + sends], refs[2 + sends :]
-    outs, own_out = refs[:-1], refs[-1]
-    units, _, _, slots, part = own_out.shape
+    if half:
+        early, outs, own_out = refs[: len(messages)], refs[len(messages) : -1], refs[-1]
+    else:
+        first_out, outs, own_out = refs[: sum(h > 0 for h in ahead)], refs[: -1], refs[-1]
+        outs = outs[len(first_out) :]
+    units, _, slots, part = own_out.shape
     channels = here.shape[2]
     pick = picks(list(src_ids) + [rec_ids.at[d : d + 1] for d in range(units)], channels)
     for u in range(used):
-        for half in range(2):
-            x = here[0, half]
-            for s in range(used):
-                x = jnp.where(scal[ORDER + u] == s + 1, held[s][0, half], x)
-            x = jnp.dot(x, perm[...], preferred_element_type=F32).astype(BF16)
-            y = lax.dot_general(
-                pick, x, (((0,), (0,)), ((), ())), preferred_element_type=F32
-            ).astype(BF16)
-            for (d, first, count), out in zip(messages, outs):
-                at = d * slots + first
-                out[u, half] = y[at : at + count]
-            for d in range(units):
-                at = (sends + d) * slots
-                own_out[d, u, half] = y[at : at + slots]
-
-
-def gather_rows(scal, after, here, held, perm, src_ids, rec_ids, messages):
+        x = here[0, 0]
+        for s in range(used):
+            x = jnp.where(scal[ORDER + u] == s + 1, held[s][0, 0], x)
+        x = jnp.dot(x, perm[...], preferred_element_type=F32).astype(BF16)
+        y = lax.dot_general(
+            pick, x, (((0,), (0,)), ((), ())), preferred_element_type=F32
+        ).astype(BF16)
+        taken = 0
+        for i, ((d, first, count), h) in enumerate(zip(messages, ahead)):
+            at = d * slots + first
+            if half and h:
+                outs[i][u, : count - h] = early[i][u]
+                outs[i][u, count - h :] = y[at : at + count]
+            elif half:
+                outs[i][u, 0] = early[i][u]
+                outs[i][u, 1] = y[at : at + count]
+            else:
+                if h:
+                    first_out[taken][u] = y[at : at + h]
+                    taken += 1
+                outs[i][u] = y[at + h : at + count]
+        for d in range(units):
+            at = (sends + d) * slots
+            own_out[d, u] = y[at : at + slots]
+
+
+def gather_rows(half, scal, after, here, held, perm, src_ids, rec_ids, messages, ahead, early):
     used, sends = len(held), len(src_ids)
     part = held[0].shape[-1]
     units, slots = rec_ids.shape
-    *sent, own = pl.pallas_call(
-        functools.partial(rows_kernel, used, sends, messages),
-        out_shape=[jax.ShapeDtypeStruct((used, 2, m[2], part), BF16) for m in messages]
-        + [jax.ShapeDtypeStruct((units, used, 2, slots, part), BF16)],
-        in_specs=[SMEM, pl.BlockSpec(memory_space=pl.ANY)] + [VMEM] * (used + 3 + sends),
-        out_specs=[VMEM] * (len(messages) + 1),
+    if half:
+        shapes = [
+            (used, 2 * m[2] - h, part) if h else (used, 2, m[2], part)
+            for m, h in zip(messages, ahead)
+        ]
+    else:
+        shapes = [(used, h, part) for h in ahead if h]
+        shapes += [(used, m[2] - h, part) for m, h in zip(messages, ahead)]
+    shapes.append((units, used, slots, part))
+    return pl.pallas_call(
+        functools.partial(rows_kernel, half, used, sends, messages, ahead),
+        out_shape=[jax.ShapeDtypeStruct(x, BF16) for x in shapes],
+        in_specs=[SMEM, ANY] + [VMEM] * (used + 3 + sends + len(early)),
+        out_specs=[VMEM] * len(shapes),
         compiler_params=params(16),
         cost_estimate=SMALL,
         name="rows",
-    )(scal, after, here, *held, perm, *src_ids, rec_ids)
-    return sent, own
+    )(scal, after, here, *held, perm, *src_ids, rec_ids, *early)
+
+
+def token_kernel(*refs):
+    refs[-1][...] = jnp.zeros(refs[-1].shape, F32)
+
+
+def token(values):
+    return pl.pallas_call(
+        token_kernel,
+        out_shape=jax.ShapeDtypeStruct((8, LANES), F32),
+        in_specs=[ANY] * len(values),
+        out_specs=VMEM,
+        compiler_params=params(4),
+        cost_estimate=LARGE,
+        name="token",
+    )(*values)
 
 
 def combine(values, classes, outputs, origin, span, period):
@@ -234,21 +272,32 @@
         at += count
 
 
-def cross_kernel(pieces, skip, weight, *refs):
-    refs = refs[skip:]
-    s_refs, own, lhs = refs[:-2], refs[-2], refs[-1]
-    used = own.shape[1]
+def cross_kernel(pieces, ahead, skip, weight, *refs):
+    *refs, own_real, own_imag, lhs = refs[skip:]
+    used = own_real.shape[1]
     rows = lhs.shape[1] // 2
-    for s_ref, (unit, first, count, at) in zip(s_refs, placed(pieces)):
-        turned = slice(rows + at.start, rows + at.stop)
+    steps = []
+    for (unit, first, count, at), h in zip(placed(pieces), ahead):
+        ref = refs.pop(0)
+        if h:
+            more = refs.pop(0)
+            steps.append((unit, 0, h, at.start, ref, 0, more, count - h))
+            steps.append((unit, h, count - h, at.start + h, more, 0, more, count))
+        elif ref.shape[2] > count:
+            steps.append((unit, first, count, at.start, ref.at[:, 0], first, ref.at[:, 1], first))
+        else:
+            steps.append((unit, first, count, at.start, ref.at[:, 0], 0, ref.at[:, 1], 0))
+    for unit, first, count, at, real_ref, real_at, imag_ref, imag_at in steps:
+        turned = slice(rows + at, rows + at + count)
+        at = slice(at, at + count)
         mine = slice(first, first + count)
-        sent = mine if s_ref.shape[2] > count else slice(0, count)
         for r in range(lhs.shape[0]):
             bins = slice(r * LANES, (r + 1) * LANES)
             real = imag = None
             for u in range(used):
-                sr, si = (s_ref[u, half, sent, bins].astype(F32) for half in range(2))
-                rr, ri = (own[unit, u, half, mine, bins].astype(F32) for half in range(2))
+                sr = real_ref[u, real_at : real_at + count, bins].astype(F32)
+                si = imag_ref[u, imag_at : imag_at + count, bins].astype(F32)
+                rr, ri = (o[unit, u, mine, bins].astype(F32) for o in (own_real, own_imag))
                 re, im = sr * rr + si * ri, si * rr - sr * ri
                 if u:
                     re, im = real + weight[u] * re, imag + weight[u] * im
@@ -259,17 +308,17 @@
             lhs[r, turned, LANES:] = (-real).astype(BF16)
 
 
-def cross_rows(weight, after, rows, own, pieces, classes):
+def cross_rows(weight, after, rows, own, pieces, ahead, classes):
     count = sum(p[2] for p in pieces)
     return pl.pallas_call(
-        functools.partial(cross_kernel, pieces, len(after)),
+        functools.partial(cross_kernel, pieces, ahead, len(after)),
         out_shape=jax.ShapeDtypeStruct((classes, 2 * count, 2 * LANES), BF16),
-        in_specs=[SMEM] + [pl.BlockSpec(memory_space=pl.ANY)] * len(after) + [VMEM] * (len(rows) + 1),
+        in_specs=[SMEM] + [ANY] * len(after) + [VMEM] * (len(rows) + 2),
         out_specs=VMEM,
-        compiler_params=params(8),
+        compiler_params=params(16),
         cost_estimate=LARGE,
         name="cross",
-    )(weight, *after, *rows, own)
+    )(weight, *after, *rows, *own)
 
 
 def lags_kernel(geometry, skip, scal, *refs):
@@ -301,7 +350,7 @@
         functools.partial(lags_kernel, geometry, len(after)),
         out_shape=[jax.ShapeDtypeStruct(shape(rows), F32)]
         + [jax.ShapeDtypeStruct(shape(rows // split), BF16)] * split,
-        in_specs=[SMEM] + [pl.BlockSpec(memory_space=pl.ANY)] * len(after) + [VMEM] * 2,
+        in_specs=[SMEM] + [ANY] * len(after) + [VMEM] * 2,
         out_specs=[VMEM] * (split + 1),
         scratch_shapes=[pltpu.VMEM((2 * columns, rows, lag_dev), F32)],
         compiler_params=params(16),
@@ -336,7 +385,7 @@
         functools.partial(cores_kernel, len(after), len(more)),
         out_shape=[jax.ShapeDtypeStruct((rows, lag_dev), F32)]
         + [jax.ShapeDtypeStruct((rows, lag_dev), BF16)] * (columns - 1),
-        in_specs=[SMEM] + [pl.BlockSpec(memory_space=pl.ANY)] * len(after) + [VMEM] * (1 + len(more)),
+        in_specs=[SMEM] + [ANY] * len(after) + [VMEM] * (1 + len(more)),
         out_specs=[VMEM] * columns,
         compiler_params=params(8),
         cost_estimate=SMALL,
@@ -506,15 +555,18 @@
     some = slots // 2
     shifts = range(places)
 
-    held = [
-        swapped(
-            lax.dynamic_slice(
-                spectra, (0, 0, 0, (column ^ s) * part), (1, 2, channels, part)
-            ),
-            "win",
-            columns,
-            s,
-        )
+    here, *held = [
+        [
+            swapped(
+                lax.dynamic_slice(
+                    spectra, (0, half, 0, (column ^ s) * part), (1, 1, channels, part)
+                ),
+                "win",
+                columns,
+                s,
+            )
+            for half in range(2)
+        ]
         for s in range(columns)
     ]
     scal, wanted, rec_ids = index(
@@ -543,21 +595,44 @@
         messages = [piece for pieces in chunks for piece in pieces]
     else:
         messages = [(d, 0, slots) for d in shifts]
-    sent, own_rows = gather_rows(
-        scal, table, held[0], held[1:], make_perm(part), src_ids, rec_ids, messages
+    ahead = [some // 2 if direct and m[0] > 1 else 0 for m in messages]
+    perm = make_perm(part)
+    *early, own_real = gather_rows(
+        0, scal, scal, here[0], [h[0] for h in held], perm, src_ids, rec_ids, messages, ahead, []
+    )
+    sent_first = early[: -len(messages)]
+    sent_first = [
+        swapped(x, "recv", places, m[0])
+        for x, m in zip(sent_first, [m for m, h in zip(messages, ahead) if h])
+    ]
+    *sent, own_imag = gather_rows(
+        1,
+        scal,
+        table,
+        here[1],
+        [h[1] for h in held],
+        perm,
+        src_ids,
+        rec_ids,
+        messages,
+        ahead,
+        early[-len(messages) :],
     )
     arrived = [swapped(x, "recv", places, m[0]) for m, x in zip(messages, sent)]
+    after = [token(sent_first)] if sent_first else []
+    arrived = [[sent_first.pop(0), x] if h else [x] for x, h in zip(arrived, ahead)]
     if not direct:
-        stacked = jnp.stack(arrived)
+        stacked = jnp.stack([x for (x,) in arrived])
         whole_rows = [
             lax.dynamic_index_in_dim(stacked, place ^ owners[b], 0, False) for b in range(blocks)
         ]
-        arrived = [whole_rows[piece[0]] for pieces in chunks for piece in pieces]
+        arrived = [[whole_rows[piece[0]]] for pieces in chunks for piece in pieces]
+        ahead = [0] * len(arrived)
     corrs, all_sums, returned, returned_pieces = [], [], [], []
-    after = []
     for q, pieces in enumerate(chunks):
-        rows = arrived[len(pieces) * q : len(pieces) * (q + 1)]
-        lhs = cross_rows(weight, after[:1], rows, own_rows, pieces, classes)
+        rows, arrived = [x for a in arrived[: len(pieces)] for x in a], arrived[len(pieces) :]
+        fore, ahead = ahead[: len(pieces)], ahead[len(pieces) :]
+        lhs = cross_rows(weight, after[:1], rows, (own_real, own_imag), pieces, fore, classes)
         keep, *sends = lag_parts(
             scal, [], lhs, table, geometry, columns, lag_dev, SPLIT if q else 2 * SPLIT, SMALL if q else LARGE
         )

time: 78.8 us -> 81.5 us (1.034)
  waiting for transfers between devices: 25.6 us -> 27.1 us
    ppermute x30 -> x33, waiting for transfers between devices: 25.6 us -> 27.1 us  [swapped(): return lax.ppermute(value, axis, [(i, i ^ step) for i in range(size)])]
    pallas_call x3 -> x5, Pallas kernels: 2.36 us -> 3.08 us  [the longest x2 2.55 us: gather_rows(): pl.pallas_call(functools.partial(rows_kernel, half, used, sends, messages...]
    ppermute x30 -> x33, starting transfers between devices: 27.8 us -> 28.4 us  [swapped(): return lax.ppermute(value, axis, [(i, i ^ step) for i in range(size)])]
  transfers between devices with their start and end apart: 30 -> 33, of which waited for: 14 -> 15; matrix products, arithmetic and copies ran while one was open for 0% -> 0% of each run, Pallas kernels for 20% -> 23%
where the time goes in v9:
time: 81.5 us; the launch traced here: 81.3 us
  starting transfers between devices  28.4 us (35%)
  waiting for transfers between devices  27.1 us (33%)
  Pallas kernels  20.4 us (25%)
  local copies, waits for them, and re-layouts  3.99 us (5%)
  between operations  1.5 us (2%)
    ppermute x33, starting transfers between devices, swapped(): return lax.ppermute(value, axis, [(i, i ^ step) for i in range(size)])  28.4 us
    ppermute x33, waiting for transfers between devices, swapped(): return lax.ppermute(value, axis, [(i, i ^ step) for i in range(size)])  27.1 us
    pallas_call x2, Pallas kernels, lag_parts(): pl.pallas_call(functools.partial(lags_kernel, geometry, len(after)), out_...  5 us
    pallas_call x1, Pallas kernels, normed_rows(): pl.pallas_call(functools.partial(normed_kernel, lag_total, chunks, len(su...  2.96 us
    unnamed x12, local copies, waits for them, and re-layouts  2.68 us
    pallas_call x2, Pallas kernels, gather_rows(): pl.pallas_call(functools.partial(rows_kernel, half, used, sends, messages...  2.55 us
    pallas_call x1, Pallas kernels, make_table(): pl.pallas_call(functools.partial(table_kernel, classes, parts), out_shape...  1.77 us
  transfers between devices with their start and end apart: 33, of which 15 were waited for; matrix products, arithmetic and copies ran while one was open for 0% of the time, Pallas kernels for 23%

profile of v9, /device:TPU:0, one launch (start us, length us, event | category | flops | bytes accessed | tf_op | source)
XLA Modules:
  0.0 81.3 jit_solution(8160873201334269220)
XLA Ops:
  0.7 1.3 %constant_dynamic-slice_fusion = (bf16[1,1,128,1024]{3,2,1,0:T(8,128)(2,1)S(1)}, bf16[1,1,128,1024]{3,2,1,0:T(8,128)(2,1)S(1)}, bf16[1,1,128,1024]{3,2,1,0:T(8,128)(2,1)S(1)}, bf16[1,1,128,1024]{3,2,1,0:T(8,128)(2,1)S(1)}) fusion(bf16[1,2,128,2048]{3,2,1,0:T(8,128)(2,1)} %param.8, s32[]{:T(128)S(6)} %select_n.9, s32[]{:T(128)S(6)} %select_n.8), kind=kLoop, calls=%fused_computation | loop fusion | bytes 2097160 | tf_op jit(solution)/shard_map/dynamic_slice | solution.py:561
  2.0 3.0 %collective-permute-start = (bf16[1,1,128,1024]{3,2,1,0:T(8,128)(2,1)S(1)}, bf16[1,1,128,1024]{3,2,1,0:T(8,128)(2,1)S(1)}, u32[]{:S(2)}, u32[]{:S(2)}) collective-permute-start(bf16[1,1,128,1024]{3,2,1,0:T(8,128)(2,1)S(1)} %get-tuple-element.91), channel_id=1, source_target_pairs={{0,2},{2,0},{1,3},{3,1},{4,6},{6,4},{5,7},{7,5},{8,10},{10,8},{9,1... | collective-permute-start | bytes 786440 | tf_op jit(solution)/shard_map/ppermute | solution.py:30
  8.4 1.2 %index.1 = (s32[128]{0:T(128)S(1)}, s32[1,64]{1,0:T(1,128)S(1)}, s32[1,64]{1,0:T(1,128)S(1)}, s32[1,64]{1,0:T(1,128)S(1)}, s32[1,64]{1,0:T(1,128)S(1)}, /*index=5*/s32[4,64]{1,0:T(4,128)S(1)}) custom-call(s32[1]{0:T(128)S(6)} %copy.10.refs_0_, s32[4]{0:T(128)S(1)} %copy-done.4, s32[4]{0:T(128)S(1)} %bitcast.1, s32[4,64]{1,0:T(4,128)S(1)} %copy-done.2, ...), custom_call_target="tpu_custom_call" | custom-call | flops 1 | bytes 1 | tf_op jit(solution)/shard_map/index/pallas_call | solution.py:93
  9.6 2.1 %collective-permute-start.1 = (s32[1,64]{1,0:T(1,128)S(1)}, s32[1,64]{1,0:T(1,128)S(1)}, u32[]{:S(2)}, u32[]{:S(2)}) collective-permute-start(s32[1,64]{1,0:T(1,128)S(1)} %get-tuple-element.48), channel_id=1, source_target_pairs={{0,4},{4,0},{8,12},{12,8},{1,5},{5,1},{9,13},{13,9},{2,6},{6,2},{1... | collective-permute-start | bytes 776 | tf_op jit(solution)/shard_map/ppermute | solution.py:30
  11.7 2.6 %collective-permute-start.2 = (s32[1,64]{1,0:T(1,128)S(1)}, s32[1,64]{1,0:T(1,128)S(1)}, u32[]{:S(2)}, u32[]{:S(2)}) collective-permute-start(s32[1,64]{1,0:T(1,128)S(1)} %get-tuple-element.49), channel_id=1, source_target_pairs={{0,8},{4,12},{8,0},{12,4},{1,9},{5,13},{9,1},{13,5},{2,10},{6,14},... | collective-permute-start | bytes 776 | tf_op jit(solution)/shard_map/ppermute | solution.py:30
  14.9 1.2 %collective-permute-done.2.refs_4_.refs_2_ = s32[1,64]{1,0:T(1,128)S(1)} collective-permute-done((s32[1,64]{1,0:T(1,128)S(1)}, s32[1,64]{1,0:T(1,128)S(1)}, u32[]{:S(2)}, u32[]{:S(2)}) %collective-permute-start.2) | collective-permute-done | bytes 288 | tf_op jit(solution)/shard_map/ppermute | solution.py:30
  16.1 3.5 %collective-permute-done.3.refs_5_.refs_3_ = s32[1,64]{1,0:T(1,128)S(1)} collective-permute-done((s32[1,64]{1,0:T(1,128)S(1)}, s32[1,64]{1,0:T(1,128)S(1)}, u32[]{:S(2)}, u32[]{:S(2)}) %collective-permute-start.3) | collective-permute-done | bytes 288 | tf_op jit(solution)/shard_map/ppermute | solution.py:30
  19.6 1.3 %rows.2 = (bf16[1,16,1024]{2,1,0:T(8,128)(2,1)S(1)}, bf16[1,16,1024]{2,1,0:T(8,128)(2,1)S(1)}, bf16[1,64,1024]{2,1,0:T(8,128)(2,1)S(1)}, bf16[1,64,1024]{2,1,0:T...) custom-call(s32[128]{0:T(128)S(1)} %get-tuple-element.46.scal.after,, ...), custom_call_target="tpu_custom_call" | custom-call | flops 1 | bytes 1 | tf_op jit(solution)/shard_map/rows/pallas_call | solution.py:215
  21.0 1.0 %collective-permute-start.5 = (bf16[1,16,1024]{2,1,0:T(8,128)(2,1)S(1)}, bf16[1,16,1024]{2,1,0:T(8,128)(2,1)S(1)}, u32[]{:S(2)}, u32[]{:S(2)}) collective-permute-start(bf16[1,16,1024]{2,1,0:T(8,128)(2,1)S(1)} %get-tuple-element.53), channel_id=1, source_target_pairs={{0,12},{4,8},{8,4},{12,0},{1,13},{5,9},{9,5},{13,1},{2,14},{6,10},... | collective-permute-start | bytes 98312 | tf_op jit(solution)/shard_map/ppermute | solution.py:30
  22.0 1.8 %table.1.after.refs_1_ = bf16[8,256,1024]{2,1,0:T(8,128)(2,1)S(1)} custom-call(s32[128]{0:T(128)S(1)} %get-tuple-element.46.scal.after, f32[2,56,1024]{2,1,0:T(8,128)S(1)} %copy-done.1), custom_call_target="tpu_custom_call" | custom-call | flops 1 | bytes 1 | tf_op jit(solution)/shard_map/table/pallas_call | solution.py:127
  23.8 1.3 %rows.3 = (bf16[1,2,64,1024]{3,2,1,0:T(8,128)(2,1)S(1)}, bf16[1,2,64,1024]{3,2,1,0:T(8,128)(2,1)S(1)}, bf16[1,112,1024]{2,1,0:T(8,128)(2,1)S(1)}, bf16[1,112,102...) custom-call(s32[128]{0:T(128)S(1)} %get-tuple-element.46.scal.after, bf16[8,256,1024]{2,1,0:T(8,128)(2,1)S(1)} %table.1.after.refs_1_, ...), custom_call_target="tpu_custom_call" | custom-call | flops 1 | bytes 1 | tf_op jit(solution)/shard_map/rows/pallas_call | solution.py:215
  25.1 2.6 %collective-permute-start.7 = (bf16[1,2,64,1024]{3,2,1,0:T(8,128)(2,1)S(1)}, bf16[1,2,64,1024]{3,2,1,0:T(8,128)(2,1)S(1)}, u32[]{:S(2)}, u32[]{:S(2)}) collective-permute-start(bf16[1,2,64,1024]{3,2,1,0:T(8,128)(2,1)S(1)} %get-tuple-element.59), channel_id=1, source_target_pairs={{0,4},{4,0},{8,12},{12,8},{1,5},{5,1},{9,13},{13,9},{2,6},{6,2},{1... | collective-permute-start | bytes 786440 | tf_op jit(solution)/shard_map/ppermute | solution.py:30
  27.6 1.0 %collective-permute-start.20 = (bf16[1,112,1024]{2,1,0:T(8,128)(2,1)S(1)}, bf16[1,112,1024]{2,1,0:T(8,128)(2,1)S(1)}, u32[]{:S(2)}, u32[]{:S(2)}) collective-permute-start(bf16[1,112,1024]{2,1,0:T(8,128)(2,1)S(1)} %get-tuple-element.75), channel_id=1, source_target_pairs={{0,8},{4,12},{8,0},{12,4},{1,9},{5,13},{9,1},{13,5},{2,10},{6,14},... | collective-permute-start | bytes 688136 | tf_op jit(solution)/shard_map/ppermute | solution.py:30
  28.6 1.5 %collective-permute-start.21 = (bf16[1,112,1024]{2,1,0:T(8,128)(2,1)S(1)}, bf16[1,112,1024]{2,1,0:T(8,128)(2,1)S(1)}, u32[]{:S(2)}, u32[]{:S(2)}) collective-permute-start(bf16[1,112,1024]{2,1,0:T(8,128)(2,1)S(1)} %get-tuple-element.76), channel_id=1, source_target_pairs={{0,12},{4,8},{8,4},{12,0},{1,13},{5,9},{9,5},{13,1},{2,14},{6,10},... | collective-permute-start | bytes 688136 | tf_op jit(solution)/shard_map/ppermute | solution.py:30
  30.1 6.3 %collective-permute-done.7.refs_2_ = bf16[1,2,64,1024]{3,2,1,0:T(8,128)(2,1)S(1)} collective-permute-done((bf16[1,2,64,1024]{3,2,1,0:T(8,128)(2,1)S(1)}, bf16[1,2,64,1024]{3,2,1,0:T(8,128)(2,1)S(1)}, u32[]{:S(2)}, u32[]{:S(2)}) %collective-permute-start.7) | collective-permute-done | bytes 262176 | tf_op jit(solution)/shard_map/ppermute | solution.py:30
  36.6 2.5 %lags.2 = (f32[2,128,1024]{2,1,0:T(8,128)S(1)}, bf16[2,16,1024]{2,1,0:T(8,128)(2,1)S(1)}, bf16[2,16,1024]{2,1,0:T(8,128)(2,1)S(1)}, bf16[2,16,1024]{2,1,0:T(8,12...) custom-call(s32[128]{0:T(128)S(1)} %get-tuple-element.46.scal.after,, ...), custom_call_target="tpu_custom_call" | custom-call | flops 20000000000 | bytes 1048576 | tf_op jit(solution)/shard_map/lags/pallas_call | solution.py:349
  43.2 0.8 cores.2
  44.0 1.5 %collective-permute-start.16 = (bf16[128,1024]{1,0:T(8,128)(2,1)S(1)}, bf16[128,1024]{1,0:T(8,128)(2,1)S(1)}, u32[]{:S(2)}, u32[]{:S(2)}) collective-permute-start(bf16[128,1024]{1,0:T(8,128)(2,1)S(1)} %get-tuple-element.72), channel_id=1, source_target_pairs={{0,2},{2,0},{1,3},{3,1},{4,6},{6,4},{5,7},{7,5},{8,10},{10,8},{9,1... | collective-permute-start | bytes 786440 | tf_op jit(solution)/shard_map/ppermute | solution.py:30
  45.8 2.5 %lags.3 = (f32[2,128,1024]{2,1,0:T(8,128)S(1)}, bf16[2,32,1024]{2,1,0:T(8,128)(2,1)S(1)}, bf16[2,32,1024]{2,1,0:T(8,128)(2,1)S(1)}, bf16[2,32,1024]{2,1,0:T(8,128)(2,1)S(1)}, bf16[2,32,1024]{2,1,0:T(8,128)(2,1)S(1)}) custom-call(s32[128]{0:T(128)S(1)} %get-tuple-element.46.scal.after, bf16[8,256,256]{2,1,0:T(8,128)(2,1)S(1)} %cross.3.refs_0_, ...), custom_call_target="tpu_custom_call" | custom-call | flops 1 | bytes 1 | tf_op jit(solution)/shard_map/lags/pallas_call | solution.py:349
  50.4 2.2 %collective-permute-done.16.refs_1_.refs_0_ = bf16[128,1024]{1,0:T(8,128)(2,1)S(1)} collective-permute-done((bf16[128,1024]{1,0:T(8,128)(2,1)S(1)}, bf16[128,1024]{1,0:T(8,128)(2,1)S(1)}, u32[]{:S(2)}, u32[]{:S(2)}) %collective-permute-start.16) | collective-permute-done | bytes 262176 | tf_op jit(solution)/shard_map/ppermute | solution.py:30
  53.3 1.5 %collective-permute-start.26 = (bf16[128,1024]{1,0:T(8,128)(2,1)S(1)}, bf16[128,1024]{1,0:T(8,128)(2,1)S(1)}, u32[]{:S(2)}, u32[]{:S(2)}) collective-permute-start(bf16[128,1024]{1,0:T(8,128)(2,1)S(1)} %get-tuple-element.83), channel_id=1, source_target_pairs={{0,2},{2,0},{1,3},{3,1},{4,6},{6,4},{5,7},{7,5},{8,10},{10,8},{9,1... | collective-permute-start | bytes 786440 | tf_op jit(solution)/shard_map/ppermute | solution.py:30
  56.3 1.3 %collective-permute-start.19 = (f32[8,128]{1,0:T(8,128)S(1)}, f32[8,128]{1,0:T(8,128)S(1)}, u32[]{:S(2)}, u32[]{:S(2)}) collective-permute-start(f32[8,128]{1,0:T(8,128)S(1)} %get-tuple-element.73.refs_0_), channel_id=1, source_target_pairs={{0,3},{1,2},{2,1},{3,0},{4,7},{5,6},{6,5},{7,4},{8,11},{9,10},{10,... | collective-permute-start | bytes 12296 | tf_op jit(solution)/shard_map/ppermute | solution.py:30
  57.6 3.7 %collective-permute-done.26.refs_1_ = bf16[128,1024]{1,0:T(8,128)(2,1)S(1)} collective-permute-done((bf16[128,1024]{1,0:T(8,128)(2,1)S(1)}, bf16[128,1024]{1,0:T(8,128)(2,1)S(1)}, u32[]{:S(2)}, u32[]{:S(2)}) %collective-permute-start.26) | collective-permute-done | bytes 262176 | tf_op jit(solution)/shard_map/ppermute | solution.py:30
  62.1 1.5 %collective-permute-start.28 = (f32[8,128]{1,0:T(8,128)S(1)}, f32[8,128]{1,0:T(8,128)S(1)}, u32[]{:S(2)}, u32[]{:S(2)}) collective-permute-start(f32[8,128]{1,0:T(8,128)S(1)} %get-tuple-element.84.refs_5_.refs_0_), channel_id=1, source_target_pairs={{0,2},{1,3},{2,0},{3,1},{4,6},{5,7},{6,4},{7,5},{8,10},{9,11},{10,... | collective-permute-start | bytes 12296 | tf_op jit(solution)/shard_map/ppermute | solution.py:30
  63.9 0.8 gradient.2
  64.7 1.2 %collective-permute-start.30 = (bf16[64,1024]{1,0:T(8,128)(2,1)S(1)}, bf16[64,1024]{1,0:T(8,128)(2,1)S(1)}, u32[]{:S(2)}, u32[]{:S(2)}) collective-permute-start(bf16[64,1024]{1,0:T(8,128)(2,1)S(1)} %get-tuple-element.87), channel_id=1, source_target_pairs={{0,4},{4,0},{8,12},{12,8},{1,5},{5,1},{9,13},{13,9},{2,6},{6,2},{1... | collective-permute-start | bytes 393224 | tf_op jit(solution)/shard_map/ppermute | solution.py:30
  66.6 0.8 gradient.3
  67.4 1.5 %collective-permute-start.31 = (bf16[64,1024]{1,0:T(8,128)(2,1)S(1)}, bf16[64,1024]{1,0:T(8,128)(2,1)S(1)}, u32[]{:S(2)}, u32[]{:S(2)}) collective-permute-start(bf16[64,1024]{1,0:T(8,128)(2,1)S(1)} %get-tuple-element.88), channel_id=1, source_target_pairs={{0,8},{4,12},{8,0},{12,4},{1,9},{5,13},{9,1},{13,5},{2,10},{6,14},... | collective-permute-start | bytes 393224 | tf_op jit(solution)/shard_map/ppermute | solution.py:30
  68.9 2.1 %collective-permute-start.32 = (bf16[64,1024]{1,0:T(8,128)(2,1)S(1)}, bf16[64,1024]{1,0:T(8,128)(2,1)S(1)}, u32[]{:S(2)}, u32[]{:S(2)}) collective-permute-start(bf16[64,1024]{1,0:T(8,128)(2,1)S(1)} %get-tuple-element.89), channel_id=1, source_target_pairs={{0,12},{4,8},{8,4},{12,0},{1,13},{5,9},{9,5},{13,1},{2,14},{6,10},... | collective-permute-start | bytes 393224 | tf_op jit(solution)/shard_map/ppermute | solution.py:30
  71.0 3.0 %normed.1 = f32[4,64,1024]{2,1,0:T(8,128)} custom-call(s32[128]{0:T(128)S(1)} %get-tuple-element.46.scal.after, f32[8,128]{1,0:T(8,128)S(1)} %get-tuple-element.73.refs_0_, f32[8,128]{1,0:T(8,128)S(1)} %collective-permute-done.17.refs_1_, f32[8,128]{1,0:T(8,128)S(1)} %collective-permute-done.18.refs_2_, f32[8,128]{1,0:T(8,128)S(1)} %collective-permute-done.19.refs_3_, ...), custom_call_target="tpu_custom_call" | custom-call | flops 1 | bytes 1 | tf_op jit(solution)/shard_map/normed/pallas_call | solution.py:505
  74.0 6.3 %collective-permute-done.31.refs_6_ = bf16[64,1024]{1,0:T(8,128)(2,1)S(1)} collective-permute-done((bf16[64,1024]{1,0:T(8,128)(2,1)S(1)}, bf16[64,1024]{1,0:T(8,128)(2,1)S(1)}, u32[]{:S(2)}, u32[]{:S(2)}) %collective-permute-start.31) | collective-permute-done | bytes 131104 | tf_op jit(solution)/shard_map/ppermute | solution.py:30
  80.3 1.1 %adjoint.1 = f32[128,1024]{1,0:T(8,128)} custom-call(s32[1,64]{1,0:T(1,128)S(1)} %get-tuple-element.47.refs_2_.refs_0_, s32[1,64]{1,0:T(1,128)S(1)} %collective-permute-done.1.refs_3_.refs_1_, s32[1,64]{1,0:T(1,128)S(1)} %collective-permute-done.2.refs_4_.refs_2_, s32[1,64]{1,0:T(1,128)S(1)} %collective-permute-done.3.refs_5_.refs_3_, ...), custom_call_target="tpu_custom_call" | custom-call | flops 1 | bytes 1 | tf_op jit(solution)/shard_map/adjoint/pallas_call | solution.py:529
  (65 shorter events, 14.0 us)
Async XLA Ops:
  2.0 17.7 %collective-permute-start = (bf16[1,1,128,1024]{3,2,1,0:T(8,128)(2,1)S(1)}, bf16[1,1,128,1024]{3,2,1,0:T(8,128)(2,1)S(1)}, u32[]{:S(2)}, u32[]{:S(2)}) collective-permute-start(bf16[1,1,128,1024]{3,2,1,0:T(8,128)(2,1)S(1)} %get-tuple-element.91), channel_id=1, source_target_pairs={{0,2},{2,0},{1,3},{3,1},{4,6},{6,4},{5,7},{7,5},{8,10},{10,8},{9,1... | collective-permute-start | bytes 786440 | tf_op jit(solution)/shard_map/ppermute | solution.py:30
  5.0 18.8 %collective-permute-start.6 = (bf16[1,1,128,1024]{3,2,1,0:T(8,128)(2,1)S(1)}, bf16[1,1,128,1024]{3,2,1,0:T(8,128)(2,1)S(1)}, u32[]{:S(2)}, u32[]{:S(2)}) collective-permute-start(bf16[1,1,128,1024]{3,2,1,0:T(8,128)(2,1)S(1)} %get-tuple-element.90), channel_id=1, source_target_pairs={{0,2},{2,0},{1,3},{3,1},{4,6},{6,4},{5,7},{7,5},{8,10},{10,8},{9,1... | collective-permute-start | bytes 786440 | tf_op jit(solution)/shard_map/ppermute | solution.py:30
  9.6 5.3 %collective-permute-start.1 = (s32[1,64]{1,0:T(1,128)S(1)}, s32[1,64]{1,0:T(1,128)S(1)}, u32[]{:S(2)}, u32[]{:S(2)}) collective-permute-start(s32[1,64]{1,0:T(1,128)S(1)} %get-tuple-element.48), channel_id=1, source_target_pairs={{0,4},{4,0},{8,12},{12,8},{1,5},{5,1},{9,13},{13,9},{2,6},{6,2},{1... | collective-permute-start | bytes 776 | tf_op jit(solution)/shard_map/ppermute | solution.py:30
  11.7 4.4 %collective-permute-start.2 = (s32[1,64]{1,0:T(1,128)S(1)}, s32[1,64]{1,0:T(1,128)S(1)}, u32[]{:S(2)}, u32[]{:S(2)}) collective-permute-start(s32[1,64]{1,0:T(1,128)S(1)} %get-tuple-element.49), channel_id=1, source_target_pairs={{0,8},{4,12},{8,0},{12,4},{1,9},{5,13},{9,1},{13,5},{2,10},{6,14},... | collective-permute-start | bytes 776 | tf_op jit(solution)/shard_map/ppermute | solution.py:30
  14.3 5.3 %collective-permute-start.3 = (s32[1,64]{1,0:T(1,128)S(1)}, s32[1,64]{1,0:T(1,128)S(1)}, u32[]{:S(2)}, u32[]{:S(2)}) collective-permute-start(s32[1,64]{1,0:T(1,128)S(1)} %get-tuple-element.50), channel_id=1, source_target_pairs={{0,12},{4,8},{8,4},{12,0},{1,13},{5,9},{9,5},{13,1},{2,14},{6,10},... | collective-permute-start | bytes 776 | tf_op jit(solution)/shard_map/ppermute | solution.py:30
  20.9 9.1 %collective-permute-start.4 = (bf16[1,16,1024]{2,1,0:T(8,128)(2,1)S(1)}, bf16[1,16,1024]{2,1,0:T(8,128)(2,1)S(1)}, u32[]{:S(2)}, u32[]{:S(2)}) collective-permute-start(bf16[1,16,1024]{2,1,0:T(8,128)(2,1)S(1)} %get-tuple-element.52), channel_id=1, source_target_pairs={{0,8},{4,12},{8,0},{12,4},{1,9},{5,13},{9,1},{13,5},{2,10},{6,14},... | collective-permute-start | bytes 98312 | tf_op jit(solution)/shard_map/ppermute | solution.py:30
  21.0 9.1 %collective-permute-start.5 = (bf16[1,16,1024]{2,1,0:T(8,128)(2,1)S(1)}, bf16[1,16,1024]{2,1,0:T(8,128)(2,1)S(1)}, u32[]{:S(2)}, u32[]{:S(2)}) collective-permute-start(bf16[1,16,1024]{2,1,0:T(8,128)(2,1)S(1)} %get-tuple-element.53), channel_id=1, source_target_pairs={{0,12},{4,8},{8,4},{12,0},{1,13},{5,9},{9,5},{13,1},{2,14},{6,10},... | collective-permute-start | bytes 98312 | tf_op jit(solution)/shard_map/ppermute | solution.py:30
  25.1 11.3 %collective-permute-start.7 = (bf16[1,2,64,1024]{3,2,1,0:T(8,128)(2,1)S(1)}, bf16[1,2,64,1024]{3,2,1,0:T(8,128)(2,1)S(1)}, u32[]{:S(2)}, u32[]{:S(2)}) collective-permute-start(bf16[1,2,64,1024]{3,2,1,0:T(8,128)(2,1)S(1)} %get-tuple-element.59), channel_id=1, source_target_pairs={{0,4},{4,0},{8,12},{12,8},{1,5},{5,1},{9,13},{13,9},{2,6},{6,2},{1... | collective-permute-start | bytes 786440 | tf_op jit(solution)/shard_map/ppermute | solution.py:30
  27.6 17.9 %collective-permute-start.20 = (bf16[1,112,1024]{2,1,0:T(8,128)(2,1)S(1)}, bf16[1,112,1024]{2,1,0:T(8,128)(2,1)S(1)}, u32[]{:S(2)}, u32[]{:S(2)}) collective-permute-start(bf16[1,112,1024]{2,1,0:T(8,128)(2,1)S(1)} %get-tuple-element.75), channel_id=1, source_target_pairs={{0,8},{4,12},{8,0},{12,4},{1,9},{5,13},{9,1},{13,5},{2,10},{6,14},... | collective-permute-start | bytes 688136 | tf_op jit(solution)/shard_map/ppermute | solution.py:30
  28.6 16.9 %collective-permute-start.21 = (bf16[1,112,1024]{2,1,0:T(8,128)(2,1)S(1)}, bf16[1,112,1024]{2,1,0:T(8,128)(2,1)S(1)}, u32[]{:S(2)}, u32[]{:S(2)}) collective-permute-start(bf16[1,112,1024]{2,1,0:T(8,128)(2,1)S(1)} %get-tuple-element.76), channel_id=1, source_target_pairs={{0,12},{4,8},{8,4},{12,0},{1,13},{5,9},{9,5},{13,1},{2,14},{6,10},... | collective-permute-start | bytes 688136 | tf_op jit(solution)/shard_map/ppermute | solution.py:30
  39.2 1.3 %collective-permute-start.10 = (bf16[2,16,1024]{2,1,0:T(8,128)(2,1)S(1)}, bf16[2,16,1024]{2,1,0:T(8,128)(2,1)S(1)}, u32[]{:S(2)}, u32[]{:S(2)}) collective-permute-start(bf16[2,16,1024]{2,1,0:T(8,128)(2,1)S(1)} %get-tuple-element.65), channel_id=1, source_target_pairs={{0,1},{1,0},{2,3},{3,2},{4,5},{5,4},{6,7},{7,6},{8,9},{9,8},{10,11... | collective-permute-start | bytes 196616 | tf_op jit(solution)/shard_map/ppermute | solution.py:30
  39.2 1.4 %collective-permute-start.11 = (bf16[2,16,1024]{2,1,0:T(8,128)(2,1)S(1)}, bf16[2,16,1024]{2,1,0:T(8,128)(2,1)S(1)}, u32[]{:S(2)}, u32[]{:S(2)}) collective-permute-start(bf16[2,16,1024]{2,1,0:T(8,128)(2,1)S(1)} %get-tuple-element.66), channel_id=1, source_target_pairs={{0,1},{1,0},{2,3},{3,2},{4,5},{5,4},{6,7},{7,6},{8,9},{9,8},{10,11... | collective-permute-start | bytes 196616 | tf_op jit(solution)/shard_map/ppermute | solution.py:30
  39.7 1.3 %collective-permute-start.12 = (bf16[2,16,1024]{2,1,0:T(8,128)(2,1)S(1)}, bf16[2,16,1024]{2,1,0:T(8,128)(2,1)S(1)}, u32[]{:S(2)}, u32[]{:S(2)}) collective-permute-start(bf16[2,16,1024]{2,1,0:T(8,128)(2,1)S(1)} %get-tuple-element.67), channel_id=1, source_target_pairs={{0,1},{1,0},{2,3},{3,2},{4,5},{5,4},{6,7},{7,6},{8,9},{9,8},{10,11... | collective-permute-start | bytes 196616 | tf_op jit(solution)/shard_map/ppermute | solution.py:30
  40.5 1.3 %collective-permute-start.13 = (bf16[2,16,1024]{2,1,0:T(8,128)(2,1)S(1)}, bf16[2,16,1024]{2,1,0:T(8,128)(2,1)S(1)}, u32[]{:S(2)}, u32[]{:S(2)}) collective-permute-start(bf16[2,16,1024]{2,1,0:T(8,128)(2,1)S(1)} %get-tuple-element.68), channel_id=1, source_target_pairs={{0,1},{1,0},{2,3},{3,2},{4,5},{5,4},{6,7},{7,6},{8,9},{9,8},{10,11... | collective-permute-start | bytes 196616 | tf_op jit(solution)/shard_map/ppermute | solution.py:30
  40.6 1.3 %collective-permute-start.14 = (bf16[2,16,1024]{2,1,0:T(8,128)(2,1)S(1)}, bf16[2,16,1024]{2,1,0:T(8,128)(2,1)S(1)}, u32[]{:S(2)}, u32[]{:S(2)}) collective-permute-start(bf16[2,16,1024]{2,1,0:T(8,128)(2,1)S(1)} %get-tuple-element.69), channel_id=1, source_target_pairs={{0,1},{1,0},{2,3},{3,2},{4,5},{5,4},{6,7},{7,6},{8,9},{9,8},{10,11... | collective-permute-start | bytes 196616 | tf_op jit(solution)/shard_map/ppermute | solution.py:30
  41.0 1.3 %collective-permute-start.15 = (bf16[2,16,1024]{2,1,0:T(8,128)(2,1)S(1)}, bf16[2,16,1024]{2,1,0:T(8,128)(2,1)S(1)}, u32[]{:S(2)}, u32[]{:S(2)}) collective-permute-start(bf16[2,16,1024]{2,1,0:T(8,128)(2,1)S(1)} %get-tuple-element.70), channel_id=1, source_target_pairs={{0,1},{1,0},{2,3},{3,2},{4,5},{5,4},{6,7},{7,6},{8,9},{9,8},{10,11... | collective-permute-start | bytes 196616 | tf_op jit(solution)/shard_map/ppermute | solution.py:30
  41.7 1.3 %collective-permute-start.8 = (bf16[2,16,1024]{2,1,0:T(8,128)(2,1)S(1)}, bf16[2,16,1024]{2,1,0:T(8,128)(2,1)S(1)}, u32[]{:S(2)}, u32[]{:S(2)}) collective-permute-start(bf16[2,16,1024]{2,1,0:T(8,128)(2,1)S(1)} %get-tuple-element.63), channel_id=1, source_target_pairs={{0,1},{1,0},{2,3},{3,2},{4,5},{5,4},{6,7},{7,6},{8,9},{9,8},{10,11... | collective-permute-start | bytes 196616 | tf_op jit(solution)/shard_map/ppermute | solution.py:30
  44.0 8.6 %collective-permute-start.16 = (bf16[128,1024]{1,0:T(8,128)(2,1)S(1)}, bf16[128,1024]{1,0:T(8,128)(2,1)S(1)}, u32[]{:S(2)}, u32[]{:S(2)}) collective-permute-start(bf16[128,1024]{1,0:T(8,128)(2,1)S(1)} %get-tuple-element.72), channel_id=1, source_target_pairs={{0,2},{2,0},{1,3},{3,1},{4,6},{6,4},{5,7},{7,5},{8,10},{10,8},{9,1... | collective-permute-start | bytes 786440 | tf_op jit(solution)/shard_map/ppermute | solution.py:30
  48.3 1.4 %collective-permute-start.22 = (bf16[2,32,1024]{2,1,0:T(8,128)(2,1)S(1)}, bf16[2,32,1024]{2,1,0:T(8,128)(2,1)S(1)}, u32[]{:S(2)}, u32[]{:S(2)}) collective-permute-start(bf16[2,32,1024]{2,1,0:T(8,128)(2,1)S(1)} %get-tuple-element.78), channel_id=1, source_target_pairs={{0,1},{1,0},{2,3},{3,2},{4,5},{5,4},{6,7},{7,6},{8,9},{9,8},{10,11... | collective-permute-start | bytes 393224 | tf_op jit(solution)/shard_map/ppermute | solution.py:30
  48.4 1.5 %collective-permute-start.23 = (bf16[2,32,1024]{2,1,0:T(8,128)(2,1)S(1)}, bf16[2,32,1024]{2,1,0:T(8,128)(2,1)S(1)}, u32[]{:S(2)}, u32[]{:S(2)}) collective-permute-start(bf16[2,32,1024]{2,1,0:T(8,128)(2,1)S(1)} %get-tuple-element.79), channel_id=1, source_target_pairs={{0,1},{1,0},{2,3},{3,2},{4,5},{5,4},{6,7},{7,6},{8,9},{9,8},{10,11... | collective-permute-start | bytes 393224 | tf_op jit(solution)/shard_map/ppermute | solution.py:30
  48.9 1.3 %collective-permute-start.24 = (bf16[2,32,1024]{2,1,0:T(8,128)(2,1)S(1)}, bf16[2,32,1024]{2,1,0:T(8,128)(2,1)S(1)}, u32[]{:S(2)}, u32[]{:S(2)}) collective-permute-start(bf16[2,32,1024]{2,1,0:T(8,128)(2,1)S(1)} %get-tuple-element.80), channel_id=1, source_target_pairs={{0,1},{1,0},{2,3},{3,2},{4,5},{5,4},{6,7},{7,6},{8,9},{9,8},{10,11... | collective-permute-start | bytes 393224 | tf_op jit(solution)/shard_map/ppermute | solution.py:30
  49.0 1.5 %collective-permute-start.25 = (bf16[2,32,1024]{2,1,0:T(8,128)(2,1)S(1)}, bf16[2,32,1024]{2,1,0:T(8,128)(2,1)S(1)}, u32[]{:S(2)}, u32[]{:S(2)}) collective-permute-start(bf16[2,32,1024]{2,1,0:T(8,128)(2,1)S(1)} %get-tuple-element.81), channel_id=1, source_target_pairs={{0,1},{1,0},{2,3},{3,2},{4,5},{5,4},{6,7},{7,6},{8,9},{9,8},{10,11... | collective-permute-start | bytes 393224 | tf_op jit(solution)/shard_map/ppermute | solution.py:30
  53.3 7.9 %collective-permute-start.26 = (bf16[128,1024]{1,0:T(8,128)(2,1)S(1)}, bf16[128,1024]{1,0:T(8,128)(2,1)S(1)}, u32[]{:S(2)}, u32[]{:S(2)}) collective-permute-start(bf16[128,1024]{1,0:T(8,128)(2,1)S(1)} %get-tuple-element.83), channel_id=1, source_target_pairs={{0,2},{2,0},{1,3},{3,1},{4,6},{6,4},{5,7},{7,5},{8,10},{10,8},{9,1... | collective-permute-start | bytes 786440 | tf_op jit(solution)/shard_map/ppermute | solution.py:30
  55.6 8.0 %collective-permute-start.17 = (f32[8,128]{1,0:T(8,128)S(1)}, f32[8,128]{1,0:T(8,128)S(1)}, u32[]{:S(2)}, u32[]{:S(2)}) collective-permute-start(f32[8,128]{1,0:T(8,128)S(1)} %get-tuple-element.73.refs_0_), channel_id=1, source_target_pairs={{0,1},{1,0},{2,3},{3,2},{4,5},{5,4},{6,7},{7,6},{8,9},{9,8},{10,11... | collective-permute-start | bytes 12296 | tf_op jit(solution)/shard_map/ppermute | solution.py:30
  55.7 8.2 %collective-permute-start.18 = (f32[8,128]{1,0:T(8,128)S(1)}, f32[8,128]{1,0:T(8,128)S(1)}, u32[]{:S(2)}, u32[]{:S(2)}) collective-permute-start(f32[8,128]{1,0:T(8,128)S(1)} %get-tuple-element.73.refs_0_), channel_id=1, source_target_pairs={{0,2},{1,3},{2,0},{3,1},{4,6},{5,7},{6,4},{7,5},{8,10},{9,11},{10,... | collective-permute-start | bytes 12296 | tf_op jit(solution)/shard_map/ppermute | solution.py:30
  56.3 7.6 %collective-permute-start.19 = (f32[8,128]{1,0:T(8,128)S(1)}, f32[8,128]{1,0:T(8,128)S(1)}, u32[]{:S(2)}, u32[]{:S(2)}) collective-permute-start(f32[8,128]{1,0:T(8,128)S(1)} %get-tuple-element.73.refs_0_), channel_id=1, source_target_pairs={{0,3},{1,2},{2,1},{3,0},{4,7},{5,6},{6,5},{7,4},{8,11},{9,10},{10,... | collective-permute-start | bytes 12296 | tf_op jit(solution)/shard_map/ppermute | solution.py:30
  62.0 3.9 %collective-permute-start.27 = (f32[8,128]{1,0:T(8,128)S(1)}, f32[8,128]{1,0:T(8,128)S(1)}, u32[]{:S(2)}, u32[]{:S(2)}) collective-permute-start(f32[8,128]{1,0:T(8,128)S(1)} %get-tuple-element.84.refs_5_.refs_0_), channel_id=1, source_target_pairs={{0,1},{1,0},{2,3},{3,2},{4,5},{5,4},{6,7},{7,6},{8,9},{9,8},{10,11... | collective-permute-start | bytes 12296 | tf_op jit(solution)/shard_map/ppermute | solution.py:30
  62.1 3.9 %collective-permute-start.28 = (f32[8,128]{1,0:T(8,128)S(1)}, f32[8,128]{1,0:T(8,128)S(1)}, u32[]{:S(2)}, u32[]{:S(2)}) collective-permute-start(f32[8,128]{1,0:T(8,128)S(1)} %get-tuple-element.84.refs_5_.refs_0_), channel_id=1, source_target_pairs={{0,2},{1,3},{2,0},{3,1},{4,6},{5,7},{6,4},{7,5},{8,10},{9,11},{10,... | collective-permute-start | bytes 12296 | tf_op jit(solution)/shard_map/ppermute | solution.py:30
  63.6 3.0 %collective-permute-start.29 = (f32[8,128]{1,0:T(8,128)S(1)}, f32[8,128]{1,0:T(8,128)S(1)}, u32[]{:S(2)}, u32[]{:S(2)}) collective-permute-start(f32[8,128]{1,0:T(8,128)S(1)} %get-tuple-element.84.refs_5_.refs_0_), channel_id=1, source_target_pairs={{0,3},{1,2},{2,1},{3,0},{4,7},{5,6},{6,5},{7,4},{8,11},{9,10},{10,... | collective-permute-start | bytes 12296 | tf_op jit(solution)/shard_map/ppermute | solution.py:30
  64.7 9.2 %collective-permute-start.30 = (bf16[64,1024]{1,0:T(8,128)(2,1)S(1)}, bf16[64,1024]{1,0:T(8,128)(2,1)S(1)}, u32[]{:S(2)}, u32[]{:S(2)}) collective-permute-start(bf16[64,1024]{1,0:T(8,128)(2,1)S(1)} %get-tuple-element.87), channel_id=1, source_target_pairs={{0,4},{4,0},{8,12},{12,8},{1,5},{5,1},{9,13},{13,9},{2,6},{6,2},{1... | collective-permute-start | bytes 393224 | tf_op jit(solution)/shard_map/ppermute | solution.py:30
  67.4 12.8 %collective-permute-start.31 = (bf16[64,1024]{1,0:T(8,128)(2,1)S(1)}, bf16[64,1024]{1,0:T(8,128)(2,1)S(1)}, u32[]{:S(2)}, u32[]{:S(2)}) collective-permute-start(bf16[64,1024]{1,0:T(8,128)(2,1)S(1)} %get-tuple-element.88), channel_id=1, source_target_pairs={{0,8},{4,12},{8,0},{12,4},{1,9},{5,13},{9,1},{13,5},{2,10},{6,14},... | collective-permute-start | bytes 393224 | tf_op jit(solution)/shard_map/ppermute | solution.py:30
  68.9 11.3 %collective-permute-start.32 = (bf16[64,1024]{1,0:T(8,128)(2,1)S(1)}, bf16[64,1024]{1,0:T(8,128)(2,1)S(1)}, u32[]{:S(2)}, u32[]{:S(2)}) collective-permute-start(bf16[64,1024]{1,0:T(8,128)(2,1)S(1)} %get-tuple-element.89), channel_id=1, source_target_pairs={{0,12},{4,8},{8,4},{12,0},{1,13},{5,9},{9,5},{13,1},{2,14},{6,10},... | collective-permute-start | bytes 393224 | tf_op jit(solution)/shard_map/ppermute | solution.py:30
  (7 other events, 34.4 us)

commit v10 on v7

--- a/solution.py
+++ b/solution.py
@@ -20,6 +20,7 @@
 VMEM = pl.BlockSpec(memory_space=pltpu.VMEM)
 SMEM = pl.BlockSpec(memory_space=pltpu.SMEM)
 HBM = pl.BlockSpec(memory_space=pltpu.HBM)
+ANY = pl.BlockSpec(memory_space=pl.ANY)
 
 
 def swapped(value, axis, size, step):
@@ -162,7 +163,7 @@
 
 def rows_kernel(used, sends, messages, scal, after, here, *refs):
     held, refs = refs[:used], refs[used:]
-    perm, src_ids, rec_ids, refs = refs[0], refs[1 : 1 + sends], refs[1 + sends], refs[2 + sends :]
+    perm, src_ids, rec_ids, refs = refs[0], refs[sends:0:-1], refs[1 + sends], refs[2 + sends :]
     outs, own_out = refs[:-1], refs[-1]
     units, _, _, slots, part = own_out.shape
     channels = here.shape[2]
@@ -197,7 +198,7 @@
         compiler_params=params(16),
         cost_estimate=SMALL,
         name="rows",
-    )(scal, after, here, *held, perm, *src_ids, rec_ids)
+    )(scal, after, here, *held, perm, *src_ids[::-1], rec_ids)
     return sent, own
 
 
@@ -264,7 +265,7 @@
     return pl.pallas_call(
         functools.partial(cross_kernel, pieces, len(after)),
         out_shape=jax.ShapeDtypeStruct((classes, 2 * count, 2 * LANES), BF16),
-        in_specs=[SMEM] + [pl.BlockSpec(memory_space=pl.ANY)] * len(after) + [VMEM] * (len(rows) + 1),
+        in_specs=[SMEM] + [ANY] * len(after) + [VMEM] * (len(rows) + 1),
         out_specs=VMEM,
         compiler_params=params(8),
         cost_estimate=LARGE,
@@ -301,7 +302,7 @@
         functools.partial(lags_kernel, geometry, len(after)),
         out_shape=[jax.ShapeDtypeStruct(shape(rows), F32)]
         + [jax.ShapeDtypeStruct(shape(rows // split), BF16)] * split,
-        in_specs=[SMEM] + [pl.BlockSpec(memory_space=pl.ANY)] * len(after) + [VMEM] * 2,
+        in_specs=[SMEM] + [ANY] * len(after) + [VMEM] * 2,
         out_specs=[VMEM] * (split + 1),
         scratch_shapes=[pltpu.VMEM((2 * columns, rows, lag_dev), F32)],
         compiler_params=params(16),
@@ -336,7 +337,7 @@
         functools.partial(cores_kernel, len(after), len(more)),
         out_shape=[jax.ShapeDtypeStruct((rows, lag_dev), F32)]
         + [jax.ShapeDtypeStruct((rows, lag_dev), BF16)] * (columns - 1),
-        in_specs=[SMEM] + [pl.BlockSpec(memory_space=pl.ANY)] * len(after) + [VMEM] * (1 + len(more)),
+        in_specs=[SMEM] + [ANY] * len(after) + [VMEM] * (1 + len(more)),
         out_specs=[VMEM] * columns,
         compiler_params=params(8),
         cost_estimate=SMALL,
@@ -344,8 +345,9 @@
     )(scal, *after, keep, *more)
 
 
-def stats_kernel(scale, pieces, others, scal, *refs):
-    own, more, refs = refs[0], refs[1 : 1 + others], refs[1 + others :]
+def stats_kernel(scale, q, pieces, others, scal, *refs):
+    earlier, (own, *refs) = refs[:q], refs[q:]
+    more, refs = refs[:others], refs[others:]
     targets, (corr, sums) = refs[: len(pieces)], refs[len(pieces) :]
     columns = []
     for target, (unit, first, count, at) in zip(targets, placed(pieces)):
@@ -358,8 +360,11 @@
         square = jnp.sum(value * value, axis=1, keepdims=True)
         product = jnp.sum(value * target[0], axis=1, keepdims=True)
         lane = lax.broadcasted_iota(jnp.int32, (count, LANES), 1)
-        columns.append(jnp.where(lane == 0, square, jnp.where(lane == 1, product, 0.0)))
-    sums[...] = jnp.concatenate(columns, axis=0).T[:8]
+        columns.append(jnp.where(lane == 2 * q, square, jnp.where(lane == 2 * q + 1, product, 0.0)))
+    total = jnp.concatenate(columns, axis=0).T[:8]
+    for e in earlier:
+        total = total + e[...]
+    sums[...] = total
 
 
 def target_specs(pieces, lag_dev):
@@ -376,30 +381,32 @@
     return pl.BlockSpec(shape, lambda i, scal: (0,) * len(shape))
 
 
-def lag_stats(scal, scale, pieces, own, more, observed):
+def lag_stats(scal, scale, q, pieces, earlier, own, more, observed):
     rows, lag_dev = own.shape
     outs = [jax.ShapeDtypeStruct((rows, lag_dev), F32), jax.ShapeDtypeStruct((8, rows), F32)]
     return pl.pallas_call(
-        functools.partial(stats_kernel, scale, pieces, len(more)),
+        functools.partial(stats_kernel, scale, q, pieces, len(more)),
         grid_spec=pltpu.PrefetchScalarGridSpec(
             num_scalar_prefetch=1,
             grid=(1,),
-            in_specs=[whole(own.shape)] * (1 + len(more)) + target_specs(pieces, lag_dev),
+            in_specs=[whole(e.shape) for e in earlier]
+            + [whole(own.shape)] * (1 + len(more))
+            + target_specs(pieces, lag_dev),
             out_specs=[whole(o.shape) for o in outs],
         ),
         out_shape=outs,
         compiler_params=params(16),
         cost_estimate=SMALL,
         name="stats",
-    )(scal, own, *more, *[observed] * len(pieces))
-
-
-def slot_scales(sums, lag_total):
+    )(scal, *earlier, own, *more, *[observed] * len(pieces))
+
+
+def slot_scales(sums, lag_total, q):
     total = sums[0][...]
     for s in sums[1:]:
         total = total + s[...]
     rows = total.shape[1]
-    square, product = total[0:1], total[1:2]
+    square, product = total[2 * q : 2 * q + 1], total[2 * q + 1 : 2 * q + 2]
     inverse = 1.0 / jnp.sqrt(square / lag_total + EPSILON)
     bending = (square * inverse * inverse - product * inverse) / lag_total
     sub = lax.broadcasted_iota(jnp.int32, (LANES, rows), 0)
@@ -407,10 +414,11 @@
     return both[:, 0:1], both[:, 1:2]
 
 
-def gradient_kernel(lag_total, pieces, parts, scal, *refs):
+def gradient_kernel(lag_total, q, pieces, parts, skip, scal, *refs):
+    refs = refs[skip:]
     sums, corr, refs = refs[:parts], refs[parts], refs[parts + 1 :]
     targets, outs = refs[: len(pieces)], refs[len(pieces) :]
-    inverse, bending = slot_scales(sums, lag_total)
+    inverse, bending = slot_scales(sums, lag_total, q)
     for target, out, (unit, first, count, at) in zip(targets, outs, placed(pieces)):
         slot = first + lax.broadcasted_iota(jnp.int32, (count, 1), 0)
         valid = jnp.where(slot < scal[COUNT + unit], inverse[at], 0.0)
@@ -418,15 +426,16 @@
         out[...] = ((normed - target[0] - normed * bending[at]) * valid).astype(BF16)
 
 
-def gradients(scal, lag_total, pieces, sums, corr, observed):
+def gradients(scal, lag_total, q, pieces, after, sums, corr, observed):
     lag_dev = corr.shape[1]
     outs = [jax.ShapeDtypeStruct((p[2], lag_dev), BF16) for p in pieces]
     return pl.pallas_call(
-        functools.partial(gradient_kernel, lag_total, pieces, len(sums)),
+        functools.partial(gradient_kernel, lag_total, q, pieces, len(sums), len(after)),
         grid_spec=pltpu.PrefetchScalarGridSpec(
             num_scalar_prefetch=1,
             grid=(1,),
-            in_specs=[whole(sums[0].shape)] * len(sums)
+            in_specs=[ANY] * len(after)
+            + [whole(sums[0].shape)] * len(sums)
             + [whole(corr.shape)]
             + target_specs(pieces, lag_dev),
             out_specs=[whole(o.shape) for o in outs],
@@ -435,14 +444,13 @@
         compiler_params=params(16),
         cost_estimate=SMALL,
         name="gradient",
-    )(scal, *sums, corr, *[observed] * len(pieces))
+    )(scal, *after, *sums, corr, *[observed] * len(pieces))
 
 
 def normed_kernel(lag_total, chunks, parts, scal, *refs):
-    out = refs[-1]
-    for q, pieces in enumerate(chunks):
-        sums, corr = refs[q * (parts + 1) : q * (parts + 1) + parts], refs[q * (parts + 1) + parts]
-        inverse, _ = slot_scales(sums, lag_total)
+    sums, corrs, out = refs[:parts], refs[parts:-1], refs[-1]
+    for q, (pieces, corr) in enumerate(zip(chunks, corrs)):
+        inverse, _ = slot_scales(sums, lag_total, q)
         for unit, first, count, at in placed(pieces):
 
             @pl.when(pl.program_id(0) == unit)
@@ -450,11 +458,11 @@
                 out[0, first : first + count] = corr[at] * inverse[at]
 
 
-def normed_rows(scal, lag_total, chunks, sums, corr, observed):
+def normed_rows(scal, lag_total, chunks, sums, corrs, observed):
     blocks, slots, lag_dev = observed.shape
-    ins = [x for s, c in zip(sums, corr) for x in (*s, c)]
-    return pl.pallas_call(
-        functools.partial(normed_kernel, lag_total, chunks, len(sums[0])),
+    ins = [*sums, *corrs]
+    return pl.pallas_call(
+        functools.partial(normed_kernel, lag_total, chunks, len(sums)),
         grid_spec=pltpu.PrefetchScalarGridSpec(
             num_scalar_prefetch=1,
             grid=(blocks,),
@@ -529,7 +537,7 @@
         scal = lax.dynamic_update_slice(scal, ranked, (ORDER,))
 
     direct = places == blocks
-    src_ids = [swapped(x, "recv", places, d) for d, x in zip(shifts, wanted)]
+    src_ids = [swapped(wanted[d], "recv", places, d) for d in reversed(shifts)][::-1]
     trig = tables(classes, span, period, bins_dev, columns, cores)
     table = make_table(scal, trig, classes, span, peers)
     if direct and blocks == 4:
@@ -546,7 +554,7 @@
     sent, own_rows = gather_rows(
         scal, table, held[0], held[1:], make_perm(part), src_ids, rec_ids, messages
     )
-    arrived = [swapped(x, "recv", places, m[0]) for m, x in zip(messages, sent)]
+    arrived = [swapped(x, "recv", places, m[0]) for m, x in reversed(list(zip(messages, sent)))][::-1]
     if not direct:
         stacked = jnp.stack(arrived)
         whole_rows = [
@@ -565,9 +573,15 @@
         own, *sends = add_cores(scal, after[1:], keep, sends)
         more = [swapped(x, "win", columns, s + 1) for s, x in enumerate(sends)]
         after = [own, *more]
-        corr, sums = lag_stats(scal, lag_scale, pieces, own, more, observed)
-        sums = [swapped(sums, ("win", "freq"), peers, s) for s in range(peers)]
-        grads = gradients(scal, lag_total, pieces, sums, corr, observed)
+        corr, sums = lag_stats(scal, lag_scale, q, pieces, all_sums, own, more, observed)
+        corrs.append(corr)
+        all_sums = [sums]
+    sums = [swapped(sums, ("win", "freq"), peers, s) for s in range(peers)]
+    after = []
+    for q in reversed(range(len(chunks))):
+        pieces = chunks[q]
+        grads = gradients(scal, lag_total, q, pieces, after, sums, corrs[q], observed)
+        after = [grads[0]]
         if not direct:
             stacked = jnp.stack(list(grads) + [jnp.zeros_like(grads[0])])
             grads = []
@@ -577,11 +591,10 @@
                     block = jnp.where(owners[b] == place ^ d, b, block)
                 grads.append(lax.dynamic_index_in_dim(stacked, block, 0, False))
             pieces = [(d, pieces[0][1], some) for d in shifts]
-        returned += [swapped(g, "recv", places, p[0]) for p, g in zip(pieces, grads)]
+        sent = [swapped(g, "recv", places, p[0]) for p, g in reversed(list(zip(pieces, grads)))]
+        returned += sent[::-1]
         returned_pieces += pieces
-        corrs.append(corr)
-        all_sums.append(sums)
-    normed = normed_rows(scal, lag_total, chunks, all_sums, corrs, observed)
+    normed = normed_rows(scal, lag_total, chunks, sums, corrs, observed)
     adjoint = adjoint_rows(src_ids, returned_pieces, returned, channels)
     return (normed, adjoint)
 

time: 78.8 us -> 79.2 us (level)
  waiting for transfers between devices: 25.6 us -> 28.5 us
  starting transfers between devices: 27.8 us -> 25.3 us
    ppermute x30 -> x27, waiting for transfers between devices: 25.6 us -> 28.5 us  [swapped(): return lax.ppermute(value, axis, [(i, i ^ step) for i in range(size)])]
    ppermute x30 -> x27, starting transfers between devices: 27.8 us -> 25.3 us  [swapped(): return lax.ppermute(value, axis, [(i, i ^ step) for i in range(size)])]
  transfers between devices with their start and end apart: 30 -> 27, of which waited for: 14 -> 15; matrix products, arithmetic and copies ran while one was open for 0% -> 0% of each run, Pallas kernels for 20% -> 18%
where the time goes in v10:
time: 79.2 us; the launch traced here: 79 us
  waiting for transfers between devices  28.5 us (36%)
  starting transfers between devices  25.3 us (32%)
  Pallas kernels  19.6 us (25%)
  local copies, waits for them, and re-layouts  4.02 us (5%)
  between operations  1.47 us (2%)
    ppermute x27, waiting for transfers between devices, swapped(): return lax.ppermute(value, axis, [(i, i ^ step) for i in range(size)])  28.5 us
    ppermute x27, starting transfers between devices, swapped(): return lax.ppermute(value, axis, [(i, i ^ step) for i in range(size)])  25.3 us
    pallas_call x2, Pallas kernels, lag_parts(): pl.pallas_call(functools.partial(lags_kernel, geometry, len(after)), out_...  4.98 us
    pallas_call x1, Pallas kernels, normed_rows(): pl.pallas_call(functools.partial(normed_kernel, lag_total, chunks, len(su...  2.95 us
    unnamed x12, local copies, waits for them, and re-layouts  2.68 us
    pallas_call x1, Pallas kernels, gather_rows(): pl.pallas_call(functools.partial(rows_kernel, used, sends, messages), out...  1.82 us
    pallas_call x1, Pallas kernels, make_table(): pl.pallas_call(functools.partial(table_kernel, classes, parts), out_shape...  1.78 us
    pallas_call x2, Pallas kernels, gradients(): pl.pallas_call(functools.partial(gradient_kernel, lag_total, q, pieces, l...  1.61 us
  transfers between devices with their start and end apart: 27, of which 15 were waited for; matrix products, arithmetic and copies ran while one was open for 0% of the time, Pallas kernels for 18%

profile of v10, /device:TPU:0, one launch (start us, length us, event | category | flops | bytes accessed | tf_op | source)
XLA Modules:
  0.0 79.0 jit_solution(7364751551055496197)
XLA Ops:
  0.7 1.3 %constant_dynamic-slice_fusion = (bf16[1,2,128,1024]{3,2,1,0:T(8,128)(2,1)S(1)}, bf16[1,2,128,1024]{3,2,1,0:T(8,128)(2,1)S(1)}) fusion(bf16[1,2,128,2048]{3,2,1,0:T(8,128)(2,1)} %param.8, s32[]{:T(128)S(6)} %select_n.7, s32[]{:T(128)S(6)} %select_n.6), kind=kLoop, calls=%fused_computation | loop fusion | bytes 2097160 | tf_op jit(solution)/shard_map/dynamic_slice | solution.py:519
  2.0 3.0 %collective-permute-start = (bf16[1,2,128,1024]{3,2,1,0:T(8,128)(2,1)S(1)}, bf16[1,2,128,1024]{3,2,1,0:T(8,128)(2,1)S(1)}, u32[]{:S(2)}, u32[]{:S(2)}) collective-permute-start(bf16[1,2,128,1024]{3,2,1,0:T(8,128)(2,1)S(1)} %get-tuple-element.76), channel_id=1, source_target_pairs={{0,2},{2,0},{1,3},{3,1},{4,6},{6,4},{5,7},{7,5},{8,10},{10,8},{9,1... | collective-permute-start | bytes 1572872 | tf_op jit(solution)/shard_map/ppermute | solution.py:30
  8.3 1.2 %index.1 = (s32[128]{0:T(128)S(1)}, s32[1,64]{1,0:T(1,128)S(1)}, s32[1,64]{1,0:T(1,128)S(1)}, s32[1,64]{1,0:T(1,128)S(1)}, s32[1,64]{1,0:T(1,128)S(1)}, /*index=5*/s32[4,64]{1,0:T(4,128)S(1)}) custom-call(s32[1]{0:T(128)S(6)} %copy.10.refs_0_, s32[4]{0:T(128)S(1)} %copy-done.4, s32[4]{0:T(128)S(1)} %bitcast.1, s32[4,64]{1,0:T(4,128)S(1)} %copy-done.2, ...), custom_call_target="tpu_custom_call" | custom-call | flops 1 | bytes 1 | tf_op jit(solution)/shard_map/index/pallas_call | solution.py:93
  9.6 3.7 %collective-permute-start.1 = (s32[1,64]{1,0:T(1,128)S(1)}, s32[1,64]{1,0:T(1,128)S(1)}, u32[]{:S(2)}, u32[]{:S(2)}) collective-permute-start(s32[1,64]{1,0:T(1,128)S(1)} %get-tuple-element.40), channel_id=1, source_target_pairs={{0,12},{4,8},{8,4},{12,0},{1,13},{5,9},{9,5},{13,1},{2,14},{6,10},... | collective-permute-start | bytes 776 | tf_op jit(solution)/shard_map/ppermute | solution.py:30
  13.2 0.8 collective-permute-start.3
  14.6 1.8 %table.1.after.refs_1_ = bf16[8,256,1024]{2,1,0:T(8,128)(2,1)S(1)} custom-call(s32[128]{0:T(128)S(1)} %get-tuple-element.39.scal, f32[2,56,1024]{2,1,0:T(8,128)S(1)} %copy-done.1), custom_call_target="tpu_custom_call" | custom-call | flops 1 | bytes 1 | tf_op jit(solution)/shard_map/table/pallas_call | solution.py:127
  16.4 1.2 %collective-permute-done.2.refs_3_.refs_0_ = s32[1,64]{1,0:T(1,128)S(1)} collective-permute-done((s32[1,64]{1,0:T(1,128)S(1)}, s32[1,64]{1,0:T(1,128)S(1)}, u32[]{:S(2)}, u32[]{:S(2)}) %collective-permute-start.2) | collective-permute-done | bytes 288 | tf_op jit(solution)/shard_map/ppermute | solution.py:30
  17.7 1.8 %rows.1 = (bf16[1,2,64,1024]{3,2,1,0:T(8,128)(2,1)S(1)}, bf16[1,2,64,1024]{3,2,1,0:T(8,128)(2,1)S(1)}, bf16[1,2,64,1024]{3,2,1,0:T(8,128)(2,1)S(1)}, bf16[1,2,64...) custom-call(s32[128]{0:T(128)S(1)} %get-tuple-element.39.scal, bf16[8,256,1024]{2,1,0:T(8,128)(2,1)S(1)} %table.1.after.refs_1_, ...), custom_call_target="tpu_custom_call" | custom-call | flops 1 | bytes 1 | tf_op jit(solution)/shard_map/rows/pallas_call | solution.py:192
  19.5 1.1 %collective-permute-start.4 = (bf16[1,2,64,1024]{3,2,1,0:T(8,128)(2,1)S(1)}, bf16[1,2,64,1024]{3,2,1,0:T(8,128)(2,1)S(1)}, u32[]{:S(2)}, u32[]{:S(2)}) collective-permute-start(bf16[1,2,64,1024]{3,2,1,0:T(8,128)(2,1)S(1)} %get-tuple-element.46), channel_id=1, source_target_pairs={{0,4},{4,0},{8,12},{12,8},{1,5},{5,1},{9,13},{13,9},{2,6},{6,2},{1... | collective-permute-start | bytes 786440 | tf_op jit(solution)/shard_map/ppermute | solution.py:30
  20.6 2.6 %collective-permute-start.14 = (bf16[1,2,64,1024]{3,2,1,0:T(8,128)(2,1)S(1)}, bf16[1,2,64,1024]{3,2,1,0:T(8,128)(2,1)S(1)}, u32[]{:S(2)}, u32[]{:S(2)}) collective-permute-start(bf16[1,2,64,1024]{3,2,1,0:T(8,128)(2,1)S(1)} %get-tuple-element.60), channel_id=1, source_target_pairs={{0,8},{4,12},{8,0},{12,4},{1,9},{5,13},{9,1},{13,5},{2,10},{6,14},... | collective-permute-start | bytes 786440 | tf_op jit(solution)/shard_map/ppermute | solution.py:30
  23.2 0.7 collective-permute-start.15
  24.0 6.8 %collective-permute-done.4.refs_1_ = bf16[1,2,64,1024]{3,2,1,0:T(8,128)(2,1)S(1)} collective-permute-done((bf16[1,2,64,1024]{3,2,1,0:T(8,128)(2,1)S(1)}, bf16[1,2,64,1024]{3,2,1,0:T(8,128)(2,1)S(1)}, u32[]{:S(2)}, u32[]{:S(2)}) %collective-permute-start.4) | collective-permute-done | bytes 262176 | tf_op jit(solution)/shard_map/ppermute | solution.py:30
  31.0 2.5 %lags.2 = (f32[2,128,1024]{2,1,0:T(8,128)S(1)}, bf16[2,16,1024]{2,1,0:T(8,128)(2,1)S(1)}, bf16[2,16,1024]{2,1,0:T(8,128)(2,1)S(1)}, bf16[2,16,1024]{2,1,0:T(8,12...) custom-call(s32[128]{0:T(128)S(1)} %get-tuple-element.39.scal, ...), custom_call_target="tpu_custom_call" | custom-call | flops 20000000000 | bytes 1048576 | tf_op jit(solution)/shard_map/lags/pallas_call | solution.py:301
  36.6 0.7 collective-permute-done.11.refs_7_
  37.5 0.8 %cores.2 = (f32[128,1024]{1,0:T(8,128)S(1)}, bf16[128,1024]{1,0:T(8,128)(2,1)S(1)}) custom-call(s32[128]{0:T(128)S(1)} %get-tuple-element.39.scal, f32[2,128,1024]{2,1,0:T(8,128)S(1)} %get-tuple-element.48.refs_0_, bf16[2,16,1024]{2,1,0:T(8,128)(2,1)S(1)} %collective-permute-done.5.refs_1_, bf16[2,16,1024]{2,1,0:T(8,128)(2,1)S(1)} %collective-permute-done.6.refs_2_, ...), custom_call_target="tpu_custom_call" | custom-call | flops 1 | bytes 1 | tf_op jit(solution)/shard_map/cores/pallas_call | solution.py:336
  38.3 1.5 %collective-permute-start.13 = (bf16[128,1024]{1,0:T(8,128)(2,1)S(1)}, bf16[128,1024]{1,0:T(8,128)(2,1)S(1)}, u32[]{:S(2)}, u32[]{:S(2)}) collective-permute-start(bf16[128,1024]{1,0:T(8,128)(2,1)S(1)} %get-tuple-element.58), channel_id=1, source_target_pairs={{0,2},{2,0},{1,3},{3,1},{4,6},{6,4},{5,7},{7,5},{8,10},{10,8},{9,1... | collective-permute-start | bytes 786440 | tf_op jit(solution)/shard_map/ppermute | solution.py:30
  39.8 2.2 %collective-permute-done.14.refs_1_ = bf16[1,2,64,1024]{3,2,1,0:T(8,128)(2,1)S(1)} collective-permute-done((bf16[1,2,64,1024]{3,2,1,0:T(8,128)(2,1)S(1)}, bf16[1,2,64,1024]{3,2,1,0:T(8,128)(2,1)S(1)}, u32[]{:S(2)}, u32[]{:S(2)}) %collective-permute-start.14) | collective-permute-done | bytes 262176 | tf_op jit(solution)/shard_map/ppermute | solution.py:30
  42.3 2.5 %lags.3 = (f32[2,128,1024]{2,1,0:T(8,128)S(1)}, bf16[2,32,1024]{2,1,0:T(8,128)(2,1)S(1)}, bf16[2,32,1024]{2,1,0:T(8,128)(2,1)S(1)}, bf16[2,32,1024]{2,1,0:T(8,128)(2,1)S(1)}, bf16[2,32,1024]{2,1,0:T(8,128)(2,1)S(1)}) custom-call(s32[128]{0:T(128)S(1)} %get-tuple-element.39.scal, bf16[8,256,256]{2,1,0:T(8,128)(2,1)S(1)} %cross.3.refs_0_, ...), custom_call_target="tpu_custom_call" | custom-call | flops 1 | bytes 1 | tf_op jit(solution)/shard_map/lags/pallas_call | solution.py:301
  47.7 1.5 %collective-permute-start.20 = (bf16[128,1024]{1,0:T(8,128)(2,1)S(1)}, bf16[128,1024]{1,0:T(8,128)(2,1)S(1)}, u32[]{:S(2)}, u32[]{:S(2)}) collective-permute-start(bf16[128,1024]{1,0:T(8,128)(2,1)S(1)} %get-tuple-element.68), channel_id=1, source_target_pairs={{0,2},{2,0},{1,3},{3,1},{4,6},{6,4},{5,7},{7,5},{8,10},{10,8},{9,1... | collective-permute-start | bytes 786440 | tf_op jit(solution)/shard_map/ppermute | solution.py:30
  49.2 0.8 stats.2
  50.0 6.3 %collective-permute-done.20.refs_2_ = bf16[128,1024]{1,0:T(8,128)(2,1)S(1)} collective-permute-done((bf16[128,1024]{1,0:T(8,128)(2,1)S(1)}, bf16[128,1024]{1,0:T(8,128)(2,1)S(1)}, u32[]{:S(2)}, u32[]{:S(2)}) %collective-permute-start.20) | collective-permute-done | bytes 262176 | tf_op jit(solution)/shard_map/ppermute | solution.py:30
  56.2 0.8 stats.3
  57.7 1.0 %collective-permute-start.22 = (f32[8,128]{1,0:T(8,128)S(1)}, f32[8,128]{1,0:T(8,128)S(1)}, u32[]{:S(2)}, u32[]{:S(2)}) collective-permute-start(f32[8,128]{1,0:T(8,128)S(1)} %get-tuple-element.69.refs_0_.refs_1_), channel_id=1, source_target_pairs={{0,2},{1,3},{2,0},{3,1},{4,6},{5,7},{6,4},{7,5},{8,10},{9,11},{10,... | collective-permute-start | bytes 12296 | tf_op jit(solution)/shard_map/ppermute | solution.py:30
  58.9 1.2 %collective-permute-done.23.refs_3_.refs_4_ = f32[8,128]{1,0:T(8,128)S(1)} collective-permute-done((f32[8,128]{1,0:T(8,128)S(1)}, f32[8,128]{1,0:T(8,128)S(1)}, u32[]{:S(2)}, u32[]{:S(2)}) %collective-permute-start.23) | collective-permute-done | bytes 4128 | tf_op jit(solution)/shard_map/ppermute | solution.py:30
  60.1 1.2 %collective-permute-done.22.refs_2_.refs_3_ = f32[8,128]{1,0:T(8,128)S(1)} collective-permute-done((f32[8,128]{1,0:T(8,128)S(1)}, f32[8,128]{1,0:T(8,128)S(1)}, u32[]{:S(2)}, u32[]{:S(2)}) %collective-permute-start.22) | collective-permute-done | bytes 4128 | tf_op jit(solution)/shard_map/ppermute | solution.py:30
  61.3 0.8 %gradient.2 = (bf16[64,1024]{1,0:T(8,128)(2,1)S(1)}, bf16[64,1024]{1,0:T(8,128)(2,1)S(1)}) custom-call(s32[128]{0:T(128)S(1)} %get-tuple-element.39.scal, f32[8,128]{1,0:T(8,128)S(1)} %get-tuple-element.69.refs_0_.refs_1_, f32[8,128]{1,0:T(8,128)S(1)} %collective-permute-done.21.refs_1_.refs_2_, f32[8,128]{1,0:T(8,128)S(1)} %collective-permute-done.22.refs_2_.refs_3_, ...), custom_call_target="tpu_custom_call" | custom-call | flops 1 | bytes 1 | tf_op jit(solution)/shard_map/gradient/pallas_call | solution.py:432
  62.1 2.2 %collective-permute-start.25 = (bf16[64,1024]{1,0:T(8,128)(2,1)S(1)}, bf16[64,1024]{1,0:T(8,128)(2,1)S(1)}, u32[]{:S(2)}, u32[]{:S(2)}) collective-permute-start(bf16[64,1024]{1,0:T(8,128)(2,1)S(1)} %get-tuple-element.73), channel_id=1, source_target_pairs={{0,12},{4,8},{8,4},{12,0},{1,13},{5,9},{9,5},{13,1},{2,14},{6,10},... | collective-permute-start | bytes 393224 | tf_op jit(solution)/shard_map/ppermute | solution.py:30
  64.3 3.2 %collective-permute-start.24 = (bf16[64,1024]{1,0:T(8,128)(2,1)S(1)}, bf16[64,1024]{1,0:T(8,128)(2,1)S(1)}, u32[]{:S(2)}, u32[]{:S(2)}) collective-permute-start(bf16[64,1024]{1,0:T(8,128)(2,1)S(1)} %get-tuple-element.72.refs_0_), channel_id=1, source_target_pairs={{0,8},{4,12},{8,0},{12,4},{1,9},{5,13},{9,1},{13,5},{2,10},{6,14},... | collective-permute-start | bytes 393224 | tf_op jit(solution)/shard_map/ppermute | solution.py:30
  67.5 0.8 %gradient.3 = (bf16[64,1024]{1,0:T(8,128)(2,1)S(1)}, bf16[64,1024]{1,0:T(8,128)(2,1)S(1)}) custom-call(s32[128]{0:T(128)S(1)} %get-tuple-element.39.scal, bf16[64,1024]{1,0:T(8,128)(2,1)S(1)} %get-tuple-element.72.refs_0_, f32[8,128]{1,0:T(8,128)S(1)} %get-tuple-element.69.refs_0_.refs_1_, f32[8,128]{1,0:T(8,128)S(1)} %collective-permute-done.21.refs_1_.refs_2_, ...), custom_call_target="tpu_custom_call" | custom-call | flops 1 | bytes 1 | tf_op jit(solution)/shard_map/gradient/pallas_call | solution.py:432
  68.5 3.0 %normed.1 = f32[4,64,1024]{2,1,0:T(8,128)} custom-call(s32[128]{0:T(128)S(1)} %get-tuple-element.39.scal, f32[8,128]{1,0:T(8,128)S(1)} %get-tuple-element.69.refs_0_.refs_1_, f32[8,128]{1,0:T(8,128)S(1)} %collective-permute-done.21.refs_1_.refs_2_, f32[8,128]{1,0:T(8,128)S(1)} %collective-permute-done.22.refs_2_.refs_3_, ...), custom_call_target="tpu_custom_call" | custom-call | flops 1 | bytes 1 | tf_op jit(solution)/shard_map/normed/pallas_call | solution.py:464
  71.5 6.5 %collective-permute-done.24.refs_4_ = bf16[64,1024]{1,0:T(8,128)(2,1)S(1)} collective-permute-done((bf16[64,1024]{1,0:T(8,128)(2,1)S(1)}, bf16[64,1024]{1,0:T(8,128)(2,1)S(1)}, u32[]{:S(2)}, u32[]{:S(2)}) %collective-permute-start.24) | collective-permute-done | bytes 131104 | tf_op jit(solution)/shard_map/ppermute | solution.py:30
  77.9 1.1 %adjoint.1 = f32[128,1024]{1,0:T(8,128)} custom-call(s32[1,64]{1,0:T(1,128)S(1)} %collective-permute-done.2.refs_3_.refs_0_, s32[1,64]{1,0:T(1,128)S(1)} %collective-permute-done.1.refs_2_.refs_1_, s32[1,64]{1,0:T(1,128)S(1)} %get-tuple-element.43.refs_5_.refs_2_, s32[1,64]{1,0:T(1,128)S(1)} %collective-permute-done.3.refs_4_.refs_3_, ...), custom_call_target="tpu_custom_call" | custom-call | flops 1 | bytes 1 | tf_op jit(solution)/shard_map/adjoint/pallas_call | solution.py:488
  (51 shorter events, 11.0 us)
Async XLA Ops:
  0.6 14.0 %copy-start.1 = (f32[2,56,1024]{2,1,0:T(8,128)S(1)}, f32[2,56,1024]{2,1,0:T(8,128)}, u32[]{:S(2)}) copy-start(f32[2,56,1024]{2,1,0:T(8,128)} %constant.16.clone.trig) | copy-start | bytes 1376260
  2.0 15.7 %collective-permute-start = (bf16[1,2,128,1024]{3,2,1,0:T(8,128)(2,1)S(1)}, bf16[1,2,128,1024]{3,2,1,0:T(8,128)(2,1)S(1)}, u32[]{:S(2)}, u32[]{:S(2)}) collective-permute-start(bf16[1,2,128,1024]{3,2,1,0:T(8,128)(2,1)S(1)} %get-tuple-element.76), channel_id=1, source_target_pairs={{0,2},{2,0},{1,3},{3,1},{4,6},{6,4},{5,7},{7,5},{8,10},{10,8},{9,1... | collective-permute-start | bytes 1572872 | tf_op jit(solution)/shard_map/ppermute | solution.py:30
  5.7 0.7 copy-start.2
  6.3 0.7 copy-start.3
  7.0 0.7 copy-start.4
  9.6 6.9 %collective-permute-start.1 = (s32[1,64]{1,0:T(1,128)S(1)}, s32[1,64]{1,0:T(1,128)S(1)}, u32[]{:S(2)}, u32[]{:S(2)}) collective-permute-start(s32[1,64]{1,0:T(1,128)S(1)} %get-tuple-element.40), channel_id=1, source_target_pairs={{0,12},{4,8},{8,4},{12,0},{1,13},{5,9},{9,5},{13,1},{2,14},{6,10},... | collective-permute-start | bytes 776 | tf_op jit(solution)/shard_map/ppermute | solution.py:30
  13.2 4.4 %collective-permute-start.2 = (s32[1,64]{1,0:T(1,128)S(1)}, s32[1,64]{1,0:T(1,128)S(1)}, u32[]{:S(2)}, u32[]{:S(2)}) collective-permute-start(s32[1,64]{1,0:T(1,128)S(1)} %get-tuple-element.41), channel_id=1, source_target_pairs={{0,8},{4,12},{8,0},{12,4},{1,9},{5,13},{9,1},{13,5},{2,10},{6,14},... | collective-permute-start | bytes 776 | tf_op jit(solution)/shard_map/ppermute | solution.py:30
  13.2 4.4 %collective-permute-start.3 = (s32[1,64]{1,0:T(1,128)S(1)}, s32[1,64]{1,0:T(1,128)S(1)}, u32[]{:S(2)}, u32[]{:S(2)}) collective-permute-start(s32[1,64]{1,0:T(1,128)S(1)} %get-tuple-element.42), channel_id=1, source_target_pairs={{0,4},{4,0},{8,12},{12,8},{1,5},{5,1},{9,13},{13,9},{2,6},{6,2},{1... | collective-permute-start | bytes 776 | tf_op jit(solution)/shard_map/ppermute | solution.py:30
  19.5 11.2 %collective-permute-start.4 = (bf16[1,2,64,1024]{3,2,1,0:T(8,128)(2,1)S(1)}, bf16[1,2,64,1024]{3,2,1,0:T(8,128)(2,1)S(1)}, u32[]{:S(2)}, u32[]{:S(2)}) collective-permute-start(bf16[1,2,64,1024]{3,2,1,0:T(8,128)(2,1)S(1)} %get-tuple-element.46), channel_id=1, source_target_pairs={{0,4},{4,0},{8,12},{12,8},{1,5},{5,1},{9,13},{13,9},{2,6},{6,2},{1... | collective-permute-start | bytes 786440 | tf_op jit(solution)/shard_map/ppermute | solution.py:30
  20.6 21.4 %collective-permute-start.14 = (bf16[1,2,64,1024]{3,2,1,0:T(8,128)(2,1)S(1)}, bf16[1,2,64,1024]{3,2,1,0:T(8,128)(2,1)S(1)}, u32[]{:S(2)}, u32[]{:S(2)}) collective-permute-start(bf16[1,2,64,1024]{3,2,1,0:T(8,128)(2,1)S(1)} %get-tuple-element.60), channel_id=1, source_target_pairs={{0,8},{4,12},{8,0},{12,4},{1,9},{5,13},{9,1},{13,5},{2,10},{6,14},... | collective-permute-start | bytes 786440 | tf_op jit(solution)/shard_map/ppermute | solution.py:30
  23.2 18.8 %collective-permute-start.15 = (bf16[1,2,64,1024]{3,2,1,0:T(8,128)(2,1)S(1)}, bf16[1,2,64,1024]{3,2,1,0:T(8,128)(2,1)S(1)}, u32[]{:S(2)}, u32[]{:S(2)}) collective-permute-start(bf16[1,2,64,1024]{3,2,1,0:T(8,128)(2,1)S(1)} %get-tuple-element.61), channel_id=1, source_target_pairs={{0,12},{4,8},{8,4},{12,0},{1,13},{5,9},{9,5},{13,1},{2,14},{6,10},... | collective-permute-start | bytes 786440 | tf_op jit(solution)/shard_map/ppermute | solution.py:30
  33.5 1.3 %collective-permute-start.5 = (bf16[2,16,1024]{2,1,0:T(8,128)(2,1)S(1)}, bf16[2,16,1024]{2,1,0:T(8,128)(2,1)S(1)}, u32[]{:S(2)}, u32[]{:S(2)}) collective-permute-start(bf16[2,16,1024]{2,1,0:T(8,128)(2,1)S(1)} %get-tuple-element.49), channel_id=1, source_target_pairs={{0,1},{1,0},{2,3},{3,2},{4,5},{5,4},{6,7},{7,6},{8,9},{9,8},{10,11... | collective-permute-start | bytes 196616 | tf_op jit(solution)/shard_map/ppermute | solution.py:30
  33.6 1.4 %collective-permute-start.6 = (bf16[2,16,1024]{2,1,0:T(8,128)(2,1)S(1)}, bf16[2,16,1024]{2,1,0:T(8,128)(2,1)S(1)}, u32[]{:S(2)}, u32[]{:S(2)}) collective-permute-start(bf16[2,16,1024]{2,1,0:T(8,128)(2,1)S(1)} %get-tuple-element.50), channel_id=1, source_target_pairs={{0,1},{1,0},{2,3},{3,2},{4,5},{5,4},{6,7},{7,6},{8,9},{9,8},{10,11... | collective-permute-start | bytes 196616 | tf_op jit(solution)/shard_map/ppermute | solution.py:30
  34.1 1.3 %collective-permute-start.7 = (bf16[2,16,1024]{2,1,0:T(8,128)(2,1)S(1)}, bf16[2,16,1024]{2,1,0:T(8,128)(2,1)S(1)}, u32[]{:S(2)}, u32[]{:S(2)}) collective-permute-start(bf16[2,16,1024]{2,1,0:T(8,128)(2,1)S(1)} %get-tuple-element.51), channel_id=1, source_target_pairs={{0,1},{1,0},{2,3},{3,2},{4,5},{5,4},{6,7},{7,6},{8,9},{9,8},{10,11... | collective-permute-start | bytes 196616 | tf_op jit(solution)/shard_map/ppermute | solution.py:30
  34.8 1.3 %collective-permute-start.8 = (bf16[2,16,1024]{2,1,0:T(8,128)(2,1)S(1)}, bf16[2,16,1024]{2,1,0:T(8,128)(2,1)S(1)}, u32[]{:S(2)}, u32[]{:S(2)}) collective-permute-start(bf16[2,16,1024]{2,1,0:T(8,128)(2,1)S(1)} %get-tuple-element.52), channel_id=1, source_target_pairs={{0,1},{1,0},{2,3},{3,2},{4,5},{5,4},{6,7},{7,6},{8,9},{9,8},{10,11... | collective-permute-start | bytes 196616 | tf_op jit(solution)/shard_map/ppermute | solution.py:30
  35.0 1.3 %collective-permute-start.9 = (bf16[2,16,1024]{2,1,0:T(8,128)(2,1)S(1)}, bf16[2,16,1024]{2,1,0:T(8,128)(2,1)S(1)}, u32[]{:S(2)}, u32[]{:S(2)}) collective-permute-start(bf16[2,16,1024]{2,1,0:T(8,128)(2,1)S(1)} %get-tuple-element.53), channel_id=1, source_target_pairs={{0,1},{1,0},{2,3},{3,2},{4,5},{5,4},{6,7},{7,6},{8,9},{9,8},{10,11... | collective-permute-start | bytes 196616 | tf_op jit(solution)/shard_map/ppermute | solution.py:30
  35.3 1.3 %collective-permute-start.10 = (bf16[2,16,1024]{2,1,0:T(8,128)(2,1)S(1)}, bf16[2,16,1024]{2,1,0:T(8,128)(2,1)S(1)}, u32[]{:S(2)}, u32[]{:S(2)}) collective-permute-start(bf16[2,16,1024]{2,1,0:T(8,128)(2,1)S(1)} %get-tuple-element.54), channel_id=1, source_target_pairs={{0,1},{1,0},{2,3},{3,2},{4,5},{5,4},{6,7},{7,6},{8,9},{9,8},{10,11... | collective-permute-start | bytes 196616 | tf_op jit(solution)/shard_map/ppermute | solution.py:30
  36.1 1.3 %collective-permute-start.11 = (bf16[2,16,1024]{2,1,0:T(8,128)(2,1)S(1)}, bf16[2,16,1024]{2,1,0:T(8,128)(2,1)S(1)}, u32[]{:S(2)}, u32[]{:S(2)}) collective-permute-start(bf16[2,16,1024]{2,1,0:T(8,128)(2,1)S(1)} %get-tuple-element.55), channel_id=1, source_target_pairs={{0,1},{1,0},{2,3},{3,2},{4,5},{5,4},{6,7},{7,6},{8,9},{9,8},{10,11... | collective-permute-start | bytes 196616 | tf_op jit(solution)/shard_map/ppermute | solution.py:30
  36.2 1.3 %collective-permute-start.12 = (bf16[2,16,1024]{2,1,0:T(8,128)(2,1)S(1)}, bf16[2,16,1024]{2,1,0:T(8,128)(2,1)S(1)}, u32[]{:S(2)}, u32[]{:S(2)}) collective-permute-start(bf16[2,16,1024]{2,1,0:T(8,128)(2,1)S(1)} %get-tuple-element.56), channel_id=1, source_target_pairs={{0,1},{1,0},{2,3},{3,2},{4,5},{5,4},{6,7},{7,6},{8,9},{9,8},{10,11... | collective-permute-start | bytes 196616 | tf_op jit(solution)/shard_map/ppermute | solution.py:30
  38.3 8.6 %collective-permute-start.13 = (bf16[128,1024]{1,0:T(8,128)(2,1)S(1)}, bf16[128,1024]{1,0:T(8,128)(2,1)S(1)}, u32[]{:S(2)}, u32[]{:S(2)}) collective-permute-start(bf16[128,1024]{1,0:T(8,128)(2,1)S(1)} %get-tuple-element.58), channel_id=1, source_target_pairs={{0,2},{2,0},{1,3},{3,1},{4,6},{6,4},{5,7},{7,5},{8,10},{10,8},{9,1... | collective-permute-start | bytes 786440 | tf_op jit(solution)/shard_map/ppermute | solution.py:30
  42.3 6.9 %copy-start = (f32[4,64,1024]{2,1,0:T(8,128)S(1)}, f32[4,64,1024]{2,1,0:T(8,128)}, u32[]{:S(2)}) copy-start(f32[4,64,1024]{2,1,0:T(8,128)} %refs_7_.1) | copy-start | bytes 3145732
  44.8 1.4 %collective-permute-start.16 = (bf16[2,32,1024]{2,1,0:T(8,128)(2,1)S(1)}, bf16[2,32,1024]{2,1,0:T(8,128)(2,1)S(1)}, u32[]{:S(2)}, u32[]{:S(2)}) collective-permute-start(bf16[2,32,1024]{2,1,0:T(8,128)(2,1)S(1)} %get-tuple-element.63), channel_id=1, source_target_pairs={{0,1},{1,0},{2,3},{3,2},{4,5},{5,4},{6,7},{7,6},{8,9},{9,8},{10,11... | collective-permute-start | bytes 393224 | tf_op jit(solution)/shard_map/ppermute | solution.py:30
  44.9 1.5 %collective-permute-start.17 = (bf16[2,32,1024]{2,1,0:T(8,128)(2,1)S(1)}, bf16[2,32,1024]{2,1,0:T(8,128)(2,1)S(1)}, u32[]{:S(2)}, u32[]{:S(2)}) collective-permute-start(bf16[2,32,1024]{2,1,0:T(8,128)(2,1)S(1)} %get-tuple-element.64), channel_id=1, source_target_pairs={{0,1},{1,0},{2,3},{3,2},{4,5},{5,4},{6,7},{7,6},{8,9},{9,8},{10,11... | collective-permute-start | bytes 393224 | tf_op jit(solution)/shard_map/ppermute | solution.py:30
  45.4 1.3 %collective-permute-start.18 = (bf16[2,32,1024]{2,1,0:T(8,128)(2,1)S(1)}, bf16[2,32,1024]{2,1,0:T(8,128)(2,1)S(1)}, u32[]{:S(2)}, u32[]{:S(2)}) collective-permute-start(bf16[2,32,1024]{2,1,0:T(8,128)(2,1)S(1)} %get-tuple-element.65), channel_id=1, source_target_pairs={{0,1},{1,0},{2,3},{3,2},{4,5},{5,4},{6,7},{7,6},{8,9},{9,8},{10,11... | collective-permute-start | bytes 393224 | tf_op jit(solution)/shard_map/ppermute | solution.py:30
  45.5 1.5 %collective-permute-start.19 = (bf16[2,32,1024]{2,1,0:T(8,128)(2,1)S(1)}, bf16[2,32,1024]{2,1,0:T(8,128)(2,1)S(1)}, u32[]{:S(2)}, u32[]{:S(2)}) collective-permute-start(bf16[2,32,1024]{2,1,0:T(8,128)(2,1)S(1)} %get-tuple-element.66), channel_id=1, source_target_pairs={{0,1},{1,0},{2,3},{3,2},{4,5},{5,4},{6,7},{7,6},{8,9},{9,8},{10,11... | collective-permute-start | bytes 393224 | tf_op jit(solution)/shard_map/ppermute | solution.py:30
  47.7 8.6 %collective-permute-start.20 = (bf16[128,1024]{1,0:T(8,128)(2,1)S(1)}, bf16[128,1024]{1,0:T(8,128)(2,1)S(1)}, u32[]{:S(2)}, u32[]{:S(2)}) collective-permute-start(bf16[128,1024]{1,0:T(8,128)(2,1)S(1)} %get-tuple-element.68), channel_id=1, source_target_pairs={{0,2},{2,0},{1,3},{3,1},{4,6},{6,4},{5,7},{7,5},{8,10},{10,8},{9,1... | collective-permute-start | bytes 786440 | tf_op jit(solution)/shard_map/ppermute | solution.py:30
  57.0 3.1 %collective-permute-start.23 = (f32[8,128]{1,0:T(8,128)S(1)}, f32[8,128]{1,0:T(8,128)S(1)}, u32[]{:S(2)}, u32[]{:S(2)}) collective-permute-start(f32[8,128]{1,0:T(8,128)S(1)} %get-tuple-element.69.refs_0_.refs_1_), channel_id=1, source_target_pairs={{0,3},{1,2},{2,1},{3,0},{4,7},{5,6},{6,5},{7,4},{8,11},{9,10},{10,... | collective-permute-start | bytes 12296 | tf_op jit(solution)/shard_map/ppermute | solution.py:30
  57.7 3.6 %collective-permute-start.22 = (f32[8,128]{1,0:T(8,128)S(1)}, f32[8,128]{1,0:T(8,128)S(1)}, u32[]{:S(2)}, u32[]{:S(2)}) collective-permute-start(f32[8,128]{1,0:T(8,128)S(1)} %get-tuple-element.69.refs_0_.refs_1_), channel_id=1, source_target_pairs={{0,2},{1,3},{2,0},{3,1},{4,6},{5,7},{6,4},{7,5},{8,10},{9,11},{10,... | collective-permute-start | bytes 12296 | tf_op jit(solution)/shard_map/ppermute | solution.py:30
  58.6 2.7 %collective-permute-start.21 = (f32[8,128]{1,0:T(8,128)S(1)}, f32[8,128]{1,0:T(8,128)S(1)}, u32[]{:S(2)}, u32[]{:S(2)}) collective-permute-start(f32[8,128]{1,0:T(8,128)S(1)} %get-tuple-element.69.refs_0_.refs_1_), channel_id=1, source_target_pairs={{0,1},{1,0},{2,3},{3,2},{4,5},{5,4},{6,7},{7,6},{8,9},{9,8},{10,11... | collective-permute-start | bytes 12296 | tf_op jit(solution)/shard_map/ppermute | solution.py:30
  62.1 9.4 %collective-permute-start.25 = (bf16[64,1024]{1,0:T(8,128)(2,1)S(1)}, bf16[64,1024]{1,0:T(8,128)(2,1)S(1)}, u32[]{:S(2)}, u32[]{:S(2)}) collective-permute-start(bf16[64,1024]{1,0:T(8,128)(2,1)S(1)} %get-tuple-element.73), channel_id=1, source_target_pairs={{0,12},{4,8},{8,4},{12,0},{1,13},{5,9},{9,5},{13,1},{2,14},{6,10},... | collective-permute-start | bytes 393224 | tf_op jit(solution)/shard_map/ppermute | solution.py:30
  64.3 13.6 %collective-permute-start.24 = (bf16[64,1024]{1,0:T(8,128)(2,1)S(1)}, bf16[64,1024]{1,0:T(8,128)(2,1)S(1)}, u32[]{:S(2)}, u32[]{:S(2)}) collective-permute-start(bf16[64,1024]{1,0:T(8,128)(2,1)S(1)} %get-tuple-element.72.refs_0_), channel_id=1, source_target_pairs={{0,8},{4,12},{8,0},{12,4},{1,9},{5,13},{9,1},{13,5},{2,10},{6,14},... | collective-permute-start | bytes 393224 | tf_op jit(solution)/shard_map/ppermute | solution.py:30
  68.3 9.6 %collective-permute-start.26 = (bf16[64,1024]{1,0:T(8,128)(2,1)S(1)}, bf16[64,1024]{1,0:T(8,128)(2,1)S(1)}, u32[]{:S(2)}, u32[]{:S(2)}) collective-permute-start(bf16[64,1024]{1,0:T(8,128)(2,1)S(1)} %get-tuple-element.75), channel_id=1, source_target_pairs={{0,4},{4,0},{8,12},{12,8},{1,5},{5,1},{9,13},{13,9},{2,6},{6,2},{1... | collective-permute-start | bytes 393224 | tf_op jit(solution)/shard_map/ppermute | solution.py:30
  (1 other events, 0.7 us)

commit v11 on v10

--- a/solution.py
+++ b/solution.py
@@ -273,38 +273,54 @@
     )(weight, *after, *rows, own)
 
 
-def lags_kernel(geometry, skip, scal, *refs):
+def lags_kernel(geometry, split, skip, scal, *refs):
     classes, span, outputs, origin, period, chunk = geometry
-    lhs, table, keep, *sends, sums = refs[skip:]
+    lhs, table, keep, *refs = refs[skip:]
+    sends, sums = refs[:split], refs[split:]
     rows = lhs.shape[1] // 2
     lag_dev = keep.shape[-1]
     cores = 2
+    at_once = span == lag_dev
+    first = scal[CORE] == 0
     for start in range(0, span, chunk):
         values = []
         for r in range(classes):
-            y = jnp.dot(lhs[r], table[r, :, start : start + chunk], preferred_element_type=F32)
-            values.append((y[:rows], y[rows:]))
-        for k, value in enumerate(combine(values, classes, outputs, origin, span, period)):
+            whole_turns = all(
+                r * (span * k - origin) * 2 % period == 0 for k in range(outputs)
+            )
+            left = lhs[r, :rows] if whole_turns else lhs[r]
+            y = jnp.dot(left, table[r, :, start : start + chunk], preferred_element_type=F32)
+            values.append((y[:rows], None if whole_turns else y[rows:]))
+        corr = combine(values, classes, outputs, origin, span, period)
+        lags = slice(start, start + chunk)
+        for column in range(keep.shape[0]) if at_once else ():
+            even, odd = corr[2 * column], corr[2 * column + 1]
+            keep[column, :, lags] = jnp.where(first, even, odd)
+            other = jnp.where(first, odd, even).astype(BF16)
+            for i, out in enumerate(sends):
+                out[column, :, lags] = other[i * out.shape[1] : (i + 1) * out.shape[1]]
+        for k, value in enumerate(corr) if not at_once else ():
             lag = span * k + start
-            lags = slice(lag % lag_dev, lag % lag_dev + chunk)
-            sums[lag // lag_dev, :, lags] = value
+            sums[0][lag // lag_dev, :, lag % lag_dev : lag % lag_dev + chunk] = value
+    if at_once:
+        return
     for column in range(keep.shape[0]):
-        keep[column] = sums[cores * column + scal[CORE]]
+        keep[column] = sums[0][cores * column + scal[CORE]]
         for i, out in enumerate(sends):
             at = slice(i * out.shape[1], (i + 1) * out.shape[1])
-            out[column] = sums[cores * column + 1 - scal[CORE], at].astype(BF16)
+            out[column] = sums[0][cores * column + 1 - scal[CORE], at].astype(BF16)
 
 
 def lag_parts(scal, after, lhs, table, geometry, columns, lag_dev, split, effort):
     rows = lhs.shape[1] // 2
     shape = lambda count: (columns, count, lag_dev)
     return pl.pallas_call(
-        functools.partial(lags_kernel, geometry, len(after)),
+        functools.partial(lags_kernel, geometry, split, len(after)),
         out_shape=[jax.ShapeDtypeStruct(shape(rows), F32)]
         + [jax.ShapeDtypeStruct(shape(rows // split), BF16)] * split,
         in_specs=[SMEM] + [ANY] * len(after) + [VMEM] * 2,
         out_specs=[VMEM] * (split + 1),
-        scratch_shapes=[pltpu.VMEM((2 * columns, rows, lag_dev), F32)],
+        scratch_shapes=[pltpu.VMEM((2 * columns, rows, lag_dev), F32)] * (geometry[1] != lag_dev),
         compiler_params=params(16),
         cost_estimate=effort,
         name="lags",
@@ -543,7 +559,7 @@
     if direct and blocks == 4:
         chunks = [
             [(0, 0, slots), (1, 0, slots)],
-            [(2, 0, slots), (3, 0, slots)],
+            [(3, 0, slots), (2, 0, slots)],
         ]
     else:
         chunks = [[(d, first, some) for d in range(blocks)] for first in (0, some)]

time: 79.2 us -> 80.9 us (1.021)
  waiting for transfers between devices: 28.5 us -> 33 us
  starting transfers between devices: 25.3 us -> 22.7 us
    ppermute x27, waiting for transfers between devices: 28.5 us -> 33 us  [swapped(): return lax.ppermute(value, axis, [(i, i ^ step) for i in range(size)])]
    ppermute x27, starting transfers between devices: 25.3 us -> 22.7 us  [swapped(): return lax.ppermute(value, axis, [(i, i ^ step) for i in range(size)])]
  transfers between devices with their start and end apart: 27 -> 27, of which waited for: 15 -> 16; matrix products, arithmetic and copies ran while one was open for 0% -> 0% of each run, Pallas kernels for 18% -> 18%
where the time goes in v11:
time: 80.9 us; the launch traced here: 80.7 us
  waiting for transfers between devices  33 us (41%)
  starting transfers between devices  22.7 us (28%)
  Pallas kernels  19.5 us (24%)
  local copies, waits for them, and re-layouts  4.02 us (5%)
  between operations  1.48 us (2%)
    ppermute x27, waiting for transfers between devices, swapped(): return lax.ppermute(value, axis, [(i, i ^ step) for i in range(size)])  33 us
    ppermute x27, starting transfers between devices, swapped(): return lax.ppermute(value, axis, [(i, i ^ step) for i in range(size)])  22.7 us
    pallas_call x2, Pallas kernels, lag_parts(): pl.pallas_call(functools.partial(lags_kernel, geometry, split, len(after)...  4.85 us
    pallas_call x1, Pallas kernels, normed_rows(): pl.pallas_call(functools.partial(normed_kernel, lag_total, chunks, len(su...  2.94 us
    unnamed x12, local copies, waits for them, and re-layouts  2.68 us
    pallas_call x1, Pallas kernels, gather_rows(): pl.pallas_call(functools.partial(rows_kernel, used, sends, messages), out...  1.82 us
    pallas_call x1, Pallas kernels, make_table(): pl.pallas_call(functools.partial(table_kernel, classes, parts), out_shape...  1.78 us
  transfers between devices with their start and end apart: 27, of which 16 were waited for; matrix products, arithmetic and copies ran while one was open for 0% of the time, Pallas kernels for 18%

profile of v11, /device:TPU:0, one launch (start us, length us, event | category | flops | bytes accessed | tf_op | source)
XLA Modules:
  0.0 80.7 jit_solution(4032489093780006371)
XLA Ops:
  0.7 1.3 %constant_dynamic-slice_fusion = (bf16[1,2,128,1024]{3,2,1,0:T(8,128)(2,1)S(1)}, bf16[1,2,128,1024]{3,2,1,0:T(8,128)(2,1)S(1)}) fusion(bf16[1,2,128,2048]{3,2,1,0:T(8,128)(2,1)} %param.8, s32[]{:T(128)S(6)} %select_n.7, s32[]{:T(128)S(6)} %select_n.6), kind=kLoop, calls=%fused_computation | loop fusion | bytes 2097160 | tf_op jit(solution)/shard_map/dynamic_slice | solution.py:535
  2.0 3.0 %collective-permute-start = (bf16[1,2,128,1024]{3,2,1,0:T(8,128)(2,1)S(1)}, bf16[1,2,128,1024]{3,2,1,0:T(8,128)(2,1)S(1)}, u32[]{:S(2)}, u32[]{:S(2)}) collective-permute-start(bf16[1,2,128,1024]{3,2,1,0:T(8,128)(2,1)S(1)} %get-tuple-element.76), channel_id=1, source_target_pairs={{0,2},{2,0},{1,3},{3,1},{4,6},{6,4},{5,7},{7,5},{8,10},{10,8},{9,1... | collective-permute-start | bytes 1572872 | tf_op jit(solution)/shard_map/ppermute | solution.py:30
  8.3 1.2 %index.1 = (s32[128]{0:T(128)S(1)}, s32[1,64]{1,0:T(1,128)S(1)}, s32[1,64]{1,0:T(1,128)S(1)}, s32[1,64]{1,0:T(1,128)S(1)}, s32[1,64]{1,0:T(1,128)S(1)}, /*index=5*/s32[4,64]{1,0:T(4,128)S(1)}) custom-call(s32[1]{0:T(128)S(6)} %copy.10.refs_0_, s32[4]{0:T(128)S(1)} %copy-done.4, s32[4]{0:T(128)S(1)} %bitcast.1, s32[4,64]{1,0:T(4,128)S(1)} %copy-done.2, ...), custom_call_target="tpu_custom_call" | custom-call | flops 1 | bytes 1 | tf_op jit(solution)/shard_map/index/pallas_call | solution.py:93
  9.6 3.7 %collective-permute-start.1 = (s32[1,64]{1,0:T(1,128)S(1)}, s32[1,64]{1,0:T(1,128)S(1)}, u32[]{:S(2)}, u32[]{:S(2)}) collective-permute-start(s32[1,64]{1,0:T(1,128)S(1)} %get-tuple-element.40), channel_id=1, source_target_pairs={{0,12},{4,8},{8,4},{12,0},{1,13},{5,9},{9,5},{13,1},{2,14},{6,10},... | collective-permute-start | bytes 776 | tf_op jit(solution)/shard_map/ppermute | solution.py:30
  13.2 0.8 collective-permute-start.3
  14.6 1.8 %table.1.after.refs_1_ = bf16[8,256,1024]{2,1,0:T(8,128)(2,1)S(1)} custom-call(s32[128]{0:T(128)S(1)} %get-tuple-element.39.scal, f32[2,56,1024]{2,1,0:T(8,128)S(1)} %copy-done.1), custom_call_target="tpu_custom_call" | custom-call | flops 1 | bytes 1 | tf_op jit(solution)/shard_map/table/pallas_call | solution.py:127
  16.4 1.2 %collective-permute-done.2.refs_3_.refs_1_ = s32[1,64]{1,0:T(1,128)S(1)} collective-permute-done((s32[1,64]{1,0:T(1,128)S(1)}, s32[1,64]{1,0:T(1,128)S(1)}, u32[]{:S(2)}, u32[]{:S(2)}) %collective-permute-start.2) | collective-permute-done | bytes 288 | tf_op jit(solution)/shard_map/ppermute | solution.py:30
  17.7 1.8 %rows.1 = (bf16[1,2,64,1024]{3,2,1,0:T(8,128)(2,1)S(1)}, bf16[1,2,64,1024]{3,2,1,0:T(8,128)(2,1)S(1)}, bf16[1,2,64,1024]{3,2,1,0:T(8,128)(2,1)S(1)}, bf16[1,2,64...) custom-call(s32[128]{0:T(128)S(1)} %get-tuple-element.39.scal, bf16[8,256,1024]{2,1,0:T(8,128)(2,1)S(1)} %table.1.after.refs_1_, ...), custom_call_target="tpu_custom_call" | custom-call | flops 1 | bytes 1 | tf_op jit(solution)/shard_map/rows/pallas_call | solution.py:192
  19.5 1.1 %collective-permute-start.4 = (bf16[1,2,64,1024]{3,2,1,0:T(8,128)(2,1)S(1)}, bf16[1,2,64,1024]{3,2,1,0:T(8,128)(2,1)S(1)}, u32[]{:S(2)}, u32[]{:S(2)}) collective-permute-start(bf16[1,2,64,1024]{3,2,1,0:T(8,128)(2,1)S(1)} %get-tuple-element.46), channel_id=1, source_target_pairs={{0,4},{4,0},{8,12},{12,8},{1,5},{5,1},{9,13},{13,9},{2,6},{6,2},{1... | collective-permute-start | bytes 786440 | tf_op jit(solution)/shard_map/ppermute | solution.py:30
  20.6 2.5 %collective-permute-start.14 = (bf16[1,2,64,1024]{3,2,1,0:T(8,128)(2,1)S(1)}, bf16[1,2,64,1024]{3,2,1,0:T(8,128)(2,1)S(1)}, u32[]{:S(2)}, u32[]{:S(2)}) collective-permute-start(bf16[1,2,64,1024]{3,2,1,0:T(8,128)(2,1)S(1)} %get-tuple-element.60), channel_id=1, source_target_pairs={{0,12},{4,8},{8,4},{12,0},{1,13},{5,9},{9,5},{13,1},{2,14},{6,10},... | collective-permute-start | bytes 786440 | tf_op jit(solution)/shard_map/ppermute | solution.py:30
  23.2 4.2 %collective-permute-done.4.refs_1_ = bf16[1,2,64,1024]{3,2,1,0:T(8,128)(2,1)S(1)} collective-permute-done((bf16[1,2,64,1024]{3,2,1,0:T(8,128)(2,1)S(1)}, bf16[1,2,64,1024]{3,2,1,0:T(8,128)(2,1)S(1)}, u32[]{:S(2)}, u32[]{:S(2)}) %collective-permute-start.4) | collective-permute-done | bytes 262176 | tf_op jit(solution)/shard_map/ppermute | solution.py:30
  27.7 2.4 %lags.2 = (f32[2,128,1024]{2,1,0:T(8,128)S(1)}, bf16[2,16,1024]{2,1,0:T(8,128)(2,1)S(1)}, bf16[2,16,1024]{2,1,0:T(8,128)(2,1)S(1)}, bf16[2,16,1024]{2,1,0:T(8,12...) custom-call(s32[128]{0:T(128)S(1)} %get-tuple-element.39.scal, ...), custom_call_target="tpu_custom_call" | custom-call | flops 20000000000 | bytes 1048576 | tf_op jit(solution)/shard_map/lags/pallas_call | solution.py:317
  33.2 0.7 collective-permute-done.11.refs_7_
  34.1 0.8 %cores.2 = (f32[128,1024]{1,0:T(8,128)S(1)}, bf16[128,1024]{1,0:T(8,128)(2,1)S(1)}) custom-call(s32[128]{0:T(128)S(1)} %get-tuple-element.39.scal, f32[2,128,1024]{2,1,0:T(8,128)S(1)} %get-tuple-element.48.refs_0_, bf16[2,16,1024]{2,1,0:T(8,128)(2,1)S(1)} %collective-permute-done.5.refs_1_, bf16[2,16,1024]{2,1,0:T(8,128)(2,1)S(1)} %collective-permute-done.6.refs_2_, ...), custom_call_target="tpu_custom_call" | custom-call | flops 1 | bytes 1 | tf_op jit(solution)/shard_map/cores/pallas_call | solution.py:352
  34.9 1.5 %collective-permute-start.13 = (bf16[128,1024]{1,0:T(8,128)(2,1)S(1)}, bf16[128,1024]{1,0:T(8,128)(2,1)S(1)}, u32[]{:S(2)}, u32[]{:S(2)}) collective-permute-start(bf16[128,1024]{1,0:T(8,128)(2,1)S(1)} %get-tuple-element.58), channel_id=1, source_target_pairs={{0,2},{2,0},{1,3},{3,1},{4,6},{6,4},{5,7},{7,5},{8,10},{10,8},{9,1... | collective-permute-start | bytes 786440 | tf_op jit(solution)/shard_map/ppermute | solution.py:30
  36.5 8.8 %collective-permute-done.15.refs_2_ = bf16[1,2,64,1024]{3,2,1,0:T(8,128)(2,1)S(1)} collective-permute-done((bf16[1,2,64,1024]{3,2,1,0:T(8,128)(2,1)S(1)}, bf16[1,2,64,1024]{3,2,1,0:T(8,128)(2,1)S(1)}, u32[]{:S(2)}, u32[]{:S(2)}) %collective-permute-start.15) | collective-permute-done | bytes 262176 | tf_op jit(solution)/shard_map/ppermute | solution.py:30
  45.5 2.4 %lags.3 = (f32[2,128,1024]{2,1,0:T(8,128)S(1)}, bf16[2,32,1024]{2,1,0:T(8,128)(2,1)S(1)}, bf16[2,32,1024]{2,1,0:T(8,128)(2,1)S(1)}, bf16[2,32,1024]{2,1,0:T(8,128)(2,1)S(1)}, bf16[2,32,1024]{2,1,0:T(8,128)(2,1)S(1)}) custom-call(s32[128]{0:T(128)S(1)} %get-tuple-element.39.scal, bf16[8,256,256]{2,1,0:T(8,128)(2,1)S(1)} %cross.3.refs_0_, ...), custom_call_target="tpu_custom_call" | custom-call | flops 1 | bytes 1 | tf_op jit(solution)/shard_map/lags/pallas_call | solution.py:317
  50.8 1.6 %collective-permute-start.20 = (bf16[128,1024]{1,0:T(8,128)(2,1)S(1)}, bf16[128,1024]{1,0:T(8,128)(2,1)S(1)}, u32[]{:S(2)}, u32[]{:S(2)}) collective-permute-start(bf16[128,1024]{1,0:T(8,128)(2,1)S(1)} %get-tuple-element.68), channel_id=1, source_target_pairs={{0,2},{2,0},{1,3},{3,1},{4,6},{6,4},{5,7},{7,5},{8,10},{10,8},{9,1... | collective-permute-start | bytes 786440 | tf_op jit(solution)/shard_map/ppermute | solution.py:30
  52.3 0.8 stats.2
  53.1 6.3 %collective-permute-done.20.refs_2_ = bf16[128,1024]{1,0:T(8,128)(2,1)S(1)} collective-permute-done((bf16[128,1024]{1,0:T(8,128)(2,1)S(1)}, bf16[128,1024]{1,0:T(8,128)(2,1)S(1)}, u32[]{:S(2)}, u32[]{:S(2)}) %collective-permute-start.20) | collective-permute-done | bytes 262176 | tf_op jit(solution)/shard_map/ppermute | solution.py:30
  59.4 0.8 stats.3
  60.8 1.0 %collective-permute-start.22 = (f32[8,128]{1,0:T(8,128)S(1)}, f32[8,128]{1,0:T(8,128)S(1)}, u32[]{:S(2)}, u32[]{:S(2)}) collective-permute-start(f32[8,128]{1,0:T(8,128)S(1)} %get-tuple-element.69.refs_0_.refs_1_), channel_id=1, source_target_pairs={{0,2},{1,3},{2,0},{3,1},{4,6},{5,7},{6,4},{7,5},{8,10},{9,11},{10,... | collective-permute-start | bytes 12296 | tf_op jit(solution)/shard_map/ppermute | solution.py:30
  62.1 1.2 %collective-permute-done.23.refs_3_.refs_4_ = f32[8,128]{1,0:T(8,128)S(1)} collective-permute-done((f32[8,128]{1,0:T(8,128)S(1)}, f32[8,128]{1,0:T(8,128)S(1)}, u32[]{:S(2)}, u32[]{:S(2)}) %collective-permute-start.23) | collective-permute-done | bytes 4128 | tf_op jit(solution)/shard_map/ppermute | solution.py:30
  63.2 1.2 %collective-permute-done.22.refs_2_.refs_3_ = f32[8,128]{1,0:T(8,128)S(1)} collective-permute-done((f32[8,128]{1,0:T(8,128)S(1)}, f32[8,128]{1,0:T(8,128)S(1)}, u32[]{:S(2)}, u32[]{:S(2)}) %collective-permute-start.22) | collective-permute-done | bytes 4128 | tf_op jit(solution)/shard_map/ppermute | solution.py:30
  64.4 0.8 gradient.2
  65.3 2.7 %collective-permute-start.24 = (bf16[64,1024]{1,0:T(8,128)(2,1)S(1)}, bf16[64,1024]{1,0:T(8,128)(2,1)S(1)}, u32[]{:S(2)}, u32[]{:S(2)}) collective-permute-start(bf16[64,1024]{1,0:T(8,128)(2,1)S(1)} %get-tuple-element.72.refs_0_), channel_id=1, source_target_pairs={{0,12},{4,8},{8,4},{12,0},{1,13},{5,9},{9,5},{13,1},{2,14},{6,10},... | collective-permute-start | bytes 393224 | tf_op jit(solution)/shard_map/ppermute | solution.py:30
  68.0 0.8 %gradient.3 = (bf16[64,1024]{1,0:T(8,128)(2,1)S(1)}, bf16[64,1024]{1,0:T(8,128)(2,1)S(1)}) custom-call(s32[128]{0:T(128)S(1)} %get-tuple-element.39.scal, bf16[64,1024]{1,0:T(8,128)(2,1)S(1)} %get-tuple-element.72.refs_0_, f32[8,128]{1,0:T(8,128)S(1)} %get-tuple-element.69.refs_0_.refs_1_, f32[8,128]{1,0:T(8,128)S(1)} %collective-permute-done.21.refs_1_.refs_2_, ...), custom_call_target="tpu_custom_call" | custom-call | flops 1 | bytes 1 | tf_op jit(solution)/shard_map/gradient/pallas_call | solution.py:448
  68.8 0.8 %collective-permute-start.26 = (bf16[64,1024]{1,0:T(8,128)(2,1)S(1)}, bf16[64,1024]{1,0:T(8,128)(2,1)S(1)}, u32[]{:S(2)}, u32[]{:S(2)}) collective-permute-start(bf16[64,1024]{1,0:T(8,128)(2,1)S(1)} %get-tuple-element.75), channel_id=1, source_target_pairs={{0,4},{4,0},{8,12},{12,8},{1,5},{5,1},{9,13},{13,9},{2,6},{6,2},{1... | collective-permute-start | bytes 393224 | tf_op jit(solution)/shard_map/ppermute | solution.py:30
  69.7 2.9 %normed.1 = f32[4,64,1024]{2,1,0:T(8,128)} custom-call(s32[128]{0:T(128)S(1)} %get-tuple-element.39.scal, f32[8,128]{1,0:T(8,128)S(1)} %get-tuple-element.69.refs_0_.refs_1_, f32[8,128]{1,0:T(8,128)S(1)} %collective-permute-done.21.refs_1_.refs_2_, f32[8,128]{1,0:T(8,128)S(1)} %collective-permute-done.22.refs_2_.refs_3_, ...), custom_call_target="tpu_custom_call" | custom-call | flops 1 | bytes 1 | tf_op jit(solution)/shard_map/normed/pallas_call | solution.py:480
  72.6 4.9 %collective-permute-done.25.refs_5_ = bf16[64,1024]{1,0:T(8,128)(2,1)S(1)} collective-permute-done((bf16[64,1024]{1,0:T(8,128)(2,1)S(1)}, bf16[64,1024]{1,0:T(8,128)(2,1)S(1)}, u32[]{:S(2)}, u32[]{:S(2)}) %collective-permute-start.25) | collective-permute-done | bytes 131104 | tf_op jit(solution)/shard_map/ppermute | solution.py:30
  77.5 2.2 %collective-permute-done.26.refs_7_ = bf16[64,1024]{1,0:T(8,128)(2,1)S(1)} collective-permute-done((bf16[64,1024]{1,0:T(8,128)(2,1)S(1)}, bf16[64,1024]{1,0:T(8,128)(2,1)S(1)}, u32[]{:S(2)}, u32[]{:S(2)}) %collective-permute-start.26) | collective-permute-done | bytes 131104 | tf_op jit(solution)/shard_map/ppermute | solution.py:30
  79.7 1.1 %adjoint.1 = f32[128,1024]{1,0:T(8,128)} custom-call(s32[1,64]{1,0:T(1,128)S(1)} %collective-permute-done.1.refs_2_.refs_0_, s32[1,64]{1,0:T(1,128)S(1)} %collective-permute-done.2.refs_3_.refs_1_, s32[1,64]{1,0:T(1,128)S(1)} %get-tuple-element.43.refs_5_.refs_2_, s32[1,64]{1,0:T(1,128)S(1)} %collective-permute-done.3.refs_4_.refs_3_, ...), custom_call_target="tpu_custom_call" | custom-call | flops 1 | bytes 1 | tf_op jit(solution)/shard_map/adjoint/pallas_call | solution.py:504
  (51 shorter events, 11.0 us)
Async XLA Ops:
  0.6 14.0 %copy-start.1 = (f32[2,56,1024]{2,1,0:T(8,128)S(1)}, f32[2,56,1024]{2,1,0:T(8,128)}, u32[]{:S(2)}) copy-start(f32[2,56,1024]{2,1,0:T(8,128)} %constant.16.clone.trig) | copy-start | bytes 1376260
  2.0 15.7 %collective-permute-start = (bf16[1,2,128,1024]{3,2,1,0:T(8,128)(2,1)S(1)}, bf16[1,2,128,1024]{3,2,1,0:T(8,128)(2,1)S(1)}, u32[]{:S(2)}, u32[]{:S(2)}) collective-permute-start(bf16[1,2,128,1024]{3,2,1,0:T(8,128)(2,1)S(1)} %get-tuple-element.76), channel_id=1, source_target_pairs={{0,2},{2,0},{1,3},{3,1},{4,6},{6,4},{5,7},{7,5},{8,10},{10,8},{9,1... | collective-permute-start | bytes 1572872 | tf_op jit(solution)/shard_map/ppermute | solution.py:30
  5.7 0.7 copy-start.2
  6.3 0.7 copy-start.3
  7.0 0.7 copy-start.4
  9.6 6.9 %collective-permute-start.1 = (s32[1,64]{1,0:T(1,128)S(1)}, s32[1,64]{1,0:T(1,128)S(1)}, u32[]{:S(2)}, u32[]{:S(2)}) collective-permute-start(s32[1,64]{1,0:T(1,128)S(1)} %get-tuple-element.40), channel_id=1, source_target_pairs={{0,12},{4,8},{8,4},{12,0},{1,13},{5,9},{9,5},{13,1},{2,14},{6,10},... | collective-permute-start | bytes 776 | tf_op jit(solution)/shard_map/ppermute | solution.py:30
  13.2 4.4 %collective-permute-start.2 = (s32[1,64]{1,0:T(1,128)S(1)}, s32[1,64]{1,0:T(1,128)S(1)}, u32[]{:S(2)}, u32[]{:S(2)}) collective-permute-start(s32[1,64]{1,0:T(1,128)S(1)} %get-tuple-element.41), channel_id=1, source_target_pairs={{0,8},{4,12},{8,0},{12,4},{1,9},{5,13},{9,1},{13,5},{2,10},{6,14},... | collective-permute-start | bytes 776 | tf_op jit(solution)/shard_map/ppermute | solution.py:30
  13.2 4.4 %collective-permute-start.3 = (s32[1,64]{1,0:T(1,128)S(1)}, s32[1,64]{1,0:T(1,128)S(1)}, u32[]{:S(2)}, u32[]{:S(2)}) collective-permute-start(s32[1,64]{1,0:T(1,128)S(1)} %get-tuple-element.42), channel_id=1, source_target_pairs={{0,4},{4,0},{8,12},{12,8},{1,5},{5,1},{9,13},{13,9},{2,6},{6,2},{1... | collective-permute-start | bytes 776 | tf_op jit(solution)/shard_map/ppermute | solution.py:30
  19.5 7.9 %collective-permute-start.4 = (bf16[1,2,64,1024]{3,2,1,0:T(8,128)(2,1)S(1)}, bf16[1,2,64,1024]{3,2,1,0:T(8,128)(2,1)S(1)}, u32[]{:S(2)}, u32[]{:S(2)}) collective-permute-start(bf16[1,2,64,1024]{3,2,1,0:T(8,128)(2,1)S(1)} %get-tuple-element.46), channel_id=1, source_target_pairs={{0,4},{4,0},{8,12},{12,8},{1,5},{5,1},{9,13},{13,9},{2,6},{6,2},{1... | collective-permute-start | bytes 786440 | tf_op jit(solution)/shard_map/ppermute | solution.py:30
  20.6 15.8 %collective-permute-start.14 = (bf16[1,2,64,1024]{3,2,1,0:T(8,128)(2,1)S(1)}, bf16[1,2,64,1024]{3,2,1,0:T(8,128)(2,1)S(1)}, u32[]{:S(2)}, u32[]{:S(2)}) collective-permute-start(bf16[1,2,64,1024]{3,2,1,0:T(8,128)(2,1)S(1)} %get-tuple-element.60), channel_id=1, source_target_pairs={{0,12},{4,8},{8,4},{12,0},{1,13},{5,9},{9,5},{13,1},{2,14},{6,10},... | collective-permute-start | bytes 786440 | tf_op jit(solution)/shard_map/ppermute | solution.py:30
  23.1 22.1 %collective-permute-start.15 = (bf16[1,2,64,1024]{3,2,1,0:T(8,128)(2,1)S(1)}, bf16[1,2,64,1024]{3,2,1,0:T(8,128)(2,1)S(1)}, u32[]{:S(2)}, u32[]{:S(2)}) collective-permute-start(bf16[1,2,64,1024]{3,2,1,0:T(8,128)(2,1)S(1)} %get-tuple-element.61), channel_id=1, source_target_pairs={{0,8},{4,12},{8,0},{12,4},{1,9},{5,13},{9,1},{13,5},{2,10},{6,14},... | collective-permute-start | bytes 786440 | tf_op jit(solution)/shard_map/ppermute | solution.py:30
  30.1 1.3 %collective-permute-start.5 = (bf16[2,16,1024]{2,1,0:T(8,128)(2,1)S(1)}, bf16[2,16,1024]{2,1,0:T(8,128)(2,1)S(1)}, u32[]{:S(2)}, u32[]{:S(2)}) collective-permute-start(bf16[2,16,1024]{2,1,0:T(8,128)(2,1)S(1)} %get-tuple-element.49), channel_id=1, source_target_pairs={{0,1},{1,0},{2,3},{3,2},{4,5},{5,4},{6,7},{7,6},{8,9},{9,8},{10,11... | collective-permute-start | bytes 196616 | tf_op jit(solution)/shard_map/ppermute | solution.py:30
  30.2 1.4 %collective-permute-start.6 = (bf16[2,16,1024]{2,1,0:T(8,128)(2,1)S(1)}, bf16[2,16,1024]{2,1,0:T(8,128)(2,1)S(1)}, u32[]{:S(2)}, u32[]{:S(2)}) collective-permute-start(bf16[2,16,1024]{2,1,0:T(8,128)(2,1)S(1)} %get-tuple-element.50), channel_id=1, source_target_pairs={{0,1},{1,0},{2,3},{3,2},{4,5},{5,4},{6,7},{7,6},{8,9},{9,8},{10,11... | collective-permute-start | bytes 196616 | tf_op jit(solution)/shard_map/ppermute | solution.py:30
  30.7 1.3 %collective-permute-start.7 = (bf16[2,16,1024]{2,1,0:T(8,128)(2,1)S(1)}, bf16[2,16,1024]{2,1,0:T(8,128)(2,1)S(1)}, u32[]{:S(2)}, u32[]{:S(2)}) collective-permute-start(bf16[2,16,1024]{2,1,0:T(8,128)(2,1)S(1)} %get-tuple-element.51), channel_id=1, source_target_pairs={{0,1},{1,0},{2,3},{3,2},{4,5},{5,4},{6,7},{7,6},{8,9},{9,8},{10,11... | collective-permute-start | bytes 196616 | tf_op jit(solution)/shard_map/ppermute | solution.py:30
  31.4 1.3 %collective-permute-start.8 = (bf16[2,16,1024]{2,1,0:T(8,128)(2,1)S(1)}, bf16[2,16,1024]{2,1,0:T(8,128)(2,1)S(1)}, u32[]{:S(2)}, u32[]{:S(2)}) collective-permute-start(bf16[2,16,1024]{2,1,0:T(8,128)(2,1)S(1)} %get-tuple-element.52), channel_id=1, source_target_pairs={{0,1},{1,0},{2,3},{3,2},{4,5},{5,4},{6,7},{7,6},{8,9},{9,8},{10,11... | collective-permute-start | bytes 196616 | tf_op jit(solution)/shard_map/ppermute | solution.py:30
  31.6 1.3 %collective-permute-start.9 = (bf16[2,16,1024]{2,1,0:T(8,128)(2,1)S(1)}, bf16[2,16,1024]{2,1,0:T(8,128)(2,1)S(1)}, u32[]{:S(2)}, u32[]{:S(2)}) collective-permute-start(bf16[2,16,1024]{2,1,0:T(8,128)(2,1)S(1)} %get-tuple-element.53), channel_id=1, source_target_pairs={{0,1},{1,0},{2,3},{3,2},{4,5},{5,4},{6,7},{7,6},{8,9},{9,8},{10,11... | collective-permute-start | bytes 196616 | tf_op jit(solution)/shard_map/ppermute | solution.py:30
  32.0 1.3 %collective-permute-start.10 = (bf16[2,16,1024]{2,1,0:T(8,128)(2,1)S(1)}, bf16[2,16,1024]{2,1,0:T(8,128)(2,1)S(1)}, u32[]{:S(2)}, u32[]{:S(2)}) collective-permute-start(bf16[2,16,1024]{2,1,0:T(8,128)(2,1)S(1)} %get-tuple-element.54), channel_id=1, source_target_pairs={{0,1},{1,0},{2,3},{3,2},{4,5},{5,4},{6,7},{7,6},{8,9},{9,8},{10,11... | collective-permute-start | bytes 196616 | tf_op jit(solution)/shard_map/ppermute | solution.py:30
  32.7 1.3 %collective-permute-start.11 = (bf16[2,16,1024]{2,1,0:T(8,128)(2,1)S(1)}, bf16[2,16,1024]{2,1,0:T(8,128)(2,1)S(1)}, u32[]{:S(2)}, u32[]{:S(2)}) collective-permute-start(bf16[2,16,1024]{2,1,0:T(8,128)(2,1)S(1)} %get-tuple-element.55), channel_id=1, source_target_pairs={{0,1},{1,0},{2,3},{3,2},{4,5},{5,4},{6,7},{7,6},{8,9},{9,8},{10,11... | collective-permute-start | bytes 196616 | tf_op jit(solution)/shard_map/ppermute | solution.py:30
  32.9 1.3 %collective-permute-start.12 = (bf16[2,16,1024]{2,1,0:T(8,128)(2,1)S(1)}, bf16[2,16,1024]{2,1,0:T(8,128)(2,1)S(1)}, u32[]{:S(2)}, u32[]{:S(2)}) collective-permute-start(bf16[2,16,1024]{2,1,0:T(8,128)(2,1)S(1)} %get-tuple-element.56), channel_id=1, source_target_pairs={{0,1},{1,0},{2,3},{3,2},{4,5},{5,4},{6,7},{7,6},{8,9},{9,8},{10,11... | collective-permute-start | bytes 196616 | tf_op jit(solution)/shard_map/ppermute | solution.py:30
  34.9 15.1 %collective-permute-start.13 = (bf16[128,1024]{1,0:T(8,128)(2,1)S(1)}, bf16[128,1024]{1,0:T(8,128)(2,1)S(1)}, u32[]{:S(2)}, u32[]{:S(2)}) collective-permute-start(bf16[128,1024]{1,0:T(8,128)(2,1)S(1)} %get-tuple-element.58), channel_id=1, source_target_pairs={{0,2},{2,0},{1,3},{3,1},{4,6},{6,4},{5,7},{7,5},{8,10},{10,8},{9,1... | collective-permute-start | bytes 786440 | tf_op jit(solution)/shard_map/ppermute | solution.py:30
  45.5 6.8 %copy-start = (f32[4,64,1024]{2,1,0:T(8,128)S(1)}, f32[4,64,1024]{2,1,0:T(8,128)}, u32[]{:S(2)}) copy-start(f32[4,64,1024]{2,1,0:T(8,128)} %refs_7_.1) | copy-start | bytes 3145732
  48.0 1.4 %collective-permute-start.16 = (bf16[2,32,1024]{2,1,0:T(8,128)(2,1)S(1)}, bf16[2,32,1024]{2,1,0:T(8,128)(2,1)S(1)}, u32[]{:S(2)}, u32[]{:S(2)}) collective-permute-start(bf16[2,32,1024]{2,1,0:T(8,128)(2,1)S(1)} %get-tuple-element.63), channel_id=1, source_target_pairs={{0,1},{1,0},{2,3},{3,2},{4,5},{5,4},{6,7},{7,6},{8,9},{9,8},{10,11... | collective-permute-start | bytes 393224 | tf_op jit(solution)/shard_map/ppermute | solution.py:30
  48.0 1.5 %collective-permute-start.17 = (bf16[2,32,1024]{2,1,0:T(8,128)(2,1)S(1)}, bf16[2,32,1024]{2,1,0:T(8,128)(2,1)S(1)}, u32[]{:S(2)}, u32[]{:S(2)}) collective-permute-start(bf16[2,32,1024]{2,1,0:T(8,128)(2,1)S(1)} %get-tuple-element.64), channel_id=1, source_target_pairs={{0,1},{1,0},{2,3},{3,2},{4,5},{5,4},{6,7},{7,6},{8,9},{9,8},{10,11... | collective-permute-start | bytes 393224 | tf_op jit(solution)/shard_map/ppermute | solution.py:30
  48.5 1.3 %collective-permute-start.18 = (bf16[2,32,1024]{2,1,0:T(8,128)(2,1)S(1)}, bf16[2,32,1024]{2,1,0:T(8,128)(2,1)S(1)}, u32[]{:S(2)}, u32[]{:S(2)}) collective-permute-start(bf16[2,32,1024]{2,1,0:T(8,128)(2,1)S(1)} %get-tuple-element.65), channel_id=1, source_target_pairs={{0,1},{1,0},{2,3},{3,2},{4,5},{5,4},{6,7},{7,6},{8,9},{9,8},{10,11... | collective-permute-start | bytes 393224 | tf_op jit(solution)/shard_map/ppermute | solution.py:30
  48.6 1.5 %collective-permute-start.19 = (bf16[2,32,1024]{2,1,0:T(8,128)(2,1)S(1)}, bf16[2,32,1024]{2,1,0:T(8,128)(2,1)S(1)}, u32[]{:S(2)}, u32[]{:S(2)}) collective-permute-start(bf16[2,32,1024]{2,1,0:T(8,128)(2,1)S(1)} %get-tuple-element.66), channel_id=1, source_target_pairs={{0,1},{1,0},{2,3},{3,2},{4,5},{5,4},{6,7},{7,6},{8,9},{9,8},{10,11... | collective-permute-start | bytes 393224 | tf_op jit(solution)/shard_map/ppermute | solution.py:30
  50.8 8.6 %collective-permute-start.20 = (bf16[128,1024]{1,0:T(8,128)(2,1)S(1)}, bf16[128,1024]{1,0:T(8,128)(2,1)S(1)}, u32[]{:S(2)}, u32[]{:S(2)}) collective-permute-start(bf16[128,1024]{1,0:T(8,128)(2,1)S(1)} %get-tuple-element.68), channel_id=1, source_target_pairs={{0,2},{2,0},{1,3},{3,1},{4,6},{6,4},{5,7},{7,5},{8,10},{10,8},{9,1... | collective-permute-start | bytes 786440 | tf_op jit(solution)/shard_map/ppermute | solution.py:30
  60.2 3.1 %collective-permute-start.23 = (f32[8,128]{1,0:T(8,128)S(1)}, f32[8,128]{1,0:T(8,128)S(1)}, u32[]{:S(2)}, u32[]{:S(2)}) collective-permute-start(f32[8,128]{1,0:T(8,128)S(1)} %get-tuple-element.69.refs_0_.refs_1_), channel_id=1, source_target_pairs={{0,3},{1,2},{2,1},{3,0},{4,7},{5,6},{6,5},{7,4},{8,11},{9,10},{10,... | collective-permute-start | bytes 12296 | tf_op jit(solution)/shard_map/ppermute | solution.py:30
  60.8 3.6 %collective-permute-start.22 = (f32[8,128]{1,0:T(8,128)S(1)}, f32[8,128]{1,0:T(8,128)S(1)}, u32[]{:S(2)}, u32[]{:S(2)}) collective-permute-start(f32[8,128]{1,0:T(8,128)S(1)} %get-tuple-element.69.refs_0_.refs_1_), channel_id=1, source_target_pairs={{0,2},{1,3},{2,0},{3,1},{4,6},{5,7},{6,4},{7,5},{8,10},{9,11},{10,... | collective-permute-start | bytes 12296 | tf_op jit(solution)/shard_map/ppermute | solution.py:30
  61.8 2.7 %collective-permute-start.21 = (f32[8,128]{1,0:T(8,128)S(1)}, f32[8,128]{1,0:T(8,128)S(1)}, u32[]{:S(2)}, u32[]{:S(2)}) collective-permute-start(f32[8,128]{1,0:T(8,128)S(1)} %get-tuple-element.69.refs_0_.refs_1_), channel_id=1, source_target_pairs={{0,1},{1,0},{2,3},{3,2},{4,5},{5,4},{6,7},{7,6},{8,9},{9,8},{10,11... | collective-permute-start | bytes 12296 | tf_op jit(solution)/shard_map/ppermute | solution.py:30
  65.2 12.2 %collective-permute-start.25 = (bf16[64,1024]{1,0:T(8,128)(2,1)S(1)}, bf16[64,1024]{1,0:T(8,128)(2,1)S(1)}, u32[]{:S(2)}, u32[]{:S(2)}) collective-permute-start(bf16[64,1024]{1,0:T(8,128)(2,1)S(1)} %get-tuple-element.73), channel_id=1, source_target_pairs={{0,8},{4,12},{8,0},{12,4},{1,9},{5,13},{9,1},{13,5},{2,10},{6,14},... | collective-permute-start | bytes 393224 | tf_op jit(solution)/shard_map/ppermute | solution.py:30
  65.3 12.2 %collective-permute-start.24 = (bf16[64,1024]{1,0:T(8,128)(2,1)S(1)}, bf16[64,1024]{1,0:T(8,128)(2,1)S(1)}, u32[]{:S(2)}, u32[]{:S(2)}) collective-permute-start(bf16[64,1024]{1,0:T(8,128)(2,1)S(1)} %get-tuple-element.72.refs_0_), channel_id=1, source_target_pairs={{0,12},{4,8},{8,4},{12,0},{1,13},{5,9},{9,5},{13,1},{2,14},{6,10},... | collective-permute-start | bytes 393224 | tf_op jit(solution)/shard_map/ppermute | solution.py:30
  68.8 10.8 %collective-permute-start.26 = (bf16[64,1024]{1,0:T(8,128)(2,1)S(1)}, bf16[64,1024]{1,0:T(8,128)(2,1)S(1)}, u32[]{:S(2)}, u32[]{:S(2)}) collective-permute-start(bf16[64,1024]{1,0:T(8,128)(2,1)S(1)} %get-tuple-element.75), channel_id=1, source_target_pairs={{0,4},{4,0},{8,12},{12,8},{1,5},{5,1},{9,13},{13,9},{2,6},{6,2},{1... | collective-permute-start | bytes 393224 | tf_op jit(solution)/shard_map/ppermute | solution.py:30
  (1 other events, 0.7 us)

commit v12 on v11

--- a/solution.py
+++ b/solution.py
@@ -13,7 +13,6 @@
 EPSILON = 1e-06
 MIB = 1 << 20
 LANES = 128
-SPLIT = 4
 CORE, COLUMN, ORDER, BLOCK, COUNT = 0, 1, 2, 8, 16
 BF16 = jnp.bfloat16
 F32 = jnp.float32
@@ -162,44 +161,67 @@
 
 
 def rows_kernel(used, sends, messages, scal, after, here, *refs):
-    held, refs = refs[:used], refs[used:]
-    perm, src_ids, rec_ids, refs = refs[0], refs[sends:0:-1], refs[1 + sends], refs[2 + sends :]
-    outs, own_out = refs[:-1], refs[-1]
-    units, _, _, slots, part = own_out.shape
-    channels = here.shape[2]
-    pick = picks(list(src_ids) + [rec_ids.at[d : d + 1] for d in range(units)], channels)
+    held, perm, src_ids, refs = refs[:used], refs[used], refs[used + 1 : used + 1 + sends], refs[used + 1 + sends :]
+    outs, kept = refs[:-1], refs[-1]
+    _, _, channels, part = kept.shape
+    slots = src_ids[0].shape[1]
+    pick = picks(src_ids[::-1], channels)
     for u in range(used):
+        x = here[0].reshape(2 * channels, part)
+        for s in range(used):
+            x = jnp.where(scal[ORDER + u] == s + 1, held[s][0].reshape(2 * channels, part), x)
+        x = jnp.dot(x, perm[...], preferred_element_type=F32).astype(BF16)
         for half in range(2):
-            x = here[0, half]
-            for s in range(used):
-                x = jnp.where(scal[ORDER + u] == s + 1, held[s][0, half], x)
-            x = jnp.dot(x, perm[...], preferred_element_type=F32).astype(BF16)
+            z = x[half * channels : (half + 1) * channels]
+            kept[u, half] = z
             y = lax.dot_general(
-                pick, x, (((0,), (0,)), ((), ())), preferred_element_type=F32
+                pick, z, (((0,), (0,)), ((), ())), preferred_element_type=F32
             ).astype(BF16)
             for (d, first, count), out in zip(messages, outs):
                 at = d * slots + first
                 out[u, half] = y[at : at + count]
+
+
+def gather_rows(scal, after, here, held, perm, src_ids, messages):
+    used = len(held)
+    channels, part = held[0].shape[-2:]
+    *sent, kept = pl.pallas_call(
+        functools.partial(rows_kernel, used, len(src_ids), messages),
+        out_shape=[jax.ShapeDtypeStruct((used, 2, m[2], part), BF16) for m in messages]
+        + [jax.ShapeDtypeStruct((used, 2, channels, part), BF16)],
+        in_specs=[SMEM, ANY] + [VMEM] * (used + 2 + len(src_ids)),
+        out_specs=[VMEM] * (len(messages) + 1),
+        compiler_params=params(16),
+        cost_estimate=SMALL,
+        name="rows",
+    )(scal, after, here, *held, perm, *src_ids[::-1])
+    return sent, kept
+
+
+def own_kernel(kept, rec_ids, own):
+    units, used, _, slots, _ = own.shape
+    pick = picks([rec_ids.at[d : d + 1] for d in range(units)], kept.shape[2])
+    for u in range(used):
+        for half in range(2):
+            y = lax.dot_general(
+                pick, kept[u, half], (((0,), (0,)), ((), ())), preferred_element_type=F32
+            ).astype(BF16)
             for d in range(units):
-                at = (sends + d) * slots
-                own_out[d, u, half] = y[at : at + slots]
-
-
-def gather_rows(scal, after, here, held, perm, src_ids, rec_ids, messages):
-    used, sends = len(held), len(src_ids)
-    part = held[0].shape[-1]
+                own[d, u, half] = y[d * slots : (d + 1) * slots]
+
+
+def gather_own(kept, rec_ids):
+    used, _, _, part = kept.shape
     units, slots = rec_ids.shape
-    *sent, own = pl.pallas_call(
-        functools.partial(rows_kernel, used, sends, messages),
-        out_shape=[jax.ShapeDtypeStruct((used, 2, m[2], part), BF16) for m in messages]
-        + [jax.ShapeDtypeStruct((units, used, 2, slots, part), BF16)],
-        in_specs=[SMEM, pl.BlockSpec(memory_space=pl.ANY)] + [VMEM] * (used + 3 + sends),
-        out_specs=[VMEM] * (len(messages) + 1),
-        compiler_params=params(16),
-        cost_estimate=SMALL,
-        name="rows",
-    )(scal, after, here, *held, perm, *src_ids[::-1], rec_ids)
-    return sent, own
+    return pl.pallas_call(
+        own_kernel,
+        out_shape=jax.ShapeDtypeStruct((units, used, 2, slots, part), BF16),
+        in_specs=[VMEM] * 2,
+        out_specs=VMEM,
+        compiler_params=params(16),
+        cost_estimate=SMALL,
+        name="own",
+    )(kept, rec_ids)
 
 
 def combine(values, classes, outputs, origin, span, period):
@@ -260,7 +282,7 @@
             lhs[r, turned, LANES:] = (-real).astype(BF16)
 
 
-def cross_rows(weight, after, rows, own, pieces, classes):
+def cross_rows(weight, after, rows, own, pieces, classes, effort):
     count = sum(p[2] for p in pieces)
     return pl.pallas_call(
         functools.partial(cross_kernel, pieces, len(after)),
@@ -268,7 +290,7 @@
         in_specs=[SMEM] + [ANY] * len(after) + [VMEM] * (len(rows) + 1),
         out_specs=VMEM,
         compiler_params=params(8),
-        cost_estimate=LARGE,
+        cost_estimate=effort,
         name="cross",
     )(weight, *after, *rows, own)
 
@@ -362,7 +384,8 @@
 
 
 def stats_kernel(scale, q, pieces, others, scal, *refs):
-    earlier, (own, *refs) = refs[:q], refs[q:]
+    count = min(q, 1)
+    earlier, (own, *refs) = refs[:count], refs[count:]
     more, refs = refs[:others], refs[others:]
     targets, (corr, sums) = refs[: len(pieces)], refs[len(pieces) :]
     columns = []
@@ -377,6 +400,9 @@
         product = jnp.sum(value * target[0], axis=1, keepdims=True)
         lane = lax.broadcasted_iota(jnp.int32, (count, LANES), 1)
         columns.append(jnp.where(lane == 2 * q, square, jnp.where(lane == 2 * q + 1, product, 0.0)))
+    spare = sums.shape[1] - own.shape[0]
+    if spare:
+        columns.append(jnp.zeros((spare, LANES), F32))
     total = jnp.concatenate(columns, axis=0).T[:8]
     for e in earlier:
         total = total + e[...]
@@ -399,7 +425,7 @@
 
 def lag_stats(scal, scale, q, pieces, earlier, own, more, observed):
     rows, lag_dev = own.shape
-    outs = [jax.ShapeDtypeStruct((rows, lag_dev), F32), jax.ShapeDtypeStruct((8, rows), F32)]
+    outs = [jax.ShapeDtypeStruct((rows, lag_dev), F32), jax.ShapeDtypeStruct((8, -(-rows // LANES) * LANES), F32)]
     return pl.pallas_call(
         functools.partial(stats_kernel, scale, q, pieces, len(more)),
         grid_spec=pltpu.PrefetchScalarGridSpec(
@@ -559,7 +585,8 @@
     if direct and blocks == 4:
         chunks = [
             [(0, 0, slots), (1, 0, slots)],
-            [(3, 0, slots), (2, 0, slots)],
+            [(2, 0, slots)],
+            [(3, 0, slots)],
         ]
     else:
         chunks = [[(d, first, some) for d in range(blocks)] for first in (0, some)]
@@ -567,9 +594,8 @@
         messages = [piece for pieces in chunks for piece in pieces]
     else:
         messages = [(d, 0, slots) for d in shifts]
-    sent, own_rows = gather_rows(
-        scal, table, held[0], held[1:], make_perm(part), src_ids, rec_ids, messages
-    )
+    sent, kept = gather_rows(scal, table, held[0], held[1:], make_perm(part), src_ids, messages)
+    own_rows = gather_own(kept, rec_ids)
     arrived = [swapped(x, "recv", places, m[0]) for m, x in reversed(list(zip(messages, sent)))][::-1]
     if not direct:
         stacked = jnp.stack(arrived)
@@ -580,15 +606,18 @@
     corrs, all_sums, returned, returned_pieces = [], [], [], []
     after = []
     for q, pieces in enumerate(chunks):
-        rows = arrived[len(pieces) * q : len(pieces) * (q + 1)]
-        lhs = cross_rows(weight, after[:1], rows, own_rows, pieces, classes)
+        rows, arrived = arrived[: len(pieces)], arrived[len(pieces) :]
+        lhs = cross_rows(
+            weight, after[:1] + (arrived if q == 1 else []), rows, own_rows, pieces, classes, LARGE if q < 2 else SMALL
+        )
+        groups = sum(p[2] for p in pieces) // (32 if q else 16)
         keep, *sends = lag_parts(
-            scal, [], lhs, table, geometry, columns, lag_dev, SPLIT if q else 2 * SPLIT, SMALL if q else LARGE
+            scal, [], lhs, table, geometry, columns, lag_dev, groups, SMALL if q else LARGE
         )
         sends = [swapped(x, "freq", cores, 1) for x in sends]
         own, *sends = add_cores(scal, after[1:], keep, sends)
         more = [swapped(x, "win", columns, s + 1) for s, x in enumerate(sends)]
-        after = [own, *more]
+        after = [own, *more] if q == 0 else []
         corr, sums = lag_stats(scal, lag_scale, q, pieces, all_sums, own, more, observed)
         corrs.append(corr)
         all_sums = [sums]

time: 80.9 us -> 78.9 us (0.975)
  waiting for transfers between devices: 33 us -> 26 us
  Pallas kernels: 19.5 us -> 22.9 us
  starting transfers between devices: 22.7 us -> 24.3 us
    ppermute x27 -> x28, waiting for transfers between devices: 33 us -> 26 us  [swapped(): return lax.ppermute(value, axis, [(i, i ^ step) for i in range(size)])]
    ppermute x27 -> x28, starting transfers between devices: 22.7 us -> 24.3 us  [swapped(): return lax.ppermute(value, axis, [(i, i ^ step) for i in range(size)])]
    pallas_call x2 -> x3, Pallas kernels: 4.85 us -> 5.78 us  [lag_parts(): pl.pallas_call(functools.partial(lags_kernel, geometry, split, len(after)...]
    pallas_call x2 -> x3, Pallas kernels: 1.61 us -> 2.31 us  [gradients(): pl.pallas_call(functools.partial(gradient_kernel, lag_total, q, pieces, l...]
    pallas_call x2 -> x3, Pallas kernels: 1.55 us -> 2.21 us  [lag_stats(): pl.pallas_call(functools.partial(stats_kernel, scale, q, pieces, len(more...]
    pallas_call x2 -> x3, Pallas kernels: 1.52 us -> 2.06 us  [add_cores(): pl.pallas_call(functools.partial(cores_kernel, len(after), len(more)), ou...]
    pallas_call x1 -> x2, Pallas kernels: 1.82 us -> 2.07 us  [the longest x1 1.55 us: gather_rows(): pl.pallas_call(functools.partial(rows_kernel, used, len(src_ids), message...]
  transfers between devices with their start and end apart: 27 -> 28, of which waited for: 16 -> 12; matrix products, arithmetic and copies ran while one was open for 0% -> 0% of each run, Pallas kernels for 18% -> 24%
where the time goes in v12:
time: 78.9 us; the launch traced here: 78.7 us
  waiting for transfers between devices  26 us (33%)
  starting transfers between devices  24.3 us (31%)
  Pallas kernels  22.9 us (29%)
  local copies, waits for them, and re-layouts  4 us (5%)
  between operations  1.51 us (2%)
    ppermute x28, waiting for transfers between devices, swapped(): return lax.ppermute(value, axis, [(i, i ^ step) for i in range(size)])  26 us
    ppermute x28, starting transfers between devices, swapped(): return lax.ppermute(value, axis, [(i, i ^ step) for i in range(size)])  24.3 us
    pallas_call x3, Pallas kernels, lag_parts(): pl.pallas_call(functools.partial(lags_kernel, geometry, split, len(after)...  5.78 us
    pallas_call x1, Pallas kernels, normed_rows(): pl.pallas_call(functools.partial(normed_kernel, lag_total, chunks, len(su...  3.22 us
    unnamed x12, local copies, waits for them, and re-layouts  2.68 us
    pallas_call x3, Pallas kernels, gradients(): pl.pallas_call(functools.partial(gradient_kernel, lag_total, q, pieces, l...  2.31 us
    pallas_call x3, Pallas kernels, lag_stats(): pl.pallas_call(functools.partial(stats_kernel, scale, q, pieces, len(more...  2.21 us
    pallas_call x3, Pallas kernels, add_cores(): pl.pallas_call(functools.partial(cores_kernel, len(after), len(more)), ou...  2.06 us
  transfers between devices with their start and end apart: 28, of which 12 were waited for; matrix products, arithmetic and copies ran while one was open for 0% of the time, Pallas kernels for 24%

profile of v12, /device:TPU:0, one launch (start us, length us, event | category | flops | bytes accessed | tf_op | source)
XLA Modules:
  0.0 78.7 jit_solution(3657972324060939617)
XLA Ops:
  0.7 1.3 %constant_dynamic-slice_fusion = (bf16[1,2,128,1024]{3,2,1,0:T(8,128)(2,1)S(1)}, bf16[1,2,128,1024]{3,2,1,0:T(8,128)(2,1)S(1)}) fusion(bf16[1,2,128,2048]{3,2,1,0:T(8,128)(2,1)} %param.8, s32[]{:T(128)S(6)} %select_n.7, s32[]{:T(128)S(6)} %select_n.6), kind=kLoop, calls=%fused_computation | loop fusion | bytes 2097160 | tf_op jit(solution)/shard_map/dynamic_slice | solution.py:561
  2.0 3.0 %collective-permute-start = (bf16[1,2,128,1024]{3,2,1,0:T(8,128)(2,1)S(1)}, bf16[1,2,128,1024]{3,2,1,0:T(8,128)(2,1)S(1)}, u32[]{:S(2)}, u32[]{:S(2)}) collective-permute-start(bf16[1,2,128,1024]{3,2,1,0:T(8,128)(2,1)S(1)} %get-tuple-element.82), channel_id=1, source_target_pairs={{0,2},{2,0},{1,3},{3,1},{4,6},{6,4},{5,7},{7,5},{8,10},{10,8},{9,1... | collective-permute-start | bytes 1572872 | tf_op jit(solution)/shard_map/ppermute | solution.py:29
  8.3 1.2 %index.1 = (s32[128]{0:T(128)S(1)}, s32[1,64]{1,0:T(1,128)S(1)}, s32[1,64]{1,0:T(1,128)S(1)}, s32[1,64]{1,0:T(1,128)S(1)}, s32[1,64]{1,0:T(1,128)S(1)}, /*index=5*/s32[4,64]{1,0:T(4,128)S(1)}) custom-call(s32[1]{0:T(128)S(6)} %copy.10.refs_0_, s32[4]{0:T(128)S(1)} %copy-done.4, s32[4]{0:T(128)S(1)} %bitcast.1, s32[4,64]{1,0:T(4,128)S(1)} %copy-done.2, ...), custom_call_target="tpu_custom_call" | custom-call | flops 1 | bytes 1 | tf_op jit(solution)/shard_map/index/pallas_call | solution.py:92
  9.5 3.7 %collective-permute-start.1 = (s32[1,64]{1,0:T(1,128)S(1)}, s32[1,64]{1,0:T(1,128)S(1)}, u32[]{:S(2)}, u32[]{:S(2)}) collective-permute-start(s32[1,64]{1,0:T(1,128)S(1)} %get-tuple-element.43), channel_id=1, source_target_pairs={{0,12},{4,8},{8,4},{12,0},{1,13},{5,9},{9,5},{13,1},{2,14},{6,10},... | collective-permute-start | bytes 776 | tf_op jit(solution)/shard_map/ppermute | solution.py:29
  13.2 0.8 collective-permute-start.3
  14.6 1.8 %table.1.after.refs_1_ = bf16[8,256,1024]{2,1,0:T(8,128)(2,1)S(1)} custom-call(s32[128]{0:T(128)S(1)} %get-tuple-element.42.scal, f32[2,56,1024]{2,1,0:T(8,128)S(1)} %copy-done.1), custom_call_target="tpu_custom_call" | custom-call | flops 1 | bytes 1 | tf_op jit(solution)/shard_map/table/pallas_call | solution.py:126
  16.4 1.2 %collective-permute-done.2.refs_3_.refs_1_ = s32[1,64]{1,0:T(1,128)S(1)} collective-permute-done((s32[1,64]{1,0:T(1,128)S(1)}, s32[1,64]{1,0:T(1,128)S(1)}, u32[]{:S(2)}, u32[]{:S(2)}) %collective-permute-start.2) | collective-permute-done | bytes 288 | tf_op jit(solution)/shard_map/ppermute | solution.py:29
  17.7 1.6 %rows.1 = (bf16[1,2,64,1024]{3,2,1,0:T(8,128)(2,1)S(1)}, bf16[1,2,64,1024]{3,2,1,0:T(8,128)(2,1)S(1)}, bf16[1,2,64,1024]{3,2,1,0:T(8,128)(2,1)S(1)}, bf16[1,2,64...) custom-call(s32[128]{0:T(128)S(1)} %get-tuple-element.42.scal, bf16[8,256,1024]{2,1,0:T(8,128)(2,1)S(1)} %table.1.after.refs_1_, ...), custom_call_target="tpu_custom_call" | custom-call | flops 1 | bytes 1 | tf_op jit(solution)/shard_map/rows/pallas_call | solution.py:188
  19.2 1.1 %collective-permute-start.4 = (bf16[1,2,64,1024]{3,2,1,0:T(8,128)(2,1)S(1)}, bf16[1,2,64,1024]{3,2,1,0:T(8,128)(2,1)S(1)}, u32[]{:S(2)}, u32[]{:S(2)}) collective-permute-start(bf16[1,2,64,1024]{3,2,1,0:T(8,128)(2,1)S(1)} %get-tuple-element.48), channel_id=1, source_target_pairs={{0,4},{4,0},{8,12},{12,8},{1,5},{5,1},{9,13},{13,9},{2,6},{6,2},{1... | collective-permute-start | bytes 786440 | tf_op jit(solution)/shard_map/ppermute | solution.py:29
  20.4 2.5 %collective-permute-start.14 = (bf16[1,2,64,1024]{3,2,1,0:T(8,128)(2,1)S(1)}, bf16[1,2,64,1024]{3,2,1,0:T(8,128)(2,1)S(1)}, u32[]{:S(2)}, u32[]{:S(2)}) collective-permute-start(bf16[1,2,64,1024]{3,2,1,0:T(8,128)(2,1)S(1)} %get-tuple-element.63), channel_id=1, source_target_pairs={{0,12},{4,8},{8,4},{12,0},{1,13},{5,9},{9,5},{13,1},{2,14},{6,10},... | collective-permute-start | bytes 786440 | tf_op jit(solution)/shard_map/ppermute | solution.py:29
  23.5 3.6 %collective-permute-done.4.refs_1_ = bf16[1,2,64,1024]{3,2,1,0:T(8,128)(2,1)S(1)} collective-permute-done((bf16[1,2,64,1024]{3,2,1,0:T(8,128)(2,1)S(1)}, bf16[1,2,64,1024]{3,2,1,0:T(8,128)(2,1)S(1)}, u32[]{:S(2)}, u32[]{:S(2)}) %collective-permute-start.4) | collective-permute-done | bytes 262176 | tf_op jit(solution)/shard_map/ppermute | solution.py:29
  27.4 2.3 %lags.3 = (f32[2,128,1024]{2,1,0:T(8,128)S(1)}, bf16[2,16,1024]{2,1,0:T(8,128)(2,1)S(1)}, bf16[2,16,1024]{2,1,0:T(8,128)(2,1)S(1)}, bf16[2,16,1024]{2,1,0:T(8,12...) custom-call(s32[128]{0:T(128)S(1)} %get-tuple-element.42.scal, ...), custom_call_target="tpu_custom_call" | custom-call | flops 20000000000 | bytes 1048576 | tf_op jit(solution)/shard_map/lags/pallas_call | solution.py:339
  33.7 0.8 %cores.3 = (f32[128,1024]{1,0:T(8,128)S(1)}, bf16[128,1024]{1,0:T(8,128)(2,1)S(1)}) custom-call(s32[128]{0:T(128)S(1)} %get-tuple-element.42.scal, f32[2,128,1024]{2,1,0:T(8,128)S(1)} %get-tuple-element.51.refs_0_, bf16[2,16,1024]{2,1,0:T(8,128)(2,1)S(1)} %collective-permute-done.5.refs_1_, bf16[2,16,1024]{2,1,0:T(8,128)(2,1)S(1)} %collective-permute-done.6.refs_2_, ...), custom_call_target="tpu_custom_call" | custom-call | flops 1 | bytes 1 | tf_op jit(solution)/shard_map/cores/pallas_call | solution.py:374
  34.5 1.6 %collective-permute-start.13 = (bf16[128,1024]{1,0:T(8,128)(2,1)S(1)}, bf16[128,1024]{1,0:T(8,128)(2,1)S(1)}, u32[]{:S(2)}, u32[]{:S(2)}) collective-permute-start(bf16[128,1024]{1,0:T(8,128)(2,1)S(1)} %get-tuple-element.61), channel_id=1, source_target_pairs={{0,2},{2,0},{1,3},{3,1},{4,6},{6,4},{5,7},{7,5},{8,10},{10,8},{9,1... | collective-permute-start | bytes 786440 | tf_op jit(solution)/shard_map/ppermute | solution.py:29
  36.1 8.8 %collective-permute-done.15.refs_2_ = bf16[1,2,64,1024]{3,2,1,0:T(8,128)(2,1)S(1)} collective-permute-done((bf16[1,2,64,1024]{3,2,1,0:T(8,128)(2,1)S(1)}, bf16[1,2,64,1024]{3,2,1,0:T(8,128)(2,1)S(1)}, u32[]{:S(2)}, u32[]{:S(2)}) %collective-permute-start.15) | collective-permute-done | bytes 262176 | tf_op jit(solution)/shard_map/ppermute | solution.py:29
  45.1 1.7 %lags.4 = (f32[2,64,1024]{2,1,0:T(8,128)S(1)}, bf16[2,32,1024]{2,1,0:T(8,128)(2,1)S(1)}, bf16[2,32,1024]{2,1,0:T(8,128)(2,1)S(1)}) custom-call(s32[128]{0:T(128)S(1)} %get-tuple-element.42.scal, bf16[8,128,256]{2,1,0:T(8,128)(2,1)S(1)} %cross.4.refs_0_, bf16[8,256,1024]{2,1,0:T(8,128)(2,1)S(1)} %table.1.after.refs_1_), custom_call_target="tpu_custom_call" | custom-call | flops 1 | bytes 1 | tf_op jit(solution)/shard_map/lags/pallas_call | solution.py:339
  47.5 1.7 %lags.5 = (f32[2,64,1024]{2,1,0:T(8,128)S(1)}, bf16[2,32,1024]{2,1,0:T(8,128)(2,1)S(1)}, bf16[2,32,1024]{2,1,0:T(8,128)(2,1)S(1)}) custom-call(s32[128]{0:T(128)S(1)} %get-tuple-element.42.scal, bf16[8,128,256]{2,1,0:T(8,128)(2,1)S(1)} %cross.5.refs_0_, bf16[8,256,1024]{2,1,0:T(8,128)(2,1)S(1)} %table.1.after.refs_1_), custom_call_target="tpu_custom_call" | custom-call | flops 1 | bytes 1 | tf_op jit(solution)/shard_map/lags/pallas_call | solution.py:339
  50.5 1.6 %collective-permute-start.18 = (bf16[64,1024]{1,0:T(8,128)(2,1)S(1)}, bf16[64,1024]{1,0:T(8,128)(2,1)S(1)}, u32[]{:S(2)}, u32[]{:S(2)}) collective-permute-start(bf16[64,1024]{1,0:T(8,128)(2,1)S(1)} %get-tuple-element.69), channel_id=1, source_target_pairs={{0,2},{2,0},{1,3},{3,1},{4,6},{6,4},{5,7},{7,5},{8,10},{10,8},{9,1... | collective-permute-start | bytes 393224 | tf_op jit(solution)/shard_map/ppermute | solution.py:29
  53.3 0.8 stats.3
  54.1 2.8 %collective-permute-done.18.refs_2_ = bf16[64,1024]{1,0:T(8,128)(2,1)S(1)} collective-permute-done((bf16[64,1024]{1,0:T(8,128)(2,1)S(1)}, bf16[64,1024]{1,0:T(8,128)(2,1)S(1)}, u32[]{:S(2)}, u32[]{:S(2)}) %collective-permute-start.18) | collective-permute-done | bytes 131104 | tf_op jit(solution)/shard_map/ppermute | solution.py:29
  57.6 1.2 %collective-permute-done.21.refs_2_ = bf16[64,1024]{1,0:T(8,128)(2,1)S(1)} collective-permute-done((bf16[64,1024]{1,0:T(8,128)(2,1)S(1)}, bf16[64,1024]{1,0:T(8,128)(2,1)S(1)}, u32[]{:S(2)}, u32[]{:S(2)}) %collective-permute-start.21) | collective-permute-done | bytes 131104 | tf_op jit(solution)/shard_map/ppermute | solution.py:29
  60.0 1.2 %collective-permute-start.23 = (f32[8,128]{1,0:T(8,128)S(1)}, f32[8,128]{1,0:T(8,128)S(1)}, u32[]{:S(2)}, u32[]{:S(2)}) collective-permute-start(f32[8,128]{1,0:T(8,128)S(1)} %get-tuple-element.76.refs_0_.refs_1_), channel_id=1, source_target_pairs={{0,2},{1,3},{2,0},{3,1},{4,6},{5,7},{6,4},{7,5},{8,10},{9,11},{10,... | collective-permute-start | bytes 12296 | tf_op jit(solution)/shard_map/ppermute | solution.py:29
  61.5 1.2 %collective-permute-done.24.refs_3_.refs_4_ = f32[8,128]{1,0:T(8,128)S(1)} collective-permute-done((f32[8,128]{1,0:T(8,128)S(1)}, f32[8,128]{1,0:T(8,128)S(1)}, u32[]{:S(2)}, u32[]{:S(2)}) %collective-permute-start.24) | collective-permute-done | bytes 4128 | tf_op jit(solution)/shard_map/ppermute | solution.py:29
  62.6 0.9 %collective-permute-done.23.refs_2_.refs_3_ = f32[8,128]{1,0:T(8,128)S(1)} collective-permute-done((f32[8,128]{1,0:T(8,128)S(1)}, f32[8,128]{1,0:T(8,128)S(1)}, u32[]{:S(2)}, u32[]{:S(2)}) %collective-permute-start.23) | collective-permute-done | bytes 4128 | tf_op jit(solution)/shard_map/ppermute | solution.py:29
  63.6 0.8 gradient.3.refs_0_
  64.3 2.7 %collective-permute-start.25 = (bf16[64,1024]{1,0:T(8,128)(2,1)S(1)}, bf16[64,1024]{1,0:T(8,128)(2,1)S(1)}, u32[]{:S(2)}, u32[]{:S(2)}) collective-permute-start(bf16[64,1024]{1,0:T(8,128)(2,1)S(1)} %gradient.3.refs_0_), channel_id=1, source_target_pairs={{0,12},{4,8},{8,4},{12,0},{1,13},{5,9},{9,5},{13,1},{2,14},{6,10},... | collective-permute-start | bytes 393224 | tf_op jit(solution)/shard_map/ppermute | solution.py:29
  67.0 0.8 gradient.4.refs_0_
  67.9 0.8 %gradient.5 = (bf16[64,1024]{1,0:T(8,128)(2,1)S(1)}, bf16[64,1024]{1,0:T(8,128)(2,1)S(1)}) custom-call(s32[128]{0:T(128)S(1)} %get-tuple-element.42.scal, bf16[64,1024]{1,0:T(8,128)(2,1)S(1)} %gradient.4.refs_0_, f32[8,128]{1,0:T(8,128)S(1)} %get-tuple-element.76.refs_0_.refs_1_, f32[8,128]{1,0:T(8,128)S(1)} %collective-permute-done.22.refs_1_.refs_2_, ...), custom_call_target="tpu_custom_call" | custom-call | flops 1 | bytes 1 | tf_op jit(solution)/shard_map/gradient/pallas_call | solution.py:474
  68.7 1.8 %collective-permute-start.27 = (bf16[64,1024]{1,0:T(8,128)(2,1)S(1)}, bf16[64,1024]{1,0:T(8,128)(2,1)S(1)}, u32[]{:S(2)}, u32[]{:S(2)}) collective-permute-start(bf16[64,1024]{1,0:T(8,128)(2,1)S(1)} %get-tuple-element.81), channel_id=1, source_target_pairs={{0,4},{4,0},{8,12},{12,8},{1,5},{5,1},{9,13},{13,9},{2,6},{6,2},{1... | collective-permute-start | bytes 393224 | tf_op jit(solution)/shard_map/ppermute | solution.py:29
  70.5 3.2 %normed.1 = f32[4,64,1024]{2,1,0:T(8,128)} custom-call(s32[128]{0:T(128)S(1)} %get-tuple-element.42.scal, f32[8,128]{1,0:T(8,128)S(1)} %get-tuple-element.76.refs_0_.refs_1_, f32[8,128]{1,0:T(8,128)S(1)} %collective-permute-done.22.refs_1_.refs_2_, f32[8,128]{1,0:T(8,128)S(1)} %collective-permute-done.23.refs_2_.refs_3_, ...), custom_call_target="tpu_custom_call" | custom-call | flops 1 | bytes 1 | tf_op jit(solution)/shard_map/normed/pallas_call | solution.py:506
  73.7 3.9 %collective-permute-done.26.refs_5_ = bf16[64,1024]{1,0:T(8,128)(2,1)S(1)} collective-permute-done((bf16[64,1024]{1,0:T(8,128)(2,1)S(1)}, bf16[64,1024]{1,0:T(8,128)(2,1)S(1)}, u32[]{:S(2)}, u32[]{:S(2)}) %collective-permute-start.26) | collective-permute-done | bytes 131104 | tf_op jit(solution)/shard_map/ppermute | solution.py:29
  77.6 1.1 %adjoint.1 = f32[128,1024]{1,0:T(8,128)} custom-call(s32[1,64]{1,0:T(1,128)S(1)} %collective-permute-done.1.refs_2_.refs_0_, s32[1,64]{1,0:T(1,128)S(1)} %collective-permute-done.2.refs_3_.refs_1_, s32[1,64]{1,0:T(1,128)S(1)} %get-tuple-element.46.refs_5_.refs_2_, s32[1,64]{1,0:T(1,128)S(1)} %collective-permute-done.3.refs_4_.refs_3_, ...), custom_call_target="tpu_custom_call" | custom-call | flops 1 | bytes 1 | tf_op jit(solution)/shard_map/adjoint/pallas_call | solution.py:530
  (59 shorter events, 13.6 us)
Async XLA Ops:
  0.6 14.0 %copy-start.1 = (f32[2,56,1024]{2,1,0:T(8,128)S(1)}, f32[2,56,1024]{2,1,0:T(8,128)}, u32[]{:S(2)}) copy-start(f32[2,56,1024]{2,1,0:T(8,128)} %constant.16.clone.trig) | copy-start | bytes 1376260
  2.0 15.7 %collective-permute-start = (bf16[1,2,128,1024]{3,2,1,0:T(8,128)(2,1)S(1)}, bf16[1,2,128,1024]{3,2,1,0:T(8,128)(2,1)S(1)}, u32[]{:S(2)}, u32[]{:S(2)}) collective-permute-start(bf16[1,2,128,1024]{3,2,1,0:T(8,128)(2,1)S(1)} %get-tuple-element.82), channel_id=1, source_target_pairs={{0,2},{2,0},{1,3},{3,1},{4,6},{6,4},{5,7},{7,5},{8,10},{10,8},{9,1... | collective-permute-start | bytes 1572872 | tf_op jit(solution)/shard_map/ppermute | solution.py:29
  5.6 0.7 copy-start.2
  6.3 0.7 copy-start.3
  9.5 6.9 %collective-permute-start.1 = (s32[1,64]{1,0:T(1,128)S(1)}, s32[1,64]{1,0:T(1,128)S(1)}, u32[]{:S(2)}, u32[]{:S(2)}) collective-permute-start(s32[1,64]{1,0:T(1,128)S(1)} %get-tuple-element.43), channel_id=1, source_target_pairs={{0,12},{4,8},{8,4},{12,0},{1,13},{5,9},{9,5},{13,1},{2,14},{6,10},... | collective-permute-start | bytes 776 | tf_op jit(solution)/shard_map/ppermute | solution.py:29
  13.2 4.4 %collective-permute-start.2 = (s32[1,64]{1,0:T(1,128)S(1)}, s32[1,64]{1,0:T(1,128)S(1)}, u32[]{:S(2)}, u32[]{:S(2)}) collective-permute-start(s32[1,64]{1,0:T(1,128)S(1)} %get-tuple-element.44), channel_id=1, source_target_pairs={{0,8},{4,12},{8,0},{12,4},{1,9},{5,13},{9,1},{13,5},{2,10},{6,14},... | collective-permute-start | bytes 776 | tf_op jit(solution)/shard_map/ppermute | solution.py:29
  13.2 4.4 %collective-permute-start.3 = (s32[1,64]{1,0:T(1,128)S(1)}, s32[1,64]{1,0:T(1,128)S(1)}, u32[]{:S(2)}, u32[]{:S(2)}) collective-permute-start(s32[1,64]{1,0:T(1,128)S(1)} %get-tuple-element.45), channel_id=1, source_target_pairs={{0,4},{4,0},{8,12},{12,8},{1,5},{5,1},{9,13},{13,9},{2,6},{6,2},{1... | collective-permute-start | bytes 776 | tf_op jit(solution)/shard_map/ppermute | solution.py:29
  19.2 7.9 %collective-permute-start.4 = (bf16[1,2,64,1024]{3,2,1,0:T(8,128)(2,1)S(1)}, bf16[1,2,64,1024]{3,2,1,0:T(8,128)(2,1)S(1)}, u32[]{:S(2)}, u32[]{:S(2)}) collective-permute-start(bf16[1,2,64,1024]{3,2,1,0:T(8,128)(2,1)S(1)} %get-tuple-element.48), channel_id=1, source_target_pairs={{0,4},{4,0},{8,12},{12,8},{1,5},{5,1},{9,13},{13,9},{2,6},{6,2},{1... | collective-permute-start | bytes 786440 | tf_op jit(solution)/shard_map/ppermute | solution.py:29
  20.4 15.8 %collective-permute-start.14 = (bf16[1,2,64,1024]{3,2,1,0:T(8,128)(2,1)S(1)}, bf16[1,2,64,1024]{3,2,1,0:T(8,128)(2,1)S(1)}, u32[]{:S(2)}, u32[]{:S(2)}) collective-permute-start(bf16[1,2,64,1024]{3,2,1,0:T(8,128)(2,1)S(1)} %get-tuple-element.63), channel_id=1, source_target_pairs={{0,12},{4,8},{8,4},{12,0},{1,13},{5,9},{9,5},{13,1},{2,14},{6,10},... | collective-permute-start | bytes 786440 | tf_op jit(solution)/shard_map/ppermute | solution.py:29
  22.8 22.1 %collective-permute-start.15 = (bf16[1,2,64,1024]{3,2,1,0:T(8,128)(2,1)S(1)}, bf16[1,2,64,1024]{3,2,1,0:T(8,128)(2,1)S(1)}, u32[]{:S(2)}, u32[]{:S(2)}) collective-permute-start(bf16[1,2,64,1024]{3,2,1,0:T(8,128)(2,1)S(1)} %get-tuple-element.64), channel_id=1, source_target_pairs={{0,8},{4,12},{8,0},{12,4},{1,9},{5,13},{9,1},{13,5},{2,10},{6,14},... | collective-permute-start | bytes 786440 | tf_op jit(solution)/shard_map/ppermute | solution.py:29
  29.7 1.3 %collective-permute-start.5 = (bf16[2,16,1024]{2,1,0:T(8,128)(2,1)S(1)}, bf16[2,16,1024]{2,1,0:T(8,128)(2,1)S(1)}, u32[]{:S(2)}, u32[]{:S(2)}) collective-permute-start(bf16[2,16,1024]{2,1,0:T(8,128)(2,1)S(1)} %get-tuple-element.52), channel_id=1, source_target_pairs={{0,1},{1,0},{2,3},{3,2},{4,5},{5,4},{6,7},{7,6},{8,9},{9,8},{10,11... | collective-permute-start | bytes 196616 | tf_op jit(solution)/shard_map/ppermute | solution.py:29
  29.8 1.4 %collective-permute-start.6 = (bf16[2,16,1024]{2,1,0:T(8,128)(2,1)S(1)}, bf16[2,16,1024]{2,1,0:T(8,128)(2,1)S(1)}, u32[]{:S(2)}, u32[]{:S(2)}) collective-permute-start(bf16[2,16,1024]{2,1,0:T(8,128)(2,1)S(1)} %get-tuple-element.53), channel_id=1, source_target_pairs={{0,1},{1,0},{2,3},{3,2},{4,5},{5,4},{6,7},{7,6},{8,9},{9,8},{10,11... | collective-permute-start | bytes 196616 | tf_op jit(solution)/shard_map/ppermute | solution.py:29
  30.3 1.3 %collective-permute-start.7 = (bf16[2,16,1024]{2,1,0:T(8,128)(2,1)S(1)}, bf16[2,16,1024]{2,1,0:T(8,128)(2,1)S(1)}, u32[]{:S(2)}, u32[]{:S(2)}) collective-permute-start(bf16[2,16,1024]{2,1,0:T(8,128)(2,1)S(1)} %get-tuple-element.54), channel_id=1, source_target_pairs={{0,1},{1,0},{2,3},{3,2},{4,5},{5,4},{6,7},{7,6},{8,9},{9,8},{10,11... | collective-permute-start | bytes 196616 | tf_op jit(solution)/shard_map/ppermute | solution.py:29
  31.1 1.3 %collective-permute-start.8 = (bf16[2,16,1024]{2,1,0:T(8,128)(2,1)S(1)}, bf16[2,16,1024]{2,1,0:T(8,128)(2,1)S(1)}, u32[]{:S(2)}, u32[]{:S(2)}) collective-permute-start(bf16[2,16,1024]{2,1,0:T(8,128)(2,1)S(1)} %get-tuple-element.55), channel_id=1, source_target_pairs={{0,1},{1,0},{2,3},{3,2},{4,5},{5,4},{6,7},{7,6},{8,9},{9,8},{10,11... | collective-permute-start | bytes 196616 | tf_op jit(solution)/shard_map/ppermute | solution.py:29
  31.2 1.3 %collective-permute-start.9 = (bf16[2,16,1024]{2,1,0:T(8,128)(2,1)S(1)}, bf16[2,16,1024]{2,1,0:T(8,128)(2,1)S(1)}, u32[]{:S(2)}, u32[]{:S(2)}) collective-permute-start(bf16[2,16,1024]{2,1,0:T(8,128)(2,1)S(1)} %get-tuple-element.56), channel_id=1, source_target_pairs={{0,1},{1,0},{2,3},{3,2},{4,5},{5,4},{6,7},{7,6},{8,9},{9,8},{10,11... | collective-permute-start | bytes 196616 | tf_op jit(solution)/shard_map/ppermute | solution.py:29
  31.6 1.3 %collective-permute-start.10 = (bf16[2,16,1024]{2,1,0:T(8,128)(2,1)S(1)}, bf16[2,16,1024]{2,1,0:T(8,128)(2,1)S(1)}, u32[]{:S(2)}, u32[]{:S(2)}) collective-permute-start(bf16[2,16,1024]{2,1,0:T(8,128)(2,1)S(1)} %get-tuple-element.57), channel_id=1, source_target_pairs={{0,1},{1,0},{2,3},{3,2},{4,5},{5,4},{6,7},{7,6},{8,9},{9,8},{10,11... | collective-permute-start | bytes 196616 | tf_op jit(solution)/shard_map/ppermute | solution.py:29
  32.3 1.3 %collective-permute-start.11 = (bf16[2,16,1024]{2,1,0:T(8,128)(2,1)S(1)}, bf16[2,16,1024]{2,1,0:T(8,128)(2,1)S(1)}, u32[]{:S(2)}, u32[]{:S(2)}) collective-permute-start(bf16[2,16,1024]{2,1,0:T(8,128)(2,1)S(1)} %get-tuple-element.58), channel_id=1, source_target_pairs={{0,1},{1,0},{2,3},{3,2},{4,5},{5,4},{6,7},{7,6},{8,9},{9,8},{10,11... | collective-permute-start | bytes 196616 | tf_op jit(solution)/shard_map/ppermute | solution.py:29
  32.5 1.3 %collective-permute-start.12 = (bf16[2,16,1024]{2,1,0:T(8,128)(2,1)S(1)}, bf16[2,16,1024]{2,1,0:T(8,128)(2,1)S(1)}, u32[]{:S(2)}, u32[]{:S(2)}) collective-permute-start(bf16[2,16,1024]{2,1,0:T(8,128)(2,1)S(1)} %get-tuple-element.59), channel_id=1, source_target_pairs={{0,1},{1,0},{2,3},{3,2},{4,5},{5,4},{6,7},{7,6},{8,9},{9,8},{10,11... | collective-permute-start | bytes 196616 | tf_op jit(solution)/shard_map/ppermute | solution.py:29
  34.5 15.3 %collective-permute-start.13 = (bf16[128,1024]{1,0:T(8,128)(2,1)S(1)}, bf16[128,1024]{1,0:T(8,128)(2,1)S(1)}, u32[]{:S(2)}, u32[]{:S(2)}) collective-permute-start(bf16[128,1024]{1,0:T(8,128)(2,1)S(1)} %get-tuple-element.61), channel_id=1, source_target_pairs={{0,2},{2,0},{1,3},{3,1},{4,6},{6,4},{5,7},{7,5},{8,10},{10,8},{9,1... | collective-permute-start | bytes 786440 | tf_op jit(solution)/shard_map/ppermute | solution.py:29
  46.8 3.0 %collective-permute-start.16 = (bf16[2,32,1024]{2,1,0:T(8,128)(2,1)S(1)}, bf16[2,32,1024]{2,1,0:T(8,128)(2,1)S(1)}, u32[]{:S(2)}, u32[]{:S(2)}) collective-permute-start(bf16[2,32,1024]{2,1,0:T(8,128)(2,1)S(1)} %get-tuple-element.66), channel_id=1, source_target_pairs={{0,1},{1,0},{2,3},{3,2},{4,5},{5,4},{6,7},{7,6},{8,9},{9,8},{10,11... | collective-permute-start | bytes 393224 | tf_op jit(solution)/shard_map/ppermute | solution.py:29
  46.9 6.4 %copy-start = (f32[4,64,1024]{2,1,0:T(8,128)S(1)}, f32[4,64,1024]{2,1,0:T(8,128)}, u32[]{:S(2)}) copy-start(f32[4,64,1024]{2,1,0:T(8,128)} %refs_7_.1) | copy-start | bytes 3145732
  46.9 2.9 %collective-permute-start.17 = (bf16[2,32,1024]{2,1,0:T(8,128)(2,1)S(1)}, bf16[2,32,1024]{2,1,0:T(8,128)(2,1)S(1)}, u32[]{:S(2)}, u32[]{:S(2)}) collective-permute-start(bf16[2,32,1024]{2,1,0:T(8,128)(2,1)S(1)} %get-tuple-element.67), channel_id=1, source_target_pairs={{0,1},{1,0},{2,3},{3,2},{4,5},{5,4},{6,7},{7,6},{8,9},{9,8},{10,11... | collective-permute-start | bytes 393224 | tf_op jit(solution)/shard_map/ppermute | solution.py:29
  49.3 2.8 %collective-permute-start.19 = (bf16[2,32,1024]{2,1,0:T(8,128)(2,1)S(1)}, bf16[2,32,1024]{2,1,0:T(8,128)(2,1)S(1)}, u32[]{:S(2)}, u32[]{:S(2)}) collective-permute-start(bf16[2,32,1024]{2,1,0:T(8,128)(2,1)S(1)} %get-tuple-element.72), channel_id=1, source_target_pairs={{0,1},{1,0},{2,3},{3,2},{4,5},{5,4},{6,7},{7,6},{8,9},{9,8},{10,11... | collective-permute-start | bytes 393224 | tf_op jit(solution)/shard_map/ppermute | solution.py:29
  49.4 2.6 %collective-permute-start.20 = (bf16[2,32,1024]{2,1,0:T(8,128)(2,1)S(1)}, bf16[2,32,1024]{2,1,0:T(8,128)(2,1)S(1)}, u32[]{:S(2)}, u32[]{:S(2)}) collective-permute-start(bf16[2,32,1024]{2,1,0:T(8,128)(2,1)S(1)} %get-tuple-element.73), channel_id=1, source_target_pairs={{0,1},{1,0},{2,3},{3,2},{4,5},{5,4},{6,7},{7,6},{8,9},{9,8},{10,11... | collective-permute-start | bytes 393224 | tf_op jit(solution)/shard_map/ppermute | solution.py:29
  50.5 6.4 %collective-permute-start.18 = (bf16[64,1024]{1,0:T(8,128)(2,1)S(1)}, bf16[64,1024]{1,0:T(8,128)(2,1)S(1)}, u32[]{:S(2)}, u32[]{:S(2)}) collective-permute-start(bf16[64,1024]{1,0:T(8,128)(2,1)S(1)} %get-tuple-element.69), channel_id=1, source_target_pairs={{0,2},{2,0},{1,3},{3,1},{4,6},{6,4},{5,7},{7,5},{8,10},{10,8},{9,1... | collective-permute-start | bytes 393224 | tf_op jit(solution)/shard_map/ppermute | solution.py:29
  52.7 6.2 %collective-permute-start.21 = (bf16[64,1024]{1,0:T(8,128)(2,1)S(1)}, bf16[64,1024]{1,0:T(8,128)(2,1)S(1)}, u32[]{:S(2)}, u32[]{:S(2)}) collective-permute-start(bf16[64,1024]{1,0:T(8,128)(2,1)S(1)} %get-tuple-element.75), channel_id=1, source_target_pairs={{0,2},{2,0},{1,3},{3,1},{4,6},{6,4},{5,7},{7,5},{8,10},{10,8},{9,1... | collective-permute-start | bytes 393224 | tf_op jit(solution)/shard_map/ppermute | solution.py:29
  59.6 3.1 %collective-permute-start.24 = (f32[8,128]{1,0:T(8,128)S(1)}, f32[8,128]{1,0:T(8,128)S(1)}, u32[]{:S(2)}, u32[]{:S(2)}) collective-permute-start(f32[8,128]{1,0:T(8,128)S(1)} %get-tuple-element.76.refs_0_.refs_1_), channel_id=1, source_target_pairs={{0,3},{1,2},{2,1},{3,0},{4,7},{5,6},{6,5},{7,4},{8,11},{9,10},{10,... | collective-permute-start | bytes 12296 | tf_op jit(solution)/shard_map/ppermute | solution.py:29
  60.0 3.6 %collective-permute-start.23 = (f32[8,128]{1,0:T(8,128)S(1)}, f32[8,128]{1,0:T(8,128)S(1)}, u32[]{:S(2)}, u32[]{:S(2)}) collective-permute-start(f32[8,128]{1,0:T(8,128)S(1)} %get-tuple-element.76.refs_0_.refs_1_), channel_id=1, source_target_pairs={{0,2},{1,3},{2,0},{3,1},{4,6},{5,7},{6,4},{7,5},{8,10},{9,11},{10,... | collective-permute-start | bytes 12296 | tf_op jit(solution)/shard_map/ppermute | solution.py:29
  61.2 2.4 %collective-permute-start.22 = (f32[8,128]{1,0:T(8,128)S(1)}, f32[8,128]{1,0:T(8,128)S(1)}, u32[]{:S(2)}, u32[]{:S(2)}) collective-permute-start(f32[8,128]{1,0:T(8,128)S(1)} %get-tuple-element.76.refs_0_.refs_1_), channel_id=1, source_target_pairs={{0,1},{1,0},{2,3},{3,2},{4,5},{5,4},{6,7},{7,6},{8,9},{9,8},{10,11... | collective-permute-start | bytes 12296 | tf_op jit(solution)/shard_map/ppermute | solution.py:29
  64.3 13.3 %collective-permute-start.25 = (bf16[64,1024]{1,0:T(8,128)(2,1)S(1)}, bf16[64,1024]{1,0:T(8,128)(2,1)S(1)}, u32[]{:S(2)}, u32[]{:S(2)}) collective-permute-start(bf16[64,1024]{1,0:T(8,128)(2,1)S(1)} %gradient.3.refs_0_), channel_id=1, source_target_pairs={{0,12},{4,8},{8,4},{12,0},{1,13},{5,9},{9,5},{13,1},{2,14},{6,10},... | collective-permute-start | bytes 393224 | tf_op jit(solution)/shard_map/ppermute | solution.py:29
  67.8 9.8 %collective-permute-start.26 = (bf16[64,1024]{1,0:T(8,128)(2,1)S(1)}, bf16[64,1024]{1,0:T(8,128)(2,1)S(1)}, u32[]{:S(2)}, u32[]{:S(2)}) collective-permute-start(bf16[64,1024]{1,0:T(8,128)(2,1)S(1)} %gradient.4.refs_0_), channel_id=1, source_target_pairs={{0,8},{4,12},{8,0},{12,4},{1,9},{5,13},{9,1},{13,5},{2,10},{6,14},... | collective-permute-start | bytes 393224 | tf_op jit(solution)/shard_map/ppermute | solution.py:29
  68.7 8.9 %collective-permute-start.27 = (bf16[64,1024]{1,0:T(8,128)(2,1)S(1)}, bf16[64,1024]{1,0:T(8,128)(2,1)S(1)}, u32[]{:S(2)}, u32[]{:S(2)}) collective-permute-start(bf16[64,1024]{1,0:T(8,128)(2,1)S(1)} %get-tuple-element.81), channel_id=1, source_target_pairs={{0,4},{4,0},{8,12},{12,8},{1,5},{5,1},{9,13},{13,9},{2,6},{6,2},{1... | collective-permute-start | bytes 393224 | tf_op jit(solution)/shard_map/ppermute | solution.py:29
  (2 other events, 1.3 us)

commit v13 on v12

--- a/solution.py
+++ b/solution.py
@@ -122,19 +122,6 @@
         table[r, LANES:] = (-(sa * cb + ca * sb)).astype(BF16)
 
 
-def make_table(scal, trig, classes, span, parts):
-    return pl.pallas_call(
-        functools.partial(table_kernel, classes, parts),
-        out_shape=jax.ShapeDtypeStruct((classes, 2 * LANES, span), BF16),
-        in_specs=[SMEM, VMEM],
-        out_specs=VMEM,
-        scratch_shapes=[pltpu.VMEM((2, LANES, span), F32)],
-        compiler_params=params(12),
-        cost_estimate=SMALL,
-        name="table",
-    )(scal, jnp.asarray(trig))
-
-
 def perm_kernel(perm):
     part = perm.shape[0]
     classes = part // LANES
@@ -160,7 +147,7 @@
     return (lax.broadcasted_iota(jnp.int32, (channels, row.shape[1]), 0) == row).astype(BF16)
 
 
-def rows_kernel(used, sends, messages, scal, after, here, *refs):
+def rows_kernel(used, sends, messages, scal, here, *refs):
     held, perm, src_ids, refs = refs[:used], refs[used], refs[used + 1 : used + 1 + sends], refs[used + 1 + sends :]
     outs, kept = refs[:-1], refs[-1]
     _, _, channels, part = kept.shape
@@ -182,23 +169,23 @@
                 out[u, half] = y[at : at + count]
 
 
-def gather_rows(scal, after, here, held, perm, src_ids, messages):
+def gather_rows(scal, here, held, perm, src_ids, messages):
     used = len(held)
     channels, part = held[0].shape[-2:]
     *sent, kept = pl.pallas_call(
         functools.partial(rows_kernel, used, len(src_ids), messages),
         out_shape=[jax.ShapeDtypeStruct((used, 2, m[2], part), BF16) for m in messages]
         + [jax.ShapeDtypeStruct((used, 2, channels, part), BF16)],
-        in_specs=[SMEM, ANY] + [VMEM] * (used + 2 + len(src_ids)),
+        in_specs=[SMEM] + [VMEM] * (used + 2 + len(src_ids)),
         out_specs=[VMEM] * (len(messages) + 1),
         compiler_params=params(16),
         cost_estimate=SMALL,
         name="rows",
-    )(scal, after, here, *held, perm, *src_ids[::-1])
+    )(scal, here, *held, perm, *src_ids[::-1])
     return sent, kept
 
 
-def own_kernel(kept, rec_ids, own):
+def own_kernel(classes, parts, scal, kept, rec_ids, trig, own, table, base):
     units, used, _, slots, _ = own.shape
     pick = picks([rec_ids.at[d : d + 1] for d in range(units)], kept.shape[2])
     for u in range(used):
@@ -208,20 +195,25 @@
             ).astype(BF16)
             for d in range(units):
                 own[d, u, half] = y[d * slots : (d + 1) * slots]
-
-
-def gather_own(kept, rec_ids):
+    table_kernel(classes, parts, scal, trig, table, base)
+
+
+def gather_own(scal, kept, rec_ids, trig, classes, span, parts):
     used, _, _, part = kept.shape
     units, slots = rec_ids.shape
     return pl.pallas_call(
-        own_kernel,
-        out_shape=jax.ShapeDtypeStruct((units, used, 2, slots, part), BF16),
-        in_specs=[VMEM] * 2,
-        out_specs=VMEM,
+        functools.partial(own_kernel, classes, parts),
+        out_shape=[
+            jax.ShapeDtypeStruct((units, used, 2, slots, part), BF16),
+            jax.ShapeDtypeStruct((classes, 2 * LANES, span), BF16),
+        ],
+        in_specs=[SMEM] + [VMEM] * 3,
+        out_specs=[VMEM] * 2,
+        scratch_shapes=[pltpu.VMEM((2, LANES, span), F32)],
         compiler_params=params(16),
         cost_estimate=SMALL,
         name="own",
-    )(kept, rec_ids)
+    )(scal, kept, rec_ids, jnp.asarray(trig))
 
 
 def combine(values, classes, outputs, origin, span, period):
@@ -456,29 +448,32 @@
     return both[:, 0:1], both[:, 1:2]
 
 
-def gradient_kernel(lag_total, q, pieces, parts, skip, scal, *refs):
-    refs = refs[skip:]
-    sums, corr, refs = refs[:parts], refs[parts], refs[parts + 1 :]
-    targets, outs = refs[: len(pieces)], refs[len(pieces) :]
-    inverse, bending = slot_scales(sums, lag_total, q)
-    for target, out, (unit, first, count, at) in zip(targets, outs, placed(pieces)):
-        slot = first + lax.broadcasted_iota(jnp.int32, (count, 1), 0)
-        valid = jnp.where(slot < scal[COUNT + unit], inverse[at], 0.0)
-        normed = corr[at] * inverse[at]
-        out[...] = ((normed - target[0] - normed * bending[at]) * valid).astype(BF16)
-
-
-def gradients(scal, lag_total, q, pieces, after, sums, corr, observed):
-    lag_dev = corr.shape[1]
+def gradient_kernel(lag_total, chunks, parts, skip, scal, *refs):
+    sums, refs = refs[skip : skip + parts], refs[skip + parts :]
+    corrs, refs = refs[: len(chunks)], refs[len(chunks) :]
+    targets, outs = refs[: len(refs) // 2], refs[len(refs) // 2 :]
+    i = 0
+    for corr, (q, pieces) in zip(corrs, chunks):
+        inverse, bending = slot_scales(sums, lag_total, q)
+        for unit, first, count, at in placed(pieces):
+            slot = first + lax.broadcasted_iota(jnp.int32, (count, 1), 0)
+            valid = jnp.where(slot < scal[COUNT + unit], inverse[at], 0.0)
+            normed = corr[at] * inverse[at]
+            outs[i][...] = ((normed - targets[i][0] - normed * bending[at]) * valid).astype(BF16)
+            i += 1
+
+
+def gradients(scal, lag_total, chunks, after, sums, corrs, observed):
+    lag_dev = observed.shape[2]
+    pieces = [p for _, some in chunks for p in some]
     outs = [jax.ShapeDtypeStruct((p[2], lag_dev), BF16) for p in pieces]
     return pl.pallas_call(
-        functools.partial(gradient_kernel, lag_total, q, pieces, len(sums), len(after)),
+        functools.partial(gradient_kernel, lag_total, chunks, len(sums), len(after)),
         grid_spec=pltpu.PrefetchScalarGridSpec(
             num_scalar_prefetch=1,
             grid=(1,),
             in_specs=[ANY] * len(after)
-            + [whole(sums[0].shape)] * len(sums)
-            + [whole(corr.shape)]
+            + [whole(x.shape) for x in (*sums, *corrs)]
             + target_specs(pieces, lag_dev),
             out_specs=[whole(o.shape) for o in outs],
         ),
@@ -486,7 +481,7 @@
         compiler_params=params(16),
         cost_estimate=SMALL,
         name="gradient",
-    )(scal, *after, *sums, corr, *[observed] * len(pieces))
+    )(scal, *after, *sums, *corrs, *[observed] * len(pieces))
 
 
 def normed_kernel(lag_total, chunks, parts, scal, *refs):
@@ -556,17 +551,10 @@
     some = slots // 2
     shifts = range(places)
 
-    held = [
-        swapped(
-            lax.dynamic_slice(
-                spectra, (0, 0, 0, (column ^ s) * part), (1, 2, channels, part)
-            ),
-            "win",
-            columns,
-            s,
-        )
-        for s in range(columns)
-    ]
+    def cut(values, s):
+        return lax.dynamic_slice(values, (0, 0, 0, (column ^ s) * part), (1, 2, channels, part))
+
+    here, *held = [swapped(cut(spectra, s), "win", columns, s) for s in range(columns)]
     scal, wanted, rec_ids = index(
         window_keep, owners, pair_count, pair_src, pair_rec, places
     )
@@ -581,7 +569,6 @@
     direct = places == blocks
     src_ids = [swapped(wanted[d], "recv", places, d) for d in reversed(shifts)][::-1]
     trig = tables(classes, span, period, bins_dev, columns, cores)
-    table = make_table(scal, trig, classes, span, peers)
     if direct and blocks == 4:
         chunks = [
             [(0, 0, slots), (1, 0, slots)],
@@ -594,8 +581,8 @@
         messages = [piece for pieces in chunks for piece in pieces]
     else:
         messages = [(d, 0, slots) for d in shifts]
-    sent, kept = gather_rows(scal, table, held[0], held[1:], make_perm(part), src_ids, messages)
-    own_rows = gather_own(kept, rec_ids)
+    sent, kept = gather_rows(scal, here, held, make_perm(part), src_ids, messages)
+    own_rows, table = gather_own(scal, kept, rec_ids, trig, classes, span, peers)
     arrived = [swapped(x, "recv", places, m[0]) for m, x in reversed(list(zip(messages, sent)))][::-1]
     if not direct:
         stacked = jnp.stack(arrived)
@@ -623,9 +610,10 @@
         all_sums = [sums]
     sums = [swapped(sums, ("win", "freq"), peers, s) for s in range(peers)]
     after = []
-    for q in reversed(range(len(chunks))):
-        pieces = chunks[q]
-        grads = gradients(scal, lag_total, q, pieces, after, sums, corrs[q], observed)
+    numbered = list(enumerate(chunks))
+    for group in (numbered[:0:-1], numbered[:1]):
+        grads = gradients(scal, lag_total, group, after, sums, [corrs[q] for q, _ in group], observed)
+        pieces = [p for _, some_pieces in group for p in some_pieces]
         after = [grads[0]]
         if not direct:
             stacked = jnp.stack(list(grads) + [jnp.zeros_like(grads[0])])

time: 78.9 us -> 79.7 us (1.010)
    pallas_call x5 -> x3, Pallas kernels: 4.61 us -> 4.7 us  [the longest x1 3.07 us: gather_own(): pl.pallas_call(functools.partial(own_kernel, classes, parts), out_shape=[...]
  transfers between devices with their start and end apart: 28 -> 28, of which waited for: 12 -> 13; matrix products, arithmetic and copies ran while one was open for 0% -> 0% of each run, Pallas kernels for 24% -> 24%
where the time goes in v13:
time: 79.7 us; the launch traced here: 79.5 us
  waiting for transfers between devices  26.6 us (33%)
  starting transfers between devices  24.3 us (30%)
  Pallas kernels  23.2 us (29%)
  local copies, waits for them, and re-layouts  4 us (5%)
  between operations  1.48 us (2%)
    ppermute x28, waiting for transfers between devices, swapped(): return lax.ppermute(value, axis, [(i, i ^ step) for i in range(size)])  26.6 us
    ppermute x28, starting transfers between devices, swapped(): return lax.ppermute(value, axis, [(i, i ^ step) for i in range(size)])  24.3 us
    pallas_call x3, Pallas kernels, lag_parts(): pl.pallas_call(functools.partial(lags_kernel, geometry, split, len(after)...  5.94 us
    pallas_call x1, Pallas kernels, normed_rows(): pl.pallas_call(functools.partial(normed_kernel, lag_total, chunks, len(su...  3.22 us
    pallas_call x1, Pallas kernels, gather_own(): pl.pallas_call(functools.partial(own_kernel, classes, parts), out_shape=[...  3.07 us
    unnamed x12, local copies, waits for them, and re-layouts  2.68 us
    pallas_call x3, Pallas kernels, lag_stats(): pl.pallas_call(functools.partial(stats_kernel, scale, q, pieces, len(more...  2.22 us
    pallas_call x3, Pallas kernels, add_cores(): pl.pallas_call(functools.partial(cores_kernel, len(after), len(more)), ou...  2.06 us
  transfers between devices with their start and end apart: 28, of which 13 were waited for; matrix products, arithmetic and copies ran while one was open for 0% of the time, Pallas kernels for 24%

profile of v13, /device:TPU:0, one launch (start us, length us, event | category | flops | bytes accessed | tf_op | source)
XLA Modules:
  0.0 79.5 jit_solution(5873277186996049723)
XLA Ops:
  0.7 1.3 %constant_dynamic-slice_fusion = (bf16[1,2,128,1024]{3,2,1,0:T(8,128)(2,1)S(1)}, bf16[1,2,128,1024]{3,2,1,0:T(8,128)(2,1)S(1)}) fusion(bf16[1,2,128,2048]{3,2,1,0:T(8,128)(2,1)} %param.8, s32[]{:T(128)S(6)} %select_n.7, s32[]{:T(128)S(6)} %select_n.6), kind=kLoop, calls=%fused_computation | loop fusion | bytes 2097160 | tf_op jit(solution)/shard_map/dynamic_slice | solution.py:555
  2.0 3.0 %collective-permute-start = (bf16[1,2,128,1024]{3,2,1,0:T(8,128)(2,1)S(1)}, bf16[1,2,128,1024]{3,2,1,0:T(8,128)(2,1)S(1)}, u32[]{:S(2)}, u32[]{:S(2)}) collective-permute-start(bf16[1,2,128,1024]{3,2,1,0:T(8,128)(2,1)S(1)} %get-tuple-element.90), channel_id=1, source_target_pairs={{0,2},{2,0},{1,3},{3,1},{4,6},{6,4},{5,7},{7,5},{8,10},{10,8},{9,1... | collective-permute-start | bytes 1572872 | tf_op jit(solution)/shard_map/ppermute | solution.py:29
  8.3 1.2 %index.1 = (s32[128]{0:T(128)S(1)}, s32[1,64]{1,0:T(1,128)S(1)}, s32[1,64]{1,0:T(1,128)S(1)}, s32[1,64]{1,0:T(1,128)S(1)}, s32[1,64]{1,0:T(1,128)S(1)}, /*index=5*/s32[4,64]{1,0:T(4,128)S(1)}) custom-call(s32[1]{0:T(128)S(6)} %copy.10.refs_0_, s32[4]{0:T(128)S(1)} %copy-done.4, s32[4]{0:T(128)S(1)} %bitcast.1, s32[4,64]{1,0:T(4,128)S(1)} %copy-done.2, ...), custom_call_target="tpu_custom_call" | custom-call | flops 1 | bytes 1 | tf_op jit(solution)/shard_map/index/pallas_call | solution.py:92
  9.5 3.7 %collective-permute-start.1 = (s32[1,64]{1,0:T(1,128)S(1)}, s32[1,64]{1,0:T(1,128)S(1)}, u32[]{:S(2)}, u32[]{:S(2)}) collective-permute-start(s32[1,64]{1,0:T(1,128)S(1)} %get-tuple-element.47), channel_id=1, source_target_pairs={{0,12},{4,8},{8,4},{12,0},{1,13},{5,9},{9,5},{13,1},{2,14},{6,10},... | collective-permute-start | bytes 776 | tf_op jit(solution)/shard_map/ppermute | solution.py:29
  13.2 0.8 collective-permute-start.3
  14.9 2.7 %collective-permute-done.2.refs_3_.refs_1_ = s32[1,64]{1,0:T(1,128)S(1)} collective-permute-done((s32[1,64]{1,0:T(1,128)S(1)}, s32[1,64]{1,0:T(1,128)S(1)}, u32[]{:S(2)}, u32[]{:S(2)}) %collective-permute-start.2) | collective-permute-done | bytes 288 | tf_op jit(solution)/shard_map/ppermute | solution.py:29
  17.7 1.6 %rows.1 = (bf16[1,2,64,1024]{3,2,1,0:T(8,128)(2,1)S(1)}, bf16[1,2,64,1024]{3,2,1,0:T(8,128)(2,1)S(1)}, bf16[1,2,64,1024]{3,2,1,0:T(8,128)(2,1)S(1)}, bf16[1,2,64...) custom-call(s32[128]{0:T(128)S(1)} %get-tuple-element.46.scal, ...), custom_call_target="tpu_custom_call" | custom-call | flops 1 | bytes 1 | tf_op jit(solution)/shard_map/rows/pallas_call | solution.py:175
  19.2 1.1 %collective-permute-start.4 = (bf16[1,2,64,1024]{3,2,1,0:T(8,128)(2,1)S(1)}, bf16[1,2,64,1024]{3,2,1,0:T(8,128)(2,1)S(1)}, u32[]{:S(2)}, u32[]{:S(2)}) collective-permute-start(bf16[1,2,64,1024]{3,2,1,0:T(8,128)(2,1)S(1)} %get-tuple-element.52), channel_id=1, source_target_pairs={{0,4},{4,0},{8,12},{12,8},{1,5},{5,1},{9,13},{13,9},{2,6},{6,2},{1... | collective-permute-start | bytes 786440 | tf_op jit(solution)/shard_map/ppermute | solution.py:29
  20.4 2.5 %collective-permute-start.14 = (bf16[1,2,64,1024]{3,2,1,0:T(8,128)(2,1)S(1)}, bf16[1,2,64,1024]{3,2,1,0:T(8,128)(2,1)S(1)}, u32[]{:S(2)}, u32[]{:S(2)}) collective-permute-start(bf16[1,2,64,1024]{3,2,1,0:T(8,128)(2,1)S(1)} %get-tuple-element.69), channel_id=1, source_target_pairs={{0,12},{4,8},{8,4},{12,0},{1,13},{5,9},{9,5},{13,1},{2,14},{6,10},... | collective-permute-start | bytes 786440 | tf_op jit(solution)/shard_map/ppermute | solution.py:29
  23.0 3.1 %own.1 = (bf16[4,1,2,64,1024]{4,3,2,1,0:T(8,128)(2,1)S(1)}, bf16[8,256,1024]{2,1,0:T(8,128)(2,1)S(1)}) custom-call(s32[128]{0:T(128)S(1)} %get-tuple-element.46.scal, bf16[1,2,128,1024]{3,2,1,0:T(8,128)(2,1)S(1)} %get-tuple-element.53.kept, s32[4,64]{1,0:T(4,128)S(1)} %get-tuple-element.54.rec_ids, f32[2,56,1024]{2,1,0:T(8,128)S(1)} %copy-done.1), custom_call_target="tpu_custom_call" | custom-call | flops 1 | bytes 1 | tf_op jit(solution)/shard_map/own/pallas_call | solution.py:204
  26.0 1.1 %collective-permute-done.4.refs_1_ = bf16[1,2,64,1024]{3,2,1,0:T(8,128)(2,1)S(1)} collective-permute-done((bf16[1,2,64,1024]{3,2,1,0:T(8,128)(2,1)S(1)}, bf16[1,2,64,1024]{3,2,1,0:T(8,128)(2,1)S(1)}, u32[]{:S(2)}, u32[]{:S(2)}) %collective-permute-start.4) | collective-permute-done | bytes 262176 | tf_op jit(solution)/shard_map/ppermute | solution.py:29
  27.4 2.5 %lags.3 = (f32[2,128,1024]{2,1,0:T(8,128)S(1)}, bf16[2,16,1024]{2,1,0:T(8,128)(2,1)S(1)}, bf16[2,16,1024]{2,1,0:T(8,128)(2,1)S(1)}, bf16[2,16,1024]{2,1,0:T(8,12...) custom-call(s32[128]{0:T(128)S(1)} %get-tuple-element.46.scal, ...), custom_call_target="tpu_custom_call" | custom-call | flops 20000000000 | bytes 1048576 | tf_op jit(solution)/shard_map/lags/pallas_call | solution.py:331
  33.0 0.7 collective-permute-done.11.refs_7_
  33.9 0.8 %cores.3 = (f32[128,1024]{1,0:T(8,128)S(1)}, bf16[128,1024]{1,0:T(8,128)(2,1)S(1)}) custom-call(s32[128]{0:T(128)S(1)} %get-tuple-element.46.scal, f32[2,128,1024]{2,1,0:T(8,128)S(1)} %get-tuple-element.57.refs_0_, bf16[2,16,1024]{2,1,0:T(8,128)(2,1)S(1)} %collective-permute-done.5.refs_1_, bf16[2,16,1024]{2,1,0:T(8,128)(2,1)S(1)} %collective-permute-done.6.refs_2_, ...), custom_call_target="tpu_custom_call" | custom-call | flops 1 | bytes 1 | tf_op jit(solution)/shard_map/cores/pallas_call | solution.py:366
  34.7 1.6 %collective-permute-start.13 = (bf16[128,1024]{1,0:T(8,128)(2,1)S(1)}, bf16[128,1024]{1,0:T(8,128)(2,1)S(1)}, u32[]{:S(2)}, u32[]{:S(2)}) collective-permute-start(bf16[128,1024]{1,0:T(8,128)(2,1)S(1)} %get-tuple-element.67), channel_id=1, source_target_pairs={{0,2},{2,0},{1,3},{3,1},{4,6},{6,4},{5,7},{7,5},{8,10},{10,8},{9,1... | collective-permute-start | bytes 786440 | tf_op jit(solution)/shard_map/ppermute | solution.py:29
  36.3 8.7 %collective-permute-done.15.refs_2_ = bf16[1,2,64,1024]{3,2,1,0:T(8,128)(2,1)S(1)} collective-permute-done((bf16[1,2,64,1024]{3,2,1,0:T(8,128)(2,1)S(1)}, bf16[1,2,64,1024]{3,2,1,0:T(8,128)(2,1)S(1)}, u32[]{:S(2)}, u32[]{:S(2)}) %collective-permute-start.15) | collective-permute-done | bytes 262176 | tf_op jit(solution)/shard_map/ppermute | solution.py:29
  45.1 1.7 %lags.4 = (f32[2,64,1024]{2,1,0:T(8,128)S(1)}, bf16[2,32,1024]{2,1,0:T(8,128)(2,1)S(1)}, bf16[2,32,1024]{2,1,0:T(8,128)(2,1)S(1)}) custom-call(s32[128]{0:T(128)S(1)} %get-tuple-element.46.scal, bf16[8,128,256]{2,1,0:T(8,128)(2,1)S(1)} %cross.4.refs_0_, bf16[8,256,1024]{2,1,0:T(8,128)(2,1)S(1)} %get-tuple-element.56.refs_1_), custom_call_target="tpu_custom_call" | custom-call | flops 1 | bytes 1 | tf_op jit(solution)/shard_map/lags/pallas_call | solution.py:331
  47.6 1.7 %lags.5 = (f32[2,64,1024]{2,1,0:T(8,128)S(1)}, bf16[2,32,1024]{2,1,0:T(8,128)(2,1)S(1)}, bf16[2,32,1024]{2,1,0:T(8,128)(2,1)S(1)}) custom-call(s32[128]{0:T(128)S(1)} %get-tuple-element.46.scal, bf16[8,128,256]{2,1,0:T(8,128)(2,1)S(1)} %cross.5.refs_0_, bf16[8,256,1024]{2,1,0:T(8,128)(2,1)S(1)} %get-tuple-element.56.refs_1_), custom_call_target="tpu_custom_call" | custom-call | flops 1 | bytes 1 | tf_op jit(solution)/shard_map/lags/pallas_call | solution.py:331
  50.5 1.6 %collective-permute-start.18 = (bf16[64,1024]{1,0:T(8,128)(2,1)S(1)}, bf16[64,1024]{1,0:T(8,128)(2,1)S(1)}, u32[]{:S(2)}, u32[]{:S(2)}) collective-permute-start(bf16[64,1024]{1,0:T(8,128)(2,1)S(1)} %get-tuple-element.75), channel_id=1, source_target_pairs={{0,2},{2,0},{1,3},{3,1},{4,6},{6,4},{5,7},{7,5},{8,10},{10,8},{9,1... | collective-permute-start | bytes 393224 | tf_op jit(solution)/shard_map/ppermute | solution.py:29
  53.3 0.8 stats.3
  54.1 2.8 %collective-permute-done.18.refs_2_ = bf16[64,1024]{1,0:T(8,128)(2,1)S(1)} collective-permute-done((bf16[64,1024]{1,0:T(8,128)(2,1)S(1)}, bf16[64,1024]{1,0:T(8,128)(2,1)S(1)}, u32[]{:S(2)}, u32[]{:S(2)}) %collective-permute-start.18) | collective-permute-done | bytes 131104 | tf_op jit(solution)/shard_map/ppermute | solution.py:29
  57.7 1.2 %collective-permute-done.21.refs_2_ = bf16[64,1024]{1,0:T(8,128)(2,1)S(1)} collective-permute-done((bf16[64,1024]{1,0:T(8,128)(2,1)S(1)}, bf16[64,1024]{1,0:T(8,128)(2,1)S(1)}, u32[]{:S(2)}, u32[]{:S(2)}) %collective-permute-start.21) | collective-permute-done | bytes 131104 | tf_op jit(solution)/shard_map/ppermute | solution.py:29
  59.6 1.6 %collective-permute-start.23 = (f32[8,128]{1,0:T(8,128)S(1)}, f32[8,128]{1,0:T(8,128)S(1)}, u32[]{:S(2)}, u32[]{:S(2)}) collective-permute-start(f32[8,128]{1,0:T(8,128)S(1)} %get-tuple-element.82.refs_0_.refs_1_), channel_id=1, source_target_pairs={{0,2},{1,3},{2,0},{3,1},{4,6},{5,7},{6,4},{7,5},{8,10},{9,11},{10,... | collective-permute-start | bytes 12296 | tf_op jit(solution)/shard_map/ppermute | solution.py:29
  61.5 1.8 %collective-permute-done.23.refs_2_.refs_3_ = f32[8,128]{1,0:T(8,128)S(1)} collective-permute-done((f32[8,128]{1,0:T(8,128)S(1)}, f32[8,128]{1,0:T(8,128)S(1)}, u32[]{:S(2)}, u32[]{:S(2)}) %collective-permute-start.23) | collective-permute-done | bytes 4128 | tf_op jit(solution)/shard_map/ppermute | solution.py:29
  63.3 0.9 %collective-permute-done.24.refs_3_.refs_4_ = f32[8,128]{1,0:T(8,128)S(1)} collective-permute-done((f32[8,128]{1,0:T(8,128)S(1)}, f32[8,128]{1,0:T(8,128)S(1)}, u32[]{:S(2)}, u32[]{:S(2)}) %collective-permute-start.24) | collective-permute-done | bytes 4128 | tf_op jit(solution)/shard_map/ppermute | solution.py:29
  64.2 0.8 %gradient.2 = (bf16[64,1024]{1,0:T(8,128)(2,1)S(1)}, bf16[64,1024]{1,0:T(8,128)(2,1)S(1)}) custom-call(s32[128]{0:T(128)S(1)} %get-tuple-element.46.scal, f32[8,128]{1,0:T(8,128)S(1)} %get-tuple-element.82.refs_0_.refs_1_, f32[8,128]{1,0:T(8,128)S(1)} %collective-permute-done.22.refs_1_.refs_2_, f32[8,128]{1,0:T(8,128)S(1)} %collective-permute-done.23.refs_2_.refs_3_, ...), custom_call_target="tpu_custom_call" | custom-call | flops 1 | bytes 1 | tf_op jit(solution)/shard_map/gradient/pallas_call | solution.py:470
  65.1 2.7 %collective-permute-start.25 = (bf16[64,1024]{1,0:T(8,128)(2,1)S(1)}, bf16[64,1024]{1,0:T(8,128)(2,1)S(1)}, u32[]{:S(2)}, u32[]{:S(2)}) collective-permute-start(bf16[64,1024]{1,0:T(8,128)(2,1)S(1)} %get-tuple-element.86.refs_0_), channel_id=1, source_target_pairs={{0,12},{4,8},{8,4},{12,0},{1,13},{5,9},{9,5},{13,1},{2,14},{6,10},... | collective-permute-start | bytes 393224 | tf_op jit(solution)/shard_map/ppermute | solution.py:29
  67.8 0.8 %gradient.3 = (bf16[64,1024]{1,0:T(8,128)(2,1)S(1)}, bf16[64,1024]{1,0:T(8,128)(2,1)S(1)}) custom-call(s32[128]{0:T(128)S(1)} %get-tuple-element.46.scal, bf16[64,1024]{1,0:T(8,128)(2,1)S(1)} %get-tuple-element.86.refs_0_, f32[8,128]{1,0:T(8,128)S(1)} %get-tuple-element.82.refs_0_.refs_1_, f32[8,128]{1,0:T(8,128)S(1)} %collective-permute-done.22.refs_1_.refs_2_, ...), custom_call_target="tpu_custom_call" | custom-call | flops 1 | bytes 1 | tf_op jit(solution)/shard_map/gradient/pallas_call | solution.py:470
  68.6 1.8 %collective-permute-start.27 = (bf16[64,1024]{1,0:T(8,128)(2,1)S(1)}, bf16[64,1024]{1,0:T(8,128)(2,1)S(1)}, u32[]{:S(2)}, u32[]{:S(2)}) collective-permute-start(bf16[64,1024]{1,0:T(8,128)(2,1)S(1)} %get-tuple-element.89), channel_id=1, source_target_pairs={{0,4},{4,0},{8,12},{12,8},{1,5},{5,1},{9,13},{13,9},{2,6},{6,2},{1... | collective-permute-start | bytes 393224 | tf_op jit(solution)/shard_map/ppermute | solution.py:29
  70.4 3.2 %normed.1 = f32[4,64,1024]{2,1,0:T(8,128)} custom-call(s32[128]{0:T(128)S(1)} %get-tuple-element.46.scal, f32[8,128]{1,0:T(8,128)S(1)} %get-tuple-element.82.refs_0_.refs_1_, f32[8,128]{1,0:T(8,128)S(1)} %collective-permute-done.22.refs_1_.refs_2_, f32[8,128]{1,0:T(8,128)S(1)} %collective-permute-done.23.refs_2_.refs_3_, ...), custom_call_target="tpu_custom_call" | custom-call | flops 1 | bytes 1 | tf_op jit(solution)/shard_map/normed/pallas_call | solution.py:501
  73.6 4.8 %collective-permute-done.26.refs_5_ = bf16[64,1024]{1,0:T(8,128)(2,1)S(1)} collective-permute-done((bf16[64,1024]{1,0:T(8,128)(2,1)S(1)}, bf16[64,1024]{1,0:T(8,128)(2,1)S(1)}, u32[]{:S(2)}, u32[]{:S(2)}) %collective-permute-start.26) | collective-permute-done | bytes 131104 | tf_op jit(solution)/shard_map/ppermute | solution.py:29
  78.4 1.1 %adjoint.1 = f32[128,1024]{1,0:T(8,128)} custom-call(s32[1,64]{1,0:T(1,128)S(1)} %collective-permute-done.1.refs_2_.refs_0_, s32[1,64]{1,0:T(1,128)S(1)} %collective-permute-done.2.refs_3_.refs_1_, s32[1,64]{1,0:T(1,128)S(1)} %get-tuple-element.50.refs_5_.refs_2_, s32[1,64]{1,0:T(1,128)S(1)} %collective-permute-done.3.refs_4_.refs_3_, ...), custom_call_target="tpu_custom_call" | custom-call | flops 1 | bytes 1 | tf_op jit(solution)/shard_map/adjoint/pallas_call | solution.py:525
  (57 shorter events, 12.3 us)
Async XLA Ops:
  0.6 22.3 %copy-start.1 = (f32[2,56,1024]{2,1,0:T(8,128)S(1)}, f32[2,56,1024]{2,1,0:T(8,128)}, u32[]{:S(2)}) copy-start(f32[2,56,1024]{2,1,0:T(8,128)} %constant.16.clone.trig) | copy-start | bytes 1376260
  2.0 15.7 %collective-permute-start = (bf16[1,2,128,1024]{3,2,1,0:T(8,128)(2,1)S(1)}, bf16[1,2,128,1024]{3,2,1,0:T(8,128)(2,1)S(1)}, u32[]{:S(2)}, u32[]{:S(2)}) collective-permute-start(bf16[1,2,128,1024]{3,2,1,0:T(8,128)(2,1)S(1)} %get-tuple-element.90), channel_id=1, source_target_pairs={{0,2},{2,0},{1,3},{3,1},{4,6},{6,4},{5,7},{7,5},{8,10},{10,8},{9,1... | collective-permute-start | bytes 1572872 | tf_op jit(solution)/shard_map/ppermute | solution.py:29
  5.6 0.7 copy-start.2
  6.3 0.7 copy-start.3
  9.5 5.4 %collective-permute-start.1 = (s32[1,64]{1,0:T(1,128)S(1)}, s32[1,64]{1,0:T(1,128)S(1)}, u32[]{:S(2)}, u32[]{:S(2)}) collective-permute-start(s32[1,64]{1,0:T(1,128)S(1)} %get-tuple-element.47), channel_id=1, source_target_pairs={{0,12},{4,8},{8,4},{12,0},{1,13},{5,9},{9,5},{13,1},{2,14},{6,10},... | collective-permute-start | bytes 776 | tf_op jit(solution)/shard_map/ppermute | solution.py:29
  13.2 4.4 %collective-permute-start.2 = (s32[1,64]{1,0:T(1,128)S(1)}, s32[1,64]{1,0:T(1,128)S(1)}, u32[]{:S(2)}, u32[]{:S(2)}) collective-permute-start(s32[1,64]{1,0:T(1,128)S(1)} %get-tuple-element.48), channel_id=1, source_target_pairs={{0,8},{4,12},{8,0},{12,4},{1,9},{5,13},{9,1},{13,5},{2,10},{6,14},... | collective-permute-start | bytes 776 | tf_op jit(solution)/shard_map/ppermute | solution.py:29
  13.2 4.4 %collective-permute-start.3 = (s32[1,64]{1,0:T(1,128)S(1)}, s32[1,64]{1,0:T(1,128)S(1)}, u32[]{:S(2)}, u32[]{:S(2)}) collective-permute-start(s32[1,64]{1,0:T(1,128)S(1)} %get-tuple-element.49), channel_id=1, source_target_pairs={{0,4},{4,0},{8,12},{12,8},{1,5},{5,1},{9,13},{13,9},{2,6},{6,2},{1... | collective-permute-start | bytes 776 | tf_op jit(solution)/shard_map/ppermute | solution.py:29
  19.2 7.9 %collective-permute-start.4 = (bf16[1,2,64,1024]{3,2,1,0:T(8,128)(2,1)S(1)}, bf16[1,2,64,1024]{3,2,1,0:T(8,128)(2,1)S(1)}, u32[]{:S(2)}, u32[]{:S(2)}) collective-permute-start(bf16[1,2,64,1024]{3,2,1,0:T(8,128)(2,1)S(1)} %get-tuple-element.52), channel_id=1, source_target_pairs={{0,4},{4,0},{8,12},{12,8},{1,5},{5,1},{9,13},{13,9},{2,6},{6,2},{1... | collective-permute-start | bytes 786440 | tf_op jit(solution)/shard_map/ppermute | solution.py:29
  20.4 15.9 %collective-permute-start.14 = (bf16[1,2,64,1024]{3,2,1,0:T(8,128)(2,1)S(1)}, bf16[1,2,64,1024]{3,2,1,0:T(8,128)(2,1)S(1)}, u32[]{:S(2)}, u32[]{:S(2)}) collective-permute-start(bf16[1,2,64,1024]{3,2,1,0:T(8,128)(2,1)S(1)} %get-tuple-element.69), channel_id=1, source_target_pairs={{0,12},{4,8},{8,4},{12,0},{1,13},{5,9},{9,5},{13,1},{2,14},{6,10},... | collective-permute-start | bytes 786440 | tf_op jit(solution)/shard_map/ppermute | solution.py:29
  22.8 22.1 %collective-permute-start.15 = (bf16[1,2,64,1024]{3,2,1,0:T(8,128)(2,1)S(1)}, bf16[1,2,64,1024]{3,2,1,0:T(8,128)(2,1)S(1)}, u32[]{:S(2)}, u32[]{:S(2)}) collective-permute-start(bf16[1,2,64,1024]{3,2,1,0:T(8,128)(2,1)S(1)} %get-tuple-element.70), channel_id=1, source_target_pairs={{0,8},{4,12},{8,0},{12,4},{1,9},{5,13},{9,1},{13,5},{2,10},{6,14},... | collective-permute-start | bytes 786440 | tf_op jit(solution)/shard_map/ppermute | solution.py:29
  29.9 1.3 %collective-permute-start.5 = (bf16[2,16,1024]{2,1,0:T(8,128)(2,1)S(1)}, bf16[2,16,1024]{2,1,0:T(8,128)(2,1)S(1)}, u32[]{:S(2)}, u32[]{:S(2)}) collective-permute-start(bf16[2,16,1024]{2,1,0:T(8,128)(2,1)S(1)} %get-tuple-element.58), channel_id=1, source_target_pairs={{0,1},{1,0},{2,3},{3,2},{4,5},{5,4},{6,7},{7,6},{8,9},{9,8},{10,11... | collective-permute-start | bytes 196616 | tf_op jit(solution)/shard_map/ppermute | solution.py:29
  30.0 1.4 %collective-permute-start.6 = (bf16[2,16,1024]{2,1,0:T(8,128)(2,1)S(1)}, bf16[2,16,1024]{2,1,0:T(8,128)(2,1)S(1)}, u32[]{:S(2)}, u32[]{:S(2)}) collective-permute-start(bf16[2,16,1024]{2,1,0:T(8,128)(2,1)S(1)} %get-tuple-element.59), channel_id=1, source_target_pairs={{0,1},{1,0},{2,3},{3,2},{4,5},{5,4},{6,7},{7,6},{8,9},{9,8},{10,11... | collective-permute-start | bytes 196616 | tf_op jit(solution)/shard_map/ppermute | solution.py:29
  30.5 1.3 %collective-permute-start.7 = (bf16[2,16,1024]{2,1,0:T(8,128)(2,1)S(1)}, bf16[2,16,1024]{2,1,0:T(8,128)(2,1)S(1)}, u32[]{:S(2)}, u32[]{:S(2)}) collective-permute-start(bf16[2,16,1024]{2,1,0:T(8,128)(2,1)S(1)} %get-tuple-element.60), channel_id=1, source_target_pairs={{0,1},{1,0},{2,3},{3,2},{4,5},{5,4},{6,7},{7,6},{8,9},{9,8},{10,11... | collective-permute-start | bytes 196616 | tf_op jit(solution)/shard_map/ppermute | solution.py:29
  31.2 1.3 %collective-permute-start.8 = (bf16[2,16,1024]{2,1,0:T(8,128)(2,1)S(1)}, bf16[2,16,1024]{2,1,0:T(8,128)(2,1)S(1)}, u32[]{:S(2)}, u32[]{:S(2)}) collective-permute-start(bf16[2,16,1024]{2,1,0:T(8,128)(2,1)S(1)} %get-tuple-element.61), channel_id=1, source_target_pairs={{0,1},{1,0},{2,3},{3,2},{4,5},{5,4},{6,7},{7,6},{8,9},{9,8},{10,11... | collective-permute-start | bytes 196616 | tf_op jit(solution)/shard_map/ppermute | solution.py:29
  31.4 1.3 %collective-permute-start.9 = (bf16[2,16,1024]{2,1,0:T(8,128)(2,1)S(1)}, bf16[2,16,1024]{2,1,0:T(8,128)(2,1)S(1)}, u32[]{:S(2)}, u32[]{:S(2)}) collective-permute-start(bf16[2,16,1024]{2,1,0:T(8,128)(2,1)S(1)} %get-tuple-element.62), channel_id=1, source_target_pairs={{0,1},{1,0},{2,3},{3,2},{4,5},{5,4},{6,7},{7,6},{8,9},{9,8},{10,11... | collective-permute-start | bytes 196616 | tf_op jit(solution)/shard_map/ppermute | solution.py:29
  31.7 1.3 %collective-permute-start.10 = (bf16[2,16,1024]{2,1,0:T(8,128)(2,1)S(1)}, bf16[2,16,1024]{2,1,0:T(8,128)(2,1)S(1)}, u32[]{:S(2)}, u32[]{:S(2)}) collective-permute-start(bf16[2,16,1024]{2,1,0:T(8,128)(2,1)S(1)} %get-tuple-element.63), channel_id=1, source_target_pairs={{0,1},{1,0},{2,3},{3,2},{4,5},{5,4},{6,7},{7,6},{8,9},{9,8},{10,11... | collective-permute-start | bytes 196616 | tf_op jit(solution)/shard_map/ppermute | solution.py:29
  32.5 1.3 %collective-permute-start.11 = (bf16[2,16,1024]{2,1,0:T(8,128)(2,1)S(1)}, bf16[2,16,1024]{2,1,0:T(8,128)(2,1)S(1)}, u32[]{:S(2)}, u32[]{:S(2)}) collective-permute-start(bf16[2,16,1024]{2,1,0:T(8,128)(2,1)S(1)} %get-tuple-element.64), channel_id=1, source_target_pairs={{0,1},{1,0},{2,3},{3,2},{4,5},{5,4},{6,7},{7,6},{8,9},{9,8},{10,11... | collective-permute-start | bytes 196616 | tf_op jit(solution)/shard_map/ppermute | solution.py:29
  32.6 1.3 %collective-permute-start.12 = (bf16[2,16,1024]{2,1,0:T(8,128)(2,1)S(1)}, bf16[2,16,1024]{2,1,0:T(8,128)(2,1)S(1)}, u32[]{:S(2)}, u32[]{:S(2)}) collective-permute-start(bf16[2,16,1024]{2,1,0:T(8,128)(2,1)S(1)} %get-tuple-element.65), channel_id=1, source_target_pairs={{0,1},{1,0},{2,3},{3,2},{4,5},{5,4},{6,7},{7,6},{8,9},{9,8},{10,11... | collective-permute-start | bytes 196616 | tf_op jit(solution)/shard_map/ppermute | solution.py:29
  34.7 15.2 %collective-permute-start.13 = (bf16[128,1024]{1,0:T(8,128)(2,1)S(1)}, bf16[128,1024]{1,0:T(8,128)(2,1)S(1)}, u32[]{:S(2)}, u32[]{:S(2)}) collective-permute-start(bf16[128,1024]{1,0:T(8,128)(2,1)S(1)} %get-tuple-element.67), channel_id=1, source_target_pairs={{0,2},{2,0},{1,3},{3,1},{4,6},{6,4},{5,7},{7,5},{8,10},{10,8},{9,1... | collective-permute-start | bytes 786440 | tf_op jit(solution)/shard_map/ppermute | solution.py:29
  46.8 3.0 %collective-permute-start.16 = (bf16[2,32,1024]{2,1,0:T(8,128)(2,1)S(1)}, bf16[2,32,1024]{2,1,0:T(8,128)(2,1)S(1)}, u32[]{:S(2)}, u32[]{:S(2)}) collective-permute-start(bf16[2,32,1024]{2,1,0:T(8,128)(2,1)S(1)} %get-tuple-element.72), channel_id=1, source_target_pairs={{0,1},{1,0},{2,3},{3,2},{4,5},{5,4},{6,7},{7,6},{8,9},{9,8},{10,11... | collective-permute-start | bytes 393224 | tf_op jit(solution)/shard_map/ppermute | solution.py:29
  46.9 6.4 %copy-start = (f32[4,64,1024]{2,1,0:T(8,128)S(1)}, f32[4,64,1024]{2,1,0:T(8,128)}, u32[]{:S(2)}) copy-start(f32[4,64,1024]{2,1,0:T(8,128)} %refs_7_.3) | copy-start | bytes 3145732
  46.9 2.9 %collective-permute-start.17 = (bf16[2,32,1024]{2,1,0:T(8,128)(2,1)S(1)}, bf16[2,32,1024]{2,1,0:T(8,128)(2,1)S(1)}, u32[]{:S(2)}, u32[]{:S(2)}) collective-permute-start(bf16[2,32,1024]{2,1,0:T(8,128)(2,1)S(1)} %get-tuple-element.73), channel_id=1, source_target_pairs={{0,1},{1,0},{2,3},{3,2},{4,5},{5,4},{6,7},{7,6},{8,9},{9,8},{10,11... | collective-permute-start | bytes 393224 | tf_op jit(solution)/shard_map/ppermute | solution.py:29
  49.3 2.8 %collective-permute-start.19 = (bf16[2,32,1024]{2,1,0:T(8,128)(2,1)S(1)}, bf16[2,32,1024]{2,1,0:T(8,128)(2,1)S(1)}, u32[]{:S(2)}, u32[]{:S(2)}) collective-permute-start(bf16[2,32,1024]{2,1,0:T(8,128)(2,1)S(1)} %get-tuple-element.78), channel_id=1, source_target_pairs={{0,1},{1,0},{2,3},{3,2},{4,5},{5,4},{6,7},{7,6},{8,9},{9,8},{10,11... | collective-permute-start | bytes 393224 | tf_op jit(solution)/shard_map/ppermute | solution.py:29
  49.4 2.6 %collective-permute-start.20 = (bf16[2,32,1024]{2,1,0:T(8,128)(2,1)S(1)}, bf16[2,32,1024]{2,1,0:T(8,128)(2,1)S(1)}, u32[]{:S(2)}, u32[]{:S(2)}) collective-permute-start(bf16[2,32,1024]{2,1,0:T(8,128)(2,1)S(1)} %get-tuple-element.79), channel_id=1, source_target_pairs={{0,1},{1,0},{2,3},{3,2},{4,5},{5,4},{6,7},{7,6},{8,9},{9,8},{10,11... | collective-permute-start | bytes 393224 | tf_op jit(solution)/shard_map/ppermute | solution.py:29
  50.5 6.4 %collective-permute-start.18 = (bf16[64,1024]{1,0:T(8,128)(2,1)S(1)}, bf16[64,1024]{1,0:T(8,128)(2,1)S(1)}, u32[]{:S(2)}, u32[]{:S(2)}) collective-permute-start(bf16[64,1024]{1,0:T(8,128)(2,1)S(1)} %get-tuple-element.75), channel_id=1, source_target_pairs={{0,2},{2,0},{1,3},{3,1},{4,6},{6,4},{5,7},{7,5},{8,10},{10,8},{9,1... | collective-permute-start | bytes 393224 | tf_op jit(solution)/shard_map/ppermute | solution.py:29
  52.7 6.2 %collective-permute-start.21 = (bf16[64,1024]{1,0:T(8,128)(2,1)S(1)}, bf16[64,1024]{1,0:T(8,128)(2,1)S(1)}, u32[]{:S(2)}, u32[]{:S(2)}) collective-permute-start(bf16[64,1024]{1,0:T(8,128)(2,1)S(1)} %get-tuple-element.81), channel_id=1, source_target_pairs={{0,2},{2,0},{1,3},{3,1},{4,6},{6,4},{5,7},{7,5},{8,10},{10,8},{9,1... | collective-permute-start | bytes 393224 | tf_op jit(solution)/shard_map/ppermute | solution.py:29
  59.6 1.9 %collective-permute-start.22 = (f32[8,128]{1,0:T(8,128)S(1)}, f32[8,128]{1,0:T(8,128)S(1)}, u32[]{:S(2)}, u32[]{:S(2)}) collective-permute-start(f32[8,128]{1,0:T(8,128)S(1)} %get-tuple-element.82.refs_0_.refs_1_), channel_id=1, source_target_pairs={{0,1},{1,0},{2,3},{3,2},{4,5},{5,4},{6,7},{7,6},{8,9},{9,8},{10,11... | collective-permute-start | bytes 12296 | tf_op jit(solution)/shard_map/ppermute | solution.py:29
  59.6 3.7 %collective-permute-start.23 = (f32[8,128]{1,0:T(8,128)S(1)}, f32[8,128]{1,0:T(8,128)S(1)}, u32[]{:S(2)}, u32[]{:S(2)}) collective-permute-start(f32[8,128]{1,0:T(8,128)S(1)} %get-tuple-element.82.refs_0_.refs_1_), channel_id=1, source_target_pairs={{0,2},{1,3},{2,0},{3,1},{4,6},{5,7},{6,4},{7,5},{8,10},{9,11},{10,... | collective-permute-start | bytes 12296 | tf_op jit(solution)/shard_map/ppermute | solution.py:29
  61.2 3.0 %collective-permute-start.24 = (f32[8,128]{1,0:T(8,128)S(1)}, f32[8,128]{1,0:T(8,128)S(1)}, u32[]{:S(2)}, u32[]{:S(2)}) collective-permute-start(f32[8,128]{1,0:T(8,128)S(1)} %get-tuple-element.82.refs_0_.refs_1_), channel_id=1, source_target_pairs={{0,3},{1,2},{2,1},{3,0},{4,7},{5,6},{6,5},{7,4},{8,11},{9,10},{10,... | collective-permute-start | bytes 12296 | tf_op jit(solution)/shard_map/ppermute | solution.py:29
  65.1 8.6 %collective-permute-start.25 = (bf16[64,1024]{1,0:T(8,128)(2,1)S(1)}, bf16[64,1024]{1,0:T(8,128)(2,1)S(1)}, u32[]{:S(2)}, u32[]{:S(2)}) collective-permute-start(bf16[64,1024]{1,0:T(8,128)(2,1)S(1)} %get-tuple-element.86.refs_0_), channel_id=1, source_target_pairs={{0,12},{4,8},{8,4},{12,0},{1,13},{5,9},{9,5},{13,1},{2,14},{6,10},... | collective-permute-start | bytes 393224 | tf_op jit(solution)/shard_map/ppermute | solution.py:29
  67.8 10.6 %collective-permute-start.26 = (bf16[64,1024]{1,0:T(8,128)(2,1)S(1)}, bf16[64,1024]{1,0:T(8,128)(2,1)S(1)}, u32[]{:S(2)}, u32[]{:S(2)}) collective-permute-start(bf16[64,1024]{1,0:T(8,128)(2,1)S(1)} %get-tuple-element.87), channel_id=1, source_target_pairs={{0,8},{4,12},{8,0},{12,4},{1,9},{5,13},{9,1},{13,5},{2,10},{6,14},... | collective-permute-start | bytes 393224 | tf_op jit(solution)/shard_map/ppermute | solution.py:29
  68.6 9.8 %collective-permute-start.27 = (bf16[64,1024]{1,0:T(8,128)(2,1)S(1)}, bf16[64,1024]{1,0:T(8,128)(2,1)S(1)}, u32[]{:S(2)}, u32[]{:S(2)}) collective-permute-start(bf16[64,1024]{1,0:T(8,128)(2,1)S(1)} %get-tuple-element.89), channel_id=1, source_target_pairs={{0,4},{4,0},{8,12},{12,8},{1,5},{5,1},{9,13},{13,9},{2,6},{6,2},{1... | collective-permute-start | bytes 393224 | tf_op jit(solution)/shard_map/ppermute | solution.py:29
  (2 other events, 1.3 us)

commit v14 on v13

--- a/solution.py
+++ b/solution.py
@@ -572,8 +572,8 @@
     if direct and blocks == 4:
         chunks = [
             [(0, 0, slots), (1, 0, slots)],
+            [(3, 0, slots)],
             [(2, 0, slots)],
-            [(3, 0, slots)],
         ]
     else:
         chunks = [[(d, first, some) for d in range(blocks)] for first in (0, some)]
@@ -608,10 +608,10 @@
         corr, sums = lag_stats(scal, lag_scale, q, pieces, all_sums, own, more, observed)
         corrs.append(corr)
         all_sums = [sums]
-    sums = [swapped(sums, ("win", "freq"), peers, s) for s in range(peers)]
+    sums = [swapped(sums, ("win", "freq"), peers, s) for s in reversed(range(peers))]
     after = []
     numbered = list(enumerate(chunks))
-    for group in (numbered[:0:-1], numbered[:1]):
+    for group in (numbered[1:], numbered[:1]):
         grads = gradients(scal, lag_total, group, after, sums, [corrs[q] for q, _ in group], observed)
         pieces = [p for _, some_pieces in group for p in some_pieces]
         after = [grads[0]]

time: 79.7 us -> 78.3 us (0.982)
  waiting for transfers between devices: 26.6 us -> 23.5 us
  starting transfers between devices: 24.3 us -> 26 us
    ppermute x28, waiting for transfers between devices: 26.6 us -> 23.5 us  [swapped(): return lax.ppermute(value, axis, [(i, i ^ step) for i in range(size)])]
    ppermute x28, starting transfers between devices: 24.3 us -> 26 us  [swapped(): return lax.ppermute(value, axis, [(i, i ^ step) for i in range(size)])]
where the time goes in v14:
time: 78.3 us; the launch traced here: 78.1 us
  starting transfers between devices  26 us (33%)
  waiting for transfers between devices  23.5 us (30%)
  Pallas kernels  23.2 us (30%)
  local copies, waits for them, and re-layouts  4 us (5%)
  between operations  1.47 us (2%)
    ppermute x28, starting transfers between devices, swapped(): return lax.ppermute(value, axis, [(i, i ^ step) for i in range(size)])  26 us
    ppermute x28, waiting for transfers between devices, swapped(): return lax.ppermute(value, axis, [(i, i ^ step) for i in range(size)])  23.5 us
    pallas_call x3, Pallas kernels, lag_parts(): pl.pallas_call(functools.partial(lags_kernel, geometry, split, len(after)...  5.94 us
    pallas_call x1, Pallas kernels, normed_rows(): pl.pallas_call(functools.partial(normed_kernel, lag_total, chunks, len(su...  3.22 us
    pallas_call x1, Pallas kernels, gather_own(): pl.pallas_call(functools.partial(own_kernel, classes, parts), out_shape=[...  3.07 us
    unnamed x12, local copies, waits for them, and re-layouts  2.68 us
    pallas_call x3, Pallas kernels, lag_stats(): pl.pallas_call(functools.partial(stats_kernel, scale, q, pieces, len(more...  2.22 us
    pallas_call x3, Pallas kernels, add_cores(): pl.pallas_call(functools.partial(cores_kernel, len(after), len(more)), ou...  2.06 us
  transfers between devices with their start and end apart: 28, of which 13 were waited for; matrix products, arithmetic and copies ran while one was open for 0% of the time, Pallas kernels for 24%

profile of v14, /device:TPU:0, one launch (start us, length us, event | category | flops | bytes accessed | tf_op | source)
XLA Modules:
  0.0 78.1 jit_solution(14389526657864804808)
XLA Ops:
  0.7 1.3 %constant_dynamic-slice_fusion = (bf16[1,2,128,1024]{3,2,1,0:T(8,128)(2,1)S(1)}, bf16[1,2,128,1024]{3,2,1,0:T(8,128)(2,1)S(1)}) fusion(bf16[1,2,128,2048]{3,2,1,0:T(8,128)(2,1)} %param.8, s32[]{:T(128)S(6)} %select_n.7, s32[]{:T(128)S(6)} %select_n.6), kind=kLoop, calls=%fused_computation | loop fusion | bytes 2097160 | tf_op jit(solution)/shard_map/dynamic_slice | solution.py:555
  2.0 3.0 %collective-permute-start = (bf16[1,2,128,1024]{3,2,1,0:T(8,128)(2,1)S(1)}, bf16[1,2,128,1024]{3,2,1,0:T(8,128)(2,1)S(1)}, u32[]{:S(2)}, u32[]{:S(2)}) collective-permute-start(bf16[1,2,128,1024]{3,2,1,0:T(8,128)(2,1)S(1)} %get-tuple-element.90), channel_id=1, source_target_pairs={{0,2},{2,0},{1,3},{3,1},{4,6},{6,4},{5,7},{7,5},{8,10},{10,8},{9,1... | collective-permute-start | bytes 1572872 | tf_op jit(solution)/shard_map/ppermute | solution.py:29
  8.3 1.2 %index.1 = (s32[128]{0:T(128)S(1)}, s32[1,64]{1,0:T(1,128)S(1)}, s32[1,64]{1,0:T(1,128)S(1)}, s32[1,64]{1,0:T(1,128)S(1)}, s32[1,64]{1,0:T(1,128)S(1)}, /*index=5*/s32[4,64]{1,0:T(4,128)S(1)}) custom-call(s32[1]{0:T(128)S(6)} %copy.10.refs_0_, s32[4]{0:T(128)S(1)} %copy-done.4, s32[4]{0:T(128)S(1)} %bitcast.1, s32[4,64]{1,0:T(4,128)S(1)} %copy-done.2, ...), custom_call_target="tpu_custom_call" | custom-call | flops 1 | bytes 1 | tf_op jit(solution)/shard_map/index/pallas_call | solution.py:92
  9.5 3.7 %collective-permute-start.1 = (s32[1,64]{1,0:T(1,128)S(1)}, s32[1,64]{1,0:T(1,128)S(1)}, u32[]{:S(2)}, u32[]{:S(2)}) collective-permute-start(s32[1,64]{1,0:T(1,128)S(1)} %get-tuple-element.47), channel_id=1, source_target_pairs={{0,12},{4,8},{8,4},{12,0},{1,13},{5,9},{9,5},{13,1},{2,14},{6,10},... | collective-permute-start | bytes 776 | tf_op jit(solution)/shard_map/ppermute | solution.py:29
  13.2 0.8 %collective-permute-start.3 = (s32[1,64]{1,0:T(1,128)S(1)}, s32[1,64]{1,0:T(1,128)S(1)}, u32[]{:S(2)}, u32[]{:S(2)}) collective-permute-start(s32[1,64]{1,0:T(1,128)S(1)} %get-tuple-element.49), channel_id=1, source_target_pairs={{0,4},{4,0},{8,12},{12,8},{1,5},{5,1},{9,13},{13,9},{2,6},{6,2},{1... | collective-permute-start | bytes 776 | tf_op jit(solution)/shard_map/ppermute | solution.py:29
  14.9 2.7 %collective-permute-done.2.refs_3_.refs_1_ = s32[1,64]{1,0:T(1,128)S(1)} collective-permute-done((s32[1,64]{1,0:T(1,128)S(1)}, s32[1,64]{1,0:T(1,128)S(1)}, u32[]{:S(2)}, u32[]{:S(2)}) %collective-permute-start.2) | collective-permute-done | bytes 288 | tf_op jit(solution)/shard_map/ppermute | solution.py:29
  17.7 1.6 %rows.1 = (bf16[1,2,64,1024]{3,2,1,0:T(8,128)(2,1)S(1)}, bf16[1,2,64,1024]{3,2,1,0:T(8,128)(2,1)S(1)}, bf16[1,2,64,1024]{3,2,1,0:T(8,128)(2,1)S(1)}, bf16[1,2,64...) custom-call(s32[128]{0:T(128)S(1)} %get-tuple-element.46.scal, ...), custom_call_target="tpu_custom_call" | custom-call | flops 1 | bytes 1 | tf_op jit(solution)/shard_map/rows/pallas_call | solution.py:175
  19.2 1.1 %collective-permute-start.4 = (bf16[1,2,64,1024]{3,2,1,0:T(8,128)(2,1)S(1)}, bf16[1,2,64,1024]{3,2,1,0:T(8,128)(2,1)S(1)}, u32[]{:S(2)}, u32[]{:S(2)}) collective-permute-start(bf16[1,2,64,1024]{3,2,1,0:T(8,128)(2,1)S(1)} %get-tuple-element.52), channel_id=1, source_target_pairs={{0,4},{4,0},{8,12},{12,8},{1,5},{5,1},{9,13},{13,9},{2,6},{6,2},{1... | collective-permute-start | bytes 786440 | tf_op jit(solution)/shard_map/ppermute | solution.py:29
  20.4 2.6 %collective-permute-start.14 = (bf16[1,2,64,1024]{3,2,1,0:T(8,128)(2,1)S(1)}, bf16[1,2,64,1024]{3,2,1,0:T(8,128)(2,1)S(1)}, u32[]{:S(2)}, u32[]{:S(2)}) collective-permute-start(bf16[1,2,64,1024]{3,2,1,0:T(8,128)(2,1)S(1)} %get-tuple-element.69), channel_id=1, source_target_pairs={{0,8},{4,12},{8,0},{12,4},{1,9},{5,13},{9,1},{13,5},{2,10},{6,14},... | collective-permute-start | bytes 786440 | tf_op jit(solution)/shard_map/ppermute | solution.py:29
  23.7 3.1 %own.1 = (bf16[4,1,2,64,1024]{4,3,2,1,0:T(8,128)(2,1)S(1)}, bf16[8,256,1024]{2,1,0:T(8,128)(2,1)S(1)}) custom-call(s32[128]{0:T(128)S(1)} %get-tuple-element.46.scal, bf16[1,2,128,1024]{3,2,1,0:T(8,128)(2,1)S(1)} %get-tuple-element.53.kept, s32[4,64]{1,0:T(4,128)S(1)} %get-tuple-element.54.rec_ids, f32[2,56,1024]{2,1,0:T(8,128)S(1)} %copy-done.1), custom_call_target="tpu_custom_call" | custom-call | flops 1 | bytes 1 | tf_op jit(solution)/shard_map/own/pallas_call | solution.py:204
  26.8 3.7 %collective-permute-done.4.refs_1_ = bf16[1,2,64,1024]{3,2,1,0:T(8,128)(2,1)S(1)} collective-permute-done((bf16[1,2,64,1024]{3,2,1,0:T(8,128)(2,1)S(1)}, bf16[1,2,64,1024]{3,2,1,0:T(8,128)(2,1)S(1)}, u32[]{:S(2)}, u32[]{:S(2)}) %collective-permute-start.4) | collective-permute-done | bytes 262176 | tf_op jit(solution)/shard_map/ppermute | solution.py:29
  30.7 2.5 %lags.3 = (f32[2,128,1024]{2,1,0:T(8,128)S(1)}, bf16[2,16,1024]{2,1,0:T(8,128)(2,1)S(1)}, bf16[2,16,1024]{2,1,0:T(8,128)(2,1)S(1)}, bf16[2,16,1024]{2,1,0:T(8,12...) custom-call(s32[128]{0:T(128)S(1)} %get-tuple-element.46.scal, ...), custom_call_target="tpu_custom_call" | custom-call | flops 20000000000 | bytes 1048576 | tf_op jit(solution)/shard_map/lags/pallas_call | solution.py:331
  36.3 0.7 collective-permute-done.11.refs_7_
  37.2 0.8 %cores.3 = (f32[128,1024]{1,0:T(8,128)S(1)}, bf16[128,1024]{1,0:T(8,128)(2,1)S(1)}) custom-call(s32[128]{0:T(128)S(1)} %get-tuple-element.46.scal, f32[2,128,1024]{2,1,0:T(8,128)S(1)} %get-tuple-element.57.refs_0_, bf16[2,16,1024]{2,1,0:T(8,128)(2,1)S(1)} %collective-permute-done.5.refs_1_, bf16[2,16,1024]{2,1,0:T(8,128)(2,1)S(1)} %collective-permute-done.6.refs_2_, ...), custom_call_target="tpu_custom_call" | custom-call | flops 1 | bytes 1 | tf_op jit(solution)/shard_map/cores/pallas_call | solution.py:366
  38.0 1.5 %collective-permute-start.13 = (bf16[128,1024]{1,0:T(8,128)(2,1)S(1)}, bf16[128,1024]{1,0:T(8,128)(2,1)S(1)}, u32[]{:S(2)}, u32[]{:S(2)}) collective-permute-start(bf16[128,1024]{1,0:T(8,128)(2,1)S(1)} %get-tuple-element.67), channel_id=1, source_target_pairs={{0,2},{2,0},{1,3},{3,1},{4,6},{6,4},{5,7},{7,5},{8,10},{10,8},{9,1... | collective-permute-start | bytes 786440 | tf_op jit(solution)/shard_map/ppermute | solution.py:29
  39.5 2.2 %collective-permute-done.14.refs_1_.refs_0_ = bf16[1,2,64,1024]{3,2,1,0:T(8,128)(2,1)S(1)} collective-permute-done((bf16[1,2,64,1024]{3,2,1,0:T(8,128)(2,1)S(1)}, bf16[1,2,64,1024]{3,2,1,0:T(8,128)(2,1)S(1)}, u32[]{:S(2)}, u32[]{:S(2)}) %collective-permute-start.14) | collective-permute-done | bytes 262176 | tf_op jit(solution)/shard_map/ppermute | solution.py:29
  41.9 1.7 %lags.4 = (f32[2,64,1024]{2,1,0:T(8,128)S(1)}, bf16[2,32,1024]{2,1,0:T(8,128)(2,1)S(1)}, bf16[2,32,1024]{2,1,0:T(8,128)(2,1)S(1)}) custom-call(s32[128]{0:T(128)S(1)} %get-tuple-element.46.scal, bf16[8,128,256]{2,1,0:T(8,128)(2,1)S(1)} %cross.4.refs_0_, bf16[8,256,1024]{2,1,0:T(8,128)(2,1)S(1)} %get-tuple-element.56.refs_1_), custom_call_target="tpu_custom_call" | custom-call | flops 1 | bytes 1 | tf_op jit(solution)/shard_map/lags/pallas_call | solution.py:331
  44.4 1.7 %lags.5 = (f32[2,64,1024]{2,1,0:T(8,128)S(1)}, bf16[2,32,1024]{2,1,0:T(8,128)(2,1)S(1)}, bf16[2,32,1024]{2,1,0:T(8,128)(2,1)S(1)}) custom-call(s32[128]{0:T(128)S(1)} %get-tuple-element.46.scal, bf16[8,128,256]{2,1,0:T(8,128)(2,1)S(1)} %cross.5.refs_0_, bf16[8,256,1024]{2,1,0:T(8,128)(2,1)S(1)} %get-tuple-element.56.refs_1_), custom_call_target="tpu_custom_call" | custom-call | flops 1 | bytes 1 | tf_op jit(solution)/shard_map/lags/pallas_call | solution.py:331
  47.3 1.6 %collective-permute-start.18 = (bf16[64,1024]{1,0:T(8,128)(2,1)S(1)}, bf16[64,1024]{1,0:T(8,128)(2,1)S(1)}, u32[]{:S(2)}, u32[]{:S(2)}) collective-permute-start(bf16[64,1024]{1,0:T(8,128)(2,1)S(1)} %get-tuple-element.75), channel_id=1, source_target_pairs={{0,2},{2,0},{1,3},{3,1},{4,6},{6,4},{5,7},{7,5},{8,10},{10,8},{9,1... | collective-permute-start | bytes 393224 | tf_op jit(solution)/shard_map/ppermute | solution.py:29
  50.1 0.8 stats.3
  50.9 2.8 %collective-permute-done.18.refs_2_ = bf16[64,1024]{1,0:T(8,128)(2,1)S(1)} collective-permute-done((bf16[64,1024]{1,0:T(8,128)(2,1)S(1)}, bf16[64,1024]{1,0:T(8,128)(2,1)S(1)}, u32[]{:S(2)}, u32[]{:S(2)}) %collective-permute-start.18) | collective-permute-done | bytes 131104 | tf_op jit(solution)/shard_map/ppermute | solution.py:29
  54.4 1.2 %collective-permute-done.21.refs_2_ = bf16[64,1024]{1,0:T(8,128)(2,1)S(1)} collective-permute-done((bf16[64,1024]{1,0:T(8,128)(2,1)S(1)}, bf16[64,1024]{1,0:T(8,128)(2,1)S(1)}, u32[]{:S(2)}, u32[]{:S(2)}) %collective-permute-start.21) | collective-permute-done | bytes 131104 | tf_op jit(solution)/shard_map/ppermute | solution.py:29
  56.8 1.2 %collective-permute-start.23 = (f32[8,128]{1,0:T(8,128)S(1)}, f32[8,128]{1,0:T(8,128)S(1)}, u32[]{:S(2)}, u32[]{:S(2)}) collective-permute-start(f32[8,128]{1,0:T(8,128)S(1)} %get-tuple-element.82.refs_3_.refs_4_), channel_id=1, source_target_pairs={{0,2},{1,3},{2,0},{3,1},{4,6},{5,7},{6,4},{7,5},{8,10},{9,11},{10,... | collective-permute-start | bytes 12296 | tf_op jit(solution)/shard_map/ppermute | solution.py:29
  58.3 1.2 %collective-permute-done.22.refs_0_.refs_1_ = f32[8,128]{1,0:T(8,128)S(1)} collective-permute-done((f32[8,128]{1,0:T(8,128)S(1)}, f32[8,128]{1,0:T(8,128)S(1)}, u32[]{:S(2)}, u32[]{:S(2)}) %collective-permute-start.22) | collective-permute-done | bytes 4128 | tf_op jit(solution)/shard_map/ppermute | solution.py:29
  59.4 0.9 %collective-permute-done.23.refs_1_.refs_2_ = f32[8,128]{1,0:T(8,128)S(1)} collective-permute-done((f32[8,128]{1,0:T(8,128)S(1)}, f32[8,128]{1,0:T(8,128)S(1)}, u32[]{:S(2)}, u32[]{:S(2)}) %collective-permute-start.23) | collective-permute-done | bytes 4128 | tf_op jit(solution)/shard_map/ppermute | solution.py:29
  60.4 0.8 %gradient.2 = (bf16[64,1024]{1,0:T(8,128)(2,1)S(1)}, bf16[64,1024]{1,0:T(8,128)(2,1)S(1)}) custom-call(s32[128]{0:T(128)S(1)} %get-tuple-element.46.scal, f32[8,128]{1,0:T(8,128)S(1)} %collective-permute-done.22.refs_0_.refs_1_, f32[8,128]{1,0:T(8,128)S(1)} %collective-permute-done.23.refs_1_.refs_2_, f32[8,128]{1,0:T(8,128)S(1)} %collective-permute-done.24.refs_2_.refs_3_, ...), custom_call_target="tpu_custom_call" | custom-call | flops 1 | bytes 1 | tf_op jit(solution)/shard_map/gradient/pallas_call | solution.py:470
  61.2 2.7 %collective-permute-start.25 = (bf16[64,1024]{1,0:T(8,128)(2,1)S(1)}, bf16[64,1024]{1,0:T(8,128)(2,1)S(1)}, u32[]{:S(2)}, u32[]{:S(2)}) collective-permute-start(bf16[64,1024]{1,0:T(8,128)(2,1)S(1)} %get-tuple-element.86.refs_0_), channel_id=1, source_target_pairs={{0,12},{4,8},{8,4},{12,0},{1,13},{5,9},{9,5},{13,1},{2,14},{6,10},... | collective-permute-start | bytes 393224 | tf_op jit(solution)/shard_map/ppermute | solution.py:29
  63.9 2.7 %collective-permute-start.26 = (bf16[64,1024]{1,0:T(8,128)(2,1)S(1)}, bf16[64,1024]{1,0:T(8,128)(2,1)S(1)}, u32[]{:S(2)}, u32[]{:S(2)}) collective-permute-start(bf16[64,1024]{1,0:T(8,128)(2,1)S(1)} %get-tuple-element.87), channel_id=1, source_target_pairs={{0,8},{4,12},{8,0},{12,4},{1,9},{5,13},{9,1},{13,5},{2,10},{6,14},... | collective-permute-start | bytes 393224 | tf_op jit(solution)/shard_map/ppermute | solution.py:29
  66.6 0.8 %gradient.3 = (bf16[64,1024]{1,0:T(8,128)(2,1)S(1)}, bf16[64,1024]{1,0:T(8,128)(2,1)S(1)}) custom-call(s32[128]{0:T(128)S(1)} %get-tuple-element.46.scal, bf16[64,1024]{1,0:T(8,128)(2,1)S(1)} %get-tuple-element.86.refs_0_, f32[8,128]{1,0:T(8,128)S(1)} %collective-permute-done.22.refs_0_.refs_1_, f32[8,128]{1,0:T(8,128)S(1)} %collective-permute-done.23.refs_1_.refs_2_, ...), custom_call_target="tpu_custom_call" | custom-call | flops 1 | bytes 1 | tf_op jit(solution)/shard_map/gradient/pallas_call | solution.py:470
  67.6 3.2 %normed.1 = f32[4,64,1024]{2,1,0:T(8,128)} custom-call(s32[128]{0:T(128)S(1)} %get-tuple-element.46.scal, f32[8,128]{1,0:T(8,128)S(1)} %collective-permute-done.22.refs_0_.refs_1_, f32[8,128]{1,0:T(8,128)S(1)} %collective-permute-done.23.refs_1_.refs_2_, f32[8,128]{1,0:T(8,128)S(1)} %collective-permute-done.24.refs_2_.refs_3_, ...), custom_call_target="tpu_custom_call" | custom-call | flops 1 | bytes 1 | tf_op jit(solution)/shard_map/normed/pallas_call | solution.py:501
  70.8 6.2 %collective-permute-done.26.refs_5_ = bf16[64,1024]{1,0:T(8,128)(2,1)S(1)} collective-permute-done((bf16[64,1024]{1,0:T(8,128)(2,1)S(1)}, bf16[64,1024]{1,0:T(8,128)(2,1)S(1)}, u32[]{:S(2)}, u32[]{:S(2)}) %collective-permute-start.26) | collective-permute-done | bytes 131104 | tf_op jit(solution)/shard_map/ppermute | solution.py:29
  77.0 1.1 %adjoint.1 = f32[128,1024]{1,0:T(8,128)} custom-call(s32[1,64]{1,0:T(1,128)S(1)} %collective-permute-done.1.refs_2_.refs_0_, s32[1,64]{1,0:T(1,128)S(1)} %collective-permute-done.2.refs_3_.refs_1_, s32[1,64]{1,0:T(1,128)S(1)} %get-tuple-element.50.refs_5_.refs_2_, s32[1,64]{1,0:T(1,128)S(1)} %collective-permute-done.3.refs_4_.refs_3_, ...), custom_call_target="tpu_custom_call" | custom-call | flops 1 | bytes 1 | tf_op jit(solution)/shard_map/adjoint/pallas_call | solution.py:525
  (57 shorter events, 13.4 us)
Async XLA Ops:
  0.6 23.1 %copy-start.1 = (f32[2,56,1024]{2,1,0:T(8,128)S(1)}, f32[2,56,1024]{2,1,0:T(8,128)}, u32[]{:S(2)}) copy-start(f32[2,56,1024]{2,1,0:T(8,128)} %constant.16.clone.trig) | copy-start | bytes 1376260
  2.0 15.7 %collective-permute-start = (bf16[1,2,128,1024]{3,2,1,0:T(8,128)(2,1)S(1)}, bf16[1,2,128,1024]{3,2,1,0:T(8,128)(2,1)S(1)}, u32[]{:S(2)}, u32[]{:S(2)}) collective-permute-start(bf16[1,2,128,1024]{3,2,1,0:T(8,128)(2,1)S(1)} %get-tuple-element.90), channel_id=1, source_target_pairs={{0,2},{2,0},{1,3},{3,1},{4,6},{6,4},{5,7},{7,5},{8,10},{10,8},{9,1... | collective-permute-start | bytes 1572872 | tf_op jit(solution)/shard_map/ppermute | solution.py:29
  5.6 0.7 copy-start.2
  6.3 0.7 copy-start.3
  9.5 5.4 %collective-permute-start.1 = (s32[1,64]{1,0:T(1,128)S(1)}, s32[1,64]{1,0:T(1,128)S(1)}, u32[]{:S(2)}, u32[]{:S(2)}) collective-permute-start(s32[1,64]{1,0:T(1,128)S(1)} %get-tuple-element.47), channel_id=1, source_target_pairs={{0,12},{4,8},{8,4},{12,0},{1,13},{5,9},{9,5},{13,1},{2,14},{6,10},... | collective-permute-start | bytes 776 | tf_op jit(solution)/shard_map/ppermute | solution.py:29
  13.2 4.4 %collective-permute-start.2 = (s32[1,64]{1,0:T(1,128)S(1)}, s32[1,64]{1,0:T(1,128)S(1)}, u32[]{:S(2)}, u32[]{:S(2)}) collective-permute-start(s32[1,64]{1,0:T(1,128)S(1)} %get-tuple-element.48), channel_id=1, source_target_pairs={{0,8},{4,12},{8,0},{12,4},{1,9},{5,13},{9,1},{13,5},{2,10},{6,14},... | collective-permute-start | bytes 776 | tf_op jit(solution)/shard_map/ppermute | solution.py:29
  13.2 4.4 %collective-permute-start.3 = (s32[1,64]{1,0:T(1,128)S(1)}, s32[1,64]{1,0:T(1,128)S(1)}, u32[]{:S(2)}, u32[]{:S(2)}) collective-permute-start(s32[1,64]{1,0:T(1,128)S(1)} %get-tuple-element.49), channel_id=1, source_target_pairs={{0,4},{4,0},{8,12},{12,8},{1,5},{5,1},{9,13},{13,9},{2,6},{6,2},{1... | collective-permute-start | bytes 776 | tf_op jit(solution)/shard_map/ppermute | solution.py:29
  19.2 11.2 %collective-permute-start.4 = (bf16[1,2,64,1024]{3,2,1,0:T(8,128)(2,1)S(1)}, bf16[1,2,64,1024]{3,2,1,0:T(8,128)(2,1)S(1)}, u32[]{:S(2)}, u32[]{:S(2)}) collective-permute-start(bf16[1,2,64,1024]{3,2,1,0:T(8,128)(2,1)S(1)} %get-tuple-element.52), channel_id=1, source_target_pairs={{0,4},{4,0},{8,12},{12,8},{1,5},{5,1},{9,13},{13,9},{2,6},{6,2},{1... | collective-permute-start | bytes 786440 | tf_op jit(solution)/shard_map/ppermute | solution.py:29
  20.4 21.4 %collective-permute-start.14 = (bf16[1,2,64,1024]{3,2,1,0:T(8,128)(2,1)S(1)}, bf16[1,2,64,1024]{3,2,1,0:T(8,128)(2,1)S(1)}, u32[]{:S(2)}, u32[]{:S(2)}) collective-permute-start(bf16[1,2,64,1024]{3,2,1,0:T(8,128)(2,1)S(1)} %get-tuple-element.69), channel_id=1, source_target_pairs={{0,8},{4,12},{8,0},{12,4},{1,9},{5,13},{9,1},{13,5},{2,10},{6,14},... | collective-permute-start | bytes 786440 | tf_op jit(solution)/shard_map/ppermute | solution.py:29
  23.0 18.8 %collective-permute-start.15 = (bf16[1,2,64,1024]{3,2,1,0:T(8,128)(2,1)S(1)}, bf16[1,2,64,1024]{3,2,1,0:T(8,128)(2,1)S(1)}, u32[]{:S(2)}, u32[]{:S(2)}) collective-permute-start(bf16[1,2,64,1024]{3,2,1,0:T(8,128)(2,1)S(1)} %get-tuple-element.70), channel_id=1, source_target_pairs={{0,12},{4,8},{8,4},{12,0},{1,13},{5,9},{9,5},{13,1},{2,14},{6,10},... | collective-permute-start | bytes 786440 | tf_op jit(solution)/shard_map/ppermute | solution.py:29
  33.2 1.3 %collective-permute-start.5 = (bf16[2,16,1024]{2,1,0:T(8,128)(2,1)S(1)}, bf16[2,16,1024]{2,1,0:T(8,128)(2,1)S(1)}, u32[]{:S(2)}, u32[]{:S(2)}) collective-permute-start(bf16[2,16,1024]{2,1,0:T(8,128)(2,1)S(1)} %get-tuple-element.58), channel_id=1, source_target_pairs={{0,1},{1,0},{2,3},{3,2},{4,5},{5,4},{6,7},{7,6},{8,9},{9,8},{10,11... | collective-permute-start | bytes 196616 | tf_op jit(solution)/shard_map/ppermute | solution.py:29
  33.3 1.4 %collective-permute-start.6 = (bf16[2,16,1024]{2,1,0:T(8,128)(2,1)S(1)}, bf16[2,16,1024]{2,1,0:T(8,128)(2,1)S(1)}, u32[]{:S(2)}, u32[]{:S(2)}) collective-permute-start(bf16[2,16,1024]{2,1,0:T(8,128)(2,1)S(1)} %get-tuple-element.59), channel_id=1, source_target_pairs={{0,1},{1,0},{2,3},{3,2},{4,5},{5,4},{6,7},{7,6},{8,9},{9,8},{10,11... | collective-permute-start | bytes 196616 | tf_op jit(solution)/shard_map/ppermute | solution.py:29
  33.8 1.3 %collective-permute-start.7 = (bf16[2,16,1024]{2,1,0:T(8,128)(2,1)S(1)}, bf16[2,16,1024]{2,1,0:T(8,128)(2,1)S(1)}, u32[]{:S(2)}, u32[]{:S(2)}) collective-permute-start(bf16[2,16,1024]{2,1,0:T(8,128)(2,1)S(1)} %get-tuple-element.60), channel_id=1, source_target_pairs={{0,1},{1,0},{2,3},{3,2},{4,5},{5,4},{6,7},{7,6},{8,9},{9,8},{10,11... | collective-permute-start | bytes 196616 | tf_op jit(solution)/shard_map/ppermute | solution.py:29
  34.5 1.3 %collective-permute-start.8 = (bf16[2,16,1024]{2,1,0:T(8,128)(2,1)S(1)}, bf16[2,16,1024]{2,1,0:T(8,128)(2,1)S(1)}, u32[]{:S(2)}, u32[]{:S(2)}) collective-permute-start(bf16[2,16,1024]{2,1,0:T(8,128)(2,1)S(1)} %get-tuple-element.61), channel_id=1, source_target_pairs={{0,1},{1,0},{2,3},{3,2},{4,5},{5,4},{6,7},{7,6},{8,9},{9,8},{10,11... | collective-permute-start | bytes 196616 | tf_op jit(solution)/shard_map/ppermute | solution.py:29
  34.7 1.3 %collective-permute-start.9 = (bf16[2,16,1024]{2,1,0:T(8,128)(2,1)S(1)}, bf16[2,16,1024]{2,1,0:T(8,128)(2,1)S(1)}, u32[]{:S(2)}, u32[]{:S(2)}) collective-permute-start(bf16[2,16,1024]{2,1,0:T(8,128)(2,1)S(1)} %get-tuple-element.62), channel_id=1, source_target_pairs={{0,1},{1,0},{2,3},{3,2},{4,5},{5,4},{6,7},{7,6},{8,9},{9,8},{10,11... | collective-permute-start | bytes 196616 | tf_op jit(solution)/shard_map/ppermute | solution.py:29
  35.1 1.3 %collective-permute-start.10 = (bf16[2,16,1024]{2,1,0:T(8,128)(2,1)S(1)}, bf16[2,16,1024]{2,1,0:T(8,128)(2,1)S(1)}, u32[]{:S(2)}, u32[]{:S(2)}) collective-permute-start(bf16[2,16,1024]{2,1,0:T(8,128)(2,1)S(1)} %get-tuple-element.63), channel_id=1, source_target_pairs={{0,1},{1,0},{2,3},{3,2},{4,5},{5,4},{6,7},{7,6},{8,9},{9,8},{10,11... | collective-permute-start | bytes 196616 | tf_op jit(solution)/shard_map/ppermute | solution.py:29
  35.8 1.3 %collective-permute-start.11 = (bf16[2,16,1024]{2,1,0:T(8,128)(2,1)S(1)}, bf16[2,16,1024]{2,1,0:T(8,128)(2,1)S(1)}, u32[]{:S(2)}, u32[]{:S(2)}) collective-permute-start(bf16[2,16,1024]{2,1,0:T(8,128)(2,1)S(1)} %get-tuple-element.64), channel_id=1, source_target_pairs={{0,1},{1,0},{2,3},{3,2},{4,5},{5,4},{6,7},{7,6},{8,9},{9,8},{10,11... | collective-permute-start | bytes 196616 | tf_op jit(solution)/shard_map/ppermute | solution.py:29
  36.0 1.3 %collective-permute-start.12 = (bf16[2,16,1024]{2,1,0:T(8,128)(2,1)S(1)}, bf16[2,16,1024]{2,1,0:T(8,128)(2,1)S(1)}, u32[]{:S(2)}, u32[]{:S(2)}) collective-permute-start(bf16[2,16,1024]{2,1,0:T(8,128)(2,1)S(1)} %get-tuple-element.65), channel_id=1, source_target_pairs={{0,1},{1,0},{2,3},{3,2},{4,5},{5,4},{6,7},{7,6},{8,9},{9,8},{10,11... | collective-permute-start | bytes 196616 | tf_op jit(solution)/shard_map/ppermute | solution.py:29
  38.0 8.6 %collective-permute-start.13 = (bf16[128,1024]{1,0:T(8,128)(2,1)S(1)}, bf16[128,1024]{1,0:T(8,128)(2,1)S(1)}, u32[]{:S(2)}, u32[]{:S(2)}) collective-permute-start(bf16[128,1024]{1,0:T(8,128)(2,1)S(1)} %get-tuple-element.67), channel_id=1, source_target_pairs={{0,2},{2,0},{1,3},{3,1},{4,6},{6,4},{5,7},{7,5},{8,10},{10,8},{9,1... | collective-permute-start | bytes 786440 | tf_op jit(solution)/shard_map/ppermute | solution.py:29
  43.6 3.0 %collective-permute-start.16 = (bf16[2,32,1024]{2,1,0:T(8,128)(2,1)S(1)}, bf16[2,32,1024]{2,1,0:T(8,128)(2,1)S(1)}, u32[]{:S(2)}, u32[]{:S(2)}) collective-permute-start(bf16[2,32,1024]{2,1,0:T(8,128)(2,1)S(1)} %get-tuple-element.72), channel_id=1, source_target_pairs={{0,1},{1,0},{2,3},{3,2},{4,5},{5,4},{6,7},{7,6},{8,9},{9,8},{10,11... | collective-permute-start | bytes 393224 | tf_op jit(solution)/shard_map/ppermute | solution.py:29
  43.7 6.4 %copy-start = (f32[4,64,1024]{2,1,0:T(8,128)S(1)}, f32[4,64,1024]{2,1,0:T(8,128)}, u32[]{:S(2)}) copy-start(f32[4,64,1024]{2,1,0:T(8,128)} %refs_7_.3) | copy-start | bytes 3145732
  43.7 2.9 %collective-permute-start.17 = (bf16[2,32,1024]{2,1,0:T(8,128)(2,1)S(1)}, bf16[2,32,1024]{2,1,0:T(8,128)(2,1)S(1)}, u32[]{:S(2)}, u32[]{:S(2)}) collective-permute-start(bf16[2,32,1024]{2,1,0:T(8,128)(2,1)S(1)} %get-tuple-element.73), channel_id=1, source_target_pairs={{0,1},{1,0},{2,3},{3,2},{4,5},{5,4},{6,7},{7,6},{8,9},{9,8},{10,11... | collective-permute-start | bytes 393224 | tf_op jit(solution)/shard_map/ppermute | solution.py:29
  46.1 2.8 %collective-permute-start.19 = (bf16[2,32,1024]{2,1,0:T(8,128)(2,1)S(1)}, bf16[2,32,1024]{2,1,0:T(8,128)(2,1)S(1)}, u32[]{:S(2)}, u32[]{:S(2)}) collective-permute-start(bf16[2,32,1024]{2,1,0:T(8,128)(2,1)S(1)} %get-tuple-element.78), channel_id=1, source_target_pairs={{0,1},{1,0},{2,3},{3,2},{4,5},{5,4},{6,7},{7,6},{8,9},{9,8},{10,11... | collective-permute-start | bytes 393224 | tf_op jit(solution)/shard_map/ppermute | solution.py:29
  46.2 2.6 %collective-permute-start.20 = (bf16[2,32,1024]{2,1,0:T(8,128)(2,1)S(1)}, bf16[2,32,1024]{2,1,0:T(8,128)(2,1)S(1)}, u32[]{:S(2)}, u32[]{:S(2)}) collective-permute-start(bf16[2,32,1024]{2,1,0:T(8,128)(2,1)S(1)} %get-tuple-element.79), channel_id=1, source_target_pairs={{0,1},{1,0},{2,3},{3,2},{4,5},{5,4},{6,7},{7,6},{8,9},{9,8},{10,11... | collective-permute-start | bytes 393224 | tf_op jit(solution)/shard_map/ppermute | solution.py:29
  47.3 6.4 %collective-permute-start.18 = (bf16[64,1024]{1,0:T(8,128)(2,1)S(1)}, bf16[64,1024]{1,0:T(8,128)(2,1)S(1)}, u32[]{:S(2)}, u32[]{:S(2)}) collective-permute-start(bf16[64,1024]{1,0:T(8,128)(2,1)S(1)} %get-tuple-element.75), channel_id=1, source_target_pairs={{0,2},{2,0},{1,3},{3,1},{4,6},{6,4},{5,7},{7,5},{8,10},{10,8},{9,1... | collective-permute-start | bytes 393224 | tf_op jit(solution)/shard_map/ppermute | solution.py:29
  49.5 6.2 %collective-permute-start.21 = (bf16[64,1024]{1,0:T(8,128)(2,1)S(1)}, bf16[64,1024]{1,0:T(8,128)(2,1)S(1)}, u32[]{:S(2)}, u32[]{:S(2)}) collective-permute-start(bf16[64,1024]{1,0:T(8,128)(2,1)S(1)} %get-tuple-element.81), channel_id=1, source_target_pairs={{0,2},{2,0},{1,3},{3,1},{4,6},{6,4},{5,7},{7,5},{8,10},{10,8},{9,1... | collective-permute-start | bytes 393224 | tf_op jit(solution)/shard_map/ppermute | solution.py:29
  56.4 3.1 %collective-permute-start.22 = (f32[8,128]{1,0:T(8,128)S(1)}, f32[8,128]{1,0:T(8,128)S(1)}, u32[]{:S(2)}, u32[]{:S(2)}) collective-permute-start(f32[8,128]{1,0:T(8,128)S(1)} %get-tuple-element.82.refs_3_.refs_4_), channel_id=1, source_target_pairs={{0,3},{1,2},{2,1},{3,0},{4,7},{5,6},{6,5},{7,4},{8,11},{9,10},{10,... | collective-permute-start | bytes 12296 | tf_op jit(solution)/shard_map/ppermute | solution.py:29
  56.8 3.6 %collective-permute-start.23 = (f32[8,128]{1,0:T(8,128)S(1)}, f32[8,128]{1,0:T(8,128)S(1)}, u32[]{:S(2)}, u32[]{:S(2)}) collective-permute-start(f32[8,128]{1,0:T(8,128)S(1)} %get-tuple-element.82.refs_3_.refs_4_), channel_id=1, source_target_pairs={{0,2},{1,3},{2,0},{3,1},{4,6},{5,7},{6,4},{7,5},{8,10},{9,11},{10,... | collective-permute-start | bytes 12296 | tf_op jit(solution)/shard_map/ppermute | solution.py:29
  58.0 2.4 %collective-permute-start.24 = (f32[8,128]{1,0:T(8,128)S(1)}, f32[8,128]{1,0:T(8,128)S(1)}, u32[]{:S(2)}, u32[]{:S(2)}) collective-permute-start(f32[8,128]{1,0:T(8,128)S(1)} %get-tuple-element.82.refs_3_.refs_4_), channel_id=1, source_target_pairs={{0,1},{1,0},{2,3},{3,2},{4,5},{5,4},{6,7},{7,6},{8,9},{9,8},{10,11... | collective-permute-start | bytes 12296 | tf_op jit(solution)/shard_map/ppermute | solution.py:29
  61.2 9.6 %collective-permute-start.25 = (bf16[64,1024]{1,0:T(8,128)(2,1)S(1)}, bf16[64,1024]{1,0:T(8,128)(2,1)S(1)}, u32[]{:S(2)}, u32[]{:S(2)}) collective-permute-start(bf16[64,1024]{1,0:T(8,128)(2,1)S(1)} %get-tuple-element.86.refs_0_), channel_id=1, source_target_pairs={{0,12},{4,8},{8,4},{12,0},{1,13},{5,9},{9,5},{13,1},{2,14},{6,10},... | collective-permute-start | bytes 393224 | tf_op jit(solution)/shard_map/ppermute | solution.py:29
  63.9 13.1 %collective-permute-start.26 = (bf16[64,1024]{1,0:T(8,128)(2,1)S(1)}, bf16[64,1024]{1,0:T(8,128)(2,1)S(1)}, u32[]{:S(2)}, u32[]{:S(2)}) collective-permute-start(bf16[64,1024]{1,0:T(8,128)(2,1)S(1)} %get-tuple-element.87), channel_id=1, source_target_pairs={{0,8},{4,12},{8,0},{12,4},{1,9},{5,13},{9,1},{13,5},{2,10},{6,14},... | collective-permute-start | bytes 393224 | tf_op jit(solution)/shard_map/ppermute | solution.py:29
  67.4 9.6 %collective-permute-start.27 = (bf16[64,1024]{1,0:T(8,128)(2,1)S(1)}, bf16[64,1024]{1,0:T(8,128)(2,1)S(1)}, u32[]{:S(2)}, u32[]{:S(2)}) collective-permute-start(bf16[64,1024]{1,0:T(8,128)(2,1)S(1)} %get-tuple-element.89), channel_id=1, source_target_pairs={{0,4},{4,0},{8,12},{12,8},{1,5},{5,1},{9,13},{13,9},{2,6},{6,2},{1... | collective-permute-start | bytes 393224 | tf_op jit(solution)/shard_map/ppermute | solution.py:29
  (2 other events, 1.3 us)

commit v15 on v14

--- a/solution.py
+++ b/solution.py
@@ -375,8 +375,8 @@
     )(scal, *after, keep, *more)
 
 
-def stats_kernel(scale, q, pieces, others, scal, *refs):
-    count = min(q, 1)
+def stats_kernel(scale, q, pieces, others, count, skip, scal, *refs):
+    refs = refs[skip:]
     earlier, (own, *refs) = refs[:count], refs[count:]
     more, refs = refs[:others], refs[others:]
     targets, (corr, sums) = refs[: len(pieces)], refs[len(pieces) :]
@@ -415,15 +415,18 @@
     return pl.BlockSpec(shape, lambda i, scal: (0,) * len(shape))
 
 
-def lag_stats(scal, scale, q, pieces, earlier, own, more, observed):
+def lag_stats(scal, scale, q, pieces, after, earlier, own, more, observed):
     rows, lag_dev = own.shape
     outs = [jax.ShapeDtypeStruct((rows, lag_dev), F32), jax.ShapeDtypeStruct((8, -(-rows // LANES) * LANES), F32)]
     return pl.pallas_call(
-        functools.partial(stats_kernel, scale, q, pieces, len(more)),
+        functools.partial(
+            stats_kernel, scale, q, pieces, len(more), len(earlier), len(after)
+        ),
         grid_spec=pltpu.PrefetchScalarGridSpec(
             num_scalar_prefetch=1,
             grid=(1,),
-            in_specs=[whole(e.shape) for e in earlier]
+            in_specs=[ANY] * len(after)
+            + [whole(e.shape) for e in earlier]
             + [whole(own.shape)] * (1 + len(more))
             + target_specs(pieces, lag_dev),
             out_specs=[whole(o.shape) for o in outs],
@@ -432,7 +435,7 @@
         compiler_params=params(16),
         cost_estimate=SMALL,
         name="stats",
-    )(scal, *earlier, own, *more, *[observed] * len(pieces))
+    )(scal, *after, *earlier, own, *more, *[observed] * len(pieces))
 
 
 def slot_scales(sums, lag_total, q):
@@ -485,8 +488,9 @@
 
 
 def normed_kernel(lag_total, chunks, parts, scal, *refs):
-    sums, corrs, out = refs[:parts], refs[parts:-1], refs[-1]
-    for q, (pieces, corr) in enumerate(zip(chunks, corrs)):
+    out = refs[-1]
+    for q, pieces in enumerate(chunks):
+        sums, corr = refs[q * (parts + 1) : q * (parts + 1) + parts], refs[q * (parts + 1) + parts]
         inverse, _ = slot_scales(sums, lag_total, q)
         for unit, first, count, at in placed(pieces):
 
@@ -497,9 +501,9 @@
 
 def normed_rows(scal, lag_total, chunks, sums, corrs, observed):
     blocks, slots, lag_dev = observed.shape
-    ins = [*sums, *corrs]
-    return pl.pallas_call(
-        functools.partial(normed_kernel, lag_total, chunks, len(sums)),
+    ins = [x for s, c in zip(sums, corrs) for x in (*s, c)]
+    return pl.pallas_call(
+        functools.partial(normed_kernel, lag_total, chunks, len(sums[0])),
         grid_spec=pltpu.PrefetchScalarGridSpec(
             num_scalar_prefetch=1,
             grid=(blocks,),
@@ -571,8 +575,8 @@
     trig = tables(classes, span, period, bins_dev, columns, cores)
     if direct and blocks == 4:
         chunks = [
-            [(0, 0, slots), (1, 0, slots)],
-            [(3, 0, slots)],
+            [(0, 0, slots), (3, 0, slots)],
+            [(1, 0, slots)],
             [(2, 0, slots)],
         ]
     else:
@@ -590,7 +594,7 @@
             lax.dynamic_index_in_dim(stacked, place ^ owners[b], 0, False) for b in range(blocks)
         ]
         arrived = [whole_rows[piece[0]] for pieces in chunks for piece in pieces]
-    corrs, all_sums, returned, returned_pieces = [], [], [], []
+    corrs, all_sums, sums_of, returned, returned_pieces, early = [], [], [], [], [], []
     after = []
     for q, pieces in enumerate(chunks):
         rows, arrived = arrived[: len(pieces)], arrived[len(pieces) :]
@@ -605,16 +609,21 @@
         own, *sends = add_cores(scal, after[1:], keep, sends)
         more = [swapped(x, "win", columns, s + 1) for s, x in enumerate(sends)]
         after = [own, *more] if q == 0 else []
-        corr, sums = lag_stats(scal, lag_scale, q, pieces, all_sums, own, more, observed)
+        last = q == len(chunks) - 1
+        corr, sums = lag_stats(
+            scal, lag_scale, q, pieces, early if last else [], all_sums, own, more, observed
+        )
         corrs.append(corr)
         all_sums = [sums]
-    sums = [swapped(sums, ("win", "freq"), peers, s) for s in reversed(range(peers))]
-    after = []
-    numbered = list(enumerate(chunks))
-    for group in (numbered[1:], numbered[:1]):
-        grads = gradients(scal, lag_total, group, after, sums, [corrs[q] for q, _ in group], observed)
-        pieces = [p for _, some_pieces in group for p in some_pieces]
-        after = [grads[0]]
+        if q and not last:
+            continue
+        sums = [swapped(sums, ("win", "freq"), peers, s) for s in reversed(range(peers))]
+        all_sums = []
+        group = list(enumerate(chunks))[:1] if q == 0 else list(enumerate(chunks))[:0:-1]
+        sums_of += [sums] * len(group)
+        grads = gradients(scal, lag_total, group, [], sums, [corrs[i] for i, _ in group], observed)
+        early = [grads[0]]
+        back = [p for _, these in group for p in these]
         if not direct:
             stacked = jnp.stack(list(grads) + [jnp.zeros_like(grads[0])])
             grads = []
@@ -623,11 +632,10 @@
                 for b in range(blocks):
                     block = jnp.where(owners[b] == place ^ d, b, block)
                 grads.append(lax.dynamic_index_in_dim(stacked, block, 0, False))
-            pieces = [(d, pieces[0][1], some) for d in shifts]
-        sent = [swapped(g, "recv", places, p[0]) for p, g in reversed(list(zip(pieces, grads)))]
-        returned += sent[::-1]
-        returned_pieces += pieces
-    normed = normed_rows(scal, lag_total, chunks, sums, corrs, observed)
+            back = [(d, back[0][1], some) for d in shifts]
+        returned += [swapped(g, "recv", places, p[0]) for p, g in zip(back, grads)]
+        returned_pieces += back
+    normed = normed_rows(scal, lag_total, chunks, sums_of, corrs, observed)
     adjoint = adjoint_rows(src_ids, returned_pieces, returned, channels)
     return (normed, adjoint)
 

time: 78.3 us -> 82.6 us (1.055)
  starting transfers between devices: 26 us -> 33.2 us
  waiting for transfers between devices: 23.5 us -> 20.6 us
    ppermute x28 -> x31, starting transfers between devices: 26 us -> 33.2 us  [swapped(): return lax.ppermute(value, axis, [(i, i ^ step) for i in range(size)])]
    ppermute x28 -> x31, waiting for transfers between devices: 23.5 us -> 20.6 us  [swapped(): return lax.ppermute(value, axis, [(i, i ^ step) for i in range(size)])]
  transfers between devices with their start and end apart: 28 -> 31, of which waited for: 13 -> 13; matrix products, arithmetic and copies ran while one was open for 0% -> 0% of each run, Pallas kernels for 24% -> 24%
where the time goes in v15:
time: 82.6 us; the launch traced here: 82.4 us
  starting transfers between devices  33.2 us (40%)
  Pallas kernels  23.2 us (28%)
  waiting for transfers between devices  20.6 us (25%)
  local copies, waits for them, and re-layouts  4 us (5%)
  between operations  1.49 us (2%)
    ppermute x31, starting transfers between devices, swapped(): return lax.ppermute(value, axis, [(i, i ^ step) for i in range(size)])  33.2 us
    ppermute x31, waiting for transfers between devices, swapped(): return lax.ppermute(value, axis, [(i, i ^ step) for i in range(size)])  20.6 us
    pallas_call x3, Pallas kernels, lag_parts(): pl.pallas_call(functools.partial(lags_kernel, geometry, split, len(after)...  5.94 us
    pallas_call x1, Pallas kernels, normed_rows(): pl.pallas_call(functools.partial(normed_kernel, lag_total, chunks, len(su...  3.26 us
    pallas_call x1, Pallas kernels, gather_own(): pl.pallas_call(functools.partial(own_kernel, classes, parts), out_shape=[...  3.07 us
    unnamed x12, local copies, waits for them, and re-layouts  2.68 us
    pallas_call x3, Pallas kernels, lag_stats(): pl.pallas_call(functools.partial(stats_kernel, scale, q, pieces, len(more...  2.24 us
    pallas_call x3, Pallas kernels, add_cores(): pl.pallas_call(functools.partial(cores_kernel, len(after), len(more)), ou...  2.06 us
  transfers between devices with their start and end apart: 31, of which 13 were waited for; matrix products, arithmetic and copies ran while one was open for 0% of the time, Pallas kernels for 24%

profile of v15, /device:TPU:0, one launch (start us, length us, event | category | flops | bytes accessed | tf_op | source)
XLA Modules:
  0.0 82.4 jit_solution(9251123012860746382)
XLA Ops:
  0.7 1.3 %constant_dynamic-slice_fusion = (bf16[1,2,128,1024]{3,2,1,0:T(8,128)(2,1)S(1)}, bf16[1,2,128,1024]{3,2,1,0:T(8,128)(2,1)S(1)}) fusion(bf16[1,2,128,2048]{3,2,1,0:T(8,128)(2,1)} %param.8, s32[]{:T(128)S(6)} %select_n.7, s32[]{:T(128)S(6)} %select_n.6), kind=kLoop, calls=%fused_computation | loop fusion | bytes 2097160 | tf_op jit(solution)/shard_map/dynamic_slice | solution.py:559
  2.0 3.0 %collective-permute-start = (bf16[1,2,128,1024]{3,2,1,0:T(8,128)(2,1)S(1)}, bf16[1,2,128,1024]{3,2,1,0:T(8,128)(2,1)S(1)}, u32[]{:S(2)}, u32[]{:S(2)}) collective-permute-start(bf16[1,2,128,1024]{3,2,1,0:T(8,128)(2,1)S(1)} %get-tuple-element.90), channel_id=1, source_target_pairs={{0,2},{2,0},{1,3},{3,1},{4,6},{6,4},{5,7},{7,5},{8,10},{10,8},{9,1... | collective-permute-start | bytes 1572872 | tf_op jit(solution)/shard_map/ppermute | solution.py:29
  8.3 1.2 %index.1 = (s32[128]{0:T(128)S(1)}, s32[1,64]{1,0:T(1,128)S(1)}, s32[1,64]{1,0:T(1,128)S(1)}, s32[1,64]{1,0:T(1,128)S(1)}, s32[1,64]{1,0:T(1,128)S(1)}, /*index=5*/s32[4,64]{1,0:T(4,128)S(1)}) custom-call(s32[1]{0:T(128)S(6)} %copy.10.refs_0_, s32[4]{0:T(128)S(1)} %copy-done.4, s32[4]{0:T(128)S(1)} %bitcast.1, s32[4,64]{1,0:T(4,128)S(1)} %copy-done.2, ...), custom_call_target="tpu_custom_call" | custom-call | flops 1 | bytes 1 | tf_op jit(solution)/shard_map/index/pallas_call | solution.py:92
  9.5 3.7 %collective-permute-start.1 = (s32[1,64]{1,0:T(1,128)S(1)}, s32[1,64]{1,0:T(1,128)S(1)}, u32[]{:S(2)}, u32[]{:S(2)}) collective-permute-start(s32[1,64]{1,0:T(1,128)S(1)} %get-tuple-element.47), channel_id=1, source_target_pairs={{0,12},{4,8},{8,4},{12,0},{1,13},{5,9},{9,5},{13,1},{2,14},{6,10},... | collective-permute-start | bytes 776 | tf_op jit(solution)/shard_map/ppermute | solution.py:29
  13.2 0.8 collective-permute-start.3
  14.9 2.7 %collective-permute-done.2.refs_3_.refs_2_ = s32[1,64]{1,0:T(1,128)S(1)} collective-permute-done((s32[1,64]{1,0:T(1,128)S(1)}, s32[1,64]{1,0:T(1,128)S(1)}, u32[]{:S(2)}, u32[]{:S(2)}) %collective-permute-start.2) | collective-permute-done | bytes 288 | tf_op jit(solution)/shard_map/ppermute | solution.py:29
  17.7 1.6 %rows.1 = (bf16[1,2,64,1024]{3,2,1,0:T(8,128)(2,1)S(1)}, bf16[1,2,64,1024]{3,2,1,0:T(8,128)(2,1)S(1)}, bf16[1,2,64,1024]{3,2,1,0:T(8,128)(2,1)S(1)}, bf16[1,2,64...) custom-call(s32[128]{0:T(128)S(1)} %get-tuple-element.46.scal, ...), custom_call_target="tpu_custom_call" | custom-call | flops 1 | bytes 1 | tf_op jit(solution)/shard_map/rows/pallas_call | solution.py:175
  19.2 3.2 %collective-permute-start.4 = (bf16[1,2,64,1024]{3,2,1,0:T(8,128)(2,1)S(1)}, bf16[1,2,64,1024]{3,2,1,0:T(8,128)(2,1)S(1)}, u32[]{:S(2)}, u32[]{:S(2)}) collective-permute-start(bf16[1,2,64,1024]{3,2,1,0:T(8,128)(2,1)S(1)} %get-tuple-element.52), channel_id=1, source_target_pairs={{0,12},{4,8},{8,4},{12,0},{1,13},{5,9},{9,5},{13,1},{2,14},{6,10},... | collective-permute-start | bytes 786440 | tf_op jit(solution)/shard_map/ppermute | solution.py:29
  22.4 1.3 %collective-permute-start.18 = (bf16[1,2,64,1024]{3,2,1,0:T(8,128)(2,1)S(1)}, bf16[1,2,64,1024]{3,2,1,0:T(8,128)(2,1)S(1)}, u32[]{:S(2)}, u32[]{:S(2)}) collective-permute-start(bf16[1,2,64,1024]{3,2,1,0:T(8,128)(2,1)S(1)} %get-tuple-element.72), channel_id=1, source_target_pairs={{0,4},{4,0},{8,12},{12,8},{1,5},{5,1},{9,13},{13,9},{2,6},{6,2},{1... | collective-permute-start | bytes 786440 | tf_op jit(solution)/shard_map/ppermute | solution.py:29
  23.7 3.1 %own.1 = (bf16[4,1,2,64,1024]{4,3,2,1,0:T(8,128)(2,1)S(1)}, bf16[8,256,1024]{2,1,0:T(8,128)(2,1)S(1)}) custom-call(s32[128]{0:T(128)S(1)} %get-tuple-element.46.scal, bf16[1,2,128,1024]{3,2,1,0:T(8,128)(2,1)S(1)} %get-tuple-element.53.kept, s32[4,64]{1,0:T(4,128)S(1)} %get-tuple-element.54.rec_ids, f32[2,56,1024]{2,1,0:T(8,128)S(1)} %copy-done.1), custom_call_target="tpu_custom_call" | custom-call | flops 1 | bytes 1 | tf_op jit(solution)/shard_map/own/pallas_call | solution.py:204
  26.8 3.7 %collective-permute-done.4.refs_1_ = bf16[1,2,64,1024]{3,2,1,0:T(8,128)(2,1)S(1)} collective-permute-done((bf16[1,2,64,1024]{3,2,1,0:T(8,128)(2,1)S(1)}, bf16[1,2,64,1024]{3,2,1,0:T(8,128)(2,1)S(1)}, u32[]{:S(2)}, u32[]{:S(2)}) %collective-permute-start.4) | collective-permute-done | bytes 262176 | tf_op jit(solution)/shard_map/ppermute | solution.py:29
  30.7 2.5 %lags.3 = (f32[2,128,1024]{2,1,0:T(8,128)S(1)}, bf16[2,16,1024]{2,1,0:T(8,128)(2,1)S(1)}, bf16[2,16,1024]{2,1,0:T(8,128)(2,1)S(1)}, bf16[2,16,1024]{2,1,0:T(8,12...) custom-call(s32[128]{0:T(128)S(1)} %get-tuple-element.46.scal, ...), custom_call_target="tpu_custom_call" | custom-call | flops 20000000000 | bytes 1048576 | tf_op jit(solution)/shard_map/lags/pallas_call | solution.py:331
  37.2 0.8 cores.3
  38.0 1.1 %collective-permute-start.13 = (bf16[128,1024]{1,0:T(8,128)(2,1)S(1)}, bf16[128,1024]{1,0:T(8,128)(2,1)S(1)}, u32[]{:S(2)}, u32[]{:S(2)}) collective-permute-start(bf16[128,1024]{1,0:T(8,128)(2,1)S(1)} %get-tuple-element.67), channel_id=1, source_target_pairs={{0,2},{2,0},{1,3},{3,1},{4,6},{6,4},{5,7},{7,5},{8,10},{10,8},{9,1... | collective-permute-start | bytes 786440 | tf_op jit(solution)/shard_map/ppermute | solution.py:29
  39.1 4.8 %collective-permute-done.17.refs_1_.refs_0_ = bf16[1,2,64,1024]{3,2,1,0:T(8,128)(2,1)S(1)} collective-permute-done((bf16[1,2,64,1024]{3,2,1,0:T(8,128)(2,1)S(1)}, bf16[1,2,64,1024]{3,2,1,0:T(8,128)(2,1)S(1)}, u32[]{:S(2)}, u32[]{:S(2)}) %collective-permute-start.17) | collective-permute-done | bytes 262176 | tf_op jit(solution)/shard_map/ppermute | solution.py:29
  44.0 1.7 %lags.4 = (f32[2,64,1024]{2,1,0:T(8,128)S(1)}, bf16[2,32,1024]{2,1,0:T(8,128)(2,1)S(1)}, bf16[2,32,1024]{2,1,0:T(8,128)(2,1)S(1)}) custom-call(s32[128]{0:T(128)S(1)} %get-tuple-element.46.scal, bf16[8,128,256]{2,1,0:T(8,128)(2,1)S(1)} %cross.4.refs_0_, bf16[8,256,1024]{2,1,0:T(8,128)(2,1)S(1)} %get-tuple-element.56.refs_1_), custom_call_target="tpu_custom_call" | custom-call | flops 1 | bytes 1 | tf_op jit(solution)/shard_map/lags/pallas_call | solution.py:331
  46.4 1.7 %lags.5 = (f32[2,64,1024]{2,1,0:T(8,128)S(1)}, bf16[2,32,1024]{2,1,0:T(8,128)(2,1)S(1)}, bf16[2,32,1024]{2,1,0:T(8,128)(2,1)S(1)}) custom-call(s32[128]{0:T(128)S(1)} %get-tuple-element.46.scal, bf16[8,128,256]{2,1,0:T(8,128)(2,1)S(1)} %cross.5.refs_0_, bf16[8,256,1024]{2,1,0:T(8,128)(2,1)S(1)} %get-tuple-element.56.refs_1_), custom_call_target="tpu_custom_call" | custom-call | flops 1 | bytes 1 | tf_op jit(solution)/shard_map/lags/pallas_call | solution.py:331
  49.4 1.6 %collective-permute-start.21 = (bf16[64,1024]{1,0:T(8,128)(2,1)S(1)}, bf16[64,1024]{1,0:T(8,128)(2,1)S(1)}, u32[]{:S(2)}, u32[]{:S(2)}) collective-permute-start(bf16[64,1024]{1,0:T(8,128)(2,1)S(1)} %get-tuple-element.77), channel_id=1, source_target_pairs={{0,2},{2,0},{1,3},{3,1},{4,6},{6,4},{5,7},{7,5},{8,10},{10,8},{9,1... | collective-permute-start | bytes 393224 | tf_op jit(solution)/shard_map/ppermute | solution.py:29
  52.2 0.8 stats.3
  53.6 0.9 %collective-permute-start.15 = (f32[8,128]{1,0:T(8,128)S(1)}, f32[8,128]{1,0:T(8,128)S(1)}, u32[]{:S(2)}, u32[]{:S(2)}) collective-permute-start(f32[8,128]{1,0:T(8,128)S(1)} %get-tuple-element.68.refs_3_), channel_id=1, source_target_pairs={{0,2},{1,3},{2,0},{3,1},{4,6},{5,7},{6,4},{7,5},{8,10},{9,11},{10,... | collective-permute-start | bytes 12296 | tf_op jit(solution)/shard_map/ppermute | solution.py:29
  54.9 2.1 %collective-permute-done.14.refs_0_ = f32[8,128]{1,0:T(8,128)S(1)} collective-permute-done((f32[8,128]{1,0:T(8,128)S(1)}, f32[8,128]{1,0:T(8,128)S(1)}, u32[]{:S(2)}, u32[]{:S(2)}) %collective-permute-start.14) | collective-permute-done | bytes 4128 | tf_op jit(solution)/shard_map/ppermute | solution.py:29
  57.0 1.0 %collective-permute-done.15.refs_1_ = f32[8,128]{1,0:T(8,128)S(1)} collective-permute-done((f32[8,128]{1,0:T(8,128)S(1)}, f32[8,128]{1,0:T(8,128)S(1)}, u32[]{:S(2)}, u32[]{:S(2)}) %collective-permute-start.15) | collective-permute-done | bytes 4128 | tf_op jit(solution)/shard_map/ppermute | solution.py:29
  57.9 0.8 gradient.2
  59.5 0.7 stats.5
  60.2 1.1 %collective-permute-start.25 = (f32[8,128]{1,0:T(8,128)S(1)}, f32[8,128]{1,0:T(8,128)S(1)}, u32[]{:S(2)}, u32[]{:S(2)}) collective-permute-start(f32[8,128]{1,0:T(8,128)S(1)} %get-tuple-element.84.refs_8_.refs_13_.refs_3_), channel_id=1, source_target_pairs={{0,3},{1,2},{2,1},{3,0},{4,7},{5,6},{6,5},{7,4},{8,11},{9,10},{10,... | collective-permute-start | bytes 12296 | tf_op jit(solution)/shard_map/ppermute | solution.py:29
  62.1 2.5 %collective-permute-start.28 = (bf16[64,1024]{1,0:T(8,128)(2,1)S(1)}, bf16[64,1024]{1,0:T(8,128)(2,1)S(1)}, u32[]{:S(2)}, u32[]{:S(2)}) collective-permute-start(bf16[64,1024]{1,0:T(8,128)(2,1)S(1)} %get-tuple-element.87), channel_id=1, source_target_pairs={{0,12},{4,8},{8,4},{12,0},{1,13},{5,9},{9,5},{13,1},{2,14},{6,10},... | collective-permute-start | bytes 393224 | tf_op jit(solution)/shard_map/ppermute | solution.py:29
  65.0 0.8 %gradient.3 = (bf16[64,1024]{1,0:T(8,128)(2,1)S(1)}, bf16[64,1024]{1,0:T(8,128)(2,1)S(1)}) custom-call(s32[128]{0:T(128)S(1)} %get-tuple-element.46.scal, f32[8,128]{1,0:T(8,128)S(1)} %collective-permute-done.25.refs_5_.refs_10_.refs_0_, f32[8,128]{1,0:T(8,128)S(1)} %collective-permute-done.26.refs_6_.refs_11_.refs_1_, ...), custom_call_target="tpu_custom_call" | custom-call | flops 1 | bytes 1 | tf_op jit(solution)/shard_map/gradient/pallas_call | solution.py:473
  65.8 8.8 %collective-permute-start.29 = (bf16[64,1024]{1,0:T(8,128)(2,1)S(1)}, bf16[64,1024]{1,0:T(8,128)(2,1)S(1)}, u32[]{:S(2)}, u32[]{:S(2)}) collective-permute-start(bf16[64,1024]{1,0:T(8,128)(2,1)S(1)} %get-tuple-element.88), channel_id=1, source_target_pairs={{0,8},{4,12},{8,0},{12,4},{1,9},{5,13},{9,1},{13,5},{2,10},{6,14},... | collective-permute-start | bytes 393224 | tf_op jit(solution)/shard_map/ppermute | solution.py:29
  74.7 3.3 %normed.1 = f32[4,64,1024]{2,1,0:T(8,128)} custom-call(s32[128]{0:T(128)S(1)} %get-tuple-element.46.scal, f32[8,128]{1,0:T(8,128)S(1)} %collective-permute-done.14.refs_0_, f32[8,128]{1,0:T(8,128)S(1)} %collective-permute-done.15.refs_1_, f32[8,128]{1,0:T(8,128)S(1)} %collective-permute-done.16.refs_2_, f32[8,128]{1,0:T(8,128)S(1)} %get-tuple-element.68.refs_3_, ...), custom_call_target="tpu_custom_call" | custom-call | flops 1 | bytes 1 | tf_op jit(solution)/shard_map/normed/pallas_call | solution.py:505
  77.9 2.6 %collective-permute-done.29.refs_6_ = bf16[64,1024]{1,0:T(8,128)(2,1)S(1)} collective-permute-done((bf16[64,1024]{1,0:T(8,128)(2,1)S(1)}, bf16[64,1024]{1,0:T(8,128)(2,1)S(1)}, u32[]{:S(2)}, u32[]{:S(2)}) %collective-permute-start.29) | collective-permute-done | bytes 131104 | tf_op jit(solution)/shard_map/ppermute | solution.py:29
  80.6 0.8 collective-permute-done.30.refs_7_
  81.3 1.1 %adjoint.1 = f32[128,1024]{1,0:T(8,128)} custom-call(s32[1,64]{1,0:T(1,128)S(1)} %get-tuple-element.50.refs_5_.refs_0_, s32[1,64]{1,0:T(1,128)S(1)} %collective-permute-done.1.refs_2_.refs_1_, s32[1,64]{1,0:T(1,128)S(1)} %collective-permute-done.2.refs_3_.refs_2_, s32[1,64]{1,0:T(1,128)S(1)} %collective-permute-done.3.refs_4_.refs_3_, ...), custom_call_target="tpu_custom_call" | custom-call | flops 1 | bytes 1 | tf_op jit(solution)/shard_map/adjoint/pallas_call | solution.py:529
  (63 shorter events, 14.0 us)
Async XLA Ops:
  0.6 23.1 %copy-start.1 = (f32[2,56,1024]{2,1,0:T(8,128)S(1)}, f32[2,56,1024]{2,1,0:T(8,128)}, u32[]{:S(2)}) copy-start(f32[2,56,1024]{2,1,0:T(8,128)} %constant.16.clone.trig) | copy-start | bytes 1376260
  2.0 15.7 %collective-permute-start = (bf16[1,2,128,1024]{3,2,1,0:T(8,128)(2,1)S(1)}, bf16[1,2,128,1024]{3,2,1,0:T(8,128)(2,1)S(1)}, u32[]{:S(2)}, u32[]{:S(2)}) collective-permute-start(bf16[1,2,128,1024]{3,2,1,0:T(8,128)(2,1)S(1)} %get-tuple-element.90), channel_id=1, source_target_pairs={{0,2},{2,0},{1,3},{3,1},{4,6},{6,4},{5,7},{7,5},{8,10},{10,8},{9,1... | collective-permute-start | bytes 1572872 | tf_op jit(solution)/shard_map/ppermute | solution.py:29
  9.5 5.4 %collective-permute-start.1 = (s32[1,64]{1,0:T(1,128)S(1)}, s32[1,64]{1,0:T(1,128)S(1)}, u32[]{:S(2)}, u32[]{:S(2)}) collective-permute-start(s32[1,64]{1,0:T(1,128)S(1)} %get-tuple-element.47), channel_id=1, source_target_pairs={{0,12},{4,8},{8,4},{12,0},{1,13},{5,9},{9,5},{13,1},{2,14},{6,10},... | collective-permute-start | bytes 776 | tf_op jit(solution)/shard_map/ppermute | solution.py:29
  13.2 4.4 %collective-permute-start.2 = (s32[1,64]{1,0:T(1,128)S(1)}, s32[1,64]{1,0:T(1,128)S(1)}, u32[]{:S(2)}, u32[]{:S(2)}) collective-permute-start(s32[1,64]{1,0:T(1,128)S(1)} %get-tuple-element.48), channel_id=1, source_target_pairs={{0,8},{4,12},{8,0},{12,4},{1,9},{5,13},{9,1},{13,5},{2,10},{6,14},... | collective-permute-start | bytes 776 | tf_op jit(solution)/shard_map/ppermute | solution.py:29
  13.2 4.4 %collective-permute-start.3 = (s32[1,64]{1,0:T(1,128)S(1)}, s32[1,64]{1,0:T(1,128)S(1)}, u32[]{:S(2)}, u32[]{:S(2)}) collective-permute-start(s32[1,64]{1,0:T(1,128)S(1)} %get-tuple-element.49), channel_id=1, source_target_pairs={{0,4},{4,0},{8,12},{12,8},{1,5},{5,1},{9,13},{13,9},{2,6},{6,2},{1... | collective-permute-start | bytes 776 | tf_op jit(solution)/shard_map/ppermute | solution.py:29
  19.2 11.2 %collective-permute-start.4 = (bf16[1,2,64,1024]{3,2,1,0:T(8,128)(2,1)S(1)}, bf16[1,2,64,1024]{3,2,1,0:T(8,128)(2,1)S(1)}, u32[]{:S(2)}, u32[]{:S(2)}) collective-permute-start(bf16[1,2,64,1024]{3,2,1,0:T(8,128)(2,1)S(1)} %get-tuple-element.52), channel_id=1, source_target_pairs={{0,12},{4,8},{8,4},{12,0},{1,13},{5,9},{9,5},{13,1},{2,14},{6,10},... | collective-permute-start | bytes 786440 | tf_op jit(solution)/shard_map/ppermute | solution.py:29
  22.4 21.4 %collective-permute-start.17 = (bf16[1,2,64,1024]{3,2,1,0:T(8,128)(2,1)S(1)}, bf16[1,2,64,1024]{3,2,1,0:T(8,128)(2,1)S(1)}, u32[]{:S(2)}, u32[]{:S(2)}) collective-permute-start(bf16[1,2,64,1024]{3,2,1,0:T(8,128)(2,1)S(1)} %get-tuple-element.71), channel_id=1, source_target_pairs={{0,8},{4,12},{8,0},{12,4},{1,9},{5,13},{9,1},{13,5},{2,10},{6,14},... | collective-permute-start | bytes 786440 | tf_op jit(solution)/shard_map/ppermute | solution.py:29
  22.4 21.4 %collective-permute-start.18 = (bf16[1,2,64,1024]{3,2,1,0:T(8,128)(2,1)S(1)}, bf16[1,2,64,1024]{3,2,1,0:T(8,128)(2,1)S(1)}, u32[]{:S(2)}, u32[]{:S(2)}) collective-permute-start(bf16[1,2,64,1024]{3,2,1,0:T(8,128)(2,1)S(1)} %get-tuple-element.72), channel_id=1, source_target_pairs={{0,4},{4,0},{8,12},{12,8},{1,5},{5,1},{9,13},{13,9},{2,6},{6,2},{1... | collective-permute-start | bytes 786440 | tf_op jit(solution)/shard_map/ppermute | solution.py:29
  33.2 1.3 %collective-permute-start.5 = (bf16[2,16,1024]{2,1,0:T(8,128)(2,1)S(1)}, bf16[2,16,1024]{2,1,0:T(8,128)(2,1)S(1)}, u32[]{:S(2)}, u32[]{:S(2)}) collective-permute-start(bf16[2,16,1024]{2,1,0:T(8,128)(2,1)S(1)} %get-tuple-element.58), channel_id=1, source_target_pairs={{0,1},{1,0},{2,3},{3,2},{4,5},{5,4},{6,7},{7,6},{8,9},{9,8},{10,11... | collective-permute-start | bytes 196616 | tf_op jit(solution)/shard_map/ppermute | solution.py:29
  33.3 1.4 %collective-permute-start.6 = (bf16[2,16,1024]{2,1,0:T(8,128)(2,1)S(1)}, bf16[2,16,1024]{2,1,0:T(8,128)(2,1)S(1)}, u32[]{:S(2)}, u32[]{:S(2)}) collective-permute-start(bf16[2,16,1024]{2,1,0:T(8,128)(2,1)S(1)} %get-tuple-element.59), channel_id=1, source_target_pairs={{0,1},{1,0},{2,3},{3,2},{4,5},{5,4},{6,7},{7,6},{8,9},{9,8},{10,11... | collective-permute-start | bytes 196616 | tf_op jit(solution)/shard_map/ppermute | solution.py:29
  33.8 1.3 %collective-permute-start.7 = (bf16[2,16,1024]{2,1,0:T(8,128)(2,1)S(1)}, bf16[2,16,1024]{2,1,0:T(8,128)(2,1)S(1)}, u32[]{:S(2)}, u32[]{:S(2)}) collective-permute-start(bf16[2,16,1024]{2,1,0:T(8,128)(2,1)S(1)} %get-tuple-element.60), channel_id=1, source_target_pairs={{0,1},{1,0},{2,3},{3,2},{4,5},{5,4},{6,7},{7,6},{8,9},{9,8},{10,11... | collective-permute-start | bytes 196616 | tf_op jit(solution)/shard_map/ppermute | solution.py:29
  34.5 1.3 %collective-permute-start.8 = (bf16[2,16,1024]{2,1,0:T(8,128)(2,1)S(1)}, bf16[2,16,1024]{2,1,0:T(8,128)(2,1)S(1)}, u32[]{:S(2)}, u32[]{:S(2)}) collective-permute-start(bf16[2,16,1024]{2,1,0:T(8,128)(2,1)S(1)} %get-tuple-element.61), channel_id=1, source_target_pairs={{0,1},{1,0},{2,3},{3,2},{4,5},{5,4},{6,7},{7,6},{8,9},{9,8},{10,11... | collective-permute-start | bytes 196616 | tf_op jit(solution)/shard_map/ppermute | solution.py:29
  34.7 1.3 %collective-permute-start.9 = (bf16[2,16,1024]{2,1,0:T(8,128)(2,1)S(1)}, bf16[2,16,1024]{2,1,0:T(8,128)(2,1)S(1)}, u32[]{:S(2)}, u32[]{:S(2)}) collective-permute-start(bf16[2,16,1024]{2,1,0:T(8,128)(2,1)S(1)} %get-tuple-element.62), channel_id=1, source_target_pairs={{0,1},{1,0},{2,3},{3,2},{4,5},{5,4},{6,7},{7,6},{8,9},{9,8},{10,11... | collective-permute-start | bytes 196616 | tf_op jit(solution)/shard_map/ppermute | solution.py:29
  35.0 1.3 %collective-permute-start.10 = (bf16[2,16,1024]{2,1,0:T(8,128)(2,1)S(1)}, bf16[2,16,1024]{2,1,0:T(8,128)(2,1)S(1)}, u32[]{:S(2)}, u32[]{:S(2)}) collective-permute-start(bf16[2,16,1024]{2,1,0:T(8,128)(2,1)S(1)} %get-tuple-element.63), channel_id=1, source_target_pairs={{0,1},{1,0},{2,3},{3,2},{4,5},{5,4},{6,7},{7,6},{8,9},{9,8},{10,11... | collective-permute-start | bytes 196616 | tf_op jit(solution)/shard_map/ppermute | solution.py:29
  35.8 1.3 %collective-permute-start.11 = (bf16[2,16,1024]{2,1,0:T(8,128)(2,1)S(1)}, bf16[2,16,1024]{2,1,0:T(8,128)(2,1)S(1)}, u32[]{:S(2)}, u32[]{:S(2)}) collective-permute-start(bf16[2,16,1024]{2,1,0:T(8,128)(2,1)S(1)} %get-tuple-element.64), channel_id=1, source_target_pairs={{0,1},{1,0},{2,3},{3,2},{4,5},{5,4},{6,7},{7,6},{8,9},{9,8},{10,11... | collective-permute-start | bytes 196616 | tf_op jit(solution)/shard_map/ppermute | solution.py:29
  35.9 1.3 %collective-permute-start.12 = (bf16[2,16,1024]{2,1,0:T(8,128)(2,1)S(1)}, bf16[2,16,1024]{2,1,0:T(8,128)(2,1)S(1)}, u32[]{:S(2)}, u32[]{:S(2)}) collective-permute-start(bf16[2,16,1024]{2,1,0:T(8,128)(2,1)S(1)} %get-tuple-element.65), channel_id=1, source_target_pairs={{0,1},{1,0},{2,3},{3,2},{4,5},{5,4},{6,7},{7,6},{8,9},{9,8},{10,11... | collective-permute-start | bytes 196616 | tf_op jit(solution)/shard_map/ppermute | solution.py:29
  38.0 10.7 %collective-permute-start.13 = (bf16[128,1024]{1,0:T(8,128)(2,1)S(1)}, bf16[128,1024]{1,0:T(8,128)(2,1)S(1)}, u32[]{:S(2)}, u32[]{:S(2)}) collective-permute-start(bf16[128,1024]{1,0:T(8,128)(2,1)S(1)} %get-tuple-element.67), channel_id=1, source_target_pairs={{0,2},{2,0},{1,3},{3,1},{4,6},{6,4},{5,7},{7,5},{8,10},{10,8},{9,1... | collective-permute-start | bytes 786440 | tf_op jit(solution)/shard_map/ppermute | solution.py:29
  45.7 3.0 %collective-permute-start.19 = (bf16[2,32,1024]{2,1,0:T(8,128)(2,1)S(1)}, bf16[2,32,1024]{2,1,0:T(8,128)(2,1)S(1)}, u32[]{:S(2)}, u32[]{:S(2)}) collective-permute-start(bf16[2,32,1024]{2,1,0:T(8,128)(2,1)S(1)} %get-tuple-element.74), channel_id=1, source_target_pairs={{0,1},{1,0},{2,3},{3,2},{4,5},{5,4},{6,7},{7,6},{8,9},{9,8},{10,11... | collective-permute-start | bytes 393224 | tf_op jit(solution)/shard_map/ppermute | solution.py:29
  45.8 2.9 %collective-permute-start.20 = (bf16[2,32,1024]{2,1,0:T(8,128)(2,1)S(1)}, bf16[2,32,1024]{2,1,0:T(8,128)(2,1)S(1)}, u32[]{:S(2)}, u32[]{:S(2)}) collective-permute-start(bf16[2,32,1024]{2,1,0:T(8,128)(2,1)S(1)} %get-tuple-element.75), channel_id=1, source_target_pairs={{0,1},{1,0},{2,3},{3,2},{4,5},{5,4},{6,7},{7,6},{8,9},{9,8},{10,11... | collective-permute-start | bytes 393224 | tf_op jit(solution)/shard_map/ppermute | solution.py:29
  48.2 2.8 %collective-permute-start.22 = (bf16[2,32,1024]{2,1,0:T(8,128)(2,1)S(1)}, bf16[2,32,1024]{2,1,0:T(8,128)(2,1)S(1)}, u32[]{:S(2)}, u32[]{:S(2)}) collective-permute-start(bf16[2,32,1024]{2,1,0:T(8,128)(2,1)S(1)} %get-tuple-element.80), channel_id=1, source_target_pairs={{0,1},{1,0},{2,3},{3,2},{4,5},{5,4},{6,7},{7,6},{8,9},{9,8},{10,11... | collective-permute-start | bytes 393224 | tf_op jit(solution)/shard_map/ppermute | solution.py:29
  48.3 2.6 %collective-permute-start.23 = (bf16[2,32,1024]{2,1,0:T(8,128)(2,1)S(1)}, bf16[2,32,1024]{2,1,0:T(8,128)(2,1)S(1)}, u32[]{:S(2)}, u32[]{:S(2)}) collective-permute-start(bf16[2,32,1024]{2,1,0:T(8,128)(2,1)S(1)} %get-tuple-element.81), channel_id=1, source_target_pairs={{0,1},{1,0},{2,3},{3,2},{4,5},{5,4},{6,7},{7,6},{8,9},{9,8},{10,11... | collective-permute-start | bytes 393224 | tf_op jit(solution)/shard_map/ppermute | solution.py:29
  49.4 9.4 %collective-permute-start.21 = (bf16[64,1024]{1,0:T(8,128)(2,1)S(1)}, bf16[64,1024]{1,0:T(8,128)(2,1)S(1)}, u32[]{:S(2)}, u32[]{:S(2)}) collective-permute-start(bf16[64,1024]{1,0:T(8,128)(2,1)S(1)} %get-tuple-element.77), channel_id=1, source_target_pairs={{0,2},{2,0},{1,3},{3,1},{4,6},{6,4},{5,7},{7,5},{8,10},{10,8},{9,1... | collective-permute-start | bytes 393224 | tf_op jit(solution)/shard_map/ppermute | solution.py:29
  51.6 7.9 %collective-permute-start.24 = (bf16[64,1024]{1,0:T(8,128)(2,1)S(1)}, bf16[64,1024]{1,0:T(8,128)(2,1)S(1)}, u32[]{:S(2)}, u32[]{:S(2)}) collective-permute-start(bf16[64,1024]{1,0:T(8,128)(2,1)S(1)} %get-tuple-element.83), channel_id=1, source_target_pairs={{0,2},{2,0},{1,3},{3,1},{4,6},{6,4},{5,7},{7,5},{8,10},{10,8},{9,1... | collective-permute-start | bytes 393224 | tf_op jit(solution)/shard_map/ppermute | solution.py:29
  53.0 4.0 %collective-permute-start.14 = (f32[8,128]{1,0:T(8,128)S(1)}, f32[8,128]{1,0:T(8,128)S(1)}, u32[]{:S(2)}, u32[]{:S(2)}) collective-permute-start(f32[8,128]{1,0:T(8,128)S(1)} %get-tuple-element.68.refs_3_), channel_id=1, source_target_pairs={{0,3},{1,2},{2,1},{3,0},{4,7},{5,6},{6,5},{7,4},{8,11},{9,10},{10,... | collective-permute-start | bytes 12296 | tf_op jit(solution)/shard_map/ppermute | solution.py:29
  53.6 4.3 %collective-permute-start.15 = (f32[8,128]{1,0:T(8,128)S(1)}, f32[8,128]{1,0:T(8,128)S(1)}, u32[]{:S(2)}, u32[]{:S(2)}) collective-permute-start(f32[8,128]{1,0:T(8,128)S(1)} %get-tuple-element.68.refs_3_), channel_id=1, source_target_pairs={{0,2},{1,3},{2,0},{3,1},{4,6},{5,7},{6,4},{7,5},{8,10},{9,11},{10,... | collective-permute-start | bytes 12296 | tf_op jit(solution)/shard_map/ppermute | solution.py:29
  54.6 3.4 %collective-permute-start.16 = (f32[8,128]{1,0:T(8,128)S(1)}, f32[8,128]{1,0:T(8,128)S(1)}, u32[]{:S(2)}, u32[]{:S(2)}) collective-permute-start(f32[8,128]{1,0:T(8,128)S(1)} %get-tuple-element.68.refs_3_), channel_id=1, source_target_pairs={{0,1},{1,0},{2,3},{3,2},{4,5},{5,4},{6,7},{7,6},{8,9},{9,8},{10,11... | collective-permute-start | bytes 12296 | tf_op jit(solution)/shard_map/ppermute | solution.py:29
  60.2 4.4 %collective-permute-start.25 = (f32[8,128]{1,0:T(8,128)S(1)}, f32[8,128]{1,0:T(8,128)S(1)}, u32[]{:S(2)}, u32[]{:S(2)}) collective-permute-start(f32[8,128]{1,0:T(8,128)S(1)} %get-tuple-element.84.refs_8_.refs_13_.refs_3_), channel_id=1, source_target_pairs={{0,3},{1,2},{2,1},{3,0},{4,7},{5,6},{6,5},{7,4},{8,11},{9,10},{10,... | collective-permute-start | bytes 12296 | tf_op jit(solution)/shard_map/ppermute | solution.py:29
  61.4 3.6 %collective-permute-start.26 = (f32[8,128]{1,0:T(8,128)S(1)}, f32[8,128]{1,0:T(8,128)S(1)}, u32[]{:S(2)}, u32[]{:S(2)}) collective-permute-start(f32[8,128]{1,0:T(8,128)S(1)} %get-tuple-element.84.refs_8_.refs_13_.refs_3_), channel_id=1, source_target_pairs={{0,2},{1,3},{2,0},{3,1},{4,6},{5,7},{6,4},{7,5},{8,10},{9,11},{10,... | collective-permute-start | bytes 12296 | tf_op jit(solution)/shard_map/ppermute | solution.py:29
  61.9 3.1 %collective-permute-start.27 = (f32[8,128]{1,0:T(8,128)S(1)}, f32[8,128]{1,0:T(8,128)S(1)}, u32[]{:S(2)}, u32[]{:S(2)}) collective-permute-start(f32[8,128]{1,0:T(8,128)S(1)} %get-tuple-element.84.refs_8_.refs_13_.refs_3_), channel_id=1, source_target_pairs={{0,1},{1,0},{2,3},{3,2},{4,5},{5,4},{6,7},{7,6},{8,9},{9,8},{10,11... | collective-permute-start | bytes 12296 | tf_op jit(solution)/shard_map/ppermute | solution.py:29
  62.1 15.8 %collective-permute-start.28 = (bf16[64,1024]{1,0:T(8,128)(2,1)S(1)}, bf16[64,1024]{1,0:T(8,128)(2,1)S(1)}, u32[]{:S(2)}, u32[]{:S(2)}) collective-permute-start(bf16[64,1024]{1,0:T(8,128)(2,1)S(1)} %get-tuple-element.87), channel_id=1, source_target_pairs={{0,12},{4,8},{8,4},{12,0},{1,13},{5,9},{9,5},{13,1},{2,14},{6,10},... | collective-permute-start | bytes 393224 | tf_op jit(solution)/shard_map/ppermute | solution.py:29
  65.8 14.7 %collective-permute-start.29 = (bf16[64,1024]{1,0:T(8,128)(2,1)S(1)}, bf16[64,1024]{1,0:T(8,128)(2,1)S(1)}, u32[]{:S(2)}, u32[]{:S(2)}) collective-permute-start(bf16[64,1024]{1,0:T(8,128)(2,1)S(1)} %get-tuple-element.88), channel_id=1, source_target_pairs={{0,8},{4,12},{8,0},{12,4},{1,9},{5,13},{9,1},{13,5},{2,10},{6,14},... | collective-permute-start | bytes 393224 | tf_op jit(solution)/shard_map/ppermute | solution.py:29
  74.7 6.7 %collective-permute-start.30 = (bf16[64,1024]{1,0:T(8,128)(2,1)S(1)}, bf16[64,1024]{1,0:T(8,128)(2,1)S(1)}, u32[]{:S(2)}, u32[]{:S(2)}) collective-permute-start(bf16[64,1024]{1,0:T(8,128)(2,1)S(1)} %get-tuple-element.89), channel_id=1, source_target_pairs={{0,4},{4,0},{8,12},{12,8},{1,5},{5,1},{9,13},{13,9},{2,6},{6,2},{1... | collective-permute-start | bytes 393224 | tf_op jit(solution)/shard_map/ppermute | solution.py:29
  (5 other events, 9.1 us)

commit v16 on v13

--- a/solution.py
+++ b/solution.py
@@ -595,7 +595,7 @@
     for q, pieces in enumerate(chunks):
         rows, arrived = arrived[: len(pieces)], arrived[len(pieces) :]
         lhs = cross_rows(
-            weight, after[:1] + (arrived if q == 1 else []), rows, own_rows, pieces, classes, LARGE if q < 2 else SMALL
+            weight, after[:1], rows, own_rows, pieces, classes, LARGE if q != 1 else SMALL
         )
         groups = sum(p[2] for p in pieces) // (32 if q else 16)
         keep, *sends = lag_parts(
@@ -608,7 +608,7 @@
         corr, sums = lag_stats(scal, lag_scale, q, pieces, all_sums, own, more, observed)
         corrs.append(corr)
         all_sums = [sums]
-    sums = [swapped(sums, ("win", "freq"), peers, s) for s in range(peers)]
+    sums = [swapped(sums, ("win", "freq"), peers, s) for s in reversed(range(peers))]
     after = []
     numbered = list(enumerate(chunks))
     for group in (numbered[:0:-1], numbered[:1]):

time: 79.7 us -> 77.4 us (0.971)
  waiting for transfers between devices: 26.6 us -> 23.6 us
    ppermute x28, waiting for transfers between devices: 26.6 us -> 23.6 us  [swapped(): return lax.ppermute(value, axis, [(i, i ^ step) for i in range(size)])]
  transfers between devices with their start and end apart: 28 -> 28, of which waited for: 13 -> 14; matrix products, arithmetic and copies ran while one was open for 0% -> 0% of each run, Pallas kernels for 24% -> 24%
where the time goes in v16:
time: 77.4 us; the launch traced here: 77.1 us
  starting transfers between devices  25 us (32%)
  waiting for transfers between devices  23.6 us (30%)
  Pallas kernels  23.1 us (30%)
  local copies, waits for them, and re-layouts  4 us (5%)
  between operations  1.48 us (2%)
    ppermute x28, starting transfers between devices, swapped(): return lax.ppermute(value, axis, [(i, i ^ step) for i in range(size)])  25 us
    ppermute x28, waiting for transfers between devices, swapped(): return lax.ppermute(value, axis, [(i, i ^ step) for i in range(size)])  23.6 us
    pallas_call x3, Pallas kernels, lag_parts(): pl.pallas_call(functools.partial(lags_kernel, geometry, split, len(after)...  5.86 us
    pallas_call x1, Pallas kernels, normed_rows(): pl.pallas_call(functools.partial(normed_kernel, lag_total, chunks, len(su...  3.22 us
    pallas_call x1, Pallas kernels, gather_own(): pl.pallas_call(functools.partial(own_kernel, classes, parts), out_shape=[...  3.07 us
    unnamed x12, local copies, waits for them, and re-layouts  2.68 us
    pallas_call x3, Pallas kernels, lag_stats(): pl.pallas_call(functools.partial(stats_kernel, scale, q, pieces, len(more...  2.21 us
    pallas_call x3, Pallas kernels, add_cores(): pl.pallas_call(functools.partial(cores_kernel, len(after), len(more)), ou...  2.06 us
  transfers between devices with their start and end apart: 28, of which 14 were waited for; matrix products, arithmetic and copies ran while one was open for 0% of the time, Pallas kernels for 24%

profile of v16, /device:TPU:0, one launch (start us, length us, event | category | flops | bytes accessed | tf_op | source)
XLA Modules:
  0.0 77.1 jit_solution(3600362923251840144)
XLA Ops:
  0.7 1.3 %constant_dynamic-slice_fusion = (bf16[1,2,128,1024]{3,2,1,0:T(8,128)(2,1)S(1)}, bf16[1,2,128,1024]{3,2,1,0:T(8,128)(2,1)S(1)}) fusion(bf16[1,2,128,2048]{3,2,1,0:T(8,128)(2,1)} %param.8, s32[]{:T(128)S(6)} %select_n.7, s32[]{:T(128)S(6)} %select_n.6), kind=kLoop, calls=%fused_computation | loop fusion | bytes 2097160 | tf_op jit(solution)/shard_map/dynamic_slice | solution.py:555
  2.0 3.0 %collective-permute-start = (bf16[1,2,128,1024]{3,2,1,0:T(8,128)(2,1)S(1)}, bf16[1,2,128,1024]{3,2,1,0:T(8,128)(2,1)S(1)}, u32[]{:S(2)}, u32[]{:S(2)}) collective-permute-start(bf16[1,2,128,1024]{3,2,1,0:T(8,128)(2,1)S(1)} %get-tuple-element.90), channel_id=1, source_target_pairs={{0,2},{2,0},{1,3},{3,1},{4,6},{6,4},{5,7},{7,5},{8,10},{10,8},{9,1... | collective-permute-start | bytes 1572872 | tf_op jit(solution)/shard_map/ppermute | solution.py:29
  8.3 1.2 %index.1 = (s32[128]{0:T(128)S(1)}, s32[1,64]{1,0:T(1,128)S(1)}, s32[1,64]{1,0:T(1,128)S(1)}, s32[1,64]{1,0:T(1,128)S(1)}, s32[1,64]{1,0:T(1,128)S(1)}, /*index=5*/s32[4,64]{1,0:T(4,128)S(1)}) custom-call(s32[1]{0:T(128)S(6)} %copy.10.refs_0_, s32[4]{0:T(128)S(1)} %copy-done.4, s32[4]{0:T(128)S(1)} %bitcast.1, s32[4,64]{1,0:T(4,128)S(1)} %copy-done.2, ...), custom_call_target="tpu_custom_call" | custom-call | flops 1 | bytes 1 | tf_op jit(solution)/shard_map/index/pallas_call | solution.py:92
  9.5 3.7 %collective-permute-start.1 = (s32[1,64]{1,0:T(1,128)S(1)}, s32[1,64]{1,0:T(1,128)S(1)}, u32[]{:S(2)}, u32[]{:S(2)}) collective-permute-start(s32[1,64]{1,0:T(1,128)S(1)} %get-tuple-element.47), channel_id=1, source_target_pairs={{0,12},{4,8},{8,4},{12,0},{1,13},{5,9},{9,5},{13,1},{2,14},{6,10},... | collective-permute-start | bytes 776 | tf_op jit(solution)/shard_map/ppermute | solution.py:29
  13.2 0.8 %collective-permute-start.3 = (s32[1,64]{1,0:T(1,128)S(1)}, s32[1,64]{1,0:T(1,128)S(1)}, u32[]{:S(2)}, u32[]{:S(2)}) collective-permute-start(s32[1,64]{1,0:T(1,128)S(1)} %get-tuple-element.49), channel_id=1, source_target_pairs={{0,4},{4,0},{8,12},{12,8},{1,5},{5,1},{9,13},{13,9},{2,6},{6,2},{1... | collective-permute-start | bytes 776 | tf_op jit(solution)/shard_map/ppermute | solution.py:29
  14.9 2.7 %collective-permute-done.2.refs_3_.refs_1_ = s32[1,64]{1,0:T(1,128)S(1)} collective-permute-done((s32[1,64]{1,0:T(1,128)S(1)}, s32[1,64]{1,0:T(1,128)S(1)}, u32[]{:S(2)}, u32[]{:S(2)}) %collective-permute-start.2) | collective-permute-done | bytes 288 | tf_op jit(solution)/shard_map/ppermute | solution.py:29
  17.7 1.6 %rows.1 = (bf16[1,2,64,1024]{3,2,1,0:T(8,128)(2,1)S(1)}, bf16[1,2,64,1024]{3,2,1,0:T(8,128)(2,1)S(1)}, bf16[1,2,64,1024]{3,2,1,0:T(8,128)(2,1)S(1)}, bf16[1,2,64...) custom-call(s32[128]{0:T(128)S(1)} %get-tuple-element.46.scal, ...), custom_call_target="tpu_custom_call" | custom-call | flops 1 | bytes 1 | tf_op jit(solution)/shard_map/rows/pallas_call | solution.py:175
  19.2 1.1 %collective-permute-start.4 = (bf16[1,2,64,1024]{3,2,1,0:T(8,128)(2,1)S(1)}, bf16[1,2,64,1024]{3,2,1,0:T(8,128)(2,1)S(1)}, u32[]{:S(2)}, u32[]{:S(2)}) collective-permute-start(bf16[1,2,64,1024]{3,2,1,0:T(8,128)(2,1)S(1)} %get-tuple-element.52), channel_id=1, source_target_pairs={{0,4},{4,0},{8,12},{12,8},{1,5},{5,1},{9,13},{13,9},{2,6},{6,2},{1... | collective-permute-start | bytes 786440 | tf_op jit(solution)/shard_map/ppermute | solution.py:29
  20.4 2.6 %collective-permute-start.14 = (bf16[1,2,64,1024]{3,2,1,0:T(8,128)(2,1)S(1)}, bf16[1,2,64,1024]{3,2,1,0:T(8,128)(2,1)S(1)}, u32[]{:S(2)}, u32[]{:S(2)}) collective-permute-start(bf16[1,2,64,1024]{3,2,1,0:T(8,128)(2,1)S(1)} %get-tuple-element.69), channel_id=1, source_target_pairs={{0,8},{4,12},{8,0},{12,4},{1,9},{5,13},{9,1},{13,5},{2,10},{6,14},... | collective-permute-start | bytes 786440 | tf_op jit(solution)/shard_map/ppermute | solution.py:29
  23.7 3.1 %own.1 = (bf16[4,1,2,64,1024]{4,3,2,1,0:T(8,128)(2,1)S(1)}, bf16[8,256,1024]{2,1,0:T(8,128)(2,1)S(1)}) custom-call(s32[128]{0:T(128)S(1)} %get-tuple-element.46.scal, bf16[1,2,128,1024]{3,2,1,0:T(8,128)(2,1)S(1)} %get-tuple-element.53.kept, s32[4,64]{1,0:T(4,128)S(1)} %get-tuple-element.54.rec_ids, f32[2,56,1024]{2,1,0:T(8,128)S(1)} %copy-done.1), custom_call_target="tpu_custom_call" | custom-call | flops 1 | bytes 1 | tf_op jit(solution)/shard_map/own/pallas_call | solution.py:204
  26.8 3.7 %collective-permute-done.4.refs_1_ = bf16[1,2,64,1024]{3,2,1,0:T(8,128)(2,1)S(1)} collective-permute-done((bf16[1,2,64,1024]{3,2,1,0:T(8,128)(2,1)S(1)}, bf16[1,2,64,1024]{3,2,1,0:T(8,128)(2,1)S(1)}, u32[]{:S(2)}, u32[]{:S(2)}) %collective-permute-start.4) | collective-permute-done | bytes 262176 | tf_op jit(solution)/shard_map/ppermute | solution.py:29
  30.7 2.4 %lags.3 = (f32[2,128,1024]{2,1,0:T(8,128)S(1)}, bf16[2,16,1024]{2,1,0:T(8,128)(2,1)S(1)}, bf16[2,16,1024]{2,1,0:T(8,128)(2,1)S(1)}, bf16[2,16,1024]{2,1,0:T(8,12...) custom-call(s32[128]{0:T(128)S(1)} %get-tuple-element.46.scal, ...), custom_call_target="tpu_custom_call" | custom-call | flops 20000000000 | bytes 1048576 | tf_op jit(solution)/shard_map/lags/pallas_call | solution.py:331
  36.2 0.7 collective-permute-done.11.refs_7_
  37.1 0.8 %cores.3 = (f32[128,1024]{1,0:T(8,128)S(1)}, bf16[128,1024]{1,0:T(8,128)(2,1)S(1)}) custom-call(s32[128]{0:T(128)S(1)} %get-tuple-element.46.scal, f32[2,128,1024]{2,1,0:T(8,128)S(1)} %get-tuple-element.57.refs_0_, bf16[2,16,1024]{2,1,0:T(8,128)(2,1)S(1)} %collective-permute-done.5.refs_1_, bf16[2,16,1024]{2,1,0:T(8,128)(2,1)S(1)} %collective-permute-done.6.refs_2_, ...), custom_call_target="tpu_custom_call" | custom-call | flops 1 | bytes 1 | tf_op jit(solution)/shard_map/cores/pallas_call | solution.py:366
  37.9 3.8 %collective-permute-done.14.refs_1_ = bf16[1,2,64,1024]{3,2,1,0:T(8,128)(2,1)S(1)} collective-permute-done((bf16[1,2,64,1024]{3,2,1,0:T(8,128)(2,1)S(1)}, bf16[1,2,64,1024]{3,2,1,0:T(8,128)(2,1)S(1)}, u32[]{:S(2)}, u32[]{:S(2)}) %collective-permute-start.14) | collective-permute-done | bytes 262176 | tf_op jit(solution)/shard_map/ppermute | solution.py:29
  41.9 1.6 %collective-permute-start.13 = (bf16[128,1024]{1,0:T(8,128)(2,1)S(1)}, bf16[128,1024]{1,0:T(8,128)(2,1)S(1)}, u32[]{:S(2)}, u32[]{:S(2)}) collective-permute-start(bf16[128,1024]{1,0:T(8,128)(2,1)S(1)} %get-tuple-element.67), channel_id=1, source_target_pairs={{0,2},{2,0},{1,3},{3,1},{4,6},{6,4},{5,7},{7,5},{8,10},{10,8},{9,1... | collective-permute-start | bytes 786440 | tf_op jit(solution)/shard_map/ppermute | solution.py:29
  43.5 1.7 %lags.4 = (f32[2,64,1024]{2,1,0:T(8,128)S(1)}, bf16[2,32,1024]{2,1,0:T(8,128)(2,1)S(1)}, bf16[2,32,1024]{2,1,0:T(8,128)(2,1)S(1)}) custom-call(s32[128]{0:T(128)S(1)} %get-tuple-element.46.scal, bf16[8,128,256]{2,1,0:T(8,128)(2,1)S(1)} %cross.4.refs_0_, bf16[8,256,1024]{2,1,0:T(8,128)(2,1)S(1)} %get-tuple-element.56.refs_1_), custom_call_target="tpu_custom_call" | custom-call | flops 1 | bytes 1 | tf_op jit(solution)/shard_map/lags/pallas_call | solution.py:331
  45.9 1.7 %lags.5 = (f32[2,64,1024]{2,1,0:T(8,128)S(1)}, bf16[2,32,1024]{2,1,0:T(8,128)(2,1)S(1)}, bf16[2,32,1024]{2,1,0:T(8,128)(2,1)S(1)}) custom-call(s32[128]{0:T(128)S(1)} %get-tuple-element.46.scal, bf16[8,128,256]{2,1,0:T(8,128)(2,1)S(1)} %cross.5.refs_0_, bf16[8,256,1024]{2,1,0:T(8,128)(2,1)S(1)} %get-tuple-element.56.refs_1_), custom_call_target="tpu_custom_call" | custom-call | flops 1 | bytes 1 | tf_op jit(solution)/shard_map/lags/pallas_call | solution.py:331
  49.0 1.6 %collective-permute-start.17 = (bf16[64,1024]{1,0:T(8,128)(2,1)S(1)}, bf16[64,1024]{1,0:T(8,128)(2,1)S(1)}, u32[]{:S(2)}, u32[]{:S(2)}) collective-permute-start(bf16[64,1024]{1,0:T(8,128)(2,1)S(1)} %get-tuple-element.74), channel_id=1, source_target_pairs={{0,2},{2,0},{1,3},{3,1},{4,6},{6,4},{5,7},{7,5},{8,10},{10,8},{9,1... | collective-permute-start | bytes 393224 | tf_op jit(solution)/shard_map/ppermute | solution.py:29
  51.8 0.8 stats.3
  52.5 2.9 %collective-permute-done.17.refs_2_ = bf16[64,1024]{1,0:T(8,128)(2,1)S(1)} collective-permute-done((bf16[64,1024]{1,0:T(8,128)(2,1)S(1)}, bf16[64,1024]{1,0:T(8,128)(2,1)S(1)}, u32[]{:S(2)}, u32[]{:S(2)}) %collective-permute-start.17) | collective-permute-done | bytes 131104 | tf_op jit(solution)/shard_map/ppermute | solution.py:29
  56.1 1.1 %collective-permute-done.21.refs_2_ = bf16[64,1024]{1,0:T(8,128)(2,1)S(1)} collective-permute-done((bf16[64,1024]{1,0:T(8,128)(2,1)S(1)}, bf16[64,1024]{1,0:T(8,128)(2,1)S(1)}, u32[]{:S(2)}, u32[]{:S(2)}) %collective-permute-start.21) | collective-permute-done | bytes 131104 | tf_op jit(solution)/shard_map/ppermute | solution.py:29
  58.0 1.1 %collective-permute-start.23 = (f32[8,128]{1,0:T(8,128)S(1)}, f32[8,128]{1,0:T(8,128)S(1)}, u32[]{:S(2)}, u32[]{:S(2)}) collective-permute-start(f32[8,128]{1,0:T(8,128)S(1)} %get-tuple-element.82.refs_3_.refs_4_), channel_id=1, source_target_pairs={{0,2},{1,3},{2,0},{3,1},{4,6},{5,7},{6,4},{7,5},{8,10},{9,11},{10,... | collective-permute-start | bytes 12296 | tf_op jit(solution)/shard_map/ppermute | solution.py:29
  59.1 0.7 collective-permute-start.24
  59.8 1.2 %collective-permute-done.22.refs_0_.refs_1_ = f32[8,128]{1,0:T(8,128)S(1)} collective-permute-done((f32[8,128]{1,0:T(8,128)S(1)}, f32[8,128]{1,0:T(8,128)S(1)}, u32[]{:S(2)}, u32[]{:S(2)}) %collective-permute-start.22) | collective-permute-done | bytes 4128 | tf_op jit(solution)/shard_map/ppermute | solution.py:29
  61.7 0.8 %gradient.2 = (bf16[64,1024]{1,0:T(8,128)(2,1)S(1)}, bf16[64,1024]{1,0:T(8,128)(2,1)S(1)}) custom-call(s32[128]{0:T(128)S(1)} %get-tuple-element.46.scal, f32[8,128]{1,0:T(8,128)S(1)} %collective-permute-done.22.refs_0_.refs_1_, f32[8,128]{1,0:T(8,128)S(1)} %collective-permute-done.23.refs_1_.refs_2_, f32[8,128]{1,0:T(8,128)S(1)} %collective-permute-done.24.refs_2_.refs_3_, ...), custom_call_target="tpu_custom_call" | custom-call | flops 1 | bytes 1 | tf_op jit(solution)/shard_map/gradient/pallas_call | solution.py:470
  62.5 2.5 %collective-permute-start.25 = (bf16[64,1024]{1,0:T(8,128)(2,1)S(1)}, bf16[64,1024]{1,0:T(8,128)(2,1)S(1)}, u32[]{:S(2)}, u32[]{:S(2)}) collective-permute-start(bf16[64,1024]{1,0:T(8,128)(2,1)S(1)} %get-tuple-element.86.refs_0_), channel_id=1, source_target_pairs={{0,12},{4,8},{8,4},{12,0},{1,13},{5,9},{9,5},{13,1},{2,14},{6,10},... | collective-permute-start | bytes 393224 | tf_op jit(solution)/shard_map/ppermute | solution.py:29
  65.0 0.8 %gradient.3 = (bf16[64,1024]{1,0:T(8,128)(2,1)S(1)}, bf16[64,1024]{1,0:T(8,128)(2,1)S(1)}) custom-call(s32[128]{0:T(128)S(1)} %get-tuple-element.46.scal, bf16[64,1024]{1,0:T(8,128)(2,1)S(1)} %get-tuple-element.86.refs_0_, f32[8,128]{1,0:T(8,128)S(1)} %collective-permute-done.22.refs_0_.refs_1_, f32[8,128]{1,0:T(8,128)S(1)} %collective-permute-done.23.refs_1_.refs_2_, ...), custom_call_target="tpu_custom_call" | custom-call | flops 1 | bytes 1 | tf_op jit(solution)/shard_map/gradient/pallas_call | solution.py:470
  65.8 2.0 %collective-permute-start.27 = (bf16[64,1024]{1,0:T(8,128)(2,1)S(1)}, bf16[64,1024]{1,0:T(8,128)(2,1)S(1)}, u32[]{:S(2)}, u32[]{:S(2)}) collective-permute-start(bf16[64,1024]{1,0:T(8,128)(2,1)S(1)} %get-tuple-element.89), channel_id=1, source_target_pairs={{0,4},{4,0},{8,12},{12,8},{1,5},{5,1},{9,13},{13,9},{2,6},{6,2},{1... | collective-permute-start | bytes 393224 | tf_op jit(solution)/shard_map/ppermute | solution.py:29
  67.8 3.2 %normed.1 = f32[4,64,1024]{2,1,0:T(8,128)} custom-call(s32[128]{0:T(128)S(1)} %get-tuple-element.46.scal, f32[8,128]{1,0:T(8,128)S(1)} %collective-permute-done.22.refs_0_.refs_1_, f32[8,128]{1,0:T(8,128)S(1)} %collective-permute-done.23.refs_1_.refs_2_, f32[8,128]{1,0:T(8,128)S(1)} %collective-permute-done.24.refs_2_.refs_3_, ...), custom_call_target="tpu_custom_call" | custom-call | flops 1 | bytes 1 | tf_op jit(solution)/shard_map/normed/pallas_call | solution.py:501
  71.1 5.0 %collective-permute-done.26.refs_5_ = bf16[64,1024]{1,0:T(8,128)(2,1)S(1)} collective-permute-done((bf16[64,1024]{1,0:T(8,128)(2,1)S(1)}, bf16[64,1024]{1,0:T(8,128)(2,1)S(1)}, u32[]{:S(2)}, u32[]{:S(2)}) %collective-permute-start.26) | collective-permute-done | bytes 131104 | tf_op jit(solution)/shard_map/ppermute | solution.py:29
  76.1 1.1 %adjoint.1 = f32[128,1024]{1,0:T(8,128)} custom-call(s32[1,64]{1,0:T(1,128)S(1)} %collective-permute-done.1.refs_2_.refs_0_, s32[1,64]{1,0:T(1,128)S(1)} %collective-permute-done.2.refs_3_.refs_1_, s32[1,64]{1,0:T(1,128)S(1)} %get-tuple-element.50.refs_5_.refs_2_, s32[1,64]{1,0:T(1,128)S(1)} %collective-permute-done.3.refs_4_.refs_3_, ...), custom_call_target="tpu_custom_call" | custom-call | flops 1 | bytes 1 | tf_op jit(solution)/shard_map/adjoint/pallas_call | solution.py:525
  (57 shorter events, 13.4 us)
Async XLA Ops:
  0.6 23.1 %copy-start.1 = (f32[2,56,1024]{2,1,0:T(8,128)S(1)}, f32[2,56,1024]{2,1,0:T(8,128)}, u32[]{:S(2)}) copy-start(f32[2,56,1024]{2,1,0:T(8,128)} %constant.16.clone.trig) | copy-start | bytes 1376260
  2.0 15.7 %collective-permute-start = (bf16[1,2,128,1024]{3,2,1,0:T(8,128)(2,1)S(1)}, bf16[1,2,128,1024]{3,2,1,0:T(8,128)(2,1)S(1)}, u32[]{:S(2)}, u32[]{:S(2)}) collective-permute-start(bf16[1,2,128,1024]{3,2,1,0:T(8,128)(2,1)S(1)} %get-tuple-element.90), channel_id=1, source_target_pairs={{0,2},{2,0},{1,3},{3,1},{4,6},{6,4},{5,7},{7,5},{8,10},{10,8},{9,1... | collective-permute-start | bytes 1572872 | tf_op jit(solution)/shard_map/ppermute | solution.py:29
  5.6 0.7 copy-start.2
  6.3 0.7 copy-start.3
  9.5 5.4 %collective-permute-start.1 = (s32[1,64]{1,0:T(1,128)S(1)}, s32[1,64]{1,0:T(1,128)S(1)}, u32[]{:S(2)}, u32[]{:S(2)}) collective-permute-start(s32[1,64]{1,0:T(1,128)S(1)} %get-tuple-element.47), channel_id=1, source_target_pairs={{0,12},{4,8},{8,4},{12,0},{1,13},{5,9},{9,5},{13,1},{2,14},{6,10},... | collective-permute-start | bytes 776 | tf_op jit(solution)/shard_map/ppermute | solution.py:29
  13.2 4.4 %collective-permute-start.2 = (s32[1,64]{1,0:T(1,128)S(1)}, s32[1,64]{1,0:T(1,128)S(1)}, u32[]{:S(2)}, u32[]{:S(2)}) collective-permute-start(s32[1,64]{1,0:T(1,128)S(1)} %get-tuple-element.48), channel_id=1, source_target_pairs={{0,8},{4,12},{8,0},{12,4},{1,9},{5,13},{9,1},{13,5},{2,10},{6,14},... | collective-permute-start | bytes 776 | tf_op jit(solution)/shard_map/ppermute | solution.py:29
  13.2 4.4 %collective-permute-start.3 = (s32[1,64]{1,0:T(1,128)S(1)}, s32[1,64]{1,0:T(1,128)S(1)}, u32[]{:S(2)}, u32[]{:S(2)}) collective-permute-start(s32[1,64]{1,0:T(1,128)S(1)} %get-tuple-element.49), channel_id=1, source_target_pairs={{0,4},{4,0},{8,12},{12,8},{1,5},{5,1},{9,13},{13,9},{2,6},{6,2},{1... | collective-permute-start | bytes 776 | tf_op jit(solution)/shard_map/ppermute | solution.py:29
  19.2 11.2 %collective-permute-start.4 = (bf16[1,2,64,1024]{3,2,1,0:T(8,128)(2,1)S(1)}, bf16[1,2,64,1024]{3,2,1,0:T(8,128)(2,1)S(1)}, u32[]{:S(2)}, u32[]{:S(2)}) collective-permute-start(bf16[1,2,64,1024]{3,2,1,0:T(8,128)(2,1)S(1)} %get-tuple-element.52), channel_id=1, source_target_pairs={{0,4},{4,0},{8,12},{12,8},{1,5},{5,1},{9,13},{13,9},{2,6},{6,2},{1... | collective-permute-start | bytes 786440 | tf_op jit(solution)/shard_map/ppermute | solution.py:29
  20.4 21.4 %collective-permute-start.14 = (bf16[1,2,64,1024]{3,2,1,0:T(8,128)(2,1)S(1)}, bf16[1,2,64,1024]{3,2,1,0:T(8,128)(2,1)S(1)}, u32[]{:S(2)}, u32[]{:S(2)}) collective-permute-start(bf16[1,2,64,1024]{3,2,1,0:T(8,128)(2,1)S(1)} %get-tuple-element.69), channel_id=1, source_target_pairs={{0,8},{4,12},{8,0},{12,4},{1,9},{5,13},{9,1},{13,5},{2,10},{6,14},... | collective-permute-start | bytes 786440 | tf_op jit(solution)/shard_map/ppermute | solution.py:29
  23.0 22.8 %collective-permute-start.18 = (bf16[1,2,64,1024]{3,2,1,0:T(8,128)(2,1)S(1)}, bf16[1,2,64,1024]{3,2,1,0:T(8,128)(2,1)S(1)}, u32[]{:S(2)}, u32[]{:S(2)}) collective-permute-start(bf16[1,2,64,1024]{3,2,1,0:T(8,128)(2,1)S(1)} %get-tuple-element.76), channel_id=1, source_target_pairs={{0,12},{4,8},{8,4},{12,0},{1,13},{5,9},{9,5},{13,1},{2,14},{6,10},... | collective-permute-start | bytes 786440 | tf_op jit(solution)/shard_map/ppermute | solution.py:29
  33.1 1.3 %collective-permute-start.5 = (bf16[2,16,1024]{2,1,0:T(8,128)(2,1)S(1)}, bf16[2,16,1024]{2,1,0:T(8,128)(2,1)S(1)}, u32[]{:S(2)}, u32[]{:S(2)}) collective-permute-start(bf16[2,16,1024]{2,1,0:T(8,128)(2,1)S(1)} %get-tuple-element.58), channel_id=1, source_target_pairs={{0,1},{1,0},{2,3},{3,2},{4,5},{5,4},{6,7},{7,6},{8,9},{9,8},{10,11... | collective-permute-start | bytes 196616 | tf_op jit(solution)/shard_map/ppermute | solution.py:29
  33.2 1.4 %collective-permute-start.6 = (bf16[2,16,1024]{2,1,0:T(8,128)(2,1)S(1)}, bf16[2,16,1024]{2,1,0:T(8,128)(2,1)S(1)}, u32[]{:S(2)}, u32[]{:S(2)}) collective-permute-start(bf16[2,16,1024]{2,1,0:T(8,128)(2,1)S(1)} %get-tuple-element.59), channel_id=1, source_target_pairs={{0,1},{1,0},{2,3},{3,2},{4,5},{5,4},{6,7},{7,6},{8,9},{9,8},{10,11... | collective-permute-start | bytes 196616 | tf_op jit(solution)/shard_map/ppermute | solution.py:29
  33.7 1.3 %collective-permute-start.7 = (bf16[2,16,1024]{2,1,0:T(8,128)(2,1)S(1)}, bf16[2,16,1024]{2,1,0:T(8,128)(2,1)S(1)}, u32[]{:S(2)}, u32[]{:S(2)}) collective-permute-start(bf16[2,16,1024]{2,1,0:T(8,128)(2,1)S(1)} %get-tuple-element.60), channel_id=1, source_target_pairs={{0,1},{1,0},{2,3},{3,2},{4,5},{5,4},{6,7},{7,6},{8,9},{9,8},{10,11... | collective-permute-start | bytes 196616 | tf_op jit(solution)/shard_map/ppermute | solution.py:29
  34.5 1.3 %collective-permute-start.8 = (bf16[2,16,1024]{2,1,0:T(8,128)(2,1)S(1)}, bf16[2,16,1024]{2,1,0:T(8,128)(2,1)S(1)}, u32[]{:S(2)}, u32[]{:S(2)}) collective-permute-start(bf16[2,16,1024]{2,1,0:T(8,128)(2,1)S(1)} %get-tuple-element.61), channel_id=1, source_target_pairs={{0,1},{1,0},{2,3},{3,2},{4,5},{5,4},{6,7},{7,6},{8,9},{9,8},{10,11... | collective-permute-start | bytes 196616 | tf_op jit(solution)/shard_map/ppermute | solution.py:29
  34.6 1.3 %collective-permute-start.9 = (bf16[2,16,1024]{2,1,0:T(8,128)(2,1)S(1)}, bf16[2,16,1024]{2,1,0:T(8,128)(2,1)S(1)}, u32[]{:S(2)}, u32[]{:S(2)}) collective-permute-start(bf16[2,16,1024]{2,1,0:T(8,128)(2,1)S(1)} %get-tuple-element.62), channel_id=1, source_target_pairs={{0,1},{1,0},{2,3},{3,2},{4,5},{5,4},{6,7},{7,6},{8,9},{9,8},{10,11... | collective-permute-start | bytes 196616 | tf_op jit(solution)/shard_map/ppermute | solution.py:29
  35.0 1.3 %collective-permute-start.10 = (bf16[2,16,1024]{2,1,0:T(8,128)(2,1)S(1)}, bf16[2,16,1024]{2,1,0:T(8,128)(2,1)S(1)}, u32[]{:S(2)}, u32[]{:S(2)}) collective-permute-start(bf16[2,16,1024]{2,1,0:T(8,128)(2,1)S(1)} %get-tuple-element.63), channel_id=1, source_target_pairs={{0,1},{1,0},{2,3},{3,2},{4,5},{5,4},{6,7},{7,6},{8,9},{9,8},{10,11... | collective-permute-start | bytes 196616 | tf_op jit(solution)/shard_map/ppermute | solution.py:29
  35.7 1.3 %collective-permute-start.11 = (bf16[2,16,1024]{2,1,0:T(8,128)(2,1)S(1)}, bf16[2,16,1024]{2,1,0:T(8,128)(2,1)S(1)}, u32[]{:S(2)}, u32[]{:S(2)}) collective-permute-start(bf16[2,16,1024]{2,1,0:T(8,128)(2,1)S(1)} %get-tuple-element.64), channel_id=1, source_target_pairs={{0,1},{1,0},{2,3},{3,2},{4,5},{5,4},{6,7},{7,6},{8,9},{9,8},{10,11... | collective-permute-start | bytes 196616 | tf_op jit(solution)/shard_map/ppermute | solution.py:29
  35.9 1.3 %collective-permute-start.12 = (bf16[2,16,1024]{2,1,0:T(8,128)(2,1)S(1)}, bf16[2,16,1024]{2,1,0:T(8,128)(2,1)S(1)}, u32[]{:S(2)}, u32[]{:S(2)}) collective-permute-start(bf16[2,16,1024]{2,1,0:T(8,128)(2,1)S(1)} %get-tuple-element.65), channel_id=1, source_target_pairs={{0,1},{1,0},{2,3},{3,2},{4,5},{5,4},{6,7},{7,6},{8,9},{9,8},{10,11... | collective-permute-start | bytes 196616 | tf_op jit(solution)/shard_map/ppermute | solution.py:29
  41.9 6.4 %collective-permute-start.13 = (bf16[128,1024]{1,0:T(8,128)(2,1)S(1)}, bf16[128,1024]{1,0:T(8,128)(2,1)S(1)}, u32[]{:S(2)}, u32[]{:S(2)}) collective-permute-start(bf16[128,1024]{1,0:T(8,128)(2,1)S(1)} %get-tuple-element.67), channel_id=1, source_target_pairs={{0,2},{2,0},{1,3},{3,1},{4,6},{6,4},{5,7},{7,5},{8,10},{10,8},{9,1... | collective-permute-start | bytes 786440 | tf_op jit(solution)/shard_map/ppermute | solution.py:29
  45.2 3.1 %collective-permute-start.15 = (bf16[2,32,1024]{2,1,0:T(8,128)(2,1)S(1)}, bf16[2,32,1024]{2,1,0:T(8,128)(2,1)S(1)}, u32[]{:S(2)}, u32[]{:S(2)}) collective-permute-start(bf16[2,32,1024]{2,1,0:T(8,128)(2,1)S(1)} %get-tuple-element.71), channel_id=1, source_target_pairs={{0,1},{1,0},{2,3},{3,2},{4,5},{5,4},{6,7},{7,6},{8,9},{9,8},{10,11... | collective-permute-start | bytes 393224 | tf_op jit(solution)/shard_map/ppermute | solution.py:29
  45.3 3.0 %collective-permute-start.16 = (bf16[2,32,1024]{2,1,0:T(8,128)(2,1)S(1)}, bf16[2,32,1024]{2,1,0:T(8,128)(2,1)S(1)}, u32[]{:S(2)}, u32[]{:S(2)}) collective-permute-start(bf16[2,32,1024]{2,1,0:T(8,128)(2,1)S(1)} %get-tuple-element.72), channel_id=1, source_target_pairs={{0,1},{1,0},{2,3},{3,2},{4,5},{5,4},{6,7},{7,6},{8,9},{9,8},{10,11... | collective-permute-start | bytes 393224 | tf_op jit(solution)/shard_map/ppermute | solution.py:29
  45.9 5.9 %copy-start = (f32[4,64,1024]{2,1,0:T(8,128)S(1)}, f32[4,64,1024]{2,1,0:T(8,128)}, u32[]{:S(2)}) copy-start(f32[4,64,1024]{2,1,0:T(8,128)} %refs_7_.3) | copy-start | bytes 3145732
  47.7 2.9 %collective-permute-start.19 = (bf16[2,32,1024]{2,1,0:T(8,128)(2,1)S(1)}, bf16[2,32,1024]{2,1,0:T(8,128)(2,1)S(1)}, u32[]{:S(2)}, u32[]{:S(2)}) collective-permute-start(bf16[2,32,1024]{2,1,0:T(8,128)(2,1)S(1)} %get-tuple-element.78), channel_id=1, source_target_pairs={{0,1},{1,0},{2,3},{3,2},{4,5},{5,4},{6,7},{7,6},{8,9},{9,8},{10,11... | collective-permute-start | bytes 393224 | tf_op jit(solution)/shard_map/ppermute | solution.py:29
  47.8 2.7 %collective-permute-start.20 = (bf16[2,32,1024]{2,1,0:T(8,128)(2,1)S(1)}, bf16[2,32,1024]{2,1,0:T(8,128)(2,1)S(1)}, u32[]{:S(2)}, u32[]{:S(2)}) collective-permute-start(bf16[2,32,1024]{2,1,0:T(8,128)(2,1)S(1)} %get-tuple-element.79), channel_id=1, source_target_pairs={{0,1},{1,0},{2,3},{3,2},{4,5},{5,4},{6,7},{7,6},{8,9},{9,8},{10,11... | collective-permute-start | bytes 393224 | tf_op jit(solution)/shard_map/ppermute | solution.py:29
  49.0 6.4 %collective-permute-start.17 = (bf16[64,1024]{1,0:T(8,128)(2,1)S(1)}, bf16[64,1024]{1,0:T(8,128)(2,1)S(1)}, u32[]{:S(2)}, u32[]{:S(2)}) collective-permute-start(bf16[64,1024]{1,0:T(8,128)(2,1)S(1)} %get-tuple-element.74), channel_id=1, source_target_pairs={{0,2},{2,0},{1,3},{3,1},{4,6},{6,4},{5,7},{7,5},{8,10},{10,8},{9,1... | collective-permute-start | bytes 393224 | tf_op jit(solution)/shard_map/ppermute | solution.py:29
  51.2 6.1 %collective-permute-start.21 = (bf16[64,1024]{1,0:T(8,128)(2,1)S(1)}, bf16[64,1024]{1,0:T(8,128)(2,1)S(1)}, u32[]{:S(2)}, u32[]{:S(2)}) collective-permute-start(bf16[64,1024]{1,0:T(8,128)(2,1)S(1)} %get-tuple-element.81), channel_id=1, source_target_pairs={{0,2},{2,0},{1,3},{3,1},{4,6},{6,4},{5,7},{7,5},{8,10},{10,8},{9,1... | collective-permute-start | bytes 393224 | tf_op jit(solution)/shard_map/ppermute | solution.py:29
  58.0 3.0 %collective-permute-start.22 = (f32[8,128]{1,0:T(8,128)S(1)}, f32[8,128]{1,0:T(8,128)S(1)}, u32[]{:S(2)}, u32[]{:S(2)}) collective-permute-start(f32[8,128]{1,0:T(8,128)S(1)} %get-tuple-element.82.refs_3_.refs_4_), channel_id=1, source_target_pairs={{0,3},{1,2},{2,1},{3,0},{4,7},{5,6},{6,5},{7,4},{8,11},{9,10},{10,... | collective-permute-start | bytes 12296 | tf_op jit(solution)/shard_map/ppermute | solution.py:29
  58.0 3.7 %collective-permute-start.23 = (f32[8,128]{1,0:T(8,128)S(1)}, f32[8,128]{1,0:T(8,128)S(1)}, u32[]{:S(2)}, u32[]{:S(2)}) collective-permute-start(f32[8,128]{1,0:T(8,128)S(1)} %get-tuple-element.82.refs_3_.refs_4_), channel_id=1, source_target_pairs={{0,2},{1,3},{2,0},{3,1},{4,6},{5,7},{6,4},{7,5},{8,10},{9,11},{10,... | collective-permute-start | bytes 12296 | tf_op jit(solution)/shard_map/ppermute | solution.py:29
  59.1 2.6 %collective-permute-start.24 = (f32[8,128]{1,0:T(8,128)S(1)}, f32[8,128]{1,0:T(8,128)S(1)}, u32[]{:S(2)}, u32[]{:S(2)}) collective-permute-start(f32[8,128]{1,0:T(8,128)S(1)} %get-tuple-element.82.refs_3_.refs_4_), channel_id=1, source_target_pairs={{0,1},{1,0},{2,3},{3,2},{4,5},{5,4},{6,7},{7,6},{8,9},{9,8},{10,11... | collective-permute-start | bytes 12296 | tf_op jit(solution)/shard_map/ppermute | solution.py:29
  62.5 8.6 %collective-permute-start.25 = (bf16[64,1024]{1,0:T(8,128)(2,1)S(1)}, bf16[64,1024]{1,0:T(8,128)(2,1)S(1)}, u32[]{:S(2)}, u32[]{:S(2)}) collective-permute-start(bf16[64,1024]{1,0:T(8,128)(2,1)S(1)} %get-tuple-element.86.refs_0_), channel_id=1, source_target_pairs={{0,12},{4,8},{8,4},{12,0},{1,13},{5,9},{9,5},{13,1},{2,14},{6,10},... | collective-permute-start | bytes 393224 | tf_op jit(solution)/shard_map/ppermute | solution.py:29
  65.0 11.1 %collective-permute-start.26 = (bf16[64,1024]{1,0:T(8,128)(2,1)S(1)}, bf16[64,1024]{1,0:T(8,128)(2,1)S(1)}, u32[]{:S(2)}, u32[]{:S(2)}) collective-permute-start(bf16[64,1024]{1,0:T(8,128)(2,1)S(1)} %get-tuple-element.87), channel_id=1, source_target_pairs={{0,8},{4,12},{8,0},{12,4},{1,9},{5,13},{9,1},{13,5},{2,10},{6,14},... | collective-permute-start | bytes 393224 | tf_op jit(solution)/shard_map/ppermute | solution.py:29
  65.8 10.2 %collective-permute-start.27 = (bf16[64,1024]{1,0:T(8,128)(2,1)S(1)}, bf16[64,1024]{1,0:T(8,128)(2,1)S(1)}, u32[]{:S(2)}, u32[]{:S(2)}) collective-permute-start(bf16[64,1024]{1,0:T(8,128)(2,1)S(1)} %get-tuple-element.89), channel_id=1, source_target_pairs={{0,4},{4,0},{8,12},{12,8},{1,5},{5,1},{9,13},{13,9},{2,6},{6,2},{1... | collective-permute-start | bytes 393224 | tf_op jit(solution)/shard_map/ppermute | solution.py:29
  (2 other events, 1.3 us)

commit v17 on v16

--- a/solution.py
+++ b/solution.py
@@ -341,6 +341,34 @@
     )(scal, *after, lhs, table)
 
 
+def cross_lags_kernel(geometry, split, skip, pieces, scal, weight, *refs):
+    count = len(pieces) + 1
+    rows, table, refs = refs[skip : skip + count], refs[skip + count], refs[skip + count + 1 :]
+    outs, lhs, sums = refs[: split + 1], refs[split + 1], refs[split + 2 :]
+    cross_kernel(pieces, 0, weight, *rows, lhs)
+    lags_kernel(geometry, split, 0, scal, lhs, table, *outs, *sums)
+
+
+def cross_lag_parts(
+    scal, weight, after, rows, own, pieces, table, geometry, columns, lag_dev, split, effort
+):
+    classes, span = geometry[:2]
+    count = sum(p[2] for p in pieces)
+    shape = lambda rows: (columns, rows, lag_dev)
+    return pl.pallas_call(
+        functools.partial(cross_lags_kernel, geometry, split, len(after), pieces),
+        out_shape=[jax.ShapeDtypeStruct(shape(count), F32)]
+        + [jax.ShapeDtypeStruct(shape(count // split), BF16)] * split,
+        in_specs=[SMEM] * 2 + [ANY] * len(after) + [VMEM] * (len(rows) + 2),
+        out_specs=[VMEM] * (split + 1),
+        scratch_shapes=[pltpu.VMEM((classes, 2 * count, 2 * LANES), BF16)]
+        + [pltpu.VMEM((2 * columns, count, lag_dev), F32)] * (span != lag_dev),
+        compiler_params=params(16),
+        cost_estimate=effort,
+        name="cross_lags",
+    )(scal, weight, *after, *rows, own, table)
+
+
 def cores_kernel(skip, split, scal, *refs):
     keep, *refs = refs[skip:]
     more, own, sends = refs[:split], refs[split], refs[split + 1 :]
@@ -594,13 +622,27 @@
     after = []
     for q, pieces in enumerate(chunks):
         rows, arrived = arrived[: len(pieces)], arrived[len(pieces) :]
-        lhs = cross_rows(
-            weight, after[:1], rows, own_rows, pieces, classes, LARGE if q != 1 else SMALL
-        )
         groups = sum(p[2] for p in pieces) // (32 if q else 16)
-        keep, *sends = lag_parts(
-            scal, [], lhs, table, geometry, columns, lag_dev, groups, SMALL if q else LARGE
-        )
+        if q:
+            keep, *sends = cross_lag_parts(
+                scal,
+                weight,
+                after[:1],
+                rows,
+                own_rows,
+                pieces,
+                table,
+                geometry,
+                columns,
+                lag_dev,
+                groups,
+                SMALL if q == 1 else LARGE,
+            )
+        else:
+            lhs = cross_rows(weight, [], rows, own_rows, pieces, classes, LARGE)
+            keep, *sends = lag_parts(
+                scal, [], lhs, table, geometry, columns, lag_dev, groups, LARGE
+            )
         sends = [swapped(x, "freq", cores, 1) for x in sends]
         own, *sends = add_cores(scal, after[1:], keep, sends)
         more = [swapped(x, "win", columns, s + 1) for s, x in enumerate(sends)]

time: 77.4 us -> 77.3 us (level)
    pallas_call x0 -> x2, Pallas kernels: none -> 3.6 us  [cross_lag_parts(): pl.pallas_call(functools.partial(cross_lags_kernel, geometry, split, len(...]
    pallas_call x3 -> x1, Pallas kernels: 5.86 us -> 2.44 us  [lag_parts(): pl.pallas_call(functools.partial(lags_kernel, geometry, split, len(after)...]
where the time goes in v17:
time: 77.3 us; the launch traced here: 77.1 us
  starting transfers between devices  24.9 us (32%)
  waiting for transfers between devices  23.7 us (31%)
  Pallas kernels  23 us (30%)
  local copies, waits for them, and re-layouts  4 us (5%)
  between operations  1.46 us (2%)
    ppermute x28, starting transfers between devices, swapped(): return lax.ppermute(value, axis, [(i, i ^ step) for i in range(size)])  24.9 us
    ppermute x28, waiting for transfers between devices, swapped(): return lax.ppermute(value, axis, [(i, i ^ step) for i in range(size)])  23.7 us
    pallas_call x2, Pallas kernels, cross_lag_parts(): pl.pallas_call(functools.partial(cross_lags_kernel, geometry, split, len(...  3.6 us
    pallas_call x1, Pallas kernels, normed_rows(): pl.pallas_call(functools.partial(normed_kernel, lag_total, chunks, len(su...  3.22 us
    pallas_call x1, Pallas kernels, gather_own(): pl.pallas_call(functools.partial(own_kernel, classes, parts), out_shape=[...  3.07 us
    unnamed x12, local copies, waits for them, and re-layouts  2.68 us
    pallas_call x1, Pallas kernels, lag_parts(): pl.pallas_call(functools.partial(lags_kernel, geometry, split, len(after)...  2.44 us
    pallas_call x3, Pallas kernels, lag_stats(): pl.pallas_call(functools.partial(stats_kernel, scale, q, pieces, len(more...  2.22 us
  transfers between devices with their start and end apart: 28, of which 14 were waited for; matrix products, arithmetic and copies ran while one was open for 0% of the time, Pallas kernels for 24%

profile of v17, /device:TPU:0, one launch (start us, length us, event | category | flops | bytes accessed | tf_op | source)
XLA Modules:
  0.0 77.1 jit_solution(11623358953945379502)
XLA Ops:
  0.7 1.3 %constant_dynamic-slice_fusion = (bf16[1,2,128,1024]{3,2,1,0:T(8,128)(2,1)S(1)}, bf16[1,2,128,1024]{3,2,1,0:T(8,128)(2,1)S(1)}) fusion(bf16[1,2,128,2048]{3,2,1,0:T(8,128)(2,1)} %param.8, s32[]{:T(128)S(6)} %select_n.7, s32[]{:T(128)S(6)} %select_n.6), kind=kLoop, calls=%fused_computation | loop fusion | bytes 2097160 | tf_op jit(solution)/shard_map/dynamic_slice | solution.py:583
  2.0 3.0 %collective-permute-start = (bf16[1,2,128,1024]{3,2,1,0:T(8,128)(2,1)S(1)}, bf16[1,2,128,1024]{3,2,1,0:T(8,128)(2,1)S(1)}, u32[]{:S(2)}, u32[]{:S(2)}) collective-permute-start(bf16[1,2,128,1024]{3,2,1,0:T(8,128)(2,1)S(1)} %get-tuple-element.90), channel_id=1, source_target_pairs={{0,2},{2,0},{1,3},{3,1},{4,6},{6,4},{5,7},{7,5},{8,10},{10,8},{9,1... | collective-permute-start | bytes 1572872 | tf_op jit(solution)/shard_map/ppermute | solution.py:29
  8.3 1.2 %index.1 = (s32[128]{0:T(128)S(1)}, s32[1,64]{1,0:T(1,128)S(1)}, s32[1,64]{1,0:T(1,128)S(1)}, s32[1,64]{1,0:T(1,128)S(1)}, s32[1,64]{1,0:T(1,128)S(1)}, /*index=5*/s32[4,64]{1,0:T(4,128)S(1)}) custom-call(s32[1]{0:T(128)S(6)} %copy.10.refs_0_, s32[4]{0:T(128)S(1)} %copy-done.4, s32[4]{0:T(128)S(1)} %bitcast.1, s32[4,64]{1,0:T(4,128)S(1)} %copy-done.2, ...), custom_call_target="tpu_custom_call" | custom-call | flops 1 | bytes 1 | tf_op jit(solution)/shard_map/index/pallas_call | solution.py:92
  9.5 3.7 %collective-permute-start.1 = (s32[1,64]{1,0:T(1,128)S(1)}, s32[1,64]{1,0:T(1,128)S(1)}, u32[]{:S(2)}, u32[]{:S(2)}) collective-permute-start(s32[1,64]{1,0:T(1,128)S(1)} %get-tuple-element.47), channel_id=1, source_target_pairs={{0,12},{4,8},{8,4},{12,0},{1,13},{5,9},{9,5},{13,1},{2,14},{6,10},... | collective-permute-start | bytes 776 | tf_op jit(solution)/shard_map/ppermute | solution.py:29
  13.2 0.8 %collective-permute-start.3 = (s32[1,64]{1,0:T(1,128)S(1)}, s32[1,64]{1,0:T(1,128)S(1)}, u32[]{:S(2)}, u32[]{:S(2)}) collective-permute-start(s32[1,64]{1,0:T(1,128)S(1)} %get-tuple-element.49), channel_id=1, source_target_pairs={{0,4},{4,0},{8,12},{12,8},{1,5},{5,1},{9,13},{13,9},{2,6},{6,2},{1... | collective-permute-start | bytes 776 | tf_op jit(solution)/shard_map/ppermute | solution.py:29
  14.9 2.7 %collective-permute-done.2.refs_3_.refs_1_ = s32[1,64]{1,0:T(1,128)S(1)} collective-permute-done((s32[1,64]{1,0:T(1,128)S(1)}, s32[1,64]{1,0:T(1,128)S(1)}, u32[]{:S(2)}, u32[]{:S(2)}) %collective-permute-start.2) | collective-permute-done | bytes 288 | tf_op jit(solution)/shard_map/ppermute | solution.py:29
  17.7 1.6 %rows.1 = (bf16[1,2,64,1024]{3,2,1,0:T(8,128)(2,1)S(1)}, bf16[1,2,64,1024]{3,2,1,0:T(8,128)(2,1)S(1)}, bf16[1,2,64,1024]{3,2,1,0:T(8,128)(2,1)S(1)}, bf16[1,2,64...) custom-call(s32[128]{0:T(128)S(1)} %get-tuple-element.46.scal, ...), custom_call_target="tpu_custom_call" | custom-call | flops 1 | bytes 1 | tf_op jit(solution)/shard_map/rows/pallas_call | solution.py:175
  19.2 1.1 %collective-permute-start.4 = (bf16[1,2,64,1024]{3,2,1,0:T(8,128)(2,1)S(1)}, bf16[1,2,64,1024]{3,2,1,0:T(8,128)(2,1)S(1)}, u32[]{:S(2)}, u32[]{:S(2)}) collective-permute-start(bf16[1,2,64,1024]{3,2,1,0:T(8,128)(2,1)S(1)} %get-tuple-element.52), channel_id=1, source_target_pairs={{0,4},{4,0},{8,12},{12,8},{1,5},{5,1},{9,13},{13,9},{2,6},{6,2},{1... | collective-permute-start | bytes 786440 | tf_op jit(solution)/shard_map/ppermute | solution.py:29
  20.4 2.6 %collective-permute-start.14 = (bf16[1,2,64,1024]{3,2,1,0:T(8,128)(2,1)S(1)}, bf16[1,2,64,1024]{3,2,1,0:T(8,128)(2,1)S(1)}, u32[]{:S(2)}, u32[]{:S(2)}) collective-permute-start(bf16[1,2,64,1024]{3,2,1,0:T(8,128)(2,1)S(1)} %get-tuple-element.69), channel_id=1, source_target_pairs={{0,8},{4,12},{8,0},{12,4},{1,9},{5,13},{9,1},{13,5},{2,10},{6,14},... | collective-permute-start | bytes 786440 | tf_op jit(solution)/shard_map/ppermute | solution.py:29
  23.7 3.1 %own.1 = (bf16[4,1,2,64,1024]{4,3,2,1,0:T(8,128)(2,1)S(1)}, bf16[8,256,1024]{2,1,0:T(8,128)(2,1)S(1)}) custom-call(s32[128]{0:T(128)S(1)} %get-tuple-element.46.scal, bf16[1,2,128,1024]{3,2,1,0:T(8,128)(2,1)S(1)} %get-tuple-element.53.kept, s32[4,64]{1,0:T(4,128)S(1)} %get-tuple-element.54.rec_ids, f32[2,56,1024]{2,1,0:T(8,128)S(1)} %copy-done.1), custom_call_target="tpu_custom_call" | custom-call | flops 1 | bytes 1 | tf_op jit(solution)/shard_map/own/pallas_call | solution.py:204
  26.8 3.7 %collective-permute-done.4.refs_1_ = bf16[1,2,64,1024]{3,2,1,0:T(8,128)(2,1)S(1)} collective-permute-done((bf16[1,2,64,1024]{3,2,1,0:T(8,128)(2,1)S(1)}, bf16[1,2,64,1024]{3,2,1,0:T(8,128)(2,1)S(1)}, u32[]{:S(2)}, u32[]{:S(2)}) %collective-permute-start.4) | collective-permute-done | bytes 262176 | tf_op jit(solution)/shard_map/ppermute | solution.py:29
  30.7 2.4 %lags.1 = (f32[2,128,1024]{2,1,0:T(8,128)S(1)}, bf16[2,16,1024]{2,1,0:T(8,128)(2,1)S(1)}, bf16[2,16,1024]{2,1,0:T(8,128)(2,1)S(1)}, bf16[2,16,1024]{2,1,0:T(8,12...) custom-call(s32[128]{0:T(128)S(1)} %get-tuple-element.46.scal, ...), custom_call_target="tpu_custom_call" | custom-call | flops 20000000000 | bytes 1048576 | tf_op jit(solution)/shard_map/lags/pallas_call | solution.py:331
  36.3 0.7 collective-permute-done.11.refs_7_
  37.2 0.8 %cores.3 = (f32[128,1024]{1,0:T(8,128)S(1)}, bf16[128,1024]{1,0:T(8,128)(2,1)S(1)}) custom-call(s32[128]{0:T(128)S(1)} %get-tuple-element.46.scal, f32[2,128,1024]{2,1,0:T(8,128)S(1)} %get-tuple-element.57.refs_0_, bf16[2,16,1024]{2,1,0:T(8,128)(2,1)S(1)} %collective-permute-done.5.refs_1_, bf16[2,16,1024]{2,1,0:T(8,128)(2,1)S(1)} %collective-permute-done.6.refs_2_, ...), custom_call_target="tpu_custom_call" | custom-call | flops 1 | bytes 1 | tf_op jit(solution)/shard_map/cores/pallas_call | solution.py:394
  38.0 1.5 %collective-permute-start.13 = (bf16[128,1024]{1,0:T(8,128)(2,1)S(1)}, bf16[128,1024]{1,0:T(8,128)(2,1)S(1)}, u32[]{:S(2)}, u32[]{:S(2)}) collective-permute-start(bf16[128,1024]{1,0:T(8,128)(2,1)S(1)} %get-tuple-element.67), channel_id=1, source_target_pairs={{0,2},{2,0},{1,3},{3,1},{4,6},{6,4},{5,7},{7,5},{8,10},{10,8},{9,1... | collective-permute-start | bytes 786440 | tf_op jit(solution)/shard_map/ppermute | solution.py:29
  39.5 2.3 %collective-permute-done.14.refs_1_ = bf16[1,2,64,1024]{3,2,1,0:T(8,128)(2,1)S(1)} collective-permute-done((bf16[1,2,64,1024]{3,2,1,0:T(8,128)(2,1)S(1)}, bf16[1,2,64,1024]{3,2,1,0:T(8,128)(2,1)S(1)}, u32[]{:S(2)}, u32[]{:S(2)}) %collective-permute-start.14) | collective-permute-done | bytes 262176 | tf_op jit(solution)/shard_map/ppermute | solution.py:29
  41.7 1.8 %cross_lags.2 = (f32[2,64,1024]{2,1,0:T(8,128)S(1)}, bf16[2,32,1024]{2,1,0:T(8,128)(2,1)S(1)}, bf16[2,32,1024]{2,1,0:T(8,128)(2,1)S(1)}) custom-call(s32[128]{0:T(128)S(1)} %get-tuple-element.46.scal, f32[1]{0:T(128)} %constant.3.clone.1.weight, f32[128,1024]{1,0:T(8,128)S(1)} %get-tuple-element.66.refs_0_, ...), custom_call_target="tpu_custom_call" | custom-call | flops 1 | bytes 1 | tf_op jit(solution)/shard_map/cross_lags/pallas_call | solution.py:358
  44.1 1.8 %cross_lags.3 = (f32[2,64,1024]{2,1,0:T(8,128)S(1)}, bf16[2,32,1024]{2,1,0:T(8,128)(2,1)S(1)}, bf16[2,32,1024]{2,1,0:T(8,128)(2,1)S(1)}) custom-call(s32[128]{0:T(128)S(1)} %get-tuple-element.46.scal, f32[1]{0:T(128)} %constant.3.clone.1.weight, bf16[1,2,64,1024]{3,2,1,0:T(8,128)(2,1)S(1)} %collective-permute-done.18.refs_0_, ...), custom_call_target="tpu_custom_call" | custom-call | flops 20000000000 | bytes 1048576 | tf_op jit(solution)/shard_map/cross_lags/pallas_call | solution.py:358
  47.2 1.5 %collective-permute-start.17 = (bf16[64,1024]{1,0:T(8,128)(2,1)S(1)}, bf16[64,1024]{1,0:T(8,128)(2,1)S(1)}, u32[]{:S(2)}, u32[]{:S(2)}) collective-permute-start(bf16[64,1024]{1,0:T(8,128)(2,1)S(1)} %get-tuple-element.74), channel_id=1, source_target_pairs={{0,2},{2,0},{1,3},{3,1},{4,6},{6,4},{5,7},{7,5},{8,10},{10,8},{9,1... | collective-permute-start | bytes 393224 | tf_op jit(solution)/shard_map/ppermute | solution.py:29
  50.0 0.8 %stats.3 = (f32[128,1024]{1,0:T(8,128)S(1)}, f32[8,128]{1,0:T(8,128)S(1)}) custom-call(s32[128]{0:T(128)S(1)} %get-tuple-element.46.scal, f32[128,1024]{1,0:T(8,128)S(1)} %get-tuple-element.66.refs_0_, bf16[128,1024]{1,0:T(8,128)(2,1)S(1)} %collective-permute-done.13.refs_1_.refs_0_, f32[4,64,1024]{2,1,0:T(8,128)S(1)} %copy-done, f32[4,64,1024]{2,1,0:T(8,128)S(1)} %copy-done), custom_call_target="tpu_custom_call" | custom-call | flops 1 | bytes 1 | tf_op jit(solution)/shard_map/stats/pallas_call | solution.py:449
  50.8 2.8 %collective-permute-done.17.refs_2_ = bf16[64,1024]{1,0:T(8,128)(2,1)S(1)} collective-permute-done((bf16[64,1024]{1,0:T(8,128)(2,1)S(1)}, bf16[64,1024]{1,0:T(8,128)(2,1)S(1)}, u32[]{:S(2)}, u32[]{:S(2)}) %collective-permute-start.17) | collective-permute-done | bytes 131104 | tf_op jit(solution)/shard_map/ppermute | solution.py:29
  54.3 1.2 %collective-permute-done.21.refs_2_ = bf16[64,1024]{1,0:T(8,128)(2,1)S(1)} collective-permute-done((bf16[64,1024]{1,0:T(8,128)(2,1)S(1)}, bf16[64,1024]{1,0:T(8,128)(2,1)S(1)}, u32[]{:S(2)}, u32[]{:S(2)}) %collective-permute-start.21) | collective-permute-done | bytes 131104 | tf_op jit(solution)/shard_map/ppermute | solution.py:29
  56.6 1.2 %collective-permute-start.23 = (f32[8,128]{1,0:T(8,128)S(1)}, f32[8,128]{1,0:T(8,128)S(1)}, u32[]{:S(2)}, u32[]{:S(2)}) collective-permute-start(f32[8,128]{1,0:T(8,128)S(1)} %get-tuple-element.82.refs_3_.refs_4_), channel_id=1, source_target_pairs={{0,2},{1,3},{2,0},{3,1},{4,6},{5,7},{6,4},{7,5},{8,10},{9,11},{10,... | collective-permute-start | bytes 12296 | tf_op jit(solution)/shard_map/ppermute | solution.py:29
  58.1 1.2 %collective-permute-done.22.refs_0_.refs_1_ = f32[8,128]{1,0:T(8,128)S(1)} collective-permute-done((f32[8,128]{1,0:T(8,128)S(1)}, f32[8,128]{1,0:T(8,128)S(1)}, u32[]{:S(2)}, u32[]{:S(2)}) %collective-permute-start.22) | collective-permute-done | bytes 4128 | tf_op jit(solution)/shard_map/ppermute | solution.py:29
  59.3 0.9 %collective-permute-done.23.refs_1_.refs_2_ = f32[8,128]{1,0:T(8,128)S(1)} collective-permute-done((f32[8,128]{1,0:T(8,128)S(1)}, f32[8,128]{1,0:T(8,128)S(1)}, u32[]{:S(2)}, u32[]{:S(2)}) %collective-permute-start.23) | collective-permute-done | bytes 4128 | tf_op jit(solution)/shard_map/ppermute | solution.py:29
  60.2 0.8 %gradient.2 = (bf16[64,1024]{1,0:T(8,128)(2,1)S(1)}, bf16[64,1024]{1,0:T(8,128)(2,1)S(1)}) custom-call(s32[128]{0:T(128)S(1)} %get-tuple-element.46.scal, f32[8,128]{1,0:T(8,128)S(1)} %collective-permute-done.22.refs_0_.refs_1_, f32[8,128]{1,0:T(8,128)S(1)} %collective-permute-done.23.refs_1_.refs_2_, f32[8,128]{1,0:T(8,128)S(1)} %collective-permute-done.24.refs_2_.refs_3_, ...), custom_call_target="tpu_custom_call" | custom-call | flops 1 | bytes 1 | tf_op jit(solution)/shard_map/gradient/pallas_call | solution.py:498
  61.1 2.8 %collective-permute-start.25 = (bf16[64,1024]{1,0:T(8,128)(2,1)S(1)}, bf16[64,1024]{1,0:T(8,128)(2,1)S(1)}, u32[]{:S(2)}, u32[]{:S(2)}) collective-permute-start(bf16[64,1024]{1,0:T(8,128)(2,1)S(1)} %get-tuple-element.86.refs_0_), channel_id=1, source_target_pairs={{0,12},{4,8},{8,4},{12,0},{1,13},{5,9},{9,5},{13,1},{2,14},{6,10},... | collective-permute-start | bytes 393224 | tf_op jit(solution)/shard_map/ppermute | solution.py:29
  64.1 0.8 %gradient.3 = (bf16[64,1024]{1,0:T(8,128)(2,1)S(1)}, bf16[64,1024]{1,0:T(8,128)(2,1)S(1)}) custom-call(s32[128]{0:T(128)S(1)} %get-tuple-element.46.scal, bf16[64,1024]{1,0:T(8,128)(2,1)S(1)} %get-tuple-element.86.refs_0_, f32[8,128]{1,0:T(8,128)S(1)} %collective-permute-done.22.refs_0_.refs_1_, f32[8,128]{1,0:T(8,128)S(1)} %collective-permute-done.23.refs_1_.refs_2_, ...), custom_call_target="tpu_custom_call" | custom-call | flops 1 | bytes 1 | tf_op jit(solution)/shard_map/gradient/pallas_call | solution.py:498
  64.9 1.5 %collective-permute-start.27 = (bf16[64,1024]{1,0:T(8,128)(2,1)S(1)}, bf16[64,1024]{1,0:T(8,128)(2,1)S(1)}, u32[]{:S(2)}, u32[]{:S(2)}) collective-permute-start(bf16[64,1024]{1,0:T(8,128)(2,1)S(1)} %get-tuple-element.89), channel_id=1, source_target_pairs={{0,4},{4,0},{8,12},{12,8},{1,5},{5,1},{9,13},{13,9},{2,6},{6,2},{1... | collective-permute-start | bytes 393224 | tf_op jit(solution)/shard_map/ppermute | solution.py:29
  66.4 3.2 %normed.1 = f32[4,64,1024]{2,1,0:T(8,128)} custom-call(s32[128]{0:T(128)S(1)} %get-tuple-element.46.scal, f32[8,128]{1,0:T(8,128)S(1)} %collective-permute-done.22.refs_0_.refs_1_, f32[8,128]{1,0:T(8,128)S(1)} %collective-permute-done.23.refs_1_.refs_2_, f32[8,128]{1,0:T(8,128)S(1)} %collective-permute-done.24.refs_2_.refs_3_, ...), custom_call_target="tpu_custom_call" | custom-call | flops 1 | bytes 1 | tf_op jit(solution)/shard_map/normed/pallas_call | solution.py:529
  69.6 6.4 %collective-permute-done.26.refs_5_ = bf16[64,1024]{1,0:T(8,128)(2,1)S(1)} collective-permute-done((bf16[64,1024]{1,0:T(8,128)(2,1)S(1)}, bf16[64,1024]{1,0:T(8,128)(2,1)S(1)}, u32[]{:S(2)}, u32[]{:S(2)}) %collective-permute-start.26) | collective-permute-done | bytes 131104 | tf_op jit(solution)/shard_map/ppermute | solution.py:29
  76.0 1.1 %adjoint.1 = f32[128,1024]{1,0:T(8,128)} custom-call(s32[1,64]{1,0:T(1,128)S(1)} %collective-permute-done.1.refs_2_.refs_0_, s32[1,64]{1,0:T(1,128)S(1)} %collective-permute-done.2.refs_3_.refs_1_, s32[1,64]{1,0:T(1,128)S(1)} %get-tuple-element.50.refs_5_.refs_2_, s32[1,64]{1,0:T(1,128)S(1)} %collective-permute-done.3.refs_4_.refs_3_, ...), custom_call_target="tpu_custom_call" | custom-call | flops 1 | bytes 1 | tf_op jit(solution)/shard_map/adjoint/pallas_call | solution.py:553
  (55 shorter events, 13.4 us)
Async XLA Ops:
  0.6 23.1 %copy-start.1 = (f32[2,56,1024]{2,1,0:T(8,128)S(1)}, f32[2,56,1024]{2,1,0:T(8,128)}, u32[]{:S(2)}) copy-start(f32[2,56,1024]{2,1,0:T(8,128)} %constant.16.clone.trig) | copy-start | bytes 1376260
  2.0 15.7 %collective-permute-start = (bf16[1,2,128,1024]{3,2,1,0:T(8,128)(2,1)S(1)}, bf16[1,2,128,1024]{3,2,1,0:T(8,128)(2,1)S(1)}, u32[]{:S(2)}, u32[]{:S(2)}) collective-permute-start(bf16[1,2,128,1024]{3,2,1,0:T(8,128)(2,1)S(1)} %get-tuple-element.90), channel_id=1, source_target_pairs={{0,2},{2,0},{1,3},{3,1},{4,6},{6,4},{5,7},{7,5},{8,10},{10,8},{9,1... | collective-permute-start | bytes 1572872 | tf_op jit(solution)/shard_map/ppermute | solution.py:29
  5.6 0.7 copy-start.2
  6.3 0.7 copy-start.3
  9.5 5.4 %collective-permute-start.1 = (s32[1,64]{1,0:T(1,128)S(1)}, s32[1,64]{1,0:T(1,128)S(1)}, u32[]{:S(2)}, u32[]{:S(2)}) collective-permute-start(s32[1,64]{1,0:T(1,128)S(1)} %get-tuple-element.47), channel_id=1, source_target_pairs={{0,12},{4,8},{8,4},{12,0},{1,13},{5,9},{9,5},{13,1},{2,14},{6,10},... | collective-permute-start | bytes 776 | tf_op jit(solution)/shard_map/ppermute | solution.py:29
  13.2 4.4 %collective-permute-start.2 = (s32[1,64]{1,0:T(1,128)S(1)}, s32[1,64]{1,0:T(1,128)S(1)}, u32[]{:S(2)}, u32[]{:S(2)}) collective-permute-start(s32[1,64]{1,0:T(1,128)S(1)} %get-tuple-element.48), channel_id=1, source_target_pairs={{0,8},{4,12},{8,0},{12,4},{1,9},{5,13},{9,1},{13,5},{2,10},{6,14},... | collective-permute-start | bytes 776 | tf_op jit(solution)/shard_map/ppermute | solution.py:29
  13.2 4.4 %collective-permute-start.3 = (s32[1,64]{1,0:T(1,128)S(1)}, s32[1,64]{1,0:T(1,128)S(1)}, u32[]{:S(2)}, u32[]{:S(2)}) collective-permute-start(s32[1,64]{1,0:T(1,128)S(1)} %get-tuple-element.49), channel_id=1, source_target_pairs={{0,4},{4,0},{8,12},{12,8},{1,5},{5,1},{9,13},{13,9},{2,6},{6,2},{1... | collective-permute-start | bytes 776 | tf_op jit(solution)/shard_map/ppermute | solution.py:29
  19.2 11.2 %collective-permute-start.4 = (bf16[1,2,64,1024]{3,2,1,0:T(8,128)(2,1)S(1)}, bf16[1,2,64,1024]{3,2,1,0:T(8,128)(2,1)S(1)}, u32[]{:S(2)}, u32[]{:S(2)}) collective-permute-start(bf16[1,2,64,1024]{3,2,1,0:T(8,128)(2,1)S(1)} %get-tuple-element.52), channel_id=1, source_target_pairs={{0,4},{4,0},{8,12},{12,8},{1,5},{5,1},{9,13},{13,9},{2,6},{6,2},{1... | collective-permute-start | bytes 786440 | tf_op jit(solution)/shard_map/ppermute | solution.py:29
  20.4 21.4 %collective-permute-start.14 = (bf16[1,2,64,1024]{3,2,1,0:T(8,128)(2,1)S(1)}, bf16[1,2,64,1024]{3,2,1,0:T(8,128)(2,1)S(1)}, u32[]{:S(2)}, u32[]{:S(2)}) collective-permute-start(bf16[1,2,64,1024]{3,2,1,0:T(8,128)(2,1)S(1)} %get-tuple-element.69), channel_id=1, source_target_pairs={{0,8},{4,12},{8,0},{12,4},{1,9},{5,13},{9,1},{13,5},{2,10},{6,14},... | collective-permute-start | bytes 786440 | tf_op jit(solution)/shard_map/ppermute | solution.py:29
  23.0 21.2 %collective-permute-start.18 = (bf16[1,2,64,1024]{3,2,1,0:T(8,128)(2,1)S(1)}, bf16[1,2,64,1024]{3,2,1,0:T(8,128)(2,1)S(1)}, u32[]{:S(2)}, u32[]{:S(2)}) collective-permute-start(bf16[1,2,64,1024]{3,2,1,0:T(8,128)(2,1)S(1)} %get-tuple-element.76), channel_id=1, source_target_pairs={{0,12},{4,8},{8,4},{12,0},{1,13},{5,9},{9,5},{13,1},{2,14},{6,10},... | collective-permute-start | bytes 786440 | tf_op jit(solution)/shard_map/ppermute | solution.py:29
  33.2 1.3 %collective-permute-start.5 = (bf16[2,16,1024]{2,1,0:T(8,128)(2,1)S(1)}, bf16[2,16,1024]{2,1,0:T(8,128)(2,1)S(1)}, u32[]{:S(2)}, u32[]{:S(2)}) collective-permute-start(bf16[2,16,1024]{2,1,0:T(8,128)(2,1)S(1)} %get-tuple-element.58), channel_id=1, source_target_pairs={{0,1},{1,0},{2,3},{3,2},{4,5},{5,4},{6,7},{7,6},{8,9},{9,8},{10,11... | collective-permute-start | bytes 196616 | tf_op jit(solution)/shard_map/ppermute | solution.py:29
  33.2 1.4 %collective-permute-start.6 = (bf16[2,16,1024]{2,1,0:T(8,128)(2,1)S(1)}, bf16[2,16,1024]{2,1,0:T(8,128)(2,1)S(1)}, u32[]{:S(2)}, u32[]{:S(2)}) collective-permute-start(bf16[2,16,1024]{2,1,0:T(8,128)(2,1)S(1)} %get-tuple-element.59), channel_id=1, source_target_pairs={{0,1},{1,0},{2,3},{3,2},{4,5},{5,4},{6,7},{7,6},{8,9},{9,8},{10,11... | collective-permute-start | bytes 196616 | tf_op jit(solution)/shard_map/ppermute | solution.py:29
  33.7 1.3 %collective-permute-start.7 = (bf16[2,16,1024]{2,1,0:T(8,128)(2,1)S(1)}, bf16[2,16,1024]{2,1,0:T(8,128)(2,1)S(1)}, u32[]{:S(2)}, u32[]{:S(2)}) collective-permute-start(bf16[2,16,1024]{2,1,0:T(8,128)(2,1)S(1)} %get-tuple-element.60), channel_id=1, source_target_pairs={{0,1},{1,0},{2,3},{3,2},{4,5},{5,4},{6,7},{7,6},{8,9},{9,8},{10,11... | collective-permute-start | bytes 196616 | tf_op jit(solution)/shard_map/ppermute | solution.py:29
  34.5 1.3 %collective-permute-start.8 = (bf16[2,16,1024]{2,1,0:T(8,128)(2,1)S(1)}, bf16[2,16,1024]{2,1,0:T(8,128)(2,1)S(1)}, u32[]{:S(2)}, u32[]{:S(2)}) collective-permute-start(bf16[2,16,1024]{2,1,0:T(8,128)(2,1)S(1)} %get-tuple-element.61), channel_id=1, source_target_pairs={{0,1},{1,0},{2,3},{3,2},{4,5},{5,4},{6,7},{7,6},{8,9},{9,8},{10,11... | collective-permute-start | bytes 196616 | tf_op jit(solution)/shard_map/ppermute | solution.py:29
  34.6 1.3 %collective-permute-start.9 = (bf16[2,16,1024]{2,1,0:T(8,128)(2,1)S(1)}, bf16[2,16,1024]{2,1,0:T(8,128)(2,1)S(1)}, u32[]{:S(2)}, u32[]{:S(2)}) collective-permute-start(bf16[2,16,1024]{2,1,0:T(8,128)(2,1)S(1)} %get-tuple-element.62), channel_id=1, source_target_pairs={{0,1},{1,0},{2,3},{3,2},{4,5},{5,4},{6,7},{7,6},{8,9},{9,8},{10,11... | collective-permute-start | bytes 196616 | tf_op jit(solution)/shard_map/ppermute | solution.py:29
  35.0 1.3 %collective-permute-start.10 = (bf16[2,16,1024]{2,1,0:T(8,128)(2,1)S(1)}, bf16[2,16,1024]{2,1,0:T(8,128)(2,1)S(1)}, u32[]{:S(2)}, u32[]{:S(2)}) collective-permute-start(bf16[2,16,1024]{2,1,0:T(8,128)(2,1)S(1)} %get-tuple-element.63), channel_id=1, source_target_pairs={{0,1},{1,0},{2,3},{3,2},{4,5},{5,4},{6,7},{7,6},{8,9},{9,8},{10,11... | collective-permute-start | bytes 196616 | tf_op jit(solution)/shard_map/ppermute | solution.py:29
  35.7 1.3 %collective-permute-start.11 = (bf16[2,16,1024]{2,1,0:T(8,128)(2,1)S(1)}, bf16[2,16,1024]{2,1,0:T(8,128)(2,1)S(1)}, u32[]{:S(2)}, u32[]{:S(2)}) collective-permute-start(bf16[2,16,1024]{2,1,0:T(8,128)(2,1)S(1)} %get-tuple-element.64), channel_id=1, source_target_pairs={{0,1},{1,0},{2,3},{3,2},{4,5},{5,4},{6,7},{7,6},{8,9},{9,8},{10,11... | collective-permute-start | bytes 196616 | tf_op jit(solution)/shard_map/ppermute | solution.py:29
  35.9 1.3 %collective-permute-start.12 = (bf16[2,16,1024]{2,1,0:T(8,128)(2,1)S(1)}, bf16[2,16,1024]{2,1,0:T(8,128)(2,1)S(1)}, u32[]{:S(2)}, u32[]{:S(2)}) collective-permute-start(bf16[2,16,1024]{2,1,0:T(8,128)(2,1)S(1)} %get-tuple-element.65), channel_id=1, source_target_pairs={{0,1},{1,0},{2,3},{3,2},{4,5},{5,4},{6,7},{7,6},{8,9},{9,8},{10,11... | collective-permute-start | bytes 196616 | tf_op jit(solution)/shard_map/ppermute | solution.py:29
  38.0 8.6 %collective-permute-start.13 = (bf16[128,1024]{1,0:T(8,128)(2,1)S(1)}, bf16[128,1024]{1,0:T(8,128)(2,1)S(1)}, u32[]{:S(2)}, u32[]{:S(2)}) collective-permute-start(bf16[128,1024]{1,0:T(8,128)(2,1)S(1)} %get-tuple-element.67), channel_id=1, source_target_pairs={{0,2},{2,0},{1,3},{3,1},{4,6},{6,4},{5,7},{7,5},{8,10},{10,8},{9,1... | collective-permute-start | bytes 786440 | tf_op jit(solution)/shard_map/ppermute | solution.py:29
  43.5 3.0 %collective-permute-start.15 = (bf16[2,32,1024]{2,1,0:T(8,128)(2,1)S(1)}, bf16[2,32,1024]{2,1,0:T(8,128)(2,1)S(1)}, u32[]{:S(2)}, u32[]{:S(2)}) collective-permute-start(bf16[2,32,1024]{2,1,0:T(8,128)(2,1)S(1)} %get-tuple-element.71), channel_id=1, source_target_pairs={{0,1},{1,0},{2,3},{3,2},{4,5},{5,4},{6,7},{7,6},{8,9},{9,8},{10,11... | collective-permute-start | bytes 393224 | tf_op jit(solution)/shard_map/ppermute | solution.py:29
  43.6 6.4 %copy-start = (f32[4,64,1024]{2,1,0:T(8,128)S(1)}, f32[4,64,1024]{2,1,0:T(8,128)}, u32[]{:S(2)}) copy-start(f32[4,64,1024]{2,1,0:T(8,128)} %refs_7_.3) | copy-start | bytes 3145732
  43.6 2.9 %collective-permute-start.16 = (bf16[2,32,1024]{2,1,0:T(8,128)(2,1)S(1)}, bf16[2,32,1024]{2,1,0:T(8,128)(2,1)S(1)}, u32[]{:S(2)}, u32[]{:S(2)}) collective-permute-start(bf16[2,32,1024]{2,1,0:T(8,128)(2,1)S(1)} %get-tuple-element.72), channel_id=1, source_target_pairs={{0,1},{1,0},{2,3},{3,2},{4,5},{5,4},{6,7},{7,6},{8,9},{9,8},{10,11... | collective-permute-start | bytes 393224 | tf_op jit(solution)/shard_map/ppermute | solution.py:29
  45.9 2.8 %collective-permute-start.19 = (bf16[2,32,1024]{2,1,0:T(8,128)(2,1)S(1)}, bf16[2,32,1024]{2,1,0:T(8,128)(2,1)S(1)}, u32[]{:S(2)}, u32[]{:S(2)}) collective-permute-start(bf16[2,32,1024]{2,1,0:T(8,128)(2,1)S(1)} %get-tuple-element.78), channel_id=1, source_target_pairs={{0,1},{1,0},{2,3},{3,2},{4,5},{5,4},{6,7},{7,6},{8,9},{9,8},{10,11... | collective-permute-start | bytes 393224 | tf_op jit(solution)/shard_map/ppermute | solution.py:29
  46.1 2.6 %collective-permute-start.20 = (bf16[2,32,1024]{2,1,0:T(8,128)(2,1)S(1)}, bf16[2,32,1024]{2,1,0:T(8,128)(2,1)S(1)}, u32[]{:S(2)}, u32[]{:S(2)}) collective-permute-start(bf16[2,32,1024]{2,1,0:T(8,128)(2,1)S(1)} %get-tuple-element.79), channel_id=1, source_target_pairs={{0,1},{1,0},{2,3},{3,2},{4,5},{5,4},{6,7},{7,6},{8,9},{9,8},{10,11... | collective-permute-start | bytes 393224 | tf_op jit(solution)/shard_map/ppermute | solution.py:29
  47.2 6.4 %collective-permute-start.17 = (bf16[64,1024]{1,0:T(8,128)(2,1)S(1)}, bf16[64,1024]{1,0:T(8,128)(2,1)S(1)}, u32[]{:S(2)}, u32[]{:S(2)}) collective-permute-start(bf16[64,1024]{1,0:T(8,128)(2,1)S(1)} %get-tuple-element.74), channel_id=1, source_target_pairs={{0,2},{2,0},{1,3},{3,1},{4,6},{6,4},{5,7},{7,5},{8,10},{10,8},{9,1... | collective-permute-start | bytes 393224 | tf_op jit(solution)/shard_map/ppermute | solution.py:29
  49.4 6.2 %collective-permute-start.21 = (bf16[64,1024]{1,0:T(8,128)(2,1)S(1)}, bf16[64,1024]{1,0:T(8,128)(2,1)S(1)}, u32[]{:S(2)}, u32[]{:S(2)}) collective-permute-start(bf16[64,1024]{1,0:T(8,128)(2,1)S(1)} %get-tuple-element.81), channel_id=1, source_target_pairs={{0,2},{2,0},{1,3},{3,1},{4,6},{6,4},{5,7},{7,5},{8,10},{10,8},{9,1... | collective-permute-start | bytes 393224 | tf_op jit(solution)/shard_map/ppermute | solution.py:29
  56.3 3.1 %collective-permute-start.22 = (f32[8,128]{1,0:T(8,128)S(1)}, f32[8,128]{1,0:T(8,128)S(1)}, u32[]{:S(2)}, u32[]{:S(2)}) collective-permute-start(f32[8,128]{1,0:T(8,128)S(1)} %get-tuple-element.82.refs_3_.refs_4_), channel_id=1, source_target_pairs={{0,3},{1,2},{2,1},{3,0},{4,7},{5,6},{6,5},{7,4},{8,11},{9,10},{10,... | collective-permute-start | bytes 12296 | tf_op jit(solution)/shard_map/ppermute | solution.py:29
  56.6 3.6 %collective-permute-start.23 = (f32[8,128]{1,0:T(8,128)S(1)}, f32[8,128]{1,0:T(8,128)S(1)}, u32[]{:S(2)}, u32[]{:S(2)}) collective-permute-start(f32[8,128]{1,0:T(8,128)S(1)} %get-tuple-element.82.refs_3_.refs_4_), channel_id=1, source_target_pairs={{0,2},{1,3},{2,0},{3,1},{4,6},{5,7},{6,4},{7,5},{8,10},{9,11},{10,... | collective-permute-start | bytes 12296 | tf_op jit(solution)/shard_map/ppermute | solution.py:29
  57.8 2.4 %collective-permute-start.24 = (f32[8,128]{1,0:T(8,128)S(1)}, f32[8,128]{1,0:T(8,128)S(1)}, u32[]{:S(2)}, u32[]{:S(2)}) collective-permute-start(f32[8,128]{1,0:T(8,128)S(1)} %get-tuple-element.82.refs_3_.refs_4_), channel_id=1, source_target_pairs={{0,1},{1,0},{2,3},{3,2},{4,5},{5,4},{6,7},{7,6},{8,9},{9,8},{10,11... | collective-permute-start | bytes 12296 | tf_op jit(solution)/shard_map/ppermute | solution.py:29
  61.1 8.5 %collective-permute-start.25 = (bf16[64,1024]{1,0:T(8,128)(2,1)S(1)}, bf16[64,1024]{1,0:T(8,128)(2,1)S(1)}, u32[]{:S(2)}, u32[]{:S(2)}) collective-permute-start(bf16[64,1024]{1,0:T(8,128)(2,1)S(1)} %get-tuple-element.86.refs_0_), channel_id=1, source_target_pairs={{0,12},{4,8},{8,4},{12,0},{1,13},{5,9},{9,5},{13,1},{2,14},{6,10},... | collective-permute-start | bytes 393224 | tf_op jit(solution)/shard_map/ppermute | solution.py:29
  63.8 12.2 %collective-permute-start.26 = (bf16[64,1024]{1,0:T(8,128)(2,1)S(1)}, bf16[64,1024]{1,0:T(8,128)(2,1)S(1)}, u32[]{:S(2)}, u32[]{:S(2)}) collective-permute-start(bf16[64,1024]{1,0:T(8,128)(2,1)S(1)} %get-tuple-element.87), channel_id=1, source_target_pairs={{0,8},{4,12},{8,0},{12,4},{1,9},{5,13},{9,1},{13,5},{2,10},{6,14},... | collective-permute-start | bytes 393224 | tf_op jit(solution)/shard_map/ppermute | solution.py:29
  64.9 11.1 %collective-permute-start.27 = (bf16[64,1024]{1,0:T(8,128)(2,1)S(1)}, bf16[64,1024]{1,0:T(8,128)(2,1)S(1)}, u32[]{:S(2)}, u32[]{:S(2)}) collective-permute-start(bf16[64,1024]{1,0:T(8,128)(2,1)S(1)} %get-tuple-element.89), channel_id=1, source_target_pairs={{0,4},{4,0},{8,12},{12,8},{1,5},{5,1},{9,13},{13,9},{2,6},{6,2},{1... | collective-permute-start | bytes 393224 | tf_op jit(solution)/shard_map/ppermute | solution.py:29
  (2 other events, 1.3 us)

commit v18 on v17

--- a/solution.py
+++ b/solution.py
@@ -600,8 +600,8 @@
     if direct and blocks == 4:
         chunks = [
             [(0, 0, slots), (1, 0, slots)],
+            [(3, 0, slots)],
             [(2, 0, slots)],
-            [(3, 0, slots)],
         ]
     else:
         chunks = [[(d, first, some) for d in range(blocks)] for first in (0, some)]
@@ -653,7 +653,7 @@
     sums = [swapped(sums, ("win", "freq"), peers, s) for s in reversed(range(peers))]
     after = []
     numbered = list(enumerate(chunks))
-    for group in (numbered[:0:-1], numbered[:1]):
+    for group in (numbered[1:], numbered[:1]):
         grads = gradients(scal, lag_total, group, after, sums, [corrs[q] for q, _ in group], observed)
         pieces = [p for _, some_pieces in group for p in some_pieces]
         after = [grads[0]]

time: 77.3 us -> 76.5 us (0.990)
  transfers between devices with their start and end apart: 28 -> 28, of which waited for: 14 -> 13; matrix products, arithmetic and copies ran while one was open for 0% -> 0% of each run, Pallas kernels for 24% -> 25%
where the time goes in v18:
time: 76.5 us; the launch traced here: 76.2 us
  starting transfers between devices  24.3 us (32%)
  waiting for transfers between devices  23.5 us (31%)
  Pallas kernels  23 us (30%)
  local copies, waits for them, and re-layouts  4 us (5%)
  between operations  1.46 us (2%)
    ppermute x28, starting transfers between devices, swapped(): return lax.ppermute(value, axis, [(i, i ^ step) for i in range(size)])  24.3 us
    ppermute x28, waiting for transfers between devices, swapped(): return lax.ppermute(value, axis, [(i, i ^ step) for i in range(size)])  23.5 us
    pallas_call x2, Pallas kernels, cross_lag_parts(): pl.pallas_call(functools.partial(cross_lags_kernel, geometry, split, len(...  3.6 us
    pallas_call x1, Pallas kernels, normed_rows(): pl.pallas_call(functools.partial(normed_kernel, lag_total, chunks, len(su...  3.22 us
    pallas_call x1, Pallas kernels, gather_own(): pl.pallas_call(functools.partial(own_kernel, classes, parts), out_shape=[...  3.07 us
    unnamed x12, local copies, waits for them, and re-layouts  2.68 us
    pallas_call x1, Pallas kernels, lag_parts(): pl.pallas_call(functools.partial(lags_kernel, geometry, split, len(after)...  2.43 us
    pallas_call x3, Pallas kernels, lag_stats(): pl.pallas_call(functools.partial(stats_kernel, scale, q, pieces, len(more...  2.22 us
  transfers between devices with their start and end apart: 28, of which 13 were waited for; matrix products, arithmetic and copies ran while one was open for 0% of the time, Pallas kernels for 25%

profile of v18, /device:TPU:0, one launch (start us, length us, event | category | flops | bytes accessed | tf_op | source)
XLA Modules:
  0.0 76.2 jit_solution(11157741909954818964)
XLA Ops:
  0.7 1.3 %constant_dynamic-slice_fusion = (bf16[1,2,128,1024]{3,2,1,0:T(8,128)(2,1)S(1)}, bf16[1,2,128,1024]{3,2,1,0:T(8,128)(2,1)S(1)}) fusion(bf16[1,2,128,2048]{3,2,1,0:T(8,128)(2,1)} %param.8, s32[]{:T(128)S(6)} %select_n.7, s32[]{:T(128)S(6)} %select_n.6), kind=kLoop, calls=%fused_computation | loop fusion | bytes 2097160 | tf_op jit(solution)/shard_map/dynamic_slice | solution.py:583
  2.0 3.0 %collective-permute-start = (bf16[1,2,128,1024]{3,2,1,0:T(8,128)(2,1)S(1)}, bf16[1,2,128,1024]{3,2,1,0:T(8,128)(2,1)S(1)}, u32[]{:S(2)}, u32[]{:S(2)}) collective-permute-start(bf16[1,2,128,1024]{3,2,1,0:T(8,128)(2,1)S(1)} %get-tuple-element.90), channel_id=1, source_target_pairs={{0,2},{2,0},{1,3},{3,1},{4,6},{6,4},{5,7},{7,5},{8,10},{10,8},{9,1... | collective-permute-start | bytes 1572872 | tf_op jit(solution)/shard_map/ppermute | solution.py:29
  8.3 1.2 %index.1 = (s32[128]{0:T(128)S(1)}, s32[1,64]{1,0:T(1,128)S(1)}, s32[1,64]{1,0:T(1,128)S(1)}, s32[1,64]{1,0:T(1,128)S(1)}, s32[1,64]{1,0:T(1,128)S(1)}, /*index=5*/s32[4,64]{1,0:T(4,128)S(1)}) custom-call(s32[1]{0:T(128)S(6)} %copy.10.refs_0_, s32[4]{0:T(128)S(1)} %copy-done.4, s32[4]{0:T(128)S(1)} %bitcast.1, s32[4,64]{1,0:T(4,128)S(1)} %copy-done.2, ...), custom_call_target="tpu_custom_call" | custom-call | flops 1 | bytes 1 | tf_op jit(solution)/shard_map/index/pallas_call | solution.py:92
  9.5 3.7 %collective-permute-start.1 = (s32[1,64]{1,0:T(1,128)S(1)}, s32[1,64]{1,0:T(1,128)S(1)}, u32[]{:S(2)}, u32[]{:S(2)}) collective-permute-start(s32[1,64]{1,0:T(1,128)S(1)} %get-tuple-element.47), channel_id=1, source_target_pairs={{0,12},{4,8},{8,4},{12,0},{1,13},{5,9},{9,5},{13,1},{2,14},{6,10},... | collective-permute-start | bytes 776 | tf_op jit(solution)/shard_map/ppermute | solution.py:29
  13.2 0.8 %collective-permute-start.3 = (s32[1,64]{1,0:T(1,128)S(1)}, s32[1,64]{1,0:T(1,128)S(1)}, u32[]{:S(2)}, u32[]{:S(2)}) collective-permute-start(s32[1,64]{1,0:T(1,128)S(1)} %get-tuple-element.49), channel_id=1, source_target_pairs={{0,4},{4,0},{8,12},{12,8},{1,5},{5,1},{9,13},{13,9},{2,6},{6,2},{1... | collective-permute-start | bytes 776 | tf_op jit(solution)/shard_map/ppermute | solution.py:29
  14.9 2.7 %collective-permute-done.2.refs_3_.refs_1_ = s32[1,64]{1,0:T(1,128)S(1)} collective-permute-done((s32[1,64]{1,0:T(1,128)S(1)}, s32[1,64]{1,0:T(1,128)S(1)}, u32[]{:S(2)}, u32[]{:S(2)}) %collective-permute-start.2) | collective-permute-done | bytes 288 | tf_op jit(solution)/shard_map/ppermute | solution.py:29
  17.7 1.6 %rows.1 = (bf16[1,2,64,1024]{3,2,1,0:T(8,128)(2,1)S(1)}, bf16[1,2,64,1024]{3,2,1,0:T(8,128)(2,1)S(1)}, bf16[1,2,64,1024]{3,2,1,0:T(8,128)(2,1)S(1)}, bf16[1,2,64...) custom-call(s32[128]{0:T(128)S(1)} %get-tuple-element.46.scal, ...), custom_call_target="tpu_custom_call" | custom-call | flops 1 | bytes 1 | tf_op jit(solution)/shard_map/rows/pallas_call | solution.py:175
  19.2 1.1 %collective-permute-start.4 = (bf16[1,2,64,1024]{3,2,1,0:T(8,128)(2,1)S(1)}, bf16[1,2,64,1024]{3,2,1,0:T(8,128)(2,1)S(1)}, u32[]{:S(2)}, u32[]{:S(2)}) collective-permute-start(bf16[1,2,64,1024]{3,2,1,0:T(8,128)(2,1)S(1)} %get-tuple-element.52), channel_id=1, source_target_pairs={{0,4},{4,0},{8,12},{12,8},{1,5},{5,1},{9,13},{13,9},{2,6},{6,2},{1... | collective-permute-start | bytes 786440 | tf_op jit(solution)/shard_map/ppermute | solution.py:29
  20.4 2.5 %collective-permute-start.14 = (bf16[1,2,64,1024]{3,2,1,0:T(8,128)(2,1)S(1)}, bf16[1,2,64,1024]{3,2,1,0:T(8,128)(2,1)S(1)}, u32[]{:S(2)}, u32[]{:S(2)}) collective-permute-start(bf16[1,2,64,1024]{3,2,1,0:T(8,128)(2,1)S(1)} %get-tuple-element.69), channel_id=1, source_target_pairs={{0,12},{4,8},{8,4},{12,0},{1,13},{5,9},{9,5},{13,1},{2,14},{6,10},... | collective-permute-start | bytes 786440 | tf_op jit(solution)/shard_map/ppermute | solution.py:29
  23.0 3.1 %own.1 = (bf16[4,1,2,64,1024]{4,3,2,1,0:T(8,128)(2,1)S(1)}, bf16[8,256,1024]{2,1,0:T(8,128)(2,1)S(1)}) custom-call(s32[128]{0:T(128)S(1)} %get-tuple-element.46.scal, bf16[1,2,128,1024]{3,2,1,0:T(8,128)(2,1)S(1)} %get-tuple-element.53.kept, s32[4,64]{1,0:T(4,128)S(1)} %get-tuple-element.54.rec_ids, f32[2,56,1024]{2,1,0:T(8,128)S(1)} %copy-done.1), custom_call_target="tpu_custom_call" | custom-call | flops 1 | bytes 1 | tf_op jit(solution)/shard_map/own/pallas_call | solution.py:204
  26.0 1.1 %collective-permute-done.4.refs_1_ = bf16[1,2,64,1024]{3,2,1,0:T(8,128)(2,1)S(1)} collective-permute-done((bf16[1,2,64,1024]{3,2,1,0:T(8,128)(2,1)S(1)}, bf16[1,2,64,1024]{3,2,1,0:T(8,128)(2,1)S(1)}, u32[]{:S(2)}, u32[]{:S(2)}) %collective-permute-start.4) | collective-permute-done | bytes 262176 | tf_op jit(solution)/shard_map/ppermute | solution.py:29
  27.4 2.4 %lags.1 = (f32[2,128,1024]{2,1,0:T(8,128)S(1)}, bf16[2,16,1024]{2,1,0:T(8,128)(2,1)S(1)}, bf16[2,16,1024]{2,1,0:T(8,128)(2,1)S(1)}, bf16[2,16,1024]{2,1,0:T(8,12...) custom-call(s32[128]{0:T(128)S(1)} %get-tuple-element.46.scal, ...), custom_call_target="tpu_custom_call" | custom-call | flops 20000000000 | bytes 1048576 | tf_op jit(solution)/shard_map/lags/pallas_call | solution.py:331
  32.9 0.7 collective-permute-done.11.refs_7_
  33.8 0.8 %cores.3 = (f32[128,1024]{1,0:T(8,128)S(1)}, bf16[128,1024]{1,0:T(8,128)(2,1)S(1)}) custom-call(s32[128]{0:T(128)S(1)} %get-tuple-element.46.scal, f32[2,128,1024]{2,1,0:T(8,128)S(1)} %get-tuple-element.57.refs_0_, bf16[2,16,1024]{2,1,0:T(8,128)(2,1)S(1)} %collective-permute-done.5.refs_1_, bf16[2,16,1024]{2,1,0:T(8,128)(2,1)S(1)} %collective-permute-done.6.refs_2_, ...), custom_call_target="tpu_custom_call" | custom-call | flops 1 | bytes 1 | tf_op jit(solution)/shard_map/cores/pallas_call | solution.py:394
  34.7 1.6 %collective-permute-start.13 = (bf16[128,1024]{1,0:T(8,128)(2,1)S(1)}, bf16[128,1024]{1,0:T(8,128)(2,1)S(1)}, u32[]{:S(2)}, u32[]{:S(2)}) collective-permute-start(bf16[128,1024]{1,0:T(8,128)(2,1)S(1)} %get-tuple-element.67), channel_id=1, source_target_pairs={{0,2},{2,0},{1,3},{3,1},{4,6},{6,4},{5,7},{7,5},{8,10},{10,8},{9,1... | collective-permute-start | bytes 786440 | tf_op jit(solution)/shard_map/ppermute | solution.py:29
  36.2 1.8 %cross_lags.2 = (f32[2,64,1024]{2,1,0:T(8,128)S(1)}, bf16[2,32,1024]{2,1,0:T(8,128)(2,1)S(1)}, bf16[2,32,1024]{2,1,0:T(8,128)(2,1)S(1)}) custom-call(s32[128]{0:T(128)S(1)} %get-tuple-element.46.scal, f32[1]{0:T(128)} %constant.3.clone.1.weight, f32[128,1024]{1,0:T(8,128)S(1)} %get-tuple-element.66.refs_0_, ...), custom_call_target="tpu_custom_call" | custom-call | flops 1 | bytes 1 | tf_op jit(solution)/shard_map/cross_lags/pallas_call | solution.py:358
  38.6 6.4 %collective-permute-done.18.refs_0_ = bf16[1,2,64,1024]{3,2,1,0:T(8,128)(2,1)S(1)} collective-permute-done((bf16[1,2,64,1024]{3,2,1,0:T(8,128)(2,1)S(1)}, bf16[1,2,64,1024]{3,2,1,0:T(8,128)(2,1)S(1)}, u32[]{:S(2)}, u32[]{:S(2)}) %collective-permute-start.18) | collective-permute-done | bytes 262176 | tf_op jit(solution)/shard_map/ppermute | solution.py:29
  45.0 1.8 %cross_lags.3 = (f32[2,64,1024]{2,1,0:T(8,128)S(1)}, bf16[2,32,1024]{2,1,0:T(8,128)(2,1)S(1)}, bf16[2,32,1024]{2,1,0:T(8,128)(2,1)S(1)}) custom-call(s32[128]{0:T(128)S(1)} %get-tuple-element.46.scal, f32[1]{0:T(128)} %constant.3.clone.1.weight, bf16[1,2,64,1024]{3,2,1,0:T(8,128)(2,1)S(1)} %collective-permute-done.18.refs_0_, ...), custom_call_target="tpu_custom_call" | custom-call | flops 20000000000 | bytes 1048576 | tf_op jit(solution)/shard_map/cross_lags/pallas_call | solution.py:358
  48.0 1.6 %collective-permute-start.17 = (bf16[64,1024]{1,0:T(8,128)(2,1)S(1)}, bf16[64,1024]{1,0:T(8,128)(2,1)S(1)}, u32[]{:S(2)}, u32[]{:S(2)}) collective-permute-start(bf16[64,1024]{1,0:T(8,128)(2,1)S(1)} %get-tuple-element.74), channel_id=1, source_target_pairs={{0,2},{2,0},{1,3},{3,1},{4,6},{6,4},{5,7},{7,5},{8,10},{10,8},{9,1... | collective-permute-start | bytes 393224 | tf_op jit(solution)/shard_map/ppermute | solution.py:29
  50.8 0.8 %stats.3 = (f32[128,1024]{1,0:T(8,128)S(1)}, f32[8,128]{1,0:T(8,128)S(1)}) custom-call(s32[128]{0:T(128)S(1)} %get-tuple-element.46.scal, f32[128,1024]{1,0:T(8,128)S(1)} %get-tuple-element.66.refs_0_, bf16[128,1024]{1,0:T(8,128)(2,1)S(1)} %collective-permute-done.13.refs_1_.refs_0_, f32[4,64,1024]{2,1,0:T(8,128)S(1)} %copy-done, f32[4,64,1024]{2,1,0:T(8,128)S(1)} %copy-done), custom_call_target="tpu_custom_call" | custom-call | flops 1 | bytes 1 | tf_op jit(solution)/shard_map/stats/pallas_call | solution.py:449
  51.6 2.8 %collective-permute-done.17.refs_2_ = bf16[64,1024]{1,0:T(8,128)(2,1)S(1)} collective-permute-done((bf16[64,1024]{1,0:T(8,128)(2,1)S(1)}, bf16[64,1024]{1,0:T(8,128)(2,1)S(1)}, u32[]{:S(2)}, u32[]{:S(2)}) %collective-permute-start.17) | collective-permute-done | bytes 131104 | tf_op jit(solution)/shard_map/ppermute | solution.py:29
  55.1 1.2 %collective-permute-done.21.refs_2_ = bf16[64,1024]{1,0:T(8,128)(2,1)S(1)} collective-permute-done((bf16[64,1024]{1,0:T(8,128)(2,1)S(1)}, bf16[64,1024]{1,0:T(8,128)(2,1)S(1)}, u32[]{:S(2)}, u32[]{:S(2)}) %collective-permute-start.21) | collective-permute-done | bytes 131104 | tf_op jit(solution)/shard_map/ppermute | solution.py:29
  57.4 1.2 %collective-permute-start.23 = (f32[8,128]{1,0:T(8,128)S(1)}, f32[8,128]{1,0:T(8,128)S(1)}, u32[]{:S(2)}, u32[]{:S(2)}) collective-permute-start(f32[8,128]{1,0:T(8,128)S(1)} %get-tuple-element.82.refs_3_.refs_4_), channel_id=1, source_target_pairs={{0,2},{1,3},{2,0},{3,1},{4,6},{5,7},{6,4},{7,5},{8,10},{9,11},{10,... | collective-permute-start | bytes 12296 | tf_op jit(solution)/shard_map/ppermute | solution.py:29
  59.0 1.2 %collective-permute-done.22.refs_0_.refs_1_ = f32[8,128]{1,0:T(8,128)S(1)} collective-permute-done((f32[8,128]{1,0:T(8,128)S(1)}, f32[8,128]{1,0:T(8,128)S(1)}, u32[]{:S(2)}, u32[]{:S(2)}) %collective-permute-start.22) | collective-permute-done | bytes 4128 | tf_op jit(solution)/shard_map/ppermute | solution.py:29
  60.1 0.9 %collective-permute-done.23.refs_1_.refs_2_ = f32[8,128]{1,0:T(8,128)S(1)} collective-permute-done((f32[8,128]{1,0:T(8,128)S(1)}, f32[8,128]{1,0:T(8,128)S(1)}, u32[]{:S(2)}, u32[]{:S(2)}) %collective-permute-start.23) | collective-permute-done | bytes 4128 | tf_op jit(solution)/shard_map/ppermute | solution.py:29
  61.0 0.8 %gradient.2 = (bf16[64,1024]{1,0:T(8,128)(2,1)S(1)}, bf16[64,1024]{1,0:T(8,128)(2,1)S(1)}) custom-call(s32[128]{0:T(128)S(1)} %get-tuple-element.46.scal, f32[8,128]{1,0:T(8,128)S(1)} %collective-permute-done.22.refs_0_.refs_1_, f32[8,128]{1,0:T(8,128)S(1)} %collective-permute-done.23.refs_1_.refs_2_, f32[8,128]{1,0:T(8,128)S(1)} %collective-permute-done.24.refs_2_.refs_3_, ...), custom_call_target="tpu_custom_call" | custom-call | flops 1 | bytes 1 | tf_op jit(solution)/shard_map/gradient/pallas_call | solution.py:498
  61.9 2.5 %collective-permute-start.25 = (bf16[64,1024]{1,0:T(8,128)(2,1)S(1)}, bf16[64,1024]{1,0:T(8,128)(2,1)S(1)}, u32[]{:S(2)}, u32[]{:S(2)}) collective-permute-start(bf16[64,1024]{1,0:T(8,128)(2,1)S(1)} %get-tuple-element.86.refs_0_), channel_id=1, source_target_pairs={{0,12},{4,8},{8,4},{12,0},{1,13},{5,9},{9,5},{13,1},{2,14},{6,10},... | collective-permute-start | bytes 393224 | tf_op jit(solution)/shard_map/ppermute | solution.py:29
  64.4 0.8 %gradient.3 = (bf16[64,1024]{1,0:T(8,128)(2,1)S(1)}, bf16[64,1024]{1,0:T(8,128)(2,1)S(1)}) custom-call(s32[128]{0:T(128)S(1)} %get-tuple-element.46.scal, bf16[64,1024]{1,0:T(8,128)(2,1)S(1)} %get-tuple-element.86.refs_0_, f32[8,128]{1,0:T(8,128)S(1)} %collective-permute-done.22.refs_0_.refs_1_, f32[8,128]{1,0:T(8,128)S(1)} %collective-permute-done.23.refs_1_.refs_2_, ...), custom_call_target="tpu_custom_call" | custom-call | flops 1 | bytes 1 | tf_op jit(solution)/shard_map/gradient/pallas_call | solution.py:498
  65.2 2.0 %collective-permute-start.27 = (bf16[64,1024]{1,0:T(8,128)(2,1)S(1)}, bf16[64,1024]{1,0:T(8,128)(2,1)S(1)}, u32[]{:S(2)}, u32[]{:S(2)}) collective-permute-start(bf16[64,1024]{1,0:T(8,128)(2,1)S(1)} %get-tuple-element.89), channel_id=1, source_target_pairs={{0,4},{4,0},{8,12},{12,8},{1,5},{5,1},{9,13},{13,9},{2,6},{6,2},{1... | collective-permute-start | bytes 393224 | tf_op jit(solution)/shard_map/ppermute | solution.py:29
  67.2 3.2 %normed.1 = f32[4,64,1024]{2,1,0:T(8,128)} custom-call(s32[128]{0:T(128)S(1)} %get-tuple-element.46.scal, f32[8,128]{1,0:T(8,128)S(1)} %collective-permute-done.22.refs_0_.refs_1_, f32[8,128]{1,0:T(8,128)S(1)} %collective-permute-done.23.refs_1_.refs_2_, f32[8,128]{1,0:T(8,128)S(1)} %collective-permute-done.24.refs_2_.refs_3_, ...), custom_call_target="tpu_custom_call" | custom-call | flops 1 | bytes 1 | tf_op jit(solution)/shard_map/normed/pallas_call | solution.py:529
  70.4 4.7 %collective-permute-done.26.refs_5_ = bf16[64,1024]{1,0:T(8,128)(2,1)S(1)} collective-permute-done((bf16[64,1024]{1,0:T(8,128)(2,1)S(1)}, bf16[64,1024]{1,0:T(8,128)(2,1)S(1)}, u32[]{:S(2)}, u32[]{:S(2)}) %collective-permute-start.26) | collective-permute-done | bytes 131104 | tf_op jit(solution)/shard_map/ppermute | solution.py:29
  75.2 1.1 %adjoint.1 = f32[128,1024]{1,0:T(8,128)} custom-call(s32[1,64]{1,0:T(1,128)S(1)} %collective-permute-done.1.refs_2_.refs_0_, s32[1,64]{1,0:T(1,128)S(1)} %collective-permute-done.2.refs_3_.refs_1_, s32[1,64]{1,0:T(1,128)S(1)} %get-tuple-element.50.refs_5_.refs_2_, s32[1,64]{1,0:T(1,128)S(1)} %collective-permute-done.3.refs_4_.refs_3_, ...), custom_call_target="tpu_custom_call" | custom-call | flops 1 | bytes 1 | tf_op jit(solution)/shard_map/adjoint/pallas_call | solution.py:553
  (55 shorter events, 12.4 us)
Async XLA Ops:
  0.6 22.3 %copy-start.1 = (f32[2,56,1024]{2,1,0:T(8,128)S(1)}, f32[2,56,1024]{2,1,0:T(8,128)}, u32[]{:S(2)}) copy-start(f32[2,56,1024]{2,1,0:T(8,128)} %constant.16.clone.trig) | copy-start | bytes 1376260
  2.0 15.7 %collective-permute-start = (bf16[1,2,128,1024]{3,2,1,0:T(8,128)(2,1)S(1)}, bf16[1,2,128,1024]{3,2,1,0:T(8,128)(2,1)S(1)}, u32[]{:S(2)}, u32[]{:S(2)}) collective-permute-start(bf16[1,2,128,1024]{3,2,1,0:T(8,128)(2,1)S(1)} %get-tuple-element.90), channel_id=1, source_target_pairs={{0,2},{2,0},{1,3},{3,1},{4,6},{6,4},{5,7},{7,5},{8,10},{10,8},{9,1... | collective-permute-start | bytes 1572872 | tf_op jit(solution)/shard_map/ppermute | solution.py:29
  5.6 0.7 copy-start.2
  6.3 0.7 copy-start.3
  9.5 5.4 %collective-permute-start.1 = (s32[1,64]{1,0:T(1,128)S(1)}, s32[1,64]{1,0:T(1,128)S(1)}, u32[]{:S(2)}, u32[]{:S(2)}) collective-permute-start(s32[1,64]{1,0:T(1,128)S(1)} %get-tuple-element.47), channel_id=1, source_target_pairs={{0,12},{4,8},{8,4},{12,0},{1,13},{5,9},{9,5},{13,1},{2,14},{6,10},... | collective-permute-start | bytes 776 | tf_op jit(solution)/shard_map/ppermute | solution.py:29
  13.2 4.4 %collective-permute-start.2 = (s32[1,64]{1,0:T(1,128)S(1)}, s32[1,64]{1,0:T(1,128)S(1)}, u32[]{:S(2)}, u32[]{:S(2)}) collective-permute-start(s32[1,64]{1,0:T(1,128)S(1)} %get-tuple-element.48), channel_id=1, source_target_pairs={{0,8},{4,12},{8,0},{12,4},{1,9},{5,13},{9,1},{13,5},{2,10},{6,14},... | collective-permute-start | bytes 776 | tf_op jit(solution)/shard_map/ppermute | solution.py:29
  13.2 4.4 %collective-permute-start.3 = (s32[1,64]{1,0:T(1,128)S(1)}, s32[1,64]{1,0:T(1,128)S(1)}, u32[]{:S(2)}, u32[]{:S(2)}) collective-permute-start(s32[1,64]{1,0:T(1,128)S(1)} %get-tuple-element.49), channel_id=1, source_target_pairs={{0,4},{4,0},{8,12},{12,8},{1,5},{5,1},{9,13},{13,9},{2,6},{6,2},{1... | collective-permute-start | bytes 776 | tf_op jit(solution)/shard_map/ppermute | solution.py:29
  19.2 7.9 %collective-permute-start.4 = (bf16[1,2,64,1024]{3,2,1,0:T(8,128)(2,1)S(1)}, bf16[1,2,64,1024]{3,2,1,0:T(8,128)(2,1)S(1)}, u32[]{:S(2)}, u32[]{:S(2)}) collective-permute-start(bf16[1,2,64,1024]{3,2,1,0:T(8,128)(2,1)S(1)} %get-tuple-element.52), channel_id=1, source_target_pairs={{0,4},{4,0},{8,12},{12,8},{1,5},{5,1},{9,13},{13,9},{2,6},{6,2},{1... | collective-permute-start | bytes 786440 | tf_op jit(solution)/shard_map/ppermute | solution.py:29
  20.4 15.8 %collective-permute-start.14 = (bf16[1,2,64,1024]{3,2,1,0:T(8,128)(2,1)S(1)}, bf16[1,2,64,1024]{3,2,1,0:T(8,128)(2,1)S(1)}, u32[]{:S(2)}, u32[]{:S(2)}) collective-permute-start(bf16[1,2,64,1024]{3,2,1,0:T(8,128)(2,1)S(1)} %get-tuple-element.69), channel_id=1, source_target_pairs={{0,12},{4,8},{8,4},{12,0},{1,13},{5,9},{9,5},{13,1},{2,14},{6,10},... | collective-permute-start | bytes 786440 | tf_op jit(solution)/shard_map/ppermute | solution.py:29
  22.8 22.1 %collective-permute-start.18 = (bf16[1,2,64,1024]{3,2,1,0:T(8,128)(2,1)S(1)}, bf16[1,2,64,1024]{3,2,1,0:T(8,128)(2,1)S(1)}, u32[]{:S(2)}, u32[]{:S(2)}) collective-permute-start(bf16[1,2,64,1024]{3,2,1,0:T(8,128)(2,1)S(1)} %get-tuple-element.76), channel_id=1, source_target_pairs={{0,8},{4,12},{8,0},{12,4},{1,9},{5,13},{9,1},{13,5},{2,10},{6,14},... | collective-permute-start | bytes 786440 | tf_op jit(solution)/shard_map/ppermute | solution.py:29
  29.8 1.3 %collective-permute-start.5 = (bf16[2,16,1024]{2,1,0:T(8,128)(2,1)S(1)}, bf16[2,16,1024]{2,1,0:T(8,128)(2,1)S(1)}, u32[]{:S(2)}, u32[]{:S(2)}) collective-permute-start(bf16[2,16,1024]{2,1,0:T(8,128)(2,1)S(1)} %get-tuple-element.58), channel_id=1, source_target_pairs={{0,1},{1,0},{2,3},{3,2},{4,5},{5,4},{6,7},{7,6},{8,9},{9,8},{10,11... | collective-permute-start | bytes 196616 | tf_op jit(solution)/shard_map/ppermute | solution.py:29
  29.9 1.4 %collective-permute-start.6 = (bf16[2,16,1024]{2,1,0:T(8,128)(2,1)S(1)}, bf16[2,16,1024]{2,1,0:T(8,128)(2,1)S(1)}, u32[]{:S(2)}, u32[]{:S(2)}) collective-permute-start(bf16[2,16,1024]{2,1,0:T(8,128)(2,1)S(1)} %get-tuple-element.59), channel_id=1, source_target_pairs={{0,1},{1,0},{2,3},{3,2},{4,5},{5,4},{6,7},{7,6},{8,9},{9,8},{10,11... | collective-permute-start | bytes 196616 | tf_op jit(solution)/shard_map/ppermute | solution.py:29
  30.4 1.3 %collective-permute-start.7 = (bf16[2,16,1024]{2,1,0:T(8,128)(2,1)S(1)}, bf16[2,16,1024]{2,1,0:T(8,128)(2,1)S(1)}, u32[]{:S(2)}, u32[]{:S(2)}) collective-permute-start(bf16[2,16,1024]{2,1,0:T(8,128)(2,1)S(1)} %get-tuple-element.60), channel_id=1, source_target_pairs={{0,1},{1,0},{2,3},{3,2},{4,5},{5,4},{6,7},{7,6},{8,9},{9,8},{10,11... | collective-permute-start | bytes 196616 | tf_op jit(solution)/shard_map/ppermute | solution.py:29
  31.2 1.3 %collective-permute-start.8 = (bf16[2,16,1024]{2,1,0:T(8,128)(2,1)S(1)}, bf16[2,16,1024]{2,1,0:T(8,128)(2,1)S(1)}, u32[]{:S(2)}, u32[]{:S(2)}) collective-permute-start(bf16[2,16,1024]{2,1,0:T(8,128)(2,1)S(1)} %get-tuple-element.61), channel_id=1, source_target_pairs={{0,1},{1,0},{2,3},{3,2},{4,5},{5,4},{6,7},{7,6},{8,9},{9,8},{10,11... | collective-permute-start | bytes 196616 | tf_op jit(solution)/shard_map/ppermute | solution.py:29
  31.3 1.3 %collective-permute-start.9 = (bf16[2,16,1024]{2,1,0:T(8,128)(2,1)S(1)}, bf16[2,16,1024]{2,1,0:T(8,128)(2,1)S(1)}, u32[]{:S(2)}, u32[]{:S(2)}) collective-permute-start(bf16[2,16,1024]{2,1,0:T(8,128)(2,1)S(1)} %get-tuple-element.62), channel_id=1, source_target_pairs={{0,1},{1,0},{2,3},{3,2},{4,5},{5,4},{6,7},{7,6},{8,9},{9,8},{10,11... | collective-permute-start | bytes 196616 | tf_op jit(solution)/shard_map/ppermute | solution.py:29
  31.7 1.3 %collective-permute-start.10 = (bf16[2,16,1024]{2,1,0:T(8,128)(2,1)S(1)}, bf16[2,16,1024]{2,1,0:T(8,128)(2,1)S(1)}, u32[]{:S(2)}, u32[]{:S(2)}) collective-permute-start(bf16[2,16,1024]{2,1,0:T(8,128)(2,1)S(1)} %get-tuple-element.63), channel_id=1, source_target_pairs={{0,1},{1,0},{2,3},{3,2},{4,5},{5,4},{6,7},{7,6},{8,9},{9,8},{10,11... | collective-permute-start | bytes 196616 | tf_op jit(solution)/shard_map/ppermute | solution.py:29
  32.4 1.3 %collective-permute-start.11 = (bf16[2,16,1024]{2,1,0:T(8,128)(2,1)S(1)}, bf16[2,16,1024]{2,1,0:T(8,128)(2,1)S(1)}, u32[]{:S(2)}, u32[]{:S(2)}) collective-permute-start(bf16[2,16,1024]{2,1,0:T(8,128)(2,1)S(1)} %get-tuple-element.64), channel_id=1, source_target_pairs={{0,1},{1,0},{2,3},{3,2},{4,5},{5,4},{6,7},{7,6},{8,9},{9,8},{10,11... | collective-permute-start | bytes 196616 | tf_op jit(solution)/shard_map/ppermute | solution.py:29
  32.6 1.3 %collective-permute-start.12 = (bf16[2,16,1024]{2,1,0:T(8,128)(2,1)S(1)}, bf16[2,16,1024]{2,1,0:T(8,128)(2,1)S(1)}, u32[]{:S(2)}, u32[]{:S(2)}) collective-permute-start(bf16[2,16,1024]{2,1,0:T(8,128)(2,1)S(1)} %get-tuple-element.65), channel_id=1, source_target_pairs={{0,1},{1,0},{2,3},{3,2},{4,5},{5,4},{6,7},{7,6},{8,9},{9,8},{10,11... | collective-permute-start | bytes 196616 | tf_op jit(solution)/shard_map/ppermute | solution.py:29
  34.7 12.7 %collective-permute-start.13 = (bf16[128,1024]{1,0:T(8,128)(2,1)S(1)}, bf16[128,1024]{1,0:T(8,128)(2,1)S(1)}, u32[]{:S(2)}, u32[]{:S(2)}) collective-permute-start(bf16[128,1024]{1,0:T(8,128)(2,1)S(1)} %get-tuple-element.67), channel_id=1, source_target_pairs={{0,2},{2,0},{1,3},{3,1},{4,6},{6,4},{5,7},{7,5},{8,10},{10,8},{9,1... | collective-permute-start | bytes 786440 | tf_op jit(solution)/shard_map/ppermute | solution.py:29
  38.0 9.3 %collective-permute-start.15 = (bf16[2,32,1024]{2,1,0:T(8,128)(2,1)S(1)}, bf16[2,32,1024]{2,1,0:T(8,128)(2,1)S(1)}, u32[]{:S(2)}, u32[]{:S(2)}) collective-permute-start(bf16[2,32,1024]{2,1,0:T(8,128)(2,1)S(1)} %get-tuple-element.71), channel_id=1, source_target_pairs={{0,1},{1,0},{2,3},{3,2},{4,5},{5,4},{6,7},{7,6},{8,9},{9,8},{10,11... | collective-permute-start | bytes 393224 | tf_op jit(solution)/shard_map/ppermute | solution.py:29
  38.2 12.6 %copy-start = (f32[4,64,1024]{2,1,0:T(8,128)S(1)}, f32[4,64,1024]{2,1,0:T(8,128)}, u32[]{:S(2)}) copy-start(f32[4,64,1024]{2,1,0:T(8,128)} %refs_7_.3) | copy-start | bytes 3145732
  38.2 9.2 %collective-permute-start.16 = (bf16[2,32,1024]{2,1,0:T(8,128)(2,1)S(1)}, bf16[2,32,1024]{2,1,0:T(8,128)(2,1)S(1)}, u32[]{:S(2)}, u32[]{:S(2)}) collective-permute-start(bf16[2,32,1024]{2,1,0:T(8,128)(2,1)S(1)} %get-tuple-element.72), channel_id=1, source_target_pairs={{0,1},{1,0},{2,3},{3,2},{4,5},{5,4},{6,7},{7,6},{8,9},{9,8},{10,11... | collective-permute-start | bytes 393224 | tf_op jit(solution)/shard_map/ppermute | solution.py:29
  46.8 2.8 %collective-permute-start.19 = (bf16[2,32,1024]{2,1,0:T(8,128)(2,1)S(1)}, bf16[2,32,1024]{2,1,0:T(8,128)(2,1)S(1)}, u32[]{:S(2)}, u32[]{:S(2)}) collective-permute-start(bf16[2,32,1024]{2,1,0:T(8,128)(2,1)S(1)} %get-tuple-element.78), channel_id=1, source_target_pairs={{0,1},{1,0},{2,3},{3,2},{4,5},{5,4},{6,7},{7,6},{8,9},{9,8},{10,11... | collective-permute-start | bytes 393224 | tf_op jit(solution)/shard_map/ppermute | solution.py:29
  46.9 2.7 %collective-permute-start.20 = (bf16[2,32,1024]{2,1,0:T(8,128)(2,1)S(1)}, bf16[2,32,1024]{2,1,0:T(8,128)(2,1)S(1)}, u32[]{:S(2)}, u32[]{:S(2)}) collective-permute-start(bf16[2,32,1024]{2,1,0:T(8,128)(2,1)S(1)} %get-tuple-element.79), channel_id=1, source_target_pairs={{0,1},{1,0},{2,3},{3,2},{4,5},{5,4},{6,7},{7,6},{8,9},{9,8},{10,11... | collective-permute-start | bytes 393224 | tf_op jit(solution)/shard_map/ppermute | solution.py:29
  48.0 6.4 %collective-permute-start.17 = (bf16[64,1024]{1,0:T(8,128)(2,1)S(1)}, bf16[64,1024]{1,0:T(8,128)(2,1)S(1)}, u32[]{:S(2)}, u32[]{:S(2)}) collective-permute-start(bf16[64,1024]{1,0:T(8,128)(2,1)S(1)} %get-tuple-element.74), channel_id=1, source_target_pairs={{0,2},{2,0},{1,3},{3,1},{4,6},{6,4},{5,7},{7,5},{8,10},{10,8},{9,1... | collective-permute-start | bytes 393224 | tf_op jit(solution)/shard_map/ppermute | solution.py:29
  50.2 6.2 %collective-permute-start.21 = (bf16[64,1024]{1,0:T(8,128)(2,1)S(1)}, bf16[64,1024]{1,0:T(8,128)(2,1)S(1)}, u32[]{:S(2)}, u32[]{:S(2)}) collective-permute-start(bf16[64,1024]{1,0:T(8,128)(2,1)S(1)} %get-tuple-element.81), channel_id=1, source_target_pairs={{0,2},{2,0},{1,3},{3,1},{4,6},{6,4},{5,7},{7,5},{8,10},{10,8},{9,1... | collective-permute-start | bytes 393224 | tf_op jit(solution)/shard_map/ppermute | solution.py:29
  57.1 3.1 %collective-permute-start.22 = (f32[8,128]{1,0:T(8,128)S(1)}, f32[8,128]{1,0:T(8,128)S(1)}, u32[]{:S(2)}, u32[]{:S(2)}) collective-permute-start(f32[8,128]{1,0:T(8,128)S(1)} %get-tuple-element.82.refs_3_.refs_4_), channel_id=1, source_target_pairs={{0,3},{1,2},{2,1},{3,0},{4,7},{5,6},{6,5},{7,4},{8,11},{9,10},{10,... | collective-permute-start | bytes 12296 | tf_op jit(solution)/shard_map/ppermute | solution.py:29
  57.4 3.6 %collective-permute-start.23 = (f32[8,128]{1,0:T(8,128)S(1)}, f32[8,128]{1,0:T(8,128)S(1)}, u32[]{:S(2)}, u32[]{:S(2)}) collective-permute-start(f32[8,128]{1,0:T(8,128)S(1)} %get-tuple-element.82.refs_3_.refs_4_), channel_id=1, source_target_pairs={{0,2},{1,3},{2,0},{3,1},{4,6},{5,7},{6,4},{7,5},{8,10},{9,11},{10,... | collective-permute-start | bytes 12296 | tf_op jit(solution)/shard_map/ppermute | solution.py:29
  58.7 2.4 %collective-permute-start.24 = (f32[8,128]{1,0:T(8,128)S(1)}, f32[8,128]{1,0:T(8,128)S(1)}, u32[]{:S(2)}, u32[]{:S(2)}) collective-permute-start(f32[8,128]{1,0:T(8,128)S(1)} %get-tuple-element.82.refs_3_.refs_4_), channel_id=1, source_target_pairs={{0,1},{1,0},{2,3},{3,2},{4,5},{5,4},{6,7},{7,6},{8,9},{9,8},{10,11... | collective-permute-start | bytes 12296 | tf_op jit(solution)/shard_map/ppermute | solution.py:29
  61.9 8.5 %collective-permute-start.25 = (bf16[64,1024]{1,0:T(8,128)(2,1)S(1)}, bf16[64,1024]{1,0:T(8,128)(2,1)S(1)}, u32[]{:S(2)}, u32[]{:S(2)}) collective-permute-start(bf16[64,1024]{1,0:T(8,128)(2,1)S(1)} %get-tuple-element.86.refs_0_), channel_id=1, source_target_pairs={{0,12},{4,8},{8,4},{12,0},{1,13},{5,9},{9,5},{13,1},{2,14},{6,10},... | collective-permute-start | bytes 393224 | tf_op jit(solution)/shard_map/ppermute | solution.py:29
  64.4 10.8 %collective-permute-start.26 = (bf16[64,1024]{1,0:T(8,128)(2,1)S(1)}, bf16[64,1024]{1,0:T(8,128)(2,1)S(1)}, u32[]{:S(2)}, u32[]{:S(2)}) collective-permute-start(bf16[64,1024]{1,0:T(8,128)(2,1)S(1)} %get-tuple-element.87), channel_id=1, source_target_pairs={{0,8},{4,12},{8,0},{12,4},{1,9},{5,13},{9,1},{13,5},{2,10},{6,14},... | collective-permute-start | bytes 393224 | tf_op jit(solution)/shard_map/ppermute | solution.py:29
  65.2 10.0 %collective-permute-start.27 = (bf16[64,1024]{1,0:T(8,128)(2,1)S(1)}, bf16[64,1024]{1,0:T(8,128)(2,1)S(1)}, u32[]{:S(2)}, u32[]{:S(2)}) collective-permute-start(bf16[64,1024]{1,0:T(8,128)(2,1)S(1)} %get-tuple-element.89), channel_id=1, source_target_pairs={{0,4},{4,0},{8,12},{12,8},{1,5},{5,1},{9,13},{13,9},{2,6},{6,2},{1... | collective-permute-start | bytes 393224 | tf_op jit(solution)/shard_map/ppermute | solution.py:29
  (2 other events, 1.3 us)

commit v19 on v18

--- a/solution.py
+++ b/solution.py
@@ -653,7 +653,7 @@
     sums = [swapped(sums, ("win", "freq"), peers, s) for s in reversed(range(peers))]
     after = []
     numbered = list(enumerate(chunks))
-    for group in (numbered[1:], numbered[:1]):
+    for group in (numbered[:0:-1], numbered[:1]):
         grads = gradients(scal, lag_total, group, after, sums, [corrs[q] for q, _ in group], observed)
         pieces = [p for _, some_pieces in group for p in some_pieces]
         after = [grads[0]]

time: 76.5 us -> 77.6 us (1.014)
  waiting for transfers between devices: 23.5 us -> 25.6 us
  starting transfers between devices: 24.3 us -> 23.4 us
    ppermute x28, waiting for transfers between devices: 23.5 us -> 25.6 us  [swapped(): return lax.ppermute(value, axis, [(i, i ^ step) for i in range(size)])]
    ppermute x28, starting transfers between devices: 24.3 us -> 23.4 us  [swapped(): return lax.ppermute(value, axis, [(i, i ^ step) for i in range(size)])]
  transfers between devices with their start and end apart: 28 -> 28, of which waited for: 13 -> 14; matrix products, arithmetic and copies ran while one was open for 0% -> 0% of each run, Pallas kernels for 25% -> 24%
where the time goes in v19:
time: 77.6 us; the launch traced here: 77.4 us
  waiting for transfers between devices  25.6 us (33%)
  starting transfers between devices  23.4 us (30%)
  Pallas kernels  23 us (30%)
  local copies, waits for them, and re-layouts  4 us (5%)
  between operations  1.46 us (2%)
    ppermute x28, waiting for transfers between devices, swapped(): return lax.ppermute(value, axis, [(i, i ^ step) for i in range(size)])  25.6 us
    ppermute x28, starting transfers between devices, swapped(): return lax.ppermute(value, axis, [(i, i ^ step) for i in range(size)])  23.4 us
    pallas_call x2, Pallas kernels, cross_lag_parts(): pl.pallas_call(functools.partial(cross_lags_kernel, geometry, split, len(...  3.6 us
    pallas_call x1, Pallas kernels, normed_rows(): pl.pallas_call(functools.partial(normed_kernel, lag_total, chunks, len(su...  3.22 us
    pallas_call x1, Pallas kernels, gather_own(): pl.pallas_call(functools.partial(own_kernel, classes, parts), out_shape=[...  3.07 us
    unnamed x12, local copies, waits for them, and re-layouts  2.68 us
    pallas_call x1, Pallas kernels, lag_parts(): pl.pallas_call(functools.partial(lags_kernel, geometry, split, len(after)...  2.43 us
    pallas_call x3, Pallas kernels, lag_stats(): pl.pallas_call(functools.partial(stats_kernel, scale, q, pieces, len(more...  2.22 us
  transfers between devices with their start and end apart: 28, of which 14 were waited for; matrix products, arithmetic and copies ran while one was open for 0% of the time, Pallas kernels for 24%

profile of v19, /device:TPU:0, one launch (start us, length us, event | category | flops | bytes accessed | tf_op | source)
XLA Modules:
  0.0 77.4 jit_solution(6725458813414621345)
XLA Ops:
  0.7 1.3 %constant_dynamic-slice_fusion = (bf16[1,2,128,1024]{3,2,1,0:T(8,128)(2,1)S(1)}, bf16[1,2,128,1024]{3,2,1,0:T(8,128)(2,1)S(1)}) fusion(bf16[1,2,128,2048]{3,2,1,0:T(8,128)(2,1)} %param.8, s32[]{:T(128)S(6)} %select_n.7, s32[]{:T(128)S(6)} %select_n.6), kind=kLoop, calls=%fused_computation | loop fusion | bytes 2097160 | tf_op jit(solution)/shard_map/dynamic_slice | solution.py:583
  2.0 3.0 %collective-permute-start = (bf16[1,2,128,1024]{3,2,1,0:T(8,128)(2,1)S(1)}, bf16[1,2,128,1024]{3,2,1,0:T(8,128)(2,1)S(1)}, u32[]{:S(2)}, u32[]{:S(2)}) collective-permute-start(bf16[1,2,128,1024]{3,2,1,0:T(8,128)(2,1)S(1)} %get-tuple-element.90), channel_id=1, source_target_pairs={{0,2},{2,0},{1,3},{3,1},{4,6},{6,4},{5,7},{7,5},{8,10},{10,8},{9,1... | collective-permute-start | bytes 1572872 | tf_op jit(solution)/shard_map/ppermute | solution.py:29
  8.3 1.2 %index.1 = (s32[128]{0:T(128)S(1)}, s32[1,64]{1,0:T(1,128)S(1)}, s32[1,64]{1,0:T(1,128)S(1)}, s32[1,64]{1,0:T(1,128)S(1)}, s32[1,64]{1,0:T(1,128)S(1)}, /*index=5*/s32[4,64]{1,0:T(4,128)S(1)}) custom-call(s32[1]{0:T(128)S(6)} %copy.10.refs_0_, s32[4]{0:T(128)S(1)} %copy-done.4, s32[4]{0:T(128)S(1)} %bitcast.1, s32[4,64]{1,0:T(4,128)S(1)} %copy-done.2, ...), custom_call_target="tpu_custom_call" | custom-call | flops 1 | bytes 1 | tf_op jit(solution)/shard_map/index/pallas_call | solution.py:92
  9.5 3.7 %collective-permute-start.1 = (s32[1,64]{1,0:T(1,128)S(1)}, s32[1,64]{1,0:T(1,128)S(1)}, u32[]{:S(2)}, u32[]{:S(2)}) collective-permute-start(s32[1,64]{1,0:T(1,128)S(1)} %get-tuple-element.47), channel_id=1, source_target_pairs={{0,12},{4,8},{8,4},{12,0},{1,13},{5,9},{9,5},{13,1},{2,14},{6,10},... | collective-permute-start | bytes 776 | tf_op jit(solution)/shard_map/ppermute | solution.py:29
  13.2 0.8 %collective-permute-start.3 = (s32[1,64]{1,0:T(1,128)S(1)}, s32[1,64]{1,0:T(1,128)S(1)}, u32[]{:S(2)}, u32[]{:S(2)}) collective-permute-start(s32[1,64]{1,0:T(1,128)S(1)} %get-tuple-element.49), channel_id=1, source_target_pairs={{0,4},{4,0},{8,12},{12,8},{1,5},{5,1},{9,13},{13,9},{2,6},{6,2},{1... | collective-permute-start | bytes 776 | tf_op jit(solution)/shard_map/ppermute | solution.py:29
  14.9 2.7 %collective-permute-done.2.refs_3_.refs_0_ = s32[1,64]{1,0:T(1,128)S(1)} collective-permute-done((s32[1,64]{1,0:T(1,128)S(1)}, s32[1,64]{1,0:T(1,128)S(1)}, u32[]{:S(2)}, u32[]{:S(2)}) %collective-permute-start.2) | collective-permute-done | bytes 288 | tf_op jit(solution)/shard_map/ppermute | solution.py:29
  17.7 1.6 %rows.1 = (bf16[1,2,64,1024]{3,2,1,0:T(8,128)(2,1)S(1)}, bf16[1,2,64,1024]{3,2,1,0:T(8,128)(2,1)S(1)}, bf16[1,2,64,1024]{3,2,1,0:T(8,128)(2,1)S(1)}, bf16[1,2,64...) custom-call(s32[128]{0:T(128)S(1)} %get-tuple-element.46.scal, ...), custom_call_target="tpu_custom_call" | custom-call | flops 1 | bytes 1 | tf_op jit(solution)/shard_map/rows/pallas_call | solution.py:175
  19.2 1.1 %collective-permute-start.4 = (bf16[1,2,64,1024]{3,2,1,0:T(8,128)(2,1)S(1)}, bf16[1,2,64,1024]{3,2,1,0:T(8,128)(2,1)S(1)}, u32[]{:S(2)}, u32[]{:S(2)}) collective-permute-start(bf16[1,2,64,1024]{3,2,1,0:T(8,128)(2,1)S(1)} %get-tuple-element.52), channel_id=1, source_target_pairs={{0,4},{4,0},{8,12},{12,8},{1,5},{5,1},{9,13},{13,9},{2,6},{6,2},{1... | collective-permute-start | bytes 786440 | tf_op jit(solution)/shard_map/ppermute | solution.py:29
  20.4 2.5 %collective-permute-start.14 = (bf16[1,2,64,1024]{3,2,1,0:T(8,128)(2,1)S(1)}, bf16[1,2,64,1024]{3,2,1,0:T(8,128)(2,1)S(1)}, u32[]{:S(2)}, u32[]{:S(2)}) collective-permute-start(bf16[1,2,64,1024]{3,2,1,0:T(8,128)(2,1)S(1)} %get-tuple-element.69), channel_id=1, source_target_pairs={{0,12},{4,8},{8,4},{12,0},{1,13},{5,9},{9,5},{13,1},{2,14},{6,10},... | collective-permute-start | bytes 786440 | tf_op jit(solution)/shard_map/ppermute | solution.py:29
  23.0 3.1 %own.1 = (bf16[4,1,2,64,1024]{4,3,2,1,0:T(8,128)(2,1)S(1)}, bf16[8,256,1024]{2,1,0:T(8,128)(2,1)S(1)}) custom-call(s32[128]{0:T(128)S(1)} %get-tuple-element.46.scal, bf16[1,2,128,1024]{3,2,1,0:T(8,128)(2,1)S(1)} %get-tuple-element.53.kept, s32[4,64]{1,0:T(4,128)S(1)} %get-tuple-element.54.rec_ids, f32[2,56,1024]{2,1,0:T(8,128)S(1)} %copy-done.1), custom_call_target="tpu_custom_call" | custom-call | flops 1 | bytes 1 | tf_op jit(solution)/shard_map/own/pallas_call | solution.py:204
  26.0 1.1 %collective-permute-done.4.refs_1_ = bf16[1,2,64,1024]{3,2,1,0:T(8,128)(2,1)S(1)} collective-permute-done((bf16[1,2,64,1024]{3,2,1,0:T(8,128)(2,1)S(1)}, bf16[1,2,64,1024]{3,2,1,0:T(8,128)(2,1)S(1)}, u32[]{:S(2)}, u32[]{:S(2)}) %collective-permute-start.4) | collective-permute-done | bytes 262176 | tf_op jit(solution)/shard_map/ppermute | solution.py:29
  27.4 2.4 %lags.1 = (f32[2,128,1024]{2,1,0:T(8,128)S(1)}, bf16[2,16,1024]{2,1,0:T(8,128)(2,1)S(1)}, bf16[2,16,1024]{2,1,0:T(8,128)(2,1)S(1)}, bf16[2,16,1024]{2,1,0:T(8,12...) custom-call(s32[128]{0:T(128)S(1)} %get-tuple-element.46.scal, ...), custom_call_target="tpu_custom_call" | custom-call | flops 20000000000 | bytes 1048576 | tf_op jit(solution)/shard_map/lags/pallas_call | solution.py:331
  33.8 0.8 %cores.3 = (f32[128,1024]{1,0:T(8,128)S(1)}, bf16[128,1024]{1,0:T(8,128)(2,1)S(1)}) custom-call(s32[128]{0:T(128)S(1)} %get-tuple-element.46.scal, f32[2,128,1024]{2,1,0:T(8,128)S(1)} %get-tuple-element.57.refs_0_, bf16[2,16,1024]{2,1,0:T(8,128)(2,1)S(1)} %collective-permute-done.5.refs_1_, bf16[2,16,1024]{2,1,0:T(8,128)(2,1)S(1)} %collective-permute-done.6.refs_2_, ...), custom_call_target="tpu_custom_call" | custom-call | flops 1 | bytes 1 | tf_op jit(solution)/shard_map/cores/pallas_call | solution.py:394
  34.7 1.6 %collective-permute-start.13 = (bf16[128,1024]{1,0:T(8,128)(2,1)S(1)}, bf16[128,1024]{1,0:T(8,128)(2,1)S(1)}, u32[]{:S(2)}, u32[]{:S(2)}) collective-permute-start(bf16[128,1024]{1,0:T(8,128)(2,1)S(1)} %get-tuple-element.67), channel_id=1, source_target_pairs={{0,2},{2,0},{1,3},{3,1},{4,6},{6,4},{5,7},{7,5},{8,10},{10,8},{9,1... | collective-permute-start | bytes 786440 | tf_op jit(solution)/shard_map/ppermute | solution.py:29
  36.2 1.8 %cross_lags.2 = (f32[2,64,1024]{2,1,0:T(8,128)S(1)}, bf16[2,32,1024]{2,1,0:T(8,128)(2,1)S(1)}, bf16[2,32,1024]{2,1,0:T(8,128)(2,1)S(1)}) custom-call(s32[128]{0:T(128)S(1)} %get-tuple-element.46.scal, f32[1]{0:T(128)} %constant.3.clone.1.weight, f32[128,1024]{1,0:T(8,128)S(1)} %get-tuple-element.66.refs_0_, ...), custom_call_target="tpu_custom_call" | custom-call | flops 1 | bytes 1 | tf_op jit(solution)/shard_map/cross_lags/pallas_call | solution.py:358
  38.6 6.4 %collective-permute-done.18.refs_0_ = bf16[1,2,64,1024]{3,2,1,0:T(8,128)(2,1)S(1)} collective-permute-done((bf16[1,2,64,1024]{3,2,1,0:T(8,128)(2,1)S(1)}, bf16[1,2,64,1024]{3,2,1,0:T(8,128)(2,1)S(1)}, u32[]{:S(2)}, u32[]{:S(2)}) %collective-permute-start.18) | collective-permute-done | bytes 262176 | tf_op jit(solution)/shard_map/ppermute | solution.py:29
  45.0 1.8 %cross_lags.3 = (f32[2,64,1024]{2,1,0:T(8,128)S(1)}, bf16[2,32,1024]{2,1,0:T(8,128)(2,1)S(1)}, bf16[2,32,1024]{2,1,0:T(8,128)(2,1)S(1)}) custom-call(s32[128]{0:T(128)S(1)} %get-tuple-element.46.scal, f32[1]{0:T(128)} %constant.3.clone.1.weight, bf16[1,2,64,1024]{3,2,1,0:T(8,128)(2,1)S(1)} %collective-permute-done.18.refs_0_, ...), custom_call_target="tpu_custom_call" | custom-call | flops 20000000000 | bytes 1048576 | tf_op jit(solution)/shard_map/cross_lags/pallas_call | solution.py:358
  48.0 1.6 %collective-permute-start.17 = (bf16[64,1024]{1,0:T(8,128)(2,1)S(1)}, bf16[64,1024]{1,0:T(8,128)(2,1)S(1)}, u32[]{:S(2)}, u32[]{:S(2)}) collective-permute-start(bf16[64,1024]{1,0:T(8,128)(2,1)S(1)} %get-tuple-element.74), channel_id=1, source_target_pairs={{0,2},{2,0},{1,3},{3,1},{4,6},{6,4},{5,7},{7,5},{8,10},{10,8},{9,1... | collective-permute-start | bytes 393224 | tf_op jit(solution)/shard_map/ppermute | solution.py:29
  50.8 0.8 stats.3
  51.6 2.8 %collective-permute-done.17.refs_2_ = bf16[64,1024]{1,0:T(8,128)(2,1)S(1)} collective-permute-done((bf16[64,1024]{1,0:T(8,128)(2,1)S(1)}, bf16[64,1024]{1,0:T(8,128)(2,1)S(1)}, u32[]{:S(2)}, u32[]{:S(2)}) %collective-permute-start.17) | collective-permute-done | bytes 131104 | tf_op jit(solution)/shard_map/ppermute | solution.py:29
  55.1 1.2 %collective-permute-done.21.refs_2_ = bf16[64,1024]{1,0:T(8,128)(2,1)S(1)} collective-permute-done((bf16[64,1024]{1,0:T(8,128)(2,1)S(1)}, bf16[64,1024]{1,0:T(8,128)(2,1)S(1)}, u32[]{:S(2)}, u32[]{:S(2)}) %collective-permute-start.21) | collective-permute-done | bytes 131104 | tf_op jit(solution)/shard_map/ppermute | solution.py:29
  57.4 1.2 %collective-permute-start.23 = (f32[8,128]{1,0:T(8,128)S(1)}, f32[8,128]{1,0:T(8,128)S(1)}, u32[]{:S(2)}, u32[]{:S(2)}) collective-permute-start(f32[8,128]{1,0:T(8,128)S(1)} %get-tuple-element.82.refs_3_.refs_4_), channel_id=1, source_target_pairs={{0,2},{1,3},{2,0},{3,1},{4,6},{5,7},{6,4},{7,5},{8,10},{9,11},{10,... | collective-permute-start | bytes 12296 | tf_op jit(solution)/shard_map/ppermute | solution.py:29
  59.0 1.2 %collective-permute-done.22.refs_0_.refs_1_ = f32[8,128]{1,0:T(8,128)S(1)} collective-permute-done((f32[8,128]{1,0:T(8,128)S(1)}, f32[8,128]{1,0:T(8,128)S(1)}, u32[]{:S(2)}, u32[]{:S(2)}) %collective-permute-start.22) | collective-permute-done | bytes 4128 | tf_op jit(solution)/shard_map/ppermute | solution.py:29
  60.1 0.9 %collective-permute-done.23.refs_1_.refs_2_ = f32[8,128]{1,0:T(8,128)S(1)} collective-permute-done((f32[8,128]{1,0:T(8,128)S(1)}, f32[8,128]{1,0:T(8,128)S(1)}, u32[]{:S(2)}, u32[]{:S(2)}) %collective-permute-start.23) | collective-permute-done | bytes 4128 | tf_op jit(solution)/shard_map/ppermute | solution.py:29
  61.0 0.8 %gradient.2 = (bf16[64,1024]{1,0:T(8,128)(2,1)S(1)}, bf16[64,1024]{1,0:T(8,128)(2,1)S(1)}) custom-call(s32[128]{0:T(128)S(1)} %get-tuple-element.46.scal, f32[8,128]{1,0:T(8,128)S(1)} %collective-permute-done.22.refs_0_.refs_1_, f32[8,128]{1,0:T(8,128)S(1)} %collective-permute-done.23.refs_1_.refs_2_, f32[8,128]{1,0:T(8,128)S(1)} %collective-permute-done.24.refs_2_.refs_3_, ...), custom_call_target="tpu_custom_call" | custom-call | flops 1 | bytes 1 | tf_op jit(solution)/shard_map/gradient/pallas_call | solution.py:498
  62.6 1.8 %collective-permute-start.26 = (bf16[64,1024]{1,0:T(8,128)(2,1)S(1)}, bf16[64,1024]{1,0:T(8,128)(2,1)S(1)}, u32[]{:S(2)}, u32[]{:S(2)}) collective-permute-start(bf16[64,1024]{1,0:T(8,128)(2,1)S(1)} %get-tuple-element.87), channel_id=1, source_target_pairs={{0,12},{4,8},{8,4},{12,0},{1,13},{5,9},{9,5},{13,1},{2,14},{6,10},... | collective-permute-start | bytes 393224 | tf_op jit(solution)/shard_map/ppermute | solution.py:29
  64.4 0.8 %gradient.3 = (bf16[64,1024]{1,0:T(8,128)(2,1)S(1)}, bf16[64,1024]{1,0:T(8,128)(2,1)S(1)}) custom-call(s32[128]{0:T(128)S(1)} %get-tuple-element.46.scal, bf16[64,1024]{1,0:T(8,128)(2,1)S(1)} %get-tuple-element.86.refs_0_, f32[8,128]{1,0:T(8,128)S(1)} %collective-permute-done.22.refs_0_.refs_1_, f32[8,128]{1,0:T(8,128)S(1)} %collective-permute-done.23.refs_1_.refs_2_, ...), custom_call_target="tpu_custom_call" | custom-call | flops 1 | bytes 1 | tf_op jit(solution)/shard_map/gradient/pallas_call | solution.py:498
  65.2 1.1 %collective-permute-start.27 = (bf16[64,1024]{1,0:T(8,128)(2,1)S(1)}, bf16[64,1024]{1,0:T(8,128)(2,1)S(1)}, u32[]{:S(2)}, u32[]{:S(2)}) collective-permute-start(bf16[64,1024]{1,0:T(8,128)(2,1)S(1)} %get-tuple-element.89), channel_id=1, source_target_pairs={{0,4},{4,0},{8,12},{12,8},{1,5},{5,1},{9,13},{13,9},{2,6},{6,2},{1... | collective-permute-start | bytes 393224 | tf_op jit(solution)/shard_map/ppermute | solution.py:29
  66.3 3.2 %normed.1 = f32[4,64,1024]{2,1,0:T(8,128)} custom-call(s32[128]{0:T(128)S(1)} %get-tuple-element.46.scal, f32[8,128]{1,0:T(8,128)S(1)} %collective-permute-done.22.refs_0_.refs_1_, f32[8,128]{1,0:T(8,128)S(1)} %collective-permute-done.23.refs_1_.refs_2_, f32[8,128]{1,0:T(8,128)S(1)} %collective-permute-done.24.refs_2_.refs_3_, ...), custom_call_target="tpu_custom_call" | custom-call | flops 1 | bytes 1 | tf_op jit(solution)/shard_map/normed/pallas_call | solution.py:529
  69.5 4.6 %collective-permute-done.25.refs_4_ = bf16[64,1024]{1,0:T(8,128)(2,1)S(1)} collective-permute-done((bf16[64,1024]{1,0:T(8,128)(2,1)S(1)}, bf16[64,1024]{1,0:T(8,128)(2,1)S(1)}, u32[]{:S(2)}, u32[]{:S(2)}) %collective-permute-start.25) | collective-permute-done | bytes 131104 | tf_op jit(solution)/shard_map/ppermute | solution.py:29
  74.1 2.2 %collective-permute-done.27.refs_7_ = bf16[64,1024]{1,0:T(8,128)(2,1)S(1)} collective-permute-done((bf16[64,1024]{1,0:T(8,128)(2,1)S(1)}, bf16[64,1024]{1,0:T(8,128)(2,1)S(1)}, u32[]{:S(2)}, u32[]{:S(2)}) %collective-permute-start.27) | collective-permute-done | bytes 131104 | tf_op jit(solution)/shard_map/ppermute | solution.py:29
  76.3 1.1 %adjoint.1 = f32[128,1024]{1,0:T(8,128)} custom-call(s32[1,64]{1,0:T(1,128)S(1)} %collective-permute-done.2.refs_3_.refs_0_, s32[1,64]{1,0:T(1,128)S(1)} %collective-permute-done.1.refs_2_.refs_1_, s32[1,64]{1,0:T(1,128)S(1)} %get-tuple-element.50.refs_5_.refs_2_, s32[1,64]{1,0:T(1,128)S(1)} %collective-permute-done.3.refs_4_.refs_3_, ...), custom_call_target="tpu_custom_call" | custom-call | flops 1 | bytes 1 | tf_op jit(solution)/shard_map/adjoint/pallas_call | solution.py:553
  (55 shorter events, 13.8 us)
Async XLA Ops:
  0.6 22.3 %copy-start.1 = (f32[2,56,1024]{2,1,0:T(8,128)S(1)}, f32[2,56,1024]{2,1,0:T(8,128)}, u32[]{:S(2)}) copy-start(f32[2,56,1024]{2,1,0:T(8,128)} %constant.16.clone.trig) | copy-start | bytes 1376260
  2.0 15.7 %collective-permute-start = (bf16[1,2,128,1024]{3,2,1,0:T(8,128)(2,1)S(1)}, bf16[1,2,128,1024]{3,2,1,0:T(8,128)(2,1)S(1)}, u32[]{:S(2)}, u32[]{:S(2)}) collective-permute-start(bf16[1,2,128,1024]{3,2,1,0:T(8,128)(2,1)S(1)} %get-tuple-element.90), channel_id=1, source_target_pairs={{0,2},{2,0},{1,3},{3,1},{4,6},{6,4},{5,7},{7,5},{8,10},{10,8},{9,1... | collective-permute-start | bytes 1572872 | tf_op jit(solution)/shard_map/ppermute | solution.py:29
  5.6 0.7 copy-start.2
  6.3 0.7 copy-start.3
  9.5 5.4 %collective-permute-start.1 = (s32[1,64]{1,0:T(1,128)S(1)}, s32[1,64]{1,0:T(1,128)S(1)}, u32[]{:S(2)}, u32[]{:S(2)}) collective-permute-start(s32[1,64]{1,0:T(1,128)S(1)} %get-tuple-element.47), channel_id=1, source_target_pairs={{0,12},{4,8},{8,4},{12,0},{1,13},{5,9},{9,5},{13,1},{2,14},{6,10},... | collective-permute-start | bytes 776 | tf_op jit(solution)/shard_map/ppermute | solution.py:29
  13.2 4.4 %collective-permute-start.2 = (s32[1,64]{1,0:T(1,128)S(1)}, s32[1,64]{1,0:T(1,128)S(1)}, u32[]{:S(2)}, u32[]{:S(2)}) collective-permute-start(s32[1,64]{1,0:T(1,128)S(1)} %get-tuple-element.48), channel_id=1, source_target_pairs={{0,8},{4,12},{8,0},{12,4},{1,9},{5,13},{9,1},{13,5},{2,10},{6,14},... | collective-permute-start | bytes 776 | tf_op jit(solution)/shard_map/ppermute | solution.py:29
  13.2 4.4 %collective-permute-start.3 = (s32[1,64]{1,0:T(1,128)S(1)}, s32[1,64]{1,0:T(1,128)S(1)}, u32[]{:S(2)}, u32[]{:S(2)}) collective-permute-start(s32[1,64]{1,0:T(1,128)S(1)} %get-tuple-element.49), channel_id=1, source_target_pairs={{0,4},{4,0},{8,12},{12,8},{1,5},{5,1},{9,13},{13,9},{2,6},{6,2},{1... | collective-permute-start | bytes 776 | tf_op jit(solution)/shard_map/ppermute | solution.py:29
  19.2 7.9 %collective-permute-start.4 = (bf16[1,2,64,1024]{3,2,1,0:T(8,128)(2,1)S(1)}, bf16[1,2,64,1024]{3,2,1,0:T(8,128)(2,1)S(1)}, u32[]{:S(2)}, u32[]{:S(2)}) collective-permute-start(bf16[1,2,64,1024]{3,2,1,0:T(8,128)(2,1)S(1)} %get-tuple-element.52), channel_id=1, source_target_pairs={{0,4},{4,0},{8,12},{12,8},{1,5},{5,1},{9,13},{13,9},{2,6},{6,2},{1... | collective-permute-start | bytes 786440 | tf_op jit(solution)/shard_map/ppermute | solution.py:29
  20.4 15.8 %collective-permute-start.14 = (bf16[1,2,64,1024]{3,2,1,0:T(8,128)(2,1)S(1)}, bf16[1,2,64,1024]{3,2,1,0:T(8,128)(2,1)S(1)}, u32[]{:S(2)}, u32[]{:S(2)}) collective-permute-start(bf16[1,2,64,1024]{3,2,1,0:T(8,128)(2,1)S(1)} %get-tuple-element.69), channel_id=1, source_target_pairs={{0,12},{4,8},{8,4},{12,0},{1,13},{5,9},{9,5},{13,1},{2,14},{6,10},... | collective-permute-start | bytes 786440 | tf_op jit(solution)/shard_map/ppermute | solution.py:29
  22.8 22.1 %collective-permute-start.18 = (bf16[1,2,64,1024]{3,2,1,0:T(8,128)(2,1)S(1)}, bf16[1,2,64,1024]{3,2,1,0:T(8,128)(2,1)S(1)}, u32[]{:S(2)}, u32[]{:S(2)}) collective-permute-start(bf16[1,2,64,1024]{3,2,1,0:T(8,128)(2,1)S(1)} %get-tuple-element.76), channel_id=1, source_target_pairs={{0,8},{4,12},{8,0},{12,4},{1,9},{5,13},{9,1},{13,5},{2,10},{6,14},... | collective-permute-start | bytes 786440 | tf_op jit(solution)/shard_map/ppermute | solution.py:29
  29.8 1.3 %collective-permute-start.5 = (bf16[2,16,1024]{2,1,0:T(8,128)(2,1)S(1)}, bf16[2,16,1024]{2,1,0:T(8,128)(2,1)S(1)}, u32[]{:S(2)}, u32[]{:S(2)}) collective-permute-start(bf16[2,16,1024]{2,1,0:T(8,128)(2,1)S(1)} %get-tuple-element.58), channel_id=1, source_target_pairs={{0,1},{1,0},{2,3},{3,2},{4,5},{5,4},{6,7},{7,6},{8,9},{9,8},{10,11... | collective-permute-start | bytes 196616 | tf_op jit(solution)/shard_map/ppermute | solution.py:29
  29.9 1.4 %collective-permute-start.6 = (bf16[2,16,1024]{2,1,0:T(8,128)(2,1)S(1)}, bf16[2,16,1024]{2,1,0:T(8,128)(2,1)S(1)}, u32[]{:S(2)}, u32[]{:S(2)}) collective-permute-start(bf16[2,16,1024]{2,1,0:T(8,128)(2,1)S(1)} %get-tuple-element.59), channel_id=1, source_target_pairs={{0,1},{1,0},{2,3},{3,2},{4,5},{5,4},{6,7},{7,6},{8,9},{9,8},{10,11... | collective-permute-start | bytes 196616 | tf_op jit(solution)/shard_map/ppermute | solution.py:29
  30.4 1.3 %collective-permute-start.7 = (bf16[2,16,1024]{2,1,0:T(8,128)(2,1)S(1)}, bf16[2,16,1024]{2,1,0:T(8,128)(2,1)S(1)}, u32[]{:S(2)}, u32[]{:S(2)}) collective-permute-start(bf16[2,16,1024]{2,1,0:T(8,128)(2,1)S(1)} %get-tuple-element.60), channel_id=1, source_target_pairs={{0,1},{1,0},{2,3},{3,2},{4,5},{5,4},{6,7},{7,6},{8,9},{9,8},{10,11... | collective-permute-start | bytes 196616 | tf_op jit(solution)/shard_map/ppermute | solution.py:29
  31.2 1.3 %collective-permute-start.8 = (bf16[2,16,1024]{2,1,0:T(8,128)(2,1)S(1)}, bf16[2,16,1024]{2,1,0:T(8,128)(2,1)S(1)}, u32[]{:S(2)}, u32[]{:S(2)}) collective-permute-start(bf16[2,16,1024]{2,1,0:T(8,128)(2,1)S(1)} %get-tuple-element.61), channel_id=1, source_target_pairs={{0,1},{1,0},{2,3},{3,2},{4,5},{5,4},{6,7},{7,6},{8,9},{9,8},{10,11... | collective-permute-start | bytes 196616 | tf_op jit(solution)/shard_map/ppermute | solution.py:29
  31.3 1.3 %collective-permute-start.9 = (bf16[2,16,1024]{2,1,0:T(8,128)(2,1)S(1)}, bf16[2,16,1024]{2,1,0:T(8,128)(2,1)S(1)}, u32[]{:S(2)}, u32[]{:S(2)}) collective-permute-start(bf16[2,16,1024]{2,1,0:T(8,128)(2,1)S(1)} %get-tuple-element.62), channel_id=1, source_target_pairs={{0,1},{1,0},{2,3},{3,2},{4,5},{5,4},{6,7},{7,6},{8,9},{9,8},{10,11... | collective-permute-start | bytes 196616 | tf_op jit(solution)/shard_map/ppermute | solution.py:29
  31.7 1.3 %collective-permute-start.10 = (bf16[2,16,1024]{2,1,0:T(8,128)(2,1)S(1)}, bf16[2,16,1024]{2,1,0:T(8,128)(2,1)S(1)}, u32[]{:S(2)}, u32[]{:S(2)}) collective-permute-start(bf16[2,16,1024]{2,1,0:T(8,128)(2,1)S(1)} %get-tuple-element.63), channel_id=1, source_target_pairs={{0,1},{1,0},{2,3},{3,2},{4,5},{5,4},{6,7},{7,6},{8,9},{9,8},{10,11... | collective-permute-start | bytes 196616 | tf_op jit(solution)/shard_map/ppermute | solution.py:29
  32.4 1.3 %collective-permute-start.11 = (bf16[2,16,1024]{2,1,0:T(8,128)(2,1)S(1)}, bf16[2,16,1024]{2,1,0:T(8,128)(2,1)S(1)}, u32[]{:S(2)}, u32[]{:S(2)}) collective-permute-start(bf16[2,16,1024]{2,1,0:T(8,128)(2,1)S(1)} %get-tuple-element.64), channel_id=1, source_target_pairs={{0,1},{1,0},{2,3},{3,2},{4,5},{5,4},{6,7},{7,6},{8,9},{9,8},{10,11... | collective-permute-start | bytes 196616 | tf_op jit(solution)/shard_map/ppermute | solution.py:29
  32.6 1.3 %collective-permute-start.12 = (bf16[2,16,1024]{2,1,0:T(8,128)(2,1)S(1)}, bf16[2,16,1024]{2,1,0:T(8,128)(2,1)S(1)}, u32[]{:S(2)}, u32[]{:S(2)}) collective-permute-start(bf16[2,16,1024]{2,1,0:T(8,128)(2,1)S(1)} %get-tuple-element.65), channel_id=1, source_target_pairs={{0,1},{1,0},{2,3},{3,2},{4,5},{5,4},{6,7},{7,6},{8,9},{9,8},{10,11... | collective-permute-start | bytes 196616 | tf_op jit(solution)/shard_map/ppermute | solution.py:29
  34.7 12.7 %collective-permute-start.13 = (bf16[128,1024]{1,0:T(8,128)(2,1)S(1)}, bf16[128,1024]{1,0:T(8,128)(2,1)S(1)}, u32[]{:S(2)}, u32[]{:S(2)}) collective-permute-start(bf16[128,1024]{1,0:T(8,128)(2,1)S(1)} %get-tuple-element.67), channel_id=1, source_target_pairs={{0,2},{2,0},{1,3},{3,1},{4,6},{6,4},{5,7},{7,5},{8,10},{10,8},{9,1... | collective-permute-start | bytes 786440 | tf_op jit(solution)/shard_map/ppermute | solution.py:29
  38.0 9.3 %collective-permute-start.15 = (bf16[2,32,1024]{2,1,0:T(8,128)(2,1)S(1)}, bf16[2,32,1024]{2,1,0:T(8,128)(2,1)S(1)}, u32[]{:S(2)}, u32[]{:S(2)}) collective-permute-start(bf16[2,32,1024]{2,1,0:T(8,128)(2,1)S(1)} %get-tuple-element.71), channel_id=1, source_target_pairs={{0,1},{1,0},{2,3},{3,2},{4,5},{5,4},{6,7},{7,6},{8,9},{9,8},{10,11... | collective-permute-start | bytes 393224 | tf_op jit(solution)/shard_map/ppermute | solution.py:29
  38.2 12.6 %copy-start = (f32[4,64,1024]{2,1,0:T(8,128)S(1)}, f32[4,64,1024]{2,1,0:T(8,128)}, u32[]{:S(2)}) copy-start(f32[4,64,1024]{2,1,0:T(8,128)} %refs_7_.3) | copy-start | bytes 3145732
  38.2 9.2 %collective-permute-start.16 = (bf16[2,32,1024]{2,1,0:T(8,128)(2,1)S(1)}, bf16[2,32,1024]{2,1,0:T(8,128)(2,1)S(1)}, u32[]{:S(2)}, u32[]{:S(2)}) collective-permute-start(bf16[2,32,1024]{2,1,0:T(8,128)(2,1)S(1)} %get-tuple-element.72), channel_id=1, source_target_pairs={{0,1},{1,0},{2,3},{3,2},{4,5},{5,4},{6,7},{7,6},{8,9},{9,8},{10,11... | collective-permute-start | bytes 393224 | tf_op jit(solution)/shard_map/ppermute | solution.py:29
  46.8 2.8 %collective-permute-start.19 = (bf16[2,32,1024]{2,1,0:T(8,128)(2,1)S(1)}, bf16[2,32,1024]{2,1,0:T(8,128)(2,1)S(1)}, u32[]{:S(2)}, u32[]{:S(2)}) collective-permute-start(bf16[2,32,1024]{2,1,0:T(8,128)(2,1)S(1)} %get-tuple-element.78), channel_id=1, source_target_pairs={{0,1},{1,0},{2,3},{3,2},{4,5},{5,4},{6,7},{7,6},{8,9},{9,8},{10,11... | collective-permute-start | bytes 393224 | tf_op jit(solution)/shard_map/ppermute | solution.py:29
  46.9 2.7 %collective-permute-start.20 = (bf16[2,32,1024]{2,1,0:T(8,128)(2,1)S(1)}, bf16[2,32,1024]{2,1,0:T(8,128)(2,1)S(1)}, u32[]{:S(2)}, u32[]{:S(2)}) collective-permute-start(bf16[2,32,1024]{2,1,0:T(8,128)(2,1)S(1)} %get-tuple-element.79), channel_id=1, source_target_pairs={{0,1},{1,0},{2,3},{3,2},{4,5},{5,4},{6,7},{7,6},{8,9},{9,8},{10,11... | collective-permute-start | bytes 393224 | tf_op jit(solution)/shard_map/ppermute | solution.py:29
  48.0 6.4 %collective-permute-start.17 = (bf16[64,1024]{1,0:T(8,128)(2,1)S(1)}, bf16[64,1024]{1,0:T(8,128)(2,1)S(1)}, u32[]{:S(2)}, u32[]{:S(2)}) collective-permute-start(bf16[64,1024]{1,0:T(8,128)(2,1)S(1)} %get-tuple-element.74), channel_id=1, source_target_pairs={{0,2},{2,0},{1,3},{3,1},{4,6},{6,4},{5,7},{7,5},{8,10},{10,8},{9,1... | collective-permute-start | bytes 393224 | tf_op jit(solution)/shard_map/ppermute | solution.py:29
  50.2 6.2 %collective-permute-start.21 = (bf16[64,1024]{1,0:T(8,128)(2,1)S(1)}, bf16[64,1024]{1,0:T(8,128)(2,1)S(1)}, u32[]{:S(2)}, u32[]{:S(2)}) collective-permute-start(bf16[64,1024]{1,0:T(8,128)(2,1)S(1)} %get-tuple-element.81), channel_id=1, source_target_pairs={{0,2},{2,0},{1,3},{3,1},{4,6},{6,4},{5,7},{7,5},{8,10},{10,8},{9,1... | collective-permute-start | bytes 393224 | tf_op jit(solution)/shard_map/ppermute | solution.py:29
  57.1 3.1 %collective-permute-start.22 = (f32[8,128]{1,0:T(8,128)S(1)}, f32[8,128]{1,0:T(8,128)S(1)}, u32[]{:S(2)}, u32[]{:S(2)}) collective-permute-start(f32[8,128]{1,0:T(8,128)S(1)} %get-tuple-element.82.refs_3_.refs_4_), channel_id=1, source_target_pairs={{0,3},{1,2},{2,1},{3,0},{4,7},{5,6},{6,5},{7,4},{8,11},{9,10},{10,... | collective-permute-start | bytes 12296 | tf_op jit(solution)/shard_map/ppermute | solution.py:29
  57.4 3.6 %collective-permute-start.23 = (f32[8,128]{1,0:T(8,128)S(1)}, f32[8,128]{1,0:T(8,128)S(1)}, u32[]{:S(2)}, u32[]{:S(2)}) collective-permute-start(f32[8,128]{1,0:T(8,128)S(1)} %get-tuple-element.82.refs_3_.refs_4_), channel_id=1, source_target_pairs={{0,2},{1,3},{2,0},{3,1},{4,6},{5,7},{6,4},{7,5},{8,10},{9,11},{10,... | collective-permute-start | bytes 12296 | tf_op jit(solution)/shard_map/ppermute | solution.py:29
  58.7 2.4 %collective-permute-start.24 = (f32[8,128]{1,0:T(8,128)S(1)}, f32[8,128]{1,0:T(8,128)S(1)}, u32[]{:S(2)}, u32[]{:S(2)}) collective-permute-start(f32[8,128]{1,0:T(8,128)S(1)} %get-tuple-element.82.refs_3_.refs_4_), channel_id=1, source_target_pairs={{0,1},{1,0},{2,3},{3,2},{4,5},{5,4},{6,7},{7,6},{8,9},{9,8},{10,11... | collective-permute-start | bytes 12296 | tf_op jit(solution)/shard_map/ppermute | solution.py:29
  61.9 12.3 %collective-permute-start.25 = (bf16[64,1024]{1,0:T(8,128)(2,1)S(1)}, bf16[64,1024]{1,0:T(8,128)(2,1)S(1)}, u32[]{:S(2)}, u32[]{:S(2)}) collective-permute-start(bf16[64,1024]{1,0:T(8,128)(2,1)S(1)} %get-tuple-element.86.refs_0_), channel_id=1, source_target_pairs={{0,8},{4,12},{8,0},{12,4},{1,9},{5,13},{9,1},{13,5},{2,10},{6,14},... | collective-permute-start | bytes 393224 | tf_op jit(solution)/shard_map/ppermute | solution.py:29
  62.6 11.5 %collective-permute-start.26 = (bf16[64,1024]{1,0:T(8,128)(2,1)S(1)}, bf16[64,1024]{1,0:T(8,128)(2,1)S(1)}, u32[]{:S(2)}, u32[]{:S(2)}) collective-permute-start(bf16[64,1024]{1,0:T(8,128)(2,1)S(1)} %get-tuple-element.87), channel_id=1, source_target_pairs={{0,12},{4,8},{8,4},{12,0},{1,13},{5,9},{9,5},{13,1},{2,14},{6,10},... | collective-permute-start | bytes 393224 | tf_op jit(solution)/shard_map/ppermute | solution.py:29
  65.2 11.1 %collective-permute-start.27 = (bf16[64,1024]{1,0:T(8,128)(2,1)S(1)}, bf16[64,1024]{1,0:T(8,128)(2,1)S(1)}, u32[]{:S(2)}, u32[]{:S(2)}) collective-permute-start(bf16[64,1024]{1,0:T(8,128)(2,1)S(1)} %get-tuple-element.89), channel_id=1, source_target_pairs={{0,4},{4,0},{8,12},{12,8},{1,5},{5,1},{9,13},{13,9},{2,6},{6,2},{1... | collective-permute-start | bytes 393224 | tf_op jit(solution)/shard_map/ppermute | solution.py:29
  (2 other events, 1.3 us)

commit v20 on v18

--- a/solution.py
+++ b/solution.py
@@ -152,7 +152,7 @@
     outs, kept = refs[:-1], refs[-1]
     _, _, channels, part = kept.shape
     slots = src_ids[0].shape[1]
-    pick = picks(src_ids[::-1], channels)
+    pick = picks(src_ids[: sends - 1][::-1], channels)
     for u in range(used):
         x = here[0].reshape(2 * channels, part)
         for s in range(used):
@@ -165,7 +165,7 @@
                 pick, z, (((0,), (0,)), ((), ())), preferred_element_type=F32
             ).astype(BF16)
             for (d, first, count), out in zip(messages, outs):
-                at = d * slots + first
+                at = (d - 1) * slots + first
                 out[u, half] = y[at : at + count]
 
 
@@ -185,9 +185,10 @@
     return sent, kept
 
 
-def own_kernel(classes, parts, scal, kept, rec_ids, trig, own, table, base):
+def own_kernel(classes, parts, scal, kept, src_ids, rec_ids, trig, here, own, table, base):
     units, used, _, slots, _ = own.shape
-    pick = picks([rec_ids.at[d : d + 1] for d in range(units)], kept.shape[2])
+    ids = [rec_ids.at[d : d + 1] for d in range(units)] + [src_ids]
+    pick = picks(ids, kept.shape[2])
     for u in range(used):
         for half in range(2):
             y = lax.dot_general(
@@ -195,25 +196,27 @@
             ).astype(BF16)
             for d in range(units):
                 own[d, u, half] = y[d * slots : (d + 1) * slots]
+            here[u, half] = y[units * slots :]
     table_kernel(classes, parts, scal, trig, table, base)
 
 
-def gather_own(scal, kept, rec_ids, trig, classes, span, parts):
+def gather_own(scal, kept, src_ids, rec_ids, trig, classes, span, parts):
     used, _, _, part = kept.shape
     units, slots = rec_ids.shape
     return pl.pallas_call(
         functools.partial(own_kernel, classes, parts),
         out_shape=[
+            jax.ShapeDtypeStruct((used, 2, slots, part), BF16),
             jax.ShapeDtypeStruct((units, used, 2, slots, part), BF16),
             jax.ShapeDtypeStruct((classes, 2 * LANES, span), BF16),
         ],
-        in_specs=[SMEM] + [VMEM] * 3,
-        out_specs=[VMEM] * 2,
+        in_specs=[SMEM] + [VMEM] * 4,
+        out_specs=[VMEM] * 3,
         scratch_shapes=[pltpu.VMEM((2, LANES, span), F32)],
         compiler_params=params(16),
         cost_estimate=SMALL,
         name="own",
-    )(scal, kept, rec_ids, jnp.asarray(trig))
+    )(scal, kept, src_ids, rec_ids, jnp.asarray(trig))
 
 
 def combine(values, classes, outputs, origin, span, period):
@@ -609,8 +612,10 @@
         messages = [piece for pieces in chunks for piece in pieces]
     else:
         messages = [(d, 0, slots) for d in shifts]
-    sent, kept = gather_rows(scal, here, held, make_perm(part), src_ids, messages)
-    own_rows, table = gather_own(scal, kept, rec_ids, trig, classes, span, peers)
+    sent, kept = gather_rows(scal, here, held, make_perm(part), src_ids, [m for m in messages if m[0]])
+    own_sent, own_rows, table = gather_own(scal, kept, src_ids[0], rec_ids, trig, classes, span, peers)
+    sent = list(sent)
+    sent = [sent.pop(0) if m[0] else own_sent for m in messages]
     arrived = [swapped(x, "recv", places, m[0]) for m, x in reversed(list(zip(messages, sent)))][::-1]
     if not direct:
         stacked = jnp.stack(arrived)

time: 76.5 us -> 76.4 us (level)
  no operation moved by 1% of the time
where the time goes in v20:
time: 76.4 us; the launch traced here: 76.2 us
  starting transfers between devices  24.3 us (32%)
  waiting for transfers between devices  23.5 us (31%)
  Pallas kernels  23 us (30%)
  local copies, waits for them, and re-layouts  4 us (5%)
  between operations  1.46 us (2%)
    ppermute x28, starting transfers between devices, swapped(): return lax.ppermute(value, axis, [(i, i ^ step) for i in range(size)])  24.3 us
    ppermute x28, waiting for transfers between devices, swapped(): return lax.ppermute(value, axis, [(i, i ^ step) for i in range(size)])  23.5 us
    pallas_call x2, Pallas kernels, cross_lag_parts(): pl.pallas_call(functools.partial(cross_lags_kernel, geometry, split, len(...  3.59 us
    pallas_call x1, Pallas kernels, normed_rows(): pl.pallas_call(functools.partial(normed_kernel, lag_total, chunks, len(su...  3.22 us
    pallas_call x1, Pallas kernels, gather_own(): pl.pallas_call(functools.partial(own_kernel, classes, parts), out_shape=[...  3.14 us
    unnamed x12, local copies, waits for them, and re-layouts  2.68 us
    pallas_call x1, Pallas kernels, lag_parts(): pl.pallas_call(functools.partial(lags_kernel, geometry, split, len(after)...  2.47 us
    pallas_call x3, Pallas kernels, lag_stats(): pl.pallas_call(functools.partial(stats_kernel, scale, q, pieces, len(more...  2.22 us
  transfers between devices with their start and end apart: 28, of which 13 were waited for; matrix products, arithmetic and copies ran while one was open for 0% of the time, Pallas kernels for 25%

profile of v20, /device:TPU:0, one launch (start us, length us, event | category | flops | bytes accessed | tf_op | source)
XLA Modules:
  0.0 76.2 jit_solution(3458097233872383954)
XLA Ops:
  0.7 1.3 %constant_dynamic-slice_fusion = (bf16[1,2,128,1024]{3,2,1,0:T(8,128)(2,1)S(1)}, bf16[1,2,128,1024]{3,2,1,0:T(8,128)(2,1)S(1)}) fusion(bf16[1,2,128,2048]{3,2,1,0:T(8,128)(2,1)} %param.8, s32[]{:T(128)S(6)} %select_n.7, s32[]{:T(128)S(6)} %select_n.6), kind=kLoop, calls=%fused_computation | loop fusion | bytes 2097160 | tf_op jit(solution)/shard_map/dynamic_slice | solution.py:586
  2.0 3.0 %collective-permute-start = (bf16[1,2,128,1024]{3,2,1,0:T(8,128)(2,1)S(1)}, bf16[1,2,128,1024]{3,2,1,0:T(8,128)(2,1)S(1)}, u32[]{:S(2)}, u32[]{:S(2)}) collective-permute-start(bf16[1,2,128,1024]{3,2,1,0:T(8,128)(2,1)S(1)} %get-tuple-element.90), channel_id=1, source_target_pairs={{0,2},{2,0},{1,3},{3,1},{4,6},{6,4},{5,7},{7,5},{8,10},{10,8},{9,1... | collective-permute-start | bytes 1572872 | tf_op jit(solution)/shard_map/ppermute | solution.py:29
  8.3 1.2 %index.1 = (s32[128]{0:T(128)S(1)}, s32[1,64]{1,0:T(1,128)S(1)}, s32[1,64]{1,0:T(1,128)S(1)}, s32[1,64]{1,0:T(1,128)S(1)}, s32[1,64]{1,0:T(1,128)S(1)}, /*index=5*/s32[4,64]{1,0:T(4,128)S(1)}) custom-call(s32[1]{0:T(128)S(6)} %copy.10.refs_0_, s32[4]{0:T(128)S(1)} %copy-done.4, s32[4]{0:T(128)S(1)} %bitcast.1, s32[4,64]{1,0:T(4,128)S(1)} %copy-done.2, ...), custom_call_target="tpu_custom_call" | custom-call | flops 1 | bytes 1 | tf_op jit(solution)/shard_map/index/pallas_call | solution.py:92
  9.5 3.7 %collective-permute-start.1 = (s32[1,64]{1,0:T(1,128)S(1)}, s32[1,64]{1,0:T(1,128)S(1)}, u32[]{:S(2)}, u32[]{:S(2)}) collective-permute-start(s32[1,64]{1,0:T(1,128)S(1)} %get-tuple-element.47), channel_id=1, source_target_pairs={{0,12},{4,8},{8,4},{12,0},{1,13},{5,9},{9,5},{13,1},{2,14},{6,10},... | collective-permute-start | bytes 776 | tf_op jit(solution)/shard_map/ppermute | solution.py:29
  13.2 0.8 %collective-permute-start.3 = (s32[1,64]{1,0:T(1,128)S(1)}, s32[1,64]{1,0:T(1,128)S(1)}, u32[]{:S(2)}, u32[]{:S(2)}) collective-permute-start(s32[1,64]{1,0:T(1,128)S(1)} %get-tuple-element.49), channel_id=1, source_target_pairs={{0,4},{4,0},{8,12},{12,8},{1,5},{5,1},{9,13},{13,9},{2,6},{6,2},{1... | collective-permute-start | bytes 776 | tf_op jit(solution)/shard_map/ppermute | solution.py:29
  14.9 2.7 %collective-permute-done.2.refs_3_.refs_1_ = s32[1,64]{1,0:T(1,128)S(1)} collective-permute-done((s32[1,64]{1,0:T(1,128)S(1)}, s32[1,64]{1,0:T(1,128)S(1)}, u32[]{:S(2)}, u32[]{:S(2)}) %collective-permute-start.2) | collective-permute-done | bytes 288 | tf_op jit(solution)/shard_map/ppermute | solution.py:29
  17.7 1.5 %rows.1 = (bf16[1,2,64,1024]{3,2,1,0:T(8,128)(2,1)S(1)}, bf16[1,2,64,1024]{3,2,1,0:T(8,128)(2,1)S(1)}, bf16[1,2,64,1024]{3,2,1,0:T(8,128)(2,1)S(1)}, bf16[1,2,128,1024]{3,2,1,0:T(8,128)(2,1)S(1)}) custom-call(s32[128]{0:T(128)S(1)} %get-tuple-element.46.scal, bf16[1,2,128,1024]{3,2,1,0:T(8,128)(2,1)S(1)} %get-tuple-element.91.here, ...), custom_call_target="tpu_custom_call" | custom-call | flops 1 | bytes 1 | tf_op jit(solution)/shard_map/rows/pallas_call | solution.py:175
  19.2 1.1 %collective-permute-start.4 = (bf16[1,2,64,1024]{3,2,1,0:T(8,128)(2,1)S(1)}, bf16[1,2,64,1024]{3,2,1,0:T(8,128)(2,1)S(1)}, u32[]{:S(2)}, u32[]{:S(2)}) collective-permute-start(bf16[1,2,64,1024]{3,2,1,0:T(8,128)(2,1)S(1)} %get-tuple-element.54), channel_id=1, source_target_pairs={{0,4},{4,0},{8,12},{12,8},{1,5},{5,1},{9,13},{13,9},{2,6},{6,2},{1... | collective-permute-start | bytes 786440 | tf_op jit(solution)/shard_map/ppermute | solution.py:29
  20.3 2.5 %collective-permute-start.14 = (bf16[1,2,64,1024]{3,2,1,0:T(8,128)(2,1)S(1)}, bf16[1,2,64,1024]{3,2,1,0:T(8,128)(2,1)S(1)}, u32[]{:S(2)}, u32[]{:S(2)}) collective-permute-start(bf16[1,2,64,1024]{3,2,1,0:T(8,128)(2,1)S(1)} %get-tuple-element.69), channel_id=1, source_target_pairs={{0,12},{4,8},{8,4},{12,0},{1,13},{5,9},{9,5},{13,1},{2,14},{6,10},... | collective-permute-start | bytes 786440 | tf_op jit(solution)/shard_map/ppermute | solution.py:29
  22.9 3.1 %own.1 = (bf16[1,2,64,1024]{3,2,1,0:T(8,128)(2,1)S(1)}, bf16[4,1,2,64,1024]{4,3,2,1,0:T(8,128)(2,1)S(1)}, bf16[8,256,1024]{2,1,0:T(8,128)(2,1)S(1)}) custom-call(s32[128]{0:T(128)S(1)} %get-tuple-element.46.scal, bf16[1,2,128,1024]{3,2,1,0:T(8,128)(2,1)S(1)} %get-tuple-element.51.kept, s32[1,64]{1,0:T(1,128)S(1)} %get-tuple-element.50.refs_5_.src_ids.refs_2_, ...), custom_call_target="tpu_custom_call" | custom-call | flops 1 | bytes 1 | tf_op jit(solution)/shard_map/own/pallas_call | solution.py:206
  26.1 1.0 %collective-permute-done.4.refs_1_ = bf16[1,2,64,1024]{3,2,1,0:T(8,128)(2,1)S(1)} collective-permute-done((bf16[1,2,64,1024]{3,2,1,0:T(8,128)(2,1)S(1)}, bf16[1,2,64,1024]{3,2,1,0:T(8,128)(2,1)S(1)}, u32[]{:S(2)}, u32[]{:S(2)}) %collective-permute-start.4) | collective-permute-done | bytes 262176 | tf_op jit(solution)/shard_map/ppermute | solution.py:29
  27.4 2.5 %lags.1 = (f32[2,128,1024]{2,1,0:T(8,128)S(1)}, bf16[2,16,1024]{2,1,0:T(8,128)(2,1)S(1)}, bf16[2,16,1024]{2,1,0:T(8,128)(2,1)S(1)}, bf16[2,16,1024]{2,1,0:T(8,12...) custom-call(s32[128]{0:T(128)S(1)} %get-tuple-element.46.scal, ...), custom_call_target="tpu_custom_call" | custom-call | flops 20000000000 | bytes 1048576 | tf_op jit(solution)/shard_map/lags/pallas_call | solution.py:334
  32.9 0.7 collective-permute-done.11.refs_7_
  33.8 0.8 %cores.3 = (f32[128,1024]{1,0:T(8,128)S(1)}, bf16[128,1024]{1,0:T(8,128)(2,1)S(1)}) custom-call(s32[128]{0:T(128)S(1)} %get-tuple-element.46.scal, f32[2,128,1024]{2,1,0:T(8,128)S(1)} %get-tuple-element.57.refs_0_, bf16[2,16,1024]{2,1,0:T(8,128)(2,1)S(1)} %collective-permute-done.5.refs_1_, bf16[2,16,1024]{2,1,0:T(8,128)(2,1)S(1)} %collective-permute-done.6.refs_2_, ...), custom_call_target="tpu_custom_call" | custom-call | flops 1 | bytes 1 | tf_op jit(solution)/shard_map/cores/pallas_call | solution.py:397
  34.7 1.5 %collective-permute-start.13 = (bf16[128,1024]{1,0:T(8,128)(2,1)S(1)}, bf16[128,1024]{1,0:T(8,128)(2,1)S(1)}, u32[]{:S(2)}, u32[]{:S(2)}) collective-permute-start(bf16[128,1024]{1,0:T(8,128)(2,1)S(1)} %get-tuple-element.67), channel_id=1, source_target_pairs={{0,2},{2,0},{1,3},{3,1},{4,6},{6,4},{5,7},{7,5},{8,10},{10,8},{9,1... | collective-permute-start | bytes 786440 | tf_op jit(solution)/shard_map/ppermute | solution.py:29
  36.2 1.8 %cross_lags.2 = (f32[2,64,1024]{2,1,0:T(8,128)S(1)}, bf16[2,32,1024]{2,1,0:T(8,128)(2,1)S(1)}, bf16[2,32,1024]{2,1,0:T(8,128)(2,1)S(1)}) custom-call(s32[128]{0:T(128)S(1)} %get-tuple-element.46.scal, f32[1]{0:T(128)} %constant.3.clone.1.weight, f32[128,1024]{1,0:T(8,128)S(1)} %get-tuple-element.66.refs_0_, ...), custom_call_target="tpu_custom_call" | custom-call | flops 1 | bytes 1 | tf_op jit(solution)/shard_map/cross_lags/pallas_call | solution.py:361
  38.6 6.3 %collective-permute-done.18.refs_0_ = bf16[1,2,64,1024]{3,2,1,0:T(8,128)(2,1)S(1)} collective-permute-done((bf16[1,2,64,1024]{3,2,1,0:T(8,128)(2,1)S(1)}, bf16[1,2,64,1024]{3,2,1,0:T(8,128)(2,1)S(1)}, u32[]{:S(2)}, u32[]{:S(2)}) %collective-permute-start.18) | collective-permute-done | bytes 262176 | tf_op jit(solution)/shard_map/ppermute | solution.py:29
  44.9 1.8 %cross_lags.3 = (f32[2,64,1024]{2,1,0:T(8,128)S(1)}, bf16[2,32,1024]{2,1,0:T(8,128)(2,1)S(1)}, bf16[2,32,1024]{2,1,0:T(8,128)(2,1)S(1)}) custom-call(s32[128]{0:T(128)S(1)} %get-tuple-element.46.scal, f32[1]{0:T(128)} %constant.3.clone.1.weight, bf16[1,2,64,1024]{3,2,1,0:T(8,128)(2,1)S(1)} %collective-permute-done.18.refs_0_, ...), custom_call_target="tpu_custom_call" | custom-call | flops 20000000000 | bytes 1048576 | tf_op jit(solution)/shard_map/cross_lags/pallas_call | solution.py:361
  48.0 1.6 %collective-permute-start.17 = (bf16[64,1024]{1,0:T(8,128)(2,1)S(1)}, bf16[64,1024]{1,0:T(8,128)(2,1)S(1)}, u32[]{:S(2)}, u32[]{:S(2)}) collective-permute-start(bf16[64,1024]{1,0:T(8,128)(2,1)S(1)} %get-tuple-element.74), channel_id=1, source_target_pairs={{0,2},{2,0},{1,3},{3,1},{4,6},{6,4},{5,7},{7,5},{8,10},{10,8},{9,1... | collective-permute-start | bytes 393224 | tf_op jit(solution)/shard_map/ppermute | solution.py:29
  50.8 0.8 %stats.3 = (f32[128,1024]{1,0:T(8,128)S(1)}, f32[8,128]{1,0:T(8,128)S(1)}) custom-call(s32[128]{0:T(128)S(1)} %get-tuple-element.46.scal, f32[128,1024]{1,0:T(8,128)S(1)} %get-tuple-element.66.refs_0_, bf16[128,1024]{1,0:T(8,128)(2,1)S(1)} %collective-permute-done.13.refs_1_.refs_0_, f32[4,64,1024]{2,1,0:T(8,128)S(1)} %copy-done, f32[4,64,1024]{2,1,0:T(8,128)S(1)} %copy-done), custom_call_target="tpu_custom_call" | custom-call | flops 1 | bytes 1 | tf_op jit(solution)/shard_map/stats/pallas_call | solution.py:452
  51.5 2.8 %collective-permute-done.17.refs_2_ = bf16[64,1024]{1,0:T(8,128)(2,1)S(1)} collective-permute-done((bf16[64,1024]{1,0:T(8,128)(2,1)S(1)}, bf16[64,1024]{1,0:T(8,128)(2,1)S(1)}, u32[]{:S(2)}, u32[]{:S(2)}) %collective-permute-start.17) | collective-permute-done | bytes 131104 | tf_op jit(solution)/shard_map/ppermute | solution.py:29
  55.1 1.2 %collective-permute-done.21.refs_2_ = bf16[64,1024]{1,0:T(8,128)(2,1)S(1)} collective-permute-done((bf16[64,1024]{1,0:T(8,128)(2,1)S(1)}, bf16[64,1024]{1,0:T(8,128)(2,1)S(1)}, u32[]{:S(2)}, u32[]{:S(2)}) %collective-permute-start.21) | collective-permute-done | bytes 131104 | tf_op jit(solution)/shard_map/ppermute | solution.py:29
  57.4 1.2 %collective-permute-start.23 = (f32[8,128]{1,0:T(8,128)S(1)}, f32[8,128]{1,0:T(8,128)S(1)}, u32[]{:S(2)}, u32[]{:S(2)}) collective-permute-start(f32[8,128]{1,0:T(8,128)S(1)} %get-tuple-element.82.refs_3_.refs_4_), channel_id=1, source_target_pairs={{0,2},{1,3},{2,0},{3,1},{4,6},{5,7},{6,4},{7,5},{8,10},{9,11},{10,... | collective-permute-start | bytes 12296 | tf_op jit(solution)/shard_map/ppermute | solution.py:29
  58.9 1.2 %collective-permute-done.22.refs_0_.refs_1_ = f32[8,128]{1,0:T(8,128)S(1)} collective-permute-done((f32[8,128]{1,0:T(8,128)S(1)}, f32[8,128]{1,0:T(8,128)S(1)}, u32[]{:S(2)}, u32[]{:S(2)}) %collective-permute-start.22) | collective-permute-done | bytes 4128 | tf_op jit(solution)/shard_map/ppermute | solution.py:29
  60.1 0.9 %collective-permute-done.23.refs_1_.refs_2_ = f32[8,128]{1,0:T(8,128)S(1)} collective-permute-done((f32[8,128]{1,0:T(8,128)S(1)}, f32[8,128]{1,0:T(8,128)S(1)}, u32[]{:S(2)}, u32[]{:S(2)}) %collective-permute-start.23) | collective-permute-done | bytes 4128 | tf_op jit(solution)/shard_map/ppermute | solution.py:29
  61.0 0.8 %gradient.2 = (bf16[64,1024]{1,0:T(8,128)(2,1)S(1)}, bf16[64,1024]{1,0:T(8,128)(2,1)S(1)}) custom-call(s32[128]{0:T(128)S(1)} %get-tuple-element.46.scal, f32[8,128]{1,0:T(8,128)S(1)} %collective-permute-done.22.refs_0_.refs_1_, f32[8,128]{1,0:T(8,128)S(1)} %collective-permute-done.23.refs_1_.refs_2_, f32[8,128]{1,0:T(8,128)S(1)} %collective-permute-done.24.refs_2_.refs_3_, ...), custom_call_target="tpu_custom_call" | custom-call | flops 1 | bytes 1 | tf_op jit(solution)/shard_map/gradient/pallas_call | solution.py:501
  61.8 2.5 %collective-permute-start.25 = (bf16[64,1024]{1,0:T(8,128)(2,1)S(1)}, bf16[64,1024]{1,0:T(8,128)(2,1)S(1)}, u32[]{:S(2)}, u32[]{:S(2)}) collective-permute-start(bf16[64,1024]{1,0:T(8,128)(2,1)S(1)} %get-tuple-element.86.refs_0_), channel_id=1, source_target_pairs={{0,12},{4,8},{8,4},{12,0},{1,13},{5,9},{9,5},{13,1},{2,14},{6,10},... | collective-permute-start | bytes 393224 | tf_op jit(solution)/shard_map/ppermute | solution.py:29
  64.3 0.8 %gradient.3 = (bf16[64,1024]{1,0:T(8,128)(2,1)S(1)}, bf16[64,1024]{1,0:T(8,128)(2,1)S(1)}) custom-call(s32[128]{0:T(128)S(1)} %get-tuple-element.46.scal, bf16[64,1024]{1,0:T(8,128)(2,1)S(1)} %get-tuple-element.86.refs_0_, f32[8,128]{1,0:T(8,128)S(1)} %collective-permute-done.22.refs_0_.refs_1_, f32[8,128]{1,0:T(8,128)S(1)} %collective-permute-done.23.refs_1_.refs_2_, ...), custom_call_target="tpu_custom_call" | custom-call | flops 1 | bytes 1 | tf_op jit(solution)/shard_map/gradient/pallas_call | solution.py:501
  65.1 2.0 %collective-permute-start.27 = (bf16[64,1024]{1,0:T(8,128)(2,1)S(1)}, bf16[64,1024]{1,0:T(8,128)(2,1)S(1)}, u32[]{:S(2)}, u32[]{:S(2)}) collective-permute-start(bf16[64,1024]{1,0:T(8,128)(2,1)S(1)} %get-tuple-element.89), channel_id=1, source_target_pairs={{0,4},{4,0},{8,12},{12,8},{1,5},{5,1},{9,13},{13,9},{2,6},{6,2},{1... | collective-permute-start | bytes 393224 | tf_op jit(solution)/shard_map/ppermute | solution.py:29
  67.2 3.2 %normed.1 = f32[4,64,1024]{2,1,0:T(8,128)} custom-call(s32[128]{0:T(128)S(1)} %get-tuple-element.46.scal, f32[8,128]{1,0:T(8,128)S(1)} %collective-permute-done.22.refs_0_.refs_1_, f32[8,128]{1,0:T(8,128)S(1)} %collective-permute-done.23.refs_1_.refs_2_, f32[8,128]{1,0:T(8,128)S(1)} %collective-permute-done.24.refs_2_.refs_3_, ...), custom_call_target="tpu_custom_call" | custom-call | flops 1 | bytes 1 | tf_op jit(solution)/shard_map/normed/pallas_call | solution.py:532
  70.4 4.7 %collective-permute-done.26.refs_5_ = bf16[64,1024]{1,0:T(8,128)(2,1)S(1)} collective-permute-done((bf16[64,1024]{1,0:T(8,128)(2,1)S(1)}, bf16[64,1024]{1,0:T(8,128)(2,1)S(1)}, u32[]{:S(2)}, u32[]{:S(2)}) %collective-permute-start.26) | collective-permute-done | bytes 131104 | tf_op jit(solution)/shard_map/ppermute | solution.py:29
  75.1 1.1 %adjoint.1 = f32[128,1024]{1,0:T(8,128)} custom-call(s32[1,64]{1,0:T(1,128)S(1)} %collective-permute-done.1.refs_2_.refs_0_, s32[1,64]{1,0:T(1,128)S(1)} %collective-permute-done.2.refs_3_.refs_1_, s32[1,64]{1,0:T(1,128)S(1)} %get-tuple-element.50.refs_5_.src_ids.refs_2_, s32[1,64]{1,0:T(1,128)S(1)} %collective-permute-done.3.refs_4_.refs_3_, ...), custom_call_target="tpu_custom_call" | custom-call | flops 1 | bytes 1 | tf_op jit(solution)/shard_map/adjoint/pallas_call | solution.py:556
  (55 shorter events, 12.4 us)
Async XLA Ops:
  0.6 22.3 %copy-start.1 = (f32[2,56,1024]{2,1,0:T(8,128)S(1)}, f32[2,56,1024]{2,1,0:T(8,128)}, u32[]{:S(2)}) copy-start(f32[2,56,1024]{2,1,0:T(8,128)} %constant.16.clone.trig) | copy-start | bytes 1376260
  2.0 15.7 %collective-permute-start = (bf16[1,2,128,1024]{3,2,1,0:T(8,128)(2,1)S(1)}, bf16[1,2,128,1024]{3,2,1,0:T(8,128)(2,1)S(1)}, u32[]{:S(2)}, u32[]{:S(2)}) collective-permute-start(bf16[1,2,128,1024]{3,2,1,0:T(8,128)(2,1)S(1)} %get-tuple-element.90), channel_id=1, source_target_pairs={{0,2},{2,0},{1,3},{3,1},{4,6},{6,4},{5,7},{7,5},{8,10},{10,8},{9,1... | collective-permute-start | bytes 1572872 | tf_op jit(solution)/shard_map/ppermute | solution.py:29
  5.6 0.7 copy-start.2
  6.3 0.7 copy-start.3
  9.5 5.4 %collective-permute-start.1 = (s32[1,64]{1,0:T(1,128)S(1)}, s32[1,64]{1,0:T(1,128)S(1)}, u32[]{:S(2)}, u32[]{:S(2)}) collective-permute-start(s32[1,64]{1,0:T(1,128)S(1)} %get-tuple-element.47), channel_id=1, source_target_pairs={{0,12},{4,8},{8,4},{12,0},{1,13},{5,9},{9,5},{13,1},{2,14},{6,10},... | collective-permute-start | bytes 776 | tf_op jit(solution)/shard_map/ppermute | solution.py:29
  13.2 4.4 %collective-permute-start.2 = (s32[1,64]{1,0:T(1,128)S(1)}, s32[1,64]{1,0:T(1,128)S(1)}, u32[]{:S(2)}, u32[]{:S(2)}) collective-permute-start(s32[1,64]{1,0:T(1,128)S(1)} %get-tuple-element.48), channel_id=1, source_target_pairs={{0,8},{4,12},{8,0},{12,4},{1,9},{5,13},{9,1},{13,5},{2,10},{6,14},... | collective-permute-start | bytes 776 | tf_op jit(solution)/shard_map/ppermute | solution.py:29
  13.2 4.4 %collective-permute-start.3 = (s32[1,64]{1,0:T(1,128)S(1)}, s32[1,64]{1,0:T(1,128)S(1)}, u32[]{:S(2)}, u32[]{:S(2)}) collective-permute-start(s32[1,64]{1,0:T(1,128)S(1)} %get-tuple-element.49), channel_id=1, source_target_pairs={{0,4},{4,0},{8,12},{12,8},{1,5},{5,1},{9,13},{13,9},{2,6},{6,2},{1... | collective-permute-start | bytes 776 | tf_op jit(solution)/shard_map/ppermute | solution.py:29
  19.2 7.9 %collective-permute-start.4 = (bf16[1,2,64,1024]{3,2,1,0:T(8,128)(2,1)S(1)}, bf16[1,2,64,1024]{3,2,1,0:T(8,128)(2,1)S(1)}, u32[]{:S(2)}, u32[]{:S(2)}) collective-permute-start(bf16[1,2,64,1024]{3,2,1,0:T(8,128)(2,1)S(1)} %get-tuple-element.54), channel_id=1, source_target_pairs={{0,4},{4,0},{8,12},{12,8},{1,5},{5,1},{9,13},{13,9},{2,6},{6,2},{1... | collective-permute-start | bytes 786440 | tf_op jit(solution)/shard_map/ppermute | solution.py:29
  20.3 15.9 %collective-permute-start.14 = (bf16[1,2,64,1024]{3,2,1,0:T(8,128)(2,1)S(1)}, bf16[1,2,64,1024]{3,2,1,0:T(8,128)(2,1)S(1)}, u32[]{:S(2)}, u32[]{:S(2)}) collective-permute-start(bf16[1,2,64,1024]{3,2,1,0:T(8,128)(2,1)S(1)} %get-tuple-element.69), channel_id=1, source_target_pairs={{0,12},{4,8},{8,4},{12,0},{1,13},{5,9},{9,5},{13,1},{2,14},{6,10},... | collective-permute-start | bytes 786440 | tf_op jit(solution)/shard_map/ppermute | solution.py:29
  22.8 22.1 %collective-permute-start.18 = (bf16[1,2,64,1024]{3,2,1,0:T(8,128)(2,1)S(1)}, bf16[1,2,64,1024]{3,2,1,0:T(8,128)(2,1)S(1)}, u32[]{:S(2)}, u32[]{:S(2)}) collective-permute-start(bf16[1,2,64,1024]{3,2,1,0:T(8,128)(2,1)S(1)} %get-tuple-element.76), channel_id=1, source_target_pairs={{0,8},{4,12},{8,0},{12,4},{1,9},{5,13},{9,1},{13,5},{2,10},{6,14},... | collective-permute-start | bytes 786440 | tf_op jit(solution)/shard_map/ppermute | solution.py:29
  29.8 1.3 %collective-permute-start.5 = (bf16[2,16,1024]{2,1,0:T(8,128)(2,1)S(1)}, bf16[2,16,1024]{2,1,0:T(8,128)(2,1)S(1)}, u32[]{:S(2)}, u32[]{:S(2)}) collective-permute-start(bf16[2,16,1024]{2,1,0:T(8,128)(2,1)S(1)} %get-tuple-element.58), channel_id=1, source_target_pairs={{0,1},{1,0},{2,3},{3,2},{4,5},{5,4},{6,7},{7,6},{8,9},{9,8},{10,11... | collective-permute-start | bytes 196616 | tf_op jit(solution)/shard_map/ppermute | solution.py:29
  29.9 1.4 %collective-permute-start.6 = (bf16[2,16,1024]{2,1,0:T(8,128)(2,1)S(1)}, bf16[2,16,1024]{2,1,0:T(8,128)(2,1)S(1)}, u32[]{:S(2)}, u32[]{:S(2)}) collective-permute-start(bf16[2,16,1024]{2,1,0:T(8,128)(2,1)S(1)} %get-tuple-element.59), channel_id=1, source_target_pairs={{0,1},{1,0},{2,3},{3,2},{4,5},{5,4},{6,7},{7,6},{8,9},{9,8},{10,11... | collective-permute-start | bytes 196616 | tf_op jit(solution)/shard_map/ppermute | solution.py:29
  30.4 1.3 %collective-permute-start.7 = (bf16[2,16,1024]{2,1,0:T(8,128)(2,1)S(1)}, bf16[2,16,1024]{2,1,0:T(8,128)(2,1)S(1)}, u32[]{:S(2)}, u32[]{:S(2)}) collective-permute-start(bf16[2,16,1024]{2,1,0:T(8,128)(2,1)S(1)} %get-tuple-element.60), channel_id=1, source_target_pairs={{0,1},{1,0},{2,3},{3,2},{4,5},{5,4},{6,7},{7,6},{8,9},{9,8},{10,11... | collective-permute-start | bytes 196616 | tf_op jit(solution)/shard_map/ppermute | solution.py:29
  31.2 1.3 %collective-permute-start.8 = (bf16[2,16,1024]{2,1,0:T(8,128)(2,1)S(1)}, bf16[2,16,1024]{2,1,0:T(8,128)(2,1)S(1)}, u32[]{:S(2)}, u32[]{:S(2)}) collective-permute-start(bf16[2,16,1024]{2,1,0:T(8,128)(2,1)S(1)} %get-tuple-element.61), channel_id=1, source_target_pairs={{0,1},{1,0},{2,3},{3,2},{4,5},{5,4},{6,7},{7,6},{8,9},{9,8},{10,11... | collective-permute-start | bytes 196616 | tf_op jit(solution)/shard_map/ppermute | solution.py:29
  31.3 1.3 %collective-permute-start.9 = (bf16[2,16,1024]{2,1,0:T(8,128)(2,1)S(1)}, bf16[2,16,1024]{2,1,0:T(8,128)(2,1)S(1)}, u32[]{:S(2)}, u32[]{:S(2)}) collective-permute-start(bf16[2,16,1024]{2,1,0:T(8,128)(2,1)S(1)} %get-tuple-element.62), channel_id=1, source_target_pairs={{0,1},{1,0},{2,3},{3,2},{4,5},{5,4},{6,7},{7,6},{8,9},{9,8},{10,11... | collective-permute-start | bytes 196616 | tf_op jit(solution)/shard_map/ppermute | solution.py:29
  31.7 1.3 %collective-permute-start.10 = (bf16[2,16,1024]{2,1,0:T(8,128)(2,1)S(1)}, bf16[2,16,1024]{2,1,0:T(8,128)(2,1)S(1)}, u32[]{:S(2)}, u32[]{:S(2)}) collective-permute-start(bf16[2,16,1024]{2,1,0:T(8,128)(2,1)S(1)} %get-tuple-element.63), channel_id=1, source_target_pairs={{0,1},{1,0},{2,3},{3,2},{4,5},{5,4},{6,7},{7,6},{8,9},{9,8},{10,11... | collective-permute-start | bytes 196616 | tf_op jit(solution)/shard_map/ppermute | solution.py:29
  32.4 1.3 %collective-permute-start.11 = (bf16[2,16,1024]{2,1,0:T(8,128)(2,1)S(1)}, bf16[2,16,1024]{2,1,0:T(8,128)(2,1)S(1)}, u32[]{:S(2)}, u32[]{:S(2)}) collective-permute-start(bf16[2,16,1024]{2,1,0:T(8,128)(2,1)S(1)} %get-tuple-element.64), channel_id=1, source_target_pairs={{0,1},{1,0},{2,3},{3,2},{4,5},{5,4},{6,7},{7,6},{8,9},{9,8},{10,11... | collective-permute-start | bytes 196616 | tf_op jit(solution)/shard_map/ppermute | solution.py:29
  32.6 1.3 %collective-permute-start.12 = (bf16[2,16,1024]{2,1,0:T(8,128)(2,1)S(1)}, bf16[2,16,1024]{2,1,0:T(8,128)(2,1)S(1)}, u32[]{:S(2)}, u32[]{:S(2)}) collective-permute-start(bf16[2,16,1024]{2,1,0:T(8,128)(2,1)S(1)} %get-tuple-element.65), channel_id=1, source_target_pairs={{0,1},{1,0},{2,3},{3,2},{4,5},{5,4},{6,7},{7,6},{8,9},{9,8},{10,11... | collective-permute-start | bytes 196616 | tf_op jit(solution)/shard_map/ppermute | solution.py:29
  34.7 12.7 %collective-permute-start.13 = (bf16[128,1024]{1,0:T(8,128)(2,1)S(1)}, bf16[128,1024]{1,0:T(8,128)(2,1)S(1)}, u32[]{:S(2)}, u32[]{:S(2)}) collective-permute-start(bf16[128,1024]{1,0:T(8,128)(2,1)S(1)} %get-tuple-element.67), channel_id=1, source_target_pairs={{0,2},{2,0},{1,3},{3,1},{4,6},{6,4},{5,7},{7,5},{8,10},{10,8},{9,1... | collective-permute-start | bytes 786440 | tf_op jit(solution)/shard_map/ppermute | solution.py:29
  38.0 9.3 %collective-permute-start.15 = (bf16[2,32,1024]{2,1,0:T(8,128)(2,1)S(1)}, bf16[2,32,1024]{2,1,0:T(8,128)(2,1)S(1)}, u32[]{:S(2)}, u32[]{:S(2)}) collective-permute-start(bf16[2,32,1024]{2,1,0:T(8,128)(2,1)S(1)} %get-tuple-element.71), channel_id=1, source_target_pairs={{0,1},{1,0},{2,3},{3,2},{4,5},{5,4},{6,7},{7,6},{8,9},{9,8},{10,11... | collective-permute-start | bytes 393224 | tf_op jit(solution)/shard_map/ppermute | solution.py:29
  38.1 12.6 %copy-start = (f32[4,64,1024]{2,1,0:T(8,128)S(1)}, f32[4,64,1024]{2,1,0:T(8,128)}, u32[]{:S(2)}) copy-start(f32[4,64,1024]{2,1,0:T(8,128)} %refs_7_.3) | copy-start | bytes 3145732
  38.1 9.2 %collective-permute-start.16 = (bf16[2,32,1024]{2,1,0:T(8,128)(2,1)S(1)}, bf16[2,32,1024]{2,1,0:T(8,128)(2,1)S(1)}, u32[]{:S(2)}, u32[]{:S(2)}) collective-permute-start(bf16[2,32,1024]{2,1,0:T(8,128)(2,1)S(1)} %get-tuple-element.72), channel_id=1, source_target_pairs={{0,1},{1,0},{2,3},{3,2},{4,5},{5,4},{6,7},{7,6},{8,9},{9,8},{10,11... | collective-permute-start | bytes 393224 | tf_op jit(solution)/shard_map/ppermute | solution.py:29
  46.7 2.8 %collective-permute-start.19 = (bf16[2,32,1024]{2,1,0:T(8,128)(2,1)S(1)}, bf16[2,32,1024]{2,1,0:T(8,128)(2,1)S(1)}, u32[]{:S(2)}, u32[]{:S(2)}) collective-permute-start(bf16[2,32,1024]{2,1,0:T(8,128)(2,1)S(1)} %get-tuple-element.78), channel_id=1, source_target_pairs={{0,1},{1,0},{2,3},{3,2},{4,5},{5,4},{6,7},{7,6},{8,9},{9,8},{10,11... | collective-permute-start | bytes 393224 | tf_op jit(solution)/shard_map/ppermute | solution.py:29
  46.8 2.7 %collective-permute-start.20 = (bf16[2,32,1024]{2,1,0:T(8,128)(2,1)S(1)}, bf16[2,32,1024]{2,1,0:T(8,128)(2,1)S(1)}, u32[]{:S(2)}, u32[]{:S(2)}) collective-permute-start(bf16[2,32,1024]{2,1,0:T(8,128)(2,1)S(1)} %get-tuple-element.79), channel_id=1, source_target_pairs={{0,1},{1,0},{2,3},{3,2},{4,5},{5,4},{6,7},{7,6},{8,9},{9,8},{10,11... | collective-permute-start | bytes 393224 | tf_op jit(solution)/shard_map/ppermute | solution.py:29
  48.0 6.4 %collective-permute-start.17 = (bf16[64,1024]{1,0:T(8,128)(2,1)S(1)}, bf16[64,1024]{1,0:T(8,128)(2,1)S(1)}, u32[]{:S(2)}, u32[]{:S(2)}) collective-permute-start(bf16[64,1024]{1,0:T(8,128)(2,1)S(1)} %get-tuple-element.74), channel_id=1, source_target_pairs={{0,2},{2,0},{1,3},{3,1},{4,6},{6,4},{5,7},{7,5},{8,10},{10,8},{9,1... | collective-permute-start | bytes 393224 | tf_op jit(solution)/shard_map/ppermute | solution.py:29
  50.2 6.2 %collective-permute-start.21 = (bf16[64,1024]{1,0:T(8,128)(2,1)S(1)}, bf16[64,1024]{1,0:T(8,128)(2,1)S(1)}, u32[]{:S(2)}, u32[]{:S(2)}) collective-permute-start(bf16[64,1024]{1,0:T(8,128)(2,1)S(1)} %get-tuple-element.81), channel_id=1, source_target_pairs={{0,2},{2,0},{1,3},{3,1},{4,6},{6,4},{5,7},{7,5},{8,10},{10,8},{9,1... | collective-permute-start | bytes 393224 | tf_op jit(solution)/shard_map/ppermute | solution.py:29
  57.0 3.1 %collective-permute-start.22 = (f32[8,128]{1,0:T(8,128)S(1)}, f32[8,128]{1,0:T(8,128)S(1)}, u32[]{:S(2)}, u32[]{:S(2)}) collective-permute-start(f32[8,128]{1,0:T(8,128)S(1)} %get-tuple-element.82.refs_3_.refs_4_), channel_id=1, source_target_pairs={{0,3},{1,2},{2,1},{3,0},{4,7},{5,6},{6,5},{7,4},{8,11},{9,10},{10,... | collective-permute-start | bytes 12296 | tf_op jit(solution)/shard_map/ppermute | solution.py:29
  57.4 3.6 %collective-permute-start.23 = (f32[8,128]{1,0:T(8,128)S(1)}, f32[8,128]{1,0:T(8,128)S(1)}, u32[]{:S(2)}, u32[]{:S(2)}) collective-permute-start(f32[8,128]{1,0:T(8,128)S(1)} %get-tuple-element.82.refs_3_.refs_4_), channel_id=1, source_target_pairs={{0,2},{1,3},{2,0},{3,1},{4,6},{5,7},{6,4},{7,5},{8,10},{9,11},{10,... | collective-permute-start | bytes 12296 | tf_op jit(solution)/shard_map/ppermute | solution.py:29
  58.6 2.4 %collective-permute-start.24 = (f32[8,128]{1,0:T(8,128)S(1)}, f32[8,128]{1,0:T(8,128)S(1)}, u32[]{:S(2)}, u32[]{:S(2)}) collective-permute-start(f32[8,128]{1,0:T(8,128)S(1)} %get-tuple-element.82.refs_3_.refs_4_), channel_id=1, source_target_pairs={{0,1},{1,0},{2,3},{3,2},{4,5},{5,4},{6,7},{7,6},{8,9},{9,8},{10,11... | collective-permute-start | bytes 12296 | tf_op jit(solution)/shard_map/ppermute | solution.py:29
  61.8 8.5 %collective-permute-start.25 = (bf16[64,1024]{1,0:T(8,128)(2,1)S(1)}, bf16[64,1024]{1,0:T(8,128)(2,1)S(1)}, u32[]{:S(2)}, u32[]{:S(2)}) collective-permute-start(bf16[64,1024]{1,0:T(8,128)(2,1)S(1)} %get-tuple-element.86.refs_0_), channel_id=1, source_target_pairs={{0,12},{4,8},{8,4},{12,0},{1,13},{5,9},{9,5},{13,1},{2,14},{6,10},... | collective-permute-start | bytes 393224 | tf_op jit(solution)/shard_map/ppermute | solution.py:29
  64.3 10.8 %collective-permute-start.26 = (bf16[64,1024]{1,0:T(8,128)(2,1)S(1)}, bf16[64,1024]{1,0:T(8,128)(2,1)S(1)}, u32[]{:S(2)}, u32[]{:S(2)}) collective-permute-start(bf16[64,1024]{1,0:T(8,128)(2,1)S(1)} %get-tuple-element.87), channel_id=1, source_target_pairs={{0,8},{4,12},{8,0},{12,4},{1,9},{5,13},{9,1},{13,5},{2,10},{6,14},... | collective-permute-start | bytes 393224 | tf_op jit(solution)/shard_map/ppermute | solution.py:29
  65.1 10.0 %collective-permute-start.27 = (bf16[64,1024]{1,0:T(8,128)(2,1)S(1)}, bf16[64,1024]{1,0:T(8,128)(2,1)S(1)}, u32[]{:S(2)}, u32[]{:S(2)}) collective-permute-start(bf16[64,1024]{1,0:T(8,128)(2,1)S(1)} %get-tuple-element.89), channel_id=1, source_target_pairs={{0,4},{4,0},{8,12},{12,8},{1,5},{5,1},{9,13},{13,9},{2,6},{6,2},{1... | collective-permute-start | bytes 393224 | tf_op jit(solution)/shard_map/ppermute | solution.py:29
  (2 other events, 1.3 us)

commit v21 on v20

--- a/solution.py
+++ b/solution.py
@@ -627,7 +627,7 @@
     after = []
     for q, pieces in enumerate(chunks):
         rows, arrived = arrived[: len(pieces)], arrived[len(pieces) :]
-        groups = sum(p[2] for p in pieces) // (32 if q else 16)
+        groups = sum(p[2] for p in pieces) // (64 if q else 16)
         if q:
             keep, *sends = cross_lag_parts(
                 scal,

time: 76.4 us -> 76.3 us (level)
    ppermute x28 -> x26, starting transfers between devices: 24.3 us -> 23.6 us  [swapped(): return lax.ppermute(value, axis, [(i, i ^ step) for i in range(size)])]
    ppermute x28 -> x26, waiting for transfers between devices: 23.5 us -> 24 us  [swapped(): return lax.ppermute(value, axis, [(i, i ^ step) for i in range(size)])]
  transfers between devices with their start and end apart: 28 -> 26, of which waited for: 13 -> 13; matrix products, arithmetic and copies ran while one was open for 0% -> 0% of each run, Pallas kernels for 25% -> 25%
where the time goes in v21:
time: 76.3 us; the launch traced here: 76.1 us
  waiting for transfers between devices  24 us (31%)
  starting transfers between devices  23.6 us (31%)
  Pallas kernels  23 us (30%)
  local copies, waits for them, and re-layouts  4 us (5%)
  between operations  1.48 us (2%)
    ppermute x26, waiting for transfers between devices, swapped(): return lax.ppermute(value, axis, [(i, i ^ step) for i in range(size)])  24 us
    ppermute x26, starting transfers between devices, swapped(): return lax.ppermute(value, axis, [(i, i ^ step) for i in range(size)])  23.6 us
    pallas_call x2, Pallas kernels, cross_lag_parts(): pl.pallas_call(functools.partial(cross_lags_kernel, geometry, split, len(...  3.59 us
    pallas_call x1, Pallas kernels, normed_rows(): pl.pallas_call(functools.partial(normed_kernel, lag_total, chunks, len(su...  3.22 us
    pallas_call x1, Pallas kernels, gather_own(): pl.pallas_call(functools.partial(own_kernel, classes, parts), out_shape=[...  3.14 us
    unnamed x12, local copies, waits for them, and re-layouts  2.68 us
    pallas_call x1, Pallas kernels, lag_parts(): pl.pallas_call(functools.partial(lags_kernel, geometry, split, len(after)...  2.47 us
    pallas_call x3, Pallas kernels, lag_stats(): pl.pallas_call(functools.partial(stats_kernel, scale, q, pieces, len(more...  2.22 us
  transfers between devices with their start and end apart: 26, of which 13 were waited for; matrix products, arithmetic and copies ran while one was open for 0% of the time, Pallas kernels for 25%

profile of v21, /device:TPU:0, one launch (start us, length us, event | category | flops | bytes accessed | tf_op | source)
XLA Modules:
  0.0 76.1 jit_solution(3767736843887557032)
XLA Ops:
  0.7 1.3 %constant_dynamic-slice_fusion = (bf16[1,2,128,1024]{3,2,1,0:T(8,128)(2,1)S(1)}, bf16[1,2,128,1024]{3,2,1,0:T(8,128)(2,1)S(1)}) fusion(bf16[1,2,128,2048]{3,2,1,0:T(8,128)(2,1)} %param.8, s32[]{:T(128)S(6)} %select_n.7, s32[]{:T(128)S(6)} %select_n.6), kind=kLoop, calls=%fused_computation | loop fusion | bytes 2097160 | tf_op jit(solution)/shard_map/dynamic_slice | solution.py:586
  2.0 3.0 %collective-permute-start = (bf16[1,2,128,1024]{3,2,1,0:T(8,128)(2,1)S(1)}, bf16[1,2,128,1024]{3,2,1,0:T(8,128)(2,1)S(1)}, u32[]{:S(2)}, u32[]{:S(2)}) collective-permute-start(bf16[1,2,128,1024]{3,2,1,0:T(8,128)(2,1)S(1)} %get-tuple-element.86), channel_id=1, source_target_pairs={{0,2},{2,0},{1,3},{3,1},{4,6},{6,4},{5,7},{7,5},{8,10},{10,8},{9,1... | collective-permute-start | bytes 1572872 | tf_op jit(solution)/shard_map/ppermute | solution.py:29
  8.3 1.2 %index.1 = (s32[128]{0:T(128)S(1)}, s32[1,64]{1,0:T(1,128)S(1)}, s32[1,64]{1,0:T(1,128)S(1)}, s32[1,64]{1,0:T(1,128)S(1)}, s32[1,64]{1,0:T(1,128)S(1)}, /*index=5*/s32[4,64]{1,0:T(4,128)S(1)}) custom-call(s32[1]{0:T(128)S(6)} %copy.10.refs_0_, s32[4]{0:T(128)S(1)} %copy-done.4, s32[4]{0:T(128)S(1)} %bitcast.1, s32[4,64]{1,0:T(4,128)S(1)} %copy-done.2, ...), custom_call_target="tpu_custom_call" | custom-call | flops 1 | bytes 1 | tf_op jit(solution)/shard_map/index/pallas_call | solution.py:92
  9.5 3.7 %collective-permute-start.1 = (s32[1,64]{1,0:T(1,128)S(1)}, s32[1,64]{1,0:T(1,128)S(1)}, u32[]{:S(2)}, u32[]{:S(2)}) collective-permute-start(s32[1,64]{1,0:T(1,128)S(1)} %get-tuple-element.45), channel_id=1, source_target_pairs={{0,12},{4,8},{8,4},{12,0},{1,13},{5,9},{9,5},{13,1},{2,14},{6,10},... | collective-permute-start | bytes 776 | tf_op jit(solution)/shard_map/ppermute | solution.py:29
  13.2 0.8 %collective-permute-start.3 = (s32[1,64]{1,0:T(1,128)S(1)}, s32[1,64]{1,0:T(1,128)S(1)}, u32[]{:S(2)}, u32[]{:S(2)}) collective-permute-start(s32[1,64]{1,0:T(1,128)S(1)} %get-tuple-element.47), channel_id=1, source_target_pairs={{0,4},{4,0},{8,12},{12,8},{1,5},{5,1},{9,13},{13,9},{2,6},{6,2},{1... | collective-permute-start | bytes 776 | tf_op jit(solution)/shard_map/ppermute | solution.py:29
  14.9 2.7 %collective-permute-done.2.refs_3_.refs_1_ = s32[1,64]{1,0:T(1,128)S(1)} collective-permute-done((s32[1,64]{1,0:T(1,128)S(1)}, s32[1,64]{1,0:T(1,128)S(1)}, u32[]{:S(2)}, u32[]{:S(2)}) %collective-permute-start.2) | collective-permute-done | bytes 288 | tf_op jit(solution)/shard_map/ppermute | solution.py:29
  17.7 1.5 %rows.1 = (bf16[1,2,64,1024]{3,2,1,0:T(8,128)(2,1)S(1)}, bf16[1,2,64,1024]{3,2,1,0:T(8,128)(2,1)S(1)}, bf16[1,2,64,1024]{3,2,1,0:T(8,128)(2,1)S(1)}, bf16[1,2,128,1024]{3,2,1,0:T(8,128)(2,1)S(1)}) custom-call(s32[128]{0:T(128)S(1)} %get-tuple-element.44.scal, bf16[1,2,128,1024]{3,2,1,0:T(8,128)(2,1)S(1)} %get-tuple-element.87.here, ...), custom_call_target="tpu_custom_call" | custom-call | flops 1 | bytes 1 | tf_op jit(solution)/shard_map/rows/pallas_call | solution.py:175
  19.2 1.1 %collective-permute-start.4 = (bf16[1,2,64,1024]{3,2,1,0:T(8,128)(2,1)S(1)}, bf16[1,2,64,1024]{3,2,1,0:T(8,128)(2,1)S(1)}, u32[]{:S(2)}, u32[]{:S(2)}) collective-permute-start(bf16[1,2,64,1024]{3,2,1,0:T(8,128)(2,1)S(1)} %get-tuple-element.52), channel_id=1, source_target_pairs={{0,4},{4,0},{8,12},{12,8},{1,5},{5,1},{9,13},{13,9},{2,6},{6,2},{1... | collective-permute-start | bytes 786440 | tf_op jit(solution)/shard_map/ppermute | solution.py:29
  20.3 2.5 %collective-permute-start.14 = (bf16[1,2,64,1024]{3,2,1,0:T(8,128)(2,1)S(1)}, bf16[1,2,64,1024]{3,2,1,0:T(8,128)(2,1)S(1)}, u32[]{:S(2)}, u32[]{:S(2)}) collective-permute-start(bf16[1,2,64,1024]{3,2,1,0:T(8,128)(2,1)S(1)} %get-tuple-element.67), channel_id=1, source_target_pairs={{0,12},{4,8},{8,4},{12,0},{1,13},{5,9},{9,5},{13,1},{2,14},{6,10},... | collective-permute-start | bytes 786440 | tf_op jit(solution)/shard_map/ppermute | solution.py:29
  22.9 3.1 %own.1 = (bf16[1,2,64,1024]{3,2,1,0:T(8,128)(2,1)S(1)}, bf16[4,1,2,64,1024]{4,3,2,1,0:T(8,128)(2,1)S(1)}, bf16[8,256,1024]{2,1,0:T(8,128)(2,1)S(1)}) custom-call(s32[128]{0:T(128)S(1)} %get-tuple-element.44.scal, bf16[1,2,128,1024]{3,2,1,0:T(8,128)(2,1)S(1)} %get-tuple-element.49.kept, s32[1,64]{1,0:T(1,128)S(1)} %get-tuple-element.48.refs_5_.src_ids.refs_2_, ...), custom_call_target="tpu_custom_call" | custom-call | flops 1 | bytes 1 | tf_op jit(solution)/shard_map/own/pallas_call | solution.py:206
  26.1 1.0 %collective-permute-done.4.refs_1_ = bf16[1,2,64,1024]{3,2,1,0:T(8,128)(2,1)S(1)} collective-permute-done((bf16[1,2,64,1024]{3,2,1,0:T(8,128)(2,1)S(1)}, bf16[1,2,64,1024]{3,2,1,0:T(8,128)(2,1)S(1)}, u32[]{:S(2)}, u32[]{:S(2)}) %collective-permute-start.4) | collective-permute-done | bytes 262176 | tf_op jit(solution)/shard_map/ppermute | solution.py:29
  27.4 2.5 %lags.1 = (f32[2,128,1024]{2,1,0:T(8,128)S(1)}, bf16[2,16,1024]{2,1,0:T(8,128)(2,1)S(1)}, bf16[2,16,1024]{2,1,0:T(8,128)(2,1)S(1)}, bf16[2,16,1024]{2,1,0:T(8,12...) custom-call(s32[128]{0:T(128)S(1)} %get-tuple-element.44.scal, ...), custom_call_target="tpu_custom_call" | custom-call | flops 20000000000 | bytes 1048576 | tf_op jit(solution)/shard_map/lags/pallas_call | solution.py:334
  33.8 0.8 %cores.3 = (f32[128,1024]{1,0:T(8,128)S(1)}, bf16[128,1024]{1,0:T(8,128)(2,1)S(1)}) custom-call(s32[128]{0:T(128)S(1)} %get-tuple-element.44.scal, f32[2,128,1024]{2,1,0:T(8,128)S(1)} %get-tuple-element.55.refs_0_, bf16[2,16,1024]{2,1,0:T(8,128)(2,1)S(1)} %collective-permute-done.5.refs_1_, bf16[2,16,1024]{2,1,0:T(8,128)(2,1)S(1)} %collective-permute-done.6.refs_2_, ...), custom_call_target="tpu_custom_call" | custom-call | flops 1 | bytes 1 | tf_op jit(solution)/shard_map/cores/pallas_call | solution.py:397
  34.7 1.5 %collective-permute-start.13 = (bf16[128,1024]{1,0:T(8,128)(2,1)S(1)}, bf16[128,1024]{1,0:T(8,128)(2,1)S(1)}, u32[]{:S(2)}, u32[]{:S(2)}) collective-permute-start(bf16[128,1024]{1,0:T(8,128)(2,1)S(1)} %get-tuple-element.65), channel_id=1, source_target_pairs={{0,2},{2,0},{1,3},{3,1},{4,6},{6,4},{5,7},{7,5},{8,10},{10,8},{9,1... | collective-permute-start | bytes 786440 | tf_op jit(solution)/shard_map/ppermute | solution.py:29
  36.2 1.8 %cross_lags.2 = (f32[2,64,1024]{2,1,0:T(8,128)S(1)}, bf16[2,64,1024]{2,1,0:T(8,128)(2,1)S(1)}) custom-call(s32[128]{0:T(128)S(1)} %get-tuple-element.44.scal, f32[1]{0:T(128)} %constant.3.clone.1.weight, f32[128,1024]{1,0:T(8,128)S(1)} %get-tuple-element.64.refs_0_, bf16[1,2,64,1024]{3,2,1,0:T(8,128)(2,1)S(1)} %collective-permute-done.14.refs_1_, ...), custom_call_target="tpu_custom_call" | custom-call | flops 1 | bytes 1 | tf_op jit(solution)/shard_map/cross_lags/pallas_call | solution.py:361
  38.2 6.8 %collective-permute-done.17.refs_0_ = bf16[1,2,64,1024]{3,2,1,0:T(8,128)(2,1)S(1)} collective-permute-done((bf16[1,2,64,1024]{3,2,1,0:T(8,128)(2,1)S(1)}, bf16[1,2,64,1024]{3,2,1,0:T(8,128)(2,1)S(1)}, u32[]{:S(2)}, u32[]{:S(2)}) %collective-permute-start.17) | collective-permute-done | bytes 262176 | tf_op jit(solution)/shard_map/ppermute | solution.py:29
  44.9 1.8 %cross_lags.3 = (f32[2,64,1024]{2,1,0:T(8,128)S(1)}, bf16[2,64,1024]{2,1,0:T(8,128)(2,1)S(1)}) custom-call(s32[128]{0:T(128)S(1)} %get-tuple-element.44.scal, f32[1]{0:T(128)} %constant.3.clone.1.weight, bf16[1,2,64,1024]{3,2,1,0:T(8,128)(2,1)S(1)} %collective-permute-done.17.refs_0_, bf16[4,1,2,64,1024]{4,3,2,1,0:T(8,128)(2,1)S(1)} %get-tuple-element.53.refs_2_.refs_1_, ...), custom_call_target="tpu_custom_call" | custom-call | flops 20000000000 | bytes 1048576 | tf_op jit(solution)/shard_map/cross_lags/pallas_call | solution.py:361
  47.5 1.6 %collective-permute-start.16 = (bf16[64,1024]{1,0:T(8,128)(2,1)S(1)}, bf16[64,1024]{1,0:T(8,128)(2,1)S(1)}, u32[]{:S(2)}, u32[]{:S(2)}) collective-permute-start(bf16[64,1024]{1,0:T(8,128)(2,1)S(1)} %get-tuple-element.71), channel_id=1, source_target_pairs={{0,2},{2,0},{1,3},{3,1},{4,6},{6,4},{5,7},{7,5},{8,10},{10,8},{9,1... | collective-permute-start | bytes 393224 | tf_op jit(solution)/shard_map/ppermute | solution.py:29
  49.6 0.9 %collective-permute-start.19 = (bf16[64,1024]{1,0:T(8,128)(2,1)S(1)}, bf16[64,1024]{1,0:T(8,128)(2,1)S(1)}, u32[]{:S(2)}, u32[]{:S(2)}) collective-permute-start(bf16[64,1024]{1,0:T(8,128)(2,1)S(1)} %get-tuple-element.77), channel_id=1, source_target_pairs={{0,2},{2,0},{1,3},{3,1},{4,6},{6,4},{5,7},{7,5},{8,10},{10,8},{9,1... | collective-permute-start | bytes 393224 | tf_op jit(solution)/shard_map/ppermute | solution.py:29
  51.3 2.5 %collective-permute-done.16.refs_2_ = bf16[64,1024]{1,0:T(8,128)(2,1)S(1)} collective-permute-done((bf16[64,1024]{1,0:T(8,128)(2,1)S(1)}, bf16[64,1024]{1,0:T(8,128)(2,1)S(1)}, u32[]{:S(2)}, u32[]{:S(2)}) %collective-permute-start.16) | collective-permute-done | bytes 131104 | tf_op jit(solution)/shard_map/ppermute | solution.py:29
  54.5 1.7 %collective-permute-done.19.refs_2_ = bf16[64,1024]{1,0:T(8,128)(2,1)S(1)} collective-permute-done((bf16[64,1024]{1,0:T(8,128)(2,1)S(1)}, bf16[64,1024]{1,0:T(8,128)(2,1)S(1)}, u32[]{:S(2)}, u32[]{:S(2)}) %collective-permute-start.19) | collective-permute-done | bytes 131104 | tf_op jit(solution)/shard_map/ppermute | solution.py:29
  56.9 0.8 %collective-permute-start.20 = (f32[8,128]{1,0:T(8,128)S(1)}, f32[8,128]{1,0:T(8,128)S(1)}, u32[]{:S(2)}, u32[]{:S(2)}) collective-permute-start(f32[8,128]{1,0:T(8,128)S(1)} %get-tuple-element.78.refs_3_.refs_4_), channel_id=1, source_target_pairs={{0,3},{1,2},{2,1},{3,0},{4,7},{5,6},{6,5},{7,4},{8,11},{9,10},{10,... | collective-permute-start | bytes 12296 | tf_op jit(solution)/shard_map/ppermute | solution.py:29
  57.8 0.8 %collective-permute-start.21 = (f32[8,128]{1,0:T(8,128)S(1)}, f32[8,128]{1,0:T(8,128)S(1)}, u32[]{:S(2)}, u32[]{:S(2)}) collective-permute-start(f32[8,128]{1,0:T(8,128)S(1)} %get-tuple-element.78.refs_3_.refs_4_), channel_id=1, source_target_pairs={{0,2},{1,3},{2,0},{3,1},{4,6},{5,7},{6,4},{7,5},{8,10},{9,11},{10,... | collective-permute-start | bytes 12296 | tf_op jit(solution)/shard_map/ppermute | solution.py:29
  58.8 1.2 %collective-permute-done.20.refs_0_.refs_1_ = f32[8,128]{1,0:T(8,128)S(1)} collective-permute-done((f32[8,128]{1,0:T(8,128)S(1)}, f32[8,128]{1,0:T(8,128)S(1)}, u32[]{:S(2)}, u32[]{:S(2)}) %collective-permute-start.20) | collective-permute-done | bytes 4128 | tf_op jit(solution)/shard_map/ppermute | solution.py:29
  60.0 1.4 %collective-permute-done.21.refs_1_.refs_2_ = f32[8,128]{1,0:T(8,128)S(1)} collective-permute-done((f32[8,128]{1,0:T(8,128)S(1)}, f32[8,128]{1,0:T(8,128)S(1)}, u32[]{:S(2)}, u32[]{:S(2)}) %collective-permute-start.21) | collective-permute-done | bytes 4128 | tf_op jit(solution)/shard_map/ppermute | solution.py:29
  61.4 0.8 %gradient.2 = (bf16[64,1024]{1,0:T(8,128)(2,1)S(1)}, bf16[64,1024]{1,0:T(8,128)(2,1)S(1)}) custom-call(s32[128]{0:T(128)S(1)} %get-tuple-element.44.scal, f32[8,128]{1,0:T(8,128)S(1)} %collective-permute-done.20.refs_0_.refs_1_, f32[8,128]{1,0:T(8,128)S(1)} %collective-permute-done.21.refs_1_.refs_2_, f32[8,128]{1,0:T(8,128)S(1)} %collective-permute-done.22.refs_2_.refs_3_, ...), custom_call_target="tpu_custom_call" | custom-call | flops 1 | bytes 1 | tf_op jit(solution)/shard_map/gradient/pallas_call | solution.py:501
  62.2 2.0 %collective-permute-start.23 = (bf16[64,1024]{1,0:T(8,128)(2,1)S(1)}, bf16[64,1024]{1,0:T(8,128)(2,1)S(1)}, u32[]{:S(2)}, u32[]{:S(2)}) collective-permute-start(bf16[64,1024]{1,0:T(8,128)(2,1)S(1)} %get-tuple-element.82.refs_0_), channel_id=1, source_target_pairs={{0,12},{4,8},{8,4},{12,0},{1,13},{5,9},{9,5},{13,1},{2,14},{6,10},... | collective-permute-start | bytes 393224 | tf_op jit(solution)/shard_map/ppermute | solution.py:29
  64.2 0.8 %gradient.3 = (bf16[64,1024]{1,0:T(8,128)(2,1)S(1)}, bf16[64,1024]{1,0:T(8,128)(2,1)S(1)}) custom-call(s32[128]{0:T(128)S(1)} %get-tuple-element.44.scal, bf16[64,1024]{1,0:T(8,128)(2,1)S(1)} %get-tuple-element.82.refs_0_, f32[8,128]{1,0:T(8,128)S(1)} %collective-permute-done.20.refs_0_.refs_1_, f32[8,128]{1,0:T(8,128)S(1)} %collective-permute-done.21.refs_1_.refs_2_, ...), custom_call_target="tpu_custom_call" | custom-call | flops 1 | bytes 1 | tf_op jit(solution)/shard_map/gradient/pallas_call | solution.py:501
  65.0 2.5 %collective-permute-start.25 = (bf16[64,1024]{1,0:T(8,128)(2,1)S(1)}, bf16[64,1024]{1,0:T(8,128)(2,1)S(1)}, u32[]{:S(2)}, u32[]{:S(2)}) collective-permute-start(bf16[64,1024]{1,0:T(8,128)(2,1)S(1)} %get-tuple-element.85), channel_id=1, source_target_pairs={{0,4},{4,0},{8,12},{12,8},{1,5},{5,1},{9,13},{13,9},{2,6},{6,2},{1... | collective-permute-start | bytes 393224 | tf_op jit(solution)/shard_map/ppermute | solution.py:29
  67.5 3.2 %normed.1 = f32[4,64,1024]{2,1,0:T(8,128)} custom-call(s32[128]{0:T(128)S(1)} %get-tuple-element.44.scal, f32[8,128]{1,0:T(8,128)S(1)} %collective-permute-done.20.refs_0_.refs_1_, f32[8,128]{1,0:T(8,128)S(1)} %collective-permute-done.21.refs_1_.refs_2_, f32[8,128]{1,0:T(8,128)S(1)} %collective-permute-done.22.refs_2_.refs_3_, ...), custom_call_target="tpu_custom_call" | custom-call | flops 1 | bytes 1 | tf_op jit(solution)/shard_map/normed/pallas_call | solution.py:532
  70.8 4.3 %collective-permute-done.24.refs_5_ = bf16[64,1024]{1,0:T(8,128)(2,1)S(1)} collective-permute-done((bf16[64,1024]{1,0:T(8,128)(2,1)S(1)}, bf16[64,1024]{1,0:T(8,128)(2,1)S(1)}, u32[]{:S(2)}, u32[]{:S(2)}) %collective-permute-start.24) | collective-permute-done | bytes 131104 | tf_op jit(solution)/shard_map/ppermute | solution.py:29
  75.0 1.1 %adjoint.1 = f32[128,1024]{1,0:T(8,128)} custom-call(s32[1,64]{1,0:T(1,128)S(1)} %collective-permute-done.1.refs_2_.refs_0_, s32[1,64]{1,0:T(1,128)S(1)} %collective-permute-done.2.refs_3_.refs_1_, s32[1,64]{1,0:T(1,128)S(1)} %get-tuple-element.48.refs_5_.src_ids.refs_2_, s32[1,64]{1,0:T(1,128)S(1)} %collective-permute-done.3.refs_4_.refs_3_, ...), custom_call_target="tpu_custom_call" | custom-call | flops 1 | bytes 1 | tf_op jit(solution)/shard_map/adjoint/pallas_call | solution.py:556
  (51 shorter events, 12.0 us)
Async XLA Ops:
  0.6 22.3 %copy-start.1 = (f32[2,56,1024]{2,1,0:T(8,128)S(1)}, f32[2,56,1024]{2,1,0:T(8,128)}, u32[]{:S(2)}) copy-start(f32[2,56,1024]{2,1,0:T(8,128)} %constant.16.clone.trig) | copy-start | bytes 1376260
  2.0 15.7 %collective-permute-start = (bf16[1,2,128,1024]{3,2,1,0:T(8,128)(2,1)S(1)}, bf16[1,2,128,1024]{3,2,1,0:T(8,128)(2,1)S(1)}, u32[]{:S(2)}, u32[]{:S(2)}) collective-permute-start(bf16[1,2,128,1024]{3,2,1,0:T(8,128)(2,1)S(1)} %get-tuple-element.86), channel_id=1, source_target_pairs={{0,2},{2,0},{1,3},{3,1},{4,6},{6,4},{5,7},{7,5},{8,10},{10,8},{9,1... | collective-permute-start | bytes 1572872 | tf_op jit(solution)/shard_map/ppermute | solution.py:29
  5.6 0.7 copy-start.2
  6.3 0.7 copy-start.3
  7.0 0.7 copy-start.4
  7.7 0.7 copy-start.5
  9.5 5.4 %collective-permute-start.1 = (s32[1,64]{1,0:T(1,128)S(1)}, s32[1,64]{1,0:T(1,128)S(1)}, u32[]{:S(2)}, u32[]{:S(2)}) collective-permute-start(s32[1,64]{1,0:T(1,128)S(1)} %get-tuple-element.45), channel_id=1, source_target_pairs={{0,12},{4,8},{8,4},{12,0},{1,13},{5,9},{9,5},{13,1},{2,14},{6,10},... | collective-permute-start | bytes 776 | tf_op jit(solution)/shard_map/ppermute | solution.py:29
  13.2 4.4 %collective-permute-start.2 = (s32[1,64]{1,0:T(1,128)S(1)}, s32[1,64]{1,0:T(1,128)S(1)}, u32[]{:S(2)}, u32[]{:S(2)}) collective-permute-start(s32[1,64]{1,0:T(1,128)S(1)} %get-tuple-element.46), channel_id=1, source_target_pairs={{0,8},{4,12},{8,0},{12,4},{1,9},{5,13},{9,1},{13,5},{2,10},{6,14},... | collective-permute-start | bytes 776 | tf_op jit(solution)/shard_map/ppermute | solution.py:29
  13.2 4.4 %collective-permute-start.3 = (s32[1,64]{1,0:T(1,128)S(1)}, s32[1,64]{1,0:T(1,128)S(1)}, u32[]{:S(2)}, u32[]{:S(2)}) collective-permute-start(s32[1,64]{1,0:T(1,128)S(1)} %get-tuple-element.47), channel_id=1, source_target_pairs={{0,4},{4,0},{8,12},{12,8},{1,5},{5,1},{9,13},{13,9},{2,6},{6,2},{1... | collective-permute-start | bytes 776 | tf_op jit(solution)/shard_map/ppermute | solution.py:29
  19.2 7.9 %collective-permute-start.4 = (bf16[1,2,64,1024]{3,2,1,0:T(8,128)(2,1)S(1)}, bf16[1,2,64,1024]{3,2,1,0:T(8,128)(2,1)S(1)}, u32[]{:S(2)}, u32[]{:S(2)}) collective-permute-start(bf16[1,2,64,1024]{3,2,1,0:T(8,128)(2,1)S(1)} %get-tuple-element.52), channel_id=1, source_target_pairs={{0,4},{4,0},{8,12},{12,8},{1,5},{5,1},{9,13},{13,9},{2,6},{6,2},{1... | collective-permute-start | bytes 786440 | tf_op jit(solution)/shard_map/ppermute | solution.py:29
  20.3 15.9 %collective-permute-start.14 = (bf16[1,2,64,1024]{3,2,1,0:T(8,128)(2,1)S(1)}, bf16[1,2,64,1024]{3,2,1,0:T(8,128)(2,1)S(1)}, u32[]{:S(2)}, u32[]{:S(2)}) collective-permute-start(bf16[1,2,64,1024]{3,2,1,0:T(8,128)(2,1)S(1)} %get-tuple-element.67), channel_id=1, source_target_pairs={{0,12},{4,8},{8,4},{12,0},{1,13},{5,9},{9,5},{13,1},{2,14},{6,10},... | collective-permute-start | bytes 786440 | tf_op jit(solution)/shard_map/ppermute | solution.py:29
  22.8 22.1 %collective-permute-start.17 = (bf16[1,2,64,1024]{3,2,1,0:T(8,128)(2,1)S(1)}, bf16[1,2,64,1024]{3,2,1,0:T(8,128)(2,1)S(1)}, u32[]{:S(2)}, u32[]{:S(2)}) collective-permute-start(bf16[1,2,64,1024]{3,2,1,0:T(8,128)(2,1)S(1)} %get-tuple-element.73), channel_id=1, source_target_pairs={{0,8},{4,12},{8,0},{12,4},{1,9},{5,13},{9,1},{13,5},{2,10},{6,14},... | collective-permute-start | bytes 786440 | tf_op jit(solution)/shard_map/ppermute | solution.py:29
  29.8 1.3 %collective-permute-start.5 = (bf16[2,16,1024]{2,1,0:T(8,128)(2,1)S(1)}, bf16[2,16,1024]{2,1,0:T(8,128)(2,1)S(1)}, u32[]{:S(2)}, u32[]{:S(2)}) collective-permute-start(bf16[2,16,1024]{2,1,0:T(8,128)(2,1)S(1)} %get-tuple-element.56), channel_id=1, source_target_pairs={{0,1},{1,0},{2,3},{3,2},{4,5},{5,4},{6,7},{7,6},{8,9},{9,8},{10,11... | collective-permute-start | bytes 196616 | tf_op jit(solution)/shard_map/ppermute | solution.py:29
  29.9 1.4 %collective-permute-start.6 = (bf16[2,16,1024]{2,1,0:T(8,128)(2,1)S(1)}, bf16[2,16,1024]{2,1,0:T(8,128)(2,1)S(1)}, u32[]{:S(2)}, u32[]{:S(2)}) collective-permute-start(bf16[2,16,1024]{2,1,0:T(8,128)(2,1)S(1)} %get-tuple-element.57), channel_id=1, source_target_pairs={{0,1},{1,0},{2,3},{3,2},{4,5},{5,4},{6,7},{7,6},{8,9},{9,8},{10,11... | collective-permute-start | bytes 196616 | tf_op jit(solution)/shard_map/ppermute | solution.py:29
  30.4 1.3 %collective-permute-start.7 = (bf16[2,16,1024]{2,1,0:T(8,128)(2,1)S(1)}, bf16[2,16,1024]{2,1,0:T(8,128)(2,1)S(1)}, u32[]{:S(2)}, u32[]{:S(2)}) collective-permute-start(bf16[2,16,1024]{2,1,0:T(8,128)(2,1)S(1)} %get-tuple-element.58), channel_id=1, source_target_pairs={{0,1},{1,0},{2,3},{3,2},{4,5},{5,4},{6,7},{7,6},{8,9},{9,8},{10,11... | collective-permute-start | bytes 196616 | tf_op jit(solution)/shard_map/ppermute | solution.py:29
  31.2 1.3 %collective-permute-start.8 = (bf16[2,16,1024]{2,1,0:T(8,128)(2,1)S(1)}, bf16[2,16,1024]{2,1,0:T(8,128)(2,1)S(1)}, u32[]{:S(2)}, u32[]{:S(2)}) collective-permute-start(bf16[2,16,1024]{2,1,0:T(8,128)(2,1)S(1)} %get-tuple-element.59), channel_id=1, source_target_pairs={{0,1},{1,0},{2,3},{3,2},{4,5},{5,4},{6,7},{7,6},{8,9},{9,8},{10,11... | collective-permute-start | bytes 196616 | tf_op jit(solution)/shard_map/ppermute | solution.py:29
  31.3 1.3 %collective-permute-start.9 = (bf16[2,16,1024]{2,1,0:T(8,128)(2,1)S(1)}, bf16[2,16,1024]{2,1,0:T(8,128)(2,1)S(1)}, u32[]{:S(2)}, u32[]{:S(2)}) collective-permute-start(bf16[2,16,1024]{2,1,0:T(8,128)(2,1)S(1)} %get-tuple-element.60), channel_id=1, source_target_pairs={{0,1},{1,0},{2,3},{3,2},{4,5},{5,4},{6,7},{7,6},{8,9},{9,8},{10,11... | collective-permute-start | bytes 196616 | tf_op jit(solution)/shard_map/ppermute | solution.py:29
  31.7 1.3 %collective-permute-start.10 = (bf16[2,16,1024]{2,1,0:T(8,128)(2,1)S(1)}, bf16[2,16,1024]{2,1,0:T(8,128)(2,1)S(1)}, u32[]{:S(2)}, u32[]{:S(2)}) collective-permute-start(bf16[2,16,1024]{2,1,0:T(8,128)(2,1)S(1)} %get-tuple-element.61), channel_id=1, source_target_pairs={{0,1},{1,0},{2,3},{3,2},{4,5},{5,4},{6,7},{7,6},{8,9},{9,8},{10,11... | collective-permute-start | bytes 196616 | tf_op jit(solution)/shard_map/ppermute | solution.py:29
  32.4 1.3 %collective-permute-start.11 = (bf16[2,16,1024]{2,1,0:T(8,128)(2,1)S(1)}, bf16[2,16,1024]{2,1,0:T(8,128)(2,1)S(1)}, u32[]{:S(2)}, u32[]{:S(2)}) collective-permute-start(bf16[2,16,1024]{2,1,0:T(8,128)(2,1)S(1)} %get-tuple-element.62), channel_id=1, source_target_pairs={{0,1},{1,0},{2,3},{3,2},{4,5},{5,4},{6,7},{7,6},{8,9},{9,8},{10,11... | collective-permute-start | bytes 196616 | tf_op jit(solution)/shard_map/ppermute | solution.py:29
  32.6 1.3 %collective-permute-start.12 = (bf16[2,16,1024]{2,1,0:T(8,128)(2,1)S(1)}, bf16[2,16,1024]{2,1,0:T(8,128)(2,1)S(1)}, u32[]{:S(2)}, u32[]{:S(2)}) collective-permute-start(bf16[2,16,1024]{2,1,0:T(8,128)(2,1)S(1)} %get-tuple-element.63), channel_id=1, source_target_pairs={{0,1},{1,0},{2,3},{3,2},{4,5},{5,4},{6,7},{7,6},{8,9},{9,8},{10,11... | collective-permute-start | bytes 196616 | tf_op jit(solution)/shard_map/ppermute | solution.py:29
  34.7 12.2 %collective-permute-start.13 = (bf16[128,1024]{1,0:T(8,128)(2,1)S(1)}, bf16[128,1024]{1,0:T(8,128)(2,1)S(1)}, u32[]{:S(2)}, u32[]{:S(2)}) collective-permute-start(bf16[128,1024]{1,0:T(8,128)(2,1)S(1)} %get-tuple-element.65), channel_id=1, source_target_pairs={{0,2},{2,0},{1,3},{3,1},{4,6},{6,4},{5,7},{7,5},{8,10},{10,8},{9,1... | collective-permute-start | bytes 786440 | tf_op jit(solution)/shard_map/ppermute | solution.py:29
  38.0 12.5 %copy-start = (f32[4,64,1024]{2,1,0:T(8,128)S(1)}, f32[4,64,1024]{2,1,0:T(8,128)}, u32[]{:S(2)}) copy-start(f32[4,64,1024]{2,1,0:T(8,128)} %refs_7_.3) | copy-start | bytes 3145732
  38.0 8.8 %collective-permute-start.15 = (bf16[2,64,1024]{2,1,0:T(8,128)(2,1)S(1)}, bf16[2,64,1024]{2,1,0:T(8,128)(2,1)S(1)}, u32[]{:S(2)}, u32[]{:S(2)}) collective-permute-start(bf16[2,64,1024]{2,1,0:T(8,128)(2,1)S(1)} %get-tuple-element.69), channel_id=1, source_target_pairs={{0,1},{1,0},{2,3},{3,2},{4,5},{5,4},{6,7},{7,6},{8,9},{9,8},{10,11... | collective-permute-start | bytes 786440 | tf_op jit(solution)/shard_map/ppermute | solution.py:29
  46.7 2.3 %collective-permute-start.18 = (bf16[2,64,1024]{2,1,0:T(8,128)(2,1)S(1)}, bf16[2,64,1024]{2,1,0:T(8,128)(2,1)S(1)}, u32[]{:S(2)}, u32[]{:S(2)}) collective-permute-start(bf16[2,64,1024]{2,1,0:T(8,128)(2,1)S(1)} %get-tuple-element.75), channel_id=1, source_target_pairs={{0,1},{1,0},{2,3},{3,2},{4,5},{5,4},{6,7},{7,6},{8,9},{9,8},{10,11... | collective-permute-start | bytes 786440 | tf_op jit(solution)/shard_map/ppermute | solution.py:29
  47.5 6.4 %collective-permute-start.16 = (bf16[64,1024]{1,0:T(8,128)(2,1)S(1)}, bf16[64,1024]{1,0:T(8,128)(2,1)S(1)}, u32[]{:S(2)}, u32[]{:S(2)}) collective-permute-start(bf16[64,1024]{1,0:T(8,128)(2,1)S(1)} %get-tuple-element.71), channel_id=1, source_target_pairs={{0,2},{2,0},{1,3},{3,1},{4,6},{6,4},{5,7},{7,5},{8,10},{10,8},{9,1... | collective-permute-start | bytes 393224 | tf_op jit(solution)/shard_map/ppermute | solution.py:29
  49.6 6.6 %collective-permute-start.19 = (bf16[64,1024]{1,0:T(8,128)(2,1)S(1)}, bf16[64,1024]{1,0:T(8,128)(2,1)S(1)}, u32[]{:S(2)}, u32[]{:S(2)}) collective-permute-start(bf16[64,1024]{1,0:T(8,128)(2,1)S(1)} %get-tuple-element.77), channel_id=1, source_target_pairs={{0,2},{2,0},{1,3},{3,1},{4,6},{6,4},{5,7},{7,5},{8,10},{10,8},{9,1... | collective-permute-start | bytes 393224 | tf_op jit(solution)/shard_map/ppermute | solution.py:29
  56.9 3.1 %collective-permute-start.20 = (f32[8,128]{1,0:T(8,128)S(1)}, f32[8,128]{1,0:T(8,128)S(1)}, u32[]{:S(2)}, u32[]{:S(2)}) collective-permute-start(f32[8,128]{1,0:T(8,128)S(1)} %get-tuple-element.78.refs_3_.refs_4_), channel_id=1, source_target_pairs={{0,3},{1,2},{2,1},{3,0},{4,7},{5,6},{6,5},{7,4},{8,11},{9,10},{10,... | collective-permute-start | bytes 12296 | tf_op jit(solution)/shard_map/ppermute | solution.py:29
  57.8 3.6 %collective-permute-start.21 = (f32[8,128]{1,0:T(8,128)S(1)}, f32[8,128]{1,0:T(8,128)S(1)}, u32[]{:S(2)}, u32[]{:S(2)}) collective-permute-start(f32[8,128]{1,0:T(8,128)S(1)} %get-tuple-element.78.refs_3_.refs_4_), channel_id=1, source_target_pairs={{0,2},{1,3},{2,0},{3,1},{4,6},{5,7},{6,4},{7,5},{8,10},{9,11},{10,... | collective-permute-start | bytes 12296 | tf_op jit(solution)/shard_map/ppermute | solution.py:29
  58.5 2.8 %collective-permute-start.22 = (f32[8,128]{1,0:T(8,128)S(1)}, f32[8,128]{1,0:T(8,128)S(1)}, u32[]{:S(2)}, u32[]{:S(2)}) collective-permute-start(f32[8,128]{1,0:T(8,128)S(1)} %get-tuple-element.78.refs_3_.refs_4_), channel_id=1, source_target_pairs={{0,1},{1,0},{2,3},{3,2},{4,5},{5,4},{6,7},{7,6},{8,9},{9,8},{10,11... | collective-permute-start | bytes 12296 | tf_op jit(solution)/shard_map/ppermute | solution.py:29
  62.2 8.5 %collective-permute-start.23 = (bf16[64,1024]{1,0:T(8,128)(2,1)S(1)}, bf16[64,1024]{1,0:T(8,128)(2,1)S(1)}, u32[]{:S(2)}, u32[]{:S(2)}) collective-permute-start(bf16[64,1024]{1,0:T(8,128)(2,1)S(1)} %get-tuple-element.82.refs_0_), channel_id=1, source_target_pairs={{0,12},{4,8},{8,4},{12,0},{1,13},{5,9},{9,5},{13,1},{2,14},{6,10},... | collective-permute-start | bytes 393224 | tf_op jit(solution)/shard_map/ppermute | solution.py:29
  64.2 10.8 %collective-permute-start.24 = (bf16[64,1024]{1,0:T(8,128)(2,1)S(1)}, bf16[64,1024]{1,0:T(8,128)(2,1)S(1)}, u32[]{:S(2)}, u32[]{:S(2)}) collective-permute-start(bf16[64,1024]{1,0:T(8,128)(2,1)S(1)} %get-tuple-element.83), channel_id=1, source_target_pairs={{0,8},{4,12},{8,0},{12,4},{1,9},{5,13},{9,1},{13,5},{2,10},{6,14},... | collective-permute-start | bytes 393224 | tf_op jit(solution)/shard_map/ppermute | solution.py:29
  65.0 10.0 %collective-permute-start.25 = (bf16[64,1024]{1,0:T(8,128)(2,1)S(1)}, bf16[64,1024]{1,0:T(8,128)(2,1)S(1)}, u32[]{:S(2)}, u32[]{:S(2)}) collective-permute-start(bf16[64,1024]{1,0:T(8,128)(2,1)S(1)} %get-tuple-element.85), channel_id=1, source_target_pairs={{0,4},{4,0},{8,12},{12,8},{1,5},{5,1},{9,13},{13,9},{2,6},{6,2},{1... | collective-permute-start | bytes 393224 | tf_op jit(solution)/shard_map/ppermute | solution.py:29
